TPU v7x, 32 devices: a whole 2x2x4 slice. The times are simulated.
32 devices in a mesh: seq: 8 (over z, core), chan: 4 (over y, x).
Axes of the slice: x: 2, y: 2, z: 4, core: 2. Of those that a mesh axis runs over, the one named last changes fastest.
Arguments:
- hyena_in: bfloat16 [2048, 3, 4096], P('seq', None, 'chan'), may hold values from -6 to 6
- prior_kv: bfloat16 [127, 4096], P(None, 'chan'), may hold values from -6 to 6
- filters: float32 [256, 128], P('chan'), may hold values from -0.5 to 0.5
- gain: float32 [4096], replicated, may hold values from 0.5 to 1.5
- w_qkv: bfloat16 [4096, 3, 4096], P('seq', None, 'chan'), may hold values from -0.09375 to 0.09375
- cache_k: bfloat16 [1216, 4096], P('seq', 'chan'), may hold values from -110 to 110
- cache_v: bfloat16 [1216, 4096], P('seq', 'chan'), may hold values from -6 to 6
Outputs:
- attn_out: bfloat16 [2048, 4096], P('seq', 'chan')
All inputs are finite; a program needn't handle non-finite values.
Results may differ from a plain program's by a relative error of at most 0.019.
The roundings to bfloat16 on the way count: a program that leaves them out, or rounds other values in their place, can miss the bound.
Values may be sent and summed in bfloat16 or wider, within the bound.
No kernel may reach another device: no remote copies, remote signals or barrier semaphores. Data moves between devices by JAX's collectives and lax.ppermute only.
A program may use at most 128 MiB of HBM per device.

v0:
```python
import functools

import jax
import jax.numpy as jnp
from jax import lax
from jax.experimental import pallas as pl
from jax.experimental.pallas import tpu as pltpu
from jax.sharding import PartitionSpec as P

D = 4096
HEADS = 32
HEAD = D // HEADS
LANES = 128
PAD = 8
BF16 = jnp.bfloat16
F32 = jnp.float32
MIB = 1024 * 1024


BRIEF = pl.CostEstimate(flops=1, transcendentals=0, bytes_accessed=1)


def whole(shape):
    return pl.BlockSpec(shape, lambda *_: (0,) * len(shape))


def conv_kernel(group, hin_ref, halo_ref, taps_ref, out_ref):
    taps = taps_ref[...]
    count = taps.shape[0]
    width = taps.shape[1]
    kv = (hin_ref[1].astype(F32) * hin_ref[2].astype(F32)).astype(BF16)
    ext = jnp.concatenate([halo_ref[...], kv], axis=0)
    rows = kv.shape[0]
    blocks = rows // width
    windows = jnp.concatenate(
        [ext[b * width : (b + 2) * width] for b in range(blocks)], axis=1
    )
    high = taps.astype(BF16)
    low = (taps - high.astype(F32)).astype(BF16)
    source = lax.broadcasted_iota(jnp.int32, (width, 2 * width), 0)
    column = lax.broadcasted_iota(jnp.int32, (width, 2 * width), 1)
    flip = jnp.where(source + column == width, 1.0, 0.0).astype(BF16)
    total = None
    for part in (high, low):
        first = jnp.dot(part, flip, preferred_element_type=F32)
        toeplitz = jnp.concatenate(
            [
                pltpu.roll(
                    jnp.broadcast_to(first[g : g + 1], (width, 2 * width)),
                    0,
                    1,
                    stride=1,
                    stride_axis=0,
                ).astype(BF16)
                for g in range(count)
            ],
            axis=0,
        )
        product = jnp.dot(toeplitz, windows, preferred_element_type=F32)
        total = product if total is None else total + product
    owner = lax.broadcasted_iota(jnp.int32, (width, blocks * LANES), 1) % LANES // group
    conv = total[:width]
    for g in range(1, count):
        conv = jnp.where(owner == g, total[g * width : (g + 1) * width], conv)
    query = hin_ref[0].astype(F32)
    for b in range(blocks):
        piece = query[b * width : (b + 1) * width] * conv[:, b * LANES : (b + 1) * LANES]
        out_ref[b * width : (b + 1) * width, :] = piece.astype(BF16)


def hyena(hin, halo, filters):
    _, rows, width = hin.shape
    taps = filters.shape[1]
    group = width // filters.shape[0]
    per_tile = LANES // group
    return pl.pallas_call(
        functools.partial(conv_kernel, group),
        grid=(width // LANES,),
        in_specs=[
            pl.BlockSpec((3, rows, LANES), lambda i: (0, 0, i)),
            pl.BlockSpec((taps, LANES), lambda i: (0, i)),
            pl.BlockSpec((per_tile, taps), lambda i: (i, 0)),
        ],
        out_specs=pl.BlockSpec((rows, LANES), lambda i: (0, i)),
        out_shape=jax.ShapeDtypeStruct((rows, width), BF16),
        compiler_params=pltpu.CompilerParams(vmem_limit_bytes=12 * MIB),
        cost_estimate=BRIEF,
        name="hyena_filters",
    )(hin, halo, filters)


def norm_kernel(half, place_ref, own_ref, x_ref, y_ref, d0_ref, d1_ref, gain_ref, *rest):
    out_ref = rest[-1]
    chan = place_ref[0]
    step = pl.program_id(0)
    diag = jnp.where(step < half, d0_ref[...], d1_ref[...])
    parts = [r.astype(F32) for r in (own_ref[...], x_ref[...], y_ref[...], diag)]
    total = sum(jnp.sum(p * p, axis=-1, keepdims=True) for p in parts)
    factor = lax.rsqrt(total / D + 1e-6)
    for m, p in enumerate(parts):
        where = chan ^ m
        out_ref[0, where] = (p * factor * gain_ref[where]).astype(BF16)


def norm(place, j, zs, own, from_x, from_y, diag0, diag1, gain, buffer):
    rows, width = own.shape
    step = min(64, rows // 2)
    half = rows // 2 // step
    band = pl.BlockSpec((step, width), lambda i: (i, 0))
    args = [place, own, from_x, from_y, diag0, diag1, gain]
    specs = [
        pl.BlockSpec(memory_space=pltpu.SMEM),
        band,
        band,
        band,
        pl.BlockSpec((step, width), lambda i: (jnp.minimum(i, half - 1), 0)),
        pl.BlockSpec((step, width), lambda i: (jnp.maximum(i - half, 0), 0)),
        whole((4, 1, width)),
    ]
    aliases = {}
    if buffer is not None:
        aliases = {len(args): 0}
        args.append(buffer)
        specs.append(pl.BlockSpec(memory_space=pl.ANY))
    return pl.pallas_call(
        functools.partial(norm_kernel, half),
        grid=(2 * half,),
        in_specs=specs,
        out_specs=pl.BlockSpec((1, 4, step, width), lambda i: (j, 0, i, 0)),
        out_shape=jax.ShapeDtypeStruct((zs, 4, rows, width), BF16),
        input_output_aliases=aliases,
        compiler_params=pltpu.CompilerParams(vmem_limit_bytes=16 * MIB),
        cost_estimate=BRIEF,
        name="norm",
    )(*args)


def project_kernel(zs, depth, place_ref, normed_ref, *refs):
    own, sib, outs = refs[:zs], refs[zs : 2 * zs], refs[2 * zs :]
    z, core = place_ref[1], place_ref[2]
    for part, out_ref in enumerate(outs):
        total = None
        for shift in range(zs):
            block = lax.rem(z + zs - shift, zs)
            for k, w_ref in enumerate((own[shift], sib[shift])):
                at = pl.multiple_of((core ^ k) * depth, depth)
                left = normed_ref[0, block, :, pl.ds(at, depth)]
                right = w_ref[part * depth : (part + 1) * depth, :]
                term = jnp.dot(left, right, preferred_element_type=F32)
                total = term if total is None else total + term
        out_ref[0] = total.astype(BF16)


def project(place, normed, own, sib, count, depth):
    zs, parts, rows, width = normed.shape
    cols = own[0].shape[1]
    weights = pl.BlockSpec((count * depth, cols), lambda j: (0, 0))
    return pl.pallas_call(
        functools.partial(project_kernel, zs, depth),
        grid=(zs,),
        in_specs=[
            pl.BlockSpec(memory_space=pltpu.SMEM),
            pl.BlockSpec((1, parts, rows, width), lambda j: (j, 0, 0, 0)),
        ]
        + [weights] * (2 * zs),
        out_specs=[pl.BlockSpec((1, rows, cols), lambda j: (j, 0, 0))] * count,
        out_shape=[jax.ShapeDtypeStruct((zs, rows, cols), BF16)] * count,
        compiler_params=pltpu.CompilerParams(vmem_limit_bytes=24 * MIB),
        cost_estimate=BRIEF,
        name="project",
    )(place, normed, *own, *sib)


NT = (((1,), (1,)), ((), ()))


def attend_kernel(shifts, place_ref, q_ref, k_ref, v_ref, ks_ref, vs_ref, ck_ref, cv_ref, out_ref):
    z, core = place_ref[1], place_ref[2]
    zs, rows, cols = k_ref.shape
    heads = range(cols // HEAD)
    factor = 1.4426950408889634 / HEAD**0.5
    shift = jnp.int32(shifts[0])
    for i, s in enumerate(shifts):
        shift = jnp.where(pl.program_id(0) == i, s, shift)
    block = lax.rem(z + shift, zs)
    hcols = [slice(h * HEAD, (h + 1) * HEAD) for h in heads]
    queries = [q_ref[0, :, hcol] for hcol in hcols]

    def fold(state, h, key, value, mask):
        s = lax.dot_general(queries[h], key, NT, preferred_element_type=F32)
        if mask is not None:
            s = jnp.where(mask, s, -1e30)
        top = jnp.max(s, axis=-1, keepdims=True) * factor
        if state is not None:
            top = jnp.maximum(top, state[0])
        weights = jnp.exp2(s * factor - top)
        total = jnp.sum(weights, axis=-1, keepdims=True)
        summed = jnp.dot(weights.astype(BF16), value, preferred_element_type=F32)
        if state is not None:
            scale = jnp.exp2(state[0] - top)
            total, summed = total + state[1] * scale, summed + state[2] * scale
        return top, total, summed

    def both(b, h):
        at = lax.rem(z + zs - b, zs)
        key = jnp.concatenate([k_ref[at, :, hcols[h]], ks_ref[at, :, hcols[h]]], axis=0)
        value = jnp.concatenate([v_ref[at, :, hcols[h]], vs_ref[at, :, hcols[h]]], axis=0)
        return key, value

    def earlier(b, states):
        return tuple(fold(states[h], h, *both(b, h), None) for h in heads)

    states = tuple(fold(None, h, ck_ref[:, hcols[h]], cv_ref[:, hcols[h]], None) for h in heads)
    states = lax.fori_loop(0, block, earlier, states)
    row = lax.broadcasted_iota(jnp.int32, (rows, 2 * rows), 0)
    col = lax.broadcasted_iota(jnp.int32, (rows, 2 * rows), 1)
    visible = jnp.where(col < rows, col, jnp.where(core == 1, 0, rows)) <= row
    for h in heads:
        _, total, summed = fold(states[h], h, *both(block, h), visible)
        out_ref[0, :, hcols[h]] = (summed / total).astype(BF16)


def attend(shifts, place, q, k, v, k_sib, v_sib, ck, cv):
    zs, rows, cols = q.shape

    def slab(i, place_ref):
        shift = jnp.int32(shifts[0])
        for n, s in enumerate(shifts):
            shift = jnp.where(i == n, s, shift)
        return lax.rem(zs - shift, zs), 0, 0

    args = (k, v, k_sib, v_sib, ck, cv)
    return pl.pallas_call(
        functools.partial(attend_kernel, shifts),
        grid_spec=pltpu.PrefetchScalarGridSpec(
            num_scalar_prefetch=1,
            grid=(len(shifts),),
            in_specs=[pl.BlockSpec((1, rows, cols), slab)] + [whole(a.shape) for a in args],
            out_specs=pl.BlockSpec((1, rows, cols), lambda i, place_ref: (i, 0, 0)),
        ),
        out_shape=jax.ShapeDtypeStruct((len(shifts), rows, cols), BF16),
        compiler_params=pltpu.CompilerParams(vmem_limit_bytes=32 * MIB),
        cost_estimate=BRIEF,
        name="attend",
    )(place, q, *args)


def pack_kernel(at, crow, *refs):
    parcels, (out_ref, scratch) = refs[:-2], refs[-2:]
    for i, piece in enumerate(parcels):
        band = piece[at : at + crow + PAD].astype(F32)
        scratch[i * crow : (i + 1) * crow, :] = band[:crow]
    out_ref[...] = scratch[...].astype(BF16)


def pack(parcels, at, crow):
    cols = parcels[0].shape[1]
    out = (len(parcels) * crow, cols)
    return pl.pallas_call(
        functools.partial(pack_kernel, at, crow),
        in_specs=[whole(p.shape) for p in parcels],
        out_specs=whole(out),
        out_shape=jax.ShapeDtypeStruct(out, BF16),
        scratch_shapes=[pltpu.VMEM(out, F32)],
        compiler_params=pltpu.CompilerParams(vmem_limit_bytes=24 * MIB),
        cost_estimate=BRIEF,
        name="pack",
    )(*parcels)


def join_kernel(place_ref, *refs):
    pieces, out_ref = refs[:-1], refs[-1]
    zs = len(pieces)
    cols = pieces[0].shape[1]
    for r, piece in enumerate(pieces):
        at = lax.rem(place_ref[1] + zs - r, zs) * cols
        out_ref[:, pl.ds(pl.multiple_of(at, cols), cols)] = piece[...]


def join(place, pieces):
    rows, cols = pieces[0].shape
    out = (rows, cols * len(pieces))
    return pl.pallas_call(
        join_kernel,
        in_specs=[pl.BlockSpec(memory_space=pltpu.SMEM)] + [whole(p.shape) for p in pieces],
        out_specs=whole(out),
        out_shape=jax.ShapeDtypeStruct(out, BF16),
        name="join",
    )(place, *pieces)


def shift_z(value, steps, zs):
    pairs = [(2 * a + k, 2 * ((a + steps) % zs) + k) for a in range(zs) for k in range(2)]
    return lax.ppermute(value, "seq", pairs)


def swap_core(value, zs):
    return lax.ppermute(value, "seq", [(2 * a + k, 2 * a + 1 - k) for a in range(zs) for k in range(2)])


def swap_chan(value, bit):
    return lax.ppermute(value, "chan", [(c, c ^ bit) for c in range(4)])


def after(value, *others):
    return lax.optimization_barrier((value, *others))[0]


def fast_body(hyena_in, prior_kv, filters, gain, w_qkv, cache_k, cache_v):
    rows, _, width = hyena_in.shape
    seqs = lax.axis_size("seq")
    zs = seqs // 2
    taps = filters.shape[1]
    depth, crow = w_qkv.shape[0], cache_k.shape[0]
    cols = width // zs
    my_seq = lax.axis_index("seq")
    z, core = my_seq // 2, my_seq % 2
    chan = lax.axis_index("chan")
    place = jnp.stack([chan, z, core]).astype(jnp.int32)

    w_t = jnp.transpose(w_qkv, (1, 0, 2))
    caches = [jnp.pad(c, ((0, PAD), (0, 0))) for c in (cache_k, cache_v)]

    def parcel(kind, r):
        at = (z + r) % zs * cols
        parts = [
            lax.dynamic_slice(w_t, (p, 0, at), (1, depth, cols))[0]
            for p in ((1, 2) if kind == "kv" else (0,))
        ]
        if kind == "kv":
            parts += [lax.dynamic_slice_in_dim(c, at, cols, 1) for c in caches]
        return jnp.concatenate(parts, axis=0)

    hin = jnp.transpose(hyena_in, (1, 0, 2))
    tail = (hin[1, rows - taps :].astype(F32) * hin[2, rows - taps :].astype(F32)).astype(BF16)
    halo = lax.ppermute(tail, "seq", [(s, s + 1) for s in range(seqs - 1)])
    halo = jnp.where(my_seq == 0, jnp.pad(prior_kv, ((taps - prior_kv.shape[0], 0), (0, 0))), halo)

    order = [("kv", 1), "acts", ("q", 1), "acts", ("q", 3), "acts", ("kv", 3), ("kv", 2), ("q", 2)]
    here = {(kind, 0): parcel(kind, 0) for kind in ("kv", "q")}
    acts = [hyena(hin, halo, filters)]
    sent = []
    for n, item in enumerate(order):
        value, steps = (acts[-1], 1) if item == "acts" else (parcel(*item), item[1])
        if n == 0:
            value = after(value, halo)
        if n >= 2:
            value = after(value, sent[n - 1] if item == ("kv", 3) else sent[n - 2])
        sent.append(shift_z(value, steps, zs))
        if item == "acts":
            acts.append(sent[-1])
        else:
            here[item] = sent[-1]
    there = {item: swap_core(here[item], zs) for item in here if item != ("q", 2)}

    pace = [("kv", 1), ("q", 1), ("q", 3), None]
    swapped = [[], [("kv", 0), ("q", 0)], [("kv", 1), ("q", 1)], [("q", 3)]]
    gain4 = gain.reshape(4, 1, width)
    half = rows // 2
    normed, diag0, diag1 = None, None, None
    for j, own in enumerate(acts):
        own = after(own, *([here[pace[j]]] if pace[j] else []), *([diag0, diag1] if j else []))
        from_x, from_y = swap_chan(own, 1), swap_chan(own, 2)
        if j:
            settled = [normed] + [there[item] for item in swapped[j]]
            from_x, from_y = after(from_x, *settled), after(from_y, *settled)
        diag0 = swap_chan(from_x[:half], 2)
        diag1 = swap_chan(from_y[half:], 1)
        normed = norm(place, j, zs, own, from_x, from_y, diag0, diag1, gain4, normed)

    mine = [here["kv", r] for r in range(zs)]
    theirs = [there["kv", r] for r in range(zs)]
    ck, cv = [pack(mine + theirs, 2 * depth + i * (crow + PAD), crow) for i in range(2)]
    k, v = project(place, after(normed, ck, cv), mine, theirs, 2, depth)
    k_sib, v_sib = swap_core(k, zs), swap_core(v, zs)
    there["q", 2] = swap_core(after(here["q", 2], k), zs)
    queries = [[side["q", r] for r in range(zs)] for side in (here, there)]
    (q,) = project(place, normed, *queries, 1, depth)
    pieces, out = {}, None
    for shifts, wait in (((2,), ()), ((1, 3), ()), ((0,), (2,))):
        ready = q if out is None else after(q, out, *[pieces[r] for r in wait])
        out = attend(shifts, place, ready, k, v, k_sib, v_sib, ck, cv)
        for i, r in enumerate(shifts):
            pieces[r] = shift_z(out[i], r, zs) if r else out[i]
    return join(place, [pieces[r] for r in range(zs)])


def shifted(value, axis, steps):
    count = lax.axis_size(axis)
    leading, last = (max(0, -steps), min(count, count - steps))
    return lax.ppermute(value, axis, [(source, source + steps) for source in range(leading, last)])


def body(hyena_in, prior_kv, filters, gain, w_qkv, cache_k, cache_v):
    rows_dev = hyena_in.shape[0]
    width = hyena_in.shape[2]
    history = prior_kv.shape[0]
    tap_count = filters.shape[1]
    head_size = D // HEADS
    heads_dev = width // head_size
    cache_rows = cache_k.shape[0]
    stride = cache_rows + rows_dev
    my_index = lax.axis_index("seq")
    stream_q = hyena_in[:, 0].astype(jnp.float32)
    kv_prod = (hyena_in[:, 1].astype(jnp.float32) * hyena_in[:, 2].astype(jnp.float32)).astype(
        jnp.bfloat16
    )
    before = shifted(kv_prod[rows_dev - history :], "seq", 1)
    before = jnp.where(my_index == 0, prior_kv, before)
    extended = jnp.concatenate([before, kv_prod], axis=0).astype(jnp.float32)
    tap_table = jnp.repeat(filters, width // filters.shape[0], axis=0).T

    def add_tap(tap_index, total):
        offset = (tap_count - 1 - tap_index).astype(jnp.int32)
        window = lax.dynamic_slice_in_dim(extended, offset, rows_dev, 0)
        coeff = lax.dynamic_index_in_dim(tap_table, tap_index.astype(jnp.int32), 0, keepdims=True)
        return total + coeff * window

    conv = lax.fori_loop(0, tap_count, add_tap, jnp.zeros((rows_dev, width), jnp.float32))
    hyena_out = (stream_q * conv).astype(jnp.bfloat16)
    whole = lax.all_gather(hyena_out, "chan", axis=1, tiled=True)
    as_float = whole.astype(jnp.float32)
    mean_sq = jnp.mean(as_float * as_float, axis=-1, keepdims=True)
    normed = (as_float * lax.rsqrt(mean_sq + 1e-06) * gain[None, :]).astype(jnp.bfloat16)
    piece = lax.all_gather(w_qkv, "seq", axis=0, tiled=True)
    flat_piece = piece.reshape(piece.shape[0], 3 * width)
    projected = jnp.dot(normed, flat_piece, preferred_element_type=jnp.float32)
    qkv = projected.astype(jnp.bfloat16).reshape(rows_dev, 3, width)
    scale = 1.0 / head_size**0.5
    keys_local = jnp.concatenate([cache_k, qkv[:, 1]], axis=0)
    vals_local = jnp.concatenate([cache_v, qkv[:, 2]], axis=0)
    head_q = qkv[:, 0].reshape(rows_dev, heads_dev, head_size)
    query_pos = my_index * rows_dev + jnp.arange(rows_dev, dtype=jnp.int32)
    run_max = jnp.full((heads_dev, rows_dev), -1e30, jnp.float32)
    key_piece = lax.all_gather(keys_local, "seq", axis=0, tiled=True)
    val_piece = lax.all_gather(vals_local, "seq", axis=0, tiled=True)
    count = key_piece.shape[0]
    row_ids = jnp.arange(count, dtype=jnp.int32)
    source = row_ids // stride
    within = row_ids % stride
    key_pos = jnp.where(within < cache_rows, -1, source * rows_dev + within - cache_rows)
    visible = (key_pos[None, :] <= query_pos[:, None])[None]
    scores = (
        jnp.einsum(
            "qhd,khd->hqk",
            head_q,
            key_piece.reshape(count, heads_dev, head_size),
            preferred_element_type=jnp.float32,
        )
        * scale
    )
    scores = jnp.where(visible, scores, jnp.float32(-1e30))
    new_max = jnp.maximum(run_max, jnp.max(scores, axis=-1))
    weights = jnp.where(visible, jnp.exp(scores - new_max[..., None]), jnp.float32(0.0))
    new_sum = jnp.sum(weights, axis=-1)
    probs = weights.astype(jnp.bfloat16)
    added = jnp.einsum(
        "hqk,khd->hqd",
        probs,
        val_piece.reshape(count, heads_dev, head_size),
        preferred_element_type=jnp.float32,
    )
    result = jnp.transpose(added / new_sum[..., None], (1, 0, 2))
    return result.reshape(rows_dev, width).astype(jnp.bfloat16)


def solution(mesh):
    sizes = mesh.shape
    paired = sizes["chan"] == 4 and HEADS // sizes["chan"] == sizes["seq"]
    return jax.shard_map(
        fast_body if paired else body,
        mesh=mesh,
        in_specs=(
            P("seq", None, "chan"),
            P(None, "chan"),
            P("chan", None),
            P(),
            P("seq", None, "chan"),
            P("seq", "chan"),
            P("seq", "chan"),
        ),
        out_specs=P("seq", "chan"),
        check_vma=False,
    )
```

profile of v0, /device:TPU:0, one launch (start us, length us, event | category | flops | bytes accessed | tf_op | source)
XLA Modules:
  0.0 188.6 jit_solution(12914592099127352041)
XLA Ops:
  0.0 1.1 fusion
  1.1 3.1 %collective-permute-start = (bf16[128,1024]{1,0:T(8,128)(2,1)S(1)}, bf16[128,1024]{1,0:T(8,128)(2,1)}, u32[]{:S(2)}, u32[]{:S(2)}) collective-permute-start(bf16[128,1024]{1,0:T(8,128)(2,1)S(1)} %fusion), channel_id=1, source_target_pairs={{0,4},{4,8},{8,12},{12,16},{16,20},{20,24},{24,28},{1,5},{5,9},{9,... | collective-permute-start | bytes 786440 | tf_op jit(solution)/shard_map/ppermute | solution.py:336
  4.2 3.4 %dynamic-slice_bitcast_fusion.1 = (bf16[512,256]{1,0:T(8,128)(2,1)}, bf16[512,256]{1,0:T(8,128)(2,1)}, bf16[512,256]{1,0:T(8,128)(2,1)}, bf16[512,256]{1,0:T(8,1...) fusion(bf16[512,3,1024]{2,0,1:T(8,128)(2,1)} %param.11, ...), kind=kLoop, calls=%fused_computation.7 | loop fusion | bytes 6291472 | tf_op jit(solution)/shard_map/squeeze | solution.py:327
  8.5 1.2 pad_select_fusion.halo_ref
  9.7 3.5 %collective-permute-start.4 = (bf16[1344,256]{1,0:T(8,128)(2,1)S(1)}, bf16[1344,256]{1,0:T(8,128)(2,1)S(1)}, u32[]{:S(2)}, u32[]{:S(2)}) collective-permute-start(bf16[1344,256]{1,0:T(8,128)(2,1)S(1)} %pad_maximum_fusion), channel_id=1, source_target_pairs={{0,8},{4,12},{8,16},{12,20},{16,24},{20,28},{24,0},{28,4},{1,9},{5... | collective-permute-start | bytes 2064392 | tf_op jit(solution)/shard_map/ppermute | solution.py:294
  13.2 6.0 %hyena_filters.1.own_ref = bf16[256,1024]{1,0:T(8,128)(2,1)S(1)} custom-call(bf16[3,256,1024]{2,1,0:T(8,128)(2,1)S(1)} %bitcast.38, bf16[128,1024]{1,0:T(8,128)(2,1)S(1)} %pad_select_fusion.halo_ref, f32[64,128]{1,0:T(8,128)S(1)} %copy-done.15), custom_call_target="tpu_custom_call" | custom-call | flops 1 | bytes 1 | tf_op jit(solution)/shard_map/hyena_filters/pallas_call | solution.py:76
  19.2 1.6 collective-permute-start.1
  20.8 10.6 %collective-permute-done.4.refs_1_ = bf16[1344,256]{1,0:T(8,128)(2,1)S(1)} collective-permute-done((bf16[1344,256]{1,0:T(8,128)(2,1)S(1)}, bf16[1344,256]{1,0:T(8,128)(2,1)S(1)}, u32[]{:S(2)}, u32[]{:S(2)}) %collective-permute-start.4) | collective-permute-done | bytes 688160 | tf_op jit(solution)/shard_map/ppermute | solution.py:294
  31.4 1.5 collective-permute-start.7
  32.9 1.5 collective-permute-start.9
  34.4 8.0 %collective-permute-done.1.own_ref = bf16[256,1024]{1,0:T(8,128)(2,1)} collective-permute-done((bf16[256,1024]{1,0:T(8,128)(2,1)S(1)}, bf16[256,1024]{1,0:T(8,128)(2,1)}, u32[]{:S(2)}, u32[]{:S(2)}) %collective-permute-start.1) | collective-permute-done | bytes 524320 | tf_op jit(solution)/shard_map/ppermute | solution.py:294
  42.4 1.4 collective-permute-start.5
  44.8 1.6 collective-permute-start.8
  46.4 1.6 collective-permute-start.10
  48.1 15.6 %collective-permute-done.5.refs_1_ = bf16[512,256]{1,0:T(8,128)(2,1)S(1)} collective-permute-done((bf16[512,256]{1,0:T(8,128)(2,1)S(1)}, bf16[512,256]{1,0:T(8,128)(2,1)S(1)}, u32[]{:S(2)}, u32[]{:S(2)}) %collective-permute-start.5) | collective-permute-done | bytes 262176 | tf_op jit(solution)/shard_map/ppermute | solution.py:294
  65.2 1.5 collective-permute-start.11
  66.7 1.5 collective-permute-start.15
  68.3 1.6 collective-permute-done.13.refs_4_
  70.4 1.0 copy-done.2
  74.4 1.9 %norm.4.rest_0_ = bf16[4,4,256,1024]{3,2,1,0:T(8,128)(2,1)S(1)} custom-call(s32[3]{0:T(128)S(1)} %pad_add_fusion.place_ref, bf16[256,1024]{1,0:T(8,128)(2,1)S(1)} %hyena_filters.1.own_ref, bf16[256,1024]{1,0:T(8,128)(2,1)S(1)} %copy-done.2, bf16[256,1024]{1,0:T(8,128)(2,1)S(1)} %copy-done.4, bf16[128,1024]{1,0:T(8,128)(2,1)S(1)} %copy-done.11, ...), custom_call_target="tpu_custom_call" | custom-call | flops 1 | bytes 1 | tf_op jit(solution)/shard_map/norm/pallas_call | solution.py:125
  76.4 1.8 collective-permute-done.11.x_ref
  78.2 1.6 collective-permute-start.14
  80.8 1.5 collective-permute-start.16
  82.3 6.2 %collective-permute-done.6.refs_3_ = bf16[512,256]{1,0:T(8,128)(2,1)} collective-permute-done((bf16[512,256]{1,0:T(8,128)(2,1)}, bf16[512,256]{1,0:T(8,128)(2,1)}, u32[]{:S(2)}, u32[]{:S(2)}) %collective-permute-start.6) | collective-permute-done | bytes 262176 | tf_op jit(solution)/shard_map/ppermute | solution.py:294
  90.0 1.7 collective-permute-start.28
  91.7 3.0 %norm.5.rest_0_ = bf16[4,4,256,1024]{3,2,1,0:T(8,128)(2,1)S(1)} custom-call(s32[3]{0:T(128)S(1)} %pad_add_fusion.place_ref, bf16[256,1024]{1,0:T(8,128)(2,1)} %collective-permute-done.1.own_ref, bf16[256,1024]{1,0:T(8,128)(2,1)S(1)} %collective-permute-done.11.x_ref, ...), custom_call_target="tpu_custom_call", output_to_operand_aliasing={{}: (7, {})} | custom-call | flops 1 | bytes 1 | tf_op jit(solution)/shard_map/norm/pallas_call | solution.py:125
  94.8 8.4 %collective-permute-done.17.x_ref = bf16[256,1024]{1,0:T(8,128)(2,1)S(1)} collective-permute-done((bf16[256,1024]{1,0:T(8,128)(2,1)}, bf16[256,1024]{1,0:T(8,128)(2,1)S(1)}, u32[]{:S(2)}, u32[]{:S(2)}) %collective-permute-start.17) | collective-permute-done | bytes 524320 | tf_op jit(solution)/shard_map/ppermute | solution.py:302
  103.8 1.2 collective-permute-start.22
  105.0 6.2 %collective-permute-done.20.d0_ref = bf16[128,1024]{1,0:T(8,128)(2,1)S(1)} collective-permute-done((bf16[128,1024]{1,0:T(8,128)(2,1)S(1)}, bf16[128,1024]{1,0:T(8,128)(2,1)S(1)}, u32[]{:S(2)}, u32[]{:S(2)}) %collective-permute-start.20) | collective-permute-done | bytes 262176 | tf_op jit(solution)/shard_map/ppermute | solution.py:302
  111.5 1.1 collective-permute-start.23
  113.6 8.3 %collective-permute-done.30.refs_2_ = bf16[1344,256]{1,0:T(8,128)(2,1)S(1)} collective-permute-done((bf16[1344,256]{1,0:T(8,128)(2,1)S(1)}, bf16[1344,256]{1,0:T(8,128)(2,1)S(1)}, u32[]{:S(2)}, u32[]{:S(2)}) %collective-permute-start.30) | collective-permute-done | bytes 688160 | tf_op jit(solution)/shard_map/ppermute | solution.py:294
  122.7 2.9 %norm.6.rest_0_ = bf16[4,4,256,1024]{3,2,1,0:T(8,128)(2,1)S(1)} custom-call(s32[3]{0:T(128)S(1)} %pad_add_fusion.place_ref, bf16[256,1024]{1,0:T(8,128)(2,1)} %collective-permute-done.2.own_ref, bf16[256,1024]{1,0:T(8,128)(2,1)S(1)} %collective-permute-done.17.x_ref, ...), custom_call_target="tpu_custom_call", output_to_operand_aliasing={{}: (7, {})} | custom-call | flops 1 | bytes 1 | tf_op jit(solution)/shard_map/norm/pallas_call | solution.py:125
  125.7 1.3 collective-permute-start.26
  127.0 1.6 collective-permute-start.27
  128.5 14.1 %collective-permute-start.29 = (bf16[512,256]{1,0:T(8,128)(2,1)S(1)}, bf16[512,256]{1,0:T(8,128)(2,1)S(1)}, u32[]{:S(2)}, u32[]{:S(2)}) collective-permute-start(bf16[512,256]{1,0:T(8,128)(2,1)S(1)} %copy-done.29), channel_id=1, source_target_pairs={{0,16},{4,20},{8,24},{12,28},{16,0},{20,4},{24,8},{28,12},{1,17},{... | collective-permute-start | bytes 786440 | tf_op jit(solution)/shard_map/ppermute | solution.py:294
  142.8 1.9 %norm.7.normed_ref = bf16[4,4,256,1024]{3,2,1,0:T(8,128)(2,1)S(1)} custom-call(s32[3]{0:T(128)S(1)} %pad_add_fusion.place_ref, bf16[256,1024]{1,0:T(8,128)(2,1)S(1)} %collective-permute-done.3.own_ref, bf16[256,1024]{1,0:T(8,128)(2,1)S(1)} %collective-permute-done.23.x_ref, ...), custom_call_target="tpu_custom_call", output_to_operand_aliasing={{}: (7, {})} | custom-call | flops 1 | bytes 1 | tf_op jit(solution)/shard_map/norm/pallas_call | solution.py:125
  144.7 5.7 %project.2 = (bf16[4,256,256]{2,1,0:T(8,128)(2,1)S(1)}, bf16[4,256,256]{2,1,0:T(8,128)(2,1)S(1)}) custom-call(s32[3]{0:T(128)S(1)} %pad_add_fusion.place_ref, bf16[4,4,256,1024]{3,2,1,0:T(8,128)(2,1)S(1)} %norm.7.normed_ref, bf16[1344,256]{1,0:T(8,128)(2,1)S(1)} %pad_maximum_fusion.1.refs_0_, bf16[1344,256]{1,0:T(8,128)(2,1)S(1)} %collective-permute-done.4.refs_1_, ...), custom_call_target="tpu_custom_call" | custom-call | flops 1 | bytes 1 | tf_op jit(solution)/shard_map/project/pallas_call | solution.py:158
  151.0 3.2 %collective-permute-done.29.refs_2_ = bf16[512,256]{1,0:T(8,128)(2,1)S(1)} collective-permute-done((bf16[512,256]{1,0:T(8,128)(2,1)S(1)}, bf16[512,256]{1,0:T(8,128)(2,1)S(1)}, u32[]{:S(2)}, u32[]{:S(2)}) %collective-permute-start.29) | collective-permute-done | bytes 262176 | tf_op jit(solution)/shard_map/ppermute | solution.py:294
  154.2 1.5 collective-permute-done.33.refs_6_
  155.7 4.0 %project.3.q_ref = bf16[4,256,256]{2,1,0:T(8,128)(2,1)S(1)} custom-call(s32[3]{0:T(128)S(1)} %pad_add_fusion.place_ref, bf16[4,4,256,1024]{3,2,1,0:T(8,128)(2,1)S(1)} %norm.7.normed_ref, bf16[512,256]{1,0:T(8,128)(2,1)S(1)} %copy-done.5, bf16[512,256]{1,0:T(8,128)(2,1)S(1)} %copy-done.9, bf16[512,256]{1,0:T(8,128)(2,1)S(1)} %collective-permute-done.29.refs_2_, ...), custom_call_target="tpu_custom_call" | custom-call | flops 1 | bytes 1 | tf_op jit(solution)/shard_map/project/pallas_call | solution.py:158
  159.8 4.8 %attend.3 = bf16[1,256,256]{2,1,0:T(8,128)(2,1)S(1)} custom-call(s32[3]{0:T(128)S(1)} %pad_add_fusion.place_ref, bf16[4,256,256]{2,1,0:T(8,128)(2,1)S(1)} %project.3.q_ref, bf16[4,256,256]{2,1,0:T(8,128)(2,1)S(1)} %get-tuple-element.48.k_ref, bf16[4,256,256]{2,1,0:T(8,128)(2,1)S(1)} %get-tuple-element.50.v_ref, ...), custom_call_target="tpu_custom_call" | custom-call | flops 1 | bytes 1 | tf_op jit(solution)/shard_map/attend/pallas_call | solution.py:233
  164.7 2.4 %collective-permute-start.36 = (bf16[256,256]{1,0:T(8,128)(2,1)S(1)}, bf16[256,256]{1,0:T(8,128)(2,1)S(1)}, u32[]{:S(2)}, u32[]{:S(2)}) collective-permute-start(bf16[256,256]{1,0:T(8,128)(2,1)S(1)} %bitcast.44), channel_id=1, source_target_pairs={{0,16},{4,20},{8,24},{12,28},{16,0},{20,4},{24,8},{28,12},{1,17},{... | collective-permute-start | bytes 393224 | tf_op jit(solution)/shard_map/ppermute | solution.py:294
  167.1 8.8 %attend.4 = bf16[2,256,256]{2,1,0:T(8,128)(2,1)S(1)} custom-call(s32[3]{0:T(128)S(1)} %pad_add_fusion.place_ref, bf16[4,256,256]{2,1,0:T(8,128)(2,1)S(1)} %project.3.q_ref, bf16[4,256,256]{2,1,0:T(8,128)(2,1)S(1)} %get-tuple-element.48.k_ref, bf16[4,256,256]{2,1,0:T(8,128)(2,1)S(1)} %get-tuple-element.50.v_ref, ...), custom_call_target="tpu_custom_call" | custom-call | flops 1 | bytes 1 | tf_op jit(solution)/shard_map/attend/pallas_call | solution.py:233
  175.9 1.9 %collective-permute-start.37 = (bf16[256,256]{1,0:T(8,128)(2,1)S(1)}, bf16[256,256]{1,0:T(8,128)(2,1)S(1)}, u32[]{:S(2)}, u32[]{:S(2)}) collective-permute-start(bf16[256,256]{1,0:T(8,128)(2,1)S(1)} %get-tuple-element.74), channel_id=1, source_target_pairs={{0,8},{4,12},{8,16},{12,20},{16,24},{20,28},{24,0},{28,4},{1,9},{5... | collective-permute-start | bytes 393224 | tf_op jit(solution)/shard_map/ppermute | solution.py:294
  177.8 2.4 %collective-permute-start.38 = (bf16[256,256]{1,0:T(8,128)(2,1)S(1)}, bf16[256,256]{1,0:T(8,128)(2,1)S(1)}, u32[]{:S(2)}, u32[]{:S(2)}) collective-permute-start(bf16[256,256]{1,0:T(8,128)(2,1)S(1)} %get-tuple-element.73), channel_id=1, source_target_pairs={{0,24},{4,28},{8,0},{12,4},{16,8},{20,12},{24,16},{28,20},{1,25},{... | collective-permute-start | bytes 393224 | tf_op jit(solution)/shard_map/ppermute | solution.py:294
  180.3 2.9 %attend.5 = bf16[1,256,256]{2,1,0:T(8,128)(2,1)S(1)} custom-call(s32[3]{0:T(128)S(1)} %pad_add_fusion.place_ref, bf16[4,256,256]{2,1,0:T(8,128)(2,1)S(1)} %project.3.q_ref, bf16[4,256,256]{2,1,0:T(8,128)(2,1)S(1)} %get-tuple-element.48.k_ref, bf16[4,256,256]{2,1,0:T(8,128)(2,1)S(1)} %get-tuple-element.50.v_ref, ...), custom_call_target="tpu_custom_call" | custom-call | flops 1 | bytes 1 | tf_op jit(solution)/shard_map/attend/pallas_call | solution.py:233
  184.5 1.4 collective-permute-done.38.refs_3_
  186.6 2.0 %join.1 = bf16[256,1024]{1,0:T(8,128)(2,1)} custom-call(s32[3]{0:T(128)} %copy-done.14, bf16[256,256]{1,0:T(8,128)(2,1)} %bitcast.39, bf16[256,256]{1,0:T(8,128)(2,1)} %copy-done.32, bf16[256,256]{1,0:T(8,128)(2,1)} %copy-done.31, bf16[256,256]{1,0:T(8,128)(2,1)} %copy-done.33), custom_call_target="tpu_custom_call" | custom-call | tf_op jit(solution)/shard_map/join/pallas_call | solution.py:283
  (129 shorter events, 15.0 us)
Async XLA Ops:
  1.1 7.4 %collective-permute-start = (bf16[128,1024]{1,0:T(8,128)(2,1)S(1)}, bf16[128,1024]{1,0:T(8,128)(2,1)}, u32[]{:S(2)}, u32[]{:S(2)}) collective-permute-start(bf16[128,1024]{1,0:T(8,128)(2,1)S(1)} %fusion), channel_id=1, source_target_pairs={{0,4},{4,8},{8,12},{12,16},{16,20},{20,24},{24,28},{1,5},{5,9},{9,... | collective-permute-start | bytes 786440 | tf_op jit(solution)/shard_map/ppermute | solution.py:336
  9.7 32.8 %copy-start.30 = (bf16[512,256]{1,0:T(8,128)(2,1)S(1)}, bf16[512,256]{1,0:T(8,128)(2,1)}, u32[]{:S(2)}) copy-start(bf16[512,256]{1,0:T(8,128)(2,1)} %get-tuple-element.32) | copy-start | bytes 786436
  9.7 38.3 %copy-start.20 = (bf16[512,256]{1,0:T(8,128)(2,1)S(1)}, bf16[512,256]{1,0:T(8,128)(2,1)}, u32[]{:S(2)}) copy-start(bf16[512,256]{1,0:T(8,128)(2,1)} %get-tuple-element.58) | copy-start | bytes 786436
  9.7 38.3 %copy-start.21 = (bf16[512,256]{1,0:T(8,128)(2,1)S(1)}, bf16[512,256]{1,0:T(8,128)(2,1)}, u32[]{:S(2)}) copy-start(bf16[512,256]{1,0:T(8,128)(2,1)} %get-tuple-element.59) | copy-start | bytes 786436
  9.7 38.2 %copy-start.25 = (bf16[160,256]{1,0:T(8,128)(2,1)S(1)}, bf16[160,256]{1,0:T(8,128)(2,1)}, u32[]{:S(2)}) copy-start(bf16[160,256]{1,0:T(8,128)(2,1)} %get-tuple-element.70) | copy-start | bytes 245764
  9.7 38.2 %copy-start.26 = (bf16[160,256]{1,0:T(8,128)(2,1)S(1)}, bf16[160,256]{1,0:T(8,128)(2,1)}, u32[]{:S(2)}) copy-start(bf16[160,256]{1,0:T(8,128)(2,1)} %get-tuple-element.77) | copy-start | bytes 245764
  9.7 21.7 %collective-permute-start.4 = (bf16[1344,256]{1,0:T(8,128)(2,1)S(1)}, bf16[1344,256]{1,0:T(8,128)(2,1)S(1)}, u32[]{:S(2)}, u32[]{:S(2)}) collective-permute-start(bf16[1344,256]{1,0:T(8,128)(2,1)S(1)} %pad_maximum_fusion), channel_id=1, source_target_pairs={{0,8},{4,12},{8,16},{12,20},{16,24},{20,28},{24,0},{28,4},{1,9},{5... | collective-permute-start | bytes 2064392 | tf_op jit(solution)/shard_map/ppermute | solution.py:294
  19.2 49.0 %copy-start.5 = (bf16[512,256]{1,0:T(8,128)(2,1)S(1)}, bf16[512,256]{1,0:T(8,128)(2,1)}, u32[]{:S(2)}) copy-start(bf16[512,256]{1,0:T(8,128)(2,1)} %get-tuple-element.57.refs_0_) | copy-start | bytes 786436
  19.2 51.2 %copy-start.7 = (f32[4096]{0:T(1024)S(1)}, f32[4096]{0:T(1024)}, u32[]{:S(2)}) copy-start(f32[4096]{0:T(1024)} %param.10) | copy-start | bytes 49156
  19.2 23.2 %collective-permute-start.1 = (bf16[256,1024]{1,0:T(8,128)(2,1)S(1)}, bf16[256,1024]{1,0:T(8,128)(2,1)}, u32[]{:S(2)}, u32[]{:S(2)}) collective-permute-start(bf16[256,1024]{1,0:T(8,128)(2,1)S(1)} %hyena_filters.1.own_ref), channel_id=1, source_target_pairs={{0,8},{4,12},{8,16},{12,20},{16,24},{20,28},{24,0},{28,4},{1,9},{5... | collective-permute-start | bytes 1572872 | tf_op jit(solution)/shard_map/ppermute | solution.py:294
  31.4 13.3 %collective-permute-start.7 = (bf16[256,1024]{1,0:T(8,128)(2,1)S(1)}, bf16[256,1024]{1,0:T(8,128)(2,1)S(1)}, u32[]{:S(2)}, u32[]{:S(2)}) collective-permute-start(bf16[256,1024]{1,0:T(8,128)(2,1)S(1)} %hyena_filters.1.own_ref), channel_id=1, source_target_pairs={{0,1},{1,0},{2,3},{3,2},{4,5},{5,4},{6,7},{7,6},{8,9},{9,8},{10,11... | collective-permute-start | bytes 1572872 | tf_op jit(solution)/shard_map/ppermute | solution.py:302
  32.9 13.5 %collective-permute-start.9 = (bf16[256,1024]{1,0:T(8,128)(2,1)S(1)}, bf16[256,1024]{1,0:T(8,128)(2,1)S(1)}, u32[]{:S(2)}, u32[]{:S(2)}) collective-permute-start(bf16[256,1024]{1,0:T(8,128)(2,1)S(1)} %hyena_filters.1.own_ref), channel_id=1, source_target_pairs={{0,2},{1,3},{2,0},{3,1},{4,6},{5,7},{6,4},{7,5},{8,10},{9,11},{10,... | collective-permute-start | bytes 1572872 | tf_op jit(solution)/shard_map/ppermute | solution.py:302
  42.4 25.8 %collective-permute-start.2 = (bf16[256,1024]{1,0:T(8,128)(2,1)}, bf16[256,1024]{1,0:T(8,128)(2,1)}, u32[]{:S(2)}, u32[]{:S(2)}) collective-permute-start(bf16[256,1024]{1,0:T(8,128)(2,1)} %collective-permute-done.1.own_ref), channel_id=1, source_target_pairs={{0,8},{4,12},{8,16},{12,20},{16,24},{20,28},{24,0},{28,4},{1,9},{5... | collective-permute-start | bytes 1572872 | tf_op jit(solution)/shard_map/ppermute | solution.py:294
  42.4 21.3 %collective-permute-start.5 = (bf16[512,256]{1,0:T(8,128)(2,1)S(1)}, bf16[512,256]{1,0:T(8,128)(2,1)S(1)}, u32[]{:S(2)}, u32[]{:S(2)}) collective-permute-start(bf16[512,256]{1,0:T(8,128)(2,1)S(1)} %copy-done.30), channel_id=1, source_target_pairs={{0,8},{4,12},{8,16},{12,20},{16,24},{20,28},{24,0},{28,4},{1,9},{5... | collective-permute-start | bytes 786440 | tf_op jit(solution)/shard_map/ppermute | solution.py:294
  44.8 18.9 %collective-permute-start.8 = (bf16[128,1024]{1,0:T(8,128)(2,1)S(1)}, bf16[128,1024]{1,0:T(8,128)(2,1)S(1)}, u32[]{:S(2)}, u32[]{:S(2)}) collective-permute-start(bf16[128,1024]{1,0:T(8,128)(2,1)S(1)} %slice.50), channel_id=1, source_target_pairs={{0,2},{1,3},{2,0},{3,1},{4,6},{5,7},{6,4},{7,5},{8,10},{9,11},{10,... | collective-permute-start | bytes 786440 | tf_op jit(solution)/shard_map/ppermute | solution.py:302
  46.4 18.1 %collective-permute-start.10 = (bf16[128,1024]{1,0:T(8,128)(2,1)S(1)}, bf16[128,1024]{1,0:T(8,128)(2,1)S(1)}, u32[]{:S(2)}, u32[]{:S(2)}) collective-permute-start(bf16[128,1024]{1,0:T(8,128)(2,1)S(1)} %slice.51), channel_id=1, source_target_pairs={{0,1},{1,0},{2,3},{3,2},{4,5},{5,4},{6,7},{7,6},{8,9},{9,8},{10,11... | collective-permute-start | bytes 786440 | tf_op jit(solution)/shard_map/ppermute | solution.py:302
  48.0 28.3 %collective-permute-start.12 = (bf16[1344,256]{1,0:T(8,128)(2,1)S(1)}, bf16[1344,256]{1,0:T(8,128)(2,1)S(1)}, u32[]{:S(2)}, u32[]{:S(2)}) collective-permute-start(bf16[1344,256]{1,0:T(8,128)(2,1)S(1)} %pad_maximum_fusion.1.refs_0_), channel_id=1, source_target_pairs={{0,4},{4,0},{8,12},{12,8},{16,20},{20,16},{24,28},{28,24},{1,5},{5... | collective-permute-start | bytes 2064392 | tf_op jit(solution)/shard_map/ppermute | solution.py:298
  65.2 13.0 %collective-permute-start.11 = (bf16[256,1024]{1,0:T(8,128)(2,1)}, bf16[256,1024]{1,0:T(8,128)(2,1)S(1)}, u32[]{:S(2)}, u32[]{:S(2)}) collective-permute-start(bf16[256,1024]{1,0:T(8,128)(2,1)} %collective-permute-done.1.own_ref), channel_id=1, source_target_pairs={{0,1},{1,0},{2,3},{3,2},{4,5},{5,4},{6,7},{7,6},{8,9},{9,8},{10,11... | collective-permute-start | bytes 1572872 | tf_op jit(solution)/shard_map/ppermute | solution.py:302
  66.7 13.1 %collective-permute-start.15 = (bf16[256,1024]{1,0:T(8,128)(2,1)}, bf16[256,1024]{1,0:T(8,128)(2,1)}, u32[]{:S(2)}, u32[]{:S(2)}) collective-permute-start(bf16[256,1024]{1,0:T(8,128)(2,1)} %collective-permute-done.1.own_ref), channel_id=1, source_target_pairs={{0,2},{1,3},{2,0},{3,1},{4,6},{5,7},{6,4},{7,5},{8,10},{9,11},{10,... | collective-permute-start | bytes 1572872 | tf_op jit(solution)/shard_map/ppermute | solution.py:302
  68.2 1.7 collective-permute-start.13
  68.2 20.3 %collective-permute-start.6 = (bf16[512,256]{1,0:T(8,128)(2,1)}, bf16[512,256]{1,0:T(8,128)(2,1)}, u32[]{:S(2)}, u32[]{:S(2)}) collective-permute-start(bf16[512,256]{1,0:T(8,128)(2,1)} %get-tuple-element.33), channel_id=1, source_target_pairs={{0,24},{4,28},{8,0},{12,4},{16,8},{20,12},{24,16},{28,20},{1,25},{... | collective-permute-start | bytes 786440 | tf_op jit(solution)/shard_map/ppermute | solution.py:294
  69.8 19.9 %collective-permute-start.3 = (bf16[256,1024]{1,0:T(8,128)(2,1)}, bf16[256,1024]{1,0:T(8,128)(2,1)S(1)}, u32[]{:S(2)}, u32[]{:S(2)}) collective-permute-start(bf16[256,1024]{1,0:T(8,128)(2,1)} %collective-permute-done.2.own_ref), channel_id=1, source_target_pairs={{0,8},{4,12},{8,16},{12,20},{16,24},{20,28},{24,0},{28,4},{1,9},{5... | collective-permute-start | bytes 1572872 | tf_op jit(solution)/shard_map/ppermute | solution.py:294
  70.4 109.9 %copy-start.14 = (s32[3]{0:T(128)}, s32[3]{0:T(128)S(1)}, u32[]{:S(2)}) copy-start(s32[3]{0:T(128)S(1)} %pad_add_fusion.place_ref) | copy-start | bytes 40
  78.2 10.4 %collective-permute-start.14 = (bf16[128,1024]{1,0:T(8,128)(2,1)S(1)}, bf16[128,1024]{1,0:T(8,128)(2,1)S(1)}, u32[]{:S(2)}, u32[]{:S(2)}) collective-permute-start(bf16[128,1024]{1,0:T(8,128)(2,1)S(1)} %slice.40), channel_id=1, source_target_pairs={{0,2},{1,3},{2,0},{3,1},{4,6},{5,7},{6,4},{7,5},{8,10},{9,11},{10,... | collective-permute-start | bytes 786440 | tf_op jit(solution)/shard_map/ppermute | solution.py:302
  80.8 7.8 %collective-permute-start.16 = (bf16[128,1024]{1,0:T(8,128)(2,1)S(1)}, bf16[128,1024]{1,0:T(8,128)(2,1)S(1)}, u32[]{:S(2)}, u32[]{:S(2)}) collective-permute-start(bf16[128,1024]{1,0:T(8,128)(2,1)S(1)} %slice.41), channel_id=1, source_target_pairs={{0,1},{1,0},{2,3},{3,2},{4,5},{5,4},{6,7},{7,6},{8,9},{9,8},{10,11... | collective-permute-start | bytes 786440 | tf_op jit(solution)/shard_map/ppermute | solution.py:302
  82.3 12.5 %collective-permute-start.18 = (bf16[1344,256]{1,0:T(8,128)(2,1)S(1)}, bf16[1344,256]{1,0:T(8,128)(2,1)S(1)}, u32[]{:S(2)}, u32[]{:S(2)}) collective-permute-start(bf16[1344,256]{1,0:T(8,128)(2,1)S(1)} %collective-permute-done.4.refs_1_), channel_id=1, source_target_pairs={{0,4},{4,0},{8,12},{12,8},{16,20},{20,16},{24,28},{28,24},{1,5},{5... | collective-permute-start | bytes 2064392 | tf_op jit(solution)/shard_map/ppermute | solution.py:298
  88.5 1.5 collective-permute-start.19
  88.6 14.6 %collective-permute-start.17 = (bf16[256,1024]{1,0:T(8,128)(2,1)}, bf16[256,1024]{1,0:T(8,128)(2,1)S(1)}, u32[]{:S(2)}, u32[]{:S(2)}) collective-permute-start(bf16[256,1024]{1,0:T(8,128)(2,1)} %collective-permute-done.2.own_ref), channel_id=1, source_target_pairs={{0,1},{1,0},{2,3},{3,2},{4,5},{5,4},{6,7},{7,6},{8,9},{9,8},{10,11... | collective-permute-start | bytes 1572872 | tf_op jit(solution)/shard_map/ppermute | solution.py:302
  89.2 14.6 %collective-permute-start.21 = (bf16[256,1024]{1,0:T(8,128)(2,1)}, bf16[256,1024]{1,0:T(8,128)(2,1)S(1)}, u32[]{:S(2)}, u32[]{:S(2)}) collective-permute-start(bf16[256,1024]{1,0:T(8,128)(2,1)} %collective-permute-done.2.own_ref), channel_id=1, source_target_pairs={{0,2},{1,3},{2,0},{3,1},{4,6},{5,7},{6,4},{7,5},{8,10},{9,11},{10,... | collective-permute-start | bytes 1572872 | tf_op jit(solution)/shard_map/ppermute | solution.py:302
  89.8 32.1 %collective-permute-start.30 = (bf16[1344,256]{1,0:T(8,128)(2,1)S(1)}, bf16[1344,256]{1,0:T(8,128)(2,1)S(1)}, u32[]{:S(2)}, u32[]{:S(2)}) collective-permute-start(bf16[1344,256]{1,0:T(8,128)(2,1)S(1)} %pad_maximum_fusion.3), channel_id=1, source_target_pairs={{0,16},{4,20},{8,24},{12,28},{16,0},{20,4},{24,8},{28,12},{1,17},{... | collective-permute-start | bytes 2064392 | tf_op jit(solution)/shard_map/ppermute | solution.py:294
  90.0 32.2 %collective-permute-start.28 = (bf16[1344,256]{1,0:T(8,128)(2,1)S(1)}, bf16[1344,256]{1,0:T(8,128)(2,1)S(1)}, u32[]{:S(2)}, u32[]{:S(2)}) collective-permute-start(bf16[1344,256]{1,0:T(8,128)(2,1)S(1)} %pad_maximum_fusion.2), channel_id=1, source_target_pairs={{0,24},{4,28},{8,0},{12,4},{16,8},{20,12},{24,16},{28,20},{1,25},{... | collective-permute-start | bytes 2064392 | tf_op jit(solution)/shard_map/ppermute | solution.py:294
  103.2 8.0 %collective-permute-start.20 = (bf16[128,1024]{1,0:T(8,128)(2,1)S(1)}, bf16[128,1024]{1,0:T(8,128)(2,1)S(1)}, u32[]{:S(2)}, u32[]{:S(2)}) collective-permute-start(bf16[128,1024]{1,0:T(8,128)(2,1)S(1)} %slice.42), channel_id=1, source_target_pairs={{0,2},{1,3},{2,0},{3,1},{4,6},{5,7},{6,4},{7,5},{8,10},{9,11},{10,... | collective-permute-start | bytes 786440 | tf_op jit(solution)/shard_map/ppermute | solution.py:302
  103.8 24.7 %copy-start.29 = (bf16[512,256]{1,0:T(8,128)(2,1)S(1)}, bf16[512,256]{1,0:T(8,128)(2,1)}, u32[]{:S(2)}) copy-start(bf16[512,256]{1,0:T(8,128)(2,1)} %get-tuple-element.45) | copy-start | bytes 786436
  103.8 7.7 %collective-permute-start.22 = (bf16[128,1024]{1,0:T(8,128)(2,1)S(1)}, bf16[128,1024]{1,0:T(8,128)(2,1)S(1)}, u32[]{:S(2)}, u32[]{:S(2)}) collective-permute-start(bf16[128,1024]{1,0:T(8,128)(2,1)S(1)} %slice.43), channel_id=1, source_target_pairs={{0,1},{1,0},{2,3},{3,2},{4,5},{5,4},{6,7},{7,6},{8,9},{9,8},{10,11... | collective-permute-start | bytes 786440 | tf_op jit(solution)/shard_map/ppermute | solution.py:302
  111.5 14.1 %collective-permute-start.23 = (bf16[256,1024]{1,0:T(8,128)(2,1)S(1)}, bf16[256,1024]{1,0:T(8,128)(2,1)S(1)}, u32[]{:S(2)}, u32[]{:S(2)}) collective-permute-start(bf16[256,1024]{1,0:T(8,128)(2,1)S(1)} %collective-permute-done.3.own_ref), channel_id=1, source_target_pairs={{0,1},{1,0},{2,3},{3,2},{4,5},{5,4},{6,7},{7,6},{8,9},{9,8},{10,11... | collective-permute-start | bytes 1572872 | tf_op jit(solution)/shard_map/ppermute | solution.py:302
  112.6 13.0 %collective-permute-start.25 = (bf16[256,1024]{1,0:T(8,128)(2,1)S(1)}, bf16[256,1024]{1,0:T(8,128)(2,1)S(1)}, u32[]{:S(2)}, u32[]{:S(2)}) collective-permute-start(bf16[256,1024]{1,0:T(8,128)(2,1)S(1)} %collective-permute-done.3.own_ref), channel_id=1, source_target_pairs={{0,2},{1,3},{2,0},{3,1},{4,6},{5,7},{6,4},{7,5},{8,10},{9,11},{10,... | collective-permute-start | bytes 1572872 | tf_op jit(solution)/shard_map/ppermute | solution.py:302
  121.8 20.8 %collective-permute-start.31 = (bf16[1344,256]{1,0:T(8,128)(2,1)S(1)}, bf16[1344,256]{1,0:T(8,128)(2,1)S(1)}, u32[]{:S(2)}, u32[]{:S(2)}) collective-permute-start(bf16[1344,256]{1,0:T(8,128)(2,1)S(1)} %collective-permute-done.30.refs_2_), channel_id=1, source_target_pairs={{0,4},{4,0},{8,12},{12,8},{16,20},{20,16},{24,28},{28,24},{1,5},{5... | collective-permute-start | bytes 2064392 | tf_op jit(solution)/shard_map/ppermute | solution.py:298
  122.2 20.4 %collective-permute-start.32 = (bf16[1344,256]{1,0:T(8,128)(2,1)S(1)}, bf16[1344,256]{1,0:T(8,128)(2,1)S(1)}, u32[]{:S(2)}, u32[]{:S(2)}) collective-permute-start(bf16[1344,256]{1,0:T(8,128)(2,1)S(1)} %collective-permute-done.28.refs_3_), channel_id=1, source_target_pairs={{0,4},{4,0},{8,12},{12,8},{16,20},{20,16},{24,28},{28,24},{1,5},{5... | collective-permute-start | bytes 2064392 | tf_op jit(solution)/shard_map/ppermute | solution.py:298
  122.4 3.2 %collective-permute-start.24 = (bf16[512,256]{1,0:T(8,128)(2,1)}, bf16[512,256]{1,0:T(8,128)(2,1)S(1)}, u32[]{:S(2)}, u32[]{:S(2)}) collective-permute-start(bf16[512,256]{1,0:T(8,128)(2,1)} %collective-permute-done.6.refs_3_), channel_id=1, source_target_pairs={{0,4},{4,0},{8,12},{12,8},{16,20},{20,16},{24,28},{28,24},{1,5},{5... | collective-permute-start | bytes 786440 | tf_op jit(solution)/shard_map/ppermute | solution.py:298
  125.7 17.1 %collective-permute-start.26 = (bf16[128,1024]{1,0:T(8,128)(2,1)S(1)}, bf16[128,1024]{1,0:T(8,128)(2,1)S(1)}, u32[]{:S(2)}, u32[]{:S(2)}) collective-permute-start(bf16[128,1024]{1,0:T(8,128)(2,1)S(1)} %slice.44), channel_id=1, source_target_pairs={{0,2},{1,3},{2,0},{3,1},{4,6},{5,7},{6,4},{7,5},{8,10},{9,11},{10,... | collective-permute-start | bytes 786440 | tf_op jit(solution)/shard_map/ppermute | solution.py:302
  127.0 15.8 %collective-permute-start.27 = (bf16[128,1024]{1,0:T(8,128)(2,1)S(1)}, bf16[128,1024]{1,0:T(8,128)(2,1)S(1)}, u32[]{:S(2)}, u32[]{:S(2)}) collective-permute-start(bf16[128,1024]{1,0:T(8,128)(2,1)S(1)} %slice.45), channel_id=1, source_target_pairs={{0,1},{1,0},{2,3},{3,2},{4,5},{5,4},{6,7},{7,6},{8,9},{9,8},{10,11... | collective-permute-start | bytes 786440 | tf_op jit(solution)/shard_map/ppermute | solution.py:302
  128.5 25.7 %collective-permute-start.29 = (bf16[512,256]{1,0:T(8,128)(2,1)S(1)}, bf16[512,256]{1,0:T(8,128)(2,1)S(1)}, u32[]{:S(2)}, u32[]{:S(2)}) collective-permute-start(bf16[512,256]{1,0:T(8,128)(2,1)S(1)} %copy-done.29), channel_id=1, source_target_pairs={{0,16},{4,20},{8,24},{12,28},{16,0},{20,4},{24,8},{28,12},{1,17},{... | collective-permute-start | bytes 786440 | tf_op jit(solution)/shard_map/ppermute | solution.py:294
  150.5 9.3 %collective-permute-start.34 = (bf16[4,256,256]{2,1,0:T(8,128)(2,1)S(1)}, bf16[4,256,256]{2,1,0:T(8,128)(2,1)S(1)}, u32[]{:S(2)}, u32[]{:S(2)}) collective-permute-start(bf16[4,256,256]{2,1,0:T(8,128)(2,1)S(1)} %get-tuple-element.48.k_ref), channel_id=1, source_target_pairs={{0,4},{4,0},{8,12},{12,8},{16,20},{20,16},{24,28},{28,24},{1,5},{5... | collective-permute-start | bytes 1572872 | tf_op jit(solution)/shard_map/ppermute | solution.py:298
  150.6 9.2 %collective-permute-start.35 = (bf16[4,256,256]{2,1,0:T(8,128)(2,1)S(1)}, bf16[4,256,256]{2,1,0:T(8,128)(2,1)S(1)}, u32[]{:S(2)}, u32[]{:S(2)}) collective-permute-start(bf16[4,256,256]{2,1,0:T(8,128)(2,1)S(1)} %get-tuple-element.50.v_ref), channel_id=1, source_target_pairs={{0,4},{4,0},{8,12},{12,8},{16,20},{20,16},{24,28},{28,24},{1,5},{5... | collective-permute-start | bytes 1572872 | tf_op jit(solution)/shard_map/ppermute | solution.py:298
  154.2 1.5 collective-permute-start.33
  164.7 15.6 %collective-permute-start.36 = (bf16[256,256]{1,0:T(8,128)(2,1)S(1)}, bf16[256,256]{1,0:T(8,128)(2,1)S(1)}, u32[]{:S(2)}, u32[]{:S(2)}) collective-permute-start(bf16[256,256]{1,0:T(8,128)(2,1)S(1)} %bitcast.44), channel_id=1, source_target_pairs={{0,16},{4,20},{8,24},{12,28},{16,0},{20,4},{24,8},{28,12},{1,17},{... | collective-permute-start | bytes 393224 | tf_op jit(solution)/shard_map/ppermute | solution.py:294
  175.9 8.6 %collective-permute-start.37 = (bf16[256,256]{1,0:T(8,128)(2,1)S(1)}, bf16[256,256]{1,0:T(8,128)(2,1)S(1)}, u32[]{:S(2)}, u32[]{:S(2)}) collective-permute-start(bf16[256,256]{1,0:T(8,128)(2,1)S(1)} %get-tuple-element.74), channel_id=1, source_target_pairs={{0,8},{4,12},{8,16},{12,20},{16,24},{20,28},{24,0},{28,4},{1,9},{5... | collective-permute-start | bytes 393224 | tf_op jit(solution)/shard_map/ppermute | solution.py:294
  177.8 8.1 %collective-permute-start.38 = (bf16[256,256]{1,0:T(8,128)(2,1)S(1)}, bf16[256,256]{1,0:T(8,128)(2,1)S(1)}, u32[]{:S(2)}, u32[]{:S(2)}) collective-permute-start(bf16[256,256]{1,0:T(8,128)(2,1)S(1)} %get-tuple-element.73), channel_id=1, source_target_pairs={{0,24},{4,28},{8,0},{12,4},{16,8},{20,12},{24,16},{28,20},{1,25},{... | collective-permute-start | bytes 393224 | tf_op jit(solution)/shard_map/ppermute | solution.py:294
  (25 other events, 147.4 us)
where the time goes:
time: 189 us
  waiting for transfers between devices  75.3 us (40%)
  starting transfers between devices  53.9 us (29%)
  Pallas kernels  44.1 us (23%)
  local copies, waits for them, and re-layouts  12.2 us (6%)
  other arithmetic  2.52 us (1%)
    ppermute x12, waiting for transfers between devices, shift_z(): return lax.ppermute(value, 'seq', pairs)  54.4 us
    ppermute x12, starting transfers between devices, shift_z(): return lax.ppermute(value, 'seq', pairs)  29.6 us
    ppermute x16, starting transfers between devices, swap_chan(): return lax.ppermute(value, 'chan', [(c, c ^ bit) for c in range(4)])  20 us
    ppermute x16, waiting for transfers between devices, swap_chan(): return lax.ppermute(value, 'chan', [(c, c ^ bit) for c in range(4)])  17.7 us
    pallas_call x3, Pallas kernels, attend(): pl.pallas_call(functools.partial(attend_kernel, shifts), grid_spec=pltpu....  16.5 us
    pallas_call x4, Pallas kernels, norm(): pl.pallas_call(functools.partial(norm_kernel, half), grid=(2 * half,), in...  9.78 us
    pallas_call x2, Pallas kernels, project(): pl.pallas_call(functools.partial(project_kernel, zs, depth), grid=(zs,),...  9.76 us
    unnamed x68, local copies, waits for them, and re-layouts  6.83 us
  transfers between devices with their start and end apart: 39, of which 17 were waited for; matrix products, arithmetic and copies ran while one was open for 3% of the time, Pallas kernels for 20%

commit v1 on v0

--- a/solution.py
+++ b/solution.py
@@ -18,6 +18,10 @@
 
 
 BRIEF = pl.CostEstimate(flops=1, transcendentals=0, bytes_accessed=1)
+
+
+VMEM = pl.BlockSpec(memory_space=pltpu.VMEM)
+SMEM = pl.BlockSpec(memory_space=pltpu.SMEM)
 
 
 def whole(shape):
@@ -89,105 +93,91 @@
     )(hin, halo, filters)
 
 
-def norm_kernel(half, place_ref, own_ref, x_ref, y_ref, d0_ref, d1_ref, gain_ref, *rest):
+def norm_kernel(j, place_ref, own_ref, x_ref, y_ref, d0_ref, d1_ref, gain_ref, *rest):
     out_ref = rest[-1]
     chan = place_ref[0]
-    step = pl.program_id(0)
-    diag = jnp.where(step < half, d0_ref[...], d1_ref[...])
-    parts = [r.astype(F32) for r in (own_ref[...], x_ref[...], y_ref[...], diag)]
-    total = sum(jnp.sum(p * p, axis=-1, keepdims=True) for p in parts)
-    factor = lax.rsqrt(total / D + 1e-6)
-    for m, p in enumerate(parts):
-        where = chan ^ m
-        out_ref[0, where] = (p * factor * gain_ref[where]).astype(BF16)
+    half = d0_ref.shape[0]
+    step = 16
+
+    def band(i, diag_ref, start):
+        at = pl.ds(pl.multiple_of(start + i * step, step), step)
+        refs = (own_ref.at[at], x_ref.at[at], y_ref.at[at], diag_ref.at[pl.ds(pl.multiple_of(i * step, step), step)])
+        parts = [r[...].astype(F32) for r in refs]
+        total = sum(jnp.sum(p * p, axis=-1, keepdims=True) for p in parts)
+        factor = lax.rsqrt(total / D + 1e-6)
+        for m, p in enumerate(parts):
+            where = chan ^ m
+            out_ref[j, where, at, :] = (p * factor * gain_ref[where]).astype(BF16)
+
+    for diag_ref, start in ((d0_ref, 0), (d1_ref, half)):
+        pl.loop(0, half // step, unroll=2)(functools.partial(band, diag_ref=diag_ref, start=start))
 
 
 def norm(place, j, zs, own, from_x, from_y, diag0, diag1, gain, buffer):
     rows, width = own.shape
-    step = min(64, rows // 2)
-    half = rows // 2 // step
-    band = pl.BlockSpec((step, width), lambda i: (i, 0))
-    args = [place, own, from_x, from_y, diag0, diag1, gain]
-    specs = [
-        pl.BlockSpec(memory_space=pltpu.SMEM),
-        band,
-        band,
-        band,
-        pl.BlockSpec((step, width), lambda i: (jnp.minimum(i, half - 1), 0)),
-        pl.BlockSpec((step, width), lambda i: (jnp.maximum(i - half, 0), 0)),
-        whole((4, 1, width)),
-    ]
-    aliases = {}
-    if buffer is not None:
-        aliases = {len(args): 0}
-        args.append(buffer)
-        specs.append(pl.BlockSpec(memory_space=pl.ANY))
-    return pl.pallas_call(
-        functools.partial(norm_kernel, half),
-        grid=(2 * half,),
-        in_specs=specs,
-        out_specs=pl.BlockSpec((1, 4, step, width), lambda i: (j, 0, i, 0)),
+    args = [place, own, from_x, from_y, diag0, diag1, gain] + ([] if buffer is None else [buffer])
+    return pl.pallas_call(
+        functools.partial(norm_kernel, j),
+        in_specs=[SMEM] + [VMEM] * (len(args) - 1),
+        out_specs=VMEM,
         out_shape=jax.ShapeDtypeStruct((zs, 4, rows, width), BF16),
-        input_output_aliases=aliases,
+        input_output_aliases={} if buffer is None else {7: 0},
         compiler_params=pltpu.CompilerParams(vmem_limit_bytes=16 * MIB),
         cost_estimate=BRIEF,
         name="norm",
     )(*args)
 
 
-def project_kernel(zs, depth, place_ref, normed_ref, *refs):
-    own, sib, outs = refs[:zs], refs[zs : 2 * zs], refs[2 * zs :]
+def project_kernel(shifts, zs, count, place_ref, normed_ref, *refs):
+    n = len(shifts)
+    own, sib, rest = refs[:n], refs[n : 2 * n], refs[2 * n :]
+    before, outs = rest[:-count], rest[-count:]
     z, core = place_ref[1], place_ref[2]
+    depth = normed_ref.shape[3] // 2
     for part, out_ref in enumerate(outs):
-        total = None
-        for shift in range(zs):
-            block = lax.rem(z + zs - shift, zs)
-            for k, w_ref in enumerate((own[shift], sib[shift])):
-                at = pl.multiple_of((core ^ k) * depth, depth)
-                left = normed_ref[0, block, :, pl.ds(at, depth)]
-                right = w_ref[part * depth : (part + 1) * depth, :]
-                term = jnp.dot(left, right, preferred_element_type=F32)
-                total = term if total is None else total + term
-        out_ref[0] = total.astype(BF16)
-
-
-def project(place, normed, own, sib, count, depth):
-    zs, parts, rows, width = normed.shape
+        for j in range(zs):
+            total = before[part][j] if before else None
+            for i, shift in enumerate(shifts):
+                block = lax.rem(z + zs - shift, zs)
+                for k, w_ref in enumerate((own[i], sib[i])):
+                    at = pl.multiple_of((core ^ k) * depth, depth)
+                    left = normed_ref[j, block, :, pl.ds(at, depth)]
+                    right = w_ref[part * depth : (part + 1) * depth, :]
+                    term = jnp.dot(left, right, preferred_element_type=F32)
+                    total = term if total is None else total + term
+            out_ref[j] = total.astype(out_ref.dtype)
+
+
+def project(place, normed, own, sib, shifts, count, rounded, before=()):
+    zs, _, rows, _ = normed.shape
     cols = own[0].shape[1]
-    weights = pl.BlockSpec((count * depth, cols), lambda j: (0, 0))
-    return pl.pallas_call(
-        functools.partial(project_kernel, zs, depth),
-        grid=(zs,),
-        in_specs=[
-            pl.BlockSpec(memory_space=pltpu.SMEM),
-            pl.BlockSpec((1, parts, rows, width), lambda j: (j, 0, 0, 0)),
-        ]
-        + [weights] * (2 * zs),
-        out_specs=[pl.BlockSpec((1, rows, cols), lambda j: (j, 0, 0))] * count,
-        out_shape=[jax.ShapeDtypeStruct((zs, rows, cols), BF16)] * count,
-        compiler_params=pltpu.CompilerParams(vmem_limit_bytes=24 * MIB),
+    args = [place, normed, *own, *sib, *before]
+    return pl.pallas_call(
+        functools.partial(project_kernel, shifts, zs, count),
+        in_specs=[SMEM] + [VMEM] * (len(args) - 1),
+        out_specs=[VMEM] * count,
+        out_shape=[jax.ShapeDtypeStruct((zs, rows, cols), BF16 if rounded else F32)] * count,
+        compiler_params=pltpu.CompilerParams(vmem_limit_bytes=16 * MIB),
         cost_estimate=BRIEF,
         name="project",
-    )(place, normed, *own, *sib)
+    )(*args)
 
 
 NT = (((1,), (1,)), ((), ()))
 
 
-def attend_kernel(shifts, place_ref, q_ref, k_ref, v_ref, ks_ref, vs_ref, ck_ref, cv_ref, out_ref):
+def attend_kernel(shifts, place_ref, q_ref, k_ref, v_ref, ks_ref, vs_ref, ck_ref, cv_ref, *outs):
     z, core = place_ref[1], place_ref[2]
     zs, rows, cols = k_ref.shape
     heads = range(cols // HEAD)
     factor = 1.4426950408889634 / HEAD**0.5
-    shift = jnp.int32(shifts[0])
-    for i, s in enumerate(shifts):
-        shift = jnp.where(pl.program_id(0) == i, s, shift)
-    block = lax.rem(z + shift, zs)
     hcols = [slice(h * HEAD, (h + 1) * HEAD) for h in heads]
-    queries = [q_ref[0, :, hcol] for hcol in hcols]
-
-    def fold(state, h, key, value, mask):
-        s = lax.dot_general(queries[h], key, NT, preferred_element_type=F32)
+    row = lax.broadcasted_iota(jnp.int32, (rows, 2 * rows), 0)
+    col = lax.broadcasted_iota(jnp.int32, (rows, 2 * rows), 1)
+    visible = jnp.where(col < rows, col, jnp.where(core == 1, 0, rows)) <= row
+
+    def fold(state, query, key, value, mask):
+        s = lax.dot_general(query, key, NT, preferred_element_type=F32)
         if mask is not None:
             s = jnp.where(mask, s, -1e30)
         top = jnp.max(s, axis=-1, keepdims=True) * factor
@@ -207,42 +197,32 @@
         value = jnp.concatenate([v_ref[at, :, hcols[h]], vs_ref[at, :, hcols[h]]], axis=0)
         return key, value
 
-    def earlier(b, states):
-        return tuple(fold(states[h], h, *both(b, h), None) for h in heads)
-
-    states = tuple(fold(None, h, ck_ref[:, hcols[h]], cv_ref[:, hcols[h]], None) for h in heads)
-    states = lax.fori_loop(0, block, earlier, states)
-    row = lax.broadcasted_iota(jnp.int32, (rows, 2 * rows), 0)
-    col = lax.broadcasted_iota(jnp.int32, (rows, 2 * rows), 1)
-    visible = jnp.where(col < rows, col, jnp.where(core == 1, 0, rows)) <= row
-    for h in heads:
-        _, total, summed = fold(states[h], h, *both(block, h), visible)
-        out_ref[0, :, hcols[h]] = (summed / total).astype(BF16)
+    for shift, out_ref in zip(shifts, outs):
+        block = lax.rem(z + shift, zs)
+        mine = lax.rem(zs - shift, zs)
+        queries = [q_ref[mine, :, hcol] for hcol in hcols]
+
+        def earlier(b, states):
+            return tuple(fold(states[h], queries[h], *both(b, h), None) for h in heads)
+
+        states = tuple(fold(None, queries[h], ck_ref[:, hcols[h]], cv_ref[:, hcols[h]], None) for h in heads)
+        states = lax.fori_loop(0, block, earlier, states)
+        for h in heads:
+            _, total, summed = fold(states[h], queries[h], *both(block, h), visible)
+            out_ref[:, hcols[h]] = (summed / total).astype(BF16)
 
 
 def attend(shifts, place, q, k, v, k_sib, v_sib, ck, cv):
-    zs, rows, cols = q.shape
-
-    def slab(i, place_ref):
-        shift = jnp.int32(shifts[0])
-        for n, s in enumerate(shifts):
-            shift = jnp.where(i == n, s, shift)
-        return lax.rem(zs - shift, zs), 0, 0
-
-    args = (k, v, k_sib, v_sib, ck, cv)
+    _, rows, cols = q.shape
     return pl.pallas_call(
         functools.partial(attend_kernel, shifts),
-        grid_spec=pltpu.PrefetchScalarGridSpec(
-            num_scalar_prefetch=1,
-            grid=(len(shifts),),
-            in_specs=[pl.BlockSpec((1, rows, cols), slab)] + [whole(a.shape) for a in args],
-            out_specs=pl.BlockSpec((1, rows, cols), lambda i, place_ref: (i, 0, 0)),
-        ),
-        out_shape=jax.ShapeDtypeStruct((len(shifts), rows, cols), BF16),
-        compiler_params=pltpu.CompilerParams(vmem_limit_bytes=32 * MIB),
+        in_specs=[SMEM] + [VMEM] * 7,
+        out_specs=[VMEM] * len(shifts),
+        out_shape=[jax.ShapeDtypeStruct((rows, cols), BF16)] * len(shifts),
+        compiler_params=pltpu.CompilerParams(vmem_limit_bytes=20 * MIB),
         cost_estimate=BRIEF,
         name="attend",
-    )(place, q, *args)
+    )(place, q, k, v, k_sib, v_sib, ck, cv)
 
 
 def pack_kernel(at, crow, *refs):
@@ -258,8 +238,8 @@
     out = (len(parcels) * crow, cols)
     return pl.pallas_call(
         functools.partial(pack_kernel, at, crow),
-        in_specs=[whole(p.shape) for p in parcels],
-        out_specs=whole(out),
+        in_specs=[VMEM] * len(parcels),
+        out_specs=VMEM,
         out_shape=jax.ShapeDtypeStruct(out, BF16),
         scratch_shapes=[pltpu.VMEM(out, F32)],
         compiler_params=pltpu.CompilerParams(vmem_limit_bytes=24 * MIB),
@@ -282,7 +262,7 @@
     out = (rows, cols * len(pieces))
     return pl.pallas_call(
         join_kernel,
-        in_specs=[pl.BlockSpec(memory_space=pltpu.SMEM)] + [whole(p.shape) for p in pieces],
+        in_specs=[SMEM] + [VMEM] * len(pieces),
         out_specs=whole(out),
         out_shape=jax.ShapeDtypeStruct(out, BF16),
         name="join",
@@ -336,30 +316,29 @@
     halo = lax.ppermute(tail, "seq", [(s, s + 1) for s in range(seqs - 1)])
     halo = jnp.where(my_seq == 0, jnp.pad(prior_kv, ((taps - prior_kv.shape[0], 0), (0, 0))), halo)
 
-    order = [("kv", 1), "acts", ("q", 1), "acts", ("q", 3), "acts", ("kv", 3), ("kv", 2), ("q", 2)]
+    order = [("q", 1), ("q", 3), "acts", ("kv", 1), "acts", ("kv", 3), "acts", ("kv", 2), ("q", 2)]
     here = {(kind, 0): parcel(kind, 0) for kind in ("kv", "q")}
     acts = [hyena(hin, halo, filters)]
     sent = []
     for n, item in enumerate(order):
         value, steps = (acts[-1], 1) if item == "acts" else (parcel(*item), item[1])
-        if n == 0:
-            value = after(value, halo)
         if n >= 2:
-            value = after(value, sent[n - 1] if item == ("kv", 3) else sent[n - 2])
+            value = after(value, sent[n - 2])
         sent.append(shift_z(value, steps, zs))
         if item == "acts":
             acts.append(sent[-1])
         else:
             here[item] = sent[-1]
-    there = {item: swap_core(here[item], zs) for item in here if item != ("q", 2)}
-
-    pace = [("kv", 1), ("q", 1), ("q", 3), None]
-    swapped = [[], [("kv", 0), ("q", 0)], [("kv", 1), ("q", 1)], [("q", 3)]]
+    late = [("kv", 2), ("q", 2)]
+    there = {item: swap_core(here[item], zs) for item in here if item not in late}
+
+    pace = [[("q", 1), ("q", 3)], [], [("kv", 1)], []]
+    swapped = [[], [("kv", 0), ("q", 0)], [("q", 1), ("q", 3)], [("kv", 1)]]
     gain4 = gain.reshape(4, 1, width)
     half = rows // 2
     normed, diag0, diag1 = None, None, None
     for j, own in enumerate(acts):
-        own = after(own, *([here[pace[j]]] if pace[j] else []), *([diag0, diag1] if j else []))
+        own = after(own, *[here[item] for item in pace[j]], *([diag0, diag1] if j else []))
         from_x, from_y = swap_chan(own, 1), swap_chan(own, 2)
         if j:
             settled = [normed] + [there[item] for item in swapped[j]]
@@ -368,20 +347,25 @@
         diag1 = swap_chan(from_y[half:], 1)
         normed = norm(place, j, zs, own, from_x, from_y, diag0, diag1, gain4, normed)
 
-    mine = [here["kv", r] for r in range(zs)]
-    theirs = [there["kv", r] for r in range(zs)]
+    def sides(kind, shifts):
+        return [[side[kind, r] for r in shifts] for side in (here, there)]
+
+    every = tuple(range(zs))
+    early = tuple(r for r in every if r != 2)
+    (q_early,) = project(place, normed, *sides("q", early), early, 1, False)
+    there["kv", 2] = swap_core(after(here["kv", 2], diag0, diag1), zs)
+    mine, theirs = sides("kv", every)
     ck, cv = [pack(mine + theirs, 2 * depth + i * (crow + PAD), crow) for i in range(2)]
-    k, v = project(place, after(normed, ck, cv), mine, theirs, 2, depth)
+    k, v = project(place, after(normed, ck, cv, q_early), mine, theirs, every, 2, True)
     k_sib, v_sib = swap_core(k, zs), swap_core(v, zs)
     there["q", 2] = swap_core(after(here["q", 2], k), zs)
-    queries = [[side["q", r] for r in range(zs)] for side in (here, there)]
-    (q,) = project(place, normed, *queries, 1, depth)
+    (q,) = project(place, normed, *sides("q", (2,)), (2,), 1, True, (q_early,))
     pieces, out = {}, None
     for shifts, wait in (((2,), ()), ((1, 3), ()), ((0,), (2,))):
-        ready = q if out is None else after(q, out, *[pieces[r] for r in wait])
+        ready = q if out is None else after(q, out[0], *[pieces[r] for r in wait])
         out = attend(shifts, place, ready, k, v, k_sib, v_sib, ck, cv)
-        for i, r in enumerate(shifts):
-            pieces[r] = shift_z(out[i], r, zs) if r else out[i]
+        for r, piece in zip(shifts, out):
+            pieces[r] = shift_z(piece, r, zs) if r else piece
     return join(place, [pieces[r] for r in range(zs)])
 
 

time: 189 us -> 189 us (level)
  waiting for transfers between devices: 75.3 us -> 90.4 us
  starting transfers between devices: 53.9 us -> 40.6 us
  Pallas kernels: 44.1 us -> 42.1 us
    ppermute x12, waiting for transfers between devices: 54.4 us -> 72 us  [shift_z(): return lax.ppermute(value, 'seq', pairs)]
    ppermute x12, starting transfers between devices: 29.6 us -> 16.2 us  [shift_z(): return lax.ppermute(value, 'seq', pairs)]
    pallas_call x12 -> x13, Pallas kernels: 38.1 us -> 36.1 us  [the longest x3 16.5 us: attend(): pl.pallas_call(functools.partial(attend_kernel, shifts), in_specs=[SMEM]...]
    unnamed x68 -> x74, local copies, waits for them, and re-layouts: 6.83 us -> 7.49 us
  transfers between devices with their start and end apart: 39 -> 39, of which waited for: 17 -> 17; matrix products, arithmetic and copies ran while one was open for 3% -> 4% of each run, Pallas kernels for 20% -> 19%
where the time goes in v1:
time: 189 us
  waiting for transfers between devices  90.4 us (48%)
  Pallas kernels  42.1 us (22%)
  starting transfers between devices  40.6 us (21%)
  local copies, waits for them, and re-layouts  12.9 us (7%)
  other arithmetic  2.34 us (1%)
    ppermute x12, waiting for transfers between devices, shift_z(): return lax.ppermute(value, 'seq', pairs)  72 us
    ppermute x16, starting transfers between devices, swap_chan(): return lax.ppermute(value, 'chan', [(c, c ^ bit) for c in range(4)])  20.1 us
    pallas_call x3, Pallas kernels, attend(): pl.pallas_call(functools.partial(attend_kernel, shifts), in_specs=[SMEM]...  16.5 us
    ppermute x12, starting transfers between devices, shift_z(): return lax.ppermute(value, 'seq', pairs)  16.2 us
    ppermute x16, waiting for transfers between devices, swap_chan(): return lax.ppermute(value, 'chan', [(c, c ^ bit) for c in range(4)])  16 us
    pallas_call x4, Pallas kernels, norm(): pl.pallas_call(functools.partial(norm_kernel, j), in_specs=[SMEM] + [VMEM...  8.78 us
    pallas_call x3, Pallas kernels, project(): pl.pallas_call(functools.partial(project_kernel, shifts, zs, count), in_s...  8.7 us
    unnamed x74, local copies, waits for them, and re-layouts  7.49 us
  transfers between devices with their start and end apart: 39, of which 17 were waited for; matrix products, arithmetic and copies ran while one was open for 4% of the time, Pallas kernels for 19%

profile of v1, /device:TPU:0, one launch (start us, length us, event | category | flops | bytes accessed | tf_op | source)
XLA Modules:
  0.0 188.9 jit_solution(5416898212385400508)
XLA Ops:
  0.0 1.1 fusion
  1.1 2.4 %collective-permute-start = (bf16[128,1024]{1,0:T(8,128)(2,1)S(1)}, bf16[128,1024]{1,0:T(8,128)(2,1)S(1)}, u32[]{:S(2)}, u32[]{:S(2)}) collective-permute-start(bf16[128,1024]{1,0:T(8,128)(2,1)S(1)} %fusion), channel_id=1, source_target_pairs={{0,4},{4,8},{8,12},{12,16},{16,20},{20,24},{24,28},{1,5},{5,9},{9,... | collective-permute-start | bytes 786440 | tf_op jit(solution)/shard_map/ppermute | solution.py:316
  3.6 3.6 %dynamic-slice_bitcast_fusion.1 = (bf16[512,256]{1,0:T(8,128)(2,1)}, bf16[512,256]{1,0:T(8,128)(2,1)}, bf16[512,256]{1,0:T(8,128)(2,1)}, bf16[512,256]{1,0:T(8,1...) fusion(bf16[512,3,1024]{2,0,1:T(8,128)(2,1)} %param.11, ...), kind=kLoop, calls=%fused_computation.7 | loop fusion | bytes 6291472 | tf_op jit(solution)/shard_map/squeeze | solution.py:307
  7.2 2.6 %collective-permute-start.1 = (bf16[512,256]{1,0:T(8,128)(2,1)}, bf16[512,256]{1,0:T(8,128)(2,1)S(1)}, u32[]{:S(2)}, u32[]{:S(2)}) collective-permute-start(bf16[512,256]{1,0:T(8,128)(2,1)} %get-tuple-element.67), channel_id=1, source_target_pairs={{0,8},{4,12},{8,16},{12,20},{16,24},{20,28},{24,0},{28,4},{1,9},{5... | collective-permute-start | bytes 786440 | tf_op jit(solution)/shard_map/ppermute | solution.py:274
  9.8 2.1 %collective-permute-start.5 = (bf16[512,256]{1,0:T(8,128)(2,1)}, bf16[512,256]{1,0:T(8,128)(2,1)S(1)}, u32[]{:S(2)}, u32[]{:S(2)}) collective-permute-start(bf16[512,256]{1,0:T(8,128)(2,1)} %get-tuple-element.64), channel_id=1, source_target_pairs={{0,24},{4,28},{8,0},{12,4},{16,8},{20,12},{24,16},{28,20},{1,25},{... | collective-permute-start | bytes 786440 | tf_op jit(solution)/shard_map/ppermute | solution.py:274
  12.0 6.0 %hyena_filters.1.own_ref = bf16[256,1024]{1,0:T(8,128)(2,1)S(1)} custom-call(bf16[3,256,1024]{2,1,0:T(8,128)(2,1)S(1)} %bitcast.32, bf16[128,1024]{1,0:T(8,128)(2,1)S(1)} %pad_select_fusion.halo_ref, f32[64,128]{1,0:T(8,128)S(1)} %copy-done.18), custom_call_target="tpu_custom_call" | custom-call | flops 1 | bytes 1 | tf_op jit(solution)/shard_map/hyena_filters/pallas_call | solution.py:80
  18.4 6.2 %collective-permute-done.5.refs_2_ = bf16[512,256]{1,0:T(8,128)(2,1)S(1)} collective-permute-done((bf16[512,256]{1,0:T(8,128)(2,1)}, bf16[512,256]{1,0:T(8,128)(2,1)S(1)}, u32[]{:S(2)}, u32[]{:S(2)}) %collective-permute-start.5) | collective-permute-done | bytes 262176 | tf_op jit(solution)/shard_map/ppermute | solution.py:274
  24.7 1.5 collective-permute-start.9
  26.1 1.5 collective-permute-start.7
  29.0 9.6 %collective-permute-done.9.y_ref = bf16[256,1024]{1,0:T(8,128)(2,1)S(1)} collective-permute-done((bf16[256,1024]{1,0:T(8,128)(2,1)S(1)}, bf16[256,1024]{1,0:T(8,128)(2,1)S(1)}, u32[]{:S(2)}, u32[]{:S(2)}) %collective-permute-start.9) | collective-permute-done | bytes 524320 | tf_op jit(solution)/shard_map/ppermute | solution.py:282
  38.6 1.5 collective-permute-start.10
  40.2 1.6 collective-permute-start.8
  42.9 3.4 %collective-permute-done.10.d1_ref = bf16[128,1024]{1,0:T(8,128)(2,1)S(1)} collective-permute-done((bf16[128,1024]{1,0:T(8,128)(2,1)S(1)}, bf16[128,1024]{1,0:T(8,128)(2,1)S(1)}, u32[]{:S(2)}, u32[]{:S(2)}) %collective-permute-start.10) | collective-permute-done | bytes 262176 | tf_op jit(solution)/shard_map/ppermute | solution.py:282
  48.2 1.5 collective-permute-start.15
  52.9 1.6 collective-permute-start.3
  54.7 1.0 copy-done.2
  55.7 1.0 copy-done.4
  58.7 1.9 %norm.4.rest_0_ = bf16[4,4,256,1024]{3,2,1,0:T(8,128)(2,1)S(1)} custom-call(s32[3]{0:T(128)S(1)} %pad_add_fusion.place_ref, bf16[256,1024]{1,0:T(8,128)(2,1)S(1)} %hyena_filters.1.own_ref, bf16[256,1024]{1,0:T(8,128)(2,1)S(1)} %copy-done.4, bf16[256,1024]{1,0:T(8,128)(2,1)S(1)} %copy-done.2, bf16[128,1024]{1,0:T(8,128)(2,1)S(1)} %copy-done.16, ...), custom_call_target="tpu_custom_call" | custom-call | flops 1 | bytes 1 | tf_op jit(solution)/shard_map/norm/pallas_call | solution.py:119
  60.6 1.2 collective-permute-start.16
  61.8 1.0 slice.34
  62.8 1.5 collective-permute-start.14
  64.3 7.7 %collective-permute-done.6.refs_1_ = bf16[1344,256]{1,0:T(8,128)(2,1)S(1)} collective-permute-done((bf16[1344,256]{1,0:T(8,128)(2,1)}, bf16[1344,256]{1,0:T(8,128)(2,1)S(1)}, u32[]{:S(2)}, u32[]{:S(2)}) %collective-permute-start.6) | collective-permute-done | bytes 688160 | tf_op jit(solution)/shard_map/ppermute | solution.py:274
  72.0 8.2 %collective-permute-done.3.own_ref = bf16[256,1024]{1,0:T(8,128)(2,1)} collective-permute-done((bf16[256,1024]{1,0:T(8,128)(2,1)}, bf16[256,1024]{1,0:T(8,128)(2,1)}, u32[]{:S(2)}, u32[]{:S(2)}) %collective-permute-start.3) | collective-permute-done | bytes 524320 | tf_op jit(solution)/shard_map/ppermute | solution.py:274
  83.1 3.1 %collective-permute-start.29 = (bf16[1344,256]{1,0:T(8,128)(2,1)S(1)}, bf16[1344,256]{1,0:T(8,128)(2,1)S(1)}, u32[]{:S(2)}, u32[]{:S(2)}) collective-permute-start(bf16[1344,256]{1,0:T(8,128)(2,1)S(1)} %pad_maximum_fusion.3), channel_id=1, source_target_pairs={{0,24},{4,28},{8,0},{12,4},{16,8},{20,12},{24,16},{28,20},{1,25},{... | collective-permute-start | bytes 2064392 | tf_op jit(solution)/shard_map/ppermute | solution.py:274
  86.2 2.6 %norm.5.rest_0_ = bf16[4,4,256,1024]{3,2,1,0:T(8,128)(2,1)S(1)} custom-call(s32[3]{0:T(128)S(1)} %pad_add_fusion.place_ref, bf16[256,1024]{1,0:T(8,128)(2,1)} %collective-permute-done.2.own_ref, bf16[256,1024]{1,0:T(8,128)(2,1)} %collective-permute-done.11.x_ref, ...), custom_call_target="tpu_custom_call", output_to_operand_aliasing={{}: (7, {})} | custom-call | flops 1 | bytes 1 | tf_op jit(solution)/shard_map/norm/pallas_call | solution.py:119
  88.8 2.4 %collective-permute-done.21.y_ref = bf16[256,1024]{1,0:T(8,128)(2,1)S(1)} collective-permute-done((bf16[256,1024]{1,0:T(8,128)(2,1)}, bf16[256,1024]{1,0:T(8,128)(2,1)S(1)}, u32[]{:S(2)}, u32[]{:S(2)}) %collective-permute-start.21) | collective-permute-done | bytes 524320 | tf_op jit(solution)/shard_map/ppermute | solution.py:282
  91.9 1.5 collective-permute-start.20
  93.4 5.5 %collective-permute-done.4.own_ref = bf16[256,1024]{1,0:T(8,128)(2,1)S(1)} collective-permute-done((bf16[256,1024]{1,0:T(8,128)(2,1)}, bf16[256,1024]{1,0:T(8,128)(2,1)S(1)}, u32[]{:S(2)}, u32[]{:S(2)}) %collective-permute-start.4) | collective-permute-done | bytes 524320 | tf_op jit(solution)/shard_map/ppermute | solution.py:274
  98.9 1.5 collective-permute-start.25
  100.4 1.2 collective-permute-start.23
  101.7 10.1 %collective-permute-done.29.refs_3_ = bf16[1344,256]{1,0:T(8,128)(2,1)S(1)} collective-permute-done((bf16[1344,256]{1,0:T(8,128)(2,1)S(1)}, bf16[1344,256]{1,0:T(8,128)(2,1)S(1)}, u32[]{:S(2)}, u32[]{:S(2)}) %collective-permute-start.29) | collective-permute-done | bytes 688160 | tf_op jit(solution)/shard_map/ppermute | solution.py:274
  111.8 1.5 collective-permute-start.30
  113.3 2.4 %norm.6.rest_0_ = bf16[4,4,256,1024]{3,2,1,0:T(8,128)(2,1)S(1)} custom-call(s32[3]{0:T(128)S(1)} %pad_add_fusion.place_ref, bf16[256,1024]{1,0:T(8,128)(2,1)} %collective-permute-done.3.own_ref, bf16[256,1024]{1,0:T(8,128)(2,1)S(1)} %collective-permute-done.17.x_ref, ...), custom_call_target="tpu_custom_call", output_to_operand_aliasing={{}: (7, {})} | custom-call | flops 1 | bytes 1 | tf_op jit(solution)/shard_map/norm/pallas_call | solution.py:119
  115.8 1.2 collective-permute-start.27
  117.1 1.6 collective-permute-start.26
  118.7 24.9 %collective-permute-done.30.refs_2_ = bf16[1344,256]{1,0:T(8,128)(2,1)S(1)} collective-permute-done((bf16[1344,256]{1,0:T(8,128)(2,1)S(1)}, bf16[1344,256]{1,0:T(8,128)(2,1)S(1)}, u32[]{:S(2)}, u32[]{:S(2)}) %collective-permute-start.30) | collective-permute-done | bytes 688160 | tf_op jit(solution)/shard_map/ppermute | solution.py:274
  143.6 1.9 %norm.7.normed_ref = bf16[4,4,256,1024]{3,2,1,0:T(8,128)(2,1)S(1)} custom-call(s32[3]{0:T(128)S(1)} %pad_add_fusion.place_ref, bf16[256,1024]{1,0:T(8,128)(2,1)S(1)} %collective-permute-done.4.own_ref, bf16[256,1024]{1,0:T(8,128)(2,1)S(1)} %collective-permute-done.23.x_ref, ...), custom_call_target="tpu_custom_call", output_to_operand_aliasing={{}: (7, {})} | custom-call | flops 1 | bytes 1 | tf_op jit(solution)/shard_map/norm/pallas_call | solution.py:119
  145.6 2.3 %project.3.refs_2_ = f32[4,256,256]{2,1,0:T(8,128)S(1)} custom-call(s32[3]{0:T(128)S(1)} %pad_add_fusion.place_ref, bf16[4,4,256,1024]{3,2,1,0:T(8,128)(2,1)S(1)} %norm.7.normed_ref, bf16[512,256]{1,0:T(8,128)(2,1)S(1)} %get-tuple-element.61.refs_0_, bf16[512,256]{1,0:T(8,128)(2,1)S(1)} %copy-done.8, bf16[512,256]{1,0:T(8,128)(2,1)S(1)} %copy-done.10, ...), custom_call_target="tpu_custom_call" | custom-call | flops 1 | bytes 1 | tf_op jit(solution)/shard_map/project/pallas_call | solution.py:155
  148.1 5.1 %project.4 = (bf16[4,256,256]{2,1,0:T(8,128)(2,1)S(1)}, bf16[4,256,256]{2,1,0:T(8,128)(2,1)S(1)}) custom-call(s32[3]{0:T(128)S(1)} %pad_add_fusion.place_ref, bf16[4,4,256,1024]{3,2,1,0:T(8,128)(2,1)S(1)} %norm.7.normed_ref, bf16[1344,256]{1,0:T(8,128)(2,1)S(1)} %pad_maximum_fusion.1.refs_0_, bf16[1344,256]{1,0:T(8,128)(2,1)S(1)} %collective-permute-done.6.refs_1_, ...), custom_call_target="tpu_custom_call" | custom-call | flops 1 | bytes 1 | tf_op jit(solution)/shard_map/project/pallas_call | solution.py:155
  153.9 6.2 %collective-permute-done.28.refs_0_ = bf16[512,256]{1,0:T(8,128)(2,1)S(1)} collective-permute-done((bf16[512,256]{1,0:T(8,128)(2,1)S(1)}, bf16[512,256]{1,0:T(8,128)(2,1)S(1)}, u32[]{:S(2)}, u32[]{:S(2)}) %collective-permute-start.28) | collective-permute-done | bytes 262176 | tf_op jit(solution)/shard_map/ppermute | solution.py:274
  160.2 1.5 collective-permute-done.33.refs_1_
  161.7 1.3 project.5.q_ref
  163.0 4.7 %attend.3 = bf16[256,256]{1,0:T(8,128)(2,1)S(1)} custom-call(s32[3]{0:T(128)S(1)} %pad_add_fusion.place_ref, bf16[4,256,256]{2,1,0:T(8,128)(2,1)S(1)} %project.5.q_ref, bf16[4,256,256]{2,1,0:T(8,128)(2,1)S(1)} %get-tuple-element.50.k_ref, bf16[4,256,256]{2,1,0:T(8,128)(2,1)S(1)} %get-tuple-element.52.v_ref, ...), custom_call_target="tpu_custom_call" | custom-call | flops 1 | bytes 1 | tf_op jit(solution)/shard_map/attend/pallas_call | solution.py:217
  167.7 9.0 %attend.4 = (bf16[256,256]{1,0:T(8,128)(2,1)S(1)}, bf16[256,256]{1,0:T(8,128)(2,1)S(1)}) custom-call(s32[3]{0:T(128)S(1)} %pad_add_fusion.place_ref, bf16[4,256,256]{2,1,0:T(8,128)(2,1)S(1)} %project.5.q_ref, bf16[4,256,256]{2,1,0:T(8,128)(2,1)S(1)} %get-tuple-element.50.k_ref, bf16[4,256,256]{2,1,0:T(8,128)(2,1)S(1)} %get-tuple-element.52.v_ref, ...), custom_call_target="tpu_custom_call" | custom-call | flops 1 | bytes 1 | tf_op jit(solution)/shard_map/attend/pallas_call | solution.py:217
  176.8 3.8 %collective-permute-start.38 = (bf16[256,256]{1,0:T(8,128)(2,1)S(1)}, bf16[256,256]{1,0:T(8,128)(2,1)S(1)}, u32[]{:S(2)}, u32[]{:S(2)}) collective-permute-start(bf16[256,256]{1,0:T(8,128)(2,1)S(1)} %get-tuple-element.56), channel_id=1, source_target_pairs={{0,24},{4,28},{8,0},{12,4},{16,8},{20,12},{24,16},{28,20},{1,25},{... | collective-permute-start | bytes 393224 | tf_op jit(solution)/shard_map/ppermute | solution.py:274
  180.6 2.9 %attend.5.refs_0_ = bf16[256,256]{1,0:T(8,128)(2,1)S(1)} custom-call(s32[3]{0:T(128)S(1)} %pad_add_fusion.place_ref, bf16[4,256,256]{2,1,0:T(8,128)(2,1)S(1)} %project.5.q_ref, bf16[4,256,256]{2,1,0:T(8,128)(2,1)S(1)} %get-tuple-element.50.k_ref, bf16[4,256,256]{2,1,0:T(8,128)(2,1)S(1)} %get-tuple-element.52.v_ref, ...), custom_call_target="tpu_custom_call" | custom-call | flops 1 | bytes 1 | tf_op jit(solution)/shard_map/attend/pallas_call | solution.py:217
  184.9 1.4 collective-permute-done.38.refs_3_
  186.9 2.0 %join.1 = bf16[256,1024]{1,0:T(8,128)(2,1)} custom-call(s32[3]{0:T(128)} %copy-done.17, bf16[256,256]{1,0:T(8,128)(2,1)} %copy-done.5, bf16[256,256]{1,0:T(8,128)(2,1)} %copy-done.35, bf16[256,256]{1,0:T(8,128)(2,1)} %copy-done.34, bf16[256,256]{1,0:T(8,128)(2,1)} %copy-done.36), custom_call_target="tpu_custom_call" | custom-call | tf_op jit(solution)/shard_map/join/pallas_call | solution.py:263
  (135 shorter events, 17.0 us)
Async XLA Ops:
  1.1 10.8 %collective-permute-start = (bf16[128,1024]{1,0:T(8,128)(2,1)S(1)}, bf16[128,1024]{1,0:T(8,128)(2,1)S(1)}, u32[]{:S(2)}, u32[]{:S(2)}) collective-permute-start(bf16[128,1024]{1,0:T(8,128)(2,1)S(1)} %fusion), channel_id=1, source_target_pairs={{0,4},{4,8},{8,12},{12,16},{16,20},{20,24},{24,28},{1,5},{5,9},{9,... | collective-permute-start | bytes 786440 | tf_op jit(solution)/shard_map/ppermute | solution.py:316
  7.2 11.2 %collective-permute-start.1 = (bf16[512,256]{1,0:T(8,128)(2,1)}, bf16[512,256]{1,0:T(8,128)(2,1)S(1)}, u32[]{:S(2)}, u32[]{:S(2)}) collective-permute-start(bf16[512,256]{1,0:T(8,128)(2,1)} %get-tuple-element.67), channel_id=1, source_target_pairs={{0,8},{4,12},{8,16},{12,20},{16,24},{20,28},{24,0},{28,4},{1,9},{5... | collective-permute-start | bytes 786440 | tf_op jit(solution)/shard_map/ppermute | solution.py:274
  9.8 14.9 %collective-permute-start.5 = (bf16[512,256]{1,0:T(8,128)(2,1)}, bf16[512,256]{1,0:T(8,128)(2,1)S(1)}, u32[]{:S(2)}, u32[]{:S(2)}) collective-permute-start(bf16[512,256]{1,0:T(8,128)(2,1)} %get-tuple-element.64), channel_id=1, source_target_pairs={{0,24},{4,28},{8,0},{12,4},{16,8},{20,12},{24,16},{28,20},{1,25},{... | collective-permute-start | bytes 786440 | tf_op jit(solution)/shard_map/ppermute | solution.py:274
  18.0 23.7 %copy-start.25 = (bf16[512,256]{1,0:T(8,128)(2,1)S(1)}, bf16[512,256]{1,0:T(8,128)(2,1)}, u32[]{:S(2)}) copy-start(bf16[512,256]{1,0:T(8,128)(2,1)} %get-tuple-element.62) | copy-start | bytes 786436
  18.0 23.7 %copy-start.26 = (bf16[512,256]{1,0:T(8,128)(2,1)S(1)}, bf16[512,256]{1,0:T(8,128)(2,1)}, u32[]{:S(2)}) copy-start(bf16[512,256]{1,0:T(8,128)(2,1)} %get-tuple-element.63) | copy-start | bytes 786436
  18.4 23.4 %copy-start.7 = (bf16[512,256]{1,0:T(8,128)(2,1)}, bf16[512,256]{1,0:T(8,128)(2,1)S(1)}, u32[]{:S(2)}) copy-start(bf16[512,256]{1,0:T(8,128)(2,1)S(1)} %collective-permute-done.1.refs_1_) | copy-start | bytes 786436
  24.7 13.9 %collective-permute-start.9 = (bf16[256,1024]{1,0:T(8,128)(2,1)S(1)}, bf16[256,1024]{1,0:T(8,128)(2,1)S(1)}, u32[]{:S(2)}, u32[]{:S(2)}) collective-permute-start(bf16[256,1024]{1,0:T(8,128)(2,1)S(1)} %hyena_filters.1.own_ref), channel_id=1, source_target_pairs={{0,2},{1,3},{2,0},{3,1},{4,6},{5,7},{6,4},{7,5},{8,10},{9,11},{10,... | collective-permute-start | bytes 1572872 | tf_op jit(solution)/shard_map/ppermute | solution.py:282
  26.1 14.0 %collective-permute-start.7 = (bf16[256,1024]{1,0:T(8,128)(2,1)S(1)}, bf16[256,1024]{1,0:T(8,128)(2,1)S(1)}, u32[]{:S(2)}, u32[]{:S(2)}) collective-permute-start(bf16[256,1024]{1,0:T(8,128)(2,1)S(1)} %hyena_filters.1.own_ref), channel_id=1, source_target_pairs={{0,1},{1,0},{2,3},{3,2},{4,5},{5,4},{6,7},{7,6},{8,9},{9,8},{10,11... | collective-permute-start | bytes 1572872 | tf_op jit(solution)/shard_map/ppermute | solution.py:282
  27.6 15.3 %collective-permute-start.2 = (bf16[256,1024]{1,0:T(8,128)(2,1)S(1)}, bf16[256,1024]{1,0:T(8,128)(2,1)}, u32[]{:S(2)}, u32[]{:S(2)}) collective-permute-start(bf16[256,1024]{1,0:T(8,128)(2,1)S(1)} %hyena_filters.1.own_ref), channel_id=1, source_target_pairs={{0,8},{4,12},{8,16},{12,20},{16,24},{20,28},{24,0},{28,4},{1,9},{5... | collective-permute-start | bytes 1572872 | tf_op jit(solution)/shard_map/ppermute | solution.py:274
  38.6 7.7 %collective-permute-start.10 = (bf16[128,1024]{1,0:T(8,128)(2,1)S(1)}, bf16[128,1024]{1,0:T(8,128)(2,1)S(1)}, u32[]{:S(2)}, u32[]{:S(2)}) collective-permute-start(bf16[128,1024]{1,0:T(8,128)(2,1)S(1)} %slice.43), channel_id=1, source_target_pairs={{0,1},{1,0},{2,3},{3,2},{4,5},{5,4},{6,7},{7,6},{8,9},{9,8},{10,11... | collective-permute-start | bytes 786440 | tf_op jit(solution)/shard_map/ppermute | solution.py:282
  40.2 7.4 %collective-permute-start.8 = (bf16[128,1024]{1,0:T(8,128)(2,1)S(1)}, bf16[128,1024]{1,0:T(8,128)(2,1)S(1)}, u32[]{:S(2)}, u32[]{:S(2)}) collective-permute-start(bf16[128,1024]{1,0:T(8,128)(2,1)S(1)} %slice.42), channel_id=1, source_target_pairs={{0,2},{1,3},{2,0},{3,1},{4,6},{5,7},{6,4},{7,5},{8,10},{9,11},{10,... | collective-permute-start | bytes 786440 | tf_op jit(solution)/shard_map/ppermute | solution.py:282
  41.9 18.7 %collective-permute-start.12 = (bf16[1344,256]{1,0:T(8,128)(2,1)S(1)}, bf16[1344,256]{1,0:T(8,128)(2,1)S(1)}, u32[]{:S(2)}, u32[]{:S(2)}) collective-permute-start(bf16[1344,256]{1,0:T(8,128)(2,1)S(1)} %pad_maximum_fusion.1.refs_0_), channel_id=1, source_target_pairs={{0,4},{4,0},{8,12},{12,8},{16,20},{20,16},{24,28},{28,24},{1,5},{5... | collective-permute-start | bytes 2064392 | tf_op jit(solution)/shard_map/ppermute | solution.py:278
  41.9 10.3 %collective-permute-start.13 = (bf16[512,256]{1,0:T(8,128)(2,1)S(1)}, bf16[512,256]{1,0:T(8,128)(2,1)S(1)}, u32[]{:S(2)}, u32[]{:S(2)}) collective-permute-start(bf16[512,256]{1,0:T(8,128)(2,1)S(1)} %get-tuple-element.61.refs_0_), channel_id=1, source_target_pairs={{0,4},{4,0},{8,12},{12,8},{16,20},{20,16},{24,28},{28,24},{1,5},{5... | collective-permute-start | bytes 786440 | tf_op jit(solution)/shard_map/ppermute | solution.py:278
  48.2 12.3 %collective-permute-start.15 = (bf16[256,1024]{1,0:T(8,128)(2,1)}, bf16[256,1024]{1,0:T(8,128)(2,1)S(1)}, u32[]{:S(2)}, u32[]{:S(2)}) collective-permute-start(bf16[256,1024]{1,0:T(8,128)(2,1)} %collective-permute-done.2.own_ref), channel_id=1, source_target_pairs={{0,2},{1,3},{2,0},{3,1},{4,6},{5,7},{6,4},{7,5},{8,10},{9,11},{10,... | collective-permute-start | bytes 1572872 | tf_op jit(solution)/shard_map/ppermute | solution.py:282
  49.8 12.1 %collective-permute-start.11 = (bf16[256,1024]{1,0:T(8,128)(2,1)}, bf16[256,1024]{1,0:T(8,128)(2,1)}, u32[]{:S(2)}, u32[]{:S(2)}) collective-permute-start(bf16[256,1024]{1,0:T(8,128)(2,1)} %collective-permute-done.2.own_ref), channel_id=1, source_target_pairs={{0,1},{1,0},{2,3},{3,2},{4,5},{5,4},{6,7},{7,6},{8,9},{9,8},{10,11... | collective-permute-start | bytes 1572872 | tf_op jit(solution)/shard_map/ppermute | solution.py:282
  51.6 20.4 %collective-permute-start.6 = (bf16[1344,256]{1,0:T(8,128)(2,1)}, bf16[1344,256]{1,0:T(8,128)(2,1)S(1)}, u32[]{:S(2)}, u32[]{:S(2)}) collective-permute-start(bf16[1344,256]{1,0:T(8,128)(2,1)} %pad_maximum_fusion), channel_id=1, source_target_pairs={{0,8},{4,12},{8,16},{12,20},{16,24},{20,28},{24,0},{28,4},{1,9},{5... | collective-permute-start | bytes 2064392 | tf_op jit(solution)/shard_map/ppermute | solution.py:274
  52.9 27.3 %collective-permute-start.3 = (bf16[256,1024]{1,0:T(8,128)(2,1)}, bf16[256,1024]{1,0:T(8,128)(2,1)}, u32[]{:S(2)}, u32[]{:S(2)}) collective-permute-start(bf16[256,1024]{1,0:T(8,128)(2,1)} %collective-permute-done.2.own_ref), channel_id=1, source_target_pairs={{0,8},{4,12},{8,16},{12,20},{16,24},{20,28},{24,0},{28,4},{1,9},{5... | collective-permute-start | bytes 1572872 | tf_op jit(solution)/shard_map/ppermute | solution.py:274
  54.6 125.9 %copy-start.17 = (s32[3]{0:T(128)}, s32[3]{0:T(128)S(1)}, u32[]{:S(2)}) copy-start(s32[3]{0:T(128)S(1)} %pad_add_fusion.place_ref) | copy-start | bytes 40
  58.6 22.9 %copy-start.10 = (bf16[512,256]{1,0:T(8,128)(2,1)S(1)}, bf16[512,256]{1,0:T(8,128)(2,1)}, u32[]{:S(2)}) copy-start(bf16[512,256]{1,0:T(8,128)(2,1)} %copy-done.9) | copy-start | bytes 786436
  58.6 23.4 %copy-start.21 = (bf16[512,256]{1,0:T(8,128)(2,1)S(1)}, bf16[512,256]{1,0:T(8,128)(2,1)}, u32[]{:S(2)}) copy-start(bf16[512,256]{1,0:T(8,128)(2,1)} %get-tuple-element.57) | copy-start | bytes 786436
  58.6 23.4 %copy-start.22 = (bf16[512,256]{1,0:T(8,128)(2,1)S(1)}, bf16[512,256]{1,0:T(8,128)(2,1)}, u32[]{:S(2)}) copy-start(bf16[512,256]{1,0:T(8,128)(2,1)} %get-tuple-element.68) | copy-start | bytes 786436
  58.6 23.4 %copy-start.28 = (bf16[160,256]{1,0:T(8,128)(2,1)S(1)}, bf16[160,256]{1,0:T(8,128)(2,1)}, u32[]{:S(2)}) copy-start(bf16[160,256]{1,0:T(8,128)(2,1)} %get-tuple-element.73) | copy-start | bytes 245764
  58.7 23.4 %copy-start.29 = (bf16[160,256]{1,0:T(8,128)(2,1)S(1)}, bf16[160,256]{1,0:T(8,128)(2,1)}, u32[]{:S(2)}) copy-start(bf16[160,256]{1,0:T(8,128)(2,1)} %get-tuple-element.80) | copy-start | bytes 245764
  60.6 19.6 %collective-permute-start.16 = (bf16[128,1024]{1,0:T(8,128)(2,1)S(1)}, bf16[128,1024]{1,0:T(8,128)(2,1)S(1)}, u32[]{:S(2)}, u32[]{:S(2)}) collective-permute-start(bf16[128,1024]{1,0:T(8,128)(2,1)S(1)} %slice.35), channel_id=1, source_target_pairs={{0,1},{1,0},{2,3},{3,2},{4,5},{5,4},{6,7},{7,6},{8,9},{9,8},{10,11... | collective-permute-start | bytes 786440 | tf_op jit(solution)/shard_map/ppermute | solution.py:282
  62.8 17.4 %collective-permute-start.14 = (bf16[128,1024]{1,0:T(8,128)(2,1)S(1)}, bf16[128,1024]{1,0:T(8,128)(2,1)S(1)}, u32[]{:S(2)}, u32[]{:S(2)}) collective-permute-start(bf16[128,1024]{1,0:T(8,128)(2,1)S(1)} %slice.34), channel_id=1, source_target_pairs={{0,2},{1,3},{2,0},{3,1},{4,6},{5,7},{6,4},{7,5},{8,10},{9,11},{10,... | collective-permute-start | bytes 786440 | tf_op jit(solution)/shard_map/ppermute | solution.py:282
  80.2 11.0 %collective-permute-start.21 = (bf16[256,1024]{1,0:T(8,128)(2,1)}, bf16[256,1024]{1,0:T(8,128)(2,1)S(1)}, u32[]{:S(2)}, u32[]{:S(2)}) collective-permute-start(bf16[256,1024]{1,0:T(8,128)(2,1)} %collective-permute-done.3.own_ref), channel_id=1, source_target_pairs={{0,2},{1,3},{2,0},{3,1},{4,6},{5,7},{6,4},{7,5},{8,10},{9,11},{10,... | collective-permute-start | bytes 1572872 | tf_op jit(solution)/shard_map/ppermute | solution.py:282
  80.7 11.2 %collective-permute-start.17 = (bf16[256,1024]{1,0:T(8,128)(2,1)}, bf16[256,1024]{1,0:T(8,128)(2,1)S(1)}, u32[]{:S(2)}, u32[]{:S(2)}) collective-permute-start(bf16[256,1024]{1,0:T(8,128)(2,1)} %collective-permute-done.3.own_ref), channel_id=1, source_target_pairs={{0,1},{1,0},{2,3},{3,2},{4,5},{5,4},{6,7},{7,6},{8,9},{9,8},{10,11... | collective-permute-start | bytes 1572872 | tf_op jit(solution)/shard_map/ppermute | solution.py:282
  81.6 1.5 collective-permute-start.18
  81.6 7.2 %collective-permute-start.19 = (bf16[512,256]{1,0:T(8,128)(2,1)S(1)}, bf16[512,256]{1,0:T(8,128)(2,1)S(1)}, u32[]{:S(2)}, u32[]{:S(2)}) collective-permute-start(bf16[512,256]{1,0:T(8,128)(2,1)S(1)} %copy-done.10), channel_id=1, source_target_pairs={{0,4},{4,0},{8,12},{12,8},{16,20},{20,16},{24,28},{28,24},{1,5},{5... | collective-permute-start | bytes 786440 | tf_op jit(solution)/shard_map/ppermute | solution.py:278
  82.1 16.8 %collective-permute-start.4 = (bf16[256,1024]{1,0:T(8,128)(2,1)}, bf16[256,1024]{1,0:T(8,128)(2,1)S(1)}, u32[]{:S(2)}, u32[]{:S(2)}) collective-permute-start(bf16[256,1024]{1,0:T(8,128)(2,1)} %collective-permute-done.3.own_ref), channel_id=1, source_target_pairs={{0,8},{4,12},{8,16},{12,20},{16,24},{20,28},{24,0},{28,4},{1,9},{5... | collective-permute-start | bytes 1572872 | tf_op jit(solution)/shard_map/ppermute | solution.py:274
  83.1 28.7 %collective-permute-start.29 = (bf16[1344,256]{1,0:T(8,128)(2,1)S(1)}, bf16[1344,256]{1,0:T(8,128)(2,1)S(1)}, u32[]{:S(2)}, u32[]{:S(2)}) collective-permute-start(bf16[1344,256]{1,0:T(8,128)(2,1)S(1)} %pad_maximum_fusion.3), channel_id=1, source_target_pairs={{0,24},{4,28},{8,0},{12,4},{16,8},{20,12},{24,16},{28,20},{1,25},{... | collective-permute-start | bytes 2064392 | tf_op jit(solution)/shard_map/ppermute | solution.py:274
  91.2 7.7 %collective-permute-start.22 = (bf16[128,1024]{1,0:T(8,128)(2,1)S(1)}, bf16[128,1024]{1,0:T(8,128)(2,1)S(1)}, u32[]{:S(2)}, u32[]{:S(2)}) collective-permute-start(bf16[128,1024]{1,0:T(8,128)(2,1)S(1)} %slice.37), channel_id=1, source_target_pairs={{0,1},{1,0},{2,3},{3,2},{4,5},{5,4},{6,7},{7,6},{8,9},{9,8},{10,11... | collective-permute-start | bytes 786440 | tf_op jit(solution)/shard_map/ppermute | solution.py:282
  91.9 7.0 %collective-permute-start.20 = (bf16[128,1024]{1,0:T(8,128)(2,1)S(1)}, bf16[128,1024]{1,0:T(8,128)(2,1)S(1)}, u32[]{:S(2)}, u32[]{:S(2)}) collective-permute-start(bf16[128,1024]{1,0:T(8,128)(2,1)S(1)} %slice.36), channel_id=1, source_target_pairs={{0,2},{1,3},{2,0},{3,1},{4,6},{5,7},{6,4},{7,5},{8,10},{9,11},{10,... | collective-permute-start | bytes 786440 | tf_op jit(solution)/shard_map/ppermute | solution.py:282
  93.4 22.4 %collective-permute-start.24 = (bf16[1344,256]{1,0:T(8,128)(2,1)S(1)}, bf16[1344,256]{1,0:T(8,128)(2,1)S(1)}, u32[]{:S(2)}, u32[]{:S(2)}) collective-permute-start(bf16[1344,256]{1,0:T(8,128)(2,1)S(1)} %collective-permute-done.6.refs_1_), channel_id=1, source_target_pairs={{0,4},{4,0},{8,12},{12,8},{16,20},{20,16},{24,28},{28,24},{1,5},{5... | collective-permute-start | bytes 2064392 | tf_op jit(solution)/shard_map/ppermute | solution.py:278
  98.9 16.9 %collective-permute-start.25 = (bf16[256,1024]{1,0:T(8,128)(2,1)S(1)}, bf16[256,1024]{1,0:T(8,128)(2,1)S(1)}, u32[]{:S(2)}, u32[]{:S(2)}) collective-permute-start(bf16[256,1024]{1,0:T(8,128)(2,1)S(1)} %collective-permute-done.4.own_ref), channel_id=1, source_target_pairs={{0,2},{1,3},{2,0},{3,1},{4,6},{5,7},{6,4},{7,5},{8,10},{9,11},{10,... | collective-permute-start | bytes 1572872 | tf_op jit(solution)/shard_map/ppermute | solution.py:282
  100.4 16.6 %collective-permute-start.23 = (bf16[256,1024]{1,0:T(8,128)(2,1)S(1)}, bf16[256,1024]{1,0:T(8,128)(2,1)S(1)}, u32[]{:S(2)}, u32[]{:S(2)}) collective-permute-start(bf16[256,1024]{1,0:T(8,128)(2,1)S(1)} %collective-permute-done.4.own_ref), channel_id=1, source_target_pairs={{0,1},{1,0},{2,3},{3,2},{4,5},{5,4},{6,7},{7,6},{8,9},{9,8},{10,11... | collective-permute-start | bytes 1572872 | tf_op jit(solution)/shard_map/ppermute | solution.py:282
  111.8 31.8 %collective-permute-start.30 = (bf16[1344,256]{1,0:T(8,128)(2,1)S(1)}, bf16[1344,256]{1,0:T(8,128)(2,1)S(1)}, u32[]{:S(2)}, u32[]{:S(2)}) collective-permute-start(bf16[1344,256]{1,0:T(8,128)(2,1)S(1)} %pad_maximum_fusion.2), channel_id=1, source_target_pairs={{0,16},{4,20},{8,24},{12,28},{16,0},{20,4},{24,8},{28,12},{1,17},{... | collective-permute-start | bytes 2064392 | tf_op jit(solution)/shard_map/ppermute | solution.py:274
  115.8 27.8 %collective-permute-start.27 = (bf16[128,1024]{1,0:T(8,128)(2,1)S(1)}, bf16[128,1024]{1,0:T(8,128)(2,1)S(1)}, u32[]{:S(2)}, u32[]{:S(2)}) collective-permute-start(bf16[128,1024]{1,0:T(8,128)(2,1)S(1)} %slice.39), channel_id=1, source_target_pairs={{0,1},{1,0},{2,3},{3,2},{4,5},{5,4},{6,7},{7,6},{8,9},{9,8},{10,11... | collective-permute-start | bytes 786440 | tf_op jit(solution)/shard_map/ppermute | solution.py:282
  117.1 26.5 %collective-permute-start.26 = (bf16[128,1024]{1,0:T(8,128)(2,1)S(1)}, bf16[128,1024]{1,0:T(8,128)(2,1)S(1)}, u32[]{:S(2)}, u32[]{:S(2)}) collective-permute-start(bf16[128,1024]{1,0:T(8,128)(2,1)S(1)} %slice.38), channel_id=1, source_target_pairs={{0,2},{1,3},{2,0},{3,1},{4,6},{5,7},{6,4},{7,5},{8,10},{9,11},{10,... | collective-permute-start | bytes 786440 | tf_op jit(solution)/shard_map/ppermute | solution.py:282
  118.7 29.4 %collective-permute-start.32 = (bf16[1344,256]{1,0:T(8,128)(2,1)S(1)}, bf16[1344,256]{1,0:T(8,128)(2,1)S(1)}, u32[]{:S(2)}, u32[]{:S(2)}) collective-permute-start(bf16[1344,256]{1,0:T(8,128)(2,1)S(1)} %collective-permute-done.29.refs_3_), channel_id=1, source_target_pairs={{0,4},{4,0},{8,12},{12,8},{16,20},{20,16},{24,28},{28,24},{1,5},{5... | collective-permute-start | bytes 2064392 | tf_op jit(solution)/shard_map/ppermute | solution.py:278
  143.6 4.4 %collective-permute-start.31 = (bf16[1344,256]{1,0:T(8,128)(2,1)S(1)}, bf16[1344,256]{1,0:T(8,128)(2,1)S(1)}, u32[]{:S(2)}, u32[]{:S(2)}) collective-permute-start(bf16[1344,256]{1,0:T(8,128)(2,1)S(1)} %collective-permute-done.30.refs_2_), channel_id=1, source_target_pairs={{0,4},{4,0},{8,12},{12,8},{16,20},{20,16},{24,28},{28,24},{1,5},{5... | collective-permute-start | bytes 2064392 | tf_op jit(solution)/shard_map/ppermute | solution.py:278
  145.6 14.6 %collective-permute-start.28 = (bf16[512,256]{1,0:T(8,128)(2,1)S(1)}, bf16[512,256]{1,0:T(8,128)(2,1)S(1)}, u32[]{:S(2)}, u32[]{:S(2)}) collective-permute-start(bf16[512,256]{1,0:T(8,128)(2,1)S(1)} %copy-done.32), channel_id=1, source_target_pairs={{0,16},{4,20},{8,24},{12,28},{16,0},{20,4},{24,8},{28,12},{1,17},{... | collective-permute-start | bytes 786440 | tf_op jit(solution)/shard_map/ppermute | solution.py:274
  153.2 9.7 %collective-permute-start.34 = (bf16[4,256,256]{2,1,0:T(8,128)(2,1)S(1)}, bf16[4,256,256]{2,1,0:T(8,128)(2,1)S(1)}, u32[]{:S(2)}, u32[]{:S(2)}) collective-permute-start(bf16[4,256,256]{2,1,0:T(8,128)(2,1)S(1)} %get-tuple-element.50.k_ref), channel_id=1, source_target_pairs={{0,4},{4,0},{8,12},{12,8},{16,20},{20,16},{24,28},{28,24},{1,5},{5... | collective-permute-start | bytes 1572872 | tf_op jit(solution)/shard_map/ppermute | solution.py:278
  153.8 9.1 %collective-permute-start.35 = (bf16[4,256,256]{2,1,0:T(8,128)(2,1)S(1)}, bf16[4,256,256]{2,1,0:T(8,128)(2,1)S(1)}, u32[]{:S(2)}, u32[]{:S(2)}) collective-permute-start(bf16[4,256,256]{2,1,0:T(8,128)(2,1)S(1)} %get-tuple-element.52.v_ref), channel_id=1, source_target_pairs={{0,4},{4,0},{8,12},{12,8},{16,20},{20,16},{24,28},{28,24},{1,5},{5... | collective-permute-start | bytes 1572872 | tf_op jit(solution)/shard_map/ppermute | solution.py:278
  160.1 1.5 collective-permute-start.33
  167.7 12.9 %collective-permute-start.36 = (bf16[256,256]{1,0:T(8,128)(2,1)S(1)}, bf16[256,256]{1,0:T(8,128)(2,1)S(1)}, u32[]{:S(2)}, u32[]{:S(2)}) collective-permute-start(bf16[256,256]{1,0:T(8,128)(2,1)S(1)} %attend.3), channel_id=1, source_target_pairs={{0,16},{4,20},{8,24},{12,28},{16,0},{20,4},{24,8},{28,12},{1,17},{... | collective-permute-start | bytes 393224 | tf_op jit(solution)/shard_map/ppermute | solution.py:274
  176.7 8.2 %collective-permute-start.37 = (bf16[256,256]{1,0:T(8,128)(2,1)S(1)}, bf16[256,256]{1,0:T(8,128)(2,1)S(1)}, u32[]{:S(2)}, u32[]{:S(2)}) collective-permute-start(bf16[256,256]{1,0:T(8,128)(2,1)S(1)} %get-tuple-element.54), channel_id=1, source_target_pairs={{0,8},{4,12},{8,16},{12,20},{16,24},{20,28},{24,0},{28,4},{1,9},{5... | collective-permute-start | bytes 393224 | tf_op jit(solution)/shard_map/ppermute | solution.py:274
  176.8 9.5 %collective-permute-start.38 = (bf16[256,256]{1,0:T(8,128)(2,1)S(1)}, bf16[256,256]{1,0:T(8,128)(2,1)S(1)}, u32[]{:S(2)}, u32[]{:S(2)}) collective-permute-start(bf16[256,256]{1,0:T(8,128)(2,1)S(1)} %get-tuple-element.56), channel_id=1, source_target_pairs={{0,24},{4,28},{8,0},{12,4},{16,8},{20,12},{24,16},{28,20},{1,25},{... | collective-permute-start | bytes 393224 | tf_op jit(solution)/shard_map/ppermute | solution.py:274
  (28 other events, 232.5 us)

commit v2 on v1

--- a/solution.py
+++ b/solution.py
@@ -166,59 +166,94 @@
 NT = (((1,), (1,)), ((), ()))
 
 
-def attend_kernel(shifts, place_ref, q_ref, k_ref, v_ref, ks_ref, vs_ref, ck_ref, cv_ref, *outs):
+def lanes(op, s):
+    full = s.shape[1] - s.shape[1] % LANES
+    rest = s[:, full:] if full < s.shape[1] else None
+    return functools.reduce(op, [s[:, i : i + LANES] for i in range(0, full, LANES)]), rest
+
+
+def attend_kernel(shifts, place_ref, q_ref, k_ref, v_ref, ks_ref, vs_ref, ck_ref, cv_ref, *refs):
+    outs, (old, new) = refs[: len(shifts)], refs[len(shifts) :]
     z, core = place_ref[1], place_ref[2]
     zs, rows, cols = k_ref.shape
     heads = range(cols // HEAD)
     factor = 1.4426950408889634 / HEAD**0.5
+    low = -1e30
     hcols = [slice(h * HEAD, (h + 1) * HEAD) for h in heads]
-    row = lax.broadcasted_iota(jnp.int32, (rows, 2 * rows), 0)
-    col = lax.broadcasted_iota(jnp.int32, (rows, 2 * rows), 1)
-    visible = jnp.where(col < rows, col, jnp.where(core == 1, 0, rows)) <= row
-
-    def fold(state, query, key, value, mask):
-        s = lax.dot_general(query, key, NT, preferred_element_type=F32)
-        if mask is not None:
-            s = jnp.where(mask, s, -1e30)
-        top = jnp.max(s, axis=-1, keepdims=True) * factor
-        if state is not None:
-            top = jnp.maximum(top, state[0])
-        weights = jnp.exp2(s * factor - top)
-        total = jnp.sum(weights, axis=-1, keepdims=True)
-        summed = jnp.dot(weights.astype(BF16), value, preferred_element_type=F32)
-        if state is not None:
-            scale = jnp.exp2(state[0] - top)
-            total, summed = total + state[1] * scale, summed + state[2] * scale
-        return top, total, summed
-
-    def both(b, h):
-        at = lax.rem(z + zs - b, zs)
-        key = jnp.concatenate([k_ref[at, :, hcols[h]], ks_ref[at, :, hcols[h]]], axis=0)
-        value = jnp.concatenate([v_ref[at, :, hcols[h]], vs_ref[at, :, hcols[h]]], axis=0)
-        return key, value
+    row = lax.broadcasted_iota(jnp.int32, (rows, rows), 0)
+    col = lax.broadcasted_iota(jnp.int32, (rows, rows), 1)
+    causal = col <= row
 
     for shift, out_ref in zip(shifts, outs):
         block = lax.rem(z + shift, zs)
         mine = lax.rem(zs - shift, zs)
         queries = [q_ref[mine, :, hcol] for hcol in hcols]
 
-        def earlier(b, states):
-            return tuple(fold(states[h], queries[h], *both(b, h), None) for h in heads)
-
-        states = tuple(fold(None, queries[h], ck_ref[:, hcols[h]], cv_ref[:, hcols[h]], None) for h in heads)
-        states = lax.fori_loop(0, block, earlier, states)
+        def score(b, tops, diagonal):
+            at = lax.rem(z + zs - b, zs)
+            result = []
+            for h, top in zip(heads, tops):
+                s = lax.dot_general(queries[h], k_ref[at, :, hcols[h]], NT, preferred_element_type=F32)
+                t = lax.dot_general(queries[h], ks_ref[at, :, hcols[h]], NT, preferred_element_type=F32)
+                if diagonal:
+                    s, t = jnp.where(causal, s, low), jnp.where(core == 1, t, low)
+                new[h, b, :, :rows] = s
+                new[h, b, :, rows:] = t
+                folded = jnp.maximum(lanes(jnp.maximum, s)[0], lanes(jnp.maximum, t)[0])
+                result.append(jnp.maximum(top, folded))
+            return tuple(result)
+
+        tops, ends = [], []
         for h in heads:
-            _, total, summed = fold(states[h], queries[h], *both(block, h), visible)
+            s = lax.dot_general(queries[h], ck_ref[:, hcols[h]], NT, preferred_element_type=F32)
+            old[h] = s
+            folded, rest = lanes(jnp.maximum, s)
+            tops.append(folded)
+            ends.append(low if rest is None else jnp.max(rest, axis=-1, keepdims=True))
+        tops = lax.fori_loop(0, block, functools.partial(score, diagonal=False), tuple(tops))
+        tops = score(block, tops, True)
+        tops = [
+            jnp.maximum(jnp.max(top, axis=-1, keepdims=True), end) * factor
+            for top, end in zip(tops, ends)
+        ]
+
+        def weigh(b, state):
+            at = lax.rem(z + zs - b, zs)
+            result = []
+            for h, (total, summed) in zip(heads, state):
+                weights = jnp.exp2(new[h, b] * factor - tops[h])
+                probs = weights.astype(BF16)
+                summed += jnp.dot(probs[:, :rows], v_ref[at, :, hcols[h]], preferred_element_type=F32)
+                summed += jnp.dot(probs[:, rows:], vs_ref[at, :, hcols[h]], preferred_element_type=F32)
+                result.append((total + lanes(jnp.add, weights)[0], summed))
+            return tuple(result)
+
+        state, ends = [], []
+        for h in heads:
+            weights = jnp.exp2(old[h] * factor - tops[h])
+            folded, rest = lanes(jnp.add, weights)
+            ends.append(0.0 if rest is None else jnp.sum(rest, axis=-1, keepdims=True))
+            state.append(
+                (folded, jnp.dot(weights.astype(BF16), cv_ref[:, hcols[h]], preferred_element_type=F32))
+            )
+        state = lax.fori_loop(0, block + 1, weigh, tuple(state))
+        for h, (total, summed), end in zip(heads, state, ends):
+            total = jnp.sum(total, axis=-1, keepdims=True) + end
             out_ref[:, hcols[h]] = (summed / total).astype(BF16)
 
 
 def attend(shifts, place, q, k, v, k_sib, v_sib, ck, cv):
-    _, rows, cols = q.shape
+    zs, rows, cols = q.shape
+    heads = cols // HEAD
     return pl.pallas_call(
         functools.partial(attend_kernel, shifts),
         in_specs=[SMEM] + [VMEM] * 7,
         out_specs=[VMEM] * len(shifts),
         out_shape=[jax.ShapeDtypeStruct((rows, cols), BF16)] * len(shifts),
+        scratch_shapes=[
+            pltpu.VMEM((heads, rows, ck.shape[0]), F32),
+            pltpu.VMEM((heads, zs, rows, 2 * rows), F32),
+        ],
         compiler_params=pltpu.CompilerParams(vmem_limit_bytes=20 * MIB),
         cost_estimate=BRIEF,
         name="attend",
@@ -332,7 +367,7 @@
     late = [("kv", 2), ("q", 2)]
     there = {item: swap_core(here[item], zs) for item in here if item not in late}
 
-    pace = [[("q", 1), ("q", 3)], [], [("kv", 1)], []]
+    pace = [[("q", 1), ("q", 3)], [("kv", 1)], [("kv", 3)], []]
     swapped = [[], [("kv", 0), ("q", 0)], [("q", 1), ("q", 3)], [("kv", 1)]]
     gain4 = gain.reshape(4, 1, width)
     half = rows // 2

time: 189 us -> 188 us (level)
  Pallas kernels: 42.1 us -> 39.5 us
    ppermute x16, waiting for transfers between devices: 16 us -> 25.7 us  [swap_chan(): return lax.ppermute(value, 'chan', [(c, c ^ bit) for c in range(4)])]
    ppermute x12, waiting for transfers between devices: 72 us -> 64.4 us  [shift_z(): return lax.ppermute(value, 'seq', pairs)]
    pallas_call x3, Pallas kernels: 16.5 us -> 13.8 us  [attend(): pl.pallas_call(functools.partial(attend_kernel, shifts), in_specs=[SMEM]...]
    unnamed x74 -> x82, local copies, waits for them, and re-layouts: 7.49 us -> 8.24 us
  transfers between devices with their start and end apart: 39 -> 39, of which waited for: 17 -> 17; matrix products, arithmetic and copies ran while one was open for 4% -> 4% of each run, Pallas kernels for 19% -> 18%
where the time goes in v2:
time: 188 us
  waiting for transfers between devices  91.6 us (49%)
  Pallas kernels  39.5 us (21%)
  starting transfers between devices  38.8 us (21%)
  local copies, waits for them, and re-layouts  14.6 us (8%)
  other arithmetic  2.36 us (1%)
    ppermute x12, waiting for transfers between devices, shift_z(): return lax.ppermute(value, 'seq', pairs)  64.4 us
    ppermute x16, waiting for transfers between devices, swap_chan(): return lax.ppermute(value, 'chan', [(c, c ^ bit) for c in range(4)])  25.7 us
    ppermute x16, starting transfers between devices, swap_chan(): return lax.ppermute(value, 'chan', [(c, c ^ bit) for c in range(4)])  18.9 us
    ppermute x12, starting transfers between devices, shift_z(): return lax.ppermute(value, 'seq', pairs)  15.5 us
    pallas_call x3, Pallas kernels, attend(): pl.pallas_call(functools.partial(attend_kernel, shifts), in_specs=[SMEM]...  13.8 us
    pallas_call x4, Pallas kernels, norm(): pl.pallas_call(functools.partial(norm_kernel, j), in_specs=[SMEM] + [VMEM...  8.93 us
    pallas_call x3, Pallas kernels, project(): pl.pallas_call(functools.partial(project_kernel, shifts, zs, count), in_s...  8.69 us
    unnamed x82, local copies, waits for them, and re-layouts  8.24 us
  transfers between devices with their start and end apart: 39, of which 17 were waited for; matrix products, arithmetic and copies ran while one was open for 4% of the time, Pallas kernels for 18%

profile of v2, /device:TPU:0, one launch (start us, length us, event | category | flops | bytes accessed | tf_op | source)
XLA Modules:
  0.0 187.5 jit_solution(5225136863309004623)
XLA Ops:
  0.0 1.1 fusion
  1.1 3.1 %collective-permute-start = (bf16[128,1024]{1,0:T(8,128)(2,1)S(1)}, bf16[128,1024]{1,0:T(8,128)(2,1)}, u32[]{:S(2)}, u32[]{:S(2)}) collective-permute-start(bf16[128,1024]{1,0:T(8,128)(2,1)S(1)} %fusion), channel_id=1, source_target_pairs={{0,4},{4,8},{8,12},{12,16},{16,20},{20,24},{24,28},{1,5},{5,9},{9,... | collective-permute-start | bytes 786440 | tf_op jit(solution)/shard_map/ppermute | solution.py:351
  4.2 3.4 %dynamic-slice_bitcast_fusion.1 = (bf16[512,256]{1,0:T(8,128)(2,1)}, bf16[512,256]{1,0:T(8,128)(2,1)}, bf16[512,256]{1,0:T(8,128)(2,1)S(1)}, bf16[512,256]{1,0:T...) fusion(bf16[512,3,1024]{2,0,1:T(8,128)(2,1)} %param.11, ...), kind=kLoop, calls=%fused_computation.7 | loop fusion | bytes 6291472 | tf_op jit(solution)/shard_map/squeeze | solution.py:342
  7.6 2.1 %collective-permute-start.1 = (bf16[512,256]{1,0:T(8,128)(2,1)}, bf16[512,256]{1,0:T(8,128)(2,1)S(1)}, u32[]{:S(2)}, u32[]{:S(2)}) collective-permute-start(bf16[512,256]{1,0:T(8,128)(2,1)} %get-tuple-element.67), channel_id=1, source_target_pairs={{0,8},{4,12},{8,16},{12,20},{16,24},{20,28},{24,0},{28,4},{1,9},{5... | collective-permute-start | bytes 786440 | tf_op jit(solution)/shard_map/ppermute | solution.py:309
  9.7 2.1 %collective-permute-start.5 = (bf16[512,256]{1,0:T(8,128)(2,1)}, bf16[512,256]{1,0:T(8,128)(2,1)S(1)}, u32[]{:S(2)}, u32[]{:S(2)}) collective-permute-start(bf16[512,256]{1,0:T(8,128)(2,1)} %get-tuple-element.62), channel_id=1, source_target_pairs={{0,24},{4,28},{8,0},{12,4},{16,8},{20,12},{24,16},{28,20},{1,25},{... | collective-permute-start | bytes 786440 | tf_op jit(solution)/shard_map/ppermute | solution.py:309
  12.8 6.0 %hyena_filters.1.own_ref = bf16[256,1024]{1,0:T(8,128)(2,1)S(1)} custom-call(bf16[3,256,1024]{2,1,0:T(8,128)(2,1)S(1)} %bitcast.32, bf16[128,1024]{1,0:T(8,128)(2,1)S(1)} %pad_select_fusion.halo_ref, f32[64,128]{1,0:T(8,128)S(1)} %copy-done.18), custom_call_target="tpu_custom_call" | custom-call | flops 1 | bytes 1 | tf_op jit(solution)/shard_map/hyena_filters/pallas_call | solution.py:80
  19.6 5.0 %collective-permute-done.5.refs_2_ = bf16[512,256]{1,0:T(8,128)(2,1)S(1)} collective-permute-done((bf16[512,256]{1,0:T(8,128)(2,1)}, bf16[512,256]{1,0:T(8,128)(2,1)S(1)}, u32[]{:S(2)}, u32[]{:S(2)}) %collective-permute-start.5) | collective-permute-done | bytes 262176 | tf_op jit(solution)/shard_map/ppermute | solution.py:309
  25.3 1.3 collective-permute-start.10
  26.6 1.5 collective-permute-start.8
  28.2 1.6 collective-permute-start.6
  30.1 9.2 %collective-permute-done.10.y_ref = bf16[256,1024]{1,0:T(8,128)(2,1)S(1)} collective-permute-done((bf16[256,1024]{1,0:T(8,128)(2,1)S(1)}, bf16[256,1024]{1,0:T(8,128)(2,1)S(1)}, u32[]{:S(2)}, u32[]{:S(2)}) %collective-permute-start.10) | collective-permute-done | bytes 524320 | tf_op jit(solution)/shard_map/ppermute | solution.py:317
  39.3 1.4 collective-permute-start.11
  40.7 1.6 collective-permute-start.9
  42.5 15.9 %collective-permute-done.2.own_ref = bf16[256,1024]{1,0:T(8,128)(2,1)} collective-permute-done((bf16[256,1024]{1,0:T(8,128)(2,1)S(1)}, bf16[256,1024]{1,0:T(8,128)(2,1)}, u32[]{:S(2)}, u32[]{:S(2)}) %collective-permute-start.2) | collective-permute-done | bytes 524320 | tf_op jit(solution)/shard_map/ppermute | solution.py:309
  62.0 2.0 %collective-permute-start.3 = (bf16[256,1024]{1,0:T(8,128)(2,1)}, bf16[256,1024]{1,0:T(8,128)(2,1)}, u32[]{:S(2)}, u32[]{:S(2)}) collective-permute-start(bf16[256,1024]{1,0:T(8,128)(2,1)} %collective-permute-done.2.own_ref), channel_id=1, source_target_pairs={{0,8},{4,12},{8,16},{12,20},{16,24},{20,28},{24,0},{28,4},{1,9},{5... | collective-permute-start | bytes 1572872 | tf_op jit(solution)/shard_map/ppermute | solution.py:309
  64.1 1.0 copy-done.2
  65.1 1.0 copy-done.4
  68.1 1.9 %norm.4.rest_0_ = bf16[4,4,256,1024]{3,2,1,0:T(8,128)(2,1)S(1)} custom-call(s32[3]{0:T(128)S(1)} %pad_add_fusion.place_ref, bf16[256,1024]{1,0:T(8,128)(2,1)S(1)} %hyena_filters.1.own_ref, bf16[256,1024]{1,0:T(8,128)(2,1)S(1)} %copy-done.4, bf16[256,1024]{1,0:T(8,128)(2,1)S(1)} %copy-done.2, bf16[128,1024]{1,0:T(8,128)(2,1)S(1)} %copy-done.16, ...), custom_call_target="tpu_custom_call" | custom-call | flops 1 | bytes 1 | tf_op jit(solution)/shard_map/norm/pallas_call | solution.py:119
  70.0 3.7 %collective-permute-done.16.y_ref = bf16[256,1024]{1,0:T(8,128)(2,1)} collective-permute-done((bf16[256,1024]{1,0:T(8,128)(2,1)}, bf16[256,1024]{1,0:T(8,128)(2,1)}, u32[]{:S(2)}, u32[]{:S(2)}) %collective-permute-start.16) | collective-permute-done | bytes 524320 | tf_op jit(solution)/shard_map/ppermute | solution.py:317
  77.0 12.4 %collective-permute-done.3.own_ref = bf16[256,1024]{1,0:T(8,128)(2,1)} collective-permute-done((bf16[256,1024]{1,0:T(8,128)(2,1)}, bf16[256,1024]{1,0:T(8,128)(2,1)}, u32[]{:S(2)}, u32[]{:S(2)}) %collective-permute-start.3) | collective-permute-done | bytes 524320 | tf_op jit(solution)/shard_map/ppermute | solution.py:309
  90.0 1.3 collective-permute-start.22
  91.3 1.5 collective-permute-start.18
  93.9 2.7 %norm.5.rest_0_ = bf16[4,4,256,1024]{3,2,1,0:T(8,128)(2,1)S(1)} custom-call(s32[3]{0:T(128)S(1)} %pad_add_fusion.place_ref, bf16[256,1024]{1,0:T(8,128)(2,1)} %collective-permute-done.2.own_ref, bf16[256,1024]{1,0:T(8,128)(2,1)} %collective-permute-done.12.x_ref, bf16[256,1024]{1,0:T(8,128)(2,1)} %collective-permute-done.16.y_ref, ...), custom_call_target="tpu_custom_call", output_to_operand_aliasing={{}: (7, {})} | custom-call | flops 1 | bytes 1 | tf_op jit(solution)/shard_map/norm/pallas_call | solution.py:119
  96.6 5.9 %collective-permute-done.22.y_ref = bf16[256,1024]{1,0:T(8,128)(2,1)S(1)} collective-permute-done((bf16[256,1024]{1,0:T(8,128)(2,1)}, bf16[256,1024]{1,0:T(8,128)(2,1)S(1)}, u32[]{:S(2)}, u32[]{:S(2)}) %collective-permute-start.22) | collective-permute-done | bytes 524320 | tf_op jit(solution)/shard_map/ppermute | solution.py:317
  102.6 1.7 collective-permute-start.23
  104.7 1.1 collective-permute-start.21
  105.9 3.4 %collective-permute-done.4.own_ref = bf16[256,1024]{1,0:T(8,128)(2,1)S(1)} collective-permute-done((bf16[256,1024]{1,0:T(8,128)(2,1)}, bf16[256,1024]{1,0:T(8,128)(2,1)S(1)}, u32[]{:S(2)}, u32[]{:S(2)}) %collective-permute-start.4) | collective-permute-done | bytes 524320 | tf_op jit(solution)/shard_map/ppermute | solution.py:309
  109.5 1.7 collective-permute-done.21.d0_ref
  111.2 1.5 collective-permute-start.26
  113.3 2.9 %collective-permute-start.30 = (bf16[1344,256]{1,0:T(8,128)(2,1)S(1)}, bf16[1344,256]{1,0:T(8,128)(2,1)S(1)}, u32[]{:S(2)}, u32[]{:S(2)}) collective-permute-start(bf16[1344,256]{1,0:T(8,128)(2,1)S(1)} %pad_maximum_fusion.3), channel_id=1, source_target_pairs={{0,16},{4,20},{8,24},{12,28},{16,0},{20,4},{24,8},{28,12},{1,17},{... | collective-permute-start | bytes 2064392 | tf_op jit(solution)/shard_map/ppermute | solution.py:309
  116.2 2.4 %norm.6.rest_0_ = bf16[4,4,256,1024]{3,2,1,0:T(8,128)(2,1)S(1)} custom-call(s32[3]{0:T(128)S(1)} %pad_add_fusion.place_ref, bf16[256,1024]{1,0:T(8,128)(2,1)} %collective-permute-done.3.own_ref, bf16[256,1024]{1,0:T(8,128)(2,1)S(1)} %collective-permute-done.18.x_ref, ...), custom_call_target="tpu_custom_call", output_to_operand_aliasing={{}: (7, {})} | custom-call | flops 1 | bytes 1 | tf_op jit(solution)/shard_map/norm/pallas_call | solution.py:119
  118.6 4.3 %collective-permute-done.26.y_ref = bf16[256,1024]{1,0:T(8,128)(2,1)S(1)} collective-permute-done((bf16[256,1024]{1,0:T(8,128)(2,1)S(1)}, bf16[256,1024]{1,0:T(8,128)(2,1)S(1)}, u32[]{:S(2)}, u32[]{:S(2)}) %collective-permute-start.26) | collective-permute-done | bytes 524320 | tf_op jit(solution)/shard_map/ppermute | solution.py:317
  122.9 1.1 collective-permute-start.28
  124.0 2.0 %collective-permute-start.27 = (bf16[128,1024]{1,0:T(8,128)(2,1)S(1)}, bf16[128,1024]{1,0:T(8,128)(2,1)S(1)}, u32[]{:S(2)}, u32[]{:S(2)}) collective-permute-start(bf16[128,1024]{1,0:T(8,128)(2,1)S(1)} %slice.38), channel_id=1, source_target_pairs={{0,2},{1,3},{2,0},{3,1},{4,6},{5,7},{6,4},{7,5},{8,10},{9,11},{10,... | collective-permute-start | bytes 786440 | tf_op jit(solution)/shard_map/ppermute | solution.py:317
  126.0 17.9 %collective-permute-done.30.refs_2_ = bf16[1344,256]{1,0:T(8,128)(2,1)S(1)} collective-permute-done((bf16[1344,256]{1,0:T(8,128)(2,1)S(1)}, bf16[1344,256]{1,0:T(8,128)(2,1)S(1)}, u32[]{:S(2)}, u32[]{:S(2)}) %collective-permute-start.30) | collective-permute-done | bytes 688160 | tf_op jit(solution)/shard_map/ppermute | solution.py:309
  144.0 1.9 %norm.7.normed_ref = bf16[4,4,256,1024]{3,2,1,0:T(8,128)(2,1)S(1)} custom-call(s32[3]{0:T(128)S(1)} %pad_add_fusion.place_ref, bf16[256,1024]{1,0:T(8,128)(2,1)S(1)} %collective-permute-done.4.own_ref, bf16[256,1024]{1,0:T(8,128)(2,1)S(1)} %collective-permute-done.24.x_ref, ...), custom_call_target="tpu_custom_call", output_to_operand_aliasing={{}: (7, {})} | custom-call | flops 1 | bytes 1 | tf_op jit(solution)/shard_map/norm/pallas_call | solution.py:119
  146.0 2.3 %project.3.refs_2_ = f32[4,256,256]{2,1,0:T(8,128)S(1)} custom-call(s32[3]{0:T(128)S(1)} %pad_add_fusion.place_ref, bf16[4,4,256,1024]{3,2,1,0:T(8,128)(2,1)S(1)} %norm.7.normed_ref, bf16[512,256]{1,0:T(8,128)(2,1)S(1)} %get-tuple-element.59.refs_0_, bf16[512,256]{1,0:T(8,128)(2,1)S(1)} %copy-done.8, bf16[512,256]{1,0:T(8,128)(2,1)S(1)} %copy-done.10, ...), custom_call_target="tpu_custom_call" | custom-call | flops 1 | bytes 1 | tf_op jit(solution)/shard_map/project/pallas_call | solution.py:155
  148.5 5.1 %project.4 = (bf16[4,256,256]{2,1,0:T(8,128)(2,1)S(1)}, bf16[4,256,256]{2,1,0:T(8,128)(2,1)S(1)}) custom-call(s32[3]{0:T(128)S(1)} %pad_add_fusion.place_ref, bf16[4,4,256,1024]{3,2,1,0:T(8,128)(2,1)S(1)} %norm.7.normed_ref, bf16[1344,256]{1,0:T(8,128)(2,1)S(1)} %pad_maximum_fusion.2.refs_0_, bf16[1344,256]{1,0:T(8,128)(2,1)S(1)} %collective-permute-done.6.refs_1_, ...), custom_call_target="tpu_custom_call" | custom-call | flops 1 | bytes 1 | tf_op jit(solution)/shard_map/project/pallas_call | solution.py:155
  154.2 6.9 %collective-permute-done.29.refs_0_ = bf16[512,256]{1,0:T(8,128)(2,1)S(1)} collective-permute-done((bf16[512,256]{1,0:T(8,128)(2,1)S(1)}, bf16[512,256]{1,0:T(8,128)(2,1)S(1)}, u32[]{:S(2)}, u32[]{:S(2)}) %collective-permute-start.29) | collective-permute-done | bytes 262176 | tf_op jit(solution)/shard_map/ppermute | solution.py:309
  161.2 1.5 collective-permute-done.33.refs_1_
  162.7 1.3 project.5.q_ref
  164.0 4.1 %attend.3 = bf16[256,256]{1,0:T(8,128)(2,1)S(1)} custom-call(s32[3]{0:T(128)S(1)} %pad_add_fusion.place_ref, bf16[4,256,256]{2,1,0:T(8,128)(2,1)S(1)} %project.5.q_ref, bf16[4,256,256]{2,1,0:T(8,128)(2,1)S(1)} %get-tuple-element.50.k_ref, bf16[4,256,256]{2,1,0:T(8,128)(2,1)S(1)} %get-tuple-element.52.v_ref, ...), custom_call_target="tpu_custom_call" | custom-call | flops 1 | bytes 1 | tf_op jit(solution)/shard_map/attend/pallas_call | solution.py:248
  168.1 7.2 %attend.4 = (bf16[256,256]{1,0:T(8,128)(2,1)S(1)}, bf16[256,256]{1,0:T(8,128)(2,1)S(1)}) custom-call(s32[3]{0:T(128)S(1)} %pad_add_fusion.place_ref, bf16[4,256,256]{2,1,0:T(8,128)(2,1)S(1)} %project.5.q_ref, bf16[4,256,256]{2,1,0:T(8,128)(2,1)S(1)} %get-tuple-element.50.k_ref, bf16[4,256,256]{2,1,0:T(8,128)(2,1)S(1)} %get-tuple-element.52.v_ref, ...), custom_call_target="tpu_custom_call" | custom-call | flops 1 | bytes 1 | tf_op jit(solution)/shard_map/attend/pallas_call | solution.py:248
  175.4 3.8 %collective-permute-start.38 = (bf16[256,256]{1,0:T(8,128)(2,1)S(1)}, bf16[256,256]{1,0:T(8,128)(2,1)S(1)}, u32[]{:S(2)}, u32[]{:S(2)}) collective-permute-start(bf16[256,256]{1,0:T(8,128)(2,1)S(1)} %get-tuple-element.56), channel_id=1, source_target_pairs={{0,24},{4,28},{8,0},{12,4},{16,8},{20,12},{24,16},{28,20},{1,25},{... | collective-permute-start | bytes 393224 | tf_op jit(solution)/shard_map/ppermute | solution.py:309
  179.2 2.6 %attend.5.refs_0_ = bf16[256,256]{1,0:T(8,128)(2,1)S(1)} custom-call(s32[3]{0:T(128)S(1)} %pad_add_fusion.place_ref, bf16[4,256,256]{2,1,0:T(8,128)(2,1)S(1)} %project.5.q_ref, bf16[4,256,256]{2,1,0:T(8,128)(2,1)S(1)} %get-tuple-element.50.k_ref, bf16[4,256,256]{2,1,0:T(8,128)(2,1)S(1)} %get-tuple-element.52.v_ref, ...), custom_call_target="tpu_custom_call" | custom-call | flops 1 | bytes 1 | tf_op jit(solution)/shard_map/attend/pallas_call | solution.py:248
  182.5 1.1 collective-permute-done.37.refs_1_
  183.5 1.4 collective-permute-done.38.refs_3_
  185.6 2.0 %join.1 = bf16[256,1024]{1,0:T(8,128)(2,1)} custom-call(s32[3]{0:T(128)} %copy-done.17, bf16[256,256]{1,0:T(8,128)(2,1)} %copy-done.5, bf16[256,256]{1,0:T(8,128)(2,1)} %copy-done.39, bf16[256,256]{1,0:T(8,128)(2,1)} %copy-done.38, bf16[256,256]{1,0:T(8,128)(2,1)} %copy-done.40), custom_call_target="tpu_custom_call" | custom-call | tf_op jit(solution)/shard_map/join/pallas_call | solution.py:298
  (143 shorter events, 17.2 us)
Async XLA Ops:
  1.1 11.6 %collective-permute-start = (bf16[128,1024]{1,0:T(8,128)(2,1)S(1)}, bf16[128,1024]{1,0:T(8,128)(2,1)}, u32[]{:S(2)}, u32[]{:S(2)}) collective-permute-start(bf16[128,1024]{1,0:T(8,128)(2,1)S(1)} %fusion), channel_id=1, source_target_pairs={{0,4},{4,8},{8,12},{12,16},{16,20},{20,24},{24,28},{1,5},{5,9},{9,... | collective-permute-start | bytes 786440 | tf_op jit(solution)/shard_map/ppermute | solution.py:351
  7.6 11.2 %collective-permute-start.1 = (bf16[512,256]{1,0:T(8,128)(2,1)}, bf16[512,256]{1,0:T(8,128)(2,1)S(1)}, u32[]{:S(2)}, u32[]{:S(2)}) collective-permute-start(bf16[512,256]{1,0:T(8,128)(2,1)} %get-tuple-element.67), channel_id=1, source_target_pairs={{0,8},{4,12},{8,16},{12,20},{16,24},{20,28},{24,0},{28,4},{1,9},{5... | collective-permute-start | bytes 786440 | tf_op jit(solution)/shard_map/ppermute | solution.py:309
  9.7 14.9 %collective-permute-start.5 = (bf16[512,256]{1,0:T(8,128)(2,1)}, bf16[512,256]{1,0:T(8,128)(2,1)S(1)}, u32[]{:S(2)}, u32[]{:S(2)}) collective-permute-start(bf16[512,256]{1,0:T(8,128)(2,1)} %get-tuple-element.62), channel_id=1, source_target_pairs={{0,24},{4,28},{8,0},{12,4},{16,8},{20,12},{24,16},{28,20},{1,25},{... | collective-permute-start | bytes 786440 | tf_op jit(solution)/shard_map/ppermute | solution.py:309
  25.3 13.9 %collective-permute-start.10 = (bf16[256,1024]{1,0:T(8,128)(2,1)S(1)}, bf16[256,1024]{1,0:T(8,128)(2,1)S(1)}, u32[]{:S(2)}, u32[]{:S(2)}) collective-permute-start(bf16[256,1024]{1,0:T(8,128)(2,1)S(1)} %hyena_filters.1.own_ref), channel_id=1, source_target_pairs={{0,2},{1,3},{2,0},{3,1},{4,6},{5,7},{6,4},{7,5},{8,10},{9,11},{10,... | collective-permute-start | bytes 1572872 | tf_op jit(solution)/shard_map/ppermute | solution.py:317
  26.6 14.1 %collective-permute-start.8 = (bf16[256,1024]{1,0:T(8,128)(2,1)S(1)}, bf16[256,1024]{1,0:T(8,128)(2,1)S(1)}, u32[]{:S(2)}, u32[]{:S(2)}) collective-permute-start(bf16[256,1024]{1,0:T(8,128)(2,1)S(1)} %hyena_filters.1.own_ref), channel_id=1, source_target_pairs={{0,1},{1,0},{2,3},{3,2},{4,5},{5,4},{6,7},{7,6},{8,9},{9,8},{10,11... | collective-permute-start | bytes 1572872 | tf_op jit(solution)/shard_map/ppermute | solution.py:317
  28.1 32.1 %copy-start.21 = (bf16[512,256]{1,0:T(8,128)(2,1)S(1)}, bf16[512,256]{1,0:T(8,128)(2,1)}, u32[]{:S(2)}) copy-start(bf16[512,256]{1,0:T(8,128)(2,1)} %get-tuple-element.65) | copy-start | bytes 786436
  28.2 32.1 %copy-start.22 = (bf16[512,256]{1,0:T(8,128)(2,1)S(1)}, bf16[512,256]{1,0:T(8,128)(2,1)}, u32[]{:S(2)}) copy-start(bf16[512,256]{1,0:T(8,128)(2,1)} %get-tuple-element.66) | copy-start | bytes 786436
  28.2 32.1 %copy-start.28 = (bf16[160,256]{1,0:T(8,128)(2,1)S(1)}, bf16[160,256]{1,0:T(8,128)(2,1)}, u32[]{:S(2)}) copy-start(bf16[160,256]{1,0:T(8,128)(2,1)} %get-tuple-element.76) | copy-start | bytes 245764
  28.2 32.1 %copy-start.29 = (bf16[160,256]{1,0:T(8,128)(2,1)S(1)}, bf16[160,256]{1,0:T(8,128)(2,1)}, u32[]{:S(2)}) copy-start(bf16[160,256]{1,0:T(8,128)(2,1)} %get-tuple-element.77) | copy-start | bytes 245764
  28.2 30.1 %collective-permute-start.6 = (bf16[1344,256]{1,0:T(8,128)(2,1)S(1)}, bf16[1344,256]{1,0:T(8,128)(2,1)S(1)}, u32[]{:S(2)}, u32[]{:S(2)}) collective-permute-start(bf16[1344,256]{1,0:T(8,128)(2,1)S(1)} %pad_maximum_fusion.1), channel_id=1, source_target_pairs={{0,8},{4,12},{8,16},{12,20},{16,24},{20,28},{24,0},{28,4},{1,9},{5... | collective-permute-start | bytes 2064392 | tf_op jit(solution)/shard_map/ppermute | solution.py:309
  29.7 28.6 %collective-permute-start.2 = (bf16[256,1024]{1,0:T(8,128)(2,1)S(1)}, bf16[256,1024]{1,0:T(8,128)(2,1)}, u32[]{:S(2)}, u32[]{:S(2)}) collective-permute-start(bf16[256,1024]{1,0:T(8,128)(2,1)S(1)} %hyena_filters.1.own_ref), channel_id=1, source_target_pairs={{0,8},{4,12},{8,16},{12,20},{16,24},{20,28},{24,0},{28,4},{1,9},{5... | collective-permute-start | bytes 1572872 | tf_op jit(solution)/shard_map/ppermute | solution.py:309
  39.3 19.0 %collective-permute-start.11 = (bf16[128,1024]{1,0:T(8,128)(2,1)S(1)}, bf16[128,1024]{1,0:T(8,128)(2,1)S(1)}, u32[]{:S(2)}, u32[]{:S(2)}) collective-permute-start(bf16[128,1024]{1,0:T(8,128)(2,1)S(1)} %slice.43), channel_id=1, source_target_pairs={{0,1},{1,0},{2,3},{3,2},{4,5},{5,4},{6,7},{7,6},{8,9},{9,8},{10,11... | collective-permute-start | bytes 786440 | tf_op jit(solution)/shard_map/ppermute | solution.py:317
  40.7 18.4 %collective-permute-start.9 = (bf16[128,1024]{1,0:T(8,128)(2,1)S(1)}, bf16[128,1024]{1,0:T(8,128)(2,1)S(1)}, u32[]{:S(2)}, u32[]{:S(2)}) collective-permute-start(bf16[128,1024]{1,0:T(8,128)(2,1)S(1)} %slice.42), channel_id=1, source_target_pairs={{0,2},{1,3},{2,0},{3,1},{4,6},{5,7},{6,4},{7,5},{8,10},{9,11},{10,... | collective-permute-start | bytes 786440 | tf_op jit(solution)/shard_map/ppermute | solution.py:317
  42.4 27.6 %collective-permute-start.13 = (bf16[1344,256]{1,0:T(8,128)(2,1)S(1)}, bf16[1344,256]{1,0:T(8,128)(2,1)S(1)}, u32[]{:S(2)}, u32[]{:S(2)}) collective-permute-start(bf16[1344,256]{1,0:T(8,128)(2,1)S(1)} %pad_maximum_fusion.2.refs_0_), channel_id=1, source_target_pairs={{0,4},{4,0},{8,12},{12,8},{16,20},{20,16},{24,28},{28,24},{1,5},{5... | collective-permute-start | bytes 2064392 | tf_op jit(solution)/shard_map/ppermute | solution.py:313
  58.3 2.9 %collective-permute-start.14 = (bf16[512,256]{1,0:T(8,128)(2,1)S(1)}, bf16[512,256]{1,0:T(8,128)(2,1)S(1)}, u32[]{:S(2)}, u32[]{:S(2)}) collective-permute-start(bf16[512,256]{1,0:T(8,128)(2,1)S(1)} %get-tuple-element.59.refs_0_), channel_id=1, source_target_pairs={{0,4},{4,0},{8,12},{12,8},{16,20},{20,16},{24,28},{28,24},{1,5},{5... | collective-permute-start | bytes 786440 | tf_op jit(solution)/shard_map/ppermute | solution.py:313
  59.0 14.7 %collective-permute-start.16 = (bf16[256,1024]{1,0:T(8,128)(2,1)}, bf16[256,1024]{1,0:T(8,128)(2,1)}, u32[]{:S(2)}, u32[]{:S(2)}) collective-permute-start(bf16[256,1024]{1,0:T(8,128)(2,1)} %collective-permute-done.2.own_ref), channel_id=1, source_target_pairs={{0,2},{1,3},{2,0},{3,1},{4,6},{5,7},{6,4},{7,5},{8,10},{9,11},{10,... | collective-permute-start | bytes 1572872 | tf_op jit(solution)/shard_map/ppermute | solution.py:317
  59.6 15.7 %collective-permute-start.12 = (bf16[256,1024]{1,0:T(8,128)(2,1)}, bf16[256,1024]{1,0:T(8,128)(2,1)}, u32[]{:S(2)}, u32[]{:S(2)}) collective-permute-start(bf16[256,1024]{1,0:T(8,128)(2,1)} %collective-permute-done.2.own_ref), channel_id=1, source_target_pairs={{0,1},{1,0},{2,3},{3,2},{4,5},{5,4},{6,7},{7,6},{8,9},{9,8},{10,11... | collective-permute-start | bytes 1572872 | tf_op jit(solution)/shard_map/ppermute | solution.py:317
  61.2 28.7 %collective-permute-start.7 = (bf16[1344,256]{1,0:T(8,128)(2,1)}, bf16[1344,256]{1,0:T(8,128)(2,1)S(1)}, u32[]{:S(2)}, u32[]{:S(2)}) collective-permute-start(bf16[1344,256]{1,0:T(8,128)(2,1)} %pad_maximum_fusion), channel_id=1, source_target_pairs={{0,24},{4,28},{8,0},{12,4},{16,8},{20,12},{24,16},{28,20},{1,25},{... | collective-permute-start | bytes 2064392 | tf_op jit(solution)/shard_map/ppermute | solution.py:309
  62.0 27.4 %collective-permute-start.3 = (bf16[256,1024]{1,0:T(8,128)(2,1)}, bf16[256,1024]{1,0:T(8,128)(2,1)}, u32[]{:S(2)}, u32[]{:S(2)}) collective-permute-start(bf16[256,1024]{1,0:T(8,128)(2,1)} %collective-permute-done.2.own_ref), channel_id=1, source_target_pairs={{0,8},{4,12},{8,16},{12,20},{16,24},{20,28},{24,0},{28,4},{1,9},{5... | collective-permute-start | bytes 1572872 | tf_op jit(solution)/shard_map/ppermute | solution.py:309
  64.1 115.2 %copy-start.17 = (s32[3]{0:T(128)}, s32[3]{0:T(128)S(1)}, u32[]{:S(2)}) copy-start(s32[3]{0:T(128)S(1)} %pad_add_fusion.place_ref) | copy-start | bytes 40
  74.7 15.3 %collective-permute-start.17 = (bf16[128,1024]{1,0:T(8,128)(2,1)S(1)}, bf16[128,1024]{1,0:T(8,128)(2,1)S(1)}, u32[]{:S(2)}, u32[]{:S(2)}) collective-permute-start(bf16[128,1024]{1,0:T(8,128)(2,1)S(1)} %slice.35), channel_id=1, source_target_pairs={{0,1},{1,0},{2,3},{3,2},{4,5},{5,4},{6,7},{7,6},{8,9},{9,8},{10,11... | collective-permute-start | bytes 786440 | tf_op jit(solution)/shard_map/ppermute | solution.py:317
  76.2 37.0 %copy-start.19 = (bf16[512,256]{1,0:T(8,128)(2,1)S(1)}, bf16[512,256]{1,0:T(8,128)(2,1)}, u32[]{:S(2)}) copy-start(bf16[512,256]{1,0:T(8,128)(2,1)} %get-tuple-element.57) | copy-start | bytes 786436
  76.3 37.0 %copy-start.20 = (bf16[512,256]{1,0:T(8,128)(2,1)S(1)}, bf16[512,256]{1,0:T(8,128)(2,1)}, u32[]{:S(2)}) copy-start(bf16[512,256]{1,0:T(8,128)(2,1)} %get-tuple-element.68) | copy-start | bytes 786436
  76.3 36.9 %copy-start.26 = (bf16[160,256]{1,0:T(8,128)(2,1)S(1)}, bf16[160,256]{1,0:T(8,128)(2,1)}, u32[]{:S(2)}) copy-start(bf16[160,256]{1,0:T(8,128)(2,1)} %get-tuple-element.73) | copy-start | bytes 245764
  76.3 36.9 %copy-start.27 = (bf16[160,256]{1,0:T(8,128)(2,1)S(1)}, bf16[160,256]{1,0:T(8,128)(2,1)}, u32[]{:S(2)}) copy-start(bf16[160,256]{1,0:T(8,128)(2,1)} %get-tuple-element.80) | copy-start | bytes 245764
  76.3 13.7 %collective-permute-start.15 = (bf16[128,1024]{1,0:T(8,128)(2,1)S(1)}, bf16[128,1024]{1,0:T(8,128)(2,1)S(1)}, u32[]{:S(2)}, u32[]{:S(2)}) collective-permute-start(bf16[128,1024]{1,0:T(8,128)(2,1)S(1)} %slice.34), channel_id=1, source_target_pairs={{0,2},{1,3},{2,0},{3,1},{4,6},{5,7},{6,4},{7,5},{8,10},{9,11},{10,... | collective-permute-start | bytes 786440 | tf_op jit(solution)/shard_map/ppermute | solution.py:317
  90.0 12.6 %collective-permute-start.22 = (bf16[256,1024]{1,0:T(8,128)(2,1)}, bf16[256,1024]{1,0:T(8,128)(2,1)S(1)}, u32[]{:S(2)}, u32[]{:S(2)}) collective-permute-start(bf16[256,1024]{1,0:T(8,128)(2,1)} %collective-permute-done.3.own_ref), channel_id=1, source_target_pairs={{0,2},{1,3},{2,0},{3,1},{4,6},{5,7},{6,4},{7,5},{8,10},{9,11},{10,... | collective-permute-start | bytes 1572872 | tf_op jit(solution)/shard_map/ppermute | solution.py:317
  91.3 13.4 %collective-permute-start.18 = (bf16[256,1024]{1,0:T(8,128)(2,1)}, bf16[256,1024]{1,0:T(8,128)(2,1)S(1)}, u32[]{:S(2)}, u32[]{:S(2)}) collective-permute-start(bf16[256,1024]{1,0:T(8,128)(2,1)} %collective-permute-done.3.own_ref), channel_id=1, source_target_pairs={{0,1},{1,0},{2,3},{3,2},{4,5},{5,4},{6,7},{7,6},{8,9},{9,8},{10,11... | collective-permute-start | bytes 1572872 | tf_op jit(solution)/shard_map/ppermute | solution.py:317
  92.8 3.8 %collective-permute-start.19 = (bf16[512,256]{1,0:T(8,128)(2,1)S(1)}, bf16[512,256]{1,0:T(8,128)(2,1)S(1)}, u32[]{:S(2)}, u32[]{:S(2)}) collective-permute-start(bf16[512,256]{1,0:T(8,128)(2,1)S(1)} %copy-done.8), channel_id=1, source_target_pairs={{0,4},{4,0},{8,12},{12,8},{16,20},{20,16},{24,28},{28,24},{1,5},{5... | collective-permute-start | bytes 786440 | tf_op jit(solution)/shard_map/ppermute | solution.py:313
  92.8 3.8 %collective-permute-start.20 = (bf16[512,256]{1,0:T(8,128)(2,1)S(1)}, bf16[512,256]{1,0:T(8,128)(2,1)S(1)}, u32[]{:S(2)}, u32[]{:S(2)}) collective-permute-start(bf16[512,256]{1,0:T(8,128)(2,1)S(1)} %copy-done.10), channel_id=1, source_target_pairs={{0,4},{4,0},{8,12},{12,8},{16,20},{20,16},{24,28},{28,24},{1,5},{5... | collective-permute-start | bytes 786440 | tf_op jit(solution)/shard_map/ppermute | solution.py:313
  93.3 15.9 %collective-permute-start.4 = (bf16[256,1024]{1,0:T(8,128)(2,1)}, bf16[256,1024]{1,0:T(8,128)(2,1)S(1)}, u32[]{:S(2)}, u32[]{:S(2)}) collective-permute-start(bf16[256,1024]{1,0:T(8,128)(2,1)} %collective-permute-done.3.own_ref), channel_id=1, source_target_pairs={{0,8},{4,12},{8,16},{12,20},{16,24},{20,28},{24,0},{28,4},{1,9},{5... | collective-permute-start | bytes 1572872 | tf_op jit(solution)/shard_map/ppermute | solution.py:309
  102.6 6.9 %collective-permute-start.23 = (bf16[128,1024]{1,0:T(8,128)(2,1)S(1)}, bf16[128,1024]{1,0:T(8,128)(2,1)S(1)}, u32[]{:S(2)}, u32[]{:S(2)}) collective-permute-start(bf16[128,1024]{1,0:T(8,128)(2,1)S(1)} %slice.37), channel_id=1, source_target_pairs={{0,1},{1,0},{2,3},{3,2},{4,5},{5,4},{6,7},{7,6},{8,9},{9,8},{10,11... | collective-permute-start | bytes 786440 | tf_op jit(solution)/shard_map/ppermute | solution.py:317
  104.7 6.5 %collective-permute-start.21 = (bf16[128,1024]{1,0:T(8,128)(2,1)S(1)}, bf16[128,1024]{1,0:T(8,128)(2,1)S(1)}, u32[]{:S(2)}, u32[]{:S(2)}) collective-permute-start(bf16[128,1024]{1,0:T(8,128)(2,1)S(1)} %slice.36), channel_id=1, source_target_pairs={{0,2},{1,3},{2,0},{3,1},{4,6},{5,7},{6,4},{7,5},{8,10},{9,11},{10,... | collective-permute-start | bytes 786440 | tf_op jit(solution)/shard_map/ppermute | solution.py:317
  105.9 12.8 %collective-permute-start.25 = (bf16[1344,256]{1,0:T(8,128)(2,1)S(1)}, bf16[1344,256]{1,0:T(8,128)(2,1)S(1)}, u32[]{:S(2)}, u32[]{:S(2)}) collective-permute-start(bf16[1344,256]{1,0:T(8,128)(2,1)S(1)} %collective-permute-done.6.refs_1_), channel_id=1, source_target_pairs={{0,4},{4,0},{8,12},{12,8},{16,20},{20,16},{24,28},{28,24},{1,5},{5... | collective-permute-start | bytes 2064392 | tf_op jit(solution)/shard_map/ppermute | solution.py:313
  111.2 11.7 %collective-permute-start.26 = (bf16[256,1024]{1,0:T(8,128)(2,1)S(1)}, bf16[256,1024]{1,0:T(8,128)(2,1)S(1)}, u32[]{:S(2)}, u32[]{:S(2)}) collective-permute-start(bf16[256,1024]{1,0:T(8,128)(2,1)S(1)} %collective-permute-done.4.own_ref), channel_id=1, source_target_pairs={{0,2},{1,3},{2,0},{3,1},{4,6},{5,7},{6,4},{7,5},{8,10},{9,11},{10,... | collective-permute-start | bytes 1572872 | tf_op jit(solution)/shard_map/ppermute | solution.py:317
  112.8 11.2 %collective-permute-start.24 = (bf16[256,1024]{1,0:T(8,128)(2,1)S(1)}, bf16[256,1024]{1,0:T(8,128)(2,1)S(1)}, u32[]{:S(2)}, u32[]{:S(2)}) collective-permute-start(bf16[256,1024]{1,0:T(8,128)(2,1)S(1)} %collective-permute-done.4.own_ref), channel_id=1, source_target_pairs={{0,1},{1,0},{2,3},{3,2},{4,5},{5,4},{6,7},{7,6},{8,9},{9,8},{10,11... | collective-permute-start | bytes 1572872 | tf_op jit(solution)/shard_map/ppermute | solution.py:317
  113.3 30.7 %collective-permute-start.30 = (bf16[1344,256]{1,0:T(8,128)(2,1)S(1)}, bf16[1344,256]{1,0:T(8,128)(2,1)S(1)}, u32[]{:S(2)}, u32[]{:S(2)}) collective-permute-start(bf16[1344,256]{1,0:T(8,128)(2,1)S(1)} %pad_maximum_fusion.3), channel_id=1, source_target_pairs={{0,16},{4,20},{8,24},{12,28},{16,0},{20,4},{24,8},{28,12},{1,17},{... | collective-permute-start | bytes 2064392 | tf_op jit(solution)/shard_map/ppermute | solution.py:309
  122.9 21.0 %collective-permute-start.28 = (bf16[128,1024]{1,0:T(8,128)(2,1)S(1)}, bf16[128,1024]{1,0:T(8,128)(2,1)S(1)}, u32[]{:S(2)}, u32[]{:S(2)}) collective-permute-start(bf16[128,1024]{1,0:T(8,128)(2,1)S(1)} %slice.39), channel_id=1, source_target_pairs={{0,1},{1,0},{2,3},{3,2},{4,5},{5,4},{6,7},{7,6},{8,9},{9,8},{10,11... | collective-permute-start | bytes 786440 | tf_op jit(solution)/shard_map/ppermute | solution.py:317
  124.0 19.9 %collective-permute-start.27 = (bf16[128,1024]{1,0:T(8,128)(2,1)S(1)}, bf16[128,1024]{1,0:T(8,128)(2,1)S(1)}, u32[]{:S(2)}, u32[]{:S(2)}) collective-permute-start(bf16[128,1024]{1,0:T(8,128)(2,1)S(1)} %slice.38), channel_id=1, source_target_pairs={{0,2},{1,3},{2,0},{3,1},{4,6},{5,7},{6,4},{7,5},{8,10},{9,11},{10,... | collective-permute-start | bytes 786440 | tf_op jit(solution)/shard_map/ppermute | solution.py:317
  126.0 22.3 %collective-permute-start.32 = (bf16[1344,256]{1,0:T(8,128)(2,1)S(1)}, bf16[1344,256]{1,0:T(8,128)(2,1)S(1)}, u32[]{:S(2)}, u32[]{:S(2)}) collective-permute-start(bf16[1344,256]{1,0:T(8,128)(2,1)S(1)} %collective-permute-done.7.refs_3_), channel_id=1, source_target_pairs={{0,4},{4,0},{8,12},{12,8},{16,20},{20,16},{24,28},{28,24},{1,5},{5... | collective-permute-start | bytes 2064392 | tf_op jit(solution)/shard_map/ppermute | solution.py:313
  143.9 4.4 %collective-permute-start.31 = (bf16[1344,256]{1,0:T(8,128)(2,1)S(1)}, bf16[1344,256]{1,0:T(8,128)(2,1)S(1)}, u32[]{:S(2)}, u32[]{:S(2)}) collective-permute-start(bf16[1344,256]{1,0:T(8,128)(2,1)S(1)} %collective-permute-done.30.refs_2_), channel_id=1, source_target_pairs={{0,4},{4,0},{8,12},{12,8},{16,20},{20,16},{24,28},{28,24},{1,5},{5... | collective-permute-start | bytes 2064392 | tf_op jit(solution)/shard_map/ppermute | solution.py:313
  145.9 15.3 %collective-permute-start.29 = (bf16[512,256]{1,0:T(8,128)(2,1)S(1)}, bf16[512,256]{1,0:T(8,128)(2,1)S(1)}, u32[]{:S(2)}, u32[]{:S(2)}) collective-permute-start(bf16[512,256]{1,0:T(8,128)(2,1)S(1)} %copy-done.36), channel_id=1, source_target_pairs={{0,16},{4,20},{8,24},{12,28},{16,0},{20,4},{24,8},{28,12},{1,17},{... | collective-permute-start | bytes 786440 | tf_op jit(solution)/shard_map/ppermute | solution.py:309
  153.5 10.4 %collective-permute-start.34 = (bf16[4,256,256]{2,1,0:T(8,128)(2,1)S(1)}, bf16[4,256,256]{2,1,0:T(8,128)(2,1)S(1)}, u32[]{:S(2)}, u32[]{:S(2)}) collective-permute-start(bf16[4,256,256]{2,1,0:T(8,128)(2,1)S(1)} %get-tuple-element.50.k_ref), channel_id=1, source_target_pairs={{0,4},{4,0},{8,12},{12,8},{16,20},{20,16},{24,28},{28,24},{1,5},{5... | collective-permute-start | bytes 1572872 | tf_op jit(solution)/shard_map/ppermute | solution.py:313
  154.2 9.8 %collective-permute-start.35 = (bf16[4,256,256]{2,1,0:T(8,128)(2,1)S(1)}, bf16[4,256,256]{2,1,0:T(8,128)(2,1)S(1)}, u32[]{:S(2)}, u32[]{:S(2)}) collective-permute-start(bf16[4,256,256]{2,1,0:T(8,128)(2,1)S(1)} %get-tuple-element.52.v_ref), channel_id=1, source_target_pairs={{0,4},{4,0},{8,12},{12,8},{16,20},{20,16},{24,28},{28,24},{1,5},{5... | collective-permute-start | bytes 1572872 | tf_op jit(solution)/shard_map/ppermute | solution.py:313
  161.2 1.5 collective-permute-start.33
  168.1 11.1 %collective-permute-start.36 = (bf16[256,256]{1,0:T(8,128)(2,1)S(1)}, bf16[256,256]{1,0:T(8,128)(2,1)S(1)}, u32[]{:S(2)}, u32[]{:S(2)}) collective-permute-start(bf16[256,256]{1,0:T(8,128)(2,1)S(1)} %attend.3), channel_id=1, source_target_pairs={{0,16},{4,20},{8,24},{12,28},{16,0},{20,4},{24,8},{28,12},{1,17},{... | collective-permute-start | bytes 393224 | tf_op jit(solution)/shard_map/ppermute | solution.py:309
  175.3 8.2 %collective-permute-start.37 = (bf16[256,256]{1,0:T(8,128)(2,1)S(1)}, bf16[256,256]{1,0:T(8,128)(2,1)S(1)}, u32[]{:S(2)}, u32[]{:S(2)}) collective-permute-start(bf16[256,256]{1,0:T(8,128)(2,1)S(1)} %get-tuple-element.54), channel_id=1, source_target_pairs={{0,8},{4,12},{8,16},{12,20},{16,24},{20,28},{24,0},{28,4},{1,9},{5... | collective-permute-start | bytes 393224 | tf_op jit(solution)/shard_map/ppermute | solution.py:309
  175.4 9.5 %collective-permute-start.38 = (bf16[256,256]{1,0:T(8,128)(2,1)S(1)}, bf16[256,256]{1,0:T(8,128)(2,1)S(1)}, u32[]{:S(2)}, u32[]{:S(2)}) collective-permute-start(bf16[256,256]{1,0:T(8,128)(2,1)S(1)} %get-tuple-element.56), channel_id=1, source_target_pairs={{0,24},{4,28},{8,0},{12,4},{16,8},{20,12},{24,16},{28,20},{1,25},{... | collective-permute-start | bytes 393224 | tf_op jit(solution)/shard_map/ppermute | solution.py:309
  (32 other events, 267.7 us)

commit v3 on v2

--- a/solution.py
+++ b/solution.py
@@ -260,24 +260,24 @@
     )(place, q, k, v, k_sib, v_sib, ck, cv)
 
 
-def pack_kernel(at, crow, *refs):
-    parcels, (out_ref, scratch) = refs[:-2], refs[-2:]
-    for i, piece in enumerate(parcels):
-        band = piece[at : at + crow + PAD].astype(F32)
-        scratch[i * crow : (i + 1) * crow, :] = band[:crow]
-    out_ref[...] = scratch[...].astype(BF16)
-
-
-def pack(parcels, at, crow):
-    cols = parcels[0].shape[1]
-    out = (len(parcels) * crow, cols)
+def pack_kernel(places, crow, *refs):
+    parcels, outs, scratch = refs[: len(places)], refs[len(places) : -1], refs[-1]
+    for n, out_ref in enumerate(outs):
+        for i, (piece, at) in enumerate(zip(parcels, places)):
+            at += n * (crow + PAD)
+            scratch[i * crow : (i + 1) * crow, :] = piece[at : at + crow + PAD].astype(F32)[:crow]
+        out_ref[...] = scratch[...].astype(BF16)
+
+
+def pack(parcels, places, crow):
+    out = (len(parcels) * crow, parcels[0].shape[1])
     return pl.pallas_call(
-        functools.partial(pack_kernel, at, crow),
+        functools.partial(pack_kernel, places, crow),
         in_specs=[VMEM] * len(parcels),
-        out_specs=VMEM,
-        out_shape=jax.ShapeDtypeStruct(out, BF16),
+        out_specs=[VMEM] * 2,
+        out_shape=[jax.ShapeDtypeStruct(out, BF16)] * 2,
         scratch_shapes=[pltpu.VMEM(out, F32)],
-        compiler_params=pltpu.CompilerParams(vmem_limit_bytes=24 * MIB),
+        compiler_params=pltpu.CompilerParams(vmem_limit_bytes=12 * MIB),
         cost_estimate=BRIEF,
         name="pack",
     )(*parcels)
@@ -336,13 +336,15 @@
     w_t = jnp.transpose(w_qkv, (1, 0, 2))
     caches = [jnp.pad(c, ((0, PAD), (0, 0))) for c in (cache_k, cache_v)]
 
-    def parcel(kind, r):
+    def parcel(kind, r, *others):
         at = (z + r) % zs * cols
+        source = after(w_t, *others) if others else w_t
         parts = [
-            lax.dynamic_slice(w_t, (p, 0, at), (1, depth, cols))[0]
-            for p in ((1, 2) if kind == "kv" else (0,))
+            lax.dynamic_slice(source, ("qkv".index(p), 0, at), (1, depth, cols))[0]
+            for p in kind
+            if p != "c"
         ]
-        if kind == "kv":
+        if "c" in kind:
             parts += [lax.dynamic_slice_in_dim(c, at, cols, 1) for c in caches]
         return jnp.concatenate(parts, axis=0)
 
@@ -351,12 +353,16 @@
     halo = lax.ppermute(tail, "seq", [(s, s + 1) for s in range(seqs - 1)])
     halo = jnp.where(my_seq == 0, jnp.pad(prior_kv, ((taps - prior_kv.shape[0], 0), (0, 0))), halo)
 
-    order = [("q", 1), ("q", 3), "acts", ("kv", 1), "acts", ("kv", 3), "acts", ("kv", 2), ("q", 2)]
-    here = {(kind, 0): parcel(kind, 0) for kind in ("kv", "q")}
+    order = ["q1", "q3", "acts", "kvc1", "acts", "kvc3", "acts", "q2", "kc2", "v2"]
     acts = [hyena(hin, halo, filters)]
+    here = {kind + "0": parcel(kind, 0, acts[0]) for kind in ("kvc", "q")}
     sent = []
     for n, item in enumerate(order):
-        value, steps = (acts[-1], 1) if item == "acts" else (parcel(*item), item[1])
+        if item == "acts":
+            value, steps = acts[-1], 1
+        else:
+            kind, steps = item[:-1], int(item[-1])
+            value = parcel(kind, steps, *acts[: int(n >= 2)])
         if n >= 2:
             value = after(value, sent[n - 2])
         sent.append(shift_z(value, steps, zs))
@@ -364,37 +370,39 @@
             acts.append(sent[-1])
         else:
             here[item] = sent[-1]
-    late = [("kv", 2), ("q", 2)]
+    late = ["q2", "kc2", "v2"]
     there = {item: swap_core(here[item], zs) for item in here if item not in late}
 
-    pace = [[("q", 1), ("q", 3)], [("kv", 1)], [("kv", 3)], []]
-    swapped = [[], [("kv", 0), ("q", 0)], [("q", 1), ("q", 3)], [("kv", 1)]]
+    pace = [[], ["kvc1"], ["kvc3"], ["q2"]]
+    swapped = [[], ["kvc0", "q0"], ["q1", "q3"], ["kvc1"]]
     gain4 = gain.reshape(4, 1, width)
     half = rows // 2
     normed, diag0, diag1 = None, None, None
     for j, own in enumerate(acts):
-        own = after(own, *[here[item] for item in pace[j]], *([diag0, diag1] if j else []))
+        own = after(own, *([diag0, diag1] if j else [here["q1"], here["q3"]]))
         from_x, from_y = swap_chan(own, 1), swap_chan(own, 2)
         if j:
-            settled = [normed] + [there[item] for item in swapped[j]]
+            settled = [normed] + [there[item] for item in swapped[j]] + [here[item] for item in pace[j]]
             from_x, from_y = after(from_x, *settled), after(from_y, *settled)
         diag0 = swap_chan(from_x[:half], 2)
         diag1 = swap_chan(from_y[half:], 1)
         normed = norm(place, j, zs, own, from_x, from_y, diag0, diag1, gain4, normed)
 
-    def sides(kind, shifts):
-        return [[side[kind, r] for r in shifts] for side in (here, there)]
-
-    every = tuple(range(zs))
-    early = tuple(r for r in every if r != 2)
-    (q_early,) = project(place, normed, *sides("q", early), early, 1, False)
-    there["kv", 2] = swap_core(after(here["kv", 2], diag0, diag1), zs)
-    mine, theirs = sides("kv", every)
-    ck, cv = [pack(mine + theirs, 2 * depth + i * (crow + PAD), crow) for i in range(2)]
-    k, v = project(place, after(normed, ck, cv, q_early), mine, theirs, every, 2, True)
-    k_sib, v_sib = swap_core(k, zs), swap_core(v, zs)
-    there["q", 2] = swap_core(after(here["q", 2], k), zs)
-    (q,) = project(place, normed, *sides("q", (2,)), (2,), 1, True, (q_early,))
+    def sides(*items):
+        return [[side[item] for item in items] for side in (here, there)]
+
+    early = (0, 1, 3)
+    there["q2"] = swap_core(after(here["q2"], diag0, diag1), zs)
+    there["kc2"] = swap_core(after(here["kc2"], diag0, diag1), zs)
+    (q,) = project(place, normed, *sides("q0", "q1", "q3", "q2"), early + (2,), 1, True)
+    k_early, v_early = project(place, normed, *sides("kvc0", "kvc1", "kvc3"), early, 2, False)
+    kept = sum(sides("kvc0", "kvc1", "kc2", "kvc3"), [])
+    ck, cv = pack(kept, [depth if i % zs == 2 else 2 * depth for i in range(2 * zs)], crow)
+    (k,) = project(place, after(normed, q, ck), *sides("kc2"), (2,), 1, True, (k_early,))
+    k_sib = swap_core(k, zs)
+    there["v2"] = swap_core(after(here["v2"], k), zs)
+    (v,) = project(place, normed, *sides("v2"), (2,), 1, True, (v_early,))
+    v_sib = swap_core(v, zs)
     pieces, out = {}, None
     for shifts, wait in (((2,), ()), ((1, 3), ()), ((0,), (2,))):
         ready = q if out is None else after(q, out[0], *[pieces[r] for r in wait])

time: 188 us -> 170 us (0.904)
  waiting for transfers between devices: 91.6 us -> 78.9 us
  local copies, waits for them, and re-layouts: 14.6 us -> 11.7 us
  starting transfers between devices: 38.8 us -> 36.2 us
    ppermute x16, waiting for transfers between devices: 25.7 us -> 11.5 us  [swap_chan(): return lax.ppermute(value, 'chan', [(c, c ^ bit) for c in range(4)])]
    ppermute x10 -> x11, waiting for transfers between devices: 1.56 us -> 5.5 us  [swap_core(): lax.ppermute(value, 'seq', [(2 * a + k, 2 * a + 1 - k) for a in range(zs)...]
    ppermute x12 -> x13, waiting for transfers between devices: 64.4 us -> 61.9 us  [shift_z(): return lax.ppermute(value, 'seq', pairs)]
    unnamed x82 -> x62, local copies, waits for them, and re-layouts: 8.24 us -> 6.76 us
    pallas_call x3 -> x4, Pallas kernels: 8.69 us -> 9.86 us  [project(): pl.pallas_call(functools.partial(project_kernel, shifts, zs, count), in_s...]
    ppermute x12 -> x13, starting transfers between devices: 15.5 us -> 14.5 us  [shift_z(): return lax.ppermute(value, 'seq', pairs)]
  transfers between devices with their start and end apart: 39 -> 41, of which waited for: 17 -> 20; matrix products, arithmetic and copies ran while one was open for 4% -> 4% of each run, Pallas kernels for 18% -> 20%
where the time goes in v3:
time: 170 us
  waiting for transfers between devices  78.9 us (46%)
  Pallas kernels  40.1 us (24%)
  starting transfers between devices  36.2 us (21%)
  local copies, waits for them, and re-layouts  11.7 us (7%)
  other arithmetic  2.46 us (1%)
    ppermute x13, waiting for transfers between devices, shift_z(): return lax.ppermute(value, 'seq', pairs)  61.9 us
    ppermute x16, starting transfers between devices, swap_chan(): return lax.ppermute(value, 'chan', [(c, c ^ bit) for c in range(4)])  17.5 us
    ppermute x13, starting transfers between devices, shift_z(): return lax.ppermute(value, 'seq', pairs)  14.5 us
    pallas_call x3, Pallas kernels, attend(): pl.pallas_call(functools.partial(attend_kernel, shifts), in_specs=[SMEM]...  13.9 us
    ppermute x16, waiting for transfers between devices, swap_chan(): return lax.ppermute(value, 'chan', [(c, c ^ bit) for c in range(4)])  11.5 us
    pallas_call x4, Pallas kernels, project(): pl.pallas_call(functools.partial(project_kernel, shifts, zs, count), in_s...  9.86 us
    pallas_call x4, Pallas kernels, norm(): pl.pallas_call(functools.partial(norm_kernel, j), in_specs=[SMEM] + [VMEM...  8.27 us
    unnamed x62, local copies, waits for them, and re-layouts  6.76 us
  transfers between devices with their start and end apart: 41, of which 20 were waited for; matrix products, arithmetic and copies ran while one was open for 4% of the time, Pallas kernels for 20%

profile of v3, /device:TPU:0, one launch (start us, length us, event | category | flops | bytes accessed | tf_op | source)
XLA Modules:
  0.0 169.8 jit_solution(1897811494117859011)
XLA Ops:
  0.0 1.2 fusion
  1.2 2.4 %collective-permute-start = (bf16[128,1024]{1,0:T(8,128)(2,1)S(1)}, bf16[128,1024]{1,0:T(8,128)(2,1)S(1)}, u32[]{:S(2)}, u32[]{:S(2)}) collective-permute-start(bf16[128,1024]{1,0:T(8,128)(2,1)S(1)} %fusion), channel_id=1, source_target_pairs={{0,4},{4,8},{8,12},{12,16},{16,20},{20,24},{24,28},{1,5},{5,9},{9,... | collective-permute-start | bytes 786440 | tf_op jit(solution)/shard_map/ppermute | solution.py:353
  3.7 1.9 %dynamic-slice_bitcast_fusion.10 = (bf16[512,256]{1,0:T(8,128)(2,1)}, bf16[512,256]{1,0:T(8,128)(2,1)}) fusion(bf16[512,3,1024]{2,0,1:T(8,128)(2,1)} %param.11, s32[]{:T(128)S(6)} %select_n.80, s32[]{:T(128)S(6)} %select_n.78), kind=kLoop, calls=%fused_computation.16 | loop fusion | bytes 1048584 | tf_op jit(solution)/shard_map/squeeze | solution.py:343
  5.6 4.6 %collective-permute-start.5 = (bf16[512,256]{1,0:T(8,128)(2,1)}, bf16[512,256]{1,0:T(8,128)(2,1)S(1)}, u32[]{:S(2)}, u32[]{:S(2)}) collective-permute-start(bf16[512,256]{1,0:T(8,128)(2,1)} %get-tuple-element.77), channel_id=1, source_target_pairs={{0,24},{4,28},{8,0},{12,4},{16,8},{20,12},{24,16},{28,20},{1,25},{... | collective-permute-start | bytes 786440 | tf_op jit(solution)/shard_map/ppermute | solution.py:309
  10.3 6.0 %hyena_filters.1.own_ref = bf16[256,1024]{1,0:T(8,128)(2,1)S(1)} custom-call(bf16[3,256,1024]{2,1,0:T(8,128)(2,1)S(1)} %bitcast.33, bf16[128,1024]{1,0:T(8,128)(2,1)S(1)} %pad_select_fusion.halo_ref, f32[64,128]{1,0:T(8,128)S(1)} %copy-done.16), custom_call_target="tpu_custom_call" | custom-call | flops 1 | bytes 1 | tf_op jit(solution)/shard_map/hyena_filters/pallas_call | solution.py:80
  17.3 5.6 %collective-permute-done.1.refs_1_ = bf16[512,256]{1,0:T(8,128)(2,1)S(1)} collective-permute-done((bf16[512,256]{1,0:T(8,128)(2,1)}, bf16[512,256]{1,0:T(8,128)(2,1)S(1)}, u32[]{:S(2)}, u32[]{:S(2)}) %collective-permute-start.1) | collective-permute-done | bytes 262176 | tf_op jit(solution)/shard_map/ppermute | solution.py:309
  22.9 1.5 collective-permute-start.6
  24.4 1.5 collective-permute-start.8
  27.2 1.2 dynamic-slice_bitcast_fusion
  29.4 1.4 collective-permute-start.13
  30.7 6.5 %collective-permute-done.6.x_ref = bf16[256,1024]{1,0:T(8,128)(2,1)S(1)} collective-permute-done((bf16[256,1024]{1,0:T(8,128)(2,1)S(1)}, bf16[256,1024]{1,0:T(8,128)(2,1)S(1)}, u32[]{:S(2)}, u32[]{:S(2)}) %collective-permute-start.6) | collective-permute-done | bytes 524320 | tf_op jit(solution)/shard_map/ppermute | solution.py:317
  37.3 1.6 collective-permute-start.7
  38.9 1.6 collective-permute-start.9
  40.6 2.8 %collective-permute-done.2.own_ref = bf16[256,1024]{1,0:T(8,128)(2,1)} collective-permute-done((bf16[256,1024]{1,0:T(8,128)(2,1)S(1)}, bf16[256,1024]{1,0:T(8,128)(2,1)}, u32[]{:S(2)}, u32[]{:S(2)}) %collective-permute-start.2) | collective-permute-done | bytes 524320 | tf_op jit(solution)/shard_map/ppermute | solution.py:309
  43.4 2.0 %collective-permute-done.7.d0_ref = bf16[128,1024]{1,0:T(8,128)(2,1)S(1)} collective-permute-done((bf16[128,1024]{1,0:T(8,128)(2,1)S(1)}, bf16[128,1024]{1,0:T(8,128)(2,1)S(1)}, u32[]{:S(2)}, u32[]{:S(2)}) %collective-permute-start.7) | collective-permute-done | bytes 262176 | tf_op jit(solution)/shard_map/ppermute | solution.py:317
  47.4 1.1 collective-permute-start.15
  48.5 1.3 collective-permute-start.10
  49.8 1.7 collective-permute-done.12.refs_4_
  51.5 1.0 copy-done.2
  52.6 1.0 copy-done.4
  55.5 1.9 %norm.4.rest_0_ = bf16[4,4,256,1024]{3,2,1,0:T(8,128)(2,1)S(1)} custom-call(s32[3]{0:T(128)S(1)} %pad_add_fusion.place_ref, bf16[256,1024]{1,0:T(8,128)(2,1)S(1)} %hyena_filters.1.own_ref, bf16[256,1024]{1,0:T(8,128)(2,1)S(1)} %copy-done.2, bf16[256,1024]{1,0:T(8,128)(2,1)S(1)} %copy-done.4, bf16[128,1024]{1,0:T(8,128)(2,1)S(1)} %copy-done.12, ...), custom_call_target="tpu_custom_call" | custom-call | flops 1 | bytes 1 | tf_op jit(solution)/shard_map/norm/pallas_call | solution.py:119
  57.7 2.3 %collective-permute-done.15.y_ref = bf16[256,1024]{1,0:T(8,128)(2,1)S(1)} collective-permute-done((bf16[256,1024]{1,0:T(8,128)(2,1)}, bf16[256,1024]{1,0:T(8,128)(2,1)S(1)}, u32[]{:S(2)}, u32[]{:S(2)}) %collective-permute-start.15) | collective-permute-done | bytes 524320 | tf_op jit(solution)/shard_map/ppermute | solution.py:317
  60.1 1.6 collective-permute-start.16
  62.6 1.3 collective-permute-start.14
  65.0 4.0 %collective-permute-done.3.own_ref = bf16[256,1024]{1,0:T(8,128)(2,1)S(1)} collective-permute-done((bf16[256,1024]{1,0:T(8,128)(2,1)}, bf16[256,1024]{1,0:T(8,128)(2,1)S(1)}, u32[]{:S(2)}, u32[]{:S(2)}) %collective-permute-start.3) | collective-permute-done | bytes 524320 | tf_op jit(solution)/shard_map/ppermute | solution.py:309
  69.0 1.2 collective-permute-start.22
  72.3 2.6 %norm.5.rest_0_ = bf16[4,4,256,1024]{3,2,1,0:T(8,128)(2,1)S(1)} custom-call(s32[3]{0:T(128)S(1)} %pad_add_fusion.place_ref, bf16[256,1024]{1,0:T(8,128)(2,1)} %collective-permute-done.2.own_ref, bf16[256,1024]{1,0:T(8,128)(2,1)} %collective-permute-done.10.x_ref, ...), custom_call_target="tpu_custom_call", output_to_operand_aliasing={{}: (7, {})} | custom-call | flops 1 | bytes 1 | tf_op jit(solution)/shard_map/norm/pallas_call | solution.py:119
  74.9 8.9 %collective-permute-done.20.refs_3_.refs_2_ = bf16[1344,256]{1,0:T(8,128)(2,1)S(1)} collective-permute-done((bf16[1344,256]{1,0:T(8,128)(2,1)S(1)}, bf16[1344,256]{1,0:T(8,128)(2,1)S(1)}, u32[]{:S(2)}, u32[]{:S(2)}) %collective-permute-start.20) | collective-permute-done | bytes 688160 | tf_op jit(solution)/shard_map/ppermute | solution.py:309
  84.9 9.4 %collective-permute-done.4.own_ref = bf16[256,1024]{1,0:T(8,128)(2,1)S(1)} collective-permute-done((bf16[256,1024]{1,0:T(8,128)(2,1)S(1)}, bf16[256,1024]{1,0:T(8,128)(2,1)S(1)}, u32[]{:S(2)}, u32[]{:S(2)}) %collective-permute-start.4) | collective-permute-done | bytes 524320 | tf_op jit(solution)/shard_map/ppermute | solution.py:309
  95.5 2.9 %collective-permute-start.31 = (bf16[832,256]{1,0:T(8,128)(2,1)S(1)}, bf16[832,256]{1,0:T(8,128)(2,1)S(1)}, u32[]{:S(2)}, u32[]{:S(2)}) collective-permute-start(bf16[832,256]{1,0:T(8,128)(2,1)S(1)} %pad_maximum_fusion.3), channel_id=1, source_target_pairs={{0,16},{4,20},{8,24},{12,28},{16,0},{20,4},{24,8},{28,12},{1,17},{... | collective-permute-start | bytes 1277960 | tf_op jit(solution)/shard_map/ppermute | solution.py:309
  98.3 1.9 %norm.6.rest_0_ = bf16[4,4,256,1024]{3,2,1,0:T(8,128)(2,1)S(1)} custom-call(s32[3]{0:T(128)S(1)} %pad_add_fusion.place_ref, bf16[256,1024]{1,0:T(8,128)(2,1)S(1)} %collective-permute-done.3.own_ref, bf16[256,1024]{1,0:T(8,128)(2,1)S(1)} %collective-permute-done.17.x_ref, ...), custom_call_target="tpu_custom_call", output_to_operand_aliasing={{}: (7, {})} | custom-call | flops 1 | bytes 1 | tf_op jit(solution)/shard_map/norm/pallas_call | solution.py:119
  100.3 16.8 %collective-permute-done.26.refs_3_ = bf16[512,256]{1,0:T(8,128)(2,1)S(1)} collective-permute-done((bf16[512,256]{1,0:T(8,128)(2,1)S(1)}, bf16[512,256]{1,0:T(8,128)(2,1)S(1)}, u32[]{:S(2)}, u32[]{:S(2)}) %collective-permute-start.26) | collective-permute-done | bytes 262176 | tf_op jit(solution)/shard_map/ppermute | solution.py:309
  118.0 1.6 collective-permute-start.28
  119.6 6.6 %collective-permute-done.31.refs_2_.refs_0_ = bf16[832,256]{1,0:T(8,128)(2,1)S(1)} collective-permute-done((bf16[832,256]{1,0:T(8,128)(2,1)S(1)}, bf16[832,256]{1,0:T(8,128)(2,1)S(1)}, u32[]{:S(2)}, u32[]{:S(2)}) %collective-permute-start.31) | collective-permute-done | bytes 426016 | tf_op jit(solution)/shard_map/ppermute | solution.py:309
  126.7 1.9 %norm.7.normed_ref = bf16[4,4,256,1024]{3,2,1,0:T(8,128)(2,1)S(1)} custom-call(s32[3]{0:T(128)S(1)} %pad_add_fusion.place_ref, bf16[256,1024]{1,0:T(8,128)(2,1)S(1)} %collective-permute-done.4.own_ref, bf16[256,1024]{1,0:T(8,128)(2,1)S(1)} %collective-permute-done.24.x_ref, ...), custom_call_target="tpu_custom_call", output_to_operand_aliasing={{}: (7, {})} | custom-call | flops 1 | bytes 1 | tf_op jit(solution)/shard_map/norm/pallas_call | solution.py:119
  128.7 4.0 %project.5 = (f32[4,256,256]{2,1,0:T(8,128)S(1)}, f32[4,256,256]{2,1,0:T(8,128)S(1)}) custom-call(s32[3]{0:T(128)S(1)} %pad_add_fusion.place_ref, bf16[4,4,256,1024]{3,2,1,0:T(8,128)(2,1)S(1)} %norm.7.normed_ref, bf16[1344,256]{1,0:T(8,128)(2,1)S(1)} %pad_maximum_fusion.refs_0_, bf16[1344,256]{1,0:T(8,128)(2,1)S(1)} %collective-permute-done.13.refs_1_, ...), custom_call_target="tpu_custom_call" | custom-call | flops 1 | bytes 1 | tf_op jit(solution)/shard_map/project/pallas_call | solution.py:155
  132.7 3.3 %project.4.q_ref = bf16[4,256,256]{2,1,0:T(8,128)(2,1)S(1)} custom-call(s32[3]{0:T(128)S(1)} %pad_add_fusion.place_ref, bf16[4,4,256,1024]{3,2,1,0:T(8,128)(2,1)S(1)} %norm.7.normed_ref, bf16[512,256]{1,0:T(8,128)(2,1)S(1)} %get-tuple-element.74.refs_0_, bf16[512,256]{1,0:T(8,128)(2,1)S(1)} %copy-done.10, bf16[512,256]{1,0:T(8,128)(2,1)S(1)} %copy-done.8, ...), custom_call_target="tpu_custom_call" | custom-call | flops 1 | bytes 1 | tf_op jit(solution)/shard_map/project/pallas_call | solution.py:155
  136.1 1.3 project.6.k_ref
  137.4 4.1 %collective-permute-done.34.refs_0_ = bf16[512,256]{1,0:T(8,128)(2,1)S(1)} collective-permute-done((bf16[512,256]{1,0:T(8,128)(2,1)S(1)}, bf16[512,256]{1,0:T(8,128)(2,1)S(1)}, u32[]{:S(2)}, u32[]{:S(2)}) %collective-permute-start.34) | collective-permute-done | bytes 262176 | tf_op jit(solution)/shard_map/ppermute | solution.py:309
  143.0 1.3 project.7.v_ref
  144.5 1.8 %collective-permute-done.37.vs_ref = bf16[4,256,256]{2,1,0:T(8,128)(2,1)S(1)} collective-permute-done((bf16[4,256,256]{2,1,0:T(8,128)(2,1)S(1)}, bf16[4,256,256]{2,1,0:T(8,128)(2,1)S(1)}, u32[]{:S(2)}, u32[]{:S(2)}) %collective-permute-start.37) | collective-permute-done | bytes 524320 | tf_op jit(solution)/shard_map/ppermute | solution.py:313
  146.2 3.9 %attend.3 = bf16[256,256]{1,0:T(8,128)(2,1)S(1)} custom-call(s32[3]{0:T(128)S(1)} %pad_add_fusion.place_ref, bf16[4,256,256]{2,1,0:T(8,128)(2,1)S(1)} %project.4.q_ref, bf16[4,256,256]{2,1,0:T(8,128)(2,1)S(1)} %project.6.k_ref, bf16[4,256,256]{2,1,0:T(8,128)(2,1)S(1)} %project.7.v_ref, bf16[4,256,256]{2,1,0:T(8,128)(2,1)S(1)} %collective-permute-done.36.ks_ref, ...), custom_call_target="tpu_custom_call" | custom-call | flops 1 | bytes 1 | tf_op jit(solution)/shard_map/attend/pallas_call | solution.py:248
  150.2 7.4 %attend.4 = (bf16[256,256]{1,0:T(8,128)(2,1)S(1)}, bf16[256,256]{1,0:T(8,128)(2,1)S(1)}) custom-call(s32[3]{0:T(128)S(1)} %pad_add_fusion.place_ref, bf16[4,256,256]{2,1,0:T(8,128)(2,1)S(1)} %project.4.q_ref, bf16[4,256,256]{2,1,0:T(8,128)(2,1)S(1)} %project.6.k_ref, bf16[4,256,256]{2,1,0:T(8,128)(2,1)S(1)} %project.7.v_ref, ...), custom_call_target="tpu_custom_call" | custom-call | flops 1 | bytes 1 | tf_op jit(solution)/shard_map/attend/pallas_call | solution.py:248
  157.7 3.8 %collective-permute-start.40 = (bf16[256,256]{1,0:T(8,128)(2,1)S(1)}, bf16[256,256]{1,0:T(8,128)(2,1)S(1)}, u32[]{:S(2)}, u32[]{:S(2)}) collective-permute-start(bf16[256,256]{1,0:T(8,128)(2,1)S(1)} %get-tuple-element.66), channel_id=1, source_target_pairs={{0,24},{4,28},{8,0},{12,4},{16,8},{20,12},{24,16},{28,20},{1,25},{... | collective-permute-start | bytes 393224 | tf_op jit(solution)/shard_map/ppermute | solution.py:309
  161.5 2.6 %attend.5.refs_0_ = bf16[256,256]{1,0:T(8,128)(2,1)S(1)} custom-call(s32[3]{0:T(128)S(1)} %pad_add_fusion.place_ref, bf16[4,256,256]{2,1,0:T(8,128)(2,1)S(1)} %project.4.q_ref, bf16[4,256,256]{2,1,0:T(8,128)(2,1)S(1)} %project.6.k_ref, bf16[4,256,256]{2,1,0:T(8,128)(2,1)S(1)} %project.7.v_ref, bf16[4,256,256]{2,1,0:T(8,128)(2,1)S(1)} %collective-permute-done.36.ks_ref, ...), custom_call_target="tpu_custom_call" | custom-call | flops 1 | bytes 1 | tf_op jit(solution)/shard_map/attend/pallas_call | solution.py:248
  164.8 1.1 collective-permute-done.39.refs_1_
  165.8 1.4 collective-permute-done.40.refs_3_
  167.8 2.0 %join.1 = bf16[256,1024]{1,0:T(8,128)(2,1)} custom-call(s32[3]{0:T(128)} %copy-done.15, bf16[256,256]{1,0:T(8,128)(2,1)} %copy-done.5, bf16[256,256]{1,0:T(8,128)(2,1)} %copy-done.29, bf16[256,256]{1,0:T(8,128)(2,1)} %copy-done.28, bf16[256,256]{1,0:T(8,128)(2,1)} %copy-done.30), custom_call_target="tpu_custom_call" | custom-call | tf_op jit(solution)/shard_map/join/pallas_call | solution.py:298
  (128 shorter events, 18.8 us)
Async XLA Ops:
  1.2 8.9 %collective-permute-start = (bf16[128,1024]{1,0:T(8,128)(2,1)S(1)}, bf16[128,1024]{1,0:T(8,128)(2,1)S(1)}, u32[]{:S(2)}, u32[]{:S(2)}) collective-permute-start(bf16[128,1024]{1,0:T(8,128)(2,1)S(1)} %fusion), channel_id=1, source_target_pairs={{0,4},{4,8},{8,12},{12,16},{16,20},{20,24},{24,28},{1,5},{5,9},{9,... | collective-permute-start | bytes 786440 | tf_op jit(solution)/shard_map/ppermute | solution.py:353
  5.6 11.7 %collective-permute-start.5 = (bf16[512,256]{1,0:T(8,128)(2,1)}, bf16[512,256]{1,0:T(8,128)(2,1)S(1)}, u32[]{:S(2)}, u32[]{:S(2)}) collective-permute-start(bf16[512,256]{1,0:T(8,128)(2,1)} %get-tuple-element.77), channel_id=1, source_target_pairs={{0,24},{4,28},{8,0},{12,4},{16,8},{20,12},{24,16},{28,20},{1,25},{... | collective-permute-start | bytes 786440 | tf_op jit(solution)/shard_map/ppermute | solution.py:309
  10.2 12.8 %collective-permute-start.1 = (bf16[512,256]{1,0:T(8,128)(2,1)}, bf16[512,256]{1,0:T(8,128)(2,1)S(1)}, u32[]{:S(2)}, u32[]{:S(2)}) collective-permute-start(bf16[512,256]{1,0:T(8,128)(2,1)} %get-tuple-element.78), channel_id=1, source_target_pairs={{0,8},{4,12},{8,16},{12,20},{16,24},{20,28},{24,0},{28,4},{1,9},{5... | collective-permute-start | bytes 786440 | tf_op jit(solution)/shard_map/ppermute | solution.py:309
  10.2 15.8 %copy-start.23 = (bf16[152,1024]{1,0:T(8,128)(2,1)S(1)}, bf16[152,1024]{1,0:T(8,128)(2,1)}, u32[]{:S(2)}) copy-start(bf16[152,1024]{1,0:T(8,128)(2,1)} %param.13) | copy-start | bytes 933892
  10.3 16.9 %copy-start.17 = (bf16[512,3,1024]{2,0,1:T(8,128)(2,1)S(1)}, bf16[512,3,1024]{2,0,1:T(8,128)(2,1)}, u32[]{:S(2)}) copy-start(bf16[512,3,1024]{2,0,1:T(8,128)(2,1)} %param.11) | copy-start | bytes 9437188
  22.9 14.3 %collective-permute-start.6 = (bf16[256,1024]{1,0:T(8,128)(2,1)S(1)}, bf16[256,1024]{1,0:T(8,128)(2,1)S(1)}, u32[]{:S(2)}, u32[]{:S(2)}) collective-permute-start(bf16[256,1024]{1,0:T(8,128)(2,1)S(1)} %hyena_filters.1.own_ref), channel_id=1, source_target_pairs={{0,1},{1,0},{2,3},{3,2},{4,5},{5,4},{6,7},{7,6},{8,9},{9,8},{10,11... | collective-permute-start | bytes 1572872 | tf_op jit(solution)/shard_map/ppermute | solution.py:317
  24.4 14.4 %collective-permute-start.8 = (bf16[256,1024]{1,0:T(8,128)(2,1)S(1)}, bf16[256,1024]{1,0:T(8,128)(2,1)S(1)}, u32[]{:S(2)}, u32[]{:S(2)}) collective-permute-start(bf16[256,1024]{1,0:T(8,128)(2,1)S(1)} %hyena_filters.1.own_ref), channel_id=1, source_target_pairs={{0,2},{1,3},{2,0},{3,1},{4,6},{5,7},{6,4},{7,5},{8,10},{9,11},{10,... | collective-permute-start | bytes 1572872 | tf_op jit(solution)/shard_map/ppermute | solution.py:317
  26.7 16.7 %collective-permute-start.2 = (bf16[256,1024]{1,0:T(8,128)(2,1)S(1)}, bf16[256,1024]{1,0:T(8,128)(2,1)}, u32[]{:S(2)}, u32[]{:S(2)}) collective-permute-start(bf16[256,1024]{1,0:T(8,128)(2,1)S(1)} %hyena_filters.1.own_ref), channel_id=1, source_target_pairs={{0,8},{4,12},{8,16},{12,20},{16,24},{20,28},{24,0},{28,4},{1,9},{5... | collective-permute-start | bytes 1572872 | tf_op jit(solution)/shard_map/ppermute | solution.py:309
  29.4 22.2 %copy-start.6 = (f32[4096]{0:T(1024)S(1)}, f32[4096]{0:T(1024)}, u32[]{:S(2)}) copy-start(f32[4096]{0:T(1024)} %param.10) | copy-start | bytes 49156
  29.4 28.3 %collective-permute-start.13 = (bf16[1344,256]{1,0:T(8,128)(2,1)}, bf16[1344,256]{1,0:T(8,128)(2,1)S(1)}, u32[]{:S(2)}, u32[]{:S(2)}) collective-permute-start(bf16[1344,256]{1,0:T(8,128)(2,1)} %pad_maximum_fusion.1), channel_id=1, source_target_pairs={{0,8},{4,12},{8,16},{12,20},{16,24},{20,28},{24,0},{28,4},{1,9},{5... | collective-permute-start | bytes 2064392 | tf_op jit(solution)/shard_map/ppermute | solution.py:309
  37.3 8.1 %collective-permute-start.7 = (bf16[128,1024]{1,0:T(8,128)(2,1)S(1)}, bf16[128,1024]{1,0:T(8,128)(2,1)S(1)}, u32[]{:S(2)}, u32[]{:S(2)}) collective-permute-start(bf16[128,1024]{1,0:T(8,128)(2,1)S(1)} %slice.42), channel_id=1, source_target_pairs={{0,2},{1,3},{2,0},{3,1},{4,6},{5,7},{6,4},{7,5},{8,10},{9,11},{10,... | collective-permute-start | bytes 786440 | tf_op jit(solution)/shard_map/ppermute | solution.py:317
  38.9 7.8 %collective-permute-start.9 = (bf16[128,1024]{1,0:T(8,128)(2,1)S(1)}, bf16[128,1024]{1,0:T(8,128)(2,1)S(1)}, u32[]{:S(2)}, u32[]{:S(2)}) collective-permute-start(bf16[128,1024]{1,0:T(8,128)(2,1)S(1)} %slice.43), channel_id=1, source_target_pairs={{0,1},{1,0},{2,3},{3,2},{4,5},{5,4},{6,7},{7,6},{8,9},{9,8},{10,11... | collective-permute-start | bytes 786440 | tf_op jit(solution)/shard_map/ppermute | solution.py:317
  40.5 17.2 %collective-permute-start.11 = (bf16[1344,256]{1,0:T(8,128)(2,1)S(1)}, bf16[1344,256]{1,0:T(8,128)(2,1)S(1)}, u32[]{:S(2)}, u32[]{:S(2)}) collective-permute-start(bf16[1344,256]{1,0:T(8,128)(2,1)S(1)} %pad_maximum_fusion.refs_0_), channel_id=1, source_target_pairs={{0,4},{4,0},{8,12},{12,8},{16,20},{20,16},{24,28},{28,24},{1,5},{5... | collective-permute-start | bytes 2064392 | tf_op jit(solution)/shard_map/ppermute | solution.py:313
  47.4 12.7 %collective-permute-start.15 = (bf16[256,1024]{1,0:T(8,128)(2,1)}, bf16[256,1024]{1,0:T(8,128)(2,1)S(1)}, u32[]{:S(2)}, u32[]{:S(2)}) collective-permute-start(bf16[256,1024]{1,0:T(8,128)(2,1)} %collective-permute-done.2.own_ref), channel_id=1, source_target_pairs={{0,2},{1,3},{2,0},{3,1},{4,6},{5,7},{6,4},{7,5},{8,10},{9,11},{10,... | collective-permute-start | bytes 1572872 | tf_op jit(solution)/shard_map/ppermute | solution.py:317
  48.5 13.2 %collective-permute-start.10 = (bf16[256,1024]{1,0:T(8,128)(2,1)}, bf16[256,1024]{1,0:T(8,128)(2,1)}, u32[]{:S(2)}, u32[]{:S(2)}) collective-permute-start(bf16[256,1024]{1,0:T(8,128)(2,1)} %collective-permute-done.2.own_ref), channel_id=1, source_target_pairs={{0,1},{1,0},{2,3},{3,2},{4,5},{5,4},{6,7},{7,6},{8,9},{9,8},{10,11... | collective-permute-start | bytes 1572872 | tf_op jit(solution)/shard_map/ppermute | solution.py:317
  49.8 1.7 collective-permute-start.12
  51.4 17.6 %collective-permute-start.3 = (bf16[256,1024]{1,0:T(8,128)(2,1)}, bf16[256,1024]{1,0:T(8,128)(2,1)S(1)}, u32[]{:S(2)}, u32[]{:S(2)}) collective-permute-start(bf16[256,1024]{1,0:T(8,128)(2,1)} %collective-permute-done.2.own_ref), channel_id=1, source_target_pairs={{0,8},{4,12},{8,16},{12,20},{16,24},{20,28},{24,0},{28,4},{1,9},{5... | collective-permute-start | bytes 1572872 | tf_op jit(solution)/shard_map/ppermute | solution.py:309
  51.5 110.0 %copy-start.15 = (s32[3]{0:T(128)}, s32[3]{0:T(128)S(1)}, u32[]{:S(2)}) copy-start(s32[3]{0:T(128)S(1)} %pad_add_fusion.place_ref) | copy-start | bytes 40
  60.1 9.0 %collective-permute-start.16 = (bf16[128,1024]{1,0:T(8,128)(2,1)S(1)}, bf16[128,1024]{1,0:T(8,128)(2,1)S(1)}, u32[]{:S(2)}, u32[]{:S(2)}) collective-permute-start(bf16[128,1024]{1,0:T(8,128)(2,1)S(1)} %slice.35), channel_id=1, source_target_pairs={{0,1},{1,0},{2,3},{3,2},{4,5},{5,4},{6,7},{7,6},{8,9},{9,8},{10,11... | collective-permute-start | bytes 786440 | tf_op jit(solution)/shard_map/ppermute | solution.py:317
  62.6 6.4 %collective-permute-start.14 = (bf16[128,1024]{1,0:T(8,128)(2,1)S(1)}, bf16[128,1024]{1,0:T(8,128)(2,1)S(1)}, u32[]{:S(2)}, u32[]{:S(2)}) collective-permute-start(bf16[128,1024]{1,0:T(8,128)(2,1)S(1)} %slice.34), channel_id=1, source_target_pairs={{0,2},{1,3},{2,0},{3,1},{4,6},{5,7},{6,4},{7,5},{8,10},{9,11},{10,... | collective-permute-start | bytes 786440 | tf_op jit(solution)/shard_map/ppermute | solution.py:317
  63.9 31.4 %copy-start.26 = (bf16[512,256]{1,0:T(8,128)(2,1)S(1)}, bf16[512,256]{1,0:T(8,128)(2,1)}, u32[]{:S(2)}) copy-start(bf16[512,256]{1,0:T(8,128)(2,1)} %get-tuple-element.50) | copy-start | bytes 786436
  63.9 31.5 %copy-start.18 = (bf16[512,256]{1,0:T(8,128)(2,1)S(1)}, bf16[512,256]{1,0:T(8,128)(2,1)}, u32[]{:S(2)}) copy-start(bf16[512,256]{1,0:T(8,128)(2,1)} %get-tuple-element.68) | copy-start | bytes 786436
  64.0 19.8 %collective-permute-start.20 = (bf16[1344,256]{1,0:T(8,128)(2,1)S(1)}, bf16[1344,256]{1,0:T(8,128)(2,1)S(1)}, u32[]{:S(2)}, u32[]{:S(2)}) collective-permute-start(bf16[1344,256]{1,0:T(8,128)(2,1)S(1)} %pad_maximum_fusion.2), channel_id=1, source_target_pairs={{0,24},{4,28},{8,0},{12,4},{16,8},{20,12},{24,16},{28,20},{1,25},{... | collective-permute-start | bytes 2064392 | tf_op jit(solution)/shard_map/ppermute | solution.py:309
  69.0 14.8 %collective-permute-start.22 = (bf16[256,1024]{1,0:T(8,128)(2,1)S(1)}, bf16[256,1024]{1,0:T(8,128)(2,1)S(1)}, u32[]{:S(2)}, u32[]{:S(2)}) collective-permute-start(bf16[256,1024]{1,0:T(8,128)(2,1)S(1)} %collective-permute-done.3.own_ref), channel_id=1, source_target_pairs={{0,2},{1,3},{2,0},{3,1},{4,6},{5,7},{6,4},{7,5},{8,10},{9,11},{10,... | collective-permute-start | bytes 1572872 | tf_op jit(solution)/shard_map/ppermute | solution.py:317
  70.2 13.9 %collective-permute-start.17 = (bf16[256,1024]{1,0:T(8,128)(2,1)S(1)}, bf16[256,1024]{1,0:T(8,128)(2,1)S(1)}, u32[]{:S(2)}, u32[]{:S(2)}) collective-permute-start(bf16[256,1024]{1,0:T(8,128)(2,1)S(1)} %collective-permute-done.3.own_ref), channel_id=1, source_target_pairs={{0,1},{1,0},{2,3},{3,2},{4,5},{5,4},{6,7},{7,6},{8,9},{9,8},{10,11... | collective-permute-start | bytes 1572872 | tf_op jit(solution)/shard_map/ppermute | solution.py:317
  70.8 1.5 collective-permute-start.18
  70.8 4.1 %collective-permute-start.19 = (bf16[512,256]{1,0:T(8,128)(2,1)S(1)}, bf16[512,256]{1,0:T(8,128)(2,1)S(1)}, u32[]{:S(2)}, u32[]{:S(2)}) collective-permute-start(bf16[512,256]{1,0:T(8,128)(2,1)S(1)} %copy-done.8), channel_id=1, source_target_pairs={{0,4},{4,0},{8,12},{12,8},{16,20},{20,16},{24,28},{28,24},{1,5},{5... | collective-permute-start | bytes 786440 | tf_op jit(solution)/shard_map/ppermute | solution.py:313
  72.3 22.0 %collective-permute-start.4 = (bf16[256,1024]{1,0:T(8,128)(2,1)S(1)}, bf16[256,1024]{1,0:T(8,128)(2,1)S(1)}, u32[]{:S(2)}, u32[]{:S(2)}) collective-permute-start(bf16[256,1024]{1,0:T(8,128)(2,1)S(1)} %collective-permute-done.3.own_ref), channel_id=1, source_target_pairs={{0,8},{4,12},{8,16},{12,20},{16,24},{20,28},{24,0},{28,4},{1,9},{5... | collective-permute-start | bytes 1572872 | tf_op jit(solution)/shard_map/ppermute | solution.py:309
  83.8 10.5 %collective-permute-start.23 = (bf16[128,1024]{1,0:T(8,128)(2,1)S(1)}, bf16[128,1024]{1,0:T(8,128)(2,1)S(1)}, u32[]{:S(2)}, u32[]{:S(2)}) collective-permute-start(bf16[128,1024]{1,0:T(8,128)(2,1)S(1)} %slice.37), channel_id=1, source_target_pairs={{0,1},{1,0},{2,3},{3,2},{4,5},{5,4},{6,7},{7,6},{8,9},{9,8},{10,11... | collective-permute-start | bytes 786440 | tf_op jit(solution)/shard_map/ppermute | solution.py:317
  84.1 10.2 %collective-permute-start.21 = (bf16[128,1024]{1,0:T(8,128)(2,1)S(1)}, bf16[128,1024]{1,0:T(8,128)(2,1)S(1)}, u32[]{:S(2)}, u32[]{:S(2)}) collective-permute-start(bf16[128,1024]{1,0:T(8,128)(2,1)S(1)} %slice.36), channel_id=1, source_target_pairs={{0,2},{1,3},{2,0},{3,1},{4,6},{5,7},{6,4},{7,5},{8,10},{9,11},{10,... | collective-permute-start | bytes 786440 | tf_op jit(solution)/shard_map/ppermute | solution.py:317
  84.9 15.4 %collective-permute-start.25 = (bf16[1344,256]{1,0:T(8,128)(2,1)S(1)}, bf16[1344,256]{1,0:T(8,128)(2,1)S(1)}, u32[]{:S(2)}, u32[]{:S(2)}) collective-permute-start(bf16[1344,256]{1,0:T(8,128)(2,1)S(1)} %collective-permute-done.13.refs_1_), channel_id=1, source_target_pairs={{0,4},{4,0},{8,12},{12,8},{16,20},{20,16},{24,28},{28,24},{1,5},{5... | collective-permute-start | bytes 2064392 | tf_op jit(solution)/shard_map/ppermute | solution.py:313
  94.3 22.9 %collective-permute-start.27 = (bf16[256,1024]{1,0:T(8,128)(2,1)S(1)}, bf16[256,1024]{1,0:T(8,128)(2,1)S(1)}, u32[]{:S(2)}, u32[]{:S(2)}) collective-permute-start(bf16[256,1024]{1,0:T(8,128)(2,1)S(1)} %collective-permute-done.4.own_ref), channel_id=1, source_target_pairs={{0,2},{1,3},{2,0},{3,1},{4,6},{5,7},{6,4},{7,5},{8,10},{9,11},{10,... | collective-permute-start | bytes 1572872 | tf_op jit(solution)/shard_map/ppermute | solution.py:317
  94.8 23.2 %collective-permute-start.24 = (bf16[256,1024]{1,0:T(8,128)(2,1)S(1)}, bf16[256,1024]{1,0:T(8,128)(2,1)S(1)}, u32[]{:S(2)}, u32[]{:S(2)}) collective-permute-start(bf16[256,1024]{1,0:T(8,128)(2,1)S(1)} %collective-permute-done.4.own_ref), channel_id=1, source_target_pairs={{0,1},{1,0},{2,3},{3,2},{4,5},{5,4},{6,7},{7,6},{8,9},{9,8},{10,11... | collective-permute-start | bytes 1572872 | tf_op jit(solution)/shard_map/ppermute | solution.py:317
  95.3 21.9 %collective-permute-start.26 = (bf16[512,256]{1,0:T(8,128)(2,1)S(1)}, bf16[512,256]{1,0:T(8,128)(2,1)S(1)}, u32[]{:S(2)}, u32[]{:S(2)}) collective-permute-start(bf16[512,256]{1,0:T(8,128)(2,1)S(1)} %copy-done.26), channel_id=1, source_target_pairs={{0,16},{4,20},{8,24},{12,28},{16,0},{20,4},{24,8},{28,12},{1,17},{... | collective-permute-start | bytes 786440 | tf_op jit(solution)/shard_map/ppermute | solution.py:309
  95.4 31.3 %copy-start.25 = (bf16[512,256]{1,0:T(8,128)(2,1)S(1)}, bf16[512,256]{1,0:T(8,128)(2,1)}, u32[]{:S(2)}) copy-start(bf16[512,256]{1,0:T(8,128)(2,1)} %get-tuple-element.59) | copy-start | bytes 786436
  95.5 30.8 %collective-permute-start.31 = (bf16[832,256]{1,0:T(8,128)(2,1)S(1)}, bf16[832,256]{1,0:T(8,128)(2,1)S(1)}, u32[]{:S(2)}, u32[]{:S(2)}) collective-permute-start(bf16[832,256]{1,0:T(8,128)(2,1)S(1)} %pad_maximum_fusion.3), channel_id=1, source_target_pairs={{0,16},{4,20},{8,24},{12,28},{16,0},{20,4},{24,8},{28,12},{1,17},{... | collective-permute-start | bytes 1277960 | tf_op jit(solution)/shard_map/ppermute | solution.py:309
  100.3 28.4 %collective-permute-start.33 = (bf16[1344,256]{1,0:T(8,128)(2,1)S(1)}, bf16[1344,256]{1,0:T(8,128)(2,1)S(1)}, u32[]{:S(2)}, u32[]{:S(2)}) collective-permute-start(bf16[1344,256]{1,0:T(8,128)(2,1)S(1)} %collective-permute-done.20.refs_3_.refs_2_), channel_id=1, source_target_pairs={{0,4},{4,0},{8,12},{12,8},{16,20},{20,16},{24,28},{28,24},{1,5},{5... | collective-permute-start | bytes 2064392 | tf_op jit(solution)/shard_map/ppermute | solution.py:313
  117.2 9.0 %collective-permute-start.29 = (bf16[128,1024]{1,0:T(8,128)(2,1)S(1)}, bf16[128,1024]{1,0:T(8,128)(2,1)S(1)}, u32[]{:S(2)}, u32[]{:S(2)}) collective-permute-start(bf16[128,1024]{1,0:T(8,128)(2,1)S(1)} %slice.39), channel_id=1, source_target_pairs={{0,1},{1,0},{2,3},{3,2},{4,5},{5,4},{6,7},{7,6},{8,9},{9,8},{10,11... | collective-permute-start | bytes 786440 | tf_op jit(solution)/shard_map/ppermute | solution.py:317
  118.0 8.2 %collective-permute-start.28 = (bf16[128,1024]{1,0:T(8,128)(2,1)S(1)}, bf16[128,1024]{1,0:T(8,128)(2,1)S(1)}, u32[]{:S(2)}, u32[]{:S(2)}) collective-permute-start(bf16[128,1024]{1,0:T(8,128)(2,1)S(1)} %slice.38), channel_id=1, source_target_pairs={{0,2},{1,3},{2,0},{3,1},{4,6},{5,7},{6,4},{7,5},{8,10},{9,11},{10,... | collective-permute-start | bytes 786440 | tf_op jit(solution)/shard_map/ppermute | solution.py:317
  126.2 9.8 %collective-permute-start.32 = (bf16[832,256]{1,0:T(8,128)(2,1)S(1)}, bf16[832,256]{1,0:T(8,128)(2,1)S(1)}, u32[]{:S(2)}, u32[]{:S(2)}) collective-permute-start(bf16[832,256]{1,0:T(8,128)(2,1)S(1)} %collective-permute-done.31.refs_2_.refs_0_), channel_id=1, source_target_pairs={{0,4},{4,0},{8,12},{12,8},{16,20},{20,16},{24,28},{28,24},{1,5},{5... | collective-permute-start | bytes 1277960 | tf_op jit(solution)/shard_map/ppermute | solution.py:313
  126.2 6.4 %collective-permute-start.30 = (bf16[512,256]{1,0:T(8,128)(2,1)S(1)}, bf16[512,256]{1,0:T(8,128)(2,1)S(1)}, u32[]{:S(2)}, u32[]{:S(2)}) collective-permute-start(bf16[512,256]{1,0:T(8,128)(2,1)S(1)} %collective-permute-done.26.refs_3_), channel_id=1, source_target_pairs={{0,4},{4,0},{8,12},{12,8},{16,20},{20,16},{24,28},{28,24},{1,5},{5... | collective-permute-start | bytes 786440 | tf_op jit(solution)/shard_map/ppermute | solution.py:313
  126.7 14.7 %collective-permute-start.34 = (bf16[512,256]{1,0:T(8,128)(2,1)S(1)}, bf16[512,256]{1,0:T(8,128)(2,1)S(1)}, u32[]{:S(2)}, u32[]{:S(2)}) collective-permute-start(bf16[512,256]{1,0:T(8,128)(2,1)S(1)} %copy-done.25), channel_id=1, source_target_pairs={{0,16},{4,20},{8,24},{12,28},{16,0},{20,4},{24,8},{28,12},{1,17},{... | collective-permute-start | bytes 786440 | tf_op jit(solution)/shard_map/ppermute | solution.py:309
  141.4 1.5 collective-permute-start.35
  141.5 3.0 %collective-permute-start.36 = (bf16[4,256,256]{2,1,0:T(8,128)(2,1)S(1)}, bf16[4,256,256]{2,1,0:T(8,128)(2,1)S(1)}, u32[]{:S(2)}, u32[]{:S(2)}) collective-permute-start(bf16[4,256,256]{2,1,0:T(8,128)(2,1)S(1)} %project.6.k_ref), channel_id=1, source_target_pairs={{0,4},{4,0},{8,12},{12,8},{16,20},{20,16},{24,28},{28,24},{1,5},{5... | collective-permute-start | bytes 1572872 | tf_op jit(solution)/shard_map/ppermute | solution.py:313
  144.3 2.0 %collective-permute-start.37 = (bf16[4,256,256]{2,1,0:T(8,128)(2,1)S(1)}, bf16[4,256,256]{2,1,0:T(8,128)(2,1)S(1)}, u32[]{:S(2)}, u32[]{:S(2)}) collective-permute-start(bf16[4,256,256]{2,1,0:T(8,128)(2,1)S(1)} %project.7.v_ref), channel_id=1, source_target_pairs={{0,4},{4,0},{8,12},{12,8},{16,20},{20,16},{24,28},{28,24},{1,5},{5... | collective-permute-start | bytes 1572872 | tf_op jit(solution)/shard_map/ppermute | solution.py:313
  150.2 11.3 %collective-permute-start.38 = (bf16[256,256]{1,0:T(8,128)(2,1)S(1)}, bf16[256,256]{1,0:T(8,128)(2,1)S(1)}, u32[]{:S(2)}, u32[]{:S(2)}) collective-permute-start(bf16[256,256]{1,0:T(8,128)(2,1)S(1)} %attend.3), channel_id=1, source_target_pairs={{0,16},{4,20},{8,24},{12,28},{16,0},{20,4},{24,8},{28,12},{1,17},{... | collective-permute-start | bytes 393224 | tf_op jit(solution)/shard_map/ppermute | solution.py:309
  157.6 8.2 %collective-permute-start.39 = (bf16[256,256]{1,0:T(8,128)(2,1)S(1)}, bf16[256,256]{1,0:T(8,128)(2,1)S(1)}, u32[]{:S(2)}, u32[]{:S(2)}) collective-permute-start(bf16[256,256]{1,0:T(8,128)(2,1)S(1)} %get-tuple-element.64), channel_id=1, source_target_pairs={{0,8},{4,12},{8,16},{12,20},{16,24},{20,28},{24,0},{28,4},{1,9},{5... | collective-permute-start | bytes 393224 | tf_op jit(solution)/shard_map/ppermute | solution.py:309
  157.7 9.5 %collective-permute-start.40 = (bf16[256,256]{1,0:T(8,128)(2,1)S(1)}, bf16[256,256]{1,0:T(8,128)(2,1)S(1)}, u32[]{:S(2)}, u32[]{:S(2)}) collective-permute-start(bf16[256,256]{1,0:T(8,128)(2,1)S(1)} %get-tuple-element.66), channel_id=1, source_target_pairs={{0,24},{4,28},{8,0},{12,4},{16,8},{20,12},{24,16},{28,20},{1,25},{... | collective-permute-start | bytes 393224 | tf_op jit(solution)/shard_map/ppermute | solution.py:309
  (24 other events, 143.7 us)

commit v4 on v3

--- a/solution.py
+++ b/solution.py
@@ -186,11 +186,10 @@
 
     for shift, out_ref in zip(shifts, outs):
         block = lax.rem(z + shift, zs)
-        mine = lax.rem(zs - shift, zs)
-        queries = [q_ref[mine, :, hcol] for hcol in hcols]
+        queries = [q_ref[place_ref[3 + block], :, hcol] for hcol in hcols]
 
         def score(b, tops, diagonal):
-            at = lax.rem(z + zs - b, zs)
+            at = place_ref[3 + b]
             result = []
             for h, top in zip(heads, tops):
                 s = lax.dot_general(queries[h], k_ref[at, :, hcols[h]], NT, preferred_element_type=F32)
@@ -218,7 +217,7 @@
         ]
 
         def weigh(b, state):
-            at = lax.rem(z + zs - b, zs)
+            at = place_ref[3 + b]
             result = []
             for h, (total, summed) in zip(heads, state):
                 weights = jnp.exp2(new[h, b] * factor - tops[h])
@@ -309,6 +308,10 @@
     return lax.ppermute(value, "seq", pairs)
 
 
+def step_z(value, steps, sources):
+    return lax.ppermute(value, "seq", [(2 * a + k, 2 * (a + steps) + k) for a in sources for k in range(2)])
+
+
 def swap_core(value, zs):
     return lax.ppermute(value, "seq", [(2 * a + k, 2 * a + 1 - k) for a in range(zs) for k in range(2)])
 
@@ -331,7 +334,8 @@
     my_seq = lax.axis_index("seq")
     z, core = my_seq // 2, my_seq % 2
     chan = lax.axis_index("chan")
-    place = jnp.stack([chan, z, core]).astype(jnp.int32)
+    slabs = jnp.array([[0, 1, 2, 3], [3, 0, 1, 2], [2, 1, 0, 3], [3, 2, 1, 0]], jnp.int32)
+    place = jnp.concatenate([jnp.stack([chan, z, core]).astype(jnp.int32), slabs[z]])
 
     w_t = jnp.transpose(w_qkv, (1, 0, 2))
     caches = [jnp.pad(c, ((0, PAD), (0, 0))) for c in (cache_k, cache_v)]
@@ -353,54 +357,78 @@
     halo = lax.ppermute(tail, "seq", [(s, s + 1) for s in range(seqs - 1)])
     halo = jnp.where(my_seq == 0, jnp.pad(prior_kv, ((taps - prior_kv.shape[0], 0), (0, 0))), halo)
 
-    order = ["q1", "q3", "acts", "kvc1", "acts", "kvc3", "acts", "q2", "kc2", "v2"]
-    acts = [hyena(hin, halo, filters)]
-    here = {kind + "0": parcel(kind, 0, acts[0]) for kind in ("kvc", "q")}
-    sent = []
-    for n, item in enumerate(order):
-        if item == "acts":
-            value, steps = acts[-1], 1
-        else:
-            kind, steps = item[:-1], int(item[-1])
-            value = parcel(kind, steps, *acts[: int(n >= 2)])
-        if n >= 2:
-            value = after(value, sent[n - 2])
-        sent.append(shift_z(value, steps, zs))
-        if item == "acts":
-            acts.append(sent[-1])
-        else:
-            here[item] = sent[-1]
-    late = ["q2", "kc2", "v2"]
-    there = {item: swap_core(here[item], zs) for item in here if item not in late}
-
-    pace = [[], ["kvc1"], ["kvc3"], ["q2"]]
-    swapped = [[], ["kvc0", "q0"], ["q1", "q3"], ["kvc1"]]
+    here, there = {}, {}
+
+    def send(item, *others):
+        kind, shift = item[:-1], int(item[-1])
+        value = parcel(kind, shift, *others)
+        here[item] = shift_z(after(value, *others), shift, zs) if shift else value
+
+    def swap(item, *others):
+        there[item] = swap_core(after(here[item], *others) if others else here[item], zs)
+
+    send("q1")
+    own = after(hyena(hin, halo, filters), here["q1"])
     gain4 = gain.reshape(4, 1, width)
     half = rows // 2
-    normed, diag0, diag1 = None, None, None
-    for j, own in enumerate(acts):
-        own = after(own, *([diag0, diag1] if j else [here["q1"], here["q3"]]))
-        from_x, from_y = swap_chan(own, 1), swap_chan(own, 2)
-        if j:
-            settled = [normed] + [there[item] for item in swapped[j]] + [here[item] for item in pace[j]]
-            from_x, from_y = after(from_x, *settled), after(from_y, *settled)
-        diag0 = swap_chan(from_x[:half], 2)
-        diag1 = swap_chan(from_y[half:], 1)
-        normed = norm(place, j, zs, own, from_x, from_y, diag0, diag1, gain4, normed)
+
+    def near(slab, *others):
+        slab = after(slab, *others) if others else slab
+        return slab, swap_chan(slab, 1), swap_chan(slab, 2)
+
+    def far(slab, from_x, from_y, *others):
+        from_x, from_y = after(from_x, *others), after(from_y, *others)
+        return slab, from_x, from_y, swap_chan(from_x[:half], 2), swap_chan(from_y[half:], 1)
+
+    slab0 = near(own)
+    up, down = step_z(own, 1, (0, 1, 2)), step_z(own, -1, (1, 2, 3))
+    send("kvc1", own)
+    send("kvc0", own)
+    send("q0", own)
+    slab = jnp.where(z < 2, down, up)
+    rest = jnp.where(z == 1, up, down)
+    up, down = after(up, *slab0), after(down, *slab0)
+    up, down = step_z(up, 1, (1, 2)), step_z(down, -1, (1, 2))
+    send("kvc3", here["kvc1"])
+    swap("kvc0")
+    swap("q0")
+    slab0 = far(*slab0, here["q0"])
+    slab1 = near(slab, *slab0[3:])
+    normed = norm(place, 0, zs, *slab0, gain4, None)
+    slab = jnp.where(z < 2, down, up)
+    ends = [(2 * a + k, 2 * b + k) for a, b in ((1, 0), (2, 3)) for k in range(2)]
+    end = lax.ppermute(after(slab, *slab1), "seq", ends)
+    send("q3", here["kvc3"])
+    slab1 = far(*slab1, normed, here["kvc1"], there["kvc0"], there["q0"])
+    slab2 = near(slab, *slab1[3:])
+    normed = norm(place, 1, zs, *slab1, gain4, normed)
+    slab = jnp.where(z % 3 == 0, end, rest)
+    send("q2", end)
+    swap("q1")
+    swap("kvc1")
+    slab2 = far(*slab2, normed, here["kvc3"], there["q1"], there["kvc1"])
+    slab3 = near(slab, *slab2[3:])
+    normed = norm(place, 2, zs, *slab2, gain4, normed)
+    send("kc2", here["q3"])
+    send("v2", here["q2"])
+    swap("q3")
+    swap("kvc3")
+    slab3 = far(*slab3, normed, here["q2"], there["q3"])
+    normed = norm(place, 3, zs, *slab3, gain4, normed)
 
     def sides(*items):
         return [[side[item] for item in items] for side in (here, there)]
 
     early = (0, 1, 3)
-    there["q2"] = swap_core(after(here["q2"], diag0, diag1), zs)
-    there["kc2"] = swap_core(after(here["kc2"], diag0, diag1), zs)
+    swap("q2", *slab3[3:])
+    swap("kc2", *slab3[3:])
     (q,) = project(place, normed, *sides("q0", "q1", "q3", "q2"), early + (2,), 1, True)
     k_early, v_early = project(place, normed, *sides("kvc0", "kvc1", "kvc3"), early, 2, False)
     kept = sum(sides("kvc0", "kvc1", "kc2", "kvc3"), [])
     ck, cv = pack(kept, [depth if i % zs == 2 else 2 * depth for i in range(2 * zs)], crow)
     (k,) = project(place, after(normed, q, ck), *sides("kc2"), (2,), 1, True, (k_early,))
     k_sib = swap_core(k, zs)
-    there["v2"] = swap_core(after(here["v2"], k), zs)
+    swap("v2", k)
     (v,) = project(place, normed, *sides("v2"), (2,), 1, True, (v_early,))
     v_sib = swap_core(v, zs)
     pieces, out = {}, None
@@ -493,7 +521,7 @@
 
 def solution(mesh):
     sizes = mesh.shape
-    paired = sizes["chan"] == 4 and HEADS // sizes["chan"] == sizes["seq"]
+    paired = sizes["chan"] == 4 and sizes["seq"] == 8
     return jax.shard_map(
         fast_body if paired else body,
         mesh=mesh,

time: 170 us -> 204 us (1.20)
  waiting for transfers between devices: 78.9 us -> 52.7 us
  starting transfers between devices: 36.2 us -> 62.1 us
  local copies, waits for them, and re-layouts: 11.7 us -> 35.9 us
  other arithmetic: 2.46 us -> 9.24 us
    ppermute x13 -> x10, waiting for transfers between devices: 61.9 us -> 36.6 us  [shift_z(): return lax.ppermute(value, 'seq', pairs)]
    unnamed x62 -> x70, local copies, waits for them, and re-layouts: 6.76 us -> 22.2 us
    ppermute x13 -> x10, starting transfers between devices: 14.5 us -> 26.6 us  [shift_z(): return lax.ppermute(value, 'seq', pairs)]
    ppermute x0 -> x5, starting transfers between devices: none -> 12 us  [the longest x4 10.6 us: step_z(): lax.ppermute(value, 'seq', [(2 * a + k, 2 * (a + steps) + k) for a in sou...]
    ppermute x0 -> x5, waiting for transfers between devices: none -> 7.29 us  [the longest x4 7.29 us: step_z(): lax.ppermute(value, 'seq', [(2 * a + k, 2 * (a + steps) + k) for a in sou...]
    ppermute x16, waiting for transfers between devices: 11.5 us -> 5.99 us  [swap_chan(): return lax.ppermute(value, 'chan', [(c, c ^ bit) for c in range(4)])]
    select_n x0 -> x3, other arithmetic: none -> 5.06 us  [the longest x2 3.79 us: fast_body(): slab = jnp.where(z < 2, down, up)]
    squeeze x2 -> x7, local copies, waits for them, and re-layouts: 3.1 us -> 7.4 us  [parcel(): lax.dynamic_slice(source, ('qkv'.index(p), 0, at), (1, depth, cols))[0]]
  transfers between devices with their start and end apart: 41 -> 43, of which waited for: 20 -> 15; matrix products, arithmetic and copies ran while one was open for 4% -> 11% of each run, Pallas kernels for 20% -> 18%
where the time goes in v4:
time: 204 us; the launch traced here: 202 us
  starting transfers between devices  62.1 us (30%)
  waiting for transfers between devices  52.7 us (26%)
  Pallas kernels  41.8 us (20%)
  local copies, waits for them, and re-layouts  35.9 us (18%)
  other arithmetic  9.24 us (5%)
    ppermute x10, waiting for transfers between devices, shift_z(): return lax.ppermute(value, 'seq', pairs)  36.6 us
    ppermute x10, starting transfers between devices, shift_z(): return lax.ppermute(value, 'seq', pairs)  26.6 us
    unnamed x70, local copies, waits for them, and re-layouts  22.2 us
    ppermute x16, starting transfers between devices, swap_chan(): return lax.ppermute(value, 'chan', [(c, c ^ bit) for c in range(4)])  18.4 us
    pallas_call x3, Pallas kernels, attend(): pl.pallas_call(functools.partial(attend_kernel, shifts), in_specs=[SMEM]...  13.9 us
    ppermute x4, starting transfers between devices, step_z(): lax.ppermute(value, 'seq', [(2 * a + k, 2 * (a + steps) + k) for a in sou...  10.6 us
    pallas_call x4, Pallas kernels, project(): pl.pallas_call(functools.partial(project_kernel, shifts, zs, count), in_s...  10.1 us
    pallas_call x4, Pallas kernels, norm(): pl.pallas_call(functools.partial(norm_kernel, j), in_specs=[SMEM] + [VMEM...  9.75 us
  transfers between devices with their start and end apart: 43, of which 15 were waited for; matrix products, arithmetic and copies ran while one was open for 11% of the time, Pallas kernels for 18%

profile of v4, /device:TPU:0, one launch (start us, length us, event | category | flops | bytes accessed | tf_op | source)
XLA Modules:
  0.0 202.4 jit_solution(15613511933958591406)
XLA Ops:
  1.2 3.1 %collective-permute-start = (bf16[128,1024]{1,0:T(8,128)(2,1)S(1)}, bf16[128,1024]{1,0:T(8,128)(2,1)}, u32[]{:S(2)}, u32[]{:S(2)}) collective-permute-start(bf16[128,1024]{1,0:T(8,128)(2,1)S(1)} %fusion), channel_id=1, source_target_pairs={{0,4},{4,8},{8,12},{12,16},{16,20},{20,24},{24,28},{1,5},{5,9},{9,... | collective-permute-start | bytes 786440 | tf_op jit(solution)/shard_map/ppermute | solution.py:357
  5.3 2.0 collective-permute-start.1
  9.2 6.0 %hyena_filters.1.own_ref = bf16[256,1024]{1,0:T(8,128)(2,1)S(1)} custom-call(bf16[3,256,1024]{2,1,0:T(8,128)(2,1)S(1)} %bitcast.37, bf16[128,1024]{1,0:T(8,128)(2,1)S(1)} %pad_select_fusion.halo_ref, f32[64,128]{1,0:T(8,128)S(1)} %copy-done.23), custom_call_target="tpu_custom_call" | custom-call | flops 1 | bytes 1 | tf_op jit(solution)/shard_map/hyena_filters/pallas_call | solution.py:80
  15.7 1.3 collective-permute-start.2
  17.0 2.9 %collective-permute-start.3 = (bf16[256,1024]{1,0:T(8,128)(2,1)S(1)}, bf16[256,1024]{1,0:T(8,128)(2,1)S(1)}, u32[]{:S(2)}, u32[]{:S(2)}) collective-permute-start(bf16[256,1024]{1,0:T(8,128)(2,1)S(1)} %hyena_filters.1.own_ref), channel_id=1, source_target_pairs={{0,1},{1,0},{2,3},{3,2},{4,5},{5,4},{6,7},{7,6},{8,9},{9,8},{10,11... | collective-permute-start | bytes 1572872 | tf_op jit(solution)/shard_map/ppermute | solution.py:320
  19.9 1.5 collective-permute-start.4
  21.4 6.5 %collective-permute-start.6 = (bf16[256,1024]{1,0:T(8,128)(2,1)S(1)}, bf16[256,1024]{1,0:T(8,128)(2,1)}, u32[]{:S(2)}, u32[]{:S(2)}) collective-permute-start(bf16[256,1024]{1,0:T(8,128)(2,1)S(1)} %hyena_filters.1.own_ref), channel_id=1, source_target_pairs={{0,8},{4,12},{8,16},{12,20},{16,24},{20,28},{1,9},{5,13},{9,17},{1... | collective-permute-start | bytes 1572872 | tf_op jit(solution)/shard_map/ppermute | solution.py:312
  28.0 1.4 dynamic-slice_bitcast_fusion.7
  31.6 2.1 %collective-permute-done.2 = bf16[256,1024]{1,0:T(8,128)(2,1)} collective-permute-done((bf16[256,1024]{1,0:T(8,128)(2,1)S(1)}, bf16[256,1024]{1,0:T(8,128)(2,1)}, u32[]{:S(2)}, u32[]{:S(2)}) %collective-permute-start.2) | collective-permute-done | bytes 524320 | tf_op jit(solution)/shard_map/ppermute | solution.py:312
  34.3 5.2 %collective-permute-done.6 = bf16[256,1024]{1,0:T(8,128)(2,1)} collective-permute-done((bf16[256,1024]{1,0:T(8,128)(2,1)S(1)}, bf16[256,1024]{1,0:T(8,128)(2,1)}, u32[]{:S(2)}, u32[]{:S(2)}) %collective-permute-start.6) | collective-permute-done | bytes 524320 | tf_op jit(solution)/shard_map/ppermute | solution.py:312
  41.7 1.9 broadcast_select_fusion.own_ref
  43.6 8.5 %collective-permute-done.13.refs_1_ = bf16[1344,256]{1,0:T(8,128)(2,1)S(1)} collective-permute-done((bf16[1344,256]{1,0:T(8,128)(2,1)}, bf16[1344,256]{1,0:T(8,128)(2,1)S(1)}, u32[]{:S(2)}, u32[]{:S(2)}) %collective-permute-start.13) | collective-permute-done | bytes 688160 | tf_op jit(solution)/shard_map/ppermute | solution.py:308
  52.0 1.3 collective-permute-start.5
  55.1 1.5 collective-permute-start.7
  60.2 4.9 %collective-permute-start.19 = (bf16[1344,256]{1,0:T(8,128)(2,1)}, bf16[1344,256]{1,0:T(8,128)(2,1)S(1)}, u32[]{:S(2)}, u32[]{:S(2)}) collective-permute-start(bf16[1344,256]{1,0:T(8,128)(2,1)} %pad_maximum_fusion.2), channel_id=1, source_target_pairs={{0,24},{4,28},{8,0},{12,4},{16,8},{20,12},{24,16},{28,20},{1,25},{... | collective-permute-start | bytes 2064392 | tf_op jit(solution)/shard_map/ppermute | solution.py:308
  67.9 2.4 %norm.4.rest_0_ = bf16[4,4,256,1024]{3,2,1,0:T(8,128)(2,1)S(1)} custom-call(s32[7]{0:T(128)S(1)} %pad_add_fusion.place_ref, bf16[256,1024]{1,0:T(8,128)(2,1)S(1)} %hyena_filters.1.own_ref, bf16[256,1024]{1,0:T(8,128)(2,1)S(1)} %copy-done.6, bf16[256,1024]{1,0:T(8,128)(2,1)} %collective-permute-done.4.y_ref, bf16[128,1024]{1,0:T(8,128)(2,1)S(1)} %copy-done.18, ...), custom_call_target="tpu_custom_call" | custom-call | flops 1 | bytes 1 | tf_op jit(solution)/shard_map/norm/pallas_call | solution.py:119
  70.3 3.3 %copy-done = bf16[4,4,256,1024]{3,2,1,0:T(8,128)(2,1)} copy-done((bf16[4,4,256,1024]{3,2,1,0:T(8,128)(2,1)}, bf16[4,4,256,1024]{3,2,1,0:T(8,128)(2,1)S(1)}, u32[]{:S(2)}) %copy-start) | copy-done | bytes 8388632
  74.6 1.6 collective-permute-start.16
  77.2 1.6 collective-permute-start.17
  78.8 1.9 broadcast_select_fusion.1.own_ref
  82.1 9.4 %collective-permute-start.27 = (bf16[512,256]{1,0:T(8,128)(2,1)S(1)}, bf16[512,256]{1,0:T(8,128)(2,1)}, u32[]{:S(2)}, u32[]{:S(2)}) collective-permute-start(bf16[512,256]{1,0:T(8,128)(2,1)S(1)} %dynamic-slice_bitcast_fusion.2), channel_id=1, source_target_pairs={{0,24},{4,28},{8,0},{12,4},{16,8},{20,12},{24,16},{28,20},{1,25},{... | collective-permute-start | bytes 786440 | tf_op jit(solution)/shard_map/ppermute | solution.py:308
  94.0 1.5 collective-permute-start.12
  95.6 3.4 %copy-done.1 = bf16[4,4,256,1024]{3,2,1,0:T(8,128)(2,1)S(1)} copy-done((bf16[4,4,256,1024]{3,2,1,0:T(8,128)(2,1)S(1)}, bf16[4,4,256,1024]{3,2,1,0:T(8,128)(2,1)}, u32[]{:S(2)}) %copy-start.1) | copy-done | bytes 8388632
  100.8 2.7 %norm.5.rest_0_ = bf16[4,4,256,1024]{3,2,1,0:T(8,128)(2,1)S(1)} custom-call(s32[7]{0:T(128)S(1)} %copy-done.22, bf16[256,1024]{1,0:T(8,128)(2,1)} %broadcast_select_fusion.own_ref, bf16[256,1024]{1,0:T(8,128)(2,1)} %collective-permute-done.10.x_ref, bf16[256,1024]{1,0:T(8,128)(2,1)} %collective-permute-done.11.y_ref, ...), custom_call_target="tpu_custom_call", output_to_operand_aliasing={{}: (7, {})} | custom-call | flops 1 | bytes 1 | tf_op jit(solution)/shard_map/norm/pallas_call | solution.py:119
  104.6 1.6 collective-permute-start.22
  107.1 1.6 collective-permute-start.24
  108.7 1.3 select_select_fusion.own_ref
  110.0 3.3 %collective-permute-done.22.d0_ref = bf16[128,1024]{1,0:T(8,128)(2,1)S(1)} collective-permute-done((bf16[128,1024]{1,0:T(8,128)(2,1)S(1)}, bf16[128,1024]{1,0:T(8,128)(2,1)S(1)}, u32[]{:S(2)}, u32[]{:S(2)}) %collective-permute-start.22) | collective-permute-done | bytes 262176 | tf_op jit(solution)/shard_map/ppermute | solution.py:320
  113.3 2.3 %collective-permute-done.24.d1_ref = bf16[128,1024]{1,0:T(8,128)(2,1)S(1)} collective-permute-done((bf16[128,1024]{1,0:T(8,128)(2,1)S(1)}, bf16[128,1024]{1,0:T(8,128)(2,1)S(1)}, u32[]{:S(2)}, u32[]{:S(2)}) %collective-permute-start.24) | collective-permute-done | bytes 262176 | tf_op jit(solution)/shard_map/ppermute | solution.py:320
  115.6 1.5 collective-permute-start.25
  119.6 3.4 %collective-permute-start.26 = (bf16[512,256]{1,0:T(8,128)(2,1)S(1)}, bf16[512,256]{1,0:T(8,128)(2,1)S(1)}, u32[]{:S(2)}, u32[]{:S(2)}) collective-permute-start(bf16[512,256]{1,0:T(8,128)(2,1)S(1)} %dynamic-slice_bitcast_fusion.3), channel_id=1, source_target_pairs={{0,16},{4,20},{8,24},{12,28},{16,0},{20,4},{24,8},{28,12},{1,17},{... | collective-permute-start | bytes 786440 | tf_op jit(solution)/shard_map/ppermute | solution.py:308
  123.1 2.7 %norm.6.rest_0_ = bf16[4,4,256,1024]{3,2,1,0:T(8,128)(2,1)S(1)} custom-call(s32[7]{0:T(128)S(1)} %copy-done.22, bf16[256,1024]{1,0:T(8,128)(2,1)} %broadcast_select_fusion.1.own_ref, bf16[256,1024]{1,0:T(8,128)(2,1)} %collective-permute-done.18.x_ref, bf16[256,1024]{1,0:T(8,128)(2,1)} %collective-permute-done.23.y_ref, ...), custom_call_target="tpu_custom_call", output_to_operand_aliasing={{}: (7, {})} | custom-call | flops 1 | bytes 1 | tf_op jit(solution)/shard_map/norm/pallas_call | solution.py:119
  125.9 18.9 %collective-permute-done.26.refs_3_ = bf16[512,256]{1,0:T(8,128)(2,1)S(1)} collective-permute-done((bf16[512,256]{1,0:T(8,128)(2,1)S(1)}, bf16[512,256]{1,0:T(8,128)(2,1)S(1)}, u32[]{:S(2)}, u32[]{:S(2)}) %collective-permute-start.26) | collective-permute-done | bytes 262176 | tf_op jit(solution)/shard_map/ppermute | solution.py:308
  144.8 1.6 collective-permute-start.30
  147.0 6.5 %collective-permute-done.33.refs_2_.refs_0_ = bf16[832,256]{1,0:T(8,128)(2,1)S(1)} collective-permute-done((bf16[832,256]{1,0:T(8,128)(2,1)S(1)}, bf16[832,256]{1,0:T(8,128)(2,1)S(1)}, u32[]{:S(2)}, u32[]{:S(2)}) %collective-permute-start.33) | collective-permute-done | bytes 426016 | tf_op jit(solution)/shard_map/ppermute | solution.py:308
  155.3 1.9 norm.7.normed_ref
  157.2 3.3 %copy-done.2 = bf16[4,4,256,1024]{3,2,1,0:T(8,128)(2,1)} copy-done((bf16[4,4,256,1024]{3,2,1,0:T(8,128)(2,1)}, bf16[4,4,256,1024]{3,2,1,0:T(8,128)(2,1)S(1)}, u32[]{:S(2)}) %copy-start.2) | copy-done | bytes 8388632
  160.5 3.4 %copy-done.3 = bf16[4,4,256,1024]{3,2,1,0:T(8,128)(2,1)S(1)} copy-done((bf16[4,4,256,1024]{3,2,1,0:T(8,128)(2,1)S(1)}, bf16[4,4,256,1024]{3,2,1,0:T(8,128)(2,1)}, u32[]{:S(2)}) %copy-start.3) | copy-done | bytes 8388632
  163.9 4.0 %project.5 = (f32[4,256,256]{2,1,0:T(8,128)S(1)}, f32[4,256,256]{2,1,0:T(8,128)S(1)}) custom-call(s32[7]{0:T(128)S(1)} %copy-done.22, bf16[4,4,256,1024]{3,2,1,0:T(8,128)(2,1)S(1)} %copy-done.3, bf16[1344,256]{1,0:T(8,128)(2,1)S(1)} %pad_maximum_fusion.1.refs_0_, bf16[1344,256]{1,0:T(8,128)(2,1)S(1)} %collective-permute-done.13.refs_1_, ...), custom_call_target="tpu_custom_call" | custom-call | flops 1 | bytes 1 | tf_op jit(solution)/shard_map/project/pallas_call | solution.py:155
  168.0 3.6 %project.4.q_ref = bf16[4,256,256]{2,1,0:T(8,128)(2,1)S(1)} custom-call(s32[7]{0:T(128)S(1)} %copy-done.22, bf16[4,4,256,1024]{3,2,1,0:T(8,128)(2,1)S(1)} %copy-done.3, bf16[512,256]{1,0:T(8,128)(2,1)S(1)} %copy-done.8, bf16[512,256]{1,0:T(8,128)(2,1)} %collective-permute-done.1.refs_1_, bf16[512,256]{1,0:T(8,128)(2,1)} %collective-permute-done.27.refs_2_, ...), custom_call_target="tpu_custom_call" | custom-call | flops 1 | bytes 1 | tf_op jit(solution)/shard_map/project/pallas_call | solution.py:155
  171.7 1.3 project.6.k_ref
  176.1 1.8 collective-permute-done.39.vs_ref
  177.9 3.9 %attend.3 = bf16[256,256]{1,0:T(8,128)(2,1)S(1)} custom-call(s32[7]{0:T(128)S(1)} %copy-done.22, bf16[4,256,256]{2,1,0:T(8,128)(2,1)S(1)} %project.4.q_ref, bf16[4,256,256]{2,1,0:T(8,128)(2,1)S(1)} %project.6.k_ref, bf16[4,256,256]{2,1,0:T(8,128)(2,1)S(1)} %project.7.v_ref, bf16[4,256,256]{2,1,0:T(8,128)(2,1)S(1)} %collective-permute-done.38.ks_ref, ...), custom_call_target="tpu_custom_call" | custom-call | flops 1 | bytes 1 | tf_op jit(solution)/shard_map/attend/pallas_call | solution.py:247
  181.8 1.6 collective-permute-start.40
  183.4 7.4 %attend.4 = (bf16[256,256]{1,0:T(8,128)(2,1)S(1)}, bf16[256,256]{1,0:T(8,128)(2,1)S(1)}) custom-call(s32[7]{0:T(128)S(1)} %copy-done.22, bf16[4,256,256]{2,1,0:T(8,128)(2,1)S(1)} %project.4.q_ref, bf16[4,256,256]{2,1,0:T(8,128)(2,1)S(1)} %project.6.k_ref, bf16[4,256,256]{2,1,0:T(8,128)(2,1)S(1)} %project.7.v_ref, ...), custom_call_target="tpu_custom_call" | custom-call | flops 1 | bytes 1 | tf_op jit(solution)/shard_map/attend/pallas_call | solution.py:247
  191.7 3.0 %collective-permute-start.42 = (bf16[256,256]{1,0:T(8,128)(2,1)S(1)}, bf16[256,256]{1,0:T(8,128)(2,1)S(1)}, u32[]{:S(2)}, u32[]{:S(2)}) collective-permute-start(bf16[256,256]{1,0:T(8,128)(2,1)S(1)} %get-tuple-element.82), channel_id=1, source_target_pairs={{0,24},{4,28},{8,0},{12,4},{16,8},{20,12},{24,16},{28,20},{1,25},{... | collective-permute-start | bytes 393224 | tf_op jit(solution)/shard_map/ppermute | solution.py:308
  194.7 2.6 %attend.5.refs_0_ = bf16[256,256]{1,0:T(8,128)(2,1)S(1)} custom-call(s32[7]{0:T(128)S(1)} %copy-done.22, bf16[4,256,256]{2,1,0:T(8,128)(2,1)S(1)} %project.4.q_ref, bf16[4,256,256]{2,1,0:T(8,128)(2,1)S(1)} %project.6.k_ref, bf16[4,256,256]{2,1,0:T(8,128)(2,1)S(1)} %project.7.v_ref, bf16[4,256,256]{2,1,0:T(8,128)(2,1)S(1)} %collective-permute-done.38.ks_ref, ...), custom_call_target="tpu_custom_call" | custom-call | flops 1 | bytes 1 | tf_op jit(solution)/shard_map/attend/pallas_call | solution.py:247
  200.5 2.0 join.1
  (150 shorter events, 39.8 us)
Async XLA Ops:
  1.2 6.9 %collective-permute-start = (bf16[128,1024]{1,0:T(8,128)(2,1)S(1)}, bf16[128,1024]{1,0:T(8,128)(2,1)}, u32[]{:S(2)}, u32[]{:S(2)}) collective-permute-start(bf16[128,1024]{1,0:T(8,128)(2,1)S(1)} %fusion), channel_id=1, source_target_pairs={{0,4},{4,8},{8,12},{12,16},{16,20},{20,24},{24,28},{1,5},{5,9},{9,... | collective-permute-start | bytes 786440 | tf_op jit(solution)/shard_map/ppermute | solution.py:357
  5.3 10.4 %collective-permute-start.1 = (bf16[512,256]{1,0:T(8,128)(2,1)S(1)}, bf16[512,256]{1,0:T(8,128)(2,1)}, u32[]{:S(2)}, u32[]{:S(2)}) collective-permute-start(bf16[512,256]{1,0:T(8,128)(2,1)S(1)} %dynamic-slice_bitcast_fusion.11), channel_id=1, source_target_pairs={{0,8},{4,12},{8,16},{12,20},{16,24},{20,28},{24,0},{28,4},{1,9},{5... | collective-permute-start | bytes 786440 | tf_op jit(solution)/shard_map/ppermute | solution.py:308
  15.7 17.9 %collective-permute-start.2 = (bf16[256,1024]{1,0:T(8,128)(2,1)S(1)}, bf16[256,1024]{1,0:T(8,128)(2,1)}, u32[]{:S(2)}, u32[]{:S(2)}) collective-permute-start(bf16[256,1024]{1,0:T(8,128)(2,1)S(1)} %hyena_filters.1.own_ref), channel_id=1, source_target_pairs={{8,0},{12,4},{16,8},{20,12},{24,16},{28,20},{9,1},{13,5},{17,9},{2... | collective-permute-start | bytes 1572872 | tf_op jit(solution)/shard_map/ppermute | solution.py:312
  17.0 16.6 %collective-permute-start.3 = (bf16[256,1024]{1,0:T(8,128)(2,1)S(1)}, bf16[256,1024]{1,0:T(8,128)(2,1)S(1)}, u32[]{:S(2)}, u32[]{:S(2)}) collective-permute-start(bf16[256,1024]{1,0:T(8,128)(2,1)S(1)} %hyena_filters.1.own_ref), channel_id=1, source_target_pairs={{0,1},{1,0},{2,3},{3,2},{4,5},{5,4},{6,7},{7,6},{8,9},{9,8},{10,11... | collective-permute-start | bytes 1572872 | tf_op jit(solution)/shard_map/ppermute | solution.py:320
  19.9 14.4 %collective-permute-start.4 = (bf16[256,1024]{1,0:T(8,128)(2,1)S(1)}, bf16[256,1024]{1,0:T(8,128)(2,1)}, u32[]{:S(2)}, u32[]{:S(2)}) collective-permute-start(bf16[256,1024]{1,0:T(8,128)(2,1)S(1)} %hyena_filters.1.own_ref), channel_id=1, source_target_pairs={{0,2},{1,3},{2,0},{3,1},{4,6},{5,7},{6,4},{7,5},{8,10},{9,11},{10,... | collective-permute-start | bytes 1572872 | tf_op jit(solution)/shard_map/ppermute | solution.py:320
  21.4 18.1 %collective-permute-start.6 = (bf16[256,1024]{1,0:T(8,128)(2,1)S(1)}, bf16[256,1024]{1,0:T(8,128)(2,1)}, u32[]{:S(2)}, u32[]{:S(2)}) collective-permute-start(bf16[256,1024]{1,0:T(8,128)(2,1)S(1)} %hyena_filters.1.own_ref), channel_id=1, source_target_pairs={{0,8},{4,12},{8,16},{12,20},{16,24},{20,28},{1,9},{5,13},{9,17},{1... | collective-permute-start | bytes 1572872 | tf_op jit(solution)/shard_map/ppermute | solution.py:312
  30.3 21.8 %collective-permute-start.13 = (bf16[1344,256]{1,0:T(8,128)(2,1)}, bf16[1344,256]{1,0:T(8,128)(2,1)S(1)}, u32[]{:S(2)}, u32[]{:S(2)}) collective-permute-start(bf16[1344,256]{1,0:T(8,128)(2,1)} %pad_maximum_fusion), channel_id=1, source_target_pairs={{0,8},{4,12},{8,16},{12,20},{16,24},{20,28},{24,0},{28,4},{1,9},{5... | collective-permute-start | bytes 2064392 | tf_op jit(solution)/shard_map/ppermute | solution.py:308
  33.6 26.6 %collective-permute-start.14 = (bf16[1344,256]{1,0:T(8,128)(2,1)S(1)}, bf16[1344,256]{1,0:T(8,128)(2,1)S(1)}, u32[]{:S(2)}, u32[]{:S(2)}) collective-permute-start(bf16[1344,256]{1,0:T(8,128)(2,1)S(1)} %pad_maximum_fusion.1.refs_0_), channel_id=1, source_target_pairs={{0,4},{4,0},{8,12},{12,8},{16,20},{20,16},{24,28},{28,24},{1,5},{5... | collective-permute-start | bytes 2064392 | tf_op jit(solution)/shard_map/ppermute | solution.py:316
  33.6 20.8 %copy-start.5 = (bf16[256,1024]{1,0:T(8,128)(2,1)}, bf16[256,1024]{1,0:T(8,128)(2,1)S(1)}, u32[]{:S(2)}) copy-start(bf16[256,1024]{1,0:T(8,128)(2,1)S(1)} %collective-permute-done.3.x_ref) | copy-start | bytes 1572868
  33.6 24.2 %collective-permute-start.15 = (bf16[512,256]{1,0:T(8,128)(2,1)S(1)}, bf16[512,256]{1,0:T(8,128)(2,1)S(1)}, u32[]{:S(2)}, u32[]{:S(2)}) collective-permute-start(bf16[512,256]{1,0:T(8,128)(2,1)S(1)} %get-tuple-element.89.refs_0_), channel_id=1, source_target_pairs={{0,4},{4,0},{8,12},{12,8},{16,20},{20,16},{24,28},{28,24},{1,5},{5... | collective-permute-start | bytes 786440 | tf_op jit(solution)/shard_map/ppermute | solution.py:316
  39.5 14.9 %collective-permute-start.8 = (bf16[128,1024]{1,0:T(8,128)(2,1)S(1)}, bf16[128,1024]{1,0:T(8,128)(2,1)S(1)}, u32[]{:S(2)}, u32[]{:S(2)}) collective-permute-start(bf16[128,1024]{1,0:T(8,128)(2,1)S(1)} %slice.32), channel_id=1, source_target_pairs={{0,2},{1,3},{2,0},{3,1},{4,6},{5,7},{6,4},{7,5},{8,10},{9,11},{10,... | collective-permute-start | bytes 786440 | tf_op jit(solution)/shard_map/ppermute | solution.py:320
  41.1 15.5 %collective-permute-start.9 = (bf16[128,1024]{1,0:T(8,128)(2,1)S(1)}, bf16[128,1024]{1,0:T(8,128)(2,1)S(1)}, u32[]{:S(2)}, u32[]{:S(2)}) collective-permute-start(bf16[128,1024]{1,0:T(8,128)(2,1)S(1)} %slice.33), channel_id=1, source_target_pairs={{0,1},{1,0},{2,3},{3,2},{4,5},{5,4},{6,7},{7,6},{8,9},{9,8},{10,11... | collective-permute-start | bytes 786440 | tf_op jit(solution)/shard_map/ppermute | solution.py:320
  43.6 22.3 %copy-start.14 = (f32[4096]{0:T(1024)S(1)}, f32[4096]{0:T(1024)}, u32[]{:S(2)}) copy-start(f32[4096]{0:T(1024)} %param.11) | copy-start | bytes 49156
  52.0 25.2 %collective-permute-start.5 = (bf16[256,1024]{1,0:T(8,128)(2,1)}, bf16[256,1024]{1,0:T(8,128)(2,1)}, u32[]{:S(2)}, u32[]{:S(2)}) collective-permute-start(bf16[256,1024]{1,0:T(8,128)(2,1)} %collective-permute-done.2), channel_id=1, source_target_pairs={{8,0},{12,4},{16,8},{20,12},{9,1},{13,5},{17,9},{21,13},{10,2},{14... | collective-permute-start | bytes 1572872 | tf_op jit(solution)/shard_map/ppermute | solution.py:312
  55.1 23.6 %collective-permute-start.7 = (bf16[256,1024]{1,0:T(8,128)(2,1)}, bf16[256,1024]{1,0:T(8,128)(2,1)}, u32[]{:S(2)}, u32[]{:S(2)}) collective-permute-start(bf16[256,1024]{1,0:T(8,128)(2,1)} %collective-permute-done.6), channel_id=1, source_target_pairs={{8,16},{12,20},{16,24},{20,28},{9,17},{13,21},{17,25},{21,29},{10,... | collective-permute-start | bytes 1572872 | tf_op jit(solution)/shard_map/ppermute | solution.py:312
  57.3 16.3 %collective-permute-start.10 = (bf16[256,1024]{1,0:T(8,128)(2,1)}, bf16[256,1024]{1,0:T(8,128)(2,1)}, u32[]{:S(2)}, u32[]{:S(2)}) collective-permute-start(bf16[256,1024]{1,0:T(8,128)(2,1)} %broadcast_select_fusion.own_ref), channel_id=1, source_target_pairs={{0,1},{1,0},{2,3},{3,2},{4,5},{5,4},{6,7},{7,6},{8,9},{9,8},{10,11... | collective-permute-start | bytes 1572872 | tf_op jit(solution)/shard_map/ppermute | solution.py:320
  58.6 16.1 %collective-permute-start.11 = (bf16[256,1024]{1,0:T(8,128)(2,1)}, bf16[256,1024]{1,0:T(8,128)(2,1)}, u32[]{:S(2)}, u32[]{:S(2)}) collective-permute-start(bf16[256,1024]{1,0:T(8,128)(2,1)} %broadcast_select_fusion.own_ref), channel_id=1, source_target_pairs={{0,2},{1,3},{2,0},{3,1},{4,6},{5,7},{6,4},{7,5},{8,10},{9,11},{10,... | collective-permute-start | bytes 1572872 | tf_op jit(solution)/shard_map/ppermute | solution.py:320
  60.2 21.0 %collective-permute-start.19 = (bf16[1344,256]{1,0:T(8,128)(2,1)}, bf16[1344,256]{1,0:T(8,128)(2,1)S(1)}, u32[]{:S(2)}, u32[]{:S(2)}) collective-permute-start(bf16[1344,256]{1,0:T(8,128)(2,1)} %pad_maximum_fusion.2), channel_id=1, source_target_pairs={{0,24},{4,28},{8,0},{12,4},{16,8},{20,12},{24,16},{28,20},{1,25},{... | collective-permute-start | bytes 2064392 | tf_op jit(solution)/shard_map/ppermute | solution.py:308
  73.6 29.9 %collective-permute-start.21 = (bf16[1344,256]{1,0:T(8,128)(2,1)S(1)}, bf16[1344,256]{1,0:T(8,128)(2,1)S(1)}, u32[]{:S(2)}, u32[]{:S(2)}) collective-permute-start(bf16[1344,256]{1,0:T(8,128)(2,1)S(1)} %collective-permute-done.13.refs_1_), channel_id=1, source_target_pairs={{0,4},{4,0},{8,12},{12,8},{16,20},{20,16},{24,28},{28,24},{1,5},{5... | collective-permute-start | bytes 2064392 | tf_op jit(solution)/shard_map/ppermute | solution.py:316
  74.6 20.9 %copy-start.22 = (s32[7]{0:T(128)S(1)}, s32[7]{0:T(128)}, u32[]{:S(2)}) copy-start(s32[7]{0:T(128)} %copy-done.21) | copy-start | bytes 88
  74.6 16.9 %collective-permute-start.16 = (bf16[128,1024]{1,0:T(8,128)(2,1)S(1)}, bf16[128,1024]{1,0:T(8,128)(2,1)S(1)}, u32[]{:S(2)}, u32[]{:S(2)}) collective-permute-start(bf16[128,1024]{1,0:T(8,128)(2,1)S(1)} %slice.34), channel_id=1, source_target_pairs={{0,2},{1,3},{2,0},{3,1},{4,6},{5,7},{6,4},{7,5},{8,10},{9,11},{10,... | collective-permute-start | bytes 786440 | tf_op jit(solution)/shard_map/ppermute | solution.py:320
  77.2 15.0 %collective-permute-start.17 = (bf16[128,1024]{1,0:T(8,128)(2,1)S(1)}, bf16[128,1024]{1,0:T(8,128)(2,1)S(1)}, u32[]{:S(2)}, u32[]{:S(2)}) collective-permute-start(bf16[128,1024]{1,0:T(8,128)(2,1)S(1)} %slice.35), channel_id=1, source_target_pairs={{0,1},{1,0},{2,3},{3,2},{4,5},{5,4},{6,7},{7,6},{8,9},{9,8},{10,11... | collective-permute-start | bytes 786440 | tf_op jit(solution)/shard_map/ppermute | solution.py:320
  82.1 13.3 %collective-permute-start.27 = (bf16[512,256]{1,0:T(8,128)(2,1)S(1)}, bf16[512,256]{1,0:T(8,128)(2,1)}, u32[]{:S(2)}, u32[]{:S(2)}) collective-permute-start(bf16[512,256]{1,0:T(8,128)(2,1)S(1)} %dynamic-slice_bitcast_fusion.2), channel_id=1, source_target_pairs={{0,24},{4,28},{8,0},{12,4},{16,8},{20,12},{24,16},{28,20},{1,25},{... | collective-permute-start | bytes 786440 | tf_op jit(solution)/shard_map/ppermute | solution.py:308
  92.9 10.7 %collective-permute-start.18 = (bf16[256,1024]{1,0:T(8,128)(2,1)}, bf16[256,1024]{1,0:T(8,128)(2,1)}, u32[]{:S(2)}, u32[]{:S(2)}) collective-permute-start(bf16[256,1024]{1,0:T(8,128)(2,1)} %broadcast_select_fusion.1.own_ref), channel_id=1, source_target_pairs={{0,1},{1,0},{2,3},{3,2},{4,5},{5,4},{6,7},{7,6},{8,9},{9,8},{10,11... | collective-permute-start | bytes 1572872 | tf_op jit(solution)/shard_map/ppermute | solution.py:320
  93.4 12.7 %collective-permute-start.23 = (bf16[256,1024]{1,0:T(8,128)(2,1)}, bf16[256,1024]{1,0:T(8,128)(2,1)}, u32[]{:S(2)}, u32[]{:S(2)}) collective-permute-start(bf16[256,1024]{1,0:T(8,128)(2,1)} %broadcast_select_fusion.1.own_ref), channel_id=1, source_target_pairs={{0,2},{1,3},{2,0},{3,1},{4,6},{5,7},{6,4},{7,5},{8,10},{9,11},{10,... | collective-permute-start | bytes 1572872 | tf_op jit(solution)/shard_map/ppermute | solution.py:320
  94.0 14.7 %collective-permute-start.12 = (bf16[256,1024]{1,0:T(8,128)(2,1)}, bf16[256,1024]{1,0:T(8,128)(2,1)}, u32[]{:S(2)}, u32[]{:S(2)}) collective-permute-start(bf16[256,1024]{1,0:T(8,128)(2,1)} %broadcast_select_fusion.1.own_ref), channel_id=1, source_target_pairs={{8,0},{12,4},{16,24},{20,28},{9,1},{13,5},{17,25},{21,29},{10,2},{... | collective-permute-start | bytes 1572872 | tf_op jit(solution)/shard_map/ppermute | solution.py:400
  95.4 8.1 %collective-permute-start.20 = (bf16[512,256]{1,0:T(8,128)(2,1)}, bf16[512,256]{1,0:T(8,128)(2,1)}, u32[]{:S(2)}, u32[]{:S(2)}) collective-permute-start(bf16[512,256]{1,0:T(8,128)(2,1)} %collective-permute-done.1.refs_1_), channel_id=1, source_target_pairs={{0,4},{4,0},{8,12},{12,8},{16,20},{20,16},{24,28},{28,24},{1,5},{5... | collective-permute-start | bytes 786440 | tf_op jit(solution)/shard_map/ppermute | solution.py:316
  104.6 8.7 %collective-permute-start.22 = (bf16[128,1024]{1,0:T(8,128)(2,1)S(1)}, bf16[128,1024]{1,0:T(8,128)(2,1)S(1)}, u32[]{:S(2)}, u32[]{:S(2)}) collective-permute-start(bf16[128,1024]{1,0:T(8,128)(2,1)S(1)} %slice.36), channel_id=1, source_target_pairs={{0,2},{1,3},{2,0},{3,1},{4,6},{5,7},{6,4},{7,5},{8,10},{9,11},{10,... | collective-permute-start | bytes 786440 | tf_op jit(solution)/shard_map/ppermute | solution.py:320
  107.1 15.8 %copy-start.24 = (bf16[160,256]{1,0:T(8,128)(2,1)S(1)}, bf16[160,256]{1,0:T(8,128)(2,1)}, u32[]{:S(2)}) copy-start(bf16[160,256]{1,0:T(8,128)(2,1)} %get-tuple-element.94) | copy-start | bytes 245764
  107.1 15.8 %copy-start.25 = (bf16[160,256]{1,0:T(8,128)(2,1)S(1)}, bf16[160,256]{1,0:T(8,128)(2,1)}, u32[]{:S(2)}) copy-start(bf16[160,256]{1,0:T(8,128)(2,1)} %get-tuple-element.101) | copy-start | bytes 245764
  107.1 8.5 %collective-permute-start.24 = (bf16[128,1024]{1,0:T(8,128)(2,1)S(1)}, bf16[128,1024]{1,0:T(8,128)(2,1)S(1)}, u32[]{:S(2)}, u32[]{:S(2)}) collective-permute-start(bf16[128,1024]{1,0:T(8,128)(2,1)S(1)} %slice.37), channel_id=1, source_target_pairs={{0,1},{1,0},{2,3},{3,2},{4,5},{5,4},{6,7},{7,6},{8,9},{9,8},{10,11... | collective-permute-start | bytes 786440 | tf_op jit(solution)/shard_map/ppermute | solution.py:320
  115.6 29.1 %collective-permute-start.25 = (bf16[256,1024]{1,0:T(8,128)(2,1)S(1)}, bf16[256,1024]{1,0:T(8,128)(2,1)S(1)}, u32[]{:S(2)}, u32[]{:S(2)}) collective-permute-start(bf16[256,1024]{1,0:T(8,128)(2,1)S(1)} %select_select_fusion.own_ref), channel_id=1, source_target_pairs={{0,1},{1,0},{2,3},{3,2},{4,5},{5,4},{6,7},{7,6},{8,9},{9,8},{10,11... | collective-permute-start | bytes 1572872 | tf_op jit(solution)/shard_map/ppermute | solution.py:320
  117.1 8.7 %collective-permute-start.28 = (bf16[512,256]{1,0:T(8,128)(2,1)}, bf16[512,256]{1,0:T(8,128)(2,1)S(1)}, u32[]{:S(2)}, u32[]{:S(2)}) collective-permute-start(bf16[512,256]{1,0:T(8,128)(2,1)} %collective-permute-done.27.refs_2_), channel_id=1, source_target_pairs={{0,4},{4,0},{8,12},{12,8},{16,20},{20,16},{24,28},{28,24},{1,5},{5... | collective-permute-start | bytes 786440 | tf_op jit(solution)/shard_map/ppermute | solution.py:316
  117.1 27.7 %collective-permute-start.29 = (bf16[256,1024]{1,0:T(8,128)(2,1)S(1)}, bf16[256,1024]{1,0:T(8,128)(2,1)S(1)}, u32[]{:S(2)}, u32[]{:S(2)}) collective-permute-start(bf16[256,1024]{1,0:T(8,128)(2,1)S(1)} %select_select_fusion.own_ref), channel_id=1, source_target_pairs={{0,2},{1,3},{2,0},{3,1},{4,6},{5,7},{6,4},{7,5},{8,10},{9,11},{10,... | collective-permute-start | bytes 1572872 | tf_op jit(solution)/shard_map/ppermute | solution.py:320
  119.6 25.2 %collective-permute-start.26 = (bf16[512,256]{1,0:T(8,128)(2,1)S(1)}, bf16[512,256]{1,0:T(8,128)(2,1)S(1)}, u32[]{:S(2)}, u32[]{:S(2)}) collective-permute-start(bf16[512,256]{1,0:T(8,128)(2,1)S(1)} %dynamic-slice_bitcast_fusion.3), channel_id=1, source_target_pairs={{0,16},{4,20},{8,24},{12,28},{16,0},{20,4},{24,8},{28,12},{1,17},{... | collective-permute-start | bytes 786440 | tf_op jit(solution)/shard_map/ppermute | solution.py:308
  123.0 30.5 %collective-permute-start.33 = (bf16[832,256]{1,0:T(8,128)(2,1)S(1)}, bf16[832,256]{1,0:T(8,128)(2,1)S(1)}, u32[]{:S(2)}, u32[]{:S(2)}) collective-permute-start(bf16[832,256]{1,0:T(8,128)(2,1)S(1)} %pad_maximum_fusion.3), channel_id=1, source_target_pairs={{0,16},{4,20},{8,24},{12,28},{16,0},{20,4},{24,8},{28,12},{1,17},{... | collective-permute-start | bytes 1277960 | tf_op jit(solution)/shard_map/ppermute | solution.py:308
  125.8 34.7 %collective-permute-start.35 = (bf16[1344,256]{1,0:T(8,128)(2,1)S(1)}, bf16[1344,256]{1,0:T(8,128)(2,1)S(1)}, u32[]{:S(2)}, u32[]{:S(2)}) collective-permute-start(bf16[1344,256]{1,0:T(8,128)(2,1)S(1)} %collective-permute-done.19.refs_3_.refs_2_), channel_id=1, source_target_pairs={{0,4},{4,0},{8,12},{12,8},{16,20},{20,16},{24,28},{28,24},{1,5},{5... | collective-permute-start | bytes 2064392 | tf_op jit(solution)/shard_map/ppermute | solution.py:316
  144.8 8.7 %collective-permute-start.30 = (bf16[128,1024]{1,0:T(8,128)(2,1)S(1)}, bf16[128,1024]{1,0:T(8,128)(2,1)S(1)}, u32[]{:S(2)}, u32[]{:S(2)}) collective-permute-start(bf16[128,1024]{1,0:T(8,128)(2,1)S(1)} %slice.38), channel_id=1, source_target_pairs={{0,2},{1,3},{2,0},{3,1},{4,6},{5,7},{6,4},{7,5},{8,10},{9,11},{10,... | collective-permute-start | bytes 786440 | tf_op jit(solution)/shard_map/ppermute | solution.py:320
  146.4 7.3 %collective-permute-start.31 = (bf16[128,1024]{1,0:T(8,128)(2,1)S(1)}, bf16[128,1024]{1,0:T(8,128)(2,1)S(1)}, u32[]{:S(2)}, u32[]{:S(2)}) collective-permute-start(bf16[128,1024]{1,0:T(8,128)(2,1)S(1)} %slice.39), channel_id=1, source_target_pairs={{0,1},{1,0},{2,3},{3,2},{4,5},{5,4},{6,7},{7,6},{8,9},{9,8},{10,11... | collective-permute-start | bytes 786440 | tf_op jit(solution)/shard_map/ppermute | solution.py:320
  153.7 17.9 %collective-permute-start.34 = (bf16[832,256]{1,0:T(8,128)(2,1)S(1)}, bf16[832,256]{1,0:T(8,128)(2,1)S(1)}, u32[]{:S(2)}, u32[]{:S(2)}) collective-permute-start(bf16[832,256]{1,0:T(8,128)(2,1)S(1)} %collective-permute-done.33.refs_2_.refs_0_), channel_id=1, source_target_pairs={{0,4},{4,0},{8,12},{12,8},{16,20},{20,16},{24,28},{28,24},{1,5},{5... | collective-permute-start | bytes 1277960 | tf_op jit(solution)/shard_map/ppermute | solution.py:316
  153.7 14.2 %collective-permute-start.32 = (bf16[512,256]{1,0:T(8,128)(2,1)S(1)}, bf16[512,256]{1,0:T(8,128)(2,1)S(1)}, u32[]{:S(2)}, u32[]{:S(2)}) collective-permute-start(bf16[512,256]{1,0:T(8,128)(2,1)S(1)} %collective-permute-done.26.refs_3_), channel_id=1, source_target_pairs={{0,4},{4,0},{8,12},{12,8},{16,20},{20,16},{24,28},{28,24},{1,5},{5... | collective-permute-start | bytes 786440 | tf_op jit(solution)/shard_map/ppermute | solution.py:316
  155.2 17.8 %collective-permute-start.36 = (bf16[512,256]{1,0:T(8,128)(2,1)S(1)}, bf16[512,256]{1,0:T(8,128)(2,1)S(1)}, u32[]{:S(2)}, u32[]{:S(2)}) collective-permute-start(bf16[512,256]{1,0:T(8,128)(2,1)S(1)} %dynamic-slice_bitcast_fusion), channel_id=1, source_target_pairs={{0,16},{4,20},{8,24},{12,28},{16,0},{20,4},{24,8},{28,12},{1,17},{... | collective-permute-start | bytes 786440 | tf_op jit(solution)/shard_map/ppermute | solution.py:308
  173.0 1.6 collective-permute-start.37
  173.1 3.0 %collective-permute-start.38 = (bf16[4,256,256]{2,1,0:T(8,128)(2,1)S(1)}, bf16[4,256,256]{2,1,0:T(8,128)(2,1)S(1)}, u32[]{:S(2)}, u32[]{:S(2)}) collective-permute-start(bf16[4,256,256]{2,1,0:T(8,128)(2,1)S(1)} %project.6.k_ref), channel_id=1, source_target_pairs={{0,4},{4,0},{8,12},{12,8},{16,20},{20,16},{24,28},{28,24},{1,5},{5... | collective-permute-start | bytes 1572872 | tf_op jit(solution)/shard_map/ppermute | solution.py:316
  175.9 2.0 collective-permute-start.39
  181.8 12.9 %collective-permute-start.40 = (bf16[256,256]{1,0:T(8,128)(2,1)S(1)}, bf16[256,256]{1,0:T(8,128)(2,1)S(1)}, u32[]{:S(2)}, u32[]{:S(2)}) collective-permute-start(bf16[256,256]{1,0:T(8,128)(2,1)S(1)} %attend.3), channel_id=1, source_target_pairs={{0,16},{4,20},{8,24},{12,28},{16,0},{20,4},{24,8},{28,12},{1,17},{... | collective-permute-start | bytes 393224 | tf_op jit(solution)/shard_map/ppermute | solution.py:308
  190.8 8.2 %collective-permute-start.41 = (bf16[256,256]{1,0:T(8,128)(2,1)S(1)}, bf16[256,256]{1,0:T(8,128)(2,1)S(1)}, u32[]{:S(2)}, u32[]{:S(2)}) collective-permute-start(bf16[256,256]{1,0:T(8,128)(2,1)S(1)} %get-tuple-element.80), channel_id=1, source_target_pairs={{0,8},{4,12},{8,16},{12,20},{16,24},{20,28},{24,0},{28,4},{1,9},{5... | collective-permute-start | bytes 393224 | tf_op jit(solution)/shard_map/ppermute | solution.py:308
  191.7 8.1 %collective-permute-start.42 = (bf16[256,256]{1,0:T(8,128)(2,1)S(1)}, bf16[256,256]{1,0:T(8,128)(2,1)S(1)}, u32[]{:S(2)}, u32[]{:S(2)}) collective-permute-start(bf16[256,256]{1,0:T(8,128)(2,1)S(1)} %get-tuple-element.82), channel_id=1, source_target_pairs={{0,24},{4,28},{8,0},{12,4},{16,8},{20,12},{24,16},{28,20},{1,25},{... | collective-permute-start | bytes 393224 | tf_op jit(solution)/shard_map/ppermute | solution.py:308
  (30 other events, 114.0 us)

commit v5 on v3

--- a/solution.py
+++ b/solution.py
@@ -87,7 +87,7 @@
         ],
         out_specs=pl.BlockSpec((rows, LANES), lambda i: (0, i)),
         out_shape=jax.ShapeDtypeStruct((rows, width), BF16),
-        compiler_params=pltpu.CompilerParams(vmem_limit_bytes=12 * MIB),
+        compiler_params=pltpu.CompilerParams(vmem_limit_bytes=8 * MIB),
         cost_estimate=BRIEF,
         name="hyena_filters",
     )(hin, halo, filters)
@@ -122,42 +122,49 @@
         out_specs=VMEM,
         out_shape=jax.ShapeDtypeStruct((zs, 4, rows, width), BF16),
         input_output_aliases={} if buffer is None else {7: 0},
-        compiler_params=pltpu.CompilerParams(vmem_limit_bytes=16 * MIB),
+        compiler_params=pltpu.CompilerParams(vmem_limit_bytes=4 * MIB),
         cost_estimate=BRIEF,
         name="norm",
     )(*args)
 
 
-def project_kernel(shifts, zs, count, place_ref, normed_ref, *refs):
+def project_kernel(shifts, slabs, parts, zs, extra, apart, place_ref, normed_ref, *refs):
+    groups = 1 + max(group for group, _ in parts)
     n = len(shifts)
-    own, sib, rest = refs[:n], refs[n : 2 * n], refs[2 * n :]
-    before, outs = rest[:-count], rest[-count:]
+    weights, rest = refs[: 2 * n * groups], refs[2 * n * groups :]
+    before, outs = rest[:extra], rest[-len(parts) * (zs if apart else 1) :]
     z, core = place_ref[1], place_ref[2]
     depth = normed_ref.shape[3] // 2
-    for part, out_ref in enumerate(outs):
-        for j in range(zs):
+    for part, (group, row) in enumerate(parts):
+        for j in slabs:
             total = before[part][j] if before else None
             for i, shift in enumerate(shifts):
                 block = lax.rem(z + zs - shift, zs)
-                for k, w_ref in enumerate((own[i], sib[i])):
+                for k in range(2):
                     at = pl.multiple_of((core ^ k) * depth, depth)
                     left = normed_ref[j, block, :, pl.ds(at, depth)]
-                    right = w_ref[part * depth : (part + 1) * depth, :]
+                    right = weights[(2 * group + k) * n + i][row : row + depth, :]
                     term = jnp.dot(left, right, preferred_element_type=F32)
                     total = term if total is None else total + term
-            out_ref[j] = total.astype(out_ref.dtype)
-
-
-def project(place, normed, own, sib, shifts, count, rounded, before=()):
+            if apart:
+                outs[part * zs + j][...] = total.astype(outs[0].dtype)
+            else:
+                outs[part][j] = total.astype(outs[0].dtype)
+
+
+def project(place, normed, groups, parts, shifts, slabs, rounded, before=(), into=(), apart=False):
     zs, _, rows, _ = normed.shape
-    cols = own[0].shape[1]
-    args = [place, normed, *own, *sib, *before]
-    return pl.pallas_call(
-        functools.partial(project_kernel, shifts, zs, count),
+    weights = [w for own, sib in groups for w in (*own, *sib)]
+    args = [place, normed, *weights, *before, *into]
+    shape = (rows, weights[0].shape[1]) if apart else (zs, rows, weights[0].shape[1])
+    out = [jax.ShapeDtypeStruct(shape, BF16 if rounded else F32)] * (len(parts) * (zs if apart else 1))
+    return pl.pallas_call(
+        functools.partial(project_kernel, shifts, slabs, parts, zs, len(before), apart),
         in_specs=[SMEM] + [VMEM] * (len(args) - 1),
-        out_specs=[VMEM] * count,
-        out_shape=[jax.ShapeDtypeStruct((zs, rows, cols), BF16 if rounded else F32)] * count,
-        compiler_params=pltpu.CompilerParams(vmem_limit_bytes=16 * MIB),
+        out_specs=[VMEM] * len(out),
+        out_shape=out,
+        input_output_aliases={len(args) - len(into) + i: i for i in range(len(into))},
+        compiler_params=pltpu.CompilerParams(vmem_limit_bytes=8 * MIB),
         cost_estimate=BRIEF,
         name="project",
     )(*args)
@@ -172,92 +179,113 @@
     return functools.reduce(op, [s[:, i : i + LANES] for i in range(0, full, LANES)]), rest
 
 
-def attend_kernel(shifts, place_ref, q_ref, k_ref, v_ref, ks_ref, vs_ref, ck_ref, cv_ref, *refs):
-    outs, (old, new) = refs[: len(shifts)], refs[len(shifts) :]
+def weigh_kernel(place_ref, q_ref, ck_ref, *refs):
     z, core = place_ref[1], place_ref[2]
-    zs, rows, cols = k_ref.shape
-    heads = range(cols // HEAD)
+    zs, rows, cols = q_ref.shape
+    k_refs, ks_refs, (old_ref, new_ref, sum_ref, k_ref, ks_ref, scratch) = refs[:zs], refs[zs : 2 * zs], refs[2 * zs :]
+    for j in range(zs):
+        k_ref[j], ks_ref[j] = k_refs[j][...], ks_refs[j][...]
+    crow = ck_ref.shape[0]
     factor = 1.4426950408889634 / HEAD**0.5
-    low = -1e30
-    hcols = [slice(h * HEAD, (h + 1) * HEAD) for h in heads]
     row = lax.broadcasted_iota(jnp.int32, (rows, rows), 0)
     col = lax.broadcasted_iota(jnp.int32, (rows, rows), 1)
     causal = col <= row
-
+    slab = [lax.rem(z + zs - b, zs) for b in range(zs)]
+
+    for block in range(zs):
+        for h in range(cols // HEAD):
+            hcol = slice(h * HEAD, (h + 1) * HEAD)
+            query = q_ref[slab[block], :, hcol]
+
+            def score(key):
+                return lax.dot_general(query, key, NT, preferred_element_type=F32)
+
+            s = score(ck_ref[:, hcol])
+            scratch[h, :, :crow] = s
+            top, end = lanes(jnp.maximum, s)
+            for b in range(block + 1):
+                s, t = score(k_ref[slab[b], :, hcol]), score(ks_ref[slab[b], :, hcol])
+                if b == block:
+                    s, t = jnp.where(causal, s, -1e30), jnp.where(core == 1, t, -1e30)
+                at = crow + 2 * rows * b
+                scratch[h, :, at : at + rows] = s
+                scratch[h, :, at + rows : at + 2 * rows] = t
+                top = jnp.maximum(top, jnp.maximum(lanes(jnp.maximum, s)[0], lanes(jnp.maximum, t)[0]))
+            top = jnp.max(top, axis=-1, keepdims=True)
+            if end is not None:
+                top = jnp.maximum(top, jnp.max(end, axis=-1, keepdims=True))
+            top = top * factor
+
+            weights = jnp.exp2(scratch[h, :, :crow] * factor - top)
+            old_ref[block, h] = weights.astype(BF16)
+            total, end = lanes(jnp.add, weights)
+            for b in range(block + 1):
+                at = crow + 2 * rows * b
+                weights = jnp.exp2(scratch[h, :, at : at + 2 * rows] * factor - top)
+                new_ref[block, h, b] = weights.astype(BF16)
+                total = total + lanes(jnp.add, weights)[0]
+            total = jnp.sum(total, axis=-1, keepdims=True)
+            if end is not None:
+                total = total + jnp.sum(end, axis=-1, keepdims=True)
+            sum_ref[block, h] = jnp.broadcast_to(total, (rows, HEAD))
+
+
+def weigh(place, q, k, k_sib, ck):
+    zs, rows, cols = q.shape
+    heads, crow = cols // HEAD, ck.shape[0]
+    return pl.pallas_call(
+        weigh_kernel,
+        in_specs=[SMEM] + [VMEM] * (2 + 2 * zs),
+        out_specs=[VMEM] * 3,
+        out_shape=[
+            jax.ShapeDtypeStruct((zs, heads, rows, crow), BF16),
+            jax.ShapeDtypeStruct((zs, heads, zs, rows, 2 * rows), BF16),
+            jax.ShapeDtypeStruct((zs, heads, rows, HEAD), F32),
+        ],
+        scratch_shapes=[pltpu.VMEM((zs, rows, cols), BF16)] * 2
+        + [pltpu.VMEM((heads, rows, -(-(crow + 2 * rows * zs) // LANES) * LANES), F32)],
+        compiler_params=pltpu.CompilerParams(vmem_limit_bytes=14 * MIB),
+        cost_estimate=BRIEF,
+        name="weigh",
+    )(place, q, ck, *k, *k_sib)
+
+
+def mix_kernel(shifts, place_ref, old_ref, new_ref, sum_ref, v_ref, vs_ref, cv_ref, *outs):
+    z = place_ref[1]
+    zs, rows, cols = v_ref.shape
+    heads = range(cols // HEAD)
+    hcols = [slice(h * HEAD, (h + 1) * HEAD) for h in heads]
     for shift, out_ref in zip(shifts, outs):
         block = lax.rem(z + shift, zs)
-        mine = lax.rem(zs - shift, zs)
-        queries = [q_ref[mine, :, hcol] for hcol in hcols]
-
-        def score(b, tops, diagonal):
+
+        def add(b, state):
             at = lax.rem(z + zs - b, zs)
             result = []
-            for h, top in zip(heads, tops):
-                s = lax.dot_general(queries[h], k_ref[at, :, hcols[h]], NT, preferred_element_type=F32)
-                t = lax.dot_general(queries[h], ks_ref[at, :, hcols[h]], NT, preferred_element_type=F32)
-                if diagonal:
-                    s, t = jnp.where(causal, s, low), jnp.where(core == 1, t, low)
-                new[h, b, :, :rows] = s
-                new[h, b, :, rows:] = t
-                folded = jnp.maximum(lanes(jnp.maximum, s)[0], lanes(jnp.maximum, t)[0])
-                result.append(jnp.maximum(top, folded))
+            for h, summed in zip(heads, state):
+                probs = new_ref[block, h, b]
+                value = jnp.concatenate([v_ref[at, :, hcols[h]], vs_ref[at, :, hcols[h]]], axis=0)
+                result.append(summed + jnp.dot(probs, value, preferred_element_type=F32))
             return tuple(result)
 
-        tops, ends = [], []
-        for h in heads:
-            s = lax.dot_general(queries[h], ck_ref[:, hcols[h]], NT, preferred_element_type=F32)
-            old[h] = s
-            folded, rest = lanes(jnp.maximum, s)
-            tops.append(folded)
-            ends.append(low if rest is None else jnp.max(rest, axis=-1, keepdims=True))
-        tops = lax.fori_loop(0, block, functools.partial(score, diagonal=False), tuple(tops))
-        tops = score(block, tops, True)
-        tops = [
-            jnp.maximum(jnp.max(top, axis=-1, keepdims=True), end) * factor
-            for top, end in zip(tops, ends)
-        ]
-
-        def weigh(b, state):
-            at = lax.rem(z + zs - b, zs)
-            result = []
-            for h, (total, summed) in zip(heads, state):
-                weights = jnp.exp2(new[h, b] * factor - tops[h])
-                probs = weights.astype(BF16)
-                summed += jnp.dot(probs[:, :rows], v_ref[at, :, hcols[h]], preferred_element_type=F32)
-                summed += jnp.dot(probs[:, rows:], vs_ref[at, :, hcols[h]], preferred_element_type=F32)
-                result.append((total + lanes(jnp.add, weights)[0], summed))
-            return tuple(result)
-
-        state, ends = [], []
-        for h in heads:
-            weights = jnp.exp2(old[h] * factor - tops[h])
-            folded, rest = lanes(jnp.add, weights)
-            ends.append(0.0 if rest is None else jnp.sum(rest, axis=-1, keepdims=True))
-            state.append(
-                (folded, jnp.dot(weights.astype(BF16), cv_ref[:, hcols[h]], preferred_element_type=F32))
-            )
-        state = lax.fori_loop(0, block + 1, weigh, tuple(state))
-        for h, (total, summed), end in zip(heads, state, ends):
-            total = jnp.sum(total, axis=-1, keepdims=True) + end
-            out_ref[:, hcols[h]] = (summed / total).astype(BF16)
-
-
-def attend(shifts, place, q, k, v, k_sib, v_sib, ck, cv):
-    zs, rows, cols = q.shape
-    heads = cols // HEAD
-    return pl.pallas_call(
-        functools.partial(attend_kernel, shifts),
-        in_specs=[SMEM] + [VMEM] * 7,
+        state = tuple(
+            jnp.dot(old_ref[block, h], cv_ref[:, hcols[h]], preferred_element_type=F32) for h in heads
+        )
+        state = lax.fori_loop(0, block + 1, add, state)
+        for h, summed in zip(heads, state):
+            out_ref[:, hcols[h]] = (summed / sum_ref[block, h]).astype(BF16)
+
+
+def mix(shifts, place, old, new, sums, v, v_sib, cv):
+    _, rows, cols = v.shape
+    return pl.pallas_call(
+        functools.partial(mix_kernel, shifts),
+        in_specs=[SMEM] + [VMEM] * 6,
         out_specs=[VMEM] * len(shifts),
         out_shape=[jax.ShapeDtypeStruct((rows, cols), BF16)] * len(shifts),
-        scratch_shapes=[
-            pltpu.VMEM((heads, rows, ck.shape[0]), F32),
-            pltpu.VMEM((heads, zs, rows, 2 * rows), F32),
-        ],
-        compiler_params=pltpu.CompilerParams(vmem_limit_bytes=20 * MIB),
+        compiler_params=pltpu.CompilerParams(vmem_limit_bytes=8 * MIB),
         cost_estimate=BRIEF,
-        name="attend",
-    )(place, q, k, v, k_sib, v_sib, ck, cv)
+        name="mix",
+    )(place, old, new, sums, v, v_sib, cv)
 
 
 def pack_kernel(places, crow, *refs):
@@ -277,7 +305,7 @@
         out_specs=[VMEM] * 2,
         out_shape=[jax.ShapeDtypeStruct(out, BF16)] * 2,
         scratch_shapes=[pltpu.VMEM(out, F32)],
-        compiler_params=pltpu.CompilerParams(vmem_limit_bytes=12 * MIB),
+        compiler_params=pltpu.CompilerParams(vmem_limit_bytes=8 * MIB),
         cost_estimate=BRIEF,
         name="pack",
     )(*parcels)
@@ -370,43 +398,54 @@
             acts.append(sent[-1])
         else:
             here[item] = sent[-1]
-    late = ["q2", "kc2", "v2"]
+    late = ["kc2", "v2"]
     there = {item: swap_core(here[item], zs) for item in here if item not in late}
 
-    pace = [[], ["kvc1"], ["kvc3"], ["q2"]]
+    pace = [[], ["kvc1"], ["kvc3"], []]
     swapped = [[], ["kvc0", "q0"], ["q1", "q3"], ["kvc1"]]
     gain4 = gain.reshape(4, 1, width)
     half = rows // 2
     normed, diag0, diag1 = None, None, None
+    every, early, last = tuple(range(zs)), (0, 1, 3), zs - 1
+
+    def sides(*items):
+        return [[side[item] for item in items] for side in (here, there)]
+
+    def project_early(slabs, into=()):
+        groups = [sides("q0", "q1", "q3"), sides("kvc0", "kvc1", "kvc3")]
+        parts = ((0, 0), (1, 0), (1, depth))
+        return project(place, normed, groups, parts, early, slabs, False, (), into)
+
+    def project_last(item, sums, *others, apart=False):
+        normed_then = after(normed, *others) if others else normed
+        return project(place, normed_then, [sides(item)], ((0, 0),), (2,), every, True, (sums,), apart=apart)
+
     for j, own in enumerate(acts):
         own = after(own, *([diag0, diag1] if j else [here["q1"], here["q3"]]))
         from_x, from_y = swap_chan(own, 1), swap_chan(own, 2)
         if j:
+            sums = project_early(every[:last]) if j == last else []
+            normed = after(normed, *sums) if j == last else normed
             settled = [normed] + [there[item] for item in swapped[j]] + [here[item] for item in pace[j]]
             from_x, from_y = after(from_x, *settled), after(from_y, *settled)
         diag0 = swap_chan(from_x[:half], 2)
         diag1 = swap_chan(from_y[half:], 1)
         normed = norm(place, j, zs, own, from_x, from_y, diag0, diag1, gain4, normed)
 
-    def sides(*items):
-        return [[side[item] for item in items] for side in (here, there)]
-
-    early = (0, 1, 3)
-    there["q2"] = swap_core(after(here["q2"], diag0, diag1), zs)
-    there["kc2"] = swap_core(after(here["kc2"], diag0, diag1), zs)
-    (q,) = project(place, normed, *sides("q0", "q1", "q3", "q2"), early + (2,), 1, True)
-    k_early, v_early = project(place, normed, *sides("kvc0", "kvc1", "kvc3"), early, 2, False)
+    there["kc2"] = swap_core(after(here["kc2"], there["q2"], diag0, diag1), zs)
+    q_sum, k_sum, v_sum = project_early(every[last:], sums)
+    (q,) = project_last("q2", q_sum)
     kept = sum(sides("kvc0", "kvc1", "kc2", "kvc3"), [])
     ck, cv = pack(kept, [depth if i % zs == 2 else 2 * depth for i in range(2 * zs)], crow)
-    (k,) = project(place, after(normed, q, ck), *sides("kc2"), (2,), 1, True, (k_early,))
-    k_sib = swap_core(k, zs)
-    there["v2"] = swap_core(after(here["v2"], k), zs)
-    (v,) = project(place, normed, *sides("v2"), (2,), 1, True, (v_early,))
+    k = project_last("kc2", k_sum, q, ck, apart=True)
+    weights = weigh(place, q, k, [swap_core(slab, zs) for slab in k], ck)
+    there["v2"] = swap_core(after(here["v2"], weights[2]), zs)
+    (v,) = project_last("v2", v_sum)
     v_sib = swap_core(v, zs)
     pieces, out = {}, None
     for shifts, wait in (((2,), ()), ((1, 3), ()), ((0,), (2,))):
-        ready = q if out is None else after(q, out[0], *[pieces[r] for r in wait])
-        out = attend(shifts, place, ready, k, v, k_sib, v_sib, ck, cv)
+        ready = v if out is None else after(v, out[0], *[pieces[r] for r in wait])
+        out = mix(shifts, place, *weights, ready, v_sib, cv)
         for r, piece in zip(shifts, out):
             pieces[r] = shift_z(piece, r, zs) if r else piece
     return join(place, [pieces[r] for r in range(zs)])

time: 170 us -> 189 us (1.11)
  starting transfers between devices: 36.2 us -> 53.8 us
  Pallas kernels: 40.1 us -> 46.8 us
  waiting for transfers between devices: 78.9 us -> 72.5 us
    ppermute x13, starting transfers between devices: 14.5 us -> 32.2 us  [shift_z(): return lax.ppermute(value, 'seq', pairs)]
    ppermute x13, waiting for transfers between devices: 61.9 us -> 49.1 us  [shift_z(): return lax.ppermute(value, 'seq', pairs)]
    pallas_call x7 -> x9, Pallas kernels: 23.7 us -> 30.3 us  [the longest x1 12.3 us: weigh(): pl.pallas_call(weigh_kernel, in_specs=[SMEM] + [VMEM] * (2 + 2 * zs), out...]
    ppermute x16, waiting for transfers between devices: 11.5 us -> 16 us  [swap_chan(): return lax.ppermute(value, 'chan', [(c, c ^ bit) for c in range(4)])]
    ppermute x11 -> x14, waiting for transfers between devices: 5.5 us -> 7.38 us  [swap_core(): lax.ppermute(value, 'seq', [(2 * a + k, 2 * a + 1 - k) for a in range(zs)...]
    unnamed x62 -> x58, local copies, waits for them, and re-layouts: 6.76 us -> 7.49 us
  transfers between devices with their start and end apart: 41 -> 44, of which waited for: 20 -> 22; matrix products, arithmetic and copies ran while one was open for 4% -> 3% of each run, Pallas kernels for 20% -> 22%
where the time goes in v5:
time: 189 us; the launch traced here: 188 us
  waiting for transfers between devices  72.5 us (38%)
  starting transfers between devices  53.8 us (28%)
  Pallas kernels  46.8 us (25%)
  local copies, waits for them, and re-layouts  12.3 us (7%)
  other arithmetic  2.46 us (1%)
    ppermute x13, waiting for transfers between devices, shift_z(): return lax.ppermute(value, 'seq', pairs)  49.1 us
    ppermute x13, starting transfers between devices, shift_z(): return lax.ppermute(value, 'seq', pairs)  32.2 us
    ppermute x16, starting transfers between devices, swap_chan(): return lax.ppermute(value, 'chan', [(c, c ^ bit) for c in range(4)])  16.4 us
    ppermute x16, waiting for transfers between devices, swap_chan(): return lax.ppermute(value, 'chan', [(c, c ^ bit) for c in range(4)])  16 us
    pallas_call x1, Pallas kernels, weigh(): pl.pallas_call(weigh_kernel, in_specs=[SMEM] + [VMEM] * (2 + 2 * zs), out...  12.3 us
    pallas_call x5, Pallas kernels, project(): pl.pallas_call(functools.partial(project_kernel, shifts, slabs, parts, zs...  11.2 us
    pallas_call x4, Pallas kernels, norm(): pl.pallas_call(functools.partial(norm_kernel, j), in_specs=[SMEM] + [VMEM...  8.44 us
    unnamed x58, local copies, waits for them, and re-layouts  7.49 us
  transfers between devices with their start and end apart: 44, of which 22 were waited for; matrix products, arithmetic and copies ran while one was open for 3% of the time, Pallas kernels for 22%

profile of v5, /device:TPU:0, one launch (start us, length us, event | category | flops | bytes accessed | tf_op | source)
XLA Modules:
  0.0 188.3 jit_solution(10844609681902158878)
XLA Ops:
  1.2 2.4 %collective-permute-start = (bf16[128,1024]{1,0:T(8,128)(2,1)S(1)}, bf16[128,1024]{1,0:T(8,128)(2,1)S(1)}, u32[]{:S(2)}, u32[]{:S(2)}) collective-permute-start(bf16[128,1024]{1,0:T(8,128)(2,1)S(1)} %fusion), channel_id=1, source_target_pairs={{0,4},{4,8},{8,12},{12,16},{16,20},{20,24},{24,28},{1,5},{5,9},{9,... | collective-permute-start | bytes 786440 | tf_op jit(solution)/shard_map/ppermute | solution.py:381
  3.7 1.8 dynamic-slice_bitcast_fusion.10
  5.5 2.6 %collective-permute-start.1 = (bf16[512,256]{1,0:T(8,128)(2,1)}, bf16[512,256]{1,0:T(8,128)(2,1)S(1)}, u32[]{:S(2)}, u32[]{:S(2)}) collective-permute-start(bf16[512,256]{1,0:T(8,128)(2,1)} %get-tuple-element.100), channel_id=1, source_target_pairs={{0,8},{4,12},{8,16},{12,20},{16,24},{20,28},{24,0},{28,4},{1,9},{5... | collective-permute-start | bytes 786440 | tf_op jit(solution)/shard_map/ppermute | solution.py:337
  8.0 2.0 %collective-permute-start.5 = (bf16[512,256]{1,0:T(8,128)(2,1)S(1)}, bf16[512,256]{1,0:T(8,128)(2,1)}, u32[]{:S(2)}, u32[]{:S(2)}) collective-permute-start(bf16[512,256]{1,0:T(8,128)(2,1)S(1)} %get-tuple-element.99), channel_id=1, source_target_pairs={{0,24},{4,28},{8,0},{12,4},{16,8},{20,12},{24,16},{28,20},{1,25},{... | collective-permute-start | bytes 786440 | tf_op jit(solution)/shard_map/ppermute | solution.py:337
  10.2 6.0 %hyena_filters.1.own_ref = bf16[256,1024]{1,0:T(8,128)(2,1)S(1)} custom-call(bf16[3,256,1024]{2,1,0:T(8,128)(2,1)S(1)} %bitcast.33, bf16[128,1024]{1,0:T(8,128)(2,1)S(1)} %pad_select_fusion.halo_ref, f32[64,128]{1,0:T(8,128)S(1)} %copy-done.14), custom_call_target="tpu_custom_call" | custom-call | flops 1 | bytes 1 | tf_op jit(solution)/shard_map/hyena_filters/pallas_call | solution.py:80
  17.4 5.3 %collective-permute-done.5.refs_2_ = bf16[512,256]{1,0:T(8,128)(2,1)} collective-permute-done((bf16[512,256]{1,0:T(8,128)(2,1)S(1)}, bf16[512,256]{1,0:T(8,128)(2,1)}, u32[]{:S(2)}, u32[]{:S(2)}) %collective-permute-start.5) | collective-permute-done | bytes 262176 | tf_op jit(solution)/shard_map/ppermute | solution.py:337
  22.6 1.5 collective-permute-start.6
  24.1 1.5 collective-permute-start.8
  27.5 1.2 dynamic-slice_bitcast_fusion
  28.8 7.7 %collective-permute-done.6.x_ref = bf16[256,1024]{1,0:T(8,128)(2,1)S(1)} collective-permute-done((bf16[256,1024]{1,0:T(8,128)(2,1)S(1)}, bf16[256,1024]{1,0:T(8,128)(2,1)S(1)}, u32[]{:S(2)}, u32[]{:S(2)}) %collective-permute-start.6) | collective-permute-done | bytes 524320 | tf_op jit(solution)/shard_map/ppermute | solution.py:345
  36.6 1.6 collective-permute-start.7
  38.2 1.6 collective-permute-start.9
  41.8 2.5 %collective-permute-done.7.d0_ref = bf16[128,1024]{1,0:T(8,128)(2,1)S(1)} collective-permute-done((bf16[128,1024]{1,0:T(8,128)(2,1)S(1)}, bf16[128,1024]{1,0:T(8,128)(2,1)S(1)}, u32[]{:S(2)}, u32[]{:S(2)}) %collective-permute-start.7) | collective-permute-done | bytes 262176 | tf_op jit(solution)/shard_map/ppermute | solution.py:345
  46.3 1.5 collective-permute-start.10
  48.7 1.7 collective-permute-done.12.refs_3_
  55.5 1.9 %norm.4.rest_0_ = bf16[4,4,256,1024]{3,2,1,0:T(8,128)(2,1)S(1)} custom-call(s32[3]{0:T(128)S(1)} %pad_add_fusion.place_ref, bf16[256,1024]{1,0:T(8,128)(2,1)S(1)} %hyena_filters.1.own_ref, bf16[256,1024]{1,0:T(8,128)(2,1)S(1)} %copy-done.2, bf16[256,1024]{1,0:T(8,128)(2,1)S(1)} %copy-done.4, bf16[128,1024]{1,0:T(8,128)(2,1)S(1)} %copy-done.10, ...), custom_call_target="tpu_custom_call" | custom-call | flops 1 | bytes 1 | tf_op jit(solution)/shard_map/norm/pallas_call | solution.py:119
  57.4 3.7 %collective-permute-done.13.refs_7_.refs_1_ = bf16[1344,256]{1,0:T(8,128)(2,1)S(1)} collective-permute-done((bf16[1344,256]{1,0:T(8,128)(2,1)}, bf16[1344,256]{1,0:T(8,128)(2,1)S(1)}, u32[]{:S(2)}, u32[]{:S(2)}) %collective-permute-start.13) | collective-permute-done | bytes 688160 | tf_op jit(solution)/shard_map/ppermute | solution.py:337
  64.0 3.3 %collective-permute-start.20 = (bf16[1344,256]{1,0:T(8,128)(2,1)S(1)}, bf16[1344,256]{1,0:T(8,128)(2,1)S(1)}, u32[]{:S(2)}, u32[]{:S(2)}) collective-permute-start(bf16[1344,256]{1,0:T(8,128)(2,1)S(1)} %pad_maximum_fusion.2), channel_id=1, source_target_pairs={{0,24},{4,28},{8,0},{12,4},{16,8},{20,12},{24,16},{28,20},{1,25},{... | collective-permute-start | bytes 2064392 | tf_op jit(solution)/shard_map/ppermute | solution.py:337
  67.3 5.2 %collective-permute-done.3.own_ref = bf16[256,1024]{1,0:T(8,128)(2,1)S(1)} collective-permute-done((bf16[256,1024]{1,0:T(8,128)(2,1)}, bf16[256,1024]{1,0:T(8,128)(2,1)S(1)}, u32[]{:S(2)}, u32[]{:S(2)}) %collective-permute-start.3) | collective-permute-done | bytes 524320 | tf_op jit(solution)/shard_map/ppermute | solution.py:337
  74.6 1.4 collective-permute-done.18.refs_4_
  76.0 11.4 %collective-permute-start.4 = (bf16[256,1024]{1,0:T(8,128)(2,1)S(1)}, bf16[256,1024]{1,0:T(8,128)(2,1)S(1)}, u32[]{:S(2)}, u32[]{:S(2)}) collective-permute-start(bf16[256,1024]{1,0:T(8,128)(2,1)S(1)} %collective-permute-done.3.own_ref), channel_id=1, source_target_pairs={{0,8},{4,12},{8,16},{12,20},{16,24},{20,28},{24,0},{28,4},{1,9},{5... | collective-permute-start | bytes 1572872 | tf_op jit(solution)/shard_map/ppermute | solution.py:337
  87.4 2.6 %norm.5.rest_0_ = bf16[4,4,256,1024]{3,2,1,0:T(8,128)(2,1)S(1)} custom-call(s32[3]{0:T(128)S(1)} %pad_add_fusion.place_ref, bf16[256,1024]{1,0:T(8,128)(2,1)} %collective-permute-done.2.own_ref, bf16[256,1024]{1,0:T(8,128)(2,1)S(1)} %collective-permute-done.10.x_ref, ...), custom_call_target="tpu_custom_call", output_to_operand_aliasing={{}: (7, {})} | custom-call | flops 1 | bytes 1 | tf_op jit(solution)/shard_map/norm/pallas_call | solution.py:119
  90.8 11.9 %collective-permute-done.4.own_ref = bf16[256,1024]{1,0:T(8,128)(2,1)S(1)} collective-permute-done((bf16[256,1024]{1,0:T(8,128)(2,1)S(1)}, bf16[256,1024]{1,0:T(8,128)(2,1)S(1)}, u32[]{:S(2)}, u32[]{:S(2)}) %collective-permute-start.4) | collective-permute-done | bytes 524320 | tf_op jit(solution)/shard_map/ppermute | solution.py:337
  103.5 1.5 collective-permute-start.27
  105.0 2.9 %collective-permute-start.30 = (bf16[512,256]{1,0:T(8,128)(2,1)S(1)}, bf16[512,256]{1,0:T(8,128)(2,1)S(1)}, u32[]{:S(2)}, u32[]{:S(2)}) collective-permute-start(bf16[512,256]{1,0:T(8,128)(2,1)S(1)} %copy-done.24), channel_id=1, source_target_pairs={{0,16},{4,20},{8,24},{12,28},{16,0},{20,4},{24,8},{28,12},{1,17},{... | collective-permute-start | bytes 786440 | tf_op jit(solution)/shard_map/ppermute | solution.py:337
  108.1 1.9 %norm.6.normed_ref.rest_0_ = bf16[4,4,256,1024]{3,2,1,0:T(8,128)(2,1)S(1)} custom-call(s32[3]{0:T(128)S(1)} %pad_add_fusion.place_ref, bf16[256,1024]{1,0:T(8,128)(2,1)S(1)} %collective-permute-done.3.own_ref, bf16[256,1024]{1,0:T(8,128)(2,1)S(1)} %collective-permute-done.17.x_ref, ...), custom_call_target="tpu_custom_call", output_to_operand_aliasing={{}: (7, {})} | custom-call | flops 1 | bytes 1 | tf_op jit(solution)/shard_map/norm/pallas_call | solution.py:119
  110.0 16.9 %collective-permute-done.30.refs_0_ = bf16[512,256]{1,0:T(8,128)(2,1)S(1)} collective-permute-done((bf16[512,256]{1,0:T(8,128)(2,1)S(1)}, bf16[512,256]{1,0:T(8,128)(2,1)S(1)}, u32[]{:S(2)}, u32[]{:S(2)}) %collective-permute-start.30) | collective-permute-done | bytes 262176 | tf_op jit(solution)/shard_map/ppermute | solution.py:337
  126.8 5.0 %project.5 = (f32[4,256,256]{2,1,0:T(8,128)S(1)}, f32[4,256,256]{2,1,0:T(8,128)S(1)}, f32[4,256,256]{2,1,0:T(8,128)S(1)}) custom-call(s32[3]{0:T(128)S(1)} %pad_add_fusion.place_ref, bf16[4,4,256,1024]{3,2,1,0:T(8,128)(2,1)S(1)} %norm.6.normed_ref.rest_0_, bf16[512,256]{1,0:T(8,128)(2,1)S(1)} %get-tuple-element.96.refs_0_, bf16[512,256]{1,0:T(8,128)(2,1)S(1)} %copy-done.6, ...), custom_call_target="tpu_custom_call" | custom-call | flops 1 | bytes 1 | tf_op jit(solution)/shard_map/project/pallas_call | solution.py:161
  132.5 1.3 collective-permute-start.29
  133.8 2.1 %collective-permute-done.32.refs_2_.refs_0_ = bf16[832,256]{1,0:T(8,128)(2,1)S(1)} collective-permute-done((bf16[832,256]{1,0:T(8,128)(2,1)S(1)}, bf16[832,256]{1,0:T(8,128)(2,1)S(1)}, u32[]{:S(2)}, u32[]{:S(2)}) %collective-permute-start.32) | collective-permute-done | bytes 426016 | tf_op jit(solution)/shard_map/ppermute | solution.py:337
  135.9 4.8 %collective-permute-done.28.d0_ref = bf16[128,1024]{1,0:T(8,128)(2,1)S(1)} collective-permute-done((bf16[128,1024]{1,0:T(8,128)(2,1)S(1)}, bf16[128,1024]{1,0:T(8,128)(2,1)S(1)}, u32[]{:S(2)}, u32[]{:S(2)}) %collective-permute-start.28) | collective-permute-done | bytes 262176 | tf_op jit(solution)/shard_map/ppermute | solution.py:345
  141.0 2.1 %norm.7.normed_ref = bf16[4,4,256,1024]{3,2,1,0:T(8,128)(2,1)S(1)} custom-call(s32[3]{0:T(128)S(1)} %pad_add_fusion.place_ref, bf16[256,1024]{1,0:T(8,128)(2,1)S(1)} %collective-permute-done.4.own_ref, bf16[256,1024]{1,0:T(8,128)(2,1)S(1)} %collective-permute-done.24.x_ref, ...), custom_call_target="tpu_custom_call", output_to_operand_aliasing={{}: (7, {})} | custom-call | flops 1 | bytes 1 | tf_op jit(solution)/shard_map/norm/pallas_call | solution.py:119
  143.1 2.5 %project.6 = (f32[4,256,256]{2,1,0:T(8,128)S(1)}, f32[4,256,256]{2,1,0:T(8,128)S(1)}, f32[4,256,256]{2,1,0:T(8,128)S(1)}) custom-call(s32[3]{0:T(128)S(1)} %pad_add_fusion.place_ref, bf16[4,4,256,1024]{3,2,1,0:T(8,128)(2,1)S(1)} %norm.7.normed_ref, ...), custom_call_target="tpu_custom_call", output_to_operand_aliasing={{0}: (14, {}), {1}: (15, {}), {2}: (16, {})} | custom-call | flops 1 | bytes 1 | tf_op jit(solution)/shard_map/project/pallas_call | solution.py:161
  145.5 1.3 project.7.q_ref
  146.9 1.3 project.8
  150.6 12.3 %weigh.1 = (bf16[4,2,256,1216]{3,2,1,0:T(8,128)(2,1)S(1)}, bf16[4,2,4,256,512]{4,3,2,1,0:T(8,128)(2,1)S(1)}, f32[4,2,256,128]{3,2,1,0:T(8,128)S(1)}) custom-call(s32[3]{0:T(128)S(1)} %pad_add_fusion.place_ref, bf16[4,256,256]{2,1,0:T(8,128)(2,1)S(1)} %project.7.q_ref, bf16[1216,256]{1,0:T(8,128)(2,1)S(1)} %get-tuple-element.71.ck_ref, ...), custom_call_target="tpu_custom_call" | custom-call | flops 1 | bytes 1 | tf_op jit(solution)/shard_map/weigh/pallas_call | solution.py:236
  163.2 1.4 collective-permute-done.39.refs_1_
  164.6 1.3 project.9.v_ref
  166.1 1.7 collective-permute-done.40.vs_ref
  167.8 2.0 %mix.3 = bf16[256,256]{1,0:T(8,128)(2,1)S(1)} custom-call(s32[3]{0:T(128)S(1)} %pad_add_fusion.place_ref, bf16[4,2,256,1216]{3,2,1,0:T(8,128)(2,1)S(1)} %get-tuple-element.78.old_ref, bf16[4,2,4,256,512]{4,3,2,1,0:T(8,128)(2,1)S(1)} %get-tuple-element.79.new_ref, f32[4,2,256,128]{3,2,1,0:T(8,128)S(1)} %get-tuple-element.80.sum_ref, ...), custom_call_target="tpu_custom_call" | custom-call | flops 1 | bytes 1 | tf_op jit(solution)/shard_map/mix/pallas_call | solution.py:280
  169.8 2.1 %collective-permute-start.41 = (bf16[256,256]{1,0:T(8,128)(2,1)S(1)}, bf16[256,256]{1,0:T(8,128)(2,1)S(1)}, u32[]{:S(2)}, u32[]{:S(2)}) collective-permute-start(bf16[256,256]{1,0:T(8,128)(2,1)S(1)} %mix.3), channel_id=1, source_target_pairs={{0,16},{4,20},{8,24},{12,28},{16,0},{20,4},{24,8},{28,12},{1,17},{... | collective-permute-start | bytes 393224 | tf_op jit(solution)/shard_map/ppermute | solution.py:337
  171.9 3.4 %mix.4 = (bf16[256,256]{1,0:T(8,128)(2,1)S(1)}, bf16[256,256]{1,0:T(8,128)(2,1)S(1)}) custom-call(s32[3]{0:T(128)S(1)} %pad_add_fusion.place_ref, bf16[4,2,256,1216]{3,2,1,0:T(8,128)(2,1)S(1)} %get-tuple-element.78.old_ref, bf16[4,2,4,256,512]{4,3,2,1,0:T(8,128)(2,1)S(1)} %get-tuple-element.79.new_ref, f32[4,2,256,128]{3,2,1,0:T(8,128)S(1)} %get-tuple-element.80.sum_ref, ...), custom_call_target="tpu_custom_call" | custom-call | flops 1 | bytes 1 | tf_op jit(solution)/shard_map/mix/pallas_call | solution.py:280
  175.3 2.2 %collective-permute-start.42 = (bf16[256,256]{1,0:T(8,128)(2,1)S(1)}, bf16[256,256]{1,0:T(8,128)(2,1)S(1)}, u32[]{:S(2)}, u32[]{:S(2)}) collective-permute-start(bf16[256,256]{1,0:T(8,128)(2,1)S(1)} %get-tuple-element.86), channel_id=1, source_target_pairs={{0,8},{4,12},{8,16},{12,20},{16,24},{20,28},{24,0},{28,4},{1,9},{5... | collective-permute-start | bytes 393224 | tf_op jit(solution)/shard_map/ppermute | solution.py:337
  177.5 2.4 %collective-permute-start.43 = (bf16[256,256]{1,0:T(8,128)(2,1)S(1)}, bf16[256,256]{1,0:T(8,128)(2,1)S(1)}, u32[]{:S(2)}, u32[]{:S(2)}) collective-permute-start(bf16[256,256]{1,0:T(8,128)(2,1)S(1)} %get-tuple-element.88), channel_id=1, source_target_pairs={{0,24},{4,28},{8,0},{12,4},{16,8},{20,12},{24,16},{28,20},{1,25},{... | collective-permute-start | bytes 393224 | tf_op jit(solution)/shard_map/ppermute | solution.py:337
  179.9 1.4 mix.5.refs_0_
  182.0 2.2 %collective-permute-done.42.refs_1_ = bf16[256,256]{1,0:T(8,128)(2,1)S(1)} collective-permute-done((bf16[256,256]{1,0:T(8,128)(2,1)S(1)}, bf16[256,256]{1,0:T(8,128)(2,1)S(1)}, u32[]{:S(2)}, u32[]{:S(2)}) %collective-permute-start.42) | collective-permute-done | bytes 131104 | tf_op jit(solution)/shard_map/ppermute | solution.py:337
  184.2 1.5 collective-permute-done.43.refs_3_
  186.4 2.0 %join.1 = bf16[256,1024]{1,0:T(8,128)(2,1)} custom-call(s32[3]{0:T(128)} %copy-done.13, bf16[256,256]{1,0:T(8,128)(2,1)} %copy-done.7, bf16[256,256]{1,0:T(8,128)(2,1)} %copy-done.27, bf16[256,256]{1,0:T(8,128)(2,1)} %copy-done.26, bf16[256,256]{1,0:T(8,128)(2,1)} %copy-done.28), custom_call_target="tpu_custom_call" | custom-call | tf_op jit(solution)/shard_map/join/pallas_call | solution.py:326
  (132 shorter events, 26.5 us)
Async XLA Ops:
  1.2 8.8 %collective-permute-start = (bf16[128,1024]{1,0:T(8,128)(2,1)S(1)}, bf16[128,1024]{1,0:T(8,128)(2,1)S(1)}, u32[]{:S(2)}, u32[]{:S(2)}) collective-permute-start(bf16[128,1024]{1,0:T(8,128)(2,1)S(1)} %fusion), channel_id=1, source_target_pairs={{0,4},{4,8},{8,12},{12,16},{16,20},{20,24},{24,28},{1,5},{5,9},{9,... | collective-permute-start | bytes 786440 | tf_op jit(solution)/shard_map/ppermute | solution.py:381
  5.5 11.2 %collective-permute-start.1 = (bf16[512,256]{1,0:T(8,128)(2,1)}, bf16[512,256]{1,0:T(8,128)(2,1)S(1)}, u32[]{:S(2)}, u32[]{:S(2)}) collective-permute-start(bf16[512,256]{1,0:T(8,128)(2,1)} %get-tuple-element.100), channel_id=1, source_target_pairs={{0,8},{4,12},{8,16},{12,20},{16,24},{20,28},{24,0},{28,4},{1,9},{5... | collective-permute-start | bytes 786440 | tf_op jit(solution)/shard_map/ppermute | solution.py:337
  8.0 14.6 %collective-permute-start.5 = (bf16[512,256]{1,0:T(8,128)(2,1)S(1)}, bf16[512,256]{1,0:T(8,128)(2,1)}, u32[]{:S(2)}, u32[]{:S(2)}) collective-permute-start(bf16[512,256]{1,0:T(8,128)(2,1)S(1)} %get-tuple-element.99), channel_id=1, source_target_pairs={{0,24},{4,28},{8,0},{12,4},{16,8},{20,12},{24,16},{28,20},{1,25},{... | collective-permute-start | bytes 786440 | tf_op jit(solution)/shard_map/ppermute | solution.py:337
  22.6 14.0 %collective-permute-start.6 = (bf16[256,1024]{1,0:T(8,128)(2,1)S(1)}, bf16[256,1024]{1,0:T(8,128)(2,1)S(1)}, u32[]{:S(2)}, u32[]{:S(2)}) collective-permute-start(bf16[256,1024]{1,0:T(8,128)(2,1)S(1)} %hyena_filters.1.own_ref), channel_id=1, source_target_pairs={{0,1},{1,0},{2,3},{3,2},{4,5},{5,4},{6,7},{7,6},{8,9},{9,8},{10,11... | collective-permute-start | bytes 1572872 | tf_op jit(solution)/shard_map/ppermute | solution.py:345
  24.1 14.1 %collective-permute-start.8 = (bf16[256,1024]{1,0:T(8,128)(2,1)S(1)}, bf16[256,1024]{1,0:T(8,128)(2,1)S(1)}, u32[]{:S(2)}, u32[]{:S(2)}) collective-permute-start(bf16[256,1024]{1,0:T(8,128)(2,1)S(1)} %hyena_filters.1.own_ref), channel_id=1, source_target_pairs={{0,2},{1,3},{2,0},{3,1},{4,6},{5,7},{6,4},{7,5},{8,10},{9,11},{10,... | collective-permute-start | bytes 1572872 | tf_op jit(solution)/shard_map/ppermute | solution.py:345
  26.4 15.4 %collective-permute-start.2 = (bf16[256,1024]{1,0:T(8,128)(2,1)S(1)}, bf16[256,1024]{1,0:T(8,128)(2,1)}, u32[]{:S(2)}, u32[]{:S(2)}) collective-permute-start(bf16[256,1024]{1,0:T(8,128)(2,1)S(1)} %hyena_filters.1.own_ref), channel_id=1, source_target_pairs={{0,8},{4,12},{8,16},{12,20},{16,24},{20,28},{24,0},{28,4},{1,9},{5... | collective-permute-start | bytes 1572872 | tf_op jit(solution)/shard_map/ppermute | solution.py:337
  28.8 28.7 %collective-permute-start.11 = (bf16[1344,256]{1,0:T(8,128)(2,1)S(1)}, bf16[1344,256]{1,0:T(8,128)(2,1)S(1)}, u32[]{:S(2)}, u32[]{:S(2)}) collective-permute-start(bf16[1344,256]{1,0:T(8,128)(2,1)S(1)} %pad_maximum_fusion.refs_6_.refs_0_), channel_id=1, source_target_pairs={{0,4},{4,0},{8,12},{12,8},{16,20},{20,16},{24,28},{28,24},{1,5},{5... | collective-permute-start | bytes 2064392 | tf_op jit(solution)/shard_map/ppermute | solution.py:341
  36.6 7.7 %collective-permute-start.7 = (bf16[128,1024]{1,0:T(8,128)(2,1)S(1)}, bf16[128,1024]{1,0:T(8,128)(2,1)S(1)}, u32[]{:S(2)}, u32[]{:S(2)}) collective-permute-start(bf16[128,1024]{1,0:T(8,128)(2,1)S(1)} %slice.42), channel_id=1, source_target_pairs={{0,2},{1,3},{2,0},{3,1},{4,6},{5,7},{6,4},{7,5},{8,10},{9,11},{10,... | collective-permute-start | bytes 786440 | tf_op jit(solution)/shard_map/ppermute | solution.py:345
  38.2 7.4 %collective-permute-start.9 = (bf16[128,1024]{1,0:T(8,128)(2,1)S(1)}, bf16[128,1024]{1,0:T(8,128)(2,1)S(1)}, u32[]{:S(2)}, u32[]{:S(2)}) collective-permute-start(bf16[128,1024]{1,0:T(8,128)(2,1)S(1)} %slice.43), channel_id=1, source_target_pairs={{0,1},{1,0},{2,3},{3,2},{4,5},{5,4},{6,7},{7,6},{8,9},{9,8},{10,11... | collective-permute-start | bytes 786440 | tf_op jit(solution)/shard_map/ppermute | solution.py:345
  40.7 20.4 %collective-permute-start.13 = (bf16[1344,256]{1,0:T(8,128)(2,1)}, bf16[1344,256]{1,0:T(8,128)(2,1)S(1)}, u32[]{:S(2)}, u32[]{:S(2)}) collective-permute-start(bf16[1344,256]{1,0:T(8,128)(2,1)} %pad_maximum_fusion.1), channel_id=1, source_target_pairs={{0,8},{4,12},{8,16},{12,20},{16,24},{20,28},{24,0},{28,4},{1,9},{5... | collective-permute-start | bytes 2064392 | tf_op jit(solution)/shard_map/ppermute | solution.py:337
  46.3 14.8 %collective-permute-start.10 = (bf16[256,1024]{1,0:T(8,128)(2,1)}, bf16[256,1024]{1,0:T(8,128)(2,1)S(1)}, u32[]{:S(2)}, u32[]{:S(2)}) collective-permute-start(bf16[256,1024]{1,0:T(8,128)(2,1)} %collective-permute-done.2.own_ref), channel_id=1, source_target_pairs={{0,1},{1,0},{2,3},{3,2},{4,5},{5,4},{6,7},{7,6},{8,9},{9,8},{10,11... | collective-permute-start | bytes 1572872 | tf_op jit(solution)/shard_map/ppermute | solution.py:345
  47.8 13.9 %collective-permute-start.15 = (bf16[256,1024]{1,0:T(8,128)(2,1)}, bf16[256,1024]{1,0:T(8,128)(2,1)}, u32[]{:S(2)}, u32[]{:S(2)}) collective-permute-start(bf16[256,1024]{1,0:T(8,128)(2,1)} %collective-permute-done.2.own_ref), channel_id=1, source_target_pairs={{0,2},{1,3},{2,0},{3,1},{4,6},{5,7},{6,4},{7,5},{8,10},{9,11},{10,... | collective-permute-start | bytes 1572872 | tf_op jit(solution)/shard_map/ppermute | solution.py:345
  48.7 1.7 collective-permute-start.12
  50.4 22.0 %collective-permute-start.3 = (bf16[256,1024]{1,0:T(8,128)(2,1)}, bf16[256,1024]{1,0:T(8,128)(2,1)S(1)}, u32[]{:S(2)}, u32[]{:S(2)}) collective-permute-start(bf16[256,1024]{1,0:T(8,128)(2,1)} %collective-permute-done.2.own_ref), channel_id=1, source_target_pairs={{0,8},{4,12},{8,16},{12,20},{16,24},{20,28},{24,0},{28,4},{1,9},{5... | collective-permute-start | bytes 1572872 | tf_op jit(solution)/shard_map/ppermute | solution.py:337
  51.5 128.4 %copy-start.13 = (s32[3]{0:T(128)}, s32[3]{0:T(128)S(1)}, u32[]{:S(2)}) copy-start(s32[3]{0:T(128)S(1)} %pad_add_fusion.place_ref) | copy-start | bytes 40
  61.1 11.3 %collective-permute-start.14 = (bf16[128,1024]{1,0:T(8,128)(2,1)S(1)}, bf16[128,1024]{1,0:T(8,128)(2,1)S(1)}, u32[]{:S(2)}, u32[]{:S(2)}) collective-permute-start(bf16[128,1024]{1,0:T(8,128)(2,1)S(1)} %slice.34), channel_id=1, source_target_pairs={{0,2},{1,3},{2,0},{3,1},{4,6},{5,7},{6,4},{7,5},{8,10},{9,11},{10,... | collective-permute-start | bytes 786440 | tf_op jit(solution)/shard_map/ppermute | solution.py:345
  62.7 9.8 %collective-permute-start.16 = (bf16[128,1024]{1,0:T(8,128)(2,1)S(1)}, bf16[128,1024]{1,0:T(8,128)(2,1)S(1)}, u32[]{:S(2)}, u32[]{:S(2)}) collective-permute-start(bf16[128,1024]{1,0:T(8,128)(2,1)S(1)} %slice.35), channel_id=1, source_target_pairs={{0,1},{1,0},{2,3},{3,2},{4,5},{5,4},{6,7},{7,6},{8,9},{9,8},{10,11... | collective-permute-start | bytes 786440 | tf_op jit(solution)/shard_map/ppermute | solution.py:345
  64.0 41.1 %copy-start.24 = (bf16[512,256]{1,0:T(8,128)(2,1)S(1)}, bf16[512,256]{1,0:T(8,128)(2,1)}, u32[]{:S(2)}) copy-start(bf16[512,256]{1,0:T(8,128)(2,1)} %get-tuple-element.67) | copy-start | bytes 786436
  64.0 44.0 %copy-start.16 = (bf16[512,256]{1,0:T(8,128)(2,1)S(1)}, bf16[512,256]{1,0:T(8,128)(2,1)}, u32[]{:S(2)}) copy-start(bf16[512,256]{1,0:T(8,128)(2,1)} %get-tuple-element.90) | copy-start | bytes 786436
  64.0 26.0 %collective-permute-start.20 = (bf16[1344,256]{1,0:T(8,128)(2,1)S(1)}, bf16[1344,256]{1,0:T(8,128)(2,1)S(1)}, u32[]{:S(2)}, u32[]{:S(2)}) collective-permute-start(bf16[1344,256]{1,0:T(8,128)(2,1)S(1)} %pad_maximum_fusion.2), channel_id=1, source_target_pairs={{0,24},{4,28},{8,0},{12,4},{16,8},{20,12},{24,16},{28,20},{1,25},{... | collective-permute-start | bytes 2064392 | tf_op jit(solution)/shard_map/ppermute | solution.py:337
  72.4 17.6 %collective-permute-start.17 = (bf16[256,1024]{1,0:T(8,128)(2,1)S(1)}, bf16[256,1024]{1,0:T(8,128)(2,1)S(1)}, u32[]{:S(2)}, u32[]{:S(2)}) collective-permute-start(bf16[256,1024]{1,0:T(8,128)(2,1)S(1)} %collective-permute-done.3.own_ref), channel_id=1, source_target_pairs={{0,1},{1,0},{2,3},{3,2},{4,5},{5,4},{6,7},{7,6},{8,9},{9,8},{10,11... | collective-permute-start | bytes 1572872 | tf_op jit(solution)/shard_map/ppermute | solution.py:345
  73.0 17.1 %collective-permute-start.22 = (bf16[256,1024]{1,0:T(8,128)(2,1)S(1)}, bf16[256,1024]{1,0:T(8,128)(2,1)S(1)}, u32[]{:S(2)}, u32[]{:S(2)}) collective-permute-start(bf16[256,1024]{1,0:T(8,128)(2,1)S(1)} %collective-permute-done.3.own_ref), channel_id=1, source_target_pairs={{0,2},{1,3},{2,0},{3,1},{4,6},{5,7},{6,4},{7,5},{8,10},{9,11},{10,... | collective-permute-start | bytes 1572872 | tf_op jit(solution)/shard_map/ppermute | solution.py:345
  74.1 1.9 collective-permute-start.18
  74.1 13.3 %collective-permute-start.19 = (bf16[512,256]{1,0:T(8,128)(2,1)}, bf16[512,256]{1,0:T(8,128)(2,1)S(1)}, u32[]{:S(2)}, u32[]{:S(2)}) collective-permute-start(bf16[512,256]{1,0:T(8,128)(2,1)} %collective-permute-done.5.refs_2_), channel_id=1, source_target_pairs={{0,4},{4,0},{8,12},{12,8},{16,20},{20,16},{24,28},{28,24},{1,5},{5... | collective-permute-start | bytes 786440 | tf_op jit(solution)/shard_map/ppermute | solution.py:341
  76.0 26.7 %collective-permute-start.4 = (bf16[256,1024]{1,0:T(8,128)(2,1)S(1)}, bf16[256,1024]{1,0:T(8,128)(2,1)S(1)}, u32[]{:S(2)}, u32[]{:S(2)}) collective-permute-start(bf16[256,1024]{1,0:T(8,128)(2,1)S(1)} %collective-permute-done.3.own_ref), channel_id=1, source_target_pairs={{0,8},{4,12},{8,16},{12,20},{16,24},{20,28},{24,0},{28,4},{1,9},{5... | collective-permute-start | bytes 1572872 | tf_op jit(solution)/shard_map/ppermute | solution.py:337
  87.4 20.6 %collective-permute-start.25 = (bf16[1344,256]{1,0:T(8,128)(2,1)S(1)}, bf16[1344,256]{1,0:T(8,128)(2,1)S(1)}, u32[]{:S(2)}, u32[]{:S(2)}) collective-permute-start(bf16[1344,256]{1,0:T(8,128)(2,1)S(1)} %collective-permute-done.13.refs_7_.refs_1_), channel_id=1, source_target_pairs={{0,4},{4,0},{8,12},{12,8},{16,20},{20,16},{24,28},{28,24},{1,5},{5... | collective-permute-start | bytes 2064392 | tf_op jit(solution)/shard_map/ppermute | solution.py:341
  90.0 12.7 %collective-permute-start.21 = (bf16[128,1024]{1,0:T(8,128)(2,1)S(1)}, bf16[128,1024]{1,0:T(8,128)(2,1)S(1)}, u32[]{:S(2)}, u32[]{:S(2)}) collective-permute-start(bf16[128,1024]{1,0:T(8,128)(2,1)S(1)} %slice.36), channel_id=1, source_target_pairs={{0,2},{1,3},{2,0},{3,1},{4,6},{5,7},{6,4},{7,5},{8,10},{9,11},{10,... | collective-permute-start | bytes 786440 | tf_op jit(solution)/shard_map/ppermute | solution.py:345
  90.2 12.6 %collective-permute-start.23 = (bf16[128,1024]{1,0:T(8,128)(2,1)S(1)}, bf16[128,1024]{1,0:T(8,128)(2,1)S(1)}, u32[]{:S(2)}, u32[]{:S(2)}) collective-permute-start(bf16[128,1024]{1,0:T(8,128)(2,1)S(1)} %slice.37), channel_id=1, source_target_pairs={{0,1},{1,0},{2,3},{3,2},{4,5},{5,4},{6,7},{7,6},{8,9},{9,8},{10,11... | collective-permute-start | bytes 786440 | tf_op jit(solution)/shard_map/ppermute | solution.py:345
  90.3 36.6 %collective-permute-start.26 = (bf16[1344,256]{1,0:T(8,128)(2,1)S(1)}, bf16[1344,256]{1,0:T(8,128)(2,1)S(1)}, u32[]{:S(2)}, u32[]{:S(2)}) collective-permute-start(bf16[1344,256]{1,0:T(8,128)(2,1)S(1)} %collective-permute-done.20.refs_8_.refs_3_), channel_id=1, source_target_pairs={{0,4},{4,0},{8,12},{12,8},{16,20},{20,16},{24,28},{28,24},{1,5},{5... | collective-permute-start | bytes 2064392 | tf_op jit(solution)/shard_map/ppermute | solution.py:341
  102.7 29.1 %collective-permute-start.24 = (bf16[256,1024]{1,0:T(8,128)(2,1)S(1)}, bf16[256,1024]{1,0:T(8,128)(2,1)S(1)}, u32[]{:S(2)}, u32[]{:S(2)}) collective-permute-start(bf16[256,1024]{1,0:T(8,128)(2,1)S(1)} %collective-permute-done.4.own_ref), channel_id=1, source_target_pairs={{0,1},{1,0},{2,3},{3,2},{4,5},{5,4},{6,7},{7,6},{8,9},{9,8},{10,11... | collective-permute-start | bytes 1572872 | tf_op jit(solution)/shard_map/ppermute | solution.py:345
  103.5 28.3 %collective-permute-start.27 = (bf16[256,1024]{1,0:T(8,128)(2,1)S(1)}, bf16[256,1024]{1,0:T(8,128)(2,1)S(1)}, u32[]{:S(2)}, u32[]{:S(2)}) collective-permute-start(bf16[256,1024]{1,0:T(8,128)(2,1)S(1)} %collective-permute-done.4.own_ref), channel_id=1, source_target_pairs={{0,2},{1,3},{2,0},{3,1},{4,6},{5,7},{6,4},{7,5},{8,10},{9,11},{10,... | collective-permute-start | bytes 1572872 | tf_op jit(solution)/shard_map/ppermute | solution.py:345
  105.0 21.8 %collective-permute-start.30 = (bf16[512,256]{1,0:T(8,128)(2,1)S(1)}, bf16[512,256]{1,0:T(8,128)(2,1)S(1)}, u32[]{:S(2)}, u32[]{:S(2)}) collective-permute-start(bf16[512,256]{1,0:T(8,128)(2,1)S(1)} %copy-done.24), channel_id=1, source_target_pairs={{0,16},{4,20},{8,24},{12,28},{16,0},{20,4},{24,8},{28,12},{1,17},{... | collective-permute-start | bytes 786440 | tf_op jit(solution)/shard_map/ppermute | solution.py:337
  108.0 27.9 %collective-permute-start.32 = (bf16[832,256]{1,0:T(8,128)(2,1)S(1)}, bf16[832,256]{1,0:T(8,128)(2,1)S(1)}, u32[]{:S(2)}, u32[]{:S(2)}) collective-permute-start(bf16[832,256]{1,0:T(8,128)(2,1)S(1)} %pad_maximum_fusion.3), channel_id=1, source_target_pairs={{0,16},{4,20},{8,24},{12,28},{16,0},{20,4},{24,8},{28,12},{1,17},{... | collective-permute-start | bytes 1277960 | tf_op jit(solution)/shard_map/ppermute | solution.py:337
  110.0 31.0 %copy-start.23 = (bf16[512,256]{1,0:T(8,128)(2,1)S(1)}, bf16[512,256]{1,0:T(8,128)(2,1)}, u32[]{:S(2)}) copy-start(bf16[512,256]{1,0:T(8,128)(2,1)} %get-tuple-element.81) | copy-start | bytes 786436
  126.8 6.9 %collective-permute-start.31 = (bf16[512,256]{1,0:T(8,128)(2,1)S(1)}, bf16[512,256]{1,0:T(8,128)(2,1)S(1)}, u32[]{:S(2)}, u32[]{:S(2)}) collective-permute-start(bf16[512,256]{1,0:T(8,128)(2,1)S(1)} %collective-permute-done.30.refs_0_), channel_id=1, source_target_pairs={{0,4},{4,0},{8,12},{12,8},{16,20},{20,16},{24,28},{28,24},{1,5},{5... | collective-permute-start | bytes 786440 | tf_op jit(solution)/shard_map/ppermute | solution.py:341
  131.9 8.8 %collective-permute-start.28 = (bf16[128,1024]{1,0:T(8,128)(2,1)S(1)}, bf16[128,1024]{1,0:T(8,128)(2,1)S(1)}, u32[]{:S(2)}, u32[]{:S(2)}) collective-permute-start(bf16[128,1024]{1,0:T(8,128)(2,1)S(1)} %slice.38), channel_id=1, source_target_pairs={{0,2},{1,3},{2,0},{3,1},{4,6},{5,7},{6,4},{7,5},{8,10},{9,11},{10,... | collective-permute-start | bytes 786440 | tf_op jit(solution)/shard_map/ppermute | solution.py:345
  132.5 8.5 %collective-permute-start.29 = (bf16[128,1024]{1,0:T(8,128)(2,1)S(1)}, bf16[128,1024]{1,0:T(8,128)(2,1)S(1)}, u32[]{:S(2)}, u32[]{:S(2)}) collective-permute-start(bf16[128,1024]{1,0:T(8,128)(2,1)S(1)} %slice.39), channel_id=1, source_target_pairs={{0,1},{1,0},{2,3},{3,2},{4,5},{5,4},{6,7},{7,6},{8,9},{9,8},{10,11... | collective-permute-start | bytes 786440 | tf_op jit(solution)/shard_map/ppermute | solution.py:345
  141.0 5.8 %collective-permute-start.33 = (bf16[832,256]{1,0:T(8,128)(2,1)S(1)}, bf16[832,256]{1,0:T(8,128)(2,1)S(1)}, u32[]{:S(2)}, u32[]{:S(2)}) collective-permute-start(bf16[832,256]{1,0:T(8,128)(2,1)S(1)} %collective-permute-done.32.refs_2_.refs_0_), channel_id=1, source_target_pairs={{0,4},{4,0},{8,12},{12,8},{16,20},{20,16},{24,28},{28,24},{1,5},{5... | collective-permute-start | bytes 1277960 | tf_op jit(solution)/shard_map/ppermute | solution.py:341
  141.0 22.0 %collective-permute-start.38 = (bf16[512,256]{1,0:T(8,128)(2,1)S(1)}, bf16[512,256]{1,0:T(8,128)(2,1)S(1)}, u32[]{:S(2)}, u32[]{:S(2)}) collective-permute-start(bf16[512,256]{1,0:T(8,128)(2,1)S(1)} %copy-done.23), channel_id=1, source_target_pairs={{0,16},{4,20},{8,24},{12,28},{16,0},{20,4},{24,8},{28,12},{1,17},{... | collective-permute-start | bytes 786440 | tf_op jit(solution)/shard_map/ppermute | solution.py:337
  148.2 1.6 collective-permute-start.34
  148.8 1.3 collective-permute-start.35
  148.8 1.5 collective-permute-start.36
  149.3 1.3 collective-permute-start.37
  163.0 1.6 collective-permute-start.39
  165.8 2.0 %collective-permute-start.40 = (bf16[4,256,256]{2,1,0:T(8,128)(2,1)S(1)}, bf16[4,256,256]{2,1,0:T(8,128)(2,1)S(1)}, u32[]{:S(2)}, u32[]{:S(2)}) collective-permute-start(bf16[4,256,256]{2,1,0:T(8,128)(2,1)S(1)} %project.9.v_ref), channel_id=1, source_target_pairs={{0,4},{4,0},{8,12},{12,8},{16,20},{20,16},{24,28},{28,24},{1,5},{5... | collective-permute-start | bytes 1572872 | tf_op jit(solution)/shard_map/ppermute | solution.py:341
  169.8 10.1 %collective-permute-start.41 = (bf16[256,256]{1,0:T(8,128)(2,1)S(1)}, bf16[256,256]{1,0:T(8,128)(2,1)S(1)}, u32[]{:S(2)}, u32[]{:S(2)}) collective-permute-start(bf16[256,256]{1,0:T(8,128)(2,1)S(1)} %mix.3), channel_id=1, source_target_pairs={{0,16},{4,20},{8,24},{12,28},{16,0},{20,4},{24,8},{28,12},{1,17},{... | collective-permute-start | bytes 393224 | tf_op jit(solution)/shard_map/ppermute | solution.py:337
  175.3 8.9 %collective-permute-start.42 = (bf16[256,256]{1,0:T(8,128)(2,1)S(1)}, bf16[256,256]{1,0:T(8,128)(2,1)S(1)}, u32[]{:S(2)}, u32[]{:S(2)}) collective-permute-start(bf16[256,256]{1,0:T(8,128)(2,1)S(1)} %get-tuple-element.86), channel_id=1, source_target_pairs={{0,8},{4,12},{8,16},{12,20},{16,24},{20,28},{24,0},{28,4},{1,9},{5... | collective-permute-start | bytes 393224 | tf_op jit(solution)/shard_map/ppermute | solution.py:337
  177.5 8.2 %collective-permute-start.43 = (bf16[256,256]{1,0:T(8,128)(2,1)S(1)}, bf16[256,256]{1,0:T(8,128)(2,1)S(1)}, u32[]{:S(2)}, u32[]{:S(2)}) collective-permute-start(bf16[256,256]{1,0:T(8,128)(2,1)S(1)} %get-tuple-element.88), channel_id=1, source_target_pairs={{0,24},{4,28},{8,0},{12,4},{16,8},{20,12},{24,16},{28,20},{1,25},{... | collective-permute-start | bytes 393224 | tf_op jit(solution)/shard_map/ppermute | solution.py:337
  (25 other events, 175.9 us)

commit v6 on v5

--- a/solution.py
+++ b/solution.py
@@ -381,7 +381,7 @@
     halo = lax.ppermute(tail, "seq", [(s, s + 1) for s in range(seqs - 1)])
     halo = jnp.where(my_seq == 0, jnp.pad(prior_kv, ((taps - prior_kv.shape[0], 0), (0, 0))), halo)
 
-    order = ["q1", "q3", "acts", "kvc1", "acts", "kvc3", "acts", "q2", "kc2", "v2"]
+    order = ["q1", "q3", "acts", "acts", "acts", "kvc1", "kvc3", "q2", "kc2", "v2"]
     acts = [hyena(hin, halo, filters)]
     here = {kind + "0": parcel(kind, 0, acts[0]) for kind in ("kvc", "q")}
     sent = []
@@ -392,7 +392,7 @@
             kind, steps = item[:-1], int(item[-1])
             value = parcel(kind, steps, *acts[: int(n >= 2)])
         if n >= 2:
-            value = after(value, sent[n - 2])
+            value = after(value, sent[n - 1] if item in ("kvc1", "kvc3") else sent[n - 2])
         sent.append(shift_z(value, steps, zs))
         if item == "acts":
             acts.append(sent[-1])
@@ -401,7 +401,8 @@
     late = ["kc2", "v2"]
     there = {item: swap_core(here[item], zs) for item in here if item not in late}
 
-    pace = [[], ["kvc1"], ["kvc3"], []]
+    ahead = [[here["q1"], here["q3"]], [acts[2]], [acts[3]], [here["kvc3"]]]
+    pace = [[], [], ["kvc1"], []]
     swapped = [[], ["kvc0", "q0"], ["q1", "q3"], ["kvc1"]]
     gain4 = gain.reshape(4, 1, width)
     half = rows // 2
@@ -421,7 +422,7 @@
         return project(place, normed_then, [sides(item)], ((0, 0),), (2,), every, True, (sums,), apart=apart)
 
     for j, own in enumerate(acts):
-        own = after(own, *([diag0, diag1] if j else [here["q1"], here["q3"]]))
+        own = after(own, *ahead[j], *([diag0, diag1] if j else []))
         from_x, from_y = swap_chan(own, 1), swap_chan(own, 2)
         if j:
             sums = project_early(every[:last]) if j == last else []

time: 189 us -> 193 us (1.021)
  waiting for transfers between devices: 72.5 us -> 80.2 us
  starting transfers between devices: 53.8 us -> 49 us
    ppermute x13, starting transfers between devices: 32.2 us -> 19.4 us  [shift_z(): return lax.ppermute(value, 'seq', pairs)]
    ppermute x16, waiting for transfers between devices: 16 us -> 25 us  [swap_chan(): return lax.ppermute(value, 'chan', [(c, c ^ bit) for c in range(4)])]
    ppermute x16, starting transfers between devices: 16.4 us -> 24.3 us  [swap_chan(): return lax.ppermute(value, 'chan', [(c, c ^ bit) for c in range(4)])]
    ppermute x14, waiting for transfers between devices: 7.38 us -> 3.99 us  [swap_core(): lax.ppermute(value, 'seq', [(2 * a + k, 2 * a + 1 - k) for a in range(zs)...]
    ppermute x13, waiting for transfers between devices: 49.1 us -> 51.2 us  [shift_z(): return lax.ppermute(value, 'seq', pairs)]
    unnamed x58 -> x64, local copies, waits for them, and re-layouts: 7.49 us -> 6.17 us
  transfers between devices with their start and end apart: 44 -> 44, of which waited for: 22 -> 21; matrix products, arithmetic and copies ran while one was open for 3% -> 4% of each run, Pallas kernels for 22% -> 22%
where the time goes in v6:
time: 193 us; the launch traced here: 192 us
  waiting for transfers between devices  80.2 us (42%)
  starting transfers between devices  49 us (25%)
  Pallas kernels  46.9 us (24%)
  local copies, waits for them, and re-layouts  13 us (7%)
  other arithmetic  2.47 us (1%)
    ppermute x13, waiting for transfers between devices, shift_z(): return lax.ppermute(value, 'seq', pairs)  51.2 us
    ppermute x16, waiting for transfers between devices, swap_chan(): return lax.ppermute(value, 'chan', [(c, c ^ bit) for c in range(4)])  25 us
    ppermute x16, starting transfers between devices, swap_chan(): return lax.ppermute(value, 'chan', [(c, c ^ bit) for c in range(4)])  24.3 us
    ppermute x13, starting transfers between devices, shift_z(): return lax.ppermute(value, 'seq', pairs)  19.4 us
    pallas_call x1, Pallas kernels, weigh(): pl.pallas_call(weigh_kernel, in_specs=[SMEM] + [VMEM] * (2 + 2 * zs), out...  12.3 us
    pallas_call x5, Pallas kernels, project(): pl.pallas_call(functools.partial(project_kernel, shifts, slabs, parts, zs...  11.1 us
    pallas_call x4, Pallas kernels, norm(): pl.pallas_call(functools.partial(norm_kernel, j), in_specs=[SMEM] + [VMEM...  8.79 us
    pallas_call x3, Pallas kernels, mix(): pl.pallas_call(functools.partial(mix_kernel, shifts), in_specs=[SMEM] + [...  6.74 us
  transfers between devices with their start and end apart: 44, of which 21 were waited for; matrix products, arithmetic and copies ran while one was open for 4% of the time, Pallas kernels for 22%

profile of v6, /device:TPU:0, one launch (start us, length us, event | category | flops | bytes accessed | tf_op | source)
XLA Modules:
  0.0 192.2 jit_solution(8130030344164499885)
XLA Ops:
  0.0 1.2 fusion
  1.2 2.4 %collective-permute-start = (bf16[128,1024]{1,0:T(8,128)(2,1)S(1)}, bf16[128,1024]{1,0:T(8,128)(2,1)S(1)}, u32[]{:S(2)}, u32[]{:S(2)}) collective-permute-start(bf16[128,1024]{1,0:T(8,128)(2,1)S(1)} %fusion), channel_id=1, source_target_pairs={{0,4},{4,8},{8,12},{12,16},{16,20},{20,24},{24,28},{1,5},{5,9},{9,... | collective-permute-start | bytes 786440 | tf_op jit(solution)/shard_map/ppermute | solution.py:381
  4.8 2.6 %collective-permute-start.1 = (bf16[512,256]{1,0:T(8,128)(2,1)S(1)}, bf16[512,256]{1,0:T(8,128)(2,1)S(1)}, u32[]{:S(2)}, u32[]{:S(2)}) collective-permute-start(bf16[512,256]{1,0:T(8,128)(2,1)S(1)} %get-tuple-element.100), channel_id=1, source_target_pairs={{0,8},{4,12},{8,16},{12,20},{16,24},{20,28},{24,0},{28,4},{1,9},{5... | collective-permute-start | bytes 786440 | tf_op jit(solution)/shard_map/ppermute | solution.py:337
  7.5 6.0 %hyena_filters.1.own_ref = bf16[256,1024]{1,0:T(8,128)(2,1)S(1)} custom-call(bf16[3,256,1024]{2,1,0:T(8,128)(2,1)S(1)} %bitcast.33, bf16[128,1024]{1,0:T(8,128)(2,1)S(1)} %pad_select_fusion.halo_ref, f32[64,128]{1,0:T(8,128)S(1)} %copy-done.20), custom_call_target="tpu_custom_call" | custom-call | flops 1 | bytes 1 | tf_op jit(solution)/shard_map/hyena_filters/pallas_call | solution.py:80
  13.5 2.1 %collective-permute-done.1.refs_1_ = bf16[512,256]{1,0:T(8,128)(2,1)S(1)} collective-permute-done((bf16[512,256]{1,0:T(8,128)(2,1)S(1)}, bf16[512,256]{1,0:T(8,128)(2,1)S(1)}, u32[]{:S(2)}, u32[]{:S(2)}) %collective-permute-start.1) | collective-permute-done | bytes 262176 | tf_op jit(solution)/shard_map/ppermute | solution.py:337
  15.7 3.5 %collective-permute-start.2 = (bf16[256,1024]{1,0:T(8,128)(2,1)S(1)}, bf16[256,1024]{1,0:T(8,128)(2,1)S(1)}, u32[]{:S(2)}, u32[]{:S(2)}) collective-permute-start(bf16[256,1024]{1,0:T(8,128)(2,1)S(1)} %hyena_filters.1.own_ref), channel_id=1, source_target_pairs={{0,8},{4,12},{8,16},{12,20},{16,24},{20,28},{24,0},{28,4},{1,9},{5... | collective-permute-start | bytes 1572872 | tf_op jit(solution)/shard_map/ppermute | solution.py:337
  19.1 2.1 %collective-permute-start.3 = (bf16[512,256]{1,0:T(8,128)(2,1)S(1)}, bf16[512,256]{1,0:T(8,128)(2,1)S(1)}, u32[]{:S(2)}, u32[]{:S(2)}) collective-permute-start(bf16[512,256]{1,0:T(8,128)(2,1)S(1)} %get-tuple-element.99), channel_id=1, source_target_pairs={{0,24},{4,28},{8,0},{12,4},{16,8},{20,12},{24,16},{28,20},{1,25},{... | collective-permute-start | bytes 786440 | tf_op jit(solution)/shard_map/ppermute | solution.py:337
  21.2 16.3 %collective-permute-done.3.refs_2_ = bf16[512,256]{1,0:T(8,128)(2,1)S(1)} collective-permute-done((bf16[512,256]{1,0:T(8,128)(2,1)S(1)}, bf16[512,256]{1,0:T(8,128)(2,1)S(1)}, u32[]{:S(2)}, u32[]{:S(2)}) %collective-permute-start.3) | collective-permute-done | bytes 262176 | tf_op jit(solution)/shard_map/ppermute | solution.py:337
  37.5 1.5 collective-permute-start.8
  39.0 1.5 collective-permute-start.10
  41.6 1.9 pad_dynamic-slice_fusion
  43.4 7.3 %collective-permute-done.8.x_ref = bf16[256,1024]{1,0:T(8,128)(2,1)S(1)} collective-permute-done((bf16[256,1024]{1,0:T(8,128)(2,1)S(1)}, bf16[256,1024]{1,0:T(8,128)(2,1)S(1)}, u32[]{:S(2)}, u32[]{:S(2)}) %collective-permute-start.8) | collective-permute-done | bytes 524320 | tf_op jit(solution)/shard_map/ppermute | solution.py:345
  50.7 1.6 collective-permute-start.9
  52.4 1.6 collective-permute-start.11
  55.6 2.8 %dynamic-slice_bitcast_fusion = (bf16[512,256]{1,0:T(8,128)(2,1)}, bf16[512,256]{1,0:T(8,128)(2,1)}, bf16[512,256]{1,0:T(8,128)(2,1)}, bf16[512,256]{1,0:T(8,128...) fusion(bf16[3,512,1024]{2,1,0:T(8,128)(2,1)} %bitcast.38, ...), kind=kLoop, calls=%fused_computation.6 | loop fusion | bytes 5242896 | tf_op jit(solution)/shard_map/squeeze | solution.py:371
  58.9 1.5 collective-permute-start.12
  61.9 7.0 %collective-permute-done.5.own_ref = bf16[256,1024]{1,0:T(8,128)(2,1)S(1)} collective-permute-done((bf16[256,1024]{1,0:T(8,128)(2,1)}, bf16[256,1024]{1,0:T(8,128)(2,1)S(1)}, u32[]{:S(2)}, u32[]{:S(2)}) %collective-permute-start.5) | collective-permute-done | bytes 524320 | tf_op jit(solution)/shard_map/ppermute | solution.py:337
  73.7 1.9 norm.4.rest_0_
  78.0 9.3 %collective-permute-done.6.refs_7_.refs_1_ = bf16[1344,256]{1,0:T(8,128)(2,1)S(1)} collective-permute-done((bf16[1344,256]{1,0:T(8,128)(2,1)}, bf16[1344,256]{1,0:T(8,128)(2,1)S(1)}, u32[]{:S(2)}, u32[]{:S(2)}) %collective-permute-start.6) | collective-permute-done | bytes 688160 | tf_op jit(solution)/shard_map/ppermute | solution.py:337
  88.4 2.4 %norm.5.rest_0_ = bf16[4,4,256,1024]{3,2,1,0:T(8,128)(2,1)S(1)} custom-call(s32[3]{0:T(128)S(1)} %pad_add_fusion.place_ref, bf16[256,1024]{1,0:T(8,128)(2,1)S(1)} %copy-done.13, bf16[256,1024]{1,0:T(8,128)(2,1)S(1)} %collective-permute-done.12.x_ref, bf16[256,1024]{1,0:T(8,128)(2,1)} %collective-permute-done.16.y_ref, ...), custom_call_target="tpu_custom_call", output_to_operand_aliasing={{}: (7, {})} | custom-call | flops 1 | bytes 1 | tf_op jit(solution)/shard_map/norm/pallas_call | solution.py:119
  90.8 8.4 %collective-permute-done.18.x_ref = bf16[256,1024]{1,0:T(8,128)(2,1)S(1)} collective-permute-done((bf16[256,1024]{1,0:T(8,128)(2,1)}, bf16[256,1024]{1,0:T(8,128)(2,1)S(1)}, u32[]{:S(2)}, u32[]{:S(2)}) %collective-permute-start.18) | collective-permute-done | bytes 524320 | tf_op jit(solution)/shard_map/ppermute | solution.py:345
  99.2 1.6 collective-permute-start.21
  102.0 3.7 %collective-permute-done.21.d0_ref = bf16[128,1024]{1,0:T(8,128)(2,1)S(1)} collective-permute-done((bf16[128,1024]{1,0:T(8,128)(2,1)S(1)}, bf16[128,1024]{1,0:T(8,128)(2,1)S(1)}, u32[]{:S(2)}, u32[]{:S(2)}) %collective-permute-start.21) | collective-permute-done | bytes 262176 | tf_op jit(solution)/shard_map/ppermute | solution.py:345
  105.7 2.1 %collective-permute-done.23.d1_ref = bf16[128,1024]{1,0:T(8,128)(2,1)S(1)} collective-permute-done((bf16[128,1024]{1,0:T(8,128)(2,1)S(1)}, bf16[128,1024]{1,0:T(8,128)(2,1)S(1)}, u32[]{:S(2)}, u32[]{:S(2)}) %collective-permute-start.23) | collective-permute-done | bytes 262176 | tf_op jit(solution)/shard_map/ppermute | solution.py:345
  107.9 1.6 collective-permute-start.27
  109.5 7.6 %collective-permute-done.30.refs_0_ = bf16[512,256]{1,0:T(8,128)(2,1)S(1)} collective-permute-done((bf16[512,256]{1,0:T(8,128)(2,1)S(1)}, bf16[512,256]{1,0:T(8,128)(2,1)S(1)}, u32[]{:S(2)}, u32[]{:S(2)}) %collective-permute-start.30) | collective-permute-done | bytes 262176 | tf_op jit(solution)/shard_map/ppermute | solution.py:337
  117.1 2.4 %norm.6.normed_ref.rest_0_ = bf16[4,4,256,1024]{3,2,1,0:T(8,128)(2,1)S(1)} custom-call(s32[3]{0:T(128)S(1)} %pad_add_fusion.place_ref, bf16[256,1024]{1,0:T(8,128)(2,1)} %collective-permute-done.4.own_ref, bf16[256,1024]{1,0:T(8,128)(2,1)S(1)} %collective-permute-done.18.x_ref, ...), custom_call_target="tpu_custom_call", output_to_operand_aliasing={{}: (7, {})} | custom-call | flops 1 | bytes 1 | tf_op jit(solution)/shard_map/norm/pallas_call | solution.py:119
  119.7 4.9 %project.5 = (f32[4,256,256]{2,1,0:T(8,128)S(1)}, f32[4,256,256]{2,1,0:T(8,128)S(1)}, f32[4,256,256]{2,1,0:T(8,128)S(1)}) custom-call(s32[3]{0:T(128)S(1)} %pad_add_fusion.place_ref, bf16[4,4,256,1024]{3,2,1,0:T(8,128)(2,1)S(1)} %norm.6.normed_ref.rest_0_, bf16[512,256]{1,0:T(8,128)(2,1)S(1)} %get-tuple-element.92.refs_0_, bf16[512,256]{1,0:T(8,128)(2,1)S(1)} %copy-done.6, ...), custom_call_target="tpu_custom_call" | custom-call | flops 1 | bytes 1 | tf_op jit(solution)/shard_map/project/pallas_call | solution.py:161
  124.6 4.4 %collective-permute-start.28 = (bf16[128,1024]{1,0:T(8,128)(2,1)S(1)}, bf16[128,1024]{1,0:T(8,128)(2,1)S(1)}, u32[]{:S(2)}, u32[]{:S(2)}) collective-permute-start(bf16[128,1024]{1,0:T(8,128)(2,1)S(1)} %slice.38), channel_id=1, source_target_pairs={{0,2},{1,3},{2,0},{3,1},{4,6},{5,7},{6,4},{7,5},{8,10},{9,11},{10,... | collective-permute-start | bytes 786440 | tf_op jit(solution)/shard_map/ppermute | solution.py:345
  129.1 6.0 %collective-permute-start.29 = (bf16[128,1024]{1,0:T(8,128)(2,1)S(1)}, bf16[128,1024]{1,0:T(8,128)(2,1)S(1)}, u32[]{:S(2)}, u32[]{:S(2)}) collective-permute-start(bf16[128,1024]{1,0:T(8,128)(2,1)S(1)} %slice.39), channel_id=1, source_target_pairs={{0,1},{1,0},{2,3},{3,2},{4,5},{5,4},{6,7},{7,6},{8,9},{9,8},{10,11... | collective-permute-start | bytes 786440 | tf_op jit(solution)/shard_map/ppermute | solution.py:345
  135.1 3.5 %collective-permute-done.32.refs_2_.refs_0_ = bf16[832,256]{1,0:T(8,128)(2,1)S(1)} collective-permute-done((bf16[832,256]{1,0:T(8,128)(2,1)S(1)}, bf16[832,256]{1,0:T(8,128)(2,1)S(1)}, u32[]{:S(2)}, u32[]{:S(2)}) %collective-permute-start.32) | collective-permute-done | bytes 426016 | tf_op jit(solution)/shard_map/ppermute | solution.py:337
  138.6 3.1 %collective-permute-done.29.d1_ref = bf16[128,1024]{1,0:T(8,128)(2,1)S(1)} collective-permute-done((bf16[128,1024]{1,0:T(8,128)(2,1)S(1)}, bf16[128,1024]{1,0:T(8,128)(2,1)S(1)}, u32[]{:S(2)}, u32[]{:S(2)}) %collective-permute-start.29) | collective-permute-done | bytes 262176 | tf_op jit(solution)/shard_map/ppermute | solution.py:345
  141.8 2.9 %collective-permute-start.38 = (bf16[512,256]{1,0:T(8,128)(2,1)S(1)}, bf16[512,256]{1,0:T(8,128)(2,1)S(1)}, u32[]{:S(2)}, u32[]{:S(2)}) collective-permute-start(bf16[512,256]{1,0:T(8,128)(2,1)S(1)} %copy-done.26), channel_id=1, source_target_pairs={{0,16},{4,20},{8,24},{12,28},{16,0},{20,4},{24,8},{28,12},{1,17},{... | collective-permute-start | bytes 786440 | tf_op jit(solution)/shard_map/ppermute | solution.py:337
  144.7 2.1 %norm.7.normed_ref = bf16[4,4,256,1024]{3,2,1,0:T(8,128)(2,1)S(1)} custom-call(s32[3]{0:T(128)S(1)} %pad_add_fusion.place_ref, bf16[256,1024]{1,0:T(8,128)(2,1)S(1)} %copy-done.11, bf16[256,1024]{1,0:T(8,128)(2,1)S(1)} %collective-permute-done.24.x_ref, bf16[256,1024]{1,0:T(8,128)(2,1)S(1)} %collective-permute-done.27.y_ref, ...), custom_call_target="tpu_custom_call", output_to_operand_aliasing={{}: (7, {})} | custom-call | flops 1 | bytes 1 | tf_op jit(solution)/shard_map/norm/pallas_call | solution.py:119
  146.8 2.4 %project.6 = (f32[4,256,256]{2,1,0:T(8,128)S(1)}, f32[4,256,256]{2,1,0:T(8,128)S(1)}, f32[4,256,256]{2,1,0:T(8,128)S(1)}) custom-call(s32[3]{0:T(128)S(1)} %pad_add_fusion.place_ref, bf16[4,4,256,1024]{3,2,1,0:T(8,128)(2,1)S(1)} %norm.7.normed_ref, ...), custom_call_target="tpu_custom_call", output_to_operand_aliasing={{0}: (14, {}), {1}: (15, {}), {2}: (16, {})} | custom-call | flops 1 | bytes 1 | tf_op jit(solution)/shard_map/project/pallas_call | solution.py:161
  149.2 1.3 project.7.q_ref
  150.6 1.3 project.8
  154.0 12.3 %weigh.1 = (bf16[4,2,256,1216]{3,2,1,0:T(8,128)(2,1)S(1)}, bf16[4,2,4,256,512]{4,3,2,1,0:T(8,128)(2,1)S(1)}, f32[4,2,256,128]{3,2,1,0:T(8,128)S(1)}) custom-call(s32[3]{0:T(128)S(1)} %pad_add_fusion.place_ref, bf16[4,256,256]{2,1,0:T(8,128)(2,1)S(1)} %project.7.q_ref, bf16[1216,256]{1,0:T(8,128)(2,1)S(1)} %get-tuple-element.71.ck_ref, ...), custom_call_target="tpu_custom_call" | custom-call | flops 1 | bytes 1 | tf_op jit(solution)/shard_map/weigh/pallas_call | solution.py:236
  166.7 1.3 collective-permute-done.39.refs_1_
  167.9 1.3 project.9.v_ref
  169.5 1.6 collective-permute-done.40.vs_ref
  171.2 2.0 %mix.3 = bf16[256,256]{1,0:T(8,128)(2,1)S(1)} custom-call(s32[3]{0:T(128)S(1)} %pad_add_fusion.place_ref, bf16[4,2,256,1216]{3,2,1,0:T(8,128)(2,1)S(1)} %get-tuple-element.78.old_ref, bf16[4,2,4,256,512]{4,3,2,1,0:T(8,128)(2,1)S(1)} %get-tuple-element.79.new_ref, f32[4,2,256,128]{3,2,1,0:T(8,128)S(1)} %get-tuple-element.80.sum_ref, ...), custom_call_target="tpu_custom_call" | custom-call | flops 1 | bytes 1 | tf_op jit(solution)/shard_map/mix/pallas_call | solution.py:280
  173.2 3.4 %mix.4 = (bf16[256,256]{1,0:T(8,128)(2,1)S(1)}, bf16[256,256]{1,0:T(8,128)(2,1)S(1)}) custom-call(s32[3]{0:T(128)S(1)} %pad_add_fusion.place_ref, bf16[4,2,256,1216]{3,2,1,0:T(8,128)(2,1)S(1)} %get-tuple-element.78.old_ref, bf16[4,2,4,256,512]{4,3,2,1,0:T(8,128)(2,1)S(1)} %get-tuple-element.79.new_ref, f32[4,2,256,128]{3,2,1,0:T(8,128)S(1)} %get-tuple-element.80.sum_ref, ...), custom_call_target="tpu_custom_call" | custom-call | flops 1 | bytes 1 | tf_op jit(solution)/shard_map/mix/pallas_call | solution.py:280
  176.6 6.2 %collective-permute-start.42 = (bf16[256,256]{1,0:T(8,128)(2,1)S(1)}, bf16[256,256]{1,0:T(8,128)(2,1)S(1)}, u32[]{:S(2)}, u32[]{:S(2)}) collective-permute-start(bf16[256,256]{1,0:T(8,128)(2,1)S(1)} %get-tuple-element.86), channel_id=1, source_target_pairs={{0,8},{4,12},{8,16},{12,20},{16,24},{20,28},{24,0},{28,4},{1,9},{5... | collective-permute-start | bytes 393224 | tf_op jit(solution)/shard_map/ppermute | solution.py:337
  183.2 1.4 mix.5.refs_0_
  185.3 2.2 %collective-permute-done.42.refs_1_ = bf16[256,256]{1,0:T(8,128)(2,1)S(1)} collective-permute-done((bf16[256,256]{1,0:T(8,128)(2,1)S(1)}, bf16[256,256]{1,0:T(8,128)(2,1)S(1)}, u32[]{:S(2)}, u32[]{:S(2)}) %collective-permute-start.42) | collective-permute-done | bytes 131104 | tf_op jit(solution)/shard_map/ppermute | solution.py:337
  187.5 2.1 %collective-permute-done.43.refs_3_ = bf16[256,256]{1,0:T(8,128)(2,1)S(1)} collective-permute-done((bf16[256,256]{1,0:T(8,128)(2,1)S(1)}, bf16[256,256]{1,0:T(8,128)(2,1)S(1)}, u32[]{:S(2)}, u32[]{:S(2)}) %collective-permute-start.43) | collective-permute-done | bytes 131104 | tf_op jit(solution)/shard_map/ppermute | solution.py:337
  190.2 2.0 %join.1 = bf16[256,1024]{1,0:T(8,128)(2,1)} custom-call(s32[3]{0:T(128)} %copy-done.19, bf16[256,256]{1,0:T(8,128)(2,1)} %copy-done.9, bf16[256,256]{1,0:T(8,128)(2,1)} %copy-done.30, bf16[256,256]{1,0:T(8,128)(2,1)} %copy-done.29, bf16[256,256]{1,0:T(8,128)(2,1)} %copy-done.31), custom_call_target="tpu_custom_call" | custom-call | tf_op jit(solution)/shard_map/join/pallas_call | solution.py:326
  (138 shorter events, 20.3 us)
Async XLA Ops:
  1.2 6.1 %collective-permute-start = (bf16[128,1024]{1,0:T(8,128)(2,1)S(1)}, bf16[128,1024]{1,0:T(8,128)(2,1)S(1)}, u32[]{:S(2)}, u32[]{:S(2)}) collective-permute-start(bf16[128,1024]{1,0:T(8,128)(2,1)S(1)} %fusion), channel_id=1, source_target_pairs={{0,4},{4,8},{8,12},{12,16},{16,20},{20,24},{24,28},{1,5},{5,9},{9,... | collective-permute-start | bytes 786440 | tf_op jit(solution)/shard_map/ppermute | solution.py:381
  4.8 10.9 %collective-permute-start.1 = (bf16[512,256]{1,0:T(8,128)(2,1)S(1)}, bf16[512,256]{1,0:T(8,128)(2,1)S(1)}, u32[]{:S(2)}, u32[]{:S(2)}) collective-permute-start(bf16[512,256]{1,0:T(8,128)(2,1)S(1)} %get-tuple-element.100), channel_id=1, source_target_pairs={{0,8},{4,12},{8,16},{12,20},{16,24},{20,28},{24,0},{28,4},{1,9},{5... | collective-permute-start | bytes 786440 | tf_op jit(solution)/shard_map/ppermute | solution.py:337
  15.7 42.7 %copy-start.5 = (bf16[512,256]{1,0:T(8,128)(2,1)}, bf16[512,256]{1,0:T(8,128)(2,1)S(1)}, u32[]{:S(2)}) copy-start(bf16[512,256]{1,0:T(8,128)(2,1)S(1)} %collective-permute-done.1.refs_1_) | copy-start | bytes 786436
  15.7 24.8 %collective-permute-start.2 = (bf16[256,1024]{1,0:T(8,128)(2,1)S(1)}, bf16[256,1024]{1,0:T(8,128)(2,1)S(1)}, u32[]{:S(2)}, u32[]{:S(2)}) collective-permute-start(bf16[256,1024]{1,0:T(8,128)(2,1)S(1)} %hyena_filters.1.own_ref), channel_id=1, source_target_pairs={{0,8},{4,12},{8,16},{12,20},{16,24},{20,28},{24,0},{28,4},{1,9},{5... | collective-permute-start | bytes 1572872 | tf_op jit(solution)/shard_map/ppermute | solution.py:337
  19.1 18.4 %collective-permute-start.3 = (bf16[512,256]{1,0:T(8,128)(2,1)S(1)}, bf16[512,256]{1,0:T(8,128)(2,1)S(1)}, u32[]{:S(2)}, u32[]{:S(2)}) collective-permute-start(bf16[512,256]{1,0:T(8,128)(2,1)S(1)} %get-tuple-element.99), channel_id=1, source_target_pairs={{0,24},{4,28},{8,0},{12,4},{16,8},{20,12},{24,16},{28,20},{1,25},{... | collective-permute-start | bytes 786440 | tf_op jit(solution)/shard_map/ppermute | solution.py:337
  37.5 13.2 %collective-permute-start.8 = (bf16[256,1024]{1,0:T(8,128)(2,1)S(1)}, bf16[256,1024]{1,0:T(8,128)(2,1)S(1)}, u32[]{:S(2)}, u32[]{:S(2)}) collective-permute-start(bf16[256,1024]{1,0:T(8,128)(2,1)S(1)} %hyena_filters.1.own_ref), channel_id=1, source_target_pairs={{0,1},{1,0},{2,3},{3,2},{4,5},{5,4},{6,7},{7,6},{8,9},{9,8},{10,11... | collective-permute-start | bytes 1572872 | tf_op jit(solution)/shard_map/ppermute | solution.py:345
  39.0 13.4 %collective-permute-start.10 = (bf16[256,1024]{1,0:T(8,128)(2,1)S(1)}, bf16[256,1024]{1,0:T(8,128)(2,1)S(1)}, u32[]{:S(2)}, u32[]{:S(2)}) collective-permute-start(bf16[256,1024]{1,0:T(8,128)(2,1)S(1)} %hyena_filters.1.own_ref), channel_id=1, source_target_pairs={{0,2},{1,3},{2,0},{3,1},{4,6},{5,7},{6,4},{7,5},{8,10},{9,11},{10,... | collective-permute-start | bytes 1572872 | tf_op jit(solution)/shard_map/ppermute | solution.py:345
  40.5 14.6 %collective-permute-start.4 = (bf16[256,1024]{1,0:T(8,128)(2,1)S(1)}, bf16[256,1024]{1,0:T(8,128)(2,1)}, u32[]{:S(2)}, u32[]{:S(2)}) collective-permute-start(bf16[256,1024]{1,0:T(8,128)(2,1)S(1)} %collective-permute-done.2.own_ref), channel_id=1, source_target_pairs={{0,8},{4,12},{8,16},{12,20},{16,24},{20,28},{24,0},{28,4},{1,9},{5... | collective-permute-start | bytes 1572872 | tf_op jit(solution)/shard_map/ppermute | solution.py:337
  50.7 7.8 %collective-permute-start.9 = (bf16[128,1024]{1,0:T(8,128)(2,1)S(1)}, bf16[128,1024]{1,0:T(8,128)(2,1)S(1)}, u32[]{:S(2)}, u32[]{:S(2)}) collective-permute-start(bf16[128,1024]{1,0:T(8,128)(2,1)S(1)} %slice.42), channel_id=1, source_target_pairs={{0,2},{1,3},{2,0},{3,1},{4,6},{5,7},{6,4},{7,5},{8,10},{9,11},{10,... | collective-permute-start | bytes 786440 | tf_op jit(solution)/shard_map/ppermute | solution.py:345
  52.4 6.6 %collective-permute-start.11 = (bf16[128,1024]{1,0:T(8,128)(2,1)S(1)}, bf16[128,1024]{1,0:T(8,128)(2,1)S(1)}, u32[]{:S(2)}, u32[]{:S(2)}) collective-permute-start(bf16[128,1024]{1,0:T(8,128)(2,1)S(1)} %slice.43), channel_id=1, source_target_pairs={{0,1},{1,0},{2,3},{3,2},{4,5},{5,4},{6,7},{7,6},{8,9},{9,8},{10,11... | collective-permute-start | bytes 786440 | tf_op jit(solution)/shard_map/ppermute | solution.py:345
  55.1 13.8 %collective-permute-start.5 = (bf16[256,1024]{1,0:T(8,128)(2,1)}, bf16[256,1024]{1,0:T(8,128)(2,1)S(1)}, u32[]{:S(2)}, u32[]{:S(2)}) collective-permute-start(bf16[256,1024]{1,0:T(8,128)(2,1)} %collective-permute-done.4.own_ref), channel_id=1, source_target_pairs={{0,8},{4,12},{8,16},{12,20},{16,24},{20,28},{24,0},{28,4},{1,9},{5... | collective-permute-start | bytes 1572872 | tf_op jit(solution)/shard_map/ppermute | solution.py:337
  58.5 17.2 %collective-permute-start.13 = (bf16[1344,256]{1,0:T(8,128)(2,1)S(1)}, bf16[1344,256]{1,0:T(8,128)(2,1)S(1)}, u32[]{:S(2)}, u32[]{:S(2)}) collective-permute-start(bf16[1344,256]{1,0:T(8,128)(2,1)S(1)} %pad_maximum_fusion.2.refs_6_.refs_0_), channel_id=1, source_target_pairs={{0,4},{4,0},{8,12},{12,8},{16,20},{20,16},{24,28},{28,24},{1,5},{5... | collective-permute-start | bytes 2064392 | tf_op jit(solution)/shard_map/ppermute | solution.py:341
  58.9 16.7 %collective-permute-start.12 = (bf16[256,1024]{1,0:T(8,128)(2,1)}, bf16[256,1024]{1,0:T(8,128)(2,1)S(1)}, u32[]{:S(2)}, u32[]{:S(2)}) collective-permute-start(bf16[256,1024]{1,0:T(8,128)(2,1)} %copy-done.12), channel_id=1, source_target_pairs={{0,1},{1,0},{2,3},{3,2},{4,5},{5,4},{6,7},{7,6},{8,9},{9,8},{10,11... | collective-permute-start | bytes 1572872 | tf_op jit(solution)/shard_map/ppermute | solution.py:345
  60.4 15.9 %collective-permute-start.16 = (bf16[256,1024]{1,0:T(8,128)(2,1)}, bf16[256,1024]{1,0:T(8,128)(2,1)}, u32[]{:S(2)}, u32[]{:S(2)}) collective-permute-start(bf16[256,1024]{1,0:T(8,128)(2,1)} %copy-done.12), channel_id=1, source_target_pairs={{0,2},{1,3},{2,0},{3,1},{4,6},{5,7},{6,4},{7,5},{8,10},{9,11},{10,... | collective-permute-start | bytes 1572872 | tf_op jit(solution)/shard_map/ppermute | solution.py:345
  68.8 18.4 %collective-permute-start.6 = (bf16[1344,256]{1,0:T(8,128)(2,1)}, bf16[1344,256]{1,0:T(8,128)(2,1)S(1)}, u32[]{:S(2)}, u32[]{:S(2)}) collective-permute-start(bf16[1344,256]{1,0:T(8,128)(2,1)} %pad_maximum_fusion.1), channel_id=1, source_target_pairs={{0,8},{4,12},{8,16},{12,20},{16,24},{20,28},{24,0},{28,4},{1,9},{5... | collective-permute-start | bytes 2064392 | tf_op jit(solution)/shard_map/ppermute | solution.py:337
  69.6 6.0 %collective-permute-start.14 = (bf16[512,256]{1,0:T(8,128)(2,1)S(1)}, bf16[512,256]{1,0:T(8,128)(2,1)}, u32[]{:S(2)}, u32[]{:S(2)}) collective-permute-start(bf16[512,256]{1,0:T(8,128)(2,1)S(1)} %get-tuple-element.92.refs_0_), channel_id=1, source_target_pairs={{0,4},{4,0},{8,12},{12,8},{16,20},{20,16},{24,28},{28,24},{1,5},{5... | collective-permute-start | bytes 786440 | tf_op jit(solution)/shard_map/ppermute | solution.py:341
  69.7 113.5 %copy-start.19 = (s32[3]{0:T(128)}, s32[3]{0:T(128)S(1)}, u32[]{:S(2)}) copy-start(s32[3]{0:T(128)S(1)} %pad_add_fusion.place_ref) | copy-start | bytes 40
  75.7 11.5 %collective-permute-start.15 = (bf16[128,1024]{1,0:T(8,128)(2,1)S(1)}, bf16[128,1024]{1,0:T(8,128)(2,1)S(1)}, u32[]{:S(2)}, u32[]{:S(2)}) collective-permute-start(bf16[128,1024]{1,0:T(8,128)(2,1)S(1)} %slice.34), channel_id=1, source_target_pairs={{0,2},{1,3},{2,0},{3,1},{4,6},{5,7},{6,4},{7,5},{8,10},{9,11},{10,... | collective-permute-start | bytes 786440 | tf_op jit(solution)/shard_map/ppermute | solution.py:345
  77.3 10.0 %collective-permute-start.17 = (bf16[128,1024]{1,0:T(8,128)(2,1)S(1)}, bf16[128,1024]{1,0:T(8,128)(2,1)S(1)}, u32[]{:S(2)}, u32[]{:S(2)}) collective-permute-start(bf16[128,1024]{1,0:T(8,128)(2,1)S(1)} %slice.35), channel_id=1, source_target_pairs={{0,1},{1,0},{2,3},{3,2},{4,5},{5,4},{6,7},{7,6},{8,9},{9,8},{10,11... | collective-permute-start | bytes 786440 | tf_op jit(solution)/shard_map/ppermute | solution.py:345
  77.9 31.5 %copy-start.27 = (bf16[512,256]{1,0:T(8,128)(2,1)S(1)}, bf16[512,256]{1,0:T(8,128)(2,1)}, u32[]{:S(2)}) copy-start(bf16[512,256]{1,0:T(8,128)(2,1)} %get-tuple-element.67) | copy-start | bytes 786436
  78.0 31.5 %copy-start.21 = (bf16[512,256]{1,0:T(8,128)(2,1)S(1)}, bf16[512,256]{1,0:T(8,128)(2,1)}, u32[]{:S(2)}) copy-start(bf16[512,256]{1,0:T(8,128)(2,1)} %get-tuple-element.90) | copy-start | bytes 786436
  87.2 14.2 %collective-permute-start.7 = (bf16[1344,256]{1,0:T(8,128)(2,1)S(1)}, bf16[1344,256]{1,0:T(8,128)(2,1)S(1)}, u32[]{:S(2)}, u32[]{:S(2)}) collective-permute-start(bf16[1344,256]{1,0:T(8,128)(2,1)S(1)} %pad_maximum_fusion), channel_id=1, source_target_pairs={{0,24},{4,28},{8,0},{12,4},{16,8},{20,12},{24,16},{28,20},{1,25},{... | collective-permute-start | bytes 2064392 | tf_op jit(solution)/shard_map/ppermute | solution.py:337
  87.2 12.0 %collective-permute-start.18 = (bf16[256,1024]{1,0:T(8,128)(2,1)}, bf16[256,1024]{1,0:T(8,128)(2,1)S(1)}, u32[]{:S(2)}, u32[]{:S(2)}) collective-permute-start(bf16[256,1024]{1,0:T(8,128)(2,1)} %collective-permute-done.4.own_ref), channel_id=1, source_target_pairs={{0,1},{1,0},{2,3},{3,2},{4,5},{5,4},{6,7},{7,6},{8,9},{9,8},{10,11... | collective-permute-start | bytes 1572872 | tf_op jit(solution)/shard_map/ppermute | solution.py:345
  87.8 13.0 %collective-permute-start.22 = (bf16[256,1024]{1,0:T(8,128)(2,1)}, bf16[256,1024]{1,0:T(8,128)(2,1)S(1)}, u32[]{:S(2)}, u32[]{:S(2)}) collective-permute-start(bf16[256,1024]{1,0:T(8,128)(2,1)} %collective-permute-done.4.own_ref), channel_id=1, source_target_pairs={{0,2},{1,3},{2,0},{3,1},{4,6},{5,7},{6,4},{7,5},{8,10},{9,11},{10,... | collective-permute-start | bytes 1572872 | tf_op jit(solution)/shard_map/ppermute | solution.py:345
  87.9 2.9 %collective-permute-start.19 = (bf16[512,256]{1,0:T(8,128)(2,1)S(1)}, bf16[512,256]{1,0:T(8,128)(2,1)S(1)}, u32[]{:S(2)}, u32[]{:S(2)}) collective-permute-start(bf16[512,256]{1,0:T(8,128)(2,1)S(1)} %copy-done.6), channel_id=1, source_target_pairs={{0,4},{4,0},{8,12},{12,8},{16,20},{20,16},{24,28},{28,24},{1,5},{5... | collective-permute-start | bytes 786440 | tf_op jit(solution)/shard_map/ppermute | solution.py:341
  87.9 2.9 %collective-permute-start.20 = (bf16[512,256]{1,0:T(8,128)(2,1)S(1)}, bf16[512,256]{1,0:T(8,128)(2,1)S(1)}, u32[]{:S(2)}, u32[]{:S(2)}) collective-permute-start(bf16[512,256]{1,0:T(8,128)(2,1)S(1)} %copy-done.8), channel_id=1, source_target_pairs={{0,4},{4,0},{8,12},{12,8},{16,20},{20,16},{24,28},{28,24},{1,5},{5... | collective-permute-start | bytes 786440 | tf_op jit(solution)/shard_map/ppermute | solution.py:341
  99.2 6.4 %collective-permute-start.21 = (bf16[128,1024]{1,0:T(8,128)(2,1)S(1)}, bf16[128,1024]{1,0:T(8,128)(2,1)S(1)}, u32[]{:S(2)}, u32[]{:S(2)}) collective-permute-start(bf16[128,1024]{1,0:T(8,128)(2,1)S(1)} %slice.36), channel_id=1, source_target_pairs={{0,2},{1,3},{2,0},{3,1},{4,6},{5,7},{6,4},{7,5},{8,10},{9,11},{10,... | collective-permute-start | bytes 786440 | tf_op jit(solution)/shard_map/ppermute | solution.py:345
  100.8 6.9 %collective-permute-start.23 = (bf16[128,1024]{1,0:T(8,128)(2,1)S(1)}, bf16[128,1024]{1,0:T(8,128)(2,1)S(1)}, u32[]{:S(2)}, u32[]{:S(2)}) collective-permute-start(bf16[128,1024]{1,0:T(8,128)(2,1)S(1)} %slice.37), channel_id=1, source_target_pairs={{0,1},{1,0},{2,3},{3,2},{4,5},{5,4},{6,7},{7,6},{8,9},{9,8},{10,11... | collective-permute-start | bytes 786440 | tf_op jit(solution)/shard_map/ppermute | solution.py:345
  101.4 18.1 %collective-permute-start.25 = (bf16[1344,256]{1,0:T(8,128)(2,1)S(1)}, bf16[1344,256]{1,0:T(8,128)(2,1)S(1)}, u32[]{:S(2)}, u32[]{:S(2)}) collective-permute-start(bf16[1344,256]{1,0:T(8,128)(2,1)S(1)} %collective-permute-done.6.refs_7_.refs_1_), channel_id=1, source_target_pairs={{0,4},{4,0},{8,12},{12,8},{16,20},{20,16},{24,28},{28,24},{1,5},{5... | collective-permute-start | bytes 2064392 | tf_op jit(solution)/shard_map/ppermute | solution.py:341
  101.5 18.2 %collective-permute-start.26 = (bf16[1344,256]{1,0:T(8,128)(2,1)S(1)}, bf16[1344,256]{1,0:T(8,128)(2,1)S(1)}, u32[]{:S(2)}, u32[]{:S(2)}) collective-permute-start(bf16[1344,256]{1,0:T(8,128)(2,1)S(1)} %collective-permute-done.7.refs_8_.refs_3_), channel_id=1, source_target_pairs={{0,4},{4,0},{8,12},{12,8},{16,20},{20,16},{24,28},{28,24},{1,5},{5... | collective-permute-start | bytes 2064392 | tf_op jit(solution)/shard_map/ppermute | solution.py:341
  107.8 16.8 %collective-permute-start.24 = (bf16[256,1024]{1,0:T(8,128)(2,1)S(1)}, bf16[256,1024]{1,0:T(8,128)(2,1)S(1)}, u32[]{:S(2)}, u32[]{:S(2)}) collective-permute-start(bf16[256,1024]{1,0:T(8,128)(2,1)S(1)} %copy-done.11), channel_id=1, source_target_pairs={{0,1},{1,0},{2,3},{3,2},{4,5},{5,4},{6,7},{7,6},{8,9},{9,8},{10,11... | collective-permute-start | bytes 1572872 | tf_op jit(solution)/shard_map/ppermute | solution.py:345
  107.9 16.7 %collective-permute-start.27 = (bf16[256,1024]{1,0:T(8,128)(2,1)S(1)}, bf16[256,1024]{1,0:T(8,128)(2,1)S(1)}, u32[]{:S(2)}, u32[]{:S(2)}) collective-permute-start(bf16[256,1024]{1,0:T(8,128)(2,1)S(1)} %copy-done.11), channel_id=1, source_target_pairs={{0,2},{1,3},{2,0},{3,1},{4,6},{5,7},{6,4},{7,5},{8,10},{9,11},{10,... | collective-permute-start | bytes 1572872 | tf_op jit(solution)/shard_map/ppermute | solution.py:345
  109.5 7.7 %collective-permute-start.30 = (bf16[512,256]{1,0:T(8,128)(2,1)S(1)}, bf16[512,256]{1,0:T(8,128)(2,1)S(1)}, u32[]{:S(2)}, u32[]{:S(2)}) collective-permute-start(bf16[512,256]{1,0:T(8,128)(2,1)S(1)} %copy-done.27), channel_id=1, source_target_pairs={{0,16},{4,20},{8,24},{12,28},{16,0},{20,4},{24,8},{28,12},{1,17},{... | collective-permute-start | bytes 786440 | tf_op jit(solution)/shard_map/ppermute | solution.py:337
  117.1 21.5 %collective-permute-start.32 = (bf16[832,256]{1,0:T(8,128)(2,1)S(1)}, bf16[832,256]{1,0:T(8,128)(2,1)S(1)}, u32[]{:S(2)}, u32[]{:S(2)}) collective-permute-start(bf16[832,256]{1,0:T(8,128)(2,1)S(1)} %pad_maximum_fusion.3), channel_id=1, source_target_pairs={{0,16},{4,20},{8,24},{12,28},{16,0},{20,4},{24,8},{28,12},{1,17},{... | collective-permute-start | bytes 1277960 | tf_op jit(solution)/shard_map/ppermute | solution.py:337
  119.6 15.5 %collective-permute-start.31 = (bf16[512,256]{1,0:T(8,128)(2,1)S(1)}, bf16[512,256]{1,0:T(8,128)(2,1)S(1)}, u32[]{:S(2)}, u32[]{:S(2)}) collective-permute-start(bf16[512,256]{1,0:T(8,128)(2,1)S(1)} %collective-permute-done.30.refs_0_), channel_id=1, source_target_pairs={{0,4},{4,0},{8,12},{12,8},{16,20},{20,16},{24,28},{28,24},{1,5},{5... | collective-permute-start | bytes 786440 | tf_op jit(solution)/shard_map/ppermute | solution.py:341
  124.6 14.0 %collective-permute-start.28 = (bf16[128,1024]{1,0:T(8,128)(2,1)S(1)}, bf16[128,1024]{1,0:T(8,128)(2,1)S(1)}, u32[]{:S(2)}, u32[]{:S(2)}) collective-permute-start(bf16[128,1024]{1,0:T(8,128)(2,1)S(1)} %slice.38), channel_id=1, source_target_pairs={{0,2},{1,3},{2,0},{3,1},{4,6},{5,7},{6,4},{7,5},{8,10},{9,11},{10,... | collective-permute-start | bytes 786440 | tf_op jit(solution)/shard_map/ppermute | solution.py:345
  129.1 12.7 %collective-permute-start.29 = (bf16[128,1024]{1,0:T(8,128)(2,1)S(1)}, bf16[128,1024]{1,0:T(8,128)(2,1)S(1)}, u32[]{:S(2)}, u32[]{:S(2)}) collective-permute-start(bf16[128,1024]{1,0:T(8,128)(2,1)S(1)} %slice.39), channel_id=1, source_target_pairs={{0,1},{1,0},{2,3},{3,2},{4,5},{5,4},{6,7},{7,6},{8,9},{9,8},{10,11... | collective-permute-start | bytes 786440 | tf_op jit(solution)/shard_map/ppermute | solution.py:345
  141.8 8.7 %collective-permute-start.33 = (bf16[832,256]{1,0:T(8,128)(2,1)S(1)}, bf16[832,256]{1,0:T(8,128)(2,1)S(1)}, u32[]{:S(2)}, u32[]{:S(2)}) collective-permute-start(bf16[832,256]{1,0:T(8,128)(2,1)S(1)} %collective-permute-done.32.refs_2_.refs_0_), channel_id=1, source_target_pairs={{0,4},{4,0},{8,12},{12,8},{16,20},{20,16},{24,28},{28,24},{1,5},{5... | collective-permute-start | bytes 1277960 | tf_op jit(solution)/shard_map/ppermute | solution.py:341
  141.8 24.5 %collective-permute-start.38 = (bf16[512,256]{1,0:T(8,128)(2,1)S(1)}, bf16[512,256]{1,0:T(8,128)(2,1)S(1)}, u32[]{:S(2)}, u32[]{:S(2)}) collective-permute-start(bf16[512,256]{1,0:T(8,128)(2,1)S(1)} %copy-done.26), channel_id=1, source_target_pairs={{0,16},{4,20},{8,24},{12,28},{16,0},{20,4},{24,8},{28,12},{1,17},{... | collective-permute-start | bytes 786440 | tf_op jit(solution)/shard_map/ppermute | solution.py:337
  151.8 1.4 collective-permute-start.34
  152.1 1.3 collective-permute-start.35
  152.4 1.3 collective-permute-start.36
  152.7 1.3 collective-permute-start.37
  166.3 1.6 collective-permute-start.39
  169.2 2.0 %collective-permute-start.40 = (bf16[4,256,256]{2,1,0:T(8,128)(2,1)S(1)}, bf16[4,256,256]{2,1,0:T(8,128)(2,1)S(1)}, u32[]{:S(2)}, u32[]{:S(2)}) collective-permute-start(bf16[4,256,256]{2,1,0:T(8,128)(2,1)S(1)} %project.9.v_ref), channel_id=1, source_target_pairs={{0,4},{4,0},{8,12},{12,8},{16,20},{20,16},{24,28},{28,24},{1,5},{5... | collective-permute-start | bytes 1572872 | tf_op jit(solution)/shard_map/ppermute | solution.py:341
  173.1 10.1 %collective-permute-start.41 = (bf16[256,256]{1,0:T(8,128)(2,1)S(1)}, bf16[256,256]{1,0:T(8,128)(2,1)S(1)}, u32[]{:S(2)}, u32[]{:S(2)}) collective-permute-start(bf16[256,256]{1,0:T(8,128)(2,1)S(1)} %mix.3), channel_id=1, source_target_pairs={{0,16},{4,20},{8,24},{12,28},{16,0},{20,4},{24,8},{28,12},{1,17},{... | collective-permute-start | bytes 393224 | tf_op jit(solution)/shard_map/ppermute | solution.py:337
  176.6 10.8 %collective-permute-start.42 = (bf16[256,256]{1,0:T(8,128)(2,1)S(1)}, bf16[256,256]{1,0:T(8,128)(2,1)S(1)}, u32[]{:S(2)}, u32[]{:S(2)}) collective-permute-start(bf16[256,256]{1,0:T(8,128)(2,1)S(1)} %get-tuple-element.86), channel_id=1, source_target_pairs={{0,8},{4,12},{8,16},{12,20},{16,24},{20,28},{24,0},{28,4},{1,9},{5... | collective-permute-start | bytes 393224 | tf_op jit(solution)/shard_map/ppermute | solution.py:337
  182.8 6.7 %collective-permute-start.43 = (bf16[256,256]{1,0:T(8,128)(2,1)S(1)}, bf16[256,256]{1,0:T(8,128)(2,1)S(1)}, u32[]{:S(2)}, u32[]{:S(2)}) collective-permute-start(bf16[256,256]{1,0:T(8,128)(2,1)S(1)} %get-tuple-element.88), channel_id=1, source_target_pairs={{0,24},{4,28},{8,0},{12,4},{16,8},{20,12},{24,16},{28,20},{1,25},{... | collective-permute-start | bytes 393224 | tf_op jit(solution)/shard_map/ppermute | solution.py:337
  (28 other events, 212.6 us)

commit v7 on v5

--- a/solution.py
+++ b/solution.py
@@ -135,7 +135,7 @@
     before, outs = rest[:extra], rest[-len(parts) * (zs if apart else 1) :]
     z, core = place_ref[1], place_ref[2]
     depth = normed_ref.shape[3] // 2
-    for part, (group, row) in enumerate(parts):
+    for part, (group, row_of) in enumerate(parts):
         for j in slabs:
             total = before[part][j] if before else None
             for i, shift in enumerate(shifts):
@@ -143,7 +143,7 @@
                 for k in range(2):
                     at = pl.multiple_of((core ^ k) * depth, depth)
                     left = normed_ref[j, block, :, pl.ds(at, depth)]
-                    right = weights[(2 * group + k) * n + i][row : row + depth, :]
+                    right = weights[(2 * group + k) * n + i][row_of[i] : row_of[i] + depth, :]
                     term = jnp.dot(left, right, preferred_element_type=F32)
                     total = term if total is None else total + term
             if apart:
@@ -180,7 +180,7 @@
 
 
 def weigh_kernel(place_ref, q_ref, ck_ref, *refs):
-    z, core = place_ref[1], place_ref[2]
+    core = place_ref[2]
     zs, rows, cols = q_ref.shape
     k_refs, ks_refs, (old_ref, new_ref, sum_ref, k_ref, ks_ref, scratch) = refs[:zs], refs[zs : 2 * zs], refs[2 * zs :]
     for j in range(zs):
@@ -190,7 +190,7 @@
     row = lax.broadcasted_iota(jnp.int32, (rows, rows), 0)
     col = lax.broadcasted_iota(jnp.int32, (rows, rows), 1)
     causal = col <= row
-    slab = [lax.rem(z + zs - b, zs) for b in range(zs)]
+    slab = [place_ref[3 + b] for b in range(zs)]
 
     for block in range(zs):
         for h in range(cols // HEAD):
@@ -259,7 +259,7 @@
         block = lax.rem(z + shift, zs)
 
         def add(b, state):
-            at = lax.rem(z + zs - b, zs)
+            at = place_ref[3 + b]
             result = []
             for h, summed in zip(heads, state):
                 probs = new_ref[block, h, b]
@@ -335,6 +335,10 @@
 def shift_z(value, steps, zs):
     pairs = [(2 * a + k, 2 * ((a + steps) % zs) + k) for a in range(zs) for k in range(2)]
     return lax.ppermute(value, "seq", pairs)
+
+
+def step_z(value, steps, sources):
+    return lax.ppermute(value, "seq", [(2 * a + k, 2 * (a + steps) + k) for a in sources for k in range(2)])
 
 
 def swap_core(value, zs):
@@ -359,7 +363,8 @@
     my_seq = lax.axis_index("seq")
     z, core = my_seq // 2, my_seq % 2
     chan = lax.axis_index("chan")
-    place = jnp.stack([chan, z, core]).astype(jnp.int32)
+    slabs = jnp.array([[0, 1, 2, 3], [3, 0, 1, 2], [2, 1, 0, 3], [3, 2, 1, 0]], jnp.int32)
+    place = jnp.concatenate([jnp.stack([chan, z, core]).astype(jnp.int32), slabs[z]])
 
     w_t = jnp.transpose(w_qkv, (1, 0, 2))
     caches = [jnp.pad(c, ((0, PAD), (0, 0))) for c in (cache_k, cache_v)]
@@ -381,65 +386,86 @@
     halo = lax.ppermute(tail, "seq", [(s, s + 1) for s in range(seqs - 1)])
     halo = jnp.where(my_seq == 0, jnp.pad(prior_kv, ((taps - prior_kv.shape[0], 0), (0, 0))), halo)
 
-    order = ["q1", "q3", "acts", "kvc1", "acts", "kvc3", "acts", "q2", "kc2", "v2"]
-    acts = [hyena(hin, halo, filters)]
-    here = {kind + "0": parcel(kind, 0, acts[0]) for kind in ("kvc", "q")}
-    sent = []
-    for n, item in enumerate(order):
-        if item == "acts":
-            value, steps = acts[-1], 1
-        else:
-            kind, steps = item[:-1], int(item[-1])
-            value = parcel(kind, steps, *acts[: int(n >= 2)])
-        if n >= 2:
-            value = after(value, sent[n - 2])
-        sent.append(shift_z(value, steps, zs))
-        if item == "acts":
-            acts.append(sent[-1])
-        else:
-            here[item] = sent[-1]
-    late = ["kc2", "v2"]
-    there = {item: swap_core(here[item], zs) for item in here if item not in late}
-
-    pace = [[], ["kvc1"], ["kvc3"], []]
-    swapped = [[], ["kvc0", "q0"], ["q1", "q3"], ["kvc1"]]
+    here, there = {}, {}
+    every, early, last = tuple(range(zs)), (0, 1, 3), zs - 1
+
+    def send(item, *others):
+        kind, shift = item[:-1], int(item[-1])
+        value = parcel(kind, shift, *others)
+        here[item] = shift_z(after(value, *others) if others else value, shift, zs) if shift else value
+
+    def swap(item, *others):
+        there[item] = swap_core(after(here[item], *others) if others else here[item], zs)
+
+    def near(slab, *others):
+        slab = after(slab, *others) if others else slab
+        return slab, swap_chan(slab, 1), swap_chan(slab, 2)
+
+    def far(slab, from_x, from_y, *others):
+        from_x, from_y = after(from_x, *others), after(from_y, *others)
+        return slab, from_x, from_y, swap_chan(from_x[:half], 2), swap_chan(from_y[half:], 1)
+
+    def sides(*items):
+        return [[side[item] for item in items] for side in (here, there)]
+
+    def project_early(slabs, into=()):
+        groups = [sides("qkvc0", "q1", "q3"), sides("qkvc0", "kvc1", "kvc3")]
+        parts = ((0, (0, 0, 0)), (1, (depth, 0, 0)), (1, (2 * depth, depth, depth)))
+        return project(place, normed, groups, parts, early, slabs, False, (), into)
+
+    def project_last(item, sums, *others, apart=False):
+        normed_then = after(normed, *others) if others else normed
+        return project(place, normed_then, [sides(item)], ((0, (0,)),), (2,), every, True, (sums,), apart=apart)
+
+    send("q1")
+    send("q3")
+    own = after(hyena(hin, halo, filters), here["q1"], here["q3"])
+    send("qkvc0", own)
+    swap("qkvc0")
     gain4 = gain.reshape(4, 1, width)
     half = rows // 2
-    normed, diag0, diag1 = None, None, None
-    every, early, last = tuple(range(zs)), (0, 1, 3), zs - 1
-
-    def sides(*items):
-        return [[side[item] for item in items] for side in (here, there)]
-
-    def project_early(slabs, into=()):
-        groups = [sides("q0", "q1", "q3"), sides("kvc0", "kvc1", "kvc3")]
-        parts = ((0, 0), (1, 0), (1, depth))
-        return project(place, normed, groups, parts, early, slabs, False, (), into)
-
-    def project_last(item, sums, *others, apart=False):
-        normed_then = after(normed, *others) if others else normed
-        return project(place, normed_then, [sides(item)], ((0, 0),), (2,), every, True, (sums,), apart=apart)
-
-    for j, own in enumerate(acts):
-        own = after(own, *([diag0, diag1] if j else [here["q1"], here["q3"]]))
-        from_x, from_y = swap_chan(own, 1), swap_chan(own, 2)
-        if j:
-            sums = project_early(every[:last]) if j == last else []
-            normed = after(normed, *sums) if j == last else normed
-            settled = [normed] + [there[item] for item in swapped[j]] + [here[item] for item in pace[j]]
-            from_x, from_y = after(from_x, *settled), after(from_y, *settled)
-        diag0 = swap_chan(from_x[:half], 2)
-        diag1 = swap_chan(from_y[half:], 1)
-        normed = norm(place, j, zs, own, from_x, from_y, diag0, diag1, gain4, normed)
-
-    there["kc2"] = swap_core(after(here["kc2"], there["q2"], diag0, diag1), zs)
+
+    slab0 = near(own)
+    up, down = step_z(own, 1, (0, 1, 2)), step_z(own, -1, (1, 2, 3))
+    send("kvc1", up, down)
+    slab = jnp.where(z < 2, down, up)
+    rest = jnp.where(z == 1, up, down)
+    up, down = after(up, *slab0), after(down, *slab0)
+    up, down = step_z(up, 1, (1, 2)), step_z(down, -1, (1, 2))
+    send("kvc3", here["kvc1"])
+    slab0 = far(*slab0, rest)
+    slab1 = near(slab, *slab0[3:])
+    normed = norm(place, 0, zs, *slab0, gain4, None)
+    slab = jnp.where(z < 2, down, up)
+    ends = [(2 * a + k, 2 * b + k) for a, b in ((1, 0), (2, 3)) for k in range(2)]
+    end = lax.ppermute(after(slab, *slab1), "seq", ends)
+    slab1 = far(*slab1, normed, here["kvc1"], there["qkvc0"])
+    slab2 = near(slab, *slab1[3:])
+    normed = norm(place, 1, zs, *slab1, gain4, normed)
+    slab = jnp.where(z % 3 == 0, end, rest)
+    send("q2", end)
+    swap("q1")
+    swap("q3")
+    swap("kvc1")
+    slab2 = far(*slab2, normed, here["kvc3"], there["q1"], there["q3"], there["kvc1"])
+    slab3 = near(slab, *slab2[3:])
+    normed = norm(place, 2, zs, *slab2, gain4, normed)
+    send("kc2", here["kvc3"])
+    send("v2", here["q2"])
+    swap("kvc3")
+    swap("q2")
+    sums = project_early(every[:last])
+    slab3 = far(*slab3, *sums)
+    normed = norm(place, 3, zs, *slab3, gain4, after(normed, *sums))
+
+    swap("kc2", there["q2"], *slab3[3:])
     q_sum, k_sum, v_sum = project_early(every[last:], sums)
     (q,) = project_last("q2", q_sum)
-    kept = sum(sides("kvc0", "kvc1", "kc2", "kvc3"), [])
-    ck, cv = pack(kept, [depth if i % zs == 2 else 2 * depth for i in range(2 * zs)], crow)
+    kept = sum(sides("qkvc0", "kvc1", "kc2", "kvc3"), [])
+    ck, cv = pack(kept, [3 * depth, 2 * depth, depth, 2 * depth] * 2, crow)
     k = project_last("kc2", k_sum, q, ck, apart=True)
     weights = weigh(place, q, k, [swap_core(slab, zs) for slab in k], ck)
-    there["v2"] = swap_core(after(here["v2"], weights[2]), zs)
+    swap("v2", weights[2])
     (v,) = project_last("v2", v_sum)
     v_sib = swap_core(v, zs)
     pieces, out = {}, None
@@ -532,7 +558,7 @@
 
 def solution(mesh):
     sizes = mesh.shape
-    paired = sizes["chan"] == 4 and HEADS // sizes["chan"] == sizes["seq"]
+    paired = sizes["chan"] == 4 and sizes["seq"] == 8
     return jax.shard_map(
         fast_body if paired else body,
         mesh=mesh,

time: 189 us -> 217 us (1.15)
  local copies, waits for them, and re-layouts: 12.3 us -> 49 us
  waiting for transfers between devices: 72.5 us -> 43.3 us
  starting transfers between devices: 53.8 us -> 64.3 us
  other arithmetic: 2.46 us -> 8.92 us
  Pallas kernels: 46.8 us -> 49.4 us
    ppermute x13 -> x10, waiting for transfers between devices: 49.1 us -> 11.1 us  [shift_z(): return lax.ppermute(value, 'seq', pairs)]
    unnamed x58 -> x85, local copies, waits for them, and re-layouts: 7.49 us -> 37.2 us
    ppermute x0 -> x5, starting transfers between devices: none -> 10.7 us  [the longest x4 9.37 us: step_z(): lax.ppermute(value, 'seq', [(2 * a + k, 2 * (a + steps) + k) for a in sou...]
    ppermute x0 -> x5, waiting for transfers between devices: none -> 6.11 us  [the longest x4 3.68 us: step_z(): lax.ppermute(value, 'seq', [(2 * a + k, 2 * (a + steps) + k) for a in sou...]
    ppermute x16, waiting for transfers between devices: 16 us -> 22 us  [swap_chan(): return lax.ppermute(value, 'chan', [(c, c ^ bit) for c in range(4)])]
    select_n x0 -> x3, other arithmetic: none -> 5.08 us  [the longest x1 2.07 us: fast_body(): rest = jnp.where(z == 1, up, down)]
    ppermute x14 -> x13, waiting for transfers between devices: 7.38 us -> 4.06 us  [swap_core(): lax.ppermute(value, 'seq', [(2 * a + k, 2 * a + 1 - k) for a in range(zs)...]
    slice x8, local copies, waits for them, and re-layouts: 1.1 us -> 3.95 us  [the longest x4 1.97 us: far(): from_x[:half]]
  transfers between devices with their start and end apart: 44 -> 45, of which waited for: 22 -> 20; matrix products, arithmetic and copies ran while one was open for 3% -> 10% of each run, Pallas kernels for 22% -> 20%
where the time goes in v7:
time: 217 us; the launch traced here: 216 us
  starting transfers between devices  64.3 us (30%)
  Pallas kernels  49.4 us (23%)
  local copies, waits for them, and re-layouts  49 us (23%)
  waiting for transfers between devices  43.3 us (20%)
  other arithmetic  8.92 us (4%)
    unnamed x85, local copies, waits for them, and re-layouts  37.2 us
    ppermute x10, starting transfers between devices, shift_z(): return lax.ppermute(value, 'seq', pairs)  31.8 us
    ppermute x16, waiting for transfers between devices, swap_chan(): return lax.ppermute(value, 'chan', [(c, c ^ bit) for c in range(4)])  22 us
    ppermute x16, starting transfers between devices, swap_chan(): return lax.ppermute(value, 'chan', [(c, c ^ bit) for c in range(4)])  17.5 us
    pallas_call x1, Pallas kernels, weigh(): pl.pallas_call(weigh_kernel, in_specs=[SMEM] + [VMEM] * (2 + 2 * zs), out...  12.4 us
    pallas_call x5, Pallas kernels, project(): pl.pallas_call(functools.partial(project_kernel, shifts, slabs, parts, zs...  11.8 us
    ppermute x10, waiting for transfers between devices, shift_z(): return lax.ppermute(value, 'seq', pairs)  11.1 us
    ppermute x4, starting transfers between devices, step_z(): lax.ppermute(value, 'seq', [(2 * a + k, 2 * (a + steps) + k) for a in sou...  9.37 us
  transfers between devices with their start and end apart: 45, of which 20 were waited for; matrix products, arithmetic and copies ran while one was open for 10% of the time, Pallas kernels for 20%

profile of v7, /device:TPU:0, one launch (start us, length us, event | category | flops | bytes accessed | tf_op | source)
XLA Modules:
  0.0 215.6 jit_solution(5526393754894025342)
XLA Ops:
  1.2 2.4 %collective-permute-start = (bf16[128,1024]{1,0:T(8,128)(2,1)S(1)}, bf16[128,1024]{1,0:T(8,128)(2,1)S(1)}, u32[]{:S(2)}, u32[]{:S(2)}) collective-permute-start(bf16[128,1024]{1,0:T(8,128)(2,1)S(1)} %fusion), channel_id=1, source_target_pairs={{0,4},{4,8},{8,12},{12,16},{16,20},{20,24},{24,28},{1,5},{5,9},{9,... | collective-permute-start | bytes 786440 | tf_op jit(solution)/shard_map/ppermute | solution.py:386
  4.8 2.6 %collective-permute-start.1 = (bf16[512,256]{1,0:T(8,128)(2,1)S(1)}, bf16[512,256]{1,0:T(8,128)(2,1)S(1)}, u32[]{:S(2)}, u32[]{:S(2)}) collective-permute-start(bf16[512,256]{1,0:T(8,128)(2,1)S(1)} %get-tuple-element.108), channel_id=1, source_target_pairs={{0,8},{4,12},{8,16},{12,20},{16,24},{20,28},{24,0},{28,4},{1,9},{5... | collective-permute-start | bytes 786440 | tf_op jit(solution)/shard_map/ppermute | solution.py:337
  7.4 2.1 collective-permute-start.2
  9.6 6.0 %hyena_filters.1.own_ref = bf16[256,1024]{1,0:T(8,128)(2,1)S(1)} custom-call(bf16[3,256,1024]{2,1,0:T(8,128)(2,1)S(1)} %bitcast.35, bf16[128,1024]{1,0:T(8,128)(2,1)S(1)} %pad_select_fusion.halo_ref, f32[64,128]{1,0:T(8,128)S(1)} %copy-done.31), custom_call_target="tpu_custom_call" | custom-call | flops 1 | bytes 1 | tf_op jit(solution)/shard_map/hyena_filters/pallas_call | solution.py:80
  15.9 6.3 %collective-permute-done.2.refs_2_ = bf16[512,256]{1,0:T(8,128)(2,1)} collective-permute-done((bf16[512,256]{1,0:T(8,128)(2,1)S(1)}, bf16[512,256]{1,0:T(8,128)(2,1)}, u32[]{:S(2)}, u32[]{:S(2)}) %collective-permute-start.2) | collective-permute-done | bytes 262176 | tf_op jit(solution)/shard_map/ppermute | solution.py:337
  23.5 1.5 collective-permute-start.4
  25.0 1.5 collective-permute-start.5
  26.5 5.4 %collective-permute-start.7 = (bf16[256,1024]{1,0:T(8,128)(2,1)S(1)}, bf16[256,1024]{1,0:T(8,128)(2,1)}, u32[]{:S(2)}, u32[]{:S(2)}) collective-permute-start(bf16[256,1024]{1,0:T(8,128)(2,1)S(1)} %hyena_filters.1.own_ref), channel_id=1, source_target_pairs={{0,8},{4,12},{8,16},{12,20},{16,24},{20,28},{1,9},{5,13},{9,17},{1... | collective-permute-start | bytes 1572872 | tf_op jit(solution)/shard_map/ppermute | solution.py:341
  36.2 2.0 collective-permute-done.3
  39.9 1.7 collective-permute-done.7
  41.6 1.5 collective-permute-start.8
  43.1 2.1 broadcast_select_fusion
  48.5 3.4 %collective-permute-done.9.d0_ref = bf16[128,1024]{1,0:T(8,128)(2,1)S(1)} collective-permute-done((bf16[128,1024]{1,0:T(8,128)(2,1)S(1)}, bf16[128,1024]{1,0:T(8,128)(2,1)S(1)}, u32[]{:S(2)}, u32[]{:S(2)}) %collective-permute-start.9) | collective-permute-done | bytes 262176 | tf_op jit(solution)/shard_map/ppermute | solution.py:349
  52.5 5.8 %collective-permute-start.14 = (bf16[1344,256]{1,0:T(8,128)(2,1)}, bf16[1344,256]{1,0:T(8,128)(2,1)S(1)}, u32[]{:S(2)}, u32[]{:S(2)}) collective-permute-start(bf16[1344,256]{1,0:T(8,128)(2,1)} %pad_maximum_fusion), channel_id=1, source_target_pairs={{0,8},{4,12},{8,16},{12,20},{16,24},{20,28},{24,0},{28,4},{1,9},{5... | collective-permute-start | bytes 2064392 | tf_op jit(solution)/shard_map/ppermute | solution.py:337
  67.5 1.9 norm.4.rest_0_
  69.4 3.3 %copy-done = bf16[4,4,256,1024]{3,2,1,0:T(8,128)(2,1)} copy-done((bf16[4,4,256,1024]{3,2,1,0:T(8,128)(2,1)}, bf16[4,4,256,1024]{3,2,1,0:T(8,128)(2,1)S(1)}, u32[]{:S(2)}) %copy-start) | copy-done | bytes 8388632
  72.7 1.9 broadcast_select_fusion.2.own_ref
  77.9 1.3 collective-permute-start.13
  80.2 1.6 collective-permute-start.17
  85.1 3.5 %collective-permute-done.17.d1_ref = bf16[128,1024]{1,0:T(8,128)(2,1)S(1)} collective-permute-done((bf16[128,1024]{1,0:T(8,128)(2,1)S(1)}, bf16[128,1024]{1,0:T(8,128)(2,1)S(1)}, u32[]{:S(2)}, u32[]{:S(2)}) %collective-permute-start.17) | collective-permute-done | bytes 262176 | tf_op jit(solution)/shard_map/ppermute | solution.py:349
  89.4 1.5 collective-permute-start.18
  92.4 2.4 %collective-permute-done.13 = bf16[256,1024]{1,0:T(8,128)(2,1)} collective-permute-done((bf16[256,1024]{1,0:T(8,128)(2,1)}, bf16[256,1024]{1,0:T(8,128)(2,1)}, u32[]{:S(2)}, u32[]{:S(2)}) %collective-permute-start.13) | collective-permute-done | bytes 524320 | tf_op jit(solution)/shard_map/ppermute | solution.py:441
  94.9 3.4 %copy-done.1 = bf16[4,4,256,1024]{3,2,1,0:T(8,128)(2,1)S(1)} copy-done((bf16[4,4,256,1024]{3,2,1,0:T(8,128)(2,1)S(1)}, bf16[4,4,256,1024]{3,2,1,0:T(8,128)(2,1)}, u32[]{:S(2)}) %copy-start.1) | copy-done | bytes 8388632
  101.8 2.6 %norm.5.rest_0_ = bf16[4,4,256,1024]{3,2,1,0:T(8,128)(2,1)S(1)} custom-call(s32[7]{0:T(128)S(1)} %copy-done.29, bf16[256,1024]{1,0:T(8,128)(2,1)S(1)} %copy-done.9, bf16[256,1024]{1,0:T(8,128)(2,1)} %collective-permute-done.11.x_ref, bf16[256,1024]{1,0:T(8,128)(2,1)} %collective-permute-done.12.y_ref, ...), custom_call_target="tpu_custom_call", output_to_operand_aliasing={{}: (7, {})} | custom-call | flops 1 | bytes 1 | tf_op jit(solution)/shard_map/norm/pallas_call | solution.py:119
  104.4 3.3 %copy-done.2 = bf16[4,4,256,1024]{3,2,1,0:T(8,128)(2,1)} copy-done((bf16[4,4,256,1024]{3,2,1,0:T(8,128)(2,1)}, bf16[4,4,256,1024]{3,2,1,0:T(8,128)(2,1)S(1)}, u32[]{:S(2)}) %copy-start.2) | copy-done | bytes 8388632
  108.8 12.7 %collective-permute-start.31 = (bf16[512,256]{1,0:T(8,128)(2,1)S(1)}, bf16[512,256]{1,0:T(8,128)(2,1)S(1)}, u32[]{:S(2)}, u32[]{:S(2)}) collective-permute-start(bf16[512,256]{1,0:T(8,128)(2,1)S(1)} %dynamic-slice_bitcast_fusion.2), channel_id=1, source_target_pairs={{0,16},{4,20},{8,24},{12,28},{16,0},{20,4},{24,8},{28,12},{1,17},{... | collective-permute-start | bytes 786440 | tf_op jit(solution)/shard_map/ppermute | solution.py:337
  122.7 1.6 collective-permute-start.23
  127.4 3.9 %collective-permute-done.23.d0_ref = bf16[128,1024]{1,0:T(8,128)(2,1)S(1)} collective-permute-done((bf16[128,1024]{1,0:T(8,128)(2,1)S(1)}, bf16[128,1024]{1,0:T(8,128)(2,1)S(1)}, u32[]{:S(2)}, u32[]{:S(2)}) %collective-permute-start.23) | collective-permute-done | bytes 262176 | tf_op jit(solution)/shard_map/ppermute | solution.py:349
  131.3 2.3 %collective-permute-done.25.d1_ref = bf16[128,1024]{1,0:T(8,128)(2,1)S(1)} collective-permute-done((bf16[128,1024]{1,0:T(8,128)(2,1)S(1)}, bf16[128,1024]{1,0:T(8,128)(2,1)S(1)}, u32[]{:S(2)}, u32[]{:S(2)}) %collective-permute-start.25) | collective-permute-done | bytes 262176 | tf_op jit(solution)/shard_map/ppermute | solution.py:349
  136.7 3.4 %copy-done.3 = bf16[4,4,256,1024]{3,2,1,0:T(8,128)(2,1)S(1)} copy-done((bf16[4,4,256,1024]{3,2,1,0:T(8,128)(2,1)S(1)}, bf16[4,4,256,1024]{3,2,1,0:T(8,128)(2,1)}, u32[]{:S(2)}) %copy-start.3) | copy-done | bytes 8388632
  140.1 2.7 %norm.6.normed_ref.rest_0_ = bf16[4,4,256,1024]{3,2,1,0:T(8,128)(2,1)S(1)} custom-call(s32[7]{0:T(128)S(1)} %copy-done.30, bf16[256,1024]{1,0:T(8,128)(2,1)} %broadcast_select_fusion.2.own_ref, bf16[256,1024]{1,0:T(8,128)(2,1)} %collective-permute-done.18.x_ref, bf16[256,1024]{1,0:T(8,128)(2,1)} %collective-permute-done.24.y_ref, ...), custom_call_target="tpu_custom_call", output_to_operand_aliasing={{}: (7, {})} | custom-call | flops 1 | bytes 1 | tf_op jit(solution)/shard_map/norm/pallas_call | solution.py:119
  142.8 3.3 %copy-done.4 = bf16[4,4,256,1024]{3,2,1,0:T(8,128)(2,1)} copy-done((bf16[4,4,256,1024]{3,2,1,0:T(8,128)(2,1)}, bf16[4,4,256,1024]{3,2,1,0:T(8,128)(2,1)S(1)}, u32[]{:S(2)}) %copy-start.4) | copy-done | bytes 8388632
  146.2 3.4 %copy-done.5 = bf16[4,4,256,1024]{3,2,1,0:T(8,128)(2,1)S(1)} copy-done((bf16[4,4,256,1024]{3,2,1,0:T(8,128)(2,1)S(1)}, bf16[4,4,256,1024]{3,2,1,0:T(8,128)(2,1)}, u32[]{:S(2)}) %copy-start.5) | copy-done | bytes 8388632
  149.5 5.3 %project.5 = (f32[4,256,256]{2,1,0:T(8,128)S(1)}, f32[4,256,256]{2,1,0:T(8,128)S(1)}, f32[4,256,256]{2,1,0:T(8,128)S(1)}) custom-call(s32[7]{0:T(128)S(1)} %copy-done.30, bf16[4,4,256,1024]{3,2,1,0:T(8,128)(2,1)S(1)} %copy-done.5, bf16[1856,256]{1,0:T(8,128)(2,1)S(1)} %get-tuple-element.116.refs_0_.refs_6_, ...), custom_call_target="tpu_custom_call" | custom-call | flops 1 | bytes 1 | tf_op jit(solution)/shard_map/project/pallas_call | solution.py:161
  157.3 6.4 %collective-permute-done.29.d0_ref = bf16[128,1024]{1,0:T(8,128)(2,1)S(1)} collective-permute-done((bf16[128,1024]{1,0:T(8,128)(2,1)S(1)}, bf16[128,1024]{1,0:T(8,128)(2,1)S(1)}, u32[]{:S(2)}, u32[]{:S(2)}) %collective-permute-start.29) | collective-permute-done | bytes 262176 | tf_op jit(solution)/shard_map/ppermute | solution.py:349
  164.7 2.8 %collective-permute-start.39 = (bf16[512,256]{1,0:T(8,128)(2,1)S(1)}, bf16[512,256]{1,0:T(8,128)(2,1)S(1)}, u32[]{:S(2)}, u32[]{:S(2)}) collective-permute-start(bf16[512,256]{1,0:T(8,128)(2,1)S(1)} %get-tuple-element.95), channel_id=1, source_target_pairs={{0,16},{4,20},{8,24},{12,28},{16,0},{20,4},{24,8},{28,12},{1,17},{... | collective-permute-start | bytes 786440 | tf_op jit(solution)/shard_map/ppermute | solution.py:337
  167.5 2.1 norm.7.normed_ref
  169.6 2.7 %project.6 = (f32[4,256,256]{2,1,0:T(8,128)S(1)}, f32[4,256,256]{2,1,0:T(8,128)S(1)}, f32[4,256,256]{2,1,0:T(8,128)S(1)}) custom-call(s32[7]{0:T(128)S(1)} %copy-done.30, bf16[4,4,256,1024]{3,2,1,0:T(8,128)(2,1)S(1)} %norm.7.normed_ref, ...), custom_call_target="tpu_custom_call", output_to_operand_aliasing={{0}: (14, {}), {1}: (15, {}), {2}: (16, {})} | custom-call | flops 1 | bytes 1 | tf_op jit(solution)/shard_map/project/pallas_call | solution.py:161
  178.2 12.4 %weigh.1 = (bf16[4,2,256,1216]{3,2,1,0:T(8,128)(2,1)S(1)}, bf16[4,2,4,256,512]{4,3,2,1,0:T(8,128)(2,1)S(1)}, f32[4,2,256,128]{3,2,1,0:T(8,128)S(1)}) custom-call(s32[7]{0:T(128)S(1)} %copy-done.30, bf16[4,256,256]{2,1,0:T(8,128)(2,1)S(1)} %project.7.q_ref, bf16[1216,256]{1,0:T(8,128)(2,1)S(1)} %get-tuple-element.84.ck_ref, ...), custom_call_target="tpu_custom_call" | custom-call | flops 1 | bytes 1 | tf_op jit(solution)/shard_map/weigh/pallas_call | solution.py:236
  191.0 1.3 collective-permute-done.40.refs_1_
  193.9 1.7 collective-permute-done.41.vs_ref
  195.6 2.0 mix.3
  197.6 3.4 %mix.4 = (bf16[256,256]{1,0:T(8,128)(2,1)S(1)}, bf16[256,256]{1,0:T(8,128)(2,1)S(1)}) custom-call(s32[7]{0:T(128)S(1)} %copy-done.30, bf16[4,2,256,1216]{3,2,1,0:T(8,128)(2,1)S(1)} %get-tuple-element.91.old_ref, bf16[4,2,4,256,512]{4,3,2,1,0:T(8,128)(2,1)S(1)} %get-tuple-element.92.new_ref, f32[4,2,256,128]{3,2,1,0:T(8,128)S(1)} %get-tuple-element.93.sum_ref, ...), custom_call_target="tpu_custom_call" | custom-call | flops 1 | bytes 1 | tf_op jit(solution)/shard_map/mix/pallas_call | solution.py:280
  201.0 2.3 %collective-permute-start.43 = (bf16[256,256]{1,0:T(8,128)(2,1)S(1)}, bf16[256,256]{1,0:T(8,128)(2,1)S(1)}, u32[]{:S(2)}, u32[]{:S(2)}) collective-permute-start(bf16[256,256]{1,0:T(8,128)(2,1)S(1)} %get-tuple-element.100), channel_id=1, source_target_pairs={{0,8},{4,12},{8,16},{12,20},{16,24},{20,28},{24,0},{28,4},{1,9},{5... | collective-permute-start | bytes 393224 | tf_op jit(solution)/shard_map/ppermute | solution.py:337
  203.3 2.3 %collective-permute-start.44 = (bf16[256,256]{1,0:T(8,128)(2,1)S(1)}, bf16[256,256]{1,0:T(8,128)(2,1)S(1)}, u32[]{:S(2)}, u32[]{:S(2)}) collective-permute-start(bf16[256,256]{1,0:T(8,128)(2,1)S(1)} %get-tuple-element.102), channel_id=1, source_target_pairs={{0,24},{4,28},{8,0},{12,4},{16,8},{20,12},{24,16},{28,20},{1,25},{... | collective-permute-start | bytes 393224 | tf_op jit(solution)/shard_map/ppermute | solution.py:337
  205.7 4.6 %collective-permute-done.42.refs_2_ = bf16[256,256]{1,0:T(8,128)(2,1)S(1)} collective-permute-done((bf16[256,256]{1,0:T(8,128)(2,1)S(1)}, bf16[256,256]{1,0:T(8,128)(2,1)S(1)}, u32[]{:S(2)}, u32[]{:S(2)}) %collective-permute-start.42) | collective-permute-done | bytes 131104 | tf_op jit(solution)/shard_map/ppermute | solution.py:337
  210.2 1.4 mix.5.refs_0_
  213.6 2.0 join.1
  (168 shorter events, 58.1 us)
Async XLA Ops:
  1.2 8.2 %collective-permute-start = (bf16[128,1024]{1,0:T(8,128)(2,1)S(1)}, bf16[128,1024]{1,0:T(8,128)(2,1)S(1)}, u32[]{:S(2)}, u32[]{:S(2)}) collective-permute-start(bf16[128,1024]{1,0:T(8,128)(2,1)S(1)} %fusion), channel_id=1, source_target_pairs={{0,4},{4,8},{8,12},{12,16},{16,20},{20,24},{24,28},{1,5},{5,9},{9,... | collective-permute-start | bytes 786440 | tf_op jit(solution)/shard_map/ppermute | solution.py:386
  4.8 11.1 %collective-permute-start.1 = (bf16[512,256]{1,0:T(8,128)(2,1)S(1)}, bf16[512,256]{1,0:T(8,128)(2,1)S(1)}, u32[]{:S(2)}, u32[]{:S(2)}) collective-permute-start(bf16[512,256]{1,0:T(8,128)(2,1)S(1)} %get-tuple-element.108), channel_id=1, source_target_pairs={{0,8},{4,12},{8,16},{12,20},{16,24},{20,28},{24,0},{28,4},{1,9},{5... | collective-permute-start | bytes 786440 | tf_op jit(solution)/shard_map/ppermute | solution.py:337
  7.4 14.8 %collective-permute-start.2 = (bf16[512,256]{1,0:T(8,128)(2,1)S(1)}, bf16[512,256]{1,0:T(8,128)(2,1)}, u32[]{:S(2)}, u32[]{:S(2)}) collective-permute-start(bf16[512,256]{1,0:T(8,128)(2,1)S(1)} %get-tuple-element.107), channel_id=1, source_target_pairs={{0,24},{4,28},{8,0},{12,4},{16,8},{20,12},{24,16},{28,20},{1,25},{... | collective-permute-start | bytes 786440 | tf_op jit(solution)/shard_map/ppermute | solution.py:337
  9.6 25.2 %copy-start.35 = (bf16[152,1024]{1,0:T(8,128)(2,1)S(1)}, bf16[152,1024]{1,0:T(8,128)(2,1)}, u32[]{:S(2)}) copy-start(bf16[152,1024]{1,0:T(8,128)(2,1)} %param.13) | copy-start | bytes 933892
  15.6 26.0 %copy-start.10 = (bf16[256,1024]{1,0:T(8,128)(2,1)}, bf16[256,1024]{1,0:T(8,128)(2,1)S(1)}, u32[]{:S(2)}) copy-start(bf16[256,1024]{1,0:T(8,128)(2,1)S(1)} %hyena_filters.1.own_ref) | copy-start | bytes 1572868
  15.6 19.8 %copy-start.36 = (bf16[152,1024]{1,0:T(8,128)(2,1)S(1)}, bf16[152,1024]{1,0:T(8,128)(2,1)}, u32[]{:S(2)}) copy-start(bf16[152,1024]{1,0:T(8,128)(2,1)} %param.14) | copy-start | bytes 933892
  22.2 15.9 %collective-permute-start.3 = (bf16[256,1024]{1,0:T(8,128)(2,1)S(1)}, bf16[256,1024]{1,0:T(8,128)(2,1)}, u32[]{:S(2)}, u32[]{:S(2)}) collective-permute-start(bf16[256,1024]{1,0:T(8,128)(2,1)S(1)} %hyena_filters.1.own_ref), channel_id=1, source_target_pairs={{8,0},{12,4},{16,8},{20,12},{24,16},{28,20},{9,1},{13,5},{17,9},{2... | collective-permute-start | bytes 1572872 | tf_op jit(solution)/shard_map/ppermute | solution.py:341
  23.5 14.6 %collective-permute-start.4 = (bf16[256,1024]{1,0:T(8,128)(2,1)S(1)}, bf16[256,1024]{1,0:T(8,128)(2,1)S(1)}, u32[]{:S(2)}, u32[]{:S(2)}) collective-permute-start(bf16[256,1024]{1,0:T(8,128)(2,1)S(1)} %hyena_filters.1.own_ref), channel_id=1, source_target_pairs={{0,1},{1,0},{2,3},{3,2},{4,5},{5,4},{6,7},{7,6},{8,9},{9,8},{10,11... | collective-permute-start | bytes 1572872 | tf_op jit(solution)/shard_map/ppermute | solution.py:349
  25.0 13.7 %collective-permute-start.5 = (bf16[256,1024]{1,0:T(8,128)(2,1)S(1)}, bf16[256,1024]{1,0:T(8,128)(2,1)S(1)}, u32[]{:S(2)}, u32[]{:S(2)}) collective-permute-start(bf16[256,1024]{1,0:T(8,128)(2,1)S(1)} %hyena_filters.1.own_ref), channel_id=1, source_target_pairs={{0,2},{1,3},{2,0},{3,1},{4,6},{5,7},{6,4},{7,5},{8,10},{9,11},{10,... | collective-permute-start | bytes 1572872 | tf_op jit(solution)/shard_map/ppermute | solution.py:349
  26.5 15.1 %collective-permute-start.7 = (bf16[256,1024]{1,0:T(8,128)(2,1)S(1)}, bf16[256,1024]{1,0:T(8,128)(2,1)}, u32[]{:S(2)}, u32[]{:S(2)}) collective-permute-start(bf16[256,1024]{1,0:T(8,128)(2,1)S(1)} %hyena_filters.1.own_ref), channel_id=1, source_target_pairs={{0,8},{4,12},{8,16},{12,20},{16,24},{20,28},{1,9},{5,13},{9,17},{1... | collective-permute-start | bytes 1572872 | tf_op jit(solution)/shard_map/ppermute | solution.py:341
  36.2 38.5 %collective-permute-start.15 = (bf16[1856,256]{1,0:T(8,128)(2,1)S(1)}, bf16[1856,256]{1,0:T(8,128)(2,1)S(1)}, u32[]{:S(2)}, u32[]{:S(2)}) collective-permute-start(bf16[1856,256]{1,0:T(8,128)(2,1)S(1)} %get-tuple-element.116.refs_0_.refs_6_), channel_id=1, source_target_pairs={{0,4},{4,0},{8,12},{12,8},{16,20},{20,16},{24,28},{28,24},{1,5},{5... | collective-permute-start | bytes 2850824 | tf_op jit(solution)/shard_map/ppermute | solution.py:345
  38.6 21.0 %collective-permute-start.6 = (bf16[256,1024]{1,0:T(8,128)(2,1)}, bf16[256,1024]{1,0:T(8,128)(2,1)}, u32[]{:S(2)}, u32[]{:S(2)}) collective-permute-start(bf16[256,1024]{1,0:T(8,128)(2,1)} %collective-permute-done.3), channel_id=1, source_target_pairs={{8,0},{12,4},{16,8},{20,12},{9,1},{13,5},{17,9},{21,13},{10,2},{14... | collective-permute-start | bytes 1572872 | tf_op jit(solution)/shard_map/ppermute | solution.py:341
  41.6 31.1 %collective-permute-start.8 = (bf16[256,1024]{1,0:T(8,128)(2,1)}, bf16[256,1024]{1,0:T(8,128)(2,1)}, u32[]{:S(2)}, u32[]{:S(2)}) collective-permute-start(bf16[256,1024]{1,0:T(8,128)(2,1)} %collective-permute-done.7), channel_id=1, source_target_pairs={{8,16},{12,20},{16,24},{20,28},{9,17},{13,21},{17,25},{21,29},{10,... | collective-permute-start | bytes 1572872 | tf_op jit(solution)/shard_map/ppermute | solution.py:341
  45.2 6.6 %collective-permute-start.9 = (bf16[128,1024]{1,0:T(8,128)(2,1)S(1)}, bf16[128,1024]{1,0:T(8,128)(2,1)S(1)}, u32[]{:S(2)}, u32[]{:S(2)}) collective-permute-start(bf16[128,1024]{1,0:T(8,128)(2,1)S(1)} %slice.32), channel_id=1, source_target_pairs={{0,2},{1,3},{2,0},{3,1},{4,6},{5,7},{6,4},{7,5},{8,10},{9,11},{10,... | collective-permute-start | bytes 786440 | tf_op jit(solution)/shard_map/ppermute | solution.py:349
  45.8 12.6 %collective-permute-start.10 = (bf16[128,1024]{1,0:T(8,128)(2,1)S(1)}, bf16[128,1024]{1,0:T(8,128)(2,1)S(1)}, u32[]{:S(2)}, u32[]{:S(2)}) collective-permute-start(bf16[128,1024]{1,0:T(8,128)(2,1)S(1)} %slice.33), channel_id=1, source_target_pairs={{0,1},{1,0},{2,3},{3,2},{4,5},{5,4},{6,7},{7,6},{8,9},{9,8},{10,11... | collective-permute-start | bytes 786440 | tf_op jit(solution)/shard_map/ppermute | solution.py:349
  52.5 22.1 %collective-permute-start.14 = (bf16[1344,256]{1,0:T(8,128)(2,1)}, bf16[1344,256]{1,0:T(8,128)(2,1)S(1)}, u32[]{:S(2)}, u32[]{:S(2)}) collective-permute-start(bf16[1344,256]{1,0:T(8,128)(2,1)} %pad_maximum_fusion), channel_id=1, source_target_pairs={{0,8},{4,12},{8,16},{12,20},{16,24},{20,28},{24,0},{28,4},{1,9},{5... | collective-permute-start | bytes 2064392 | tf_op jit(solution)/shard_map/ppermute | solution.py:337
  59.1 15.6 %collective-permute-start.11 = (bf16[256,1024]{1,0:T(8,128)(2,1)S(1)}, bf16[256,1024]{1,0:T(8,128)(2,1)}, u32[]{:S(2)}, u32[]{:S(2)}) collective-permute-start(bf16[256,1024]{1,0:T(8,128)(2,1)S(1)} %get-tuple-element.59.own_ref), channel_id=1, source_target_pairs={{0,1},{1,0},{2,3},{3,2},{4,5},{5,4},{6,7},{7,6},{8,9},{9,8},{10,11... | collective-permute-start | bytes 1572872 | tf_op jit(solution)/shard_map/ppermute | solution.py:349
  59.6 18.2 %collective-permute-start.12 = (bf16[256,1024]{1,0:T(8,128)(2,1)S(1)}, bf16[256,1024]{1,0:T(8,128)(2,1)}, u32[]{:S(2)}, u32[]{:S(2)}) collective-permute-start(bf16[256,1024]{1,0:T(8,128)(2,1)S(1)} %get-tuple-element.59.own_ref), channel_id=1, source_target_pairs={{0,2},{1,3},{2,0},{3,1},{4,6},{5,7},{6,4},{7,5},{8,10},{9,11},{10,... | collective-permute-start | bytes 1572872 | tf_op jit(solution)/shard_map/ppermute | solution.py:349
  72.7 18.1 %collective-permute-start.20 = (bf16[512,256]{1,0:T(8,128)(2,1)S(1)}, bf16[512,256]{1,0:T(8,128)(2,1)S(1)}, u32[]{:S(2)}, u32[]{:S(2)}) collective-permute-start(bf16[512,256]{1,0:T(8,128)(2,1)S(1)} %collective-permute-done.1.refs_1_), channel_id=1, source_target_pairs={{0,4},{4,0},{8,12},{12,8},{16,20},{20,16},{24,28},{28,24},{1,5},{5... | collective-permute-start | bytes 786440 | tf_op jit(solution)/shard_map/ppermute | solution.py:345
  75.6 8.8 %collective-permute-start.16 = (bf16[128,1024]{1,0:T(8,128)(2,1)S(1)}, bf16[128,1024]{1,0:T(8,128)(2,1)S(1)}, u32[]{:S(2)}, u32[]{:S(2)}) collective-permute-start(bf16[128,1024]{1,0:T(8,128)(2,1)S(1)} %slice.34), channel_id=1, source_target_pairs={{0,2},{1,3},{2,0},{3,1},{4,6},{5,7},{6,4},{7,5},{8,10},{9,11},{10,... | collective-permute-start | bytes 786440 | tf_op jit(solution)/shard_map/ppermute | solution.py:349
  77.9 17.0 %collective-permute-start.13 = (bf16[256,1024]{1,0:T(8,128)(2,1)}, bf16[256,1024]{1,0:T(8,128)(2,1)}, u32[]{:S(2)}, u32[]{:S(2)}) collective-permute-start(bf16[256,1024]{1,0:T(8,128)(2,1)} %broadcast_select_fusion.2.own_ref), channel_id=1, source_target_pairs={{8,0},{12,4},{16,24},{20,28},{9,1},{13,5},{17,25},{21,29},{10,2},{... | collective-permute-start | bytes 1572872 | tf_op jit(solution)/shard_map/ppermute | solution.py:441
  80.2 8.5 %collective-permute-start.17 = (bf16[128,1024]{1,0:T(8,128)(2,1)S(1)}, bf16[128,1024]{1,0:T(8,128)(2,1)S(1)}, u32[]{:S(2)}, u32[]{:S(2)}) collective-permute-start(bf16[128,1024]{1,0:T(8,128)(2,1)S(1)} %slice.35), channel_id=1, source_target_pairs={{0,1},{1,0},{2,3},{3,2},{4,5},{5,4},{6,7},{7,6},{8,9},{9,8},{10,11... | collective-permute-start | bytes 786440 | tf_op jit(solution)/shard_map/ppermute | solution.py:349
  82.6 38.9 %collective-permute-start.19 = (bf16[1344,256]{1,0:T(8,128)(2,1)}, bf16[1344,256]{1,0:T(8,128)(2,1)S(1)}, u32[]{:S(2)}, u32[]{:S(2)}) collective-permute-start(bf16[1344,256]{1,0:T(8,128)(2,1)} %pad_maximum_fusion.1), channel_id=1, source_target_pairs={{0,24},{4,28},{8,0},{12,4},{16,8},{20,12},{24,16},{28,20},{1,25},{... | collective-permute-start | bytes 2064392 | tf_op jit(solution)/shard_map/ppermute | solution.py:337
  85.1 36.6 %collective-permute-start.22 = (bf16[1344,256]{1,0:T(8,128)(2,1)S(1)}, bf16[1344,256]{1,0:T(8,128)(2,1)}, u32[]{:S(2)}, u32[]{:S(2)}) collective-permute-start(bf16[1344,256]{1,0:T(8,128)(2,1)S(1)} %collective-permute-done.14.refs_7_.refs_1_), channel_id=1, source_target_pairs={{0,4},{4,0},{8,12},{12,8},{16,20},{20,16},{24,28},{28,24},{1,5},{5... | collective-permute-start | bytes 2064392 | tf_op jit(solution)/shard_map/ppermute | solution.py:345
  89.4 32.4 %collective-permute-start.18 = (bf16[256,1024]{1,0:T(8,128)(2,1)}, bf16[256,1024]{1,0:T(8,128)(2,1)}, u32[]{:S(2)}, u32[]{:S(2)}) collective-permute-start(bf16[256,1024]{1,0:T(8,128)(2,1)} %broadcast_select_fusion.2.own_ref), channel_id=1, source_target_pairs={{0,1},{1,0},{2,3},{3,2},{4,5},{5,4},{6,7},{7,6},{8,9},{9,8},{10,11... | collective-permute-start | bytes 1572872 | tf_op jit(solution)/shard_map/ppermute | solution.py:349
  91.6 32.7 %collective-permute-start.24 = (bf16[256,1024]{1,0:T(8,128)(2,1)}, bf16[256,1024]{1,0:T(8,128)(2,1)}, u32[]{:S(2)}, u32[]{:S(2)}) collective-permute-start(bf16[256,1024]{1,0:T(8,128)(2,1)} %broadcast_select_fusion.2.own_ref), channel_id=1, source_target_pairs={{0,2},{1,3},{2,0},{3,1},{4,6},{5,7},{6,4},{7,5},{8,10},{9,11},{10,... | collective-permute-start | bytes 1572872 | tf_op jit(solution)/shard_map/ppermute | solution.py:349
  94.8 13.9 %collective-permute-start.21 = (bf16[512,256]{1,0:T(8,128)(2,1)}, bf16[512,256]{1,0:T(8,128)(2,1)}, u32[]{:S(2)}, u32[]{:S(2)}) collective-permute-start(bf16[512,256]{1,0:T(8,128)(2,1)} %collective-permute-done.2.refs_2_), channel_id=1, source_target_pairs={{0,4},{4,0},{8,12},{12,8},{16,20},{20,16},{24,28},{28,24},{1,5},{5... | collective-permute-start | bytes 786440 | tf_op jit(solution)/shard_map/ppermute | solution.py:345
  108.8 26.6 %collective-permute-start.31 = (bf16[512,256]{1,0:T(8,128)(2,1)S(1)}, bf16[512,256]{1,0:T(8,128)(2,1)S(1)}, u32[]{:S(2)}, u32[]{:S(2)}) collective-permute-start(bf16[512,256]{1,0:T(8,128)(2,1)S(1)} %dynamic-slice_bitcast_fusion.2), channel_id=1, source_target_pairs={{0,16},{4,20},{8,24},{12,28},{16,0},{20,4},{24,8},{28,12},{1,17},{... | collective-permute-start | bytes 786440 | tf_op jit(solution)/shard_map/ppermute | solution.py:337
  121.5 24.7 %collective-permute-start.27 = (bf16[1344,256]{1,0:T(8,128)(2,1)S(1)}, bf16[1344,256]{1,0:T(8,128)(2,1)S(1)}, u32[]{:S(2)}, u32[]{:S(2)}) collective-permute-start(bf16[1344,256]{1,0:T(8,128)(2,1)S(1)} %collective-permute-done.19.refs_8_.refs_3_), channel_id=1, source_target_pairs={{0,4},{4,0},{8,12},{12,8},{16,20},{20,16},{24,28},{28,24},{1,5},{5... | collective-permute-start | bytes 2064392 | tf_op jit(solution)/shard_map/ppermute | solution.py:345
  122.7 8.6 %collective-permute-start.23 = (bf16[128,1024]{1,0:T(8,128)(2,1)S(1)}, bf16[128,1024]{1,0:T(8,128)(2,1)S(1)}, u32[]{:S(2)}, u32[]{:S(2)}) collective-permute-start(bf16[128,1024]{1,0:T(8,128)(2,1)S(1)} %slice.36), channel_id=1, source_target_pairs={{0,2},{1,3},{2,0},{3,1},{4,6},{5,7},{6,4},{7,5},{8,10},{9,11},{10,... | collective-permute-start | bytes 786440 | tf_op jit(solution)/shard_map/ppermute | solution.py:349
  125.3 8.3 %collective-permute-start.25 = (bf16[128,1024]{1,0:T(8,128)(2,1)S(1)}, bf16[128,1024]{1,0:T(8,128)(2,1)S(1)}, u32[]{:S(2)}, u32[]{:S(2)}) collective-permute-start(bf16[128,1024]{1,0:T(8,128)(2,1)S(1)} %slice.37), channel_id=1, source_target_pairs={{0,1},{1,0},{2,3},{3,2},{4,5},{5,4},{6,7},{7,6},{8,9},{9,8},{10,11... | collective-permute-start | bytes 786440 | tf_op jit(solution)/shard_map/ppermute | solution.py:349
  133.6 21.3 %collective-permute-start.26 = (bf16[256,1024]{1,0:T(8,128)(2,1)S(1)}, bf16[256,1024]{1,0:T(8,128)(2,1)S(1)}, u32[]{:S(2)}, u32[]{:S(2)}) collective-permute-start(bf16[256,1024]{1,0:T(8,128)(2,1)S(1)} %broadcast_select_fusion.3.own_ref), channel_id=1, source_target_pairs={{0,1},{1,0},{2,3},{3,2},{4,5},{5,4},{6,7},{7,6},{8,9},{9,8},{10,11... | collective-permute-start | bytes 1572872 | tf_op jit(solution)/shard_map/ppermute | solution.py:349
  134.5 20.4 %collective-permute-start.28 = (bf16[256,1024]{1,0:T(8,128)(2,1)S(1)}, bf16[256,1024]{1,0:T(8,128)(2,1)S(1)}, u32[]{:S(2)}, u32[]{:S(2)}) collective-permute-start(bf16[256,1024]{1,0:T(8,128)(2,1)S(1)} %broadcast_select_fusion.3.own_ref), channel_id=1, source_target_pairs={{0,2},{1,3},{2,0},{3,1},{4,6},{5,7},{6,4},{7,5},{8,10},{9,11},{10,... | collective-permute-start | bytes 1572872 | tf_op jit(solution)/shard_map/ppermute | solution.py:349
  136.5 20.8 %collective-permute-start.33 = (bf16[832,256]{1,0:T(8,128)(2,1)S(1)}, bf16[832,256]{1,0:T(8,128)(2,1)S(1)}, u32[]{:S(2)}, u32[]{:S(2)}) collective-permute-start(bf16[832,256]{1,0:T(8,128)(2,1)S(1)} %pad_maximum_fusion.2), channel_id=1, source_target_pairs={{0,16},{4,20},{8,24},{12,28},{16,0},{20,4},{24,8},{28,12},{1,17},{... | collective-permute-start | bytes 1277960 | tf_op jit(solution)/shard_map/ppermute | solution.py:337
  136.7 20.7 %collective-permute-start.32 = (bf16[512,256]{1,0:T(8,128)(2,1)S(1)}, bf16[512,256]{1,0:T(8,128)(2,1)S(1)}, u32[]{:S(2)}, u32[]{:S(2)}) collective-permute-start(bf16[512,256]{1,0:T(8,128)(2,1)S(1)} %collective-permute-done.31.refs_0_), channel_id=1, source_target_pairs={{0,4},{4,0},{8,12},{12,8},{16,20},{20,16},{24,28},{28,24},{1,5},{5... | collective-permute-start | bytes 786440 | tf_op jit(solution)/shard_map/ppermute | solution.py:345
  154.9 8.8 %collective-permute-start.29 = (bf16[128,1024]{1,0:T(8,128)(2,1)S(1)}, bf16[128,1024]{1,0:T(8,128)(2,1)S(1)}, u32[]{:S(2)}, u32[]{:S(2)}) collective-permute-start(bf16[128,1024]{1,0:T(8,128)(2,1)S(1)} %slice.38), channel_id=1, source_target_pairs={{0,2},{1,3},{2,0},{3,1},{4,6},{5,7},{6,4},{7,5},{8,10},{9,11},{10,... | collective-permute-start | bytes 786440 | tf_op jit(solution)/shard_map/ppermute | solution.py:349
  156.2 8.6 %collective-permute-start.30 = (bf16[128,1024]{1,0:T(8,128)(2,1)S(1)}, bf16[128,1024]{1,0:T(8,128)(2,1)S(1)}, u32[]{:S(2)}, u32[]{:S(2)}) collective-permute-start(bf16[128,1024]{1,0:T(8,128)(2,1)S(1)} %slice.39), channel_id=1, source_target_pairs={{0,1},{1,0},{2,3},{3,2},{4,5},{5,4},{6,7},{7,6},{8,9},{9,8},{10,11... | collective-permute-start | bytes 786440 | tf_op jit(solution)/shard_map/ppermute | solution.py:349
  164.7 8.9 %collective-permute-start.34 = (bf16[832,256]{1,0:T(8,128)(2,1)S(1)}, bf16[832,256]{1,0:T(8,128)(2,1)S(1)}, u32[]{:S(2)}, u32[]{:S(2)}) collective-permute-start(bf16[832,256]{1,0:T(8,128)(2,1)S(1)} %collective-permute-done.33.refs_2_.refs_0_), channel_id=1, source_target_pairs={{0,4},{4,0},{8,12},{12,8},{16,20},{20,16},{24,28},{28,24},{1,5},{5... | collective-permute-start | bytes 1277960 | tf_op jit(solution)/shard_map/ppermute | solution.py:345
  164.7 26.0 %collective-permute-start.39 = (bf16[512,256]{1,0:T(8,128)(2,1)S(1)}, bf16[512,256]{1,0:T(8,128)(2,1)S(1)}, u32[]{:S(2)}, u32[]{:S(2)}) collective-permute-start(bf16[512,256]{1,0:T(8,128)(2,1)S(1)} %get-tuple-element.95), channel_id=1, source_target_pairs={{0,16},{4,20},{8,24},{12,28},{16,0},{20,4},{24,8},{28,12},{1,17},{... | collective-permute-start | bytes 786440 | tf_op jit(solution)/shard_map/ppermute | solution.py:337
  176.1 1.4 collective-permute-start.35
  176.4 1.3 collective-permute-start.36
  176.6 1.3 collective-permute-start.37
  176.9 1.3 collective-permute-start.38
  190.7 1.6 collective-permute-start.40
  193.6 2.0 collective-permute-start.41
  197.5 12.7 %collective-permute-start.42 = (bf16[256,256]{1,0:T(8,128)(2,1)S(1)}, bf16[256,256]{1,0:T(8,128)(2,1)S(1)}, u32[]{:S(2)}, u32[]{:S(2)}) collective-permute-start(bf16[256,256]{1,0:T(8,128)(2,1)S(1)} %mix.3), channel_id=1, source_target_pairs={{0,16},{4,20},{8,24},{12,28},{16,0},{20,4},{24,8},{28,12},{1,17},{... | collective-permute-start | bytes 393224 | tf_op jit(solution)/shard_map/ppermute | solution.py:337
  201.0 11.3 %collective-permute-start.43 = (bf16[256,256]{1,0:T(8,128)(2,1)S(1)}, bf16[256,256]{1,0:T(8,128)(2,1)S(1)}, u32[]{:S(2)}, u32[]{:S(2)}) collective-permute-start(bf16[256,256]{1,0:T(8,128)(2,1)S(1)} %get-tuple-element.100), channel_id=1, source_target_pairs={{0,8},{4,12},{8,16},{12,20},{16,24},{20,28},{24,0},{28,4},{1,9},{5... | collective-permute-start | bytes 393224 | tf_op jit(solution)/shard_map/ppermute | solution.py:337
  203.3 9.0 %collective-permute-start.44 = (bf16[256,256]{1,0:T(8,128)(2,1)S(1)}, bf16[256,256]{1,0:T(8,128)(2,1)S(1)}, u32[]{:S(2)}, u32[]{:S(2)}) collective-permute-start(bf16[256,256]{1,0:T(8,128)(2,1)S(1)} %get-tuple-element.102), channel_id=1, source_target_pairs={{0,24},{4,28},{8,0},{12,4},{16,8},{20,12},{24,16},{28,20},{1,25},{... | collective-permute-start | bytes 393224 | tf_op jit(solution)/shard_map/ppermute | solution.py:337
  (38 other events, 203.0 us)

commit v8 on v5

--- a/solution.py
+++ b/solution.py
@@ -179,10 +179,10 @@
     return functools.reduce(op, [s[:, i : i + LANES] for i in range(0, full, LANES)]), rest
 
 
-def weigh_kernel(place_ref, q_ref, ck_ref, *refs):
+def weigh_kernel(blocks, place_ref, q_ref, ck_ref, *refs):
     z, core = place_ref[1], place_ref[2]
     zs, rows, cols = q_ref.shape
-    k_refs, ks_refs, (old_ref, new_ref, sum_ref, k_ref, ks_ref, scratch) = refs[:zs], refs[zs : 2 * zs], refs[2 * zs :]
+    k_refs, ks_refs, (old_ref, new_ref, sum_ref, k_ref, ks_ref, scratch) = refs[:zs], refs[zs : 2 * zs], refs[-6:]
     for j in range(zs):
         k_ref[j], ks_ref[j] = k_refs[j][...], ks_refs[j][...]
     crow = ck_ref.shape[0]
@@ -192,7 +192,7 @@
     causal = col <= row
     slab = [lax.rem(z + zs - b, zs) for b in range(zs)]
 
-    for block in range(zs):
+    for block in blocks:
         for h in range(cols // HEAD):
             hcol = slice(h * HEAD, (h + 1) * HEAD)
             query = q_ref[slab[block], :, hcol]
@@ -230,12 +230,13 @@
             sum_ref[block, h] = jnp.broadcast_to(total, (rows, HEAD))
 
 
-def weigh(place, q, k, k_sib, ck):
+def weigh(blocks, place, q, k, k_sib, ck, into=()):
     zs, rows, cols = q.shape
     heads, crow = cols // HEAD, ck.shape[0]
     return pl.pallas_call(
-        weigh_kernel,
-        in_specs=[SMEM] + [VMEM] * (2 + 2 * zs),
+        functools.partial(weigh_kernel, blocks),
+        in_specs=[SMEM] + [VMEM] * (2 + 2 * zs + len(into)),
+        input_output_aliases={3 + 2 * zs + i: i for i in range(len(into))},
         out_specs=[VMEM] * 3,
         out_shape=[
             jax.ShapeDtypeStruct((zs, heads, rows, crow), BF16),
@@ -247,7 +248,7 @@
         compiler_params=pltpu.CompilerParams(vmem_limit_bytes=14 * MIB),
         cost_estimate=BRIEF,
         name="weigh",
-    )(place, q, ck, *k, *k_sib)
+    )(place, q, ck, *k, *k_sib, *into)
 
 
 def mix_kernel(shifts, place_ref, old_ref, new_ref, sum_ref, v_ref, vs_ref, cv_ref, *outs):
@@ -312,12 +313,17 @@
 
 
 def join_kernel(place_ref, *refs):
-    pieces, out_ref = refs[:-1], refs[-1]
+    pieces, (out_ref, sems) = refs[:-2], refs[-2:]
     zs = len(pieces)
     cols = pieces[0].shape[1]
+    copies = []
     for r, piece in enumerate(pieces):
-        at = lax.rem(place_ref[1] + zs - r, zs) * cols
-        out_ref[:, pl.ds(pl.multiple_of(at, cols), cols)] = piece[...]
+        at = pl.multiple_of(lax.rem(place_ref[1] + zs - r, zs) * cols, cols)
+        copies.append(pltpu.make_async_copy(piece, out_ref.at[:, pl.ds(at, cols)], sems.at[r]))
+    for copy in copies:
+        copy.start()
+    for copy in copies:
+        copy.wait()
 
 
 def join(place, pieces):
@@ -326,8 +332,9 @@
     return pl.pallas_call(
         join_kernel,
         in_specs=[SMEM] + [VMEM] * len(pieces),
-        out_specs=whole(out),
+        out_specs=pl.BlockSpec(memory_space=pl.ANY),
         out_shape=jax.ShapeDtypeStruct(out, BF16),
+        scratch_shapes=[pltpu.SemaphoreType.DMA((len(pieces),))],
         name="join",
     )(place, *pieces)
 
@@ -392,13 +399,13 @@
             kind, steps = item[:-1], int(item[-1])
             value = parcel(kind, steps, *acts[: int(n >= 2)])
         if n >= 2:
-            value = after(value, sent[n - 2])
+            value = after(value, sent[n - {"kvc3": 1, "kc2": 1}.get(item, 2)])
         sent.append(shift_z(value, steps, zs))
         if item == "acts":
             acts.append(sent[-1])
         else:
             here[item] = sent[-1]
-    late = ["kc2", "v2"]
+    late = ["q2", "kc2", "v2"]
     there = {item: swap_core(here[item], zs) for item in here if item not in late}
 
     pace = [[], ["kvc1"], ["kvc3"], []]
@@ -432,16 +439,20 @@
         diag1 = swap_chan(from_y[half:], 1)
         normed = norm(place, j, zs, own, from_x, from_y, diag0, diag1, gain4, normed)
 
-    there["kc2"] = swap_core(after(here["kc2"], there["q2"], diag0, diag1), zs)
+    there["q2"] = swap_core(after(here["q2"], diag0, diag1), zs)
+    there["kc2"] = swap_core(after(here["kc2"], diag0, diag1), zs)
     q_sum, k_sum, v_sum = project_early(every[last:], sums)
     (q,) = project_last("q2", q_sum)
     kept = sum(sides("kvc0", "kvc1", "kc2", "kvc3"), [])
     ck, cv = pack(kept, [depth if i % zs == 2 else 2 * depth for i in range(2 * zs)], crow)
     k = project_last("kc2", k_sum, q, ck, apart=True)
-    weights = weigh(place, q, k, [swap_core(slab, zs) for slab in k], ck)
+    k_sib = [swap_core(slab, zs) for slab in k]
+    weights = weigh((3, 0), place, q, k, k_sib, ck)
     there["v2"] = swap_core(after(here["v2"], weights[2]), zs)
-    (v,) = project_last("v2", v_sum)
+    weights = weigh((1,), place, q, k, k_sib, ck, weights)
+    (v,) = project_last("v2", v_sum, weights[2])
     v_sib = swap_core(v, zs)
+    weights = weigh((2,), place, q, k, k_sib, ck, weights)
     pieces, out = {}, None
     for shifts, wait in (((2,), ()), ((1, 3), ()), ((0,), (2,))):
         ready = v if out is None else after(v, out[0], *[pieces[r] for r in wait])

time: 189 us -> 184 us (0.974)
  starting transfers between devices: 53.8 us -> 38 us
  waiting for transfers between devices: 72.5 us -> 80.6 us
  Pallas kernels: 46.8 us -> 49 us
    ppermute x13, starting transfers between devices: 32.2 us -> 14.1 us  [shift_z(): return lax.ppermute(value, 'seq', pairs)]
    ppermute x16, waiting for transfers between devices: 16 us -> 23.4 us  [swap_chan(): return lax.ppermute(value, 'chan', [(c, c ^ bit) for c in range(4)])]
    ppermute x13, waiting for transfers between devices: 49.1 us -> 54.6 us  [shift_z(): return lax.ppermute(value, 'seq', pairs)]
    ppermute x14, waiting for transfers between devices: 7.38 us -> 2.59 us  [swap_core(): lax.ppermute(value, 'seq', [(2 * a + k, 2 * a + 1 - k) for a in range(zs)...]
    pallas_call x1 -> x3, Pallas kernels: 12.3 us -> 14.1 us  [weigh(): pl.pallas_call(functools.partial(weigh_kernel, blocks), in_specs=[SMEM] +...]
    unnamed x58 -> x62, local copies, waits for them, and re-layouts: 7.49 us -> 8.18 us
  transfers between devices with their start and end apart: 44 -> 44, of which waited for: 22 -> 25; matrix products, arithmetic and copies ran while one was open for 3% -> 3% of each run, Pallas kernels for 22% -> 24%
where the time goes in v8:
time: 184 us
  waiting for transfers between devices  80.6 us (44%)
  Pallas kernels  49 us (27%)
  starting transfers between devices  38 us (21%)
  local copies, waits for them, and re-layouts  13.1 us (7%)
  other arithmetic  2.46 us (1%)
    ppermute x13, waiting for transfers between devices, shift_z(): return lax.ppermute(value, 'seq', pairs)  54.6 us
    ppermute x16, waiting for transfers between devices, swap_chan(): return lax.ppermute(value, 'chan', [(c, c ^ bit) for c in range(4)])  23.4 us
    ppermute x16, starting transfers between devices, swap_chan(): return lax.ppermute(value, 'chan', [(c, c ^ bit) for c in range(4)])  18.2 us
    pallas_call x3, Pallas kernels, weigh(): pl.pallas_call(functools.partial(weigh_kernel, blocks), in_specs=[SMEM] +...  14.1 us
    ppermute x13, starting transfers between devices, shift_z(): return lax.ppermute(value, 'seq', pairs)  14.1 us
    pallas_call x5, Pallas kernels, project(): pl.pallas_call(functools.partial(project_kernel, shifts, slabs, parts, zs...  11.1 us
    pallas_call x4, Pallas kernels, norm(): pl.pallas_call(functools.partial(norm_kernel, j), in_specs=[SMEM] + [VMEM...  8.95 us
    unnamed x62, local copies, waits for them, and re-layouts  8.18 us
  transfers between devices with their start and end apart: 44, of which 25 were waited for; matrix products, arithmetic and copies ran while one was open for 3% of the time, Pallas kernels for 24%

profile of v8, /device:TPU:0, one launch (start us, length us, event | category | flops | bytes accessed | tf_op | source)
XLA Modules:
  0.0 183.8 jit_solution(5767069071742342488)
XLA Ops:
  1.2 2.4 %collective-permute-start = (bf16[128,1024]{1,0:T(8,128)(2,1)S(1)}, bf16[128,1024]{1,0:T(8,128)(2,1)S(1)}, u32[]{:S(2)}, u32[]{:S(2)}) collective-permute-start(bf16[128,1024]{1,0:T(8,128)(2,1)S(1)} %fusion), channel_id=1, source_target_pairs={{0,4},{4,8},{8,12},{12,16},{16,20},{20,24},{24,28},{1,5},{5,9},{9,... | collective-permute-start | bytes 786440 | tf_op jit(solution)/shard_map/ppermute | solution.py:388
  3.7 1.9 %dynamic-slice_bitcast_fusion.10 = (bf16[512,256]{1,0:T(8,128)(2,1)}, bf16[512,256]{1,0:T(8,128)(2,1)}) fusion(bf16[512,3,1024]{2,0,1:T(8,128)(2,1)} %param.11, s32[]{:T(128)S(6)} %select_n.80, s32[]{:T(128)S(6)} %select_n.78), kind=kLoop, calls=%fused_computation.16 | loop fusion | bytes 1048584 | tf_op jit(solution)/shard_map/squeeze | solution.py:378
  5.5 4.6 %collective-permute-start.5 = (bf16[512,256]{1,0:T(8,128)(2,1)}, bf16[512,256]{1,0:T(8,128)(2,1)S(1)}, u32[]{:S(2)}, u32[]{:S(2)}) collective-permute-start(bf16[512,256]{1,0:T(8,128)(2,1)} %get-tuple-element.115), channel_id=1, source_target_pairs={{0,24},{4,28},{8,0},{12,4},{16,8},{20,12},{24,16},{28,20},{1,25},{... | collective-permute-start | bytes 786440 | tf_op jit(solution)/shard_map/ppermute | solution.py:344
  10.3 6.0 %hyena_filters.1.own_ref = bf16[256,1024]{1,0:T(8,128)(2,1)S(1)} custom-call(bf16[3,256,1024]{2,1,0:T(8,128)(2,1)S(1)} %bitcast.33, bf16[128,1024]{1,0:T(8,128)(2,1)S(1)} %pad_select_fusion.halo_ref, f32[64,128]{1,0:T(8,128)S(1)} %copy-done.16), custom_call_target="tpu_custom_call" | custom-call | flops 1 | bytes 1 | tf_op jit(solution)/shard_map/hyena_filters/pallas_call | solution.py:80
  18.0 5.0 %collective-permute-done.1.refs_1_ = bf16[512,256]{1,0:T(8,128)(2,1)} collective-permute-done((bf16[512,256]{1,0:T(8,128)(2,1)}, bf16[512,256]{1,0:T(8,128)(2,1)}, u32[]{:S(2)}, u32[]{:S(2)}) %collective-permute-start.1) | collective-permute-done | bytes 262176 | tf_op jit(solution)/shard_map/ppermute | solution.py:344
  23.0 1.5 collective-permute-start.6
  24.5 1.5 collective-permute-start.8
  27.3 1.2 dynamic-slice_bitcast_fusion
  29.5 1.4 collective-permute-start.13
  30.9 6.5 %collective-permute-done.6.x_ref = bf16[256,1024]{1,0:T(8,128)(2,1)S(1)} collective-permute-done((bf16[256,1024]{1,0:T(8,128)(2,1)S(1)}, bf16[256,1024]{1,0:T(8,128)(2,1)S(1)}, u32[]{:S(2)}, u32[]{:S(2)}) %collective-permute-start.6) | collective-permute-done | bytes 524320 | tf_op jit(solution)/shard_map/ppermute | solution.py:352
  37.4 1.6 collective-permute-start.7
  39.0 1.6 collective-permute-start.9
  40.7 2.8 %collective-permute-done.2.own_ref = bf16[256,1024]{1,0:T(8,128)(2,1)} collective-permute-done((bf16[256,1024]{1,0:T(8,128)(2,1)S(1)}, bf16[256,1024]{1,0:T(8,128)(2,1)}, u32[]{:S(2)}, u32[]{:S(2)}) %collective-permute-start.2) | collective-permute-done | bytes 524320 | tf_op jit(solution)/shard_map/ppermute | solution.py:344
  43.5 2.0 %collective-permute-done.7.d0_ref = bf16[128,1024]{1,0:T(8,128)(2,1)S(1)} collective-permute-done((bf16[128,1024]{1,0:T(8,128)(2,1)S(1)}, bf16[128,1024]{1,0:T(8,128)(2,1)S(1)}, u32[]{:S(2)}, u32[]{:S(2)}) %collective-permute-start.7) | collective-permute-done | bytes 262176 | tf_op jit(solution)/shard_map/ppermute | solution.py:352
  48.6 1.3 collective-permute-start.10
  54.7 1.9 %norm.4.rest_0_ = bf16[4,4,256,1024]{3,2,1,0:T(8,128)(2,1)S(1)} custom-call(s32[3]{0:T(128)S(1)} %pad_add_fusion.place_ref, bf16[256,1024]{1,0:T(8,128)(2,1)S(1)} %hyena_filters.1.own_ref, bf16[256,1024]{1,0:T(8,128)(2,1)S(1)} %copy-done.2, bf16[256,1024]{1,0:T(8,128)(2,1)S(1)} %copy-done.4, bf16[128,1024]{1,0:T(8,128)(2,1)S(1)} %copy-done.12, ...), custom_call_target="tpu_custom_call" | custom-call | flops 1 | bytes 1 | tf_op jit(solution)/shard_map/norm/pallas_call | solution.py:119
  56.6 1.5 collective-permute-done.13.refs_7_.refs_1_
  58.1 2.0 %collective-permute-done.15.y_ref = bf16[256,1024]{1,0:T(8,128)(2,1)S(1)} collective-permute-done((bf16[256,1024]{1,0:T(8,128)(2,1)}, bf16[256,1024]{1,0:T(8,128)(2,1)S(1)}, u32[]{:S(2)}, u32[]{:S(2)}) %collective-permute-start.15) | collective-permute-done | bytes 524320 | tf_op jit(solution)/shard_map/ppermute | solution.py:352
  60.2 1.6 collective-permute-start.16
  62.7 1.3 collective-permute-start.14
  64.1 4.4 %collective-permute-done.3.own_ref = bf16[256,1024]{1,0:T(8,128)(2,1)} collective-permute-done((bf16[256,1024]{1,0:T(8,128)(2,1)}, bf16[256,1024]{1,0:T(8,128)(2,1)}, u32[]{:S(2)}, u32[]{:S(2)}) %collective-permute-start.3) | collective-permute-done | bytes 524320 | tf_op jit(solution)/shard_map/ppermute | solution.py:344
  71.4 1.5 collective-permute-done.18.refs_4_
  73.6 2.6 %norm.5.rest_0_ = bf16[4,4,256,1024]{3,2,1,0:T(8,128)(2,1)S(1)} custom-call(s32[3]{0:T(128)S(1)} %pad_add_fusion.place_ref, bf16[256,1024]{1,0:T(8,128)(2,1)} %collective-permute-done.2.own_ref, bf16[256,1024]{1,0:T(8,128)(2,1)} %collective-permute-done.10.x_ref, ...), custom_call_target="tpu_custom_call", output_to_operand_aliasing={{}: (7, {})} | custom-call | flops 1 | bytes 1 | tf_op jit(solution)/shard_map/norm/pallas_call | solution.py:119
  76.2 19.9 %collective-permute-done.20.refs_8_.refs_3_ = bf16[1344,256]{1,0:T(8,128)(2,1)S(1)} collective-permute-done((bf16[1344,256]{1,0:T(8,128)(2,1)S(1)}, bf16[1344,256]{1,0:T(8,128)(2,1)S(1)}, u32[]{:S(2)}, u32[]{:S(2)}) %collective-permute-start.20) | collective-permute-done | bytes 688160 | tf_op jit(solution)/shard_map/ppermute | solution.py:344
  97.8 5.5 %collective-permute-done.23.d1_ref = bf16[128,1024]{1,0:T(8,128)(2,1)S(1)} collective-permute-done((bf16[128,1024]{1,0:T(8,128)(2,1)S(1)}, bf16[128,1024]{1,0:T(8,128)(2,1)S(1)}, u32[]{:S(2)}, u32[]{:S(2)}) %collective-permute-start.23) | collective-permute-done | bytes 262176 | tf_op jit(solution)/shard_map/ppermute | solution.py:352
  103.3 2.6 %collective-permute-done.21.d0_ref = bf16[128,1024]{1,0:T(8,128)(2,1)S(1)} collective-permute-done((bf16[128,1024]{1,0:T(8,128)(2,1)S(1)}, bf16[128,1024]{1,0:T(8,128)(2,1)S(1)}, u32[]{:S(2)}, u32[]{:S(2)}) %collective-permute-start.21) | collective-permute-done | bytes 262176 | tf_op jit(solution)/shard_map/ppermute | solution.py:352
  105.8 1.5 collective-permute-start.24
  107.4 15.0 %collective-permute-done.30.refs_0_ = bf16[512,256]{1,0:T(8,128)(2,1)S(1)} collective-permute-done((bf16[512,256]{1,0:T(8,128)(2,1)S(1)}, bf16[512,256]{1,0:T(8,128)(2,1)S(1)}, u32[]{:S(2)}, u32[]{:S(2)}) %collective-permute-start.30) | collective-permute-done | bytes 262176 | tf_op jit(solution)/shard_map/ppermute | solution.py:344
  122.4 2.4 %norm.6.normed_ref.rest_0_ = bf16[4,4,256,1024]{3,2,1,0:T(8,128)(2,1)S(1)} custom-call(s32[3]{0:T(128)S(1)} %pad_add_fusion.place_ref, bf16[256,1024]{1,0:T(8,128)(2,1)} %collective-permute-done.3.own_ref, bf16[256,1024]{1,0:T(8,128)(2,1)S(1)} %collective-permute-done.17.x_ref, ...), custom_call_target="tpu_custom_call", output_to_operand_aliasing={{}: (7, {})} | custom-call | flops 1 | bytes 1 | tf_op jit(solution)/shard_map/norm/pallas_call | solution.py:119
  124.8 4.9 %project.5 = (f32[4,256,256]{2,1,0:T(8,128)S(1)}, f32[4,256,256]{2,1,0:T(8,128)S(1)}, f32[4,256,256]{2,1,0:T(8,128)S(1)}) custom-call(s32[3]{0:T(128)S(1)} %pad_add_fusion.place_ref, bf16[4,4,256,1024]{3,2,1,0:T(8,128)(2,1)S(1)} %norm.6.normed_ref.rest_0_, bf16[512,256]{1,0:T(8,128)(2,1)S(1)} %get-tuple-element.112.refs_0_, ...), custom_call_target="tpu_custom_call" | custom-call | flops 1 | bytes 1 | tf_op jit(solution)/shard_map/project/pallas_call | solution.py:161
  130.4 1.7 collective-permute-start.28
  133.3 3.0 %collective-permute-done.29.d1_ref = bf16[128,1024]{1,0:T(8,128)(2,1)S(1)} collective-permute-done((bf16[128,1024]{1,0:T(8,128)(2,1)S(1)}, bf16[128,1024]{1,0:T(8,128)(2,1)S(1)}, u32[]{:S(2)}, u32[]{:S(2)}) %collective-permute-start.29) | collective-permute-done | bytes 262176 | tf_op jit(solution)/shard_map/ppermute | solution.py:352
  137.4 2.9 %collective-permute-start.38 = (bf16[512,256]{1,0:T(8,128)(2,1)S(1)}, bf16[512,256]{1,0:T(8,128)(2,1)S(1)}, u32[]{:S(2)}, u32[]{:S(2)}) collective-permute-start(bf16[512,256]{1,0:T(8,128)(2,1)S(1)} %copy-done.25), channel_id=1, source_target_pairs={{0,16},{4,20},{8,24},{12,28},{16,0},{20,4},{24,8},{28,12},{1,17},{... | collective-permute-start | bytes 786440 | tf_op jit(solution)/shard_map/ppermute | solution.py:344
  140.3 2.1 %norm.7.normed_ref = bf16[4,4,256,1024]{3,2,1,0:T(8,128)(2,1)S(1)} custom-call(s32[3]{0:T(128)S(1)} %pad_add_fusion.place_ref, bf16[256,1024]{1,0:T(8,128)(2,1)S(1)} %collective-permute-done.4.own_ref, bf16[256,1024]{1,0:T(8,128)(2,1)S(1)} %collective-permute-done.24.x_ref, ...), custom_call_target="tpu_custom_call", output_to_operand_aliasing={{}: (7, {})} | custom-call | flops 1 | bytes 1 | tf_op jit(solution)/shard_map/norm/pallas_call | solution.py:119
  142.4 2.4 %project.6 = (f32[4,256,256]{2,1,0:T(8,128)S(1)}, f32[4,256,256]{2,1,0:T(8,128)S(1)}, f32[4,256,256]{2,1,0:T(8,128)S(1)}) custom-call(s32[3]{0:T(128)S(1)} %pad_add_fusion.place_ref, bf16[4,4,256,1024]{3,2,1,0:T(8,128)(2,1)S(1)} %norm.7.normed_ref, ...), custom_call_target="tpu_custom_call", output_to_operand_aliasing={{0}: (14, {}), {1}: (15, {}), {2}: (16, {})} | custom-call | flops 1 | bytes 1 | tf_op jit(solution)/shard_map/project/pallas_call | solution.py:161
  144.8 1.3 project.7.q_ref
  146.2 1.3 project.8
  149.6 6.3 %weigh.3 = (bf16[4,2,256,1216]{3,2,1,0:T(8,128)(2,1)S(1)}, bf16[4,2,4,256,512]{4,3,2,1,0:T(8,128)(2,1)S(1)}, f32[4,2,256,128]{3,2,1,0:T(8,128)S(1)}) custom-call(s32[3]{0:T(128)S(1)} %pad_add_fusion.place_ref, bf16[4,256,256]{2,1,0:T(8,128)(2,1)S(1)} %project.7.q_ref, bf16[1216,256]{1,0:T(8,128)(2,1)S(1)} %get-tuple-element.80.ck_ref, ...), custom_call_target="tpu_custom_call" | custom-call | flops 1 | bytes 1 | tf_op jit(solution)/shard_map/weigh/pallas_call | solution.py:236
  156.2 3.5 %weigh.4 = (bf16[4,2,256,1216]{3,2,1,0:T(8,128)(2,1)S(1)}, bf16[4,2,4,256,512]{4,3,2,1,0:T(8,128)(2,1)S(1)}, f32[4,2,256,128]{3,2,1,0:T(8,128)S(1)}) custom-call(s32[3]{0:T(128)S(1)} %pad_add_fusion.place_ref, bf16[4,256,256]{2,1,0:T(8,128)(2,1)S(1)} %project.7.q_ref, ...), custom_call_target="tpu_custom_call", output_to_operand_aliasing={{0}: (11, {}), {1}: (12, {}), {2}: (13, {})} | custom-call | flops 1 | bytes 1 | tf_op jit(solution)/shard_map/weigh/pallas_call | solution.py:236
  159.8 1.3 project.9.v_ref
  161.3 4.4 %weigh.5 = (bf16[4,2,256,1216]{3,2,1,0:T(8,128)(2,1)S(1)}, bf16[4,2,4,256,512]{4,3,2,1,0:T(8,128)(2,1)S(1)}, f32[4,2,256,128]{3,2,1,0:T(8,128)S(1)}) custom-call(s32[3]{0:T(128)S(1)} %pad_add_fusion.place_ref, bf16[4,256,256]{2,1,0:T(8,128)(2,1)S(1)} %project.7.q_ref, ...), custom_call_target="tpu_custom_call", output_to_operand_aliasing={{0}: (11, {}), {1}: (12, {}), {2}: (13, {})} | custom-call | flops 1 | bytes 1 | tf_op jit(solution)/shard_map/weigh/pallas_call | solution.py:236
  165.7 2.0 %mix.3 = bf16[256,256]{1,0:T(8,128)(2,1)S(1)} custom-call(s32[3]{0:T(128)S(1)} %pad_add_fusion.place_ref, bf16[4,2,256,1216]{3,2,1,0:T(8,128)(2,1)S(1)} %get-tuple-element.93.old_ref, bf16[4,2,4,256,512]{4,3,2,1,0:T(8,128)(2,1)S(1)} %get-tuple-element.94.new_ref, f32[4,2,256,128]{3,2,1,0:T(8,128)S(1)} %get-tuple-element.95.sum_ref, ...), custom_call_target="tpu_custom_call" | custom-call | flops 1 | bytes 1 | tf_op jit(solution)/shard_map/mix/pallas_call | solution.py:281
  167.8 3.4 %mix.4 = (bf16[256,256]{1,0:T(8,128)(2,1)S(1)}, bf16[256,256]{1,0:T(8,128)(2,1)S(1)}) custom-call(s32[3]{0:T(128)S(1)} %pad_add_fusion.place_ref, bf16[4,2,256,1216]{3,2,1,0:T(8,128)(2,1)S(1)} %get-tuple-element.93.old_ref, bf16[4,2,4,256,512]{4,3,2,1,0:T(8,128)(2,1)S(1)} %get-tuple-element.94.new_ref, f32[4,2,256,128]{3,2,1,0:T(8,128)S(1)} %get-tuple-element.95.sum_ref, ...), custom_call_target="tpu_custom_call" | custom-call | flops 1 | bytes 1 | tf_op jit(solution)/shard_map/mix/pallas_call | solution.py:281
  171.7 3.3 %collective-permute-start.43 = (bf16[256,256]{1,0:T(8,128)(2,1)S(1)}, bf16[256,256]{1,0:T(8,128)(2,1)S(1)}, u32[]{:S(2)}, u32[]{:S(2)}) collective-permute-start(bf16[256,256]{1,0:T(8,128)(2,1)S(1)} %get-tuple-element.104), channel_id=1, source_target_pairs={{0,24},{4,28},{8,0},{12,4},{16,8},{20,12},{24,16},{28,20},{1,25},{... | collective-permute-start | bytes 393224 | tf_op jit(solution)/shard_map/ppermute | solution.py:344
  175.4 1.4 mix.5.refs_0_
  177.5 1.9 %collective-permute-done.42.refs_1_ = bf16[256,256]{1,0:T(8,128)(2,1)S(1)} collective-permute-done((bf16[256,256]{1,0:T(8,128)(2,1)S(1)}, bf16[256,256]{1,0:T(8,128)(2,1)S(1)}, u32[]{:S(2)}, u32[]{:S(2)}) %collective-permute-start.42) | collective-permute-done | bytes 131104 | tf_op jit(solution)/shard_map/ppermute | solution.py:344
  179.3 1.7 collective-permute-done.43.refs_3_
  181.6 1.9 %join.1 = bf16[256,1024]{1,0:T(8,128)(2,1)} custom-call(s32[3]{0:T(128)} %copy-done.15, bf16[256,256]{1,0:T(8,128)(2,1)} %copy-done.9, bf16[256,256]{1,0:T(8,128)(2,1)} %copy-done.29, bf16[256,256]{1,0:T(8,128)(2,1)} %copy-done.28, bf16[256,256]{1,0:T(8,128)(2,1)} %copy-done.30), custom_call_target="tpu_custom_call" | custom-call | tf_op jit(solution)/shard_map/join/pallas_call | solution.py:332
  (138 shorter events, 27.8 us)
Async XLA Ops:
  1.2 8.9 %collective-permute-start = (bf16[128,1024]{1,0:T(8,128)(2,1)S(1)}, bf16[128,1024]{1,0:T(8,128)(2,1)S(1)}, u32[]{:S(2)}, u32[]{:S(2)}) collective-permute-start(bf16[128,1024]{1,0:T(8,128)(2,1)S(1)} %fusion), channel_id=1, source_target_pairs={{0,4},{4,8},{8,12},{12,16},{16,20},{20,24},{24,28},{1,5},{5,9},{9,... | collective-permute-start | bytes 786440 | tf_op jit(solution)/shard_map/ppermute | solution.py:388
  5.5 11.7 %collective-permute-start.5 = (bf16[512,256]{1,0:T(8,128)(2,1)}, bf16[512,256]{1,0:T(8,128)(2,1)S(1)}, u32[]{:S(2)}, u32[]{:S(2)}) collective-permute-start(bf16[512,256]{1,0:T(8,128)(2,1)} %get-tuple-element.115), channel_id=1, source_target_pairs={{0,24},{4,28},{8,0},{12,4},{16,8},{20,12},{24,16},{28,20},{1,25},{... | collective-permute-start | bytes 786440 | tf_op jit(solution)/shard_map/ppermute | solution.py:344
  10.1 12.9 %collective-permute-start.1 = (bf16[512,256]{1,0:T(8,128)(2,1)}, bf16[512,256]{1,0:T(8,128)(2,1)}, u32[]{:S(2)}, u32[]{:S(2)}) collective-permute-start(bf16[512,256]{1,0:T(8,128)(2,1)} %get-tuple-element.116), channel_id=1, source_target_pairs={{0,8},{4,12},{8,16},{12,20},{16,24},{20,28},{24,0},{28,4},{1,9},{5... | collective-permute-start | bytes 786440 | tf_op jit(solution)/shard_map/ppermute | solution.py:344
  23.0 14.3 %collective-permute-start.6 = (bf16[256,1024]{1,0:T(8,128)(2,1)S(1)}, bf16[256,1024]{1,0:T(8,128)(2,1)S(1)}, u32[]{:S(2)}, u32[]{:S(2)}) collective-permute-start(bf16[256,1024]{1,0:T(8,128)(2,1)S(1)} %hyena_filters.1.own_ref), channel_id=1, source_target_pairs={{0,1},{1,0},{2,3},{3,2},{4,5},{5,4},{6,7},{7,6},{8,9},{9,8},{10,11... | collective-permute-start | bytes 1572872 | tf_op jit(solution)/shard_map/ppermute | solution.py:352
  24.5 14.4 %collective-permute-start.8 = (bf16[256,1024]{1,0:T(8,128)(2,1)S(1)}, bf16[256,1024]{1,0:T(8,128)(2,1)S(1)}, u32[]{:S(2)}, u32[]{:S(2)}) collective-permute-start(bf16[256,1024]{1,0:T(8,128)(2,1)S(1)} %hyena_filters.1.own_ref), channel_id=1, source_target_pairs={{0,2},{1,3},{2,0},{3,1},{4,6},{5,7},{6,4},{7,5},{8,10},{9,11},{10,... | collective-permute-start | bytes 1572872 | tf_op jit(solution)/shard_map/ppermute | solution.py:352
  26.8 16.7 %collective-permute-start.2 = (bf16[256,1024]{1,0:T(8,128)(2,1)S(1)}, bf16[256,1024]{1,0:T(8,128)(2,1)}, u32[]{:S(2)}, u32[]{:S(2)}) collective-permute-start(bf16[256,1024]{1,0:T(8,128)(2,1)S(1)} %hyena_filters.1.own_ref), channel_id=1, source_target_pairs={{0,8},{4,12},{8,16},{12,20},{16,24},{20,28},{24,0},{28,4},{1,9},{5... | collective-permute-start | bytes 1572872 | tf_op jit(solution)/shard_map/ppermute | solution.py:344
  29.5 21.2 %copy-start.10 = (f32[4096]{0:T(1024)S(1)}, f32[4096]{0:T(1024)}, u32[]{:S(2)}) copy-start(f32[4096]{0:T(1024)} %param.10) | copy-start | bytes 49156
  29.5 28.6 %collective-permute-start.13 = (bf16[1344,256]{1,0:T(8,128)(2,1)}, bf16[1344,256]{1,0:T(8,128)(2,1)S(1)}, u32[]{:S(2)}, u32[]{:S(2)}) collective-permute-start(bf16[1344,256]{1,0:T(8,128)(2,1)} %pad_maximum_fusion.1), channel_id=1, source_target_pairs={{0,8},{4,12},{8,16},{12,20},{16,24},{20,28},{24,0},{28,4},{1,9},{5... | collective-permute-start | bytes 2064392 | tf_op jit(solution)/shard_map/ppermute | solution.py:344
  37.4 8.1 %collective-permute-start.7 = (bf16[128,1024]{1,0:T(8,128)(2,1)S(1)}, bf16[128,1024]{1,0:T(8,128)(2,1)S(1)}, u32[]{:S(2)}, u32[]{:S(2)}) collective-permute-start(bf16[128,1024]{1,0:T(8,128)(2,1)S(1)} %slice.42), channel_id=1, source_target_pairs={{0,2},{1,3},{2,0},{3,1},{4,6},{5,7},{6,4},{7,5},{8,10},{9,11},{10,... | collective-permute-start | bytes 786440 | tf_op jit(solution)/shard_map/ppermute | solution.py:352
  39.0 7.8 %collective-permute-start.9 = (bf16[128,1024]{1,0:T(8,128)(2,1)S(1)}, bf16[128,1024]{1,0:T(8,128)(2,1)S(1)}, u32[]{:S(2)}, u32[]{:S(2)}) collective-permute-start(bf16[128,1024]{1,0:T(8,128)(2,1)S(1)} %slice.43), channel_id=1, source_target_pairs={{0,1},{1,0},{2,3},{3,2},{4,5},{5,4},{6,7},{7,6},{8,9},{9,8},{10,11... | collective-permute-start | bytes 786440 | tf_op jit(solution)/shard_map/ppermute | solution.py:352
  40.6 17.5 %collective-permute-start.11 = (bf16[1344,256]{1,0:T(8,128)(2,1)S(1)}, bf16[1344,256]{1,0:T(8,128)(2,1)S(1)}, u32[]{:S(2)}, u32[]{:S(2)}) collective-permute-start(bf16[1344,256]{1,0:T(8,128)(2,1)S(1)} %pad_maximum_fusion.refs_6_.refs_0_), channel_id=1, source_target_pairs={{0,4},{4,0},{8,12},{12,8},{16,20},{20,16},{24,28},{28,24},{1,5},{5... | collective-permute-start | bytes 2064392 | tf_op jit(solution)/shard_map/ppermute | solution.py:348
  43.5 6.4 %collective-permute-start.12 = (bf16[512,256]{1,0:T(8,128)(2,1)S(1)}, bf16[512,256]{1,0:T(8,128)(2,1)S(1)}, u32[]{:S(2)}, u32[]{:S(2)}) collective-permute-start(bf16[512,256]{1,0:T(8,128)(2,1)S(1)} %get-tuple-element.112.refs_0_), channel_id=1, source_target_pairs={{0,4},{4,0},{8,12},{12,8},{16,20},{20,16},{24,28},{28,24},{1,5},{5... | collective-permute-start | bytes 786440 | tf_op jit(solution)/shard_map/ppermute | solution.py:348
  47.5 12.7 %collective-permute-start.15 = (bf16[256,1024]{1,0:T(8,128)(2,1)}, bf16[256,1024]{1,0:T(8,128)(2,1)S(1)}, u32[]{:S(2)}, u32[]{:S(2)}) collective-permute-start(bf16[256,1024]{1,0:T(8,128)(2,1)} %collective-permute-done.2.own_ref), channel_id=1, source_target_pairs={{0,2},{1,3},{2,0},{3,1},{4,6},{5,7},{6,4},{7,5},{8,10},{9,11},{10,... | collective-permute-start | bytes 1572872 | tf_op jit(solution)/shard_map/ppermute | solution.py:352
  48.6 13.2 %collective-permute-start.10 = (bf16[256,1024]{1,0:T(8,128)(2,1)}, bf16[256,1024]{1,0:T(8,128)(2,1)}, u32[]{:S(2)}, u32[]{:S(2)}) collective-permute-start(bf16[256,1024]{1,0:T(8,128)(2,1)} %collective-permute-done.2.own_ref), channel_id=1, source_target_pairs={{0,1},{1,0},{2,3},{3,2},{4,5},{5,4},{6,7},{7,6},{8,9},{9,8},{10,11... | collective-permute-start | bytes 1572872 | tf_op jit(solution)/shard_map/ppermute | solution.py:352
  50.6 17.9 %collective-permute-start.3 = (bf16[256,1024]{1,0:T(8,128)(2,1)}, bf16[256,1024]{1,0:T(8,128)(2,1)}, u32[]{:S(2)}, u32[]{:S(2)}) collective-permute-start(bf16[256,1024]{1,0:T(8,128)(2,1)} %collective-permute-done.2.own_ref), channel_id=1, source_target_pairs={{0,8},{4,12},{8,16},{12,20},{16,24},{20,28},{24,0},{28,4},{1,9},{5... | collective-permute-start | bytes 1572872 | tf_op jit(solution)/shard_map/ppermute | solution.py:344
  50.7 124.7 %copy-start.15 = (s32[3]{0:T(128)}, s32[3]{0:T(128)S(1)}, u32[]{:S(2)}) copy-start(s32[3]{0:T(128)S(1)} %pad_add_fusion.place_ref) | copy-start | bytes 40
  60.2 8.4 %collective-permute-start.16 = (bf16[128,1024]{1,0:T(8,128)(2,1)S(1)}, bf16[128,1024]{1,0:T(8,128)(2,1)S(1)}, u32[]{:S(2)}, u32[]{:S(2)}) collective-permute-start(bf16[128,1024]{1,0:T(8,128)(2,1)S(1)} %slice.35), channel_id=1, source_target_pairs={{0,1},{1,0},{2,3},{3,2},{4,5},{5,4},{6,7},{7,6},{8,9},{9,8},{10,11... | collective-permute-start | bytes 786440 | tf_op jit(solution)/shard_map/ppermute | solution.py:352
  62.7 6.4 %collective-permute-start.14 = (bf16[128,1024]{1,0:T(8,128)(2,1)S(1)}, bf16[128,1024]{1,0:T(8,128)(2,1)S(1)}, u32[]{:S(2)}, u32[]{:S(2)}) collective-permute-start(bf16[128,1024]{1,0:T(8,128)(2,1)S(1)} %slice.34), channel_id=1, source_target_pairs={{0,2},{1,3},{2,0},{3,1},{4,6},{5,7},{6,4},{7,5},{8,10},{9,11},{10,... | collective-permute-start | bytes 786440 | tf_op jit(solution)/shard_map/ppermute | solution.py:352
  64.0 43.3 %copy-start.26 = (bf16[512,256]{1,0:T(8,128)(2,1)S(1)}, bf16[512,256]{1,0:T(8,128)(2,1)}, u32[]{:S(2)}) copy-start(bf16[512,256]{1,0:T(8,128)(2,1)} %get-tuple-element.75) | copy-start | bytes 786436
  64.1 43.3 %copy-start.18 = (bf16[512,256]{1,0:T(8,128)(2,1)S(1)}, bf16[512,256]{1,0:T(8,128)(2,1)}, u32[]{:S(2)}) copy-start(bf16[512,256]{1,0:T(8,128)(2,1)} %get-tuple-element.106) | copy-start | bytes 786436
  68.5 27.6 %collective-permute-start.20 = (bf16[1344,256]{1,0:T(8,128)(2,1)S(1)}, bf16[1344,256]{1,0:T(8,128)(2,1)S(1)}, u32[]{:S(2)}, u32[]{:S(2)}) collective-permute-start(bf16[1344,256]{1,0:T(8,128)(2,1)S(1)} %pad_maximum_fusion.2), channel_id=1, source_target_pairs={{0,24},{4,28},{8,0},{12,4},{16,8},{20,12},{24,16},{28,20},{1,25},{... | collective-permute-start | bytes 2064392 | tf_op jit(solution)/shard_map/ppermute | solution.py:344
  69.1 26.9 %collective-permute-start.22 = (bf16[256,1024]{1,0:T(8,128)(2,1)}, bf16[256,1024]{1,0:T(8,128)(2,1)S(1)}, u32[]{:S(2)}, u32[]{:S(2)}) collective-permute-start(bf16[256,1024]{1,0:T(8,128)(2,1)} %collective-permute-done.3.own_ref), channel_id=1, source_target_pairs={{0,2},{1,3},{2,0},{3,1},{4,6},{5,7},{6,4},{7,5},{8,10},{9,11},{10,... | collective-permute-start | bytes 1572872 | tf_op jit(solution)/shard_map/ppermute | solution.py:352
  70.3 26.3 %collective-permute-start.17 = (bf16[256,1024]{1,0:T(8,128)(2,1)}, bf16[256,1024]{1,0:T(8,128)(2,1)S(1)}, u32[]{:S(2)}, u32[]{:S(2)}) collective-permute-start(bf16[256,1024]{1,0:T(8,128)(2,1)} %collective-permute-done.3.own_ref), channel_id=1, source_target_pairs={{0,1},{1,0},{2,3},{3,2},{4,5},{5,4},{6,7},{7,6},{8,9},{9,8},{10,11... | collective-permute-start | bytes 1572872 | tf_op jit(solution)/shard_map/ppermute | solution.py:352
  70.9 2.1 %collective-permute-start.18 = (bf16[512,256]{1,0:T(8,128)(2,1)}, bf16[512,256]{1,0:T(8,128)(2,1)S(1)}, u32[]{:S(2)}, u32[]{:S(2)}) collective-permute-start(bf16[512,256]{1,0:T(8,128)(2,1)} %collective-permute-done.1.refs_1_), channel_id=1, source_target_pairs={{0,4},{4,0},{8,12},{12,8},{16,20},{20,16},{24,28},{28,24},{1,5},{5... | collective-permute-start | bytes 786440 | tf_op jit(solution)/shard_map/ppermute | solution.py:348
  70.9 5.3 %collective-permute-start.19 = (bf16[512,256]{1,0:T(8,128)(2,1)S(1)}, bf16[512,256]{1,0:T(8,128)(2,1)S(1)}, u32[]{:S(2)}, u32[]{:S(2)}) collective-permute-start(bf16[512,256]{1,0:T(8,128)(2,1)S(1)} %copy-done.6), channel_id=1, source_target_pairs={{0,4},{4,0},{8,12},{12,8},{16,20},{20,16},{24,28},{28,24},{1,5},{5... | collective-permute-start | bytes 786440 | tf_op jit(solution)/shard_map/ppermute | solution.py:348
  72.9 24.8 %collective-permute-start.4 = (bf16[256,1024]{1,0:T(8,128)(2,1)}, bf16[256,1024]{1,0:T(8,128)(2,1)S(1)}, u32[]{:S(2)}, u32[]{:S(2)}) collective-permute-start(bf16[256,1024]{1,0:T(8,128)(2,1)} %collective-permute-done.3.own_ref), channel_id=1, source_target_pairs={{0,8},{4,12},{8,16},{12,20},{16,24},{20,28},{24,0},{28,4},{1,9},{5... | collective-permute-start | bytes 1572872 | tf_op jit(solution)/shard_map/ppermute | solution.py:344
  96.1 7.2 %collective-permute-start.23 = (bf16[128,1024]{1,0:T(8,128)(2,1)S(1)}, bf16[128,1024]{1,0:T(8,128)(2,1)S(1)}, u32[]{:S(2)}, u32[]{:S(2)}) collective-permute-start(bf16[128,1024]{1,0:T(8,128)(2,1)S(1)} %slice.37), channel_id=1, source_target_pairs={{0,1},{1,0},{2,3},{3,2},{4,5},{5,4},{6,7},{7,6},{8,9},{9,8},{10,11... | collective-permute-start | bytes 786440 | tf_op jit(solution)/shard_map/ppermute | solution.py:352
  96.7 9.1 %collective-permute-start.21 = (bf16[128,1024]{1,0:T(8,128)(2,1)S(1)}, bf16[128,1024]{1,0:T(8,128)(2,1)S(1)}, u32[]{:S(2)}, u32[]{:S(2)}) collective-permute-start(bf16[128,1024]{1,0:T(8,128)(2,1)S(1)} %slice.36), channel_id=1, source_target_pairs={{0,2},{1,3},{2,0},{3,1},{4,6},{5,7},{6,4},{7,5},{8,10},{9,11},{10,... | collective-permute-start | bytes 786440 | tf_op jit(solution)/shard_map/ppermute | solution.py:352
  97.3 27.5 %collective-permute-start.25 = (bf16[1344,256]{1,0:T(8,128)(2,1)S(1)}, bf16[1344,256]{1,0:T(8,128)(2,1)S(1)}, u32[]{:S(2)}, u32[]{:S(2)}) collective-permute-start(bf16[1344,256]{1,0:T(8,128)(2,1)S(1)} %collective-permute-done.13.refs_7_.refs_1_), channel_id=1, source_target_pairs={{0,4},{4,0},{8,12},{12,8},{16,20},{20,16},{24,28},{28,24},{1,5},{5... | collective-permute-start | bytes 2064392 | tf_op jit(solution)/shard_map/ppermute | solution.py:348
  97.3 27.5 %collective-permute-start.26 = (bf16[1344,256]{1,0:T(8,128)(2,1)S(1)}, bf16[1344,256]{1,0:T(8,128)(2,1)S(1)}, u32[]{:S(2)}, u32[]{:S(2)}) collective-permute-start(bf16[1344,256]{1,0:T(8,128)(2,1)S(1)} %collective-permute-done.20.refs_8_.refs_3_), channel_id=1, source_target_pairs={{0,4},{4,0},{8,12},{12,8},{16,20},{20,16},{24,28},{28,24},{1,5},{5... | collective-permute-start | bytes 2064392 | tf_op jit(solution)/shard_map/ppermute | solution.py:348
  105.8 23.9 %collective-permute-start.27 = (bf16[256,1024]{1,0:T(8,128)(2,1)S(1)}, bf16[256,1024]{1,0:T(8,128)(2,1)S(1)}, u32[]{:S(2)}, u32[]{:S(2)}) collective-permute-start(bf16[256,1024]{1,0:T(8,128)(2,1)S(1)} %collective-permute-done.4.own_ref), channel_id=1, source_target_pairs={{0,2},{1,3},{2,0},{3,1},{4,6},{5,7},{6,4},{7,5},{8,10},{9,11},{10,... | collective-permute-start | bytes 1572872 | tf_op jit(solution)/shard_map/ppermute | solution.py:352
  105.8 24.6 %collective-permute-start.24 = (bf16[256,1024]{1,0:T(8,128)(2,1)S(1)}, bf16[256,1024]{1,0:T(8,128)(2,1)S(1)}, u32[]{:S(2)}, u32[]{:S(2)}) collective-permute-start(bf16[256,1024]{1,0:T(8,128)(2,1)S(1)} %collective-permute-done.4.own_ref), channel_id=1, source_target_pairs={{0,1},{1,0},{2,3},{3,2},{4,5},{5,4},{6,7},{7,6},{8,9},{9,8},{10,11... | collective-permute-start | bytes 1572872 | tf_op jit(solution)/shard_map/ppermute | solution.py:352
  107.3 15.0 %collective-permute-start.30 = (bf16[512,256]{1,0:T(8,128)(2,1)S(1)}, bf16[512,256]{1,0:T(8,128)(2,1)S(1)}, u32[]{:S(2)}, u32[]{:S(2)}) collective-permute-start(bf16[512,256]{1,0:T(8,128)(2,1)S(1)} %copy-done.26), channel_id=1, source_target_pairs={{0,16},{4,20},{8,24},{12,28},{16,0},{20,4},{24,8},{28,12},{1,17},{... | collective-permute-start | bytes 786440 | tf_op jit(solution)/shard_map/ppermute | solution.py:344
  122.4 10.9 %collective-permute-start.32 = (bf16[832,256]{1,0:T(8,128)(2,1)S(1)}, bf16[832,256]{1,0:T(8,128)(2,1)S(1)}, u32[]{:S(2)}, u32[]{:S(2)}) collective-permute-start(bf16[832,256]{1,0:T(8,128)(2,1)S(1)} %pad_maximum_fusion.3), channel_id=1, source_target_pairs={{0,16},{4,20},{8,24},{12,28},{16,0},{20,4},{24,8},{28,12},{1,17},{... | collective-permute-start | bytes 1277960 | tf_op jit(solution)/shard_map/ppermute | solution.py:344
  129.8 6.4 %collective-permute-start.29 = (bf16[128,1024]{1,0:T(8,128)(2,1)S(1)}, bf16[128,1024]{1,0:T(8,128)(2,1)S(1)}, u32[]{:S(2)}, u32[]{:S(2)}) collective-permute-start(bf16[128,1024]{1,0:T(8,128)(2,1)S(1)} %slice.39), channel_id=1, source_target_pairs={{0,1},{1,0},{2,3},{3,2},{4,5},{5,4},{6,7},{7,6},{8,9},{9,8},{10,11... | collective-permute-start | bytes 786440 | tf_op jit(solution)/shard_map/ppermute | solution.py:352
  130.4 6.4 %collective-permute-start.28 = (bf16[128,1024]{1,0:T(8,128)(2,1)S(1)}, bf16[128,1024]{1,0:T(8,128)(2,1)S(1)}, u32[]{:S(2)}, u32[]{:S(2)}) collective-permute-start(bf16[128,1024]{1,0:T(8,128)(2,1)S(1)} %slice.38), channel_id=1, source_target_pairs={{0,2},{1,3},{2,0},{3,1},{4,6},{5,7},{6,4},{7,5},{8,10},{9,11},{10,... | collective-permute-start | bytes 786440 | tf_op jit(solution)/shard_map/ppermute | solution.py:352
  136.9 9.2 %collective-permute-start.33 = (bf16[832,256]{1,0:T(8,128)(2,1)S(1)}, bf16[832,256]{1,0:T(8,128)(2,1)S(1)}, u32[]{:S(2)}, u32[]{:S(2)}) collective-permute-start(bf16[832,256]{1,0:T(8,128)(2,1)S(1)} %collective-permute-done.32.refs_2_.refs_0_), channel_id=1, source_target_pairs={{0,4},{4,0},{8,12},{12,8},{16,20},{20,16},{24,28},{28,24},{1,5},{5... | collective-permute-start | bytes 1277960 | tf_op jit(solution)/shard_map/ppermute | solution.py:348
  136.9 7.9 %collective-permute-start.31 = (bf16[512,256]{1,0:T(8,128)(2,1)S(1)}, bf16[512,256]{1,0:T(8,128)(2,1)S(1)}, u32[]{:S(2)}, u32[]{:S(2)}) collective-permute-start(bf16[512,256]{1,0:T(8,128)(2,1)S(1)} %collective-permute-done.30.refs_0_), channel_id=1, source_target_pairs={{0,4},{4,0},{8,12},{12,8},{16,20},{20,16},{24,28},{28,24},{1,5},{5... | collective-permute-start | bytes 786440 | tf_op jit(solution)/shard_map/ppermute | solution.py:348
  137.4 18.4 %collective-permute-start.38 = (bf16[512,256]{1,0:T(8,128)(2,1)S(1)}, bf16[512,256]{1,0:T(8,128)(2,1)S(1)}, u32[]{:S(2)}, u32[]{:S(2)}) collective-permute-start(bf16[512,256]{1,0:T(8,128)(2,1)S(1)} %copy-done.25), channel_id=1, source_target_pairs={{0,16},{4,20},{8,24},{12,28},{16,0},{20,4},{24,8},{28,12},{1,17},{... | collective-permute-start | bytes 786440 | tf_op jit(solution)/shard_map/ppermute | solution.py:344
  147.5 1.4 collective-permute-start.34
  147.5 1.5 collective-permute-start.35
  148.0 1.3 collective-permute-start.36
  148.1 1.5 collective-permute-start.37
  155.9 3.9 %collective-permute-start.39 = (bf16[512,256]{1,0:T(8,128)(2,1)S(1)}, bf16[512,256]{1,0:T(8,128)(2,1)S(1)}, u32[]{:S(2)}, u32[]{:S(2)}) collective-permute-start(bf16[512,256]{1,0:T(8,128)(2,1)S(1)} %collective-permute-done.38.refs_0_), channel_id=1, source_target_pairs={{0,4},{4,0},{8,12},{12,8},{16,20},{20,16},{24,28},{28,24},{1,5},{5... | collective-permute-start | bytes 786440 | tf_op jit(solution)/shard_map/ppermute | solution.py:348
  161.0 4.6 %collective-permute-start.40 = (bf16[4,256,256]{2,1,0:T(8,128)(2,1)S(1)}, bf16[4,256,256]{2,1,0:T(8,128)(2,1)S(1)}, u32[]{:S(2)}, u32[]{:S(2)}) collective-permute-start(bf16[4,256,256]{2,1,0:T(8,128)(2,1)S(1)} %project.9.v_ref), channel_id=1, source_target_pairs={{0,4},{4,0},{8,12},{12,8},{16,20},{20,16},{24,28},{28,24},{1,5},{5... | collective-permute-start | bytes 1572872 | tf_op jit(solution)/shard_map/ppermute | solution.py:348
  167.7 7.7 %collective-permute-start.41 = (bf16[256,256]{1,0:T(8,128)(2,1)S(1)}, bf16[256,256]{1,0:T(8,128)(2,1)S(1)}, u32[]{:S(2)}, u32[]{:S(2)}) collective-permute-start(bf16[256,256]{1,0:T(8,128)(2,1)S(1)} %mix.3), channel_id=1, source_target_pairs={{0,16},{4,20},{8,24},{12,28},{16,0},{20,4},{24,8},{28,12},{1,17},{... | collective-permute-start | bytes 393224 | tf_op jit(solution)/shard_map/ppermute | solution.py:344
  171.1 8.2 %collective-permute-start.42 = (bf16[256,256]{1,0:T(8,128)(2,1)S(1)}, bf16[256,256]{1,0:T(8,128)(2,1)S(1)}, u32[]{:S(2)}, u32[]{:S(2)}) collective-permute-start(bf16[256,256]{1,0:T(8,128)(2,1)S(1)} %get-tuple-element.102), channel_id=1, source_target_pairs={{0,8},{4,12},{8,16},{12,20},{16,24},{20,28},{24,0},{28,4},{1,9},{5... | collective-permute-start | bytes 393224 | tf_op jit(solution)/shard_map/ppermute | solution.py:344
  171.7 9.3 %collective-permute-start.43 = (bf16[256,256]{1,0:T(8,128)(2,1)S(1)}, bf16[256,256]{1,0:T(8,128)(2,1)S(1)}, u32[]{:S(2)}, u32[]{:S(2)}) collective-permute-start(bf16[256,256]{1,0:T(8,128)(2,1)S(1)} %get-tuple-element.104), channel_id=1, source_target_pairs={{0,24},{4,28},{8,0},{12,4},{16,8},{20,12},{24,16},{28,20},{1,25},{... | collective-permute-start | bytes 393224 | tf_op jit(solution)/shard_map/ppermute | solution.py:344
  (27 other events, 186.4 us)

commit v9 on v3

--- a/solution.py
+++ b/solution.py
@@ -374,7 +374,7 @@
     there = {item: swap_core(here[item], zs) for item in here if item not in late}
 
     pace = [[], ["kvc1"], ["kvc3"], ["q2"]]
-    swapped = [[], ["kvc0", "q0"], ["q1", "q3"], ["kvc1"]]
+    swapped = [[], ["kvc0", "q0"], ["q1", "q3"], ["kvc1", "kvc3"]]
     gain4 = gain.reshape(4, 1, width)
     half = rows // 2
     normed, diag0, diag1 = None, None, None

time: 170 us -> 170 us (level)
  transfers between devices with their start and end apart: 41 -> 41, of which waited for: 20 -> 21; matrix products, arithmetic and copies ran while one was open for 4% -> 4% of each run, Pallas kernels for 20% -> 20%
where the time goes in v9:
time: 170 us
  waiting for transfers between devices  78.8 us (46%)
  Pallas kernels  40.1 us (24%)
  starting transfers between devices  36.3 us (21%)
  local copies, waits for them, and re-layouts  11.7 us (7%)
  other arithmetic  2.46 us (1%)
    ppermute x13, waiting for transfers between devices, shift_z(): return lax.ppermute(value, 'seq', pairs)  61.5 us
    ppermute x16, starting transfers between devices, swap_chan(): return lax.ppermute(value, 'chan', [(c, c ^ bit) for c in range(4)])  17.5 us
    ppermute x13, starting transfers between devices, shift_z(): return lax.ppermute(value, 'seq', pairs)  14.5 us
    pallas_call x3, Pallas kernels, attend(): pl.pallas_call(functools.partial(attend_kernel, shifts), in_specs=[SMEM]...  13.9 us
    ppermute x16, waiting for transfers between devices, swap_chan(): return lax.ppermute(value, 'chan', [(c, c ^ bit) for c in range(4)])  11.5 us
    pallas_call x4, Pallas kernels, project(): pl.pallas_call(functools.partial(project_kernel, shifts, zs, count), in_s...  9.85 us
    pallas_call x4, Pallas kernels, norm(): pl.pallas_call(functools.partial(norm_kernel, j), in_specs=[SMEM] + [VMEM...  8.27 us
    unnamed x62, local copies, waits for them, and re-layouts  6.76 us
  transfers between devices with their start and end apart: 41, of which 21 were waited for; matrix products, arithmetic and copies ran while one was open for 4% of the time, Pallas kernels for 20%

profile of v9, /device:TPU:0, one launch (start us, length us, event | category | flops | bytes accessed | tf_op | source)
XLA Modules:
  0.0 169.8 jit_solution(18371326427710002833)
XLA Ops:
  0.0 1.2 fusion
  1.2 2.4 %collective-permute-start = (bf16[128,1024]{1,0:T(8,128)(2,1)S(1)}, bf16[128,1024]{1,0:T(8,128)(2,1)S(1)}, u32[]{:S(2)}, u32[]{:S(2)}) collective-permute-start(bf16[128,1024]{1,0:T(8,128)(2,1)S(1)} %fusion), channel_id=1, source_target_pairs={{0,4},{4,8},{8,12},{12,16},{16,20},{20,24},{24,28},{1,5},{5,9},{9,... | collective-permute-start | bytes 786440 | tf_op jit(solution)/shard_map/ppermute | solution.py:353
  3.7 1.9 %dynamic-slice_bitcast_fusion.10 = (bf16[512,256]{1,0:T(8,128)(2,1)}, bf16[512,256]{1,0:T(8,128)(2,1)}) fusion(bf16[512,3,1024]{2,0,1:T(8,128)(2,1)} %param.11, s32[]{:T(128)S(6)} %select_n.80, s32[]{:T(128)S(6)} %select_n.78), kind=kLoop, calls=%fused_computation.16 | loop fusion | bytes 1048584 | tf_op jit(solution)/shard_map/squeeze | solution.py:343
  5.6 4.6 %collective-permute-start.5 = (bf16[512,256]{1,0:T(8,128)(2,1)}, bf16[512,256]{1,0:T(8,128)(2,1)S(1)}, u32[]{:S(2)}, u32[]{:S(2)}) collective-permute-start(bf16[512,256]{1,0:T(8,128)(2,1)} %get-tuple-element.77), channel_id=1, source_target_pairs={{0,24},{4,28},{8,0},{12,4},{16,8},{20,12},{24,16},{28,20},{1,25},{... | collective-permute-start | bytes 786440 | tf_op jit(solution)/shard_map/ppermute | solution.py:309
  10.3 6.0 %hyena_filters.1.own_ref = bf16[256,1024]{1,0:T(8,128)(2,1)S(1)} custom-call(bf16[3,256,1024]{2,1,0:T(8,128)(2,1)S(1)} %bitcast.33, bf16[128,1024]{1,0:T(8,128)(2,1)S(1)} %pad_select_fusion.halo_ref, f32[64,128]{1,0:T(8,128)S(1)} %copy-done.16), custom_call_target="tpu_custom_call" | custom-call | flops 1 | bytes 1 | tf_op jit(solution)/shard_map/hyena_filters/pallas_call | solution.py:80
  17.3 5.6 %collective-permute-done.1.refs_1_ = bf16[512,256]{1,0:T(8,128)(2,1)S(1)} collective-permute-done((bf16[512,256]{1,0:T(8,128)(2,1)}, bf16[512,256]{1,0:T(8,128)(2,1)S(1)}, u32[]{:S(2)}, u32[]{:S(2)}) %collective-permute-start.1) | collective-permute-done | bytes 262176 | tf_op jit(solution)/shard_map/ppermute | solution.py:309
  22.9 1.5 collective-permute-start.6
  24.4 1.5 collective-permute-start.8
  27.2 1.2 dynamic-slice_bitcast_fusion
  29.4 1.4 collective-permute-start.13
  30.7 6.5 %collective-permute-done.6.x_ref = bf16[256,1024]{1,0:T(8,128)(2,1)S(1)} collective-permute-done((bf16[256,1024]{1,0:T(8,128)(2,1)S(1)}, bf16[256,1024]{1,0:T(8,128)(2,1)S(1)}, u32[]{:S(2)}, u32[]{:S(2)}) %collective-permute-start.6) | collective-permute-done | bytes 524320 | tf_op jit(solution)/shard_map/ppermute | solution.py:317
  37.3 1.6 collective-permute-start.7
  38.9 1.6 collective-permute-start.9
  40.6 2.8 %collective-permute-done.2.own_ref = bf16[256,1024]{1,0:T(8,128)(2,1)} collective-permute-done((bf16[256,1024]{1,0:T(8,128)(2,1)S(1)}, bf16[256,1024]{1,0:T(8,128)(2,1)}, u32[]{:S(2)}, u32[]{:S(2)}) %collective-permute-start.2) | collective-permute-done | bytes 524320 | tf_op jit(solution)/shard_map/ppermute | solution.py:309
  43.4 2.0 %collective-permute-done.7.d0_ref = bf16[128,1024]{1,0:T(8,128)(2,1)S(1)} collective-permute-done((bf16[128,1024]{1,0:T(8,128)(2,1)S(1)}, bf16[128,1024]{1,0:T(8,128)(2,1)S(1)}, u32[]{:S(2)}, u32[]{:S(2)}) %collective-permute-start.7) | collective-permute-done | bytes 262176 | tf_op jit(solution)/shard_map/ppermute | solution.py:317
  47.4 1.1 collective-permute-start.15
  48.5 1.3 collective-permute-start.10
  49.8 1.7 collective-permute-done.12.refs_4_
  51.5 1.0 copy-done.2
  52.6 1.0 copy-done.4
  55.5 1.9 %norm.4.rest_0_ = bf16[4,4,256,1024]{3,2,1,0:T(8,128)(2,1)S(1)} custom-call(s32[3]{0:T(128)S(1)} %pad_add_fusion.place_ref, bf16[256,1024]{1,0:T(8,128)(2,1)S(1)} %hyena_filters.1.own_ref, bf16[256,1024]{1,0:T(8,128)(2,1)S(1)} %copy-done.2, bf16[256,1024]{1,0:T(8,128)(2,1)S(1)} %copy-done.4, bf16[128,1024]{1,0:T(8,128)(2,1)S(1)} %copy-done.12, ...), custom_call_target="tpu_custom_call" | custom-call | flops 1 | bytes 1 | tf_op jit(solution)/shard_map/norm/pallas_call | solution.py:119
  57.7 2.3 %collective-permute-done.15.y_ref = bf16[256,1024]{1,0:T(8,128)(2,1)S(1)} collective-permute-done((bf16[256,1024]{1,0:T(8,128)(2,1)}, bf16[256,1024]{1,0:T(8,128)(2,1)S(1)}, u32[]{:S(2)}, u32[]{:S(2)}) %collective-permute-start.15) | collective-permute-done | bytes 524320 | tf_op jit(solution)/shard_map/ppermute | solution.py:317
  60.1 1.6 collective-permute-start.16
  62.6 1.3 collective-permute-start.14
  65.0 4.0 %collective-permute-done.3.own_ref = bf16[256,1024]{1,0:T(8,128)(2,1)S(1)} collective-permute-done((bf16[256,1024]{1,0:T(8,128)(2,1)}, bf16[256,1024]{1,0:T(8,128)(2,1)S(1)}, u32[]{:S(2)}, u32[]{:S(2)}) %collective-permute-start.3) | collective-permute-done | bytes 524320 | tf_op jit(solution)/shard_map/ppermute | solution.py:309
  69.0 1.2 collective-permute-start.22
  72.8 2.6 %norm.5.rest_0_ = bf16[4,4,256,1024]{3,2,1,0:T(8,128)(2,1)S(1)} custom-call(s32[3]{0:T(128)S(1)} %pad_add_fusion.place_ref, bf16[256,1024]{1,0:T(8,128)(2,1)} %collective-permute-done.2.own_ref, bf16[256,1024]{1,0:T(8,128)(2,1)} %collective-permute-done.10.x_ref, ...), custom_call_target="tpu_custom_call", output_to_operand_aliasing={{}: (7, {})} | custom-call | flops 1 | bytes 1 | tf_op jit(solution)/shard_map/norm/pallas_call | solution.py:119
  75.4 8.4 %collective-permute-done.20.refs_3_.refs_2_ = bf16[1344,256]{1,0:T(8,128)(2,1)S(1)} collective-permute-done((bf16[1344,256]{1,0:T(8,128)(2,1)S(1)}, bf16[1344,256]{1,0:T(8,128)(2,1)S(1)}, u32[]{:S(2)}, u32[]{:S(2)}) %collective-permute-start.20) | collective-permute-done | bytes 688160 | tf_op jit(solution)/shard_map/ppermute | solution.py:309
  84.9 9.4 %collective-permute-done.4.own_ref = bf16[256,1024]{1,0:T(8,128)(2,1)S(1)} collective-permute-done((bf16[256,1024]{1,0:T(8,128)(2,1)S(1)}, bf16[256,1024]{1,0:T(8,128)(2,1)S(1)}, u32[]{:S(2)}, u32[]{:S(2)}) %collective-permute-start.4) | collective-permute-done | bytes 524320 | tf_op jit(solution)/shard_map/ppermute | solution.py:309
  95.5 2.9 %collective-permute-start.32 = (bf16[832,256]{1,0:T(8,128)(2,1)S(1)}, bf16[832,256]{1,0:T(8,128)(2,1)S(1)}, u32[]{:S(2)}, u32[]{:S(2)}) collective-permute-start(bf16[832,256]{1,0:T(8,128)(2,1)S(1)} %pad_maximum_fusion.3), channel_id=1, source_target_pairs={{0,16},{4,20},{8,24},{12,28},{16,0},{20,4},{24,8},{28,12},{1,17},{... | collective-permute-start | bytes 1277960 | tf_op jit(solution)/shard_map/ppermute | solution.py:309
  98.4 1.9 %norm.6.rest_0_ = bf16[4,4,256,1024]{3,2,1,0:T(8,128)(2,1)S(1)} custom-call(s32[3]{0:T(128)S(1)} %pad_add_fusion.place_ref, bf16[256,1024]{1,0:T(8,128)(2,1)S(1)} %collective-permute-done.3.own_ref, bf16[256,1024]{1,0:T(8,128)(2,1)S(1)} %collective-permute-done.17.x_ref, ...), custom_call_target="tpu_custom_call", output_to_operand_aliasing={{}: (7, {})} | custom-call | flops 1 | bytes 1 | tf_op jit(solution)/shard_map/norm/pallas_call | solution.py:119
  100.3 16.9 %collective-permute-done.27.refs_3_ = bf16[512,256]{1,0:T(8,128)(2,1)S(1)} collective-permute-done((bf16[512,256]{1,0:T(8,128)(2,1)S(1)}, bf16[512,256]{1,0:T(8,128)(2,1)S(1)}, u32[]{:S(2)}, u32[]{:S(2)}) %collective-permute-start.27) | collective-permute-done | bytes 262176 | tf_op jit(solution)/shard_map/ppermute | solution.py:309
  118.0 1.6 collective-permute-start.29
  119.6 6.6 %collective-permute-done.32.refs_2_.refs_0_ = bf16[832,256]{1,0:T(8,128)(2,1)S(1)} collective-permute-done((bf16[832,256]{1,0:T(8,128)(2,1)S(1)}, bf16[832,256]{1,0:T(8,128)(2,1)S(1)}, u32[]{:S(2)}, u32[]{:S(2)}) %collective-permute-start.32) | collective-permute-done | bytes 426016 | tf_op jit(solution)/shard_map/ppermute | solution.py:309
  126.7 1.9 %norm.7.normed_ref = bf16[4,4,256,1024]{3,2,1,0:T(8,128)(2,1)S(1)} custom-call(s32[3]{0:T(128)S(1)} %pad_add_fusion.place_ref, bf16[256,1024]{1,0:T(8,128)(2,1)S(1)} %collective-permute-done.4.own_ref, bf16[256,1024]{1,0:T(8,128)(2,1)S(1)} %collective-permute-done.24.x_ref, ...), custom_call_target="tpu_custom_call", output_to_operand_aliasing={{}: (7, {})} | custom-call | flops 1 | bytes 1 | tf_op jit(solution)/shard_map/norm/pallas_call | solution.py:119
  128.6 4.0 %project.5 = (f32[4,256,256]{2,1,0:T(8,128)S(1)}, f32[4,256,256]{2,1,0:T(8,128)S(1)}) custom-call(s32[3]{0:T(128)S(1)} %pad_add_fusion.place_ref, bf16[4,4,256,1024]{3,2,1,0:T(8,128)(2,1)S(1)} %norm.7.normed_ref, bf16[1344,256]{1,0:T(8,128)(2,1)S(1)} %pad_maximum_fusion.refs_0_, bf16[1344,256]{1,0:T(8,128)(2,1)S(1)} %collective-permute-done.13.refs_1_, ...), custom_call_target="tpu_custom_call" | custom-call | flops 1 | bytes 1 | tf_op jit(solution)/shard_map/project/pallas_call | solution.py:155
  132.7 3.3 %project.4.q_ref = bf16[4,256,256]{2,1,0:T(8,128)(2,1)S(1)} custom-call(s32[3]{0:T(128)S(1)} %pad_add_fusion.place_ref, bf16[4,4,256,1024]{3,2,1,0:T(8,128)(2,1)S(1)} %norm.7.normed_ref, bf16[512,256]{1,0:T(8,128)(2,1)S(1)} %get-tuple-element.74.refs_0_, bf16[512,256]{1,0:T(8,128)(2,1)S(1)} %copy-done.10, bf16[512,256]{1,0:T(8,128)(2,1)S(1)} %copy-done.8, ...), custom_call_target="tpu_custom_call" | custom-call | flops 1 | bytes 1 | tf_op jit(solution)/shard_map/project/pallas_call | solution.py:155
  136.1 1.3 project.6.k_ref
  137.4 4.1 %collective-permute-done.34.refs_0_ = bf16[512,256]{1,0:T(8,128)(2,1)S(1)} collective-permute-done((bf16[512,256]{1,0:T(8,128)(2,1)S(1)}, bf16[512,256]{1,0:T(8,128)(2,1)S(1)}, u32[]{:S(2)}, u32[]{:S(2)}) %collective-permute-start.34) | collective-permute-done | bytes 262176 | tf_op jit(solution)/shard_map/ppermute | solution.py:309
  143.0 1.3 project.7.v_ref
  144.5 1.8 %collective-permute-done.37.vs_ref = bf16[4,256,256]{2,1,0:T(8,128)(2,1)S(1)} collective-permute-done((bf16[4,256,256]{2,1,0:T(8,128)(2,1)S(1)}, bf16[4,256,256]{2,1,0:T(8,128)(2,1)S(1)}, u32[]{:S(2)}, u32[]{:S(2)}) %collective-permute-start.37) | collective-permute-done | bytes 524320 | tf_op jit(solution)/shard_map/ppermute | solution.py:313
  146.2 3.9 %attend.3 = bf16[256,256]{1,0:T(8,128)(2,1)S(1)} custom-call(s32[3]{0:T(128)S(1)} %pad_add_fusion.place_ref, bf16[4,256,256]{2,1,0:T(8,128)(2,1)S(1)} %project.4.q_ref, bf16[4,256,256]{2,1,0:T(8,128)(2,1)S(1)} %project.6.k_ref, bf16[4,256,256]{2,1,0:T(8,128)(2,1)S(1)} %project.7.v_ref, bf16[4,256,256]{2,1,0:T(8,128)(2,1)S(1)} %collective-permute-done.36.ks_ref, ...), custom_call_target="tpu_custom_call" | custom-call | flops 1 | bytes 1 | tf_op jit(solution)/shard_map/attend/pallas_call | solution.py:248
  150.2 7.4 %attend.4 = (bf16[256,256]{1,0:T(8,128)(2,1)S(1)}, bf16[256,256]{1,0:T(8,128)(2,1)S(1)}) custom-call(s32[3]{0:T(128)S(1)} %pad_add_fusion.place_ref, bf16[4,256,256]{2,1,0:T(8,128)(2,1)S(1)} %project.4.q_ref, bf16[4,256,256]{2,1,0:T(8,128)(2,1)S(1)} %project.6.k_ref, bf16[4,256,256]{2,1,0:T(8,128)(2,1)S(1)} %project.7.v_ref, ...), custom_call_target="tpu_custom_call" | custom-call | flops 1 | bytes 1 | tf_op jit(solution)/shard_map/attend/pallas_call | solution.py:248
  157.7 3.8 %collective-permute-start.40 = (bf16[256,256]{1,0:T(8,128)(2,1)S(1)}, bf16[256,256]{1,0:T(8,128)(2,1)S(1)}, u32[]{:S(2)}, u32[]{:S(2)}) collective-permute-start(bf16[256,256]{1,0:T(8,128)(2,1)S(1)} %get-tuple-element.66), channel_id=1, source_target_pairs={{0,24},{4,28},{8,0},{12,4},{16,8},{20,12},{24,16},{28,20},{1,25},{... | collective-permute-start | bytes 393224 | tf_op jit(solution)/shard_map/ppermute | solution.py:309
  161.5 2.6 %attend.5.refs_0_ = bf16[256,256]{1,0:T(8,128)(2,1)S(1)} custom-call(s32[3]{0:T(128)S(1)} %pad_add_fusion.place_ref, bf16[4,256,256]{2,1,0:T(8,128)(2,1)S(1)} %project.4.q_ref, bf16[4,256,256]{2,1,0:T(8,128)(2,1)S(1)} %project.6.k_ref, bf16[4,256,256]{2,1,0:T(8,128)(2,1)S(1)} %project.7.v_ref, bf16[4,256,256]{2,1,0:T(8,128)(2,1)S(1)} %collective-permute-done.36.ks_ref, ...), custom_call_target="tpu_custom_call" | custom-call | flops 1 | bytes 1 | tf_op jit(solution)/shard_map/attend/pallas_call | solution.py:248
  164.8 1.1 collective-permute-done.39.refs_1_
  165.8 1.4 collective-permute-done.40.refs_3_
  167.8 2.0 %join.1 = bf16[256,1024]{1,0:T(8,128)(2,1)} custom-call(s32[3]{0:T(128)} %copy-done.15, bf16[256,256]{1,0:T(8,128)(2,1)} %copy-done.5, bf16[256,256]{1,0:T(8,128)(2,1)} %copy-done.29, bf16[256,256]{1,0:T(8,128)(2,1)} %copy-done.28, bf16[256,256]{1,0:T(8,128)(2,1)} %copy-done.30), custom_call_target="tpu_custom_call" | custom-call | tf_op jit(solution)/shard_map/join/pallas_call | solution.py:298
  (128 shorter events, 19.2 us)
Async XLA Ops:
  1.2 8.9 %collective-permute-start = (bf16[128,1024]{1,0:T(8,128)(2,1)S(1)}, bf16[128,1024]{1,0:T(8,128)(2,1)S(1)}, u32[]{:S(2)}, u32[]{:S(2)}) collective-permute-start(bf16[128,1024]{1,0:T(8,128)(2,1)S(1)} %fusion), channel_id=1, source_target_pairs={{0,4},{4,8},{8,12},{12,16},{16,20},{20,24},{24,28},{1,5},{5,9},{9,... | collective-permute-start | bytes 786440 | tf_op jit(solution)/shard_map/ppermute | solution.py:353
  5.6 11.7 %collective-permute-start.5 = (bf16[512,256]{1,0:T(8,128)(2,1)}, bf16[512,256]{1,0:T(8,128)(2,1)S(1)}, u32[]{:S(2)}, u32[]{:S(2)}) collective-permute-start(bf16[512,256]{1,0:T(8,128)(2,1)} %get-tuple-element.77), channel_id=1, source_target_pairs={{0,24},{4,28},{8,0},{12,4},{16,8},{20,12},{24,16},{28,20},{1,25},{... | collective-permute-start | bytes 786440 | tf_op jit(solution)/shard_map/ppermute | solution.py:309
  10.2 12.8 %collective-permute-start.1 = (bf16[512,256]{1,0:T(8,128)(2,1)}, bf16[512,256]{1,0:T(8,128)(2,1)S(1)}, u32[]{:S(2)}, u32[]{:S(2)}) collective-permute-start(bf16[512,256]{1,0:T(8,128)(2,1)} %get-tuple-element.78), channel_id=1, source_target_pairs={{0,8},{4,12},{8,16},{12,20},{16,24},{20,28},{24,0},{28,4},{1,9},{5... | collective-permute-start | bytes 786440 | tf_op jit(solution)/shard_map/ppermute | solution.py:309
  10.2 15.8 %copy-start.23 = (bf16[152,1024]{1,0:T(8,128)(2,1)S(1)}, bf16[152,1024]{1,0:T(8,128)(2,1)}, u32[]{:S(2)}) copy-start(bf16[152,1024]{1,0:T(8,128)(2,1)} %param.13) | copy-start | bytes 933892
  10.3 16.9 %copy-start.17 = (bf16[512,3,1024]{2,0,1:T(8,128)(2,1)S(1)}, bf16[512,3,1024]{2,0,1:T(8,128)(2,1)}, u32[]{:S(2)}) copy-start(bf16[512,3,1024]{2,0,1:T(8,128)(2,1)} %param.11) | copy-start | bytes 9437188
  22.9 14.3 %collective-permute-start.6 = (bf16[256,1024]{1,0:T(8,128)(2,1)S(1)}, bf16[256,1024]{1,0:T(8,128)(2,1)S(1)}, u32[]{:S(2)}, u32[]{:S(2)}) collective-permute-start(bf16[256,1024]{1,0:T(8,128)(2,1)S(1)} %hyena_filters.1.own_ref), channel_id=1, source_target_pairs={{0,1},{1,0},{2,3},{3,2},{4,5},{5,4},{6,7},{7,6},{8,9},{9,8},{10,11... | collective-permute-start | bytes 1572872 | tf_op jit(solution)/shard_map/ppermute | solution.py:317
  24.4 14.4 %collective-permute-start.8 = (bf16[256,1024]{1,0:T(8,128)(2,1)S(1)}, bf16[256,1024]{1,0:T(8,128)(2,1)S(1)}, u32[]{:S(2)}, u32[]{:S(2)}) collective-permute-start(bf16[256,1024]{1,0:T(8,128)(2,1)S(1)} %hyena_filters.1.own_ref), channel_id=1, source_target_pairs={{0,2},{1,3},{2,0},{3,1},{4,6},{5,7},{6,4},{7,5},{8,10},{9,11},{10,... | collective-permute-start | bytes 1572872 | tf_op jit(solution)/shard_map/ppermute | solution.py:317
  26.7 16.7 %collective-permute-start.2 = (bf16[256,1024]{1,0:T(8,128)(2,1)S(1)}, bf16[256,1024]{1,0:T(8,128)(2,1)}, u32[]{:S(2)}, u32[]{:S(2)}) collective-permute-start(bf16[256,1024]{1,0:T(8,128)(2,1)S(1)} %hyena_filters.1.own_ref), channel_id=1, source_target_pairs={{0,8},{4,12},{8,16},{12,20},{16,24},{20,28},{24,0},{28,4},{1,9},{5... | collective-permute-start | bytes 1572872 | tf_op jit(solution)/shard_map/ppermute | solution.py:309
  29.4 22.2 %copy-start.6 = (f32[4096]{0:T(1024)S(1)}, f32[4096]{0:T(1024)}, u32[]{:S(2)}) copy-start(f32[4096]{0:T(1024)} %param.10) | copy-start | bytes 49156
  29.4 28.3 %collective-permute-start.13 = (bf16[1344,256]{1,0:T(8,128)(2,1)}, bf16[1344,256]{1,0:T(8,128)(2,1)S(1)}, u32[]{:S(2)}, u32[]{:S(2)}) collective-permute-start(bf16[1344,256]{1,0:T(8,128)(2,1)} %pad_maximum_fusion.1), channel_id=1, source_target_pairs={{0,8},{4,12},{8,16},{12,20},{16,24},{20,28},{24,0},{28,4},{1,9},{5... | collective-permute-start | bytes 2064392 | tf_op jit(solution)/shard_map/ppermute | solution.py:309
  37.3 8.1 %collective-permute-start.7 = (bf16[128,1024]{1,0:T(8,128)(2,1)S(1)}, bf16[128,1024]{1,0:T(8,128)(2,1)S(1)}, u32[]{:S(2)}, u32[]{:S(2)}) collective-permute-start(bf16[128,1024]{1,0:T(8,128)(2,1)S(1)} %slice.42), channel_id=1, source_target_pairs={{0,2},{1,3},{2,0},{3,1},{4,6},{5,7},{6,4},{7,5},{8,10},{9,11},{10,... | collective-permute-start | bytes 786440 | tf_op jit(solution)/shard_map/ppermute | solution.py:317
  38.9 7.8 %collective-permute-start.9 = (bf16[128,1024]{1,0:T(8,128)(2,1)S(1)}, bf16[128,1024]{1,0:T(8,128)(2,1)S(1)}, u32[]{:S(2)}, u32[]{:S(2)}) collective-permute-start(bf16[128,1024]{1,0:T(8,128)(2,1)S(1)} %slice.43), channel_id=1, source_target_pairs={{0,1},{1,0},{2,3},{3,2},{4,5},{5,4},{6,7},{7,6},{8,9},{9,8},{10,11... | collective-permute-start | bytes 786440 | tf_op jit(solution)/shard_map/ppermute | solution.py:317
  40.5 17.2 %collective-permute-start.11 = (bf16[1344,256]{1,0:T(8,128)(2,1)S(1)}, bf16[1344,256]{1,0:T(8,128)(2,1)S(1)}, u32[]{:S(2)}, u32[]{:S(2)}) collective-permute-start(bf16[1344,256]{1,0:T(8,128)(2,1)S(1)} %pad_maximum_fusion.refs_0_), channel_id=1, source_target_pairs={{0,4},{4,0},{8,12},{12,8},{16,20},{20,16},{24,28},{28,24},{1,5},{5... | collective-permute-start | bytes 2064392 | tf_op jit(solution)/shard_map/ppermute | solution.py:313
  47.4 12.7 %collective-permute-start.15 = (bf16[256,1024]{1,0:T(8,128)(2,1)}, bf16[256,1024]{1,0:T(8,128)(2,1)S(1)}, u32[]{:S(2)}, u32[]{:S(2)}) collective-permute-start(bf16[256,1024]{1,0:T(8,128)(2,1)} %collective-permute-done.2.own_ref), channel_id=1, source_target_pairs={{0,2},{1,3},{2,0},{3,1},{4,6},{5,7},{6,4},{7,5},{8,10},{9,11},{10,... | collective-permute-start | bytes 1572872 | tf_op jit(solution)/shard_map/ppermute | solution.py:317
  48.5 13.2 %collective-permute-start.10 = (bf16[256,1024]{1,0:T(8,128)(2,1)}, bf16[256,1024]{1,0:T(8,128)(2,1)}, u32[]{:S(2)}, u32[]{:S(2)}) collective-permute-start(bf16[256,1024]{1,0:T(8,128)(2,1)} %collective-permute-done.2.own_ref), channel_id=1, source_target_pairs={{0,1},{1,0},{2,3},{3,2},{4,5},{5,4},{6,7},{7,6},{8,9},{9,8},{10,11... | collective-permute-start | bytes 1572872 | tf_op jit(solution)/shard_map/ppermute | solution.py:317
  49.8 1.7 collective-permute-start.12
  51.4 17.6 %collective-permute-start.3 = (bf16[256,1024]{1,0:T(8,128)(2,1)}, bf16[256,1024]{1,0:T(8,128)(2,1)S(1)}, u32[]{:S(2)}, u32[]{:S(2)}) collective-permute-start(bf16[256,1024]{1,0:T(8,128)(2,1)} %collective-permute-done.2.own_ref), channel_id=1, source_target_pairs={{0,8},{4,12},{8,16},{12,20},{16,24},{20,28},{24,0},{28,4},{1,9},{5... | collective-permute-start | bytes 1572872 | tf_op jit(solution)/shard_map/ppermute | solution.py:309
  51.5 110.0 %copy-start.15 = (s32[3]{0:T(128)}, s32[3]{0:T(128)S(1)}, u32[]{:S(2)}) copy-start(s32[3]{0:T(128)S(1)} %pad_add_fusion.place_ref) | copy-start | bytes 40
  60.1 9.0 %collective-permute-start.16 = (bf16[128,1024]{1,0:T(8,128)(2,1)S(1)}, bf16[128,1024]{1,0:T(8,128)(2,1)S(1)}, u32[]{:S(2)}, u32[]{:S(2)}) collective-permute-start(bf16[128,1024]{1,0:T(8,128)(2,1)S(1)} %slice.35), channel_id=1, source_target_pairs={{0,1},{1,0},{2,3},{3,2},{4,5},{5,4},{6,7},{7,6},{8,9},{9,8},{10,11... | collective-permute-start | bytes 786440 | tf_op jit(solution)/shard_map/ppermute | solution.py:317
  62.6 6.4 %collective-permute-start.14 = (bf16[128,1024]{1,0:T(8,128)(2,1)S(1)}, bf16[128,1024]{1,0:T(8,128)(2,1)S(1)}, u32[]{:S(2)}, u32[]{:S(2)}) collective-permute-start(bf16[128,1024]{1,0:T(8,128)(2,1)S(1)} %slice.34), channel_id=1, source_target_pairs={{0,2},{1,3},{2,0},{3,1},{4,6},{5,7},{6,4},{7,5},{8,10},{9,11},{10,... | collective-permute-start | bytes 786440 | tf_op jit(solution)/shard_map/ppermute | solution.py:317
  63.9 31.4 %copy-start.26 = (bf16[512,256]{1,0:T(8,128)(2,1)S(1)}, bf16[512,256]{1,0:T(8,128)(2,1)}, u32[]{:S(2)}) copy-start(bf16[512,256]{1,0:T(8,128)(2,1)} %get-tuple-element.50) | copy-start | bytes 786436
  63.9 31.5 %copy-start.18 = (bf16[512,256]{1,0:T(8,128)(2,1)S(1)}, bf16[512,256]{1,0:T(8,128)(2,1)}, u32[]{:S(2)}) copy-start(bf16[512,256]{1,0:T(8,128)(2,1)} %get-tuple-element.68) | copy-start | bytes 786436
  64.0 19.8 %collective-permute-start.20 = (bf16[1344,256]{1,0:T(8,128)(2,1)S(1)}, bf16[1344,256]{1,0:T(8,128)(2,1)S(1)}, u32[]{:S(2)}, u32[]{:S(2)}) collective-permute-start(bf16[1344,256]{1,0:T(8,128)(2,1)S(1)} %pad_maximum_fusion.2), channel_id=1, source_target_pairs={{0,24},{4,28},{8,0},{12,4},{16,8},{20,12},{24,16},{28,20},{1,25},{... | collective-permute-start | bytes 2064392 | tf_op jit(solution)/shard_map/ppermute | solution.py:309
  69.0 14.8 %collective-permute-start.22 = (bf16[256,1024]{1,0:T(8,128)(2,1)S(1)}, bf16[256,1024]{1,0:T(8,128)(2,1)S(1)}, u32[]{:S(2)}, u32[]{:S(2)}) collective-permute-start(bf16[256,1024]{1,0:T(8,128)(2,1)S(1)} %collective-permute-done.3.own_ref), channel_id=1, source_target_pairs={{0,2},{1,3},{2,0},{3,1},{4,6},{5,7},{6,4},{7,5},{8,10},{9,11},{10,... | collective-permute-start | bytes 1572872 | tf_op jit(solution)/shard_map/ppermute | solution.py:317
  70.2 13.9 %collective-permute-start.17 = (bf16[256,1024]{1,0:T(8,128)(2,1)S(1)}, bf16[256,1024]{1,0:T(8,128)(2,1)S(1)}, u32[]{:S(2)}, u32[]{:S(2)}) collective-permute-start(bf16[256,1024]{1,0:T(8,128)(2,1)S(1)} %collective-permute-done.3.own_ref), channel_id=1, source_target_pairs={{0,1},{1,0},{2,3},{3,2},{4,5},{5,4},{6,7},{7,6},{8,9},{9,8},{10,11... | collective-permute-start | bytes 1572872 | tf_op jit(solution)/shard_map/ppermute | solution.py:317
  70.8 1.5 collective-permute-start.18
  70.8 1.9 %collective-permute-start.19 = (bf16[512,256]{1,0:T(8,128)(2,1)S(1)}, bf16[512,256]{1,0:T(8,128)(2,1)S(1)}, u32[]{:S(2)}, u32[]{:S(2)}) collective-permute-start(bf16[512,256]{1,0:T(8,128)(2,1)S(1)} %copy-done.8), channel_id=1, source_target_pairs={{0,4},{4,0},{8,12},{12,8},{16,20},{20,16},{24,28},{28,24},{1,5},{5... | collective-permute-start | bytes 786440 | tf_op jit(solution)/shard_map/ppermute | solution.py:313
  72.3 22.0 %collective-permute-start.4 = (bf16[256,1024]{1,0:T(8,128)(2,1)S(1)}, bf16[256,1024]{1,0:T(8,128)(2,1)S(1)}, u32[]{:S(2)}, u32[]{:S(2)}) collective-permute-start(bf16[256,1024]{1,0:T(8,128)(2,1)S(1)} %collective-permute-done.3.own_ref), channel_id=1, source_target_pairs={{0,8},{4,12},{8,16},{12,20},{16,24},{20,28},{24,0},{28,4},{1,9},{5... | collective-permute-start | bytes 1572872 | tf_op jit(solution)/shard_map/ppermute | solution.py:309
  72.7 22.8 %collective-permute-start.25 = (bf16[1344,256]{1,0:T(8,128)(2,1)S(1)}, bf16[1344,256]{1,0:T(8,128)(2,1)S(1)}, u32[]{:S(2)}, u32[]{:S(2)}) collective-permute-start(bf16[1344,256]{1,0:T(8,128)(2,1)S(1)} %collective-permute-done.13.refs_1_), channel_id=1, source_target_pairs={{0,4},{4,0},{8,12},{12,8},{16,20},{20,16},{24,28},{28,24},{1,5},{5... | collective-permute-start | bytes 2064392 | tf_op jit(solution)/shard_map/ppermute | solution.py:313
  83.8 10.5 %collective-permute-start.23 = (bf16[128,1024]{1,0:T(8,128)(2,1)S(1)}, bf16[128,1024]{1,0:T(8,128)(2,1)S(1)}, u32[]{:S(2)}, u32[]{:S(2)}) collective-permute-start(bf16[128,1024]{1,0:T(8,128)(2,1)S(1)} %slice.37), channel_id=1, source_target_pairs={{0,1},{1,0},{2,3},{3,2},{4,5},{5,4},{6,7},{7,6},{8,9},{9,8},{10,11... | collective-permute-start | bytes 786440 | tf_op jit(solution)/shard_map/ppermute | solution.py:317
  84.1 10.2 %collective-permute-start.21 = (bf16[128,1024]{1,0:T(8,128)(2,1)S(1)}, bf16[128,1024]{1,0:T(8,128)(2,1)S(1)}, u32[]{:S(2)}, u32[]{:S(2)}) collective-permute-start(bf16[128,1024]{1,0:T(8,128)(2,1)S(1)} %slice.36), channel_id=1, source_target_pairs={{0,2},{1,3},{2,0},{3,1},{4,6},{5,7},{6,4},{7,5},{8,10},{9,11},{10,... | collective-permute-start | bytes 786440 | tf_op jit(solution)/shard_map/ppermute | solution.py:317
  84.9 32.3 %collective-permute-start.26 = (bf16[1344,256]{1,0:T(8,128)(2,1)S(1)}, bf16[1344,256]{1,0:T(8,128)(2,1)S(1)}, u32[]{:S(2)}, u32[]{:S(2)}) collective-permute-start(bf16[1344,256]{1,0:T(8,128)(2,1)S(1)} %collective-permute-done.20.refs_3_.refs_2_), channel_id=1, source_target_pairs={{0,4},{4,0},{8,12},{12,8},{16,20},{20,16},{24,28},{28,24},{1,5},{5... | collective-permute-start | bytes 2064392 | tf_op jit(solution)/shard_map/ppermute | solution.py:313
  94.3 22.9 %collective-permute-start.28 = (bf16[256,1024]{1,0:T(8,128)(2,1)S(1)}, bf16[256,1024]{1,0:T(8,128)(2,1)S(1)}, u32[]{:S(2)}, u32[]{:S(2)}) collective-permute-start(bf16[256,1024]{1,0:T(8,128)(2,1)S(1)} %collective-permute-done.4.own_ref), channel_id=1, source_target_pairs={{0,2},{1,3},{2,0},{3,1},{4,6},{5,7},{6,4},{7,5},{8,10},{9,11},{10,... | collective-permute-start | bytes 1572872 | tf_op jit(solution)/shard_map/ppermute | solution.py:317
  94.8 23.2 %collective-permute-start.24 = (bf16[256,1024]{1,0:T(8,128)(2,1)S(1)}, bf16[256,1024]{1,0:T(8,128)(2,1)S(1)}, u32[]{:S(2)}, u32[]{:S(2)}) collective-permute-start(bf16[256,1024]{1,0:T(8,128)(2,1)S(1)} %collective-permute-done.4.own_ref), channel_id=1, source_target_pairs={{0,1},{1,0},{2,3},{3,2},{4,5},{5,4},{6,7},{7,6},{8,9},{9,8},{10,11... | collective-permute-start | bytes 1572872 | tf_op jit(solution)/shard_map/ppermute | solution.py:317
  95.3 21.9 %collective-permute-start.27 = (bf16[512,256]{1,0:T(8,128)(2,1)S(1)}, bf16[512,256]{1,0:T(8,128)(2,1)S(1)}, u32[]{:S(2)}, u32[]{:S(2)}) collective-permute-start(bf16[512,256]{1,0:T(8,128)(2,1)S(1)} %copy-done.26), channel_id=1, source_target_pairs={{0,16},{4,20},{8,24},{12,28},{16,0},{20,4},{24,8},{28,12},{1,17},{... | collective-permute-start | bytes 786440 | tf_op jit(solution)/shard_map/ppermute | solution.py:309
  95.4 31.3 %copy-start.25 = (bf16[512,256]{1,0:T(8,128)(2,1)S(1)}, bf16[512,256]{1,0:T(8,128)(2,1)}, u32[]{:S(2)}) copy-start(bf16[512,256]{1,0:T(8,128)(2,1)} %get-tuple-element.59) | copy-start | bytes 786436
  95.5 30.7 %collective-permute-start.32 = (bf16[832,256]{1,0:T(8,128)(2,1)S(1)}, bf16[832,256]{1,0:T(8,128)(2,1)S(1)}, u32[]{:S(2)}, u32[]{:S(2)}) collective-permute-start(bf16[832,256]{1,0:T(8,128)(2,1)S(1)} %pad_maximum_fusion.3), channel_id=1, source_target_pairs={{0,16},{4,20},{8,24},{12,28},{16,0},{20,4},{24,8},{28,12},{1,17},{... | collective-permute-start | bytes 1277960 | tf_op jit(solution)/shard_map/ppermute | solution.py:309
  117.2 9.0 %collective-permute-start.30 = (bf16[128,1024]{1,0:T(8,128)(2,1)S(1)}, bf16[128,1024]{1,0:T(8,128)(2,1)S(1)}, u32[]{:S(2)}, u32[]{:S(2)}) collective-permute-start(bf16[128,1024]{1,0:T(8,128)(2,1)S(1)} %slice.39), channel_id=1, source_target_pairs={{0,1},{1,0},{2,3},{3,2},{4,5},{5,4},{6,7},{7,6},{8,9},{9,8},{10,11... | collective-permute-start | bytes 786440 | tf_op jit(solution)/shard_map/ppermute | solution.py:317
  118.0 8.2 %collective-permute-start.29 = (bf16[128,1024]{1,0:T(8,128)(2,1)S(1)}, bf16[128,1024]{1,0:T(8,128)(2,1)S(1)}, u32[]{:S(2)}, u32[]{:S(2)}) collective-permute-start(bf16[128,1024]{1,0:T(8,128)(2,1)S(1)} %slice.38), channel_id=1, source_target_pairs={{0,2},{1,3},{2,0},{3,1},{4,6},{5,7},{6,4},{7,5},{8,10},{9,11},{10,... | collective-permute-start | bytes 786440 | tf_op jit(solution)/shard_map/ppermute | solution.py:317
  126.2 9.8 %collective-permute-start.33 = (bf16[832,256]{1,0:T(8,128)(2,1)S(1)}, bf16[832,256]{1,0:T(8,128)(2,1)S(1)}, u32[]{:S(2)}, u32[]{:S(2)}) collective-permute-start(bf16[832,256]{1,0:T(8,128)(2,1)S(1)} %collective-permute-done.32.refs_2_.refs_0_), channel_id=1, source_target_pairs={{0,4},{4,0},{8,12},{12,8},{16,20},{20,16},{24,28},{28,24},{1,5},{5... | collective-permute-start | bytes 1277960 | tf_op jit(solution)/shard_map/ppermute | solution.py:313
  126.2 6.4 %collective-permute-start.31 = (bf16[512,256]{1,0:T(8,128)(2,1)S(1)}, bf16[512,256]{1,0:T(8,128)(2,1)S(1)}, u32[]{:S(2)}, u32[]{:S(2)}) collective-permute-start(bf16[512,256]{1,0:T(8,128)(2,1)S(1)} %collective-permute-done.27.refs_3_), channel_id=1, source_target_pairs={{0,4},{4,0},{8,12},{12,8},{16,20},{20,16},{24,28},{28,24},{1,5},{5... | collective-permute-start | bytes 786440 | tf_op jit(solution)/shard_map/ppermute | solution.py:313
  126.7 14.7 %collective-permute-start.34 = (bf16[512,256]{1,0:T(8,128)(2,1)S(1)}, bf16[512,256]{1,0:T(8,128)(2,1)S(1)}, u32[]{:S(2)}, u32[]{:S(2)}) collective-permute-start(bf16[512,256]{1,0:T(8,128)(2,1)S(1)} %copy-done.25), channel_id=1, source_target_pairs={{0,16},{4,20},{8,24},{12,28},{16,0},{20,4},{24,8},{28,12},{1,17},{... | collective-permute-start | bytes 786440 | tf_op jit(solution)/shard_map/ppermute | solution.py:309
  141.4 1.5 collective-permute-start.35
  141.5 3.0 %collective-permute-start.36 = (bf16[4,256,256]{2,1,0:T(8,128)(2,1)S(1)}, bf16[4,256,256]{2,1,0:T(8,128)(2,1)S(1)}, u32[]{:S(2)}, u32[]{:S(2)}) collective-permute-start(bf16[4,256,256]{2,1,0:T(8,128)(2,1)S(1)} %project.6.k_ref), channel_id=1, source_target_pairs={{0,4},{4,0},{8,12},{12,8},{16,20},{20,16},{24,28},{28,24},{1,5},{5... | collective-permute-start | bytes 1572872 | tf_op jit(solution)/shard_map/ppermute | solution.py:313
  144.3 2.0 %collective-permute-start.37 = (bf16[4,256,256]{2,1,0:T(8,128)(2,1)S(1)}, bf16[4,256,256]{2,1,0:T(8,128)(2,1)S(1)}, u32[]{:S(2)}, u32[]{:S(2)}) collective-permute-start(bf16[4,256,256]{2,1,0:T(8,128)(2,1)S(1)} %project.7.v_ref), channel_id=1, source_target_pairs={{0,4},{4,0},{8,12},{12,8},{16,20},{20,16},{24,28},{28,24},{1,5},{5... | collective-permute-start | bytes 1572872 | tf_op jit(solution)/shard_map/ppermute | solution.py:313
  150.2 11.3 %collective-permute-start.38 = (bf16[256,256]{1,0:T(8,128)(2,1)S(1)}, bf16[256,256]{1,0:T(8,128)(2,1)S(1)}, u32[]{:S(2)}, u32[]{:S(2)}) collective-permute-start(bf16[256,256]{1,0:T(8,128)(2,1)S(1)} %attend.3), channel_id=1, source_target_pairs={{0,16},{4,20},{8,24},{12,28},{16,0},{20,4},{24,8},{28,12},{1,17},{... | collective-permute-start | bytes 393224 | tf_op jit(solution)/shard_map/ppermute | solution.py:309
  157.6 8.2 %collective-permute-start.39 = (bf16[256,256]{1,0:T(8,128)(2,1)S(1)}, bf16[256,256]{1,0:T(8,128)(2,1)S(1)}, u32[]{:S(2)}, u32[]{:S(2)}) collective-permute-start(bf16[256,256]{1,0:T(8,128)(2,1)S(1)} %get-tuple-element.64), channel_id=1, source_target_pairs={{0,8},{4,12},{8,16},{12,20},{16,24},{20,28},{24,0},{28,4},{1,9},{5... | collective-permute-start | bytes 393224 | tf_op jit(solution)/shard_map/ppermute | solution.py:309
  157.7 9.5 %collective-permute-start.40 = (bf16[256,256]{1,0:T(8,128)(2,1)S(1)}, bf16[256,256]{1,0:T(8,128)(2,1)S(1)}, u32[]{:S(2)}, u32[]{:S(2)}) collective-permute-start(bf16[256,256]{1,0:T(8,128)(2,1)S(1)} %get-tuple-element.66), channel_id=1, source_target_pairs={{0,24},{4,28},{8,0},{12,4},{16,8},{20,12},{24,16},{28,20},{1,25},{... | collective-permute-start | bytes 393224 | tf_op jit(solution)/shard_map/ppermute | solution.py:309
  (24 other events, 143.7 us)

commit v10 on v8

--- a/solution.py
+++ b/solution.py
@@ -399,7 +399,7 @@
             kind, steps = item[:-1], int(item[-1])
             value = parcel(kind, steps, *acts[: int(n >= 2)])
         if n >= 2:
-            value = after(value, sent[n - {"kvc3": 1, "kc2": 1}.get(item, 2)])
+            value = after(value, sent[n - 2])
         sent.append(shift_z(value, steps, zs))
         if item == "acts":
             acts.append(sent[-1])
@@ -439,14 +439,14 @@
         diag1 = swap_chan(from_y[half:], 1)
         normed = norm(place, j, zs, own, from_x, from_y, diag0, diag1, gain4, normed)
 
-    there["q2"] = swap_core(after(here["q2"], diag0, diag1), zs)
     there["kc2"] = swap_core(after(here["kc2"], diag0, diag1), zs)
     q_sum, k_sum, v_sum = project_early(every[last:], sums)
-    (q,) = project_last("q2", q_sum)
     kept = sum(sides("kvc0", "kvc1", "kc2", "kvc3"), [])
     ck, cv = pack(kept, [depth if i % zs == 2 else 2 * depth for i in range(2 * zs)], crow)
-    k = project_last("kc2", k_sum, q, ck, apart=True)
+    k = project_last("kc2", k_sum, ck, apart=True)
     k_sib = [swap_core(slab, zs) for slab in k]
+    there["q2"] = swap_core(after(here["q2"], k[0]), zs)
+    (q,) = project_last("q2", q_sum)
     weights = weigh((3, 0), place, q, k, k_sib, ck)
     there["v2"] = swap_core(after(here["v2"], weights[2]), zs)
     weights = weigh((1,), place, q, k, k_sib, ck, weights)

time: 184 us -> 183 us (level)
  starting transfers between devices: 38 us -> 54.1 us
  waiting for transfers between devices: 80.6 us -> 64.6 us
    ppermute x13, starting transfers between devices: 14.1 us -> 32 us  [shift_z(): return lax.ppermute(value, 'seq', pairs)]
    ppermute x16, waiting for transfers between devices: 23.4 us -> 12.1 us  [swap_chan(): return lax.ppermute(value, 'chan', [(c, c ^ bit) for c in range(4)])]
    ppermute x13, waiting for transfers between devices: 54.6 us -> 48.9 us  [shift_z(): return lax.ppermute(value, 'seq', pairs)]
    unnamed x62 -> x58, local copies, waits for them, and re-layouts: 8.18 us -> 7.52 us
  transfers between devices with their start and end apart: 44 -> 44, of which waited for: 25 -> 18; matrix products, arithmetic and copies ran while one was open for 3% -> 3% of each run, Pallas kernels for 24% -> 24%
where the time goes in v10:
time: 183 us
  waiting for transfers between devices  64.6 us (35%)
  starting transfers between devices  54.1 us (30%)
  Pallas kernels  48.6 us (27%)
  local copies, waits for them, and re-layouts  12.4 us (7%)
  other arithmetic  2.47 us (1%)
    ppermute x13, waiting for transfers between devices, shift_z(): return lax.ppermute(value, 'seq', pairs)  48.9 us
    ppermute x13, starting transfers between devices, shift_z(): return lax.ppermute(value, 'seq', pairs)  32 us
    ppermute x16, starting transfers between devices, swap_chan(): return lax.ppermute(value, 'chan', [(c, c ^ bit) for c in range(4)])  16.9 us
    pallas_call x3, Pallas kernels, weigh(): pl.pallas_call(functools.partial(weigh_kernel, blocks), in_specs=[SMEM] +...  14.2 us
    ppermute x16, waiting for transfers between devices, swap_chan(): return lax.ppermute(value, 'chan', [(c, c ^ bit) for c in range(4)])  12.1 us
    pallas_call x5, Pallas kernels, project(): pl.pallas_call(functools.partial(project_kernel, shifts, slabs, parts, zs...  11.2 us
    pallas_call x4, Pallas kernels, norm(): pl.pallas_call(functools.partial(norm_kernel, j), in_specs=[SMEM] + [VMEM...  8.44 us
    unnamed x58, local copies, waits for them, and re-layouts  7.52 us
  transfers between devices with their start and end apart: 44, of which 18 were waited for; matrix products, arithmetic and copies ran while one was open for 3% of the time, Pallas kernels for 24%

profile of v10, /device:TPU:0, one launch (start us, length us, event | category | flops | bytes accessed | tf_op | source)
XLA Modules:
  0.0 182.9 jit_solution(6913474441231437270)
XLA Ops:
  0.0 1.2 fusion
  1.2 2.4 %collective-permute-start = (bf16[128,1024]{1,0:T(8,128)(2,1)S(1)}, bf16[128,1024]{1,0:T(8,128)(2,1)S(1)}, u32[]{:S(2)}, u32[]{:S(2)}) collective-permute-start(bf16[128,1024]{1,0:T(8,128)(2,1)S(1)} %fusion), channel_id=1, source_target_pairs={{0,4},{4,8},{8,12},{12,16},{16,20},{20,24},{24,28},{1,5},{5,9},{9,... | collective-permute-start | bytes 786440 | tf_op jit(solution)/shard_map/ppermute | solution.py:388
  3.7 1.8 dynamic-slice_bitcast_fusion.10
  5.5 2.6 %collective-permute-start.1 = (bf16[512,256]{1,0:T(8,128)(2,1)}, bf16[512,256]{1,0:T(8,128)(2,1)S(1)}, u32[]{:S(2)}, u32[]{:S(2)}) collective-permute-start(bf16[512,256]{1,0:T(8,128)(2,1)} %get-tuple-element.116), channel_id=1, source_target_pairs={{0,8},{4,12},{8,16},{12,20},{16,24},{20,28},{24,0},{28,4},{1,9},{5... | collective-permute-start | bytes 786440 | tf_op jit(solution)/shard_map/ppermute | solution.py:344
  8.0 2.0 %collective-permute-start.5 = (bf16[512,256]{1,0:T(8,128)(2,1)S(1)}, bf16[512,256]{1,0:T(8,128)(2,1)}, u32[]{:S(2)}, u32[]{:S(2)}) collective-permute-start(bf16[512,256]{1,0:T(8,128)(2,1)S(1)} %get-tuple-element.115), channel_id=1, source_target_pairs={{0,24},{4,28},{8,0},{12,4},{16,8},{20,12},{24,16},{28,20},{1,25},{... | collective-permute-start | bytes 786440 | tf_op jit(solution)/shard_map/ppermute | solution.py:344
  10.2 6.0 %hyena_filters.1.own_ref = bf16[256,1024]{1,0:T(8,128)(2,1)S(1)} custom-call(bf16[3,256,1024]{2,1,0:T(8,128)(2,1)S(1)} %bitcast.33, bf16[128,1024]{1,0:T(8,128)(2,1)S(1)} %pad_select_fusion.halo_ref, f32[64,128]{1,0:T(8,128)S(1)} %copy-done.14), custom_call_target="tpu_custom_call" | custom-call | flops 1 | bytes 1 | tf_op jit(solution)/shard_map/hyena_filters/pallas_call | solution.py:80
  17.4 5.3 %collective-permute-done.5.refs_2_ = bf16[512,256]{1,0:T(8,128)(2,1)} collective-permute-done((bf16[512,256]{1,0:T(8,128)(2,1)S(1)}, bf16[512,256]{1,0:T(8,128)(2,1)}, u32[]{:S(2)}, u32[]{:S(2)}) %collective-permute-start.5) | collective-permute-done | bytes 262176 | tf_op jit(solution)/shard_map/ppermute | solution.py:344
  22.6 1.5 collective-permute-start.6
  24.1 1.5 collective-permute-start.8
  27.5 1.2 dynamic-slice_bitcast_fusion
  28.8 7.7 %collective-permute-done.6.x_ref = bf16[256,1024]{1,0:T(8,128)(2,1)S(1)} collective-permute-done((bf16[256,1024]{1,0:T(8,128)(2,1)S(1)}, bf16[256,1024]{1,0:T(8,128)(2,1)S(1)}, u32[]{:S(2)}, u32[]{:S(2)}) %collective-permute-start.6) | collective-permute-done | bytes 524320 | tf_op jit(solution)/shard_map/ppermute | solution.py:352
  36.6 1.6 collective-permute-start.7
  38.2 1.6 collective-permute-start.9
  41.8 2.5 %collective-permute-done.7.d0_ref = bf16[128,1024]{1,0:T(8,128)(2,1)S(1)} collective-permute-done((bf16[128,1024]{1,0:T(8,128)(2,1)S(1)}, bf16[128,1024]{1,0:T(8,128)(2,1)S(1)}, u32[]{:S(2)}, u32[]{:S(2)}) %collective-permute-start.7) | collective-permute-done | bytes 262176 | tf_op jit(solution)/shard_map/ppermute | solution.py:352
  47.4 1.3 collective-permute-start.10
  48.7 1.7 collective-permute-done.12.refs_3_
  55.5 1.9 %norm.4.rest_0_ = bf16[4,4,256,1024]{3,2,1,0:T(8,128)(2,1)S(1)} custom-call(s32[3]{0:T(128)S(1)} %pad_add_fusion.place_ref, bf16[256,1024]{1,0:T(8,128)(2,1)S(1)} %hyena_filters.1.own_ref, bf16[256,1024]{1,0:T(8,128)(2,1)S(1)} %copy-done.2, bf16[256,1024]{1,0:T(8,128)(2,1)S(1)} %copy-done.4, bf16[128,1024]{1,0:T(8,128)(2,1)S(1)} %copy-done.10, ...), custom_call_target="tpu_custom_call" | custom-call | flops 1 | bytes 1 | tf_op jit(solution)/shard_map/norm/pallas_call | solution.py:119
  57.5 3.7 %collective-permute-done.13.refs_7_.refs_1_ = bf16[1344,256]{1,0:T(8,128)(2,1)S(1)} collective-permute-done((bf16[1344,256]{1,0:T(8,128)(2,1)}, bf16[1344,256]{1,0:T(8,128)(2,1)S(1)}, u32[]{:S(2)}, u32[]{:S(2)}) %collective-permute-start.13) | collective-permute-done | bytes 688160 | tf_op jit(solution)/shard_map/ppermute | solution.py:344
  64.0 3.3 %collective-permute-start.20 = (bf16[1344,256]{1,0:T(8,128)(2,1)S(1)}, bf16[1344,256]{1,0:T(8,128)(2,1)S(1)}, u32[]{:S(2)}, u32[]{:S(2)}) collective-permute-start(bf16[1344,256]{1,0:T(8,128)(2,1)S(1)} %pad_maximum_fusion.2), channel_id=1, source_target_pairs={{0,24},{4,28},{8,0},{12,4},{16,8},{20,12},{24,16},{28,20},{1,25},{... | collective-permute-start | bytes 2064392 | tf_op jit(solution)/shard_map/ppermute | solution.py:344
  67.3 5.2 %collective-permute-done.3.own_ref = bf16[256,1024]{1,0:T(8,128)(2,1)S(1)} collective-permute-done((bf16[256,1024]{1,0:T(8,128)(2,1)}, bf16[256,1024]{1,0:T(8,128)(2,1)S(1)}, u32[]{:S(2)}, u32[]{:S(2)}) %collective-permute-start.3) | collective-permute-done | bytes 524320 | tf_op jit(solution)/shard_map/ppermute | solution.py:344
  74.6 1.4 collective-permute-done.18.refs_4_
  76.0 11.4 %collective-permute-start.4 = (bf16[256,1024]{1,0:T(8,128)(2,1)S(1)}, bf16[256,1024]{1,0:T(8,128)(2,1)S(1)}, u32[]{:S(2)}, u32[]{:S(2)}) collective-permute-start(bf16[256,1024]{1,0:T(8,128)(2,1)S(1)} %collective-permute-done.3.own_ref), channel_id=1, source_target_pairs={{0,8},{4,12},{8,16},{12,20},{16,24},{20,28},{24,0},{28,4},{1,9},{5... | collective-permute-start | bytes 1572872 | tf_op jit(solution)/shard_map/ppermute | solution.py:344
  87.4 2.6 %norm.5.rest_0_ = bf16[4,4,256,1024]{3,2,1,0:T(8,128)(2,1)S(1)} custom-call(s32[3]{0:T(128)S(1)} %pad_add_fusion.place_ref, bf16[256,1024]{1,0:T(8,128)(2,1)} %collective-permute-done.2.own_ref, bf16[256,1024]{1,0:T(8,128)(2,1)} %collective-permute-done.10.x_ref, ...), custom_call_target="tpu_custom_call", output_to_operand_aliasing={{}: (7, {})} | custom-call | flops 1 | bytes 1 | tf_op jit(solution)/shard_map/norm/pallas_call | solution.py:119
  90.8 11.9 %collective-permute-done.4.own_ref = bf16[256,1024]{1,0:T(8,128)(2,1)S(1)} collective-permute-done((bf16[256,1024]{1,0:T(8,128)(2,1)S(1)}, bf16[256,1024]{1,0:T(8,128)(2,1)S(1)}, u32[]{:S(2)}, u32[]{:S(2)}) %collective-permute-start.4) | collective-permute-done | bytes 524320 | tf_op jit(solution)/shard_map/ppermute | solution.py:344
  103.5 1.5 collective-permute-start.24
  105.1 3.0 %collective-permute-start.31 = (bf16[832,256]{1,0:T(8,128)(2,1)S(1)}, bf16[832,256]{1,0:T(8,128)(2,1)S(1)}, u32[]{:S(2)}, u32[]{:S(2)}) collective-permute-start(bf16[832,256]{1,0:T(8,128)(2,1)S(1)} %pad_maximum_fusion.3), channel_id=1, source_target_pairs={{0,16},{4,20},{8,24},{12,28},{16,0},{20,4},{24,8},{28,12},{1,17},{... | collective-permute-start | bytes 1277960 | tf_op jit(solution)/shard_map/ppermute | solution.py:344
  108.1 1.9 %norm.6.normed_ref.rest_0_ = bf16[4,4,256,1024]{3,2,1,0:T(8,128)(2,1)S(1)} custom-call(s32[3]{0:T(128)S(1)} %pad_add_fusion.place_ref, bf16[256,1024]{1,0:T(8,128)(2,1)S(1)} %collective-permute-done.3.own_ref, bf16[256,1024]{1,0:T(8,128)(2,1)S(1)} %collective-permute-done.17.x_ref, ...), custom_call_target="tpu_custom_call", output_to_operand_aliasing={{}: (7, {})} | custom-call | flops 1 | bytes 1 | tf_op jit(solution)/shard_map/norm/pallas_call | solution.py:119
  110.0 5.0 %project.5 = (f32[4,256,256]{2,1,0:T(8,128)S(1)}, f32[4,256,256]{2,1,0:T(8,128)S(1)}, f32[4,256,256]{2,1,0:T(8,128)S(1)}) custom-call(s32[3]{0:T(128)S(1)} %pad_add_fusion.place_ref, bf16[4,4,256,1024]{3,2,1,0:T(8,128)(2,1)S(1)} %norm.6.normed_ref.rest_0_, bf16[512,256]{1,0:T(8,128)(2,1)S(1)} %get-tuple-element.112.refs_0_, bf16[512,256]{1,0:T(8,128)(2,1)S(1)} %copy-done.6, ...), custom_call_target="tpu_custom_call" | custom-call | flops 1 | bytes 1 | tf_op jit(solution)/shard_map/project/pallas_call | solution.py:161
  117.1 1.6 collective-permute-start.28
  118.7 6.1 %collective-permute-done.31.refs_2_.refs_0_ = bf16[832,256]{1,0:T(8,128)(2,1)S(1)} collective-permute-done((bf16[832,256]{1,0:T(8,128)(2,1)S(1)}, bf16[832,256]{1,0:T(8,128)(2,1)S(1)}, u32[]{:S(2)}, u32[]{:S(2)}) %collective-permute-start.31) | collective-permute-done | bytes 426016 | tf_op jit(solution)/shard_map/ppermute | solution.py:344
  124.8 2.5 %collective-permute-start.30 = (bf16[512,256]{1,0:T(8,128)(2,1)S(1)}, bf16[512,256]{1,0:T(8,128)(2,1)S(1)}, u32[]{:S(2)}, u32[]{:S(2)}) collective-permute-start(bf16[512,256]{1,0:T(8,128)(2,1)S(1)} %copy-done.24), channel_id=1, source_target_pairs={{0,16},{4,20},{8,24},{12,28},{16,0},{20,4},{24,8},{28,12},{1,17},{... | collective-permute-start | bytes 786440 | tf_op jit(solution)/shard_map/ppermute | solution.py:344
  127.3 2.1 %norm.7.normed_ref = bf16[4,4,256,1024]{3,2,1,0:T(8,128)(2,1)S(1)} custom-call(s32[3]{0:T(128)S(1)} %pad_add_fusion.place_ref, bf16[256,1024]{1,0:T(8,128)(2,1)S(1)} %collective-permute-done.4.own_ref, bf16[256,1024]{1,0:T(8,128)(2,1)S(1)} %collective-permute-done.24.x_ref, ...), custom_call_target="tpu_custom_call", output_to_operand_aliasing={{}: (7, {})} | custom-call | flops 1 | bytes 1 | tf_op jit(solution)/shard_map/norm/pallas_call | solution.py:119
  129.4 2.5 %project.6 = (f32[4,256,256]{2,1,0:T(8,128)S(1)}, f32[4,256,256]{2,1,0:T(8,128)S(1)}, f32[4,256,256]{2,1,0:T(8,128)S(1)}) custom-call(s32[3]{0:T(128)S(1)} %pad_add_fusion.place_ref, bf16[4,4,256,1024]{3,2,1,0:T(8,128)(2,1)S(1)} %norm.7.normed_ref, ...), custom_call_target="tpu_custom_call", output_to_operand_aliasing={{0}: (14, {}), {1}: (15, {}), {2}: (16, {})} | custom-call | flops 1 | bytes 1 | tf_op jit(solution)/shard_map/project/pallas_call | solution.py:161
  132.0 1.3 project.7
  133.2 6.7 %collective-permute-done.30.refs_0_ = bf16[512,256]{1,0:T(8,128)(2,1)S(1)} collective-permute-done((bf16[512,256]{1,0:T(8,128)(2,1)S(1)}, bf16[512,256]{1,0:T(8,128)(2,1)S(1)}, u32[]{:S(2)}, u32[]{:S(2)}) %collective-permute-start.30) | collective-permute-done | bytes 262176 | tf_op jit(solution)/shard_map/ppermute | solution.py:344
  141.7 1.3 project.8.q_ref
  143.0 6.3 %weigh.3 = (bf16[4,2,256,1216]{3,2,1,0:T(8,128)(2,1)S(1)}, bf16[4,2,4,256,512]{4,3,2,1,0:T(8,128)(2,1)S(1)}, f32[4,2,256,128]{3,2,1,0:T(8,128)S(1)}) custom-call(s32[3]{0:T(128)S(1)} %pad_add_fusion.place_ref, bf16[4,256,256]{2,1,0:T(8,128)(2,1)S(1)} %project.8.q_ref, bf16[1216,256]{1,0:T(8,128)(2,1)S(1)} %get-tuple-element.78.ck_ref, ...), custom_call_target="tpu_custom_call" | custom-call | flops 1 | bytes 1 | tf_op jit(solution)/shard_map/weigh/pallas_call | solution.py:236
  149.2 6.0 %collective-permute-done.38.refs_0_ = bf16[512,256]{1,0:T(8,128)(2,1)S(1)} collective-permute-done((bf16[512,256]{1,0:T(8,128)(2,1)S(1)}, bf16[512,256]{1,0:T(8,128)(2,1)S(1)}, u32[]{:S(2)}, u32[]{:S(2)}) %collective-permute-start.38) | collective-permute-done | bytes 262176 | tf_op jit(solution)/shard_map/ppermute | solution.py:344
  155.2 3.5 %weigh.4 = (bf16[4,2,256,1216]{3,2,1,0:T(8,128)(2,1)S(1)}, bf16[4,2,4,256,512]{4,3,2,1,0:T(8,128)(2,1)S(1)}, f32[4,2,256,128]{3,2,1,0:T(8,128)S(1)}) custom-call(s32[3]{0:T(128)S(1)} %pad_add_fusion.place_ref, bf16[4,256,256]{2,1,0:T(8,128)(2,1)S(1)} %project.8.q_ref, ...), custom_call_target="tpu_custom_call", output_to_operand_aliasing={{0}: (11, {}), {1}: (12, {}), {2}: (13, {})} | custom-call | flops 1 | bytes 1 | tf_op jit(solution)/shard_map/weigh/pallas_call | solution.py:236
  158.8 1.3 project.9.v_ref
  160.6 4.4 %weigh.5 = (bf16[4,2,256,1216]{3,2,1,0:T(8,128)(2,1)S(1)}, bf16[4,2,4,256,512]{4,3,2,1,0:T(8,128)(2,1)S(1)}, f32[4,2,256,128]{3,2,1,0:T(8,128)S(1)}) custom-call(s32[3]{0:T(128)S(1)} %pad_add_fusion.place_ref, bf16[4,256,256]{2,1,0:T(8,128)(2,1)S(1)} %project.8.q_ref, ...), custom_call_target="tpu_custom_call", output_to_operand_aliasing={{0}: (11, {}), {1}: (12, {}), {2}: (13, {})} | custom-call | flops 1 | bytes 1 | tf_op jit(solution)/shard_map/weigh/pallas_call | solution.py:236
  165.0 2.0 %mix.3 = bf16[256,256]{1,0:T(8,128)(2,1)S(1)} custom-call(s32[3]{0:T(128)S(1)} %pad_add_fusion.place_ref, bf16[4,2,256,1216]{3,2,1,0:T(8,128)(2,1)S(1)} %get-tuple-element.93.old_ref, bf16[4,2,4,256,512]{4,3,2,1,0:T(8,128)(2,1)S(1)} %get-tuple-element.94.new_ref, f32[4,2,256,128]{3,2,1,0:T(8,128)S(1)} %get-tuple-element.95.sum_ref, ...), custom_call_target="tpu_custom_call" | custom-call | flops 1 | bytes 1 | tf_op jit(solution)/shard_map/mix/pallas_call | solution.py:281
  167.1 3.4 %mix.4 = (bf16[256,256]{1,0:T(8,128)(2,1)S(1)}, bf16[256,256]{1,0:T(8,128)(2,1)S(1)}) custom-call(s32[3]{0:T(128)S(1)} %pad_add_fusion.place_ref, bf16[4,2,256,1216]{3,2,1,0:T(8,128)(2,1)S(1)} %get-tuple-element.93.old_ref, bf16[4,2,4,256,512]{4,3,2,1,0:T(8,128)(2,1)S(1)} %get-tuple-element.94.new_ref, f32[4,2,256,128]{3,2,1,0:T(8,128)S(1)} %get-tuple-element.95.sum_ref, ...), custom_call_target="tpu_custom_call" | custom-call | flops 1 | bytes 1 | tf_op jit(solution)/shard_map/mix/pallas_call | solution.py:281
  171.4 3.0 %collective-permute-start.43 = (bf16[256,256]{1,0:T(8,128)(2,1)S(1)}, bf16[256,256]{1,0:T(8,128)(2,1)S(1)}, u32[]{:S(2)}, u32[]{:S(2)}) collective-permute-start(bf16[256,256]{1,0:T(8,128)(2,1)S(1)} %get-tuple-element.104), channel_id=1, source_target_pairs={{0,24},{4,28},{8,0},{12,4},{16,8},{20,12},{24,16},{28,20},{1,25},{... | collective-permute-start | bytes 393224 | tf_op jit(solution)/shard_map/ppermute | solution.py:344
  174.5 1.4 mix.5.refs_0_
  176.6 2.1 %collective-permute-done.42.refs_1_ = bf16[256,256]{1,0:T(8,128)(2,1)S(1)} collective-permute-done((bf16[256,256]{1,0:T(8,128)(2,1)S(1)}, bf16[256,256]{1,0:T(8,128)(2,1)S(1)}, u32[]{:S(2)}, u32[]{:S(2)}) %collective-permute-start.42) | collective-permute-done | bytes 131104 | tf_op jit(solution)/shard_map/ppermute | solution.py:344
  178.7 1.4 collective-permute-done.43.refs_3_
  180.8 1.9 %join.1 = bf16[256,1024]{1,0:T(8,128)(2,1)} custom-call(s32[3]{0:T(128)} %copy-done.13, bf16[256,256]{1,0:T(8,128)(2,1)} %copy-done.7, bf16[256,256]{1,0:T(8,128)(2,1)} %copy-done.27, bf16[256,256]{1,0:T(8,128)(2,1)} %copy-done.26, bf16[256,256]{1,0:T(8,128)(2,1)} %copy-done.28), custom_call_target="tpu_custom_call" | custom-call | tf_op jit(solution)/shard_map/join/pallas_call | solution.py:332
  (134 shorter events, 27.0 us)
Async XLA Ops:
  1.2 8.8 %collective-permute-start = (bf16[128,1024]{1,0:T(8,128)(2,1)S(1)}, bf16[128,1024]{1,0:T(8,128)(2,1)S(1)}, u32[]{:S(2)}, u32[]{:S(2)}) collective-permute-start(bf16[128,1024]{1,0:T(8,128)(2,1)S(1)} %fusion), channel_id=1, source_target_pairs={{0,4},{4,8},{8,12},{12,16},{16,20},{20,24},{24,28},{1,5},{5,9},{9,... | collective-permute-start | bytes 786440 | tf_op jit(solution)/shard_map/ppermute | solution.py:388
  5.5 11.2 %collective-permute-start.1 = (bf16[512,256]{1,0:T(8,128)(2,1)}, bf16[512,256]{1,0:T(8,128)(2,1)S(1)}, u32[]{:S(2)}, u32[]{:S(2)}) collective-permute-start(bf16[512,256]{1,0:T(8,128)(2,1)} %get-tuple-element.116), channel_id=1, source_target_pairs={{0,8},{4,12},{8,16},{12,20},{16,24},{20,28},{24,0},{28,4},{1,9},{5... | collective-permute-start | bytes 786440 | tf_op jit(solution)/shard_map/ppermute | solution.py:344
  8.0 14.6 %collective-permute-start.5 = (bf16[512,256]{1,0:T(8,128)(2,1)S(1)}, bf16[512,256]{1,0:T(8,128)(2,1)}, u32[]{:S(2)}, u32[]{:S(2)}) collective-permute-start(bf16[512,256]{1,0:T(8,128)(2,1)S(1)} %get-tuple-element.115), channel_id=1, source_target_pairs={{0,24},{4,28},{8,0},{12,4},{16,8},{20,12},{24,16},{28,20},{1,25},{... | collective-permute-start | bytes 786440 | tf_op jit(solution)/shard_map/ppermute | solution.py:344
  10.2 17.3 %copy-start.15 = (bf16[512,3,1024]{2,0,1:T(8,128)(2,1)S(1)}, bf16[512,3,1024]{2,0,1:T(8,128)(2,1)}, u32[]{:S(2)}) copy-start(bf16[512,3,1024]{2,0,1:T(8,128)(2,1)} %param.11) | copy-start | bytes 9437188
  22.6 14.0 %collective-permute-start.6 = (bf16[256,1024]{1,0:T(8,128)(2,1)S(1)}, bf16[256,1024]{1,0:T(8,128)(2,1)S(1)}, u32[]{:S(2)}, u32[]{:S(2)}) collective-permute-start(bf16[256,1024]{1,0:T(8,128)(2,1)S(1)} %hyena_filters.1.own_ref), channel_id=1, source_target_pairs={{0,1},{1,0},{2,3},{3,2},{4,5},{5,4},{6,7},{7,6},{8,9},{9,8},{10,11... | collective-permute-start | bytes 1572872 | tf_op jit(solution)/shard_map/ppermute | solution.py:352
  24.1 14.1 %collective-permute-start.8 = (bf16[256,1024]{1,0:T(8,128)(2,1)S(1)}, bf16[256,1024]{1,0:T(8,128)(2,1)S(1)}, u32[]{:S(2)}, u32[]{:S(2)}) collective-permute-start(bf16[256,1024]{1,0:T(8,128)(2,1)S(1)} %hyena_filters.1.own_ref), channel_id=1, source_target_pairs={{0,2},{1,3},{2,0},{3,1},{4,6},{5,7},{6,4},{7,5},{8,10},{9,11},{10,... | collective-permute-start | bytes 1572872 | tf_op jit(solution)/shard_map/ppermute | solution.py:352
  26.4 15.4 %collective-permute-start.2 = (bf16[256,1024]{1,0:T(8,128)(2,1)S(1)}, bf16[256,1024]{1,0:T(8,128)(2,1)}, u32[]{:S(2)}, u32[]{:S(2)}) collective-permute-start(bf16[256,1024]{1,0:T(8,128)(2,1)S(1)} %hyena_filters.1.own_ref), channel_id=1, source_target_pairs={{0,8},{4,12},{8,16},{12,20},{16,24},{20,28},{24,0},{28,4},{1,9},{5... | collective-permute-start | bytes 1572872 | tf_op jit(solution)/shard_map/ppermute | solution.py:344
  28.7 22.8 %copy-start.8 = (f32[4096]{0:T(1024)S(1)}, f32[4096]{0:T(1024)}, u32[]{:S(2)}) copy-start(f32[4096]{0:T(1024)} %param.10) | copy-start | bytes 49156
  28.8 28.7 %collective-permute-start.11 = (bf16[1344,256]{1,0:T(8,128)(2,1)S(1)}, bf16[1344,256]{1,0:T(8,128)(2,1)S(1)}, u32[]{:S(2)}, u32[]{:S(2)}) collective-permute-start(bf16[1344,256]{1,0:T(8,128)(2,1)S(1)} %pad_maximum_fusion.refs_6_.refs_0_), channel_id=1, source_target_pairs={{0,4},{4,0},{8,12},{12,8},{16,20},{20,16},{24,28},{28,24},{1,5},{5... | collective-permute-start | bytes 2064392 | tf_op jit(solution)/shard_map/ppermute | solution.py:348
  36.6 7.7 %collective-permute-start.7 = (bf16[128,1024]{1,0:T(8,128)(2,1)S(1)}, bf16[128,1024]{1,0:T(8,128)(2,1)S(1)}, u32[]{:S(2)}, u32[]{:S(2)}) collective-permute-start(bf16[128,1024]{1,0:T(8,128)(2,1)S(1)} %slice.42), channel_id=1, source_target_pairs={{0,2},{1,3},{2,0},{3,1},{4,6},{5,7},{6,4},{7,5},{8,10},{9,11},{10,... | collective-permute-start | bytes 786440 | tf_op jit(solution)/shard_map/ppermute | solution.py:352
  38.2 7.4 %collective-permute-start.9 = (bf16[128,1024]{1,0:T(8,128)(2,1)S(1)}, bf16[128,1024]{1,0:T(8,128)(2,1)S(1)}, u32[]{:S(2)}, u32[]{:S(2)}) collective-permute-start(bf16[128,1024]{1,0:T(8,128)(2,1)S(1)} %slice.43), channel_id=1, source_target_pairs={{0,1},{1,0},{2,3},{3,2},{4,5},{5,4},{6,7},{7,6},{8,9},{9,8},{10,11... | collective-permute-start | bytes 786440 | tf_op jit(solution)/shard_map/ppermute | solution.py:352
  40.7 20.4 %collective-permute-start.13 = (bf16[1344,256]{1,0:T(8,128)(2,1)}, bf16[1344,256]{1,0:T(8,128)(2,1)S(1)}, u32[]{:S(2)}, u32[]{:S(2)}) collective-permute-start(bf16[1344,256]{1,0:T(8,128)(2,1)} %pad_maximum_fusion.1), channel_id=1, source_target_pairs={{0,8},{4,12},{8,16},{12,20},{16,24},{20,28},{24,0},{28,4},{1,9},{5... | collective-permute-start | bytes 2064392 | tf_op jit(solution)/shard_map/ppermute | solution.py:344
  46.3 14.8 %collective-permute-start.15 = (bf16[256,1024]{1,0:T(8,128)(2,1)}, bf16[256,1024]{1,0:T(8,128)(2,1)S(1)}, u32[]{:S(2)}, u32[]{:S(2)}) collective-permute-start(bf16[256,1024]{1,0:T(8,128)(2,1)} %collective-permute-done.2.own_ref), channel_id=1, source_target_pairs={{0,2},{1,3},{2,0},{3,1},{4,6},{5,7},{6,4},{7,5},{8,10},{9,11},{10,... | collective-permute-start | bytes 1572872 | tf_op jit(solution)/shard_map/ppermute | solution.py:352
  47.4 14.3 %collective-permute-start.10 = (bf16[256,1024]{1,0:T(8,128)(2,1)}, bf16[256,1024]{1,0:T(8,128)(2,1)}, u32[]{:S(2)}, u32[]{:S(2)}) collective-permute-start(bf16[256,1024]{1,0:T(8,128)(2,1)} %collective-permute-done.2.own_ref), channel_id=1, source_target_pairs={{0,1},{1,0},{2,3},{3,2},{4,5},{5,4},{6,7},{7,6},{8,9},{9,8},{10,11... | collective-permute-start | bytes 1572872 | tf_op jit(solution)/shard_map/ppermute | solution.py:352
  48.7 1.7 collective-permute-start.12
  50.4 22.0 %collective-permute-start.3 = (bf16[256,1024]{1,0:T(8,128)(2,1)}, bf16[256,1024]{1,0:T(8,128)(2,1)S(1)}, u32[]{:S(2)}, u32[]{:S(2)}) collective-permute-start(bf16[256,1024]{1,0:T(8,128)(2,1)} %collective-permute-done.2.own_ref), channel_id=1, source_target_pairs={{0,8},{4,12},{8,16},{12,20},{16,24},{20,28},{24,0},{28,4},{1,9},{5... | collective-permute-start | bytes 1572872 | tf_op jit(solution)/shard_map/ppermute | solution.py:344
  51.5 123.0 %copy-start.13 = (s32[3]{0:T(128)}, s32[3]{0:T(128)S(1)}, u32[]{:S(2)}) copy-start(s32[3]{0:T(128)S(1)} %pad_add_fusion.place_ref) | copy-start | bytes 40
  61.1 11.3 %collective-permute-start.16 = (bf16[128,1024]{1,0:T(8,128)(2,1)S(1)}, bf16[128,1024]{1,0:T(8,128)(2,1)S(1)}, u32[]{:S(2)}, u32[]{:S(2)}) collective-permute-start(bf16[128,1024]{1,0:T(8,128)(2,1)S(1)} %slice.35), channel_id=1, source_target_pairs={{0,1},{1,0},{2,3},{3,2},{4,5},{5,4},{6,7},{7,6},{8,9},{9,8},{10,11... | collective-permute-start | bytes 786440 | tf_op jit(solution)/shard_map/ppermute | solution.py:352
  62.7 9.7 %collective-permute-start.14 = (bf16[128,1024]{1,0:T(8,128)(2,1)S(1)}, bf16[128,1024]{1,0:T(8,128)(2,1)S(1)}, u32[]{:S(2)}, u32[]{:S(2)}) collective-permute-start(bf16[128,1024]{1,0:T(8,128)(2,1)S(1)} %slice.34), channel_id=1, source_target_pairs={{0,2},{1,3},{2,0},{3,1},{4,6},{5,7},{6,4},{7,5},{8,10},{9,11},{10,... | collective-permute-start | bytes 786440 | tf_op jit(solution)/shard_map/ppermute | solution.py:352
  64.0 41.1 %copy-start.16 = (bf16[512,256]{1,0:T(8,128)(2,1)S(1)}, bf16[512,256]{1,0:T(8,128)(2,1)}, u32[]{:S(2)}) copy-start(bf16[512,256]{1,0:T(8,128)(2,1)} %get-tuple-element.106) | copy-start | bytes 786436
  64.0 26.0 %collective-permute-start.20 = (bf16[1344,256]{1,0:T(8,128)(2,1)S(1)}, bf16[1344,256]{1,0:T(8,128)(2,1)S(1)}, u32[]{:S(2)}, u32[]{:S(2)}) collective-permute-start(bf16[1344,256]{1,0:T(8,128)(2,1)S(1)} %pad_maximum_fusion.2), channel_id=1, source_target_pairs={{0,24},{4,28},{8,0},{12,4},{16,8},{20,12},{24,16},{28,20},{1,25},{... | collective-permute-start | bytes 2064392 | tf_op jit(solution)/shard_map/ppermute | solution.py:344
  72.4 17.6 %collective-permute-start.22 = (bf16[256,1024]{1,0:T(8,128)(2,1)S(1)}, bf16[256,1024]{1,0:T(8,128)(2,1)S(1)}, u32[]{:S(2)}, u32[]{:S(2)}) collective-permute-start(bf16[256,1024]{1,0:T(8,128)(2,1)S(1)} %collective-permute-done.3.own_ref), channel_id=1, source_target_pairs={{0,2},{1,3},{2,0},{3,1},{4,6},{5,7},{6,4},{7,5},{8,10},{9,11},{10,... | collective-permute-start | bytes 1572872 | tf_op jit(solution)/shard_map/ppermute | solution.py:352
  72.9 17.2 %collective-permute-start.17 = (bf16[256,1024]{1,0:T(8,128)(2,1)S(1)}, bf16[256,1024]{1,0:T(8,128)(2,1)S(1)}, u32[]{:S(2)}, u32[]{:S(2)}) collective-permute-start(bf16[256,1024]{1,0:T(8,128)(2,1)S(1)} %collective-permute-done.3.own_ref), channel_id=1, source_target_pairs={{0,1},{1,0},{2,3},{3,2},{4,5},{5,4},{6,7},{7,6},{8,9},{9,8},{10,11... | collective-permute-start | bytes 1572872 | tf_op jit(solution)/shard_map/ppermute | solution.py:352
  74.1 1.9 %collective-permute-start.18 = (bf16[512,256]{1,0:T(8,128)(2,1)S(1)}, bf16[512,256]{1,0:T(8,128)(2,1)S(1)}, u32[]{:S(2)}, u32[]{:S(2)}) collective-permute-start(bf16[512,256]{1,0:T(8,128)(2,1)S(1)} %copy-done.6), channel_id=1, source_target_pairs={{0,4},{4,0},{8,12},{12,8},{16,20},{20,16},{24,28},{28,24},{1,5},{5... | collective-permute-start | bytes 786440 | tf_op jit(solution)/shard_map/ppermute | solution.py:348
  74.1 15.9 %collective-permute-start.19 = (bf16[512,256]{1,0:T(8,128)(2,1)}, bf16[512,256]{1,0:T(8,128)(2,1)S(1)}, u32[]{:S(2)}, u32[]{:S(2)}) collective-permute-start(bf16[512,256]{1,0:T(8,128)(2,1)} %collective-permute-done.5.refs_2_), channel_id=1, source_target_pairs={{0,4},{4,0},{8,12},{12,8},{16,20},{20,16},{24,28},{28,24},{1,5},{5... | collective-permute-start | bytes 786440 | tf_op jit(solution)/shard_map/ppermute | solution.py:348
  76.0 26.8 %collective-permute-start.4 = (bf16[256,1024]{1,0:T(8,128)(2,1)S(1)}, bf16[256,1024]{1,0:T(8,128)(2,1)S(1)}, u32[]{:S(2)}, u32[]{:S(2)}) collective-permute-start(bf16[256,1024]{1,0:T(8,128)(2,1)S(1)} %collective-permute-done.3.own_ref), channel_id=1, source_target_pairs={{0,8},{4,12},{8,16},{12,20},{16,24},{20,28},{24,0},{28,4},{1,9},{5... | collective-permute-start | bytes 1572872 | tf_op jit(solution)/shard_map/ppermute | solution.py:344
  90.0 12.7 %collective-permute-start.23 = (bf16[128,1024]{1,0:T(8,128)(2,1)S(1)}, bf16[128,1024]{1,0:T(8,128)(2,1)S(1)}, u32[]{:S(2)}, u32[]{:S(2)}) collective-permute-start(bf16[128,1024]{1,0:T(8,128)(2,1)S(1)} %slice.37), channel_id=1, source_target_pairs={{0,1},{1,0},{2,3},{3,2},{4,5},{5,4},{6,7},{7,6},{8,9},{9,8},{10,11... | collective-permute-start | bytes 786440 | tf_op jit(solution)/shard_map/ppermute | solution.py:352
  90.2 12.6 %collective-permute-start.21 = (bf16[128,1024]{1,0:T(8,128)(2,1)S(1)}, bf16[128,1024]{1,0:T(8,128)(2,1)S(1)}, u32[]{:S(2)}, u32[]{:S(2)}) collective-permute-start(bf16[128,1024]{1,0:T(8,128)(2,1)S(1)} %slice.36), channel_id=1, source_target_pairs={{0,2},{1,3},{2,0},{3,1},{4,6},{5,7},{6,4},{7,5},{8,10},{9,11},{10,... | collective-permute-start | bytes 786440 | tf_op jit(solution)/shard_map/ppermute | solution.py:352
  90.3 19.7 %collective-permute-start.25 = (bf16[1344,256]{1,0:T(8,128)(2,1)S(1)}, bf16[1344,256]{1,0:T(8,128)(2,1)S(1)}, u32[]{:S(2)}, u32[]{:S(2)}) collective-permute-start(bf16[1344,256]{1,0:T(8,128)(2,1)S(1)} %collective-permute-done.13.refs_7_.refs_1_), channel_id=1, source_target_pairs={{0,4},{4,0},{8,12},{12,8},{16,20},{20,16},{24,28},{28,24},{1,5},{5... | collective-permute-start | bytes 2064392 | tf_op jit(solution)/shard_map/ppermute | solution.py:348
  90.3 19.7 %collective-permute-start.26 = (bf16[1344,256]{1,0:T(8,128)(2,1)S(1)}, bf16[1344,256]{1,0:T(8,128)(2,1)S(1)}, u32[]{:S(2)}, u32[]{:S(2)}) collective-permute-start(bf16[1344,256]{1,0:T(8,128)(2,1)S(1)} %collective-permute-done.20.refs_8_.refs_3_), channel_id=1, source_target_pairs={{0,4},{4,0},{8,12},{12,8},{16,20},{20,16},{24,28},{28,24},{1,5},{5... | collective-permute-start | bytes 2064392 | tf_op jit(solution)/shard_map/ppermute | solution.py:348
  102.7 13.5 %collective-permute-start.27 = (bf16[256,1024]{1,0:T(8,128)(2,1)S(1)}, bf16[256,1024]{1,0:T(8,128)(2,1)S(1)}, u32[]{:S(2)}, u32[]{:S(2)}) collective-permute-start(bf16[256,1024]{1,0:T(8,128)(2,1)S(1)} %collective-permute-done.4.own_ref), channel_id=1, source_target_pairs={{0,2},{1,3},{2,0},{3,1},{4,6},{5,7},{6,4},{7,5},{8,10},{9,11},{10,... | collective-permute-start | bytes 1572872 | tf_op jit(solution)/shard_map/ppermute | solution.py:352
  103.5 13.5 %collective-permute-start.24 = (bf16[256,1024]{1,0:T(8,128)(2,1)S(1)}, bf16[256,1024]{1,0:T(8,128)(2,1)S(1)}, u32[]{:S(2)}, u32[]{:S(2)}) collective-permute-start(bf16[256,1024]{1,0:T(8,128)(2,1)S(1)} %collective-permute-done.4.own_ref), channel_id=1, source_target_pairs={{0,1},{1,0},{2,3},{3,2},{4,5},{5,4},{6,7},{7,6},{8,9},{9,8},{10,11... | collective-permute-start | bytes 1572872 | tf_op jit(solution)/shard_map/ppermute | solution.py:352
  105.1 19.7 %collective-permute-start.31 = (bf16[832,256]{1,0:T(8,128)(2,1)S(1)}, bf16[832,256]{1,0:T(8,128)(2,1)S(1)}, u32[]{:S(2)}, u32[]{:S(2)}) collective-permute-start(bf16[832,256]{1,0:T(8,128)(2,1)S(1)} %pad_maximum_fusion.3), channel_id=1, source_target_pairs={{0,16},{4,20},{8,24},{12,28},{16,0},{20,4},{24,8},{28,12},{1,17},{... | collective-permute-start | bytes 1277960 | tf_op jit(solution)/shard_map/ppermute | solution.py:344
  116.2 8.5 %collective-permute-start.29 = (bf16[128,1024]{1,0:T(8,128)(2,1)S(1)}, bf16[128,1024]{1,0:T(8,128)(2,1)S(1)}, u32[]{:S(2)}, u32[]{:S(2)}) collective-permute-start(bf16[128,1024]{1,0:T(8,128)(2,1)S(1)} %slice.39), channel_id=1, source_target_pairs={{0,1},{1,0},{2,3},{3,2},{4,5},{5,4},{6,7},{7,6},{8,9},{9,8},{10,11... | collective-permute-start | bytes 786440 | tf_op jit(solution)/shard_map/ppermute | solution.py:352
  117.1 7.7 %collective-permute-start.28 = (bf16[128,1024]{1,0:T(8,128)(2,1)S(1)}, bf16[128,1024]{1,0:T(8,128)(2,1)S(1)}, u32[]{:S(2)}, u32[]{:S(2)}) collective-permute-start(bf16[128,1024]{1,0:T(8,128)(2,1)S(1)} %slice.38), channel_id=1, source_target_pairs={{0,2},{1,3},{2,0},{3,1},{4,6},{5,7},{6,4},{7,5},{8,10},{9,11},{10,... | collective-permute-start | bytes 786440 | tf_op jit(solution)/shard_map/ppermute | solution.py:352
  124.7 7.1 %collective-permute-start.32 = (bf16[832,256]{1,0:T(8,128)(2,1)S(1)}, bf16[832,256]{1,0:T(8,128)(2,1)S(1)}, u32[]{:S(2)}, u32[]{:S(2)}) collective-permute-start(bf16[832,256]{1,0:T(8,128)(2,1)S(1)} %collective-permute-done.31.refs_2_.refs_0_), channel_id=1, source_target_pairs={{0,4},{4,0},{8,12},{12,8},{16,20},{20,16},{24,28},{28,24},{1,5},{5... | collective-permute-start | bytes 1277960 | tf_op jit(solution)/shard_map/ppermute | solution.py:348
  124.8 15.2 %collective-permute-start.30 = (bf16[512,256]{1,0:T(8,128)(2,1)S(1)}, bf16[512,256]{1,0:T(8,128)(2,1)S(1)}, u32[]{:S(2)}, u32[]{:S(2)}) collective-permute-start(bf16[512,256]{1,0:T(8,128)(2,1)S(1)} %copy-done.24), channel_id=1, source_target_pairs={{0,16},{4,20},{8,24},{12,28},{16,0},{20,4},{24,8},{28,12},{1,17},{... | collective-permute-start | bytes 786440 | tf_op jit(solution)/shard_map/ppermute | solution.py:344
  140.0 1.5 collective-permute-start.33
  140.1 15.2 %collective-permute-start.38 = (bf16[512,256]{1,0:T(8,128)(2,1)S(1)}, bf16[512,256]{1,0:T(8,128)(2,1)S(1)}, u32[]{:S(2)}, u32[]{:S(2)}) collective-permute-start(bf16[512,256]{1,0:T(8,128)(2,1)S(1)} %copy-done.23), channel_id=1, source_target_pairs={{0,16},{4,20},{8,24},{12,28},{16,0},{20,4},{24,8},{28,12},{1,17},{... | collective-permute-start | bytes 786440 | tf_op jit(solution)/shard_map/ppermute | solution.py:344
  140.1 2.9 %collective-permute-start.34 = (bf16[256,256]{1,0:T(8,128)(2,1)S(1)}, bf16[256,256]{1,0:T(8,128)(2,1)S(1)}, u32[]{:S(2)}, u32[]{:S(2)}) collective-permute-start(bf16[256,256]{1,0:T(8,128)(2,1)S(1)} %get-tuple-element.81.refs_0_), channel_id=1, source_target_pairs={{0,4},{4,0},{8,12},{12,8},{16,20},{20,16},{24,28},{28,24},{1,5},{5... | collective-permute-start | bytes 393224 | tf_op jit(solution)/shard_map/ppermute | solution.py:348
  140.5 2.4 %collective-permute-start.35 = (bf16[256,256]{1,0:T(8,128)(2,1)S(1)}, bf16[256,256]{1,0:T(8,128)(2,1)S(1)}, u32[]{:S(2)}, u32[]{:S(2)}) collective-permute-start(bf16[256,256]{1,0:T(8,128)(2,1)S(1)} %get-tuple-element.84.refs_1_), channel_id=1, source_target_pairs={{0,4},{4,0},{8,12},{12,8},{16,20},{20,16},{24,28},{28,24},{1,5},{5... | collective-permute-start | bytes 393224 | tf_op jit(solution)/shard_map/ppermute | solution.py:348
  140.6 2.4 %collective-permute-start.36 = (bf16[256,256]{1,0:T(8,128)(2,1)S(1)}, bf16[256,256]{1,0:T(8,128)(2,1)S(1)}, u32[]{:S(2)}, u32[]{:S(2)}) collective-permute-start(bf16[256,256]{1,0:T(8,128)(2,1)S(1)} %get-tuple-element.85.refs_2_), channel_id=1, source_target_pairs={{0,4},{4,0},{8,12},{12,8},{16,20},{20,16},{24,28},{28,24},{1,5},{5... | collective-permute-start | bytes 393224 | tf_op jit(solution)/shard_map/ppermute | solution.py:348
  141.5 1.4 collective-permute-start.37
  155.2 3.5 %collective-permute-start.39 = (bf16[512,256]{1,0:T(8,128)(2,1)S(1)}, bf16[512,256]{1,0:T(8,128)(2,1)S(1)}, u32[]{:S(2)}, u32[]{:S(2)}) collective-permute-start(bf16[512,256]{1,0:T(8,128)(2,1)S(1)} %collective-permute-done.38.refs_0_), channel_id=1, source_target_pairs={{0,4},{4,0},{8,12},{12,8},{16,20},{20,16},{24,28},{28,24},{1,5},{5... | collective-permute-start | bytes 786440 | tf_op jit(solution)/shard_map/ppermute | solution.py:348
  160.0 5.0 %collective-permute-start.40 = (bf16[4,256,256]{2,1,0:T(8,128)(2,1)S(1)}, bf16[4,256,256]{2,1,0:T(8,128)(2,1)S(1)}, u32[]{:S(2)}, u32[]{:S(2)}) collective-permute-start(bf16[4,256,256]{2,1,0:T(8,128)(2,1)S(1)} %project.9.v_ref), channel_id=1, source_target_pairs={{0,4},{4,0},{8,12},{12,8},{16,20},{20,16},{24,28},{28,24},{1,5},{5... | collective-permute-start | bytes 1572872 | tf_op jit(solution)/shard_map/ppermute | solution.py:348
  167.0 7.5 %collective-permute-start.41 = (bf16[256,256]{1,0:T(8,128)(2,1)S(1)}, bf16[256,256]{1,0:T(8,128)(2,1)S(1)}, u32[]{:S(2)}, u32[]{:S(2)}) collective-permute-start(bf16[256,256]{1,0:T(8,128)(2,1)S(1)} %mix.3), channel_id=1, source_target_pairs={{0,16},{4,20},{8,24},{12,28},{16,0},{20,4},{24,8},{28,12},{1,17},{... | collective-permute-start | bytes 393224 | tf_op jit(solution)/shard_map/ppermute | solution.py:344
  170.5 8.2 %collective-permute-start.42 = (bf16[256,256]{1,0:T(8,128)(2,1)S(1)}, bf16[256,256]{1,0:T(8,128)(2,1)S(1)}, u32[]{:S(2)}, u32[]{:S(2)}) collective-permute-start(bf16[256,256]{1,0:T(8,128)(2,1)S(1)} %get-tuple-element.102), channel_id=1, source_target_pairs={{0,8},{4,12},{8,16},{12,20},{16,24},{20,28},{24,0},{28,4},{1,9},{5... | collective-permute-start | bytes 393224 | tf_op jit(solution)/shard_map/ppermute | solution.py:344
  171.4 8.7 %collective-permute-start.43 = (bf16[256,256]{1,0:T(8,128)(2,1)S(1)}, bf16[256,256]{1,0:T(8,128)(2,1)S(1)}, u32[]{:S(2)}, u32[]{:S(2)}) collective-permute-start(bf16[256,256]{1,0:T(8,128)(2,1)S(1)} %get-tuple-element.104), channel_id=1, source_target_pairs={{0,24},{4,28},{8,0},{12,4},{16,8},{20,12},{24,16},{28,20},{1,25},{... | collective-permute-start | bytes 393224 | tf_op jit(solution)/shard_map/ppermute | solution.py:344
  (25 other events, 158.7 us)

commit v11 on v10

--- a/solution.py
+++ b/solution.py
@@ -409,7 +409,7 @@
     there = {item: swap_core(here[item], zs) for item in here if item not in late}
 
     pace = [[], ["kvc1"], ["kvc3"], []]
-    swapped = [[], ["kvc0", "q0"], ["q1", "q3"], ["kvc1"]]
+    swapped = [[], ["q0"], ["kvc0", "q1", "q3"], ["kvc1"]]
     gain4 = gain.reshape(4, 1, width)
     half = rows // 2
     normed, diag0, diag1 = None, None, None

time: 183 us -> 179 us (0.978)
  starting transfers between devices: 54.1 us -> 39.8 us
  waiting for transfers between devices: 64.6 us -> 77.7 us
  local copies, waits for them, and re-layouts: 12.4 us -> 9.6 us
    ppermute x13, waiting for transfers between devices: 48.9 us -> 66.6 us  [shift_z(): return lax.ppermute(value, 'seq', pairs)]
    ppermute x13, starting transfers between devices: 32 us -> 15.7 us  [shift_z(): return lax.ppermute(value, 'seq', pairs)]
    unnamed x58 -> x48, local copies, waits for them, and re-layouts: 7.52 us -> 3.52 us
    ppermute x16, waiting for transfers between devices: 12.1 us -> 9.02 us  [swap_chan(): return lax.ppermute(value, 'chan', [(c, c ^ bit) for c in range(4)])]
    ppermute x16, starting transfers between devices: 16.9 us -> 19.3 us  [swap_chan(): return lax.ppermute(value, 'chan', [(c, c ^ bit) for c in range(4)])]
  transfers between devices with their start and end apart: 44 -> 44, of which waited for: 18 -> 19; matrix products, arithmetic and copies ran while one was open for 3% -> 5% of each run, Pallas kernels for 24% -> 24%
where the time goes in v11:
time: 179 us
  waiting for transfers between devices  77.7 us (43%)
  Pallas kernels  47.4 us (26%)
  starting transfers between devices  39.8 us (22%)
  local copies, waits for them, and re-layouts  9.6 us (5%)
  other arithmetic  3.56 us (2%)
    ppermute x13, waiting for transfers between devices, shift_z(): return lax.ppermute(value, 'seq', pairs)  66.6 us
    ppermute x16, starting transfers between devices, swap_chan(): return lax.ppermute(value, 'chan', [(c, c ^ bit) for c in range(4)])  19.3 us
    ppermute x13, starting transfers between devices, shift_z(): return lax.ppermute(value, 'seq', pairs)  15.7 us
    pallas_call x3, Pallas kernels, weigh(): pl.pallas_call(functools.partial(weigh_kernel, blocks), in_specs=[SMEM] +...  14.2 us
    pallas_call x5, Pallas kernels, project(): pl.pallas_call(functools.partial(project_kernel, shifts, slabs, parts, zs...  10.2 us
    ppermute x16, waiting for transfers between devices, swap_chan(): return lax.ppermute(value, 'chan', [(c, c ^ bit) for c in range(4)])  9.02 us
    pallas_call x4, Pallas kernels, norm(): pl.pallas_call(functools.partial(norm_kernel, j), in_specs=[SMEM] + [VMEM...  8.28 us
    pallas_call x3, Pallas kernels, mix(): pl.pallas_call(functools.partial(mix_kernel, shifts), in_specs=[SMEM] + [...  6.75 us
  transfers between devices with their start and end apart: 44, of which 19 were waited for; matrix products, arithmetic and copies ran while one was open for 5% of the time, Pallas kernels for 24%

profile of v11, /device:TPU:0, one launch (start us, length us, event | category | flops | bytes accessed | tf_op | source)
XLA Modules:
  0.0 178.8 jit_solution(6772871152971432654)
XLA Ops:
  1.2 2.4 %collective-permute-start = (bf16[128,1024]{1,0:T(8,128)(2,1)S(1)}, bf16[128,1024]{1,0:T(8,128)(2,1)S(1)}, u32[]{:S(2)}, u32[]{:S(2)}) collective-permute-start(bf16[128,1024]{1,0:T(8,128)(2,1)S(1)} %fusion), channel_id=1, source_target_pairs={{0,4},{4,8},{8,12},{12,16},{16,20},{20,24},{24,28},{1,5},{5,9},{9,... | collective-permute-start | bytes 786440 | tf_op jit(solution)/shard_map/ppermute | solution.py:388
  4.8 2.6 %collective-permute-start.1 = (bf16[512,256]{1,0:T(8,128)(2,1)S(1)}, bf16[512,256]{1,0:T(8,128)(2,1)S(1)}, u32[]{:S(2)}, u32[]{:S(2)}) collective-permute-start(bf16[512,256]{1,0:T(8,128)(2,1)S(1)} %get-tuple-element.116), channel_id=1, source_target_pairs={{0,8},{4,12},{8,16},{12,20},{16,24},{20,28},{24,0},{28,4},{1,9},{5... | collective-permute-start | bytes 786440 | tf_op jit(solution)/shard_map/ppermute | solution.py:344
  7.4 2.1 %collective-permute-start.5 = (bf16[512,256]{1,0:T(8,128)(2,1)S(1)}, bf16[512,256]{1,0:T(8,128)(2,1)S(1)}, u32[]{:S(2)}, u32[]{:S(2)}) collective-permute-start(bf16[512,256]{1,0:T(8,128)(2,1)S(1)} %get-tuple-element.115), channel_id=1, source_target_pairs={{0,24},{4,28},{8,0},{12,4},{16,8},{20,12},{24,16},{28,20},{1,25},{... | collective-permute-start | bytes 786440 | tf_op jit(solution)/shard_map/ppermute | solution.py:344
  9.6 6.0 %hyena_filters.1.own_ref = bf16[256,1024]{1,0:T(8,128)(2,1)S(1)} custom-call(bf16[3,256,1024]{2,1,0:T(8,128)(2,1)S(1)} %bitcast.33, bf16[128,1024]{1,0:T(8,128)(2,1)S(1)} %pad_select_fusion.halo_ref, f32[64,128]{1,0:T(8,128)S(1)} %copy-done.12), custom_call_target="tpu_custom_call" | custom-call | flops 1 | bytes 1 | tf_op jit(solution)/shard_map/hyena_filters/pallas_call | solution.py:80
  15.9 6.2 %collective-permute-done.5.refs_2_ = bf16[512,256]{1,0:T(8,128)(2,1)S(1)} collective-permute-done((bf16[512,256]{1,0:T(8,128)(2,1)S(1)}, bf16[512,256]{1,0:T(8,128)(2,1)S(1)}, u32[]{:S(2)}, u32[]{:S(2)}) %collective-permute-start.5) | collective-permute-done | bytes 262176 | tf_op jit(solution)/shard_map/ppermute | solution.py:344
  22.8 1.4 collective-permute-start.6
  24.2 1.5 collective-permute-start.8
  25.7 1.9 %pad_dynamic-slice_fusion = (bf16[160,256]{1,0:T(8,128)(2,1)S(1)}, bf16[160,256]{1,0:T(8,128)(2,1)}, bf16[160,256]{1,0:T(8,128)(2,1)}, bf16[160,256]{1,0:T(8,128...) fusion(s32[]{:T(128)S(6)} %select_n.84, ...), kind=kLoop, calls=%fused_computation.19 | loop fusion | bytes 1277968 | tf_op jit(solution)/shard_map/dynamic_slice | solution.py:383
  28.3 3.0 %dynamic-slice_bitcast_fusion = (bf16[512,256]{1,0:T(8,128)(2,1)}, bf16[512,256]{1,0:T(8,128)(2,1)}, bf16[512,256]{1,0:T(8,128)(2,1)}, bf16[512,256]{1,0:T(8,128...) fusion(bf16[3,512,1024]{2,1,0:T(8,128)(2,1)} %bitcast.38, ...), kind=kLoop, calls=%fused_computation.6 | loop fusion | bytes 5242896 | tf_op jit(solution)/shard_map/squeeze | solution.py:378
  31.2 5.5 %collective-permute-done.6.x_ref = bf16[256,1024]{1,0:T(8,128)(2,1)S(1)} collective-permute-done((bf16[256,1024]{1,0:T(8,128)(2,1)S(1)}, bf16[256,1024]{1,0:T(8,128)(2,1)S(1)}, u32[]{:S(2)}, u32[]{:S(2)}) %collective-permute-start.6) | collective-permute-done | bytes 524320 | tf_op jit(solution)/shard_map/ppermute | solution.py:352
  36.7 1.5 collective-permute-start.7
  38.3 1.6 collective-permute-start.9
  41.4 1.5 collective-permute-done.2.own_ref
  42.9 1.5 collective-permute-done.7.d0_ref
  47.5 1.3 collective-permute-start.10
  50.8 1.9 %norm.4.rest_0_ = bf16[4,4,256,1024]{3,2,1,0:T(8,128)(2,1)S(1)} custom-call(s32[3]{0:T(128)S(1)} %pad_add_fusion.place_ref, bf16[256,1024]{1,0:T(8,128)(2,1)S(1)} %hyena_filters.1.own_ref, bf16[256,1024]{1,0:T(8,128)(2,1)S(1)} %collective-permute-done.6.x_ref, bf16[256,1024]{1,0:T(8,128)(2,1)S(1)} %copy-done.2, bf16[128,1024]{1,0:T(8,128)(2,1)S(1)} %copy-done.8, ...), custom_call_target="tpu_custom_call" | custom-call | flops 1 | bytes 1 | tf_op jit(solution)/shard_map/norm/pallas_call | solution.py:119
  53.0 8.2 %collective-permute-done.12.refs_7_.refs_1_ = bf16[1344,256]{1,0:T(8,128)(2,1)S(1)} collective-permute-done((bf16[1344,256]{1,0:T(8,128)(2,1)}, bf16[1344,256]{1,0:T(8,128)(2,1)S(1)}, u32[]{:S(2)}, u32[]{:S(2)}) %collective-permute-start.12) | collective-permute-done | bytes 688160 | tf_op jit(solution)/shard_map/ppermute | solution.py:344
  63.1 7.2 %collective-permute-done.3.own_ref = bf16[256,1024]{1,0:T(8,128)(2,1)S(1)} collective-permute-done((bf16[256,1024]{1,0:T(8,128)(2,1)}, bf16[256,1024]{1,0:T(8,128)(2,1)S(1)}, u32[]{:S(2)}, u32[]{:S(2)}) %collective-permute-start.3) | collective-permute-done | bytes 524320 | tf_op jit(solution)/shard_map/ppermute | solution.py:344
  70.3 1.7 collective-permute-start.20
  73.8 1.5 collective-permute-done.19.refs_5_
  75.6 2.4 %norm.5.rest_0_ = bf16[4,4,256,1024]{3,2,1,0:T(8,128)(2,1)S(1)} custom-call(s32[3]{0:T(128)S(1)} %pad_add_fusion.place_ref, bf16[256,1024]{1,0:T(8,128)(2,1)} %collective-permute-done.2.own_ref, bf16[256,1024]{1,0:T(8,128)(2,1)S(1)} %collective-permute-done.10.x_ref, ...), custom_call_target="tpu_custom_call", output_to_operand_aliasing={{}: (7, {})} | custom-call | flops 1 | bytes 1 | tf_op jit(solution)/shard_map/norm/pallas_call | solution.py:119
  78.0 9.9 %collective-permute-done.20.refs_8_.refs_3_ = bf16[1344,256]{1,0:T(8,128)(2,1)S(1)} collective-permute-done((bf16[1344,256]{1,0:T(8,128)(2,1)S(1)}, bf16[1344,256]{1,0:T(8,128)(2,1)S(1)}, u32[]{:S(2)}, u32[]{:S(2)}) %collective-permute-start.20) | collective-permute-done | bytes 688160 | tf_op jit(solution)/shard_map/ppermute | solution.py:344
  88.6 1.3 collective-permute-start.21
  90.4 7.4 %collective-permute-done.4.own_ref = bf16[256,1024]{1,0:T(8,128)(2,1)S(1)} collective-permute-done((bf16[256,1024]{1,0:T(8,128)(2,1)S(1)}, bf16[256,1024]{1,0:T(8,128)(2,1)S(1)}, u32[]{:S(2)}, u32[]{:S(2)}) %collective-permute-start.4) | collective-permute-done | bytes 524320 | tf_op jit(solution)/shard_map/ppermute | solution.py:344
  98.6 1.5 collective-permute-start.24
  100.2 1.9 %collective-permute-start.31 = (bf16[832,256]{1,0:T(8,128)(2,1)S(1)}, bf16[832,256]{1,0:T(8,128)(2,1)S(1)}, u32[]{:S(2)}, u32[]{:S(2)}) collective-permute-start(bf16[832,256]{1,0:T(8,128)(2,1)S(1)} %pad_maximum_fusion.3), channel_id=1, source_target_pairs={{0,16},{4,20},{8,24},{12,28},{16,0},{20,4},{24,8},{28,12},{1,17},{... | collective-permute-start | bytes 1277960 | tf_op jit(solution)/shard_map/ppermute | solution.py:344
  102.1 1.9 %norm.6.normed_ref.rest_0_ = bf16[4,4,256,1024]{3,2,1,0:T(8,128)(2,1)S(1)} custom-call(s32[3]{0:T(128)S(1)} %pad_add_fusion.place_ref, bf16[256,1024]{1,0:T(8,128)(2,1)S(1)} %collective-permute-done.3.own_ref, bf16[256,1024]{1,0:T(8,128)(2,1)S(1)} %collective-permute-done.16.x_ref, ...), custom_call_target="tpu_custom_call", output_to_operand_aliasing={{}: (7, {})} | custom-call | flops 1 | bytes 1 | tf_op jit(solution)/shard_map/norm/pallas_call | solution.py:119
  104.0 4.5 %project.5 = (f32[4,256,256]{2,1,0:T(8,128)S(1)}, f32[4,256,256]{2,1,0:T(8,128)S(1)}, f32[4,256,256]{2,1,0:T(8,128)S(1)}) custom-call(s32[3]{0:T(128)S(1)} %pad_add_fusion.place_ref, bf16[4,4,256,1024]{3,2,1,0:T(8,128)(2,1)S(1)} %norm.6.normed_ref.rest_0_, bf16[512,256]{1,0:T(8,128)(2,1)S(1)} %get-tuple-element.114.refs_0_, ...), custom_call_target="tpu_custom_call" | custom-call | flops 1 | bytes 1 | tf_op jit(solution)/shard_map/project/pallas_call | solution.py:161
  108.5 1.5 collective-permute-done.27.y_ref
  109.9 1.3 collective-permute-start.29
  111.3 1.8 collective-permute-start.28
  113.0 7.6 %collective-permute-done.31.refs_2_.refs_0_ = bf16[832,256]{1,0:T(8,128)(2,1)S(1)} collective-permute-done((bf16[832,256]{1,0:T(8,128)(2,1)S(1)}, bf16[832,256]{1,0:T(8,128)(2,1)S(1)}, u32[]{:S(2)}, u32[]{:S(2)}) %collective-permute-start.31) | collective-permute-done | bytes 426016 | tf_op jit(solution)/shard_map/ppermute | solution.py:344
  121.9 2.1 %norm.7.normed_ref = bf16[4,4,256,1024]{3,2,1,0:T(8,128)(2,1)S(1)} custom-call(s32[3]{0:T(128)S(1)} %pad_add_fusion.place_ref, bf16[256,1024]{1,0:T(8,128)(2,1)S(1)} %collective-permute-done.4.own_ref, bf16[256,1024]{1,0:T(8,128)(2,1)S(1)} %collective-permute-done.24.x_ref, ...), custom_call_target="tpu_custom_call", output_to_operand_aliasing={{}: (7, {})} | custom-call | flops 1 | bytes 1 | tf_op jit(solution)/shard_map/norm/pallas_call | solution.py:119
  124.0 2.0 %project.6 = (f32[4,256,256]{2,1,0:T(8,128)S(1)}, f32[4,256,256]{2,1,0:T(8,128)S(1)}, f32[4,256,256]{2,1,0:T(8,128)S(1)}) custom-call(s32[3]{0:T(128)S(1)} %pad_add_fusion.place_ref, bf16[4,4,256,1024]{3,2,1,0:T(8,128)(2,1)S(1)} %norm.7.normed_ref, ...), custom_call_target="tpu_custom_call", output_to_operand_aliasing={{0}: (14, {}), {1}: (15, {}), {2}: (16, {})} | custom-call | flops 1 | bytes 1 | tf_op jit(solution)/shard_map/project/pallas_call | solution.py:161
  127.3 8.6 %collective-permute-done.30.refs_0_ = bf16[512,256]{1,0:T(8,128)(2,1)S(1)} collective-permute-done((bf16[512,256]{1,0:T(8,128)(2,1)S(1)}, bf16[512,256]{1,0:T(8,128)(2,1)S(1)}, u32[]{:S(2)}, u32[]{:S(2)}) %collective-permute-start.30) | collective-permute-done | bytes 262176 | tf_op jit(solution)/shard_map/ppermute | solution.py:344
  137.6 1.3 project.8.q_ref
  138.9 6.3 %weigh.3 = (bf16[4,2,256,1216]{3,2,1,0:T(8,128)(2,1)S(1)}, bf16[4,2,4,256,512]{4,3,2,1,0:T(8,128)(2,1)S(1)}, f32[4,2,256,128]{3,2,1,0:T(8,128)S(1)}) custom-call(s32[3]{0:T(128)S(1)} %pad_add_fusion.place_ref, bf16[4,256,256]{2,1,0:T(8,128)(2,1)S(1)} %project.8.q_ref, bf16[1216,256]{1,0:T(8,128)(2,1)S(1)} %get-tuple-element.78.ck_ref, ...), custom_call_target="tpu_custom_call" | custom-call | flops 1 | bytes 1 | tf_op jit(solution)/shard_map/weigh/pallas_call | solution.py:236
  145.2 5.4 %collective-permute-done.38.refs_0_ = bf16[512,256]{1,0:T(8,128)(2,1)S(1)} collective-permute-done((bf16[512,256]{1,0:T(8,128)(2,1)S(1)}, bf16[512,256]{1,0:T(8,128)(2,1)S(1)}, u32[]{:S(2)}, u32[]{:S(2)}) %collective-permute-start.38) | collective-permute-done | bytes 262176 | tf_op jit(solution)/shard_map/ppermute | solution.py:344
  150.7 3.5 %weigh.4 = (bf16[4,2,256,1216]{3,2,1,0:T(8,128)(2,1)S(1)}, bf16[4,2,4,256,512]{4,3,2,1,0:T(8,128)(2,1)S(1)}, f32[4,2,256,128]{3,2,1,0:T(8,128)S(1)}) custom-call(s32[3]{0:T(128)S(1)} %pad_add_fusion.place_ref, bf16[4,256,256]{2,1,0:T(8,128)(2,1)S(1)} %project.8.q_ref, ...), custom_call_target="tpu_custom_call", output_to_operand_aliasing={{0}: (11, {}), {1}: (12, {}), {2}: (13, {})} | custom-call | flops 1 | bytes 1 | tf_op jit(solution)/shard_map/weigh/pallas_call | solution.py:236
  156.0 4.4 %weigh.5 = (bf16[4,2,256,1216]{3,2,1,0:T(8,128)(2,1)S(1)}, bf16[4,2,4,256,512]{4,3,2,1,0:T(8,128)(2,1)S(1)}, f32[4,2,256,128]{3,2,1,0:T(8,128)S(1)}) custom-call(s32[3]{0:T(128)S(1)} %pad_add_fusion.place_ref, bf16[4,256,256]{2,1,0:T(8,128)(2,1)S(1)} %project.8.q_ref, ...), custom_call_target="tpu_custom_call", output_to_operand_aliasing={{0}: (11, {}), {1}: (12, {}), {2}: (13, {})} | custom-call | flops 1 | bytes 1 | tf_op jit(solution)/shard_map/weigh/pallas_call | solution.py:236
  160.4 2.0 %mix.3 = bf16[256,256]{1,0:T(8,128)(2,1)S(1)} custom-call(s32[3]{0:T(128)S(1)} %pad_add_fusion.place_ref, bf16[4,2,256,1216]{3,2,1,0:T(8,128)(2,1)S(1)} %get-tuple-element.93.old_ref, bf16[4,2,4,256,512]{4,3,2,1,0:T(8,128)(2,1)S(1)} %get-tuple-element.94.new_ref, f32[4,2,256,128]{3,2,1,0:T(8,128)S(1)} %get-tuple-element.95.sum_ref, ...), custom_call_target="tpu_custom_call" | custom-call | flops 1 | bytes 1 | tf_op jit(solution)/shard_map/mix/pallas_call | solution.py:281
  162.4 3.4 %mix.4 = (bf16[256,256]{1,0:T(8,128)(2,1)S(1)}, bf16[256,256]{1,0:T(8,128)(2,1)S(1)}) custom-call(s32[3]{0:T(128)S(1)} %pad_add_fusion.place_ref, bf16[4,2,256,1216]{3,2,1,0:T(8,128)(2,1)S(1)} %get-tuple-element.93.old_ref, bf16[4,2,4,256,512]{4,3,2,1,0:T(8,128)(2,1)S(1)} %get-tuple-element.94.new_ref, f32[4,2,256,128]{3,2,1,0:T(8,128)S(1)} %get-tuple-element.95.sum_ref, ...), custom_call_target="tpu_custom_call" | custom-call | flops 1 | bytes 1 | tf_op jit(solution)/shard_map/mix/pallas_call | solution.py:281
  165.8 1.5 collective-permute-start.42
  167.3 2.4 %collective-permute-start.43 = (bf16[256,256]{1,0:T(8,128)(2,1)S(1)}, bf16[256,256]{1,0:T(8,128)(2,1)S(1)}, u32[]{:S(2)}, u32[]{:S(2)}) collective-permute-start(bf16[256,256]{1,0:T(8,128)(2,1)S(1)} %get-tuple-element.104), channel_id=1, source_target_pairs={{0,24},{4,28},{8,0},{12,4},{16,8},{20,12},{24,16},{28,20},{1,25},{... | collective-permute-start | bytes 393224 | tf_op jit(solution)/shard_map/ppermute | solution.py:344
  170.5 1.4 mix.5.refs_0_
  172.6 1.5 collective-permute-done.42.refs_1_
  174.1 1.9 %collective-permute-done.43.refs_3_ = bf16[256,256]{1,0:T(8,128)(2,1)S(1)} collective-permute-done((bf16[256,256]{1,0:T(8,128)(2,1)S(1)}, bf16[256,256]{1,0:T(8,128)(2,1)S(1)}, u32[]{:S(2)}, u32[]{:S(2)}) %collective-permute-start.43) | collective-permute-done | bytes 131104 | tf_op jit(solution)/shard_map/ppermute | solution.py:344
  176.7 1.9 %join.1 = bf16[256,1024]{1,0:T(8,128)(2,1)} custom-call(s32[3]{0:T(128)} %copy-done.11, bf16[256,256]{1,0:T(8,128)(2,1)} %copy-done.5, bf16[256,256]{1,0:T(8,128)(2,1)} %copy-done.22, bf16[256,256]{1,0:T(8,128)(2,1)} %copy-done.21, bf16[256,256]{1,0:T(8,128)(2,1)} %copy-done.23), custom_call_target="tpu_custom_call" | custom-call | tf_op jit(solution)/shard_map/join/pallas_call | solution.py:332
  (124 shorter events, 25.1 us)
Async XLA Ops:
  1.2 8.2 %collective-permute-start = (bf16[128,1024]{1,0:T(8,128)(2,1)S(1)}, bf16[128,1024]{1,0:T(8,128)(2,1)S(1)}, u32[]{:S(2)}, u32[]{:S(2)}) collective-permute-start(bf16[128,1024]{1,0:T(8,128)(2,1)S(1)} %fusion), channel_id=1, source_target_pairs={{0,4},{4,8},{8,12},{12,16},{16,20},{20,24},{24,28},{1,5},{5,9},{9,... | collective-permute-start | bytes 786440 | tf_op jit(solution)/shard_map/ppermute | solution.py:388
  4.8 11.1 %collective-permute-start.1 = (bf16[512,256]{1,0:T(8,128)(2,1)S(1)}, bf16[512,256]{1,0:T(8,128)(2,1)S(1)}, u32[]{:S(2)}, u32[]{:S(2)}) collective-permute-start(bf16[512,256]{1,0:T(8,128)(2,1)S(1)} %get-tuple-element.116), channel_id=1, source_target_pairs={{0,8},{4,12},{8,16},{12,20},{16,24},{20,28},{24,0},{28,4},{1,9},{5... | collective-permute-start | bytes 786440 | tf_op jit(solution)/shard_map/ppermute | solution.py:344
  7.4 14.7 %collective-permute-start.5 = (bf16[512,256]{1,0:T(8,128)(2,1)S(1)}, bf16[512,256]{1,0:T(8,128)(2,1)S(1)}, u32[]{:S(2)}, u32[]{:S(2)}) collective-permute-start(bf16[512,256]{1,0:T(8,128)(2,1)S(1)} %get-tuple-element.115), channel_id=1, source_target_pairs={{0,24},{4,28},{8,0},{12,4},{16,8},{20,12},{24,16},{28,20},{1,25},{... | collective-permute-start | bytes 786440 | tf_op jit(solution)/shard_map/ppermute | solution.py:344
  22.8 13.9 %collective-permute-start.6 = (bf16[256,1024]{1,0:T(8,128)(2,1)S(1)}, bf16[256,1024]{1,0:T(8,128)(2,1)S(1)}, u32[]{:S(2)}, u32[]{:S(2)}) collective-permute-start(bf16[256,1024]{1,0:T(8,128)(2,1)S(1)} %hyena_filters.1.own_ref), channel_id=1, source_target_pairs={{0,1},{1,0},{2,3},{3,2},{4,5},{5,4},{6,7},{7,6},{8,9},{9,8},{10,11... | collective-permute-start | bytes 1572872 | tf_op jit(solution)/shard_map/ppermute | solution.py:352
  24.2 14.1 %collective-permute-start.8 = (bf16[256,1024]{1,0:T(8,128)(2,1)S(1)}, bf16[256,1024]{1,0:T(8,128)(2,1)S(1)}, u32[]{:S(2)}, u32[]{:S(2)}) collective-permute-start(bf16[256,1024]{1,0:T(8,128)(2,1)S(1)} %hyena_filters.1.own_ref), channel_id=1, source_target_pairs={{0,2},{1,3},{2,0},{3,1},{4,6},{5,7},{6,4},{7,5},{8,10},{9,11},{10,... | collective-permute-start | bytes 1572872 | tf_op jit(solution)/shard_map/ppermute | solution.py:352
  27.6 15.3 %collective-permute-start.2 = (bf16[256,1024]{1,0:T(8,128)(2,1)S(1)}, bf16[256,1024]{1,0:T(8,128)(2,1)}, u32[]{:S(2)}, u32[]{:S(2)}) collective-permute-start(bf16[256,1024]{1,0:T(8,128)(2,1)S(1)} %hyena_filters.1.own_ref), channel_id=1, source_target_pairs={{0,8},{4,12},{8,16},{12,20},{16,24},{20,28},{24,0},{28,4},{1,9},{5... | collective-permute-start | bytes 1572872 | tf_op jit(solution)/shard_map/ppermute | solution.py:344
  36.7 7.7 %collective-permute-start.7 = (bf16[128,1024]{1,0:T(8,128)(2,1)S(1)}, bf16[128,1024]{1,0:T(8,128)(2,1)S(1)}, u32[]{:S(2)}, u32[]{:S(2)}) collective-permute-start(bf16[128,1024]{1,0:T(8,128)(2,1)S(1)} %slice.42), channel_id=1, source_target_pairs={{0,2},{1,3},{2,0},{3,1},{4,6},{5,7},{6,4},{7,5},{8,10},{9,11},{10,... | collective-permute-start | bytes 786440 | tf_op jit(solution)/shard_map/ppermute | solution.py:352
  38.3 7.4 %collective-permute-start.9 = (bf16[128,1024]{1,0:T(8,128)(2,1)S(1)}, bf16[128,1024]{1,0:T(8,128)(2,1)S(1)}, u32[]{:S(2)}, u32[]{:S(2)}) collective-permute-start(bf16[128,1024]{1,0:T(8,128)(2,1)S(1)} %slice.43), channel_id=1, source_target_pairs={{0,1},{1,0},{2,3},{3,2},{4,5},{5,4},{6,7},{7,6},{8,9},{9,8},{10,11... | collective-permute-start | bytes 786440 | tf_op jit(solution)/shard_map/ppermute | solution.py:352
  40.8 20.4 %collective-permute-start.12 = (bf16[1344,256]{1,0:T(8,128)(2,1)}, bf16[1344,256]{1,0:T(8,128)(2,1)S(1)}, u32[]{:S(2)}, u32[]{:S(2)}) collective-permute-start(bf16[1344,256]{1,0:T(8,128)(2,1)} %pad_maximum_fusion), channel_id=1, source_target_pairs={{0,8},{4,12},{8,16},{12,20},{16,24},{20,28},{24,0},{28,4},{1,9},{5... | collective-permute-start | bytes 2064392 | tf_op jit(solution)/shard_map/ppermute | solution.py:344
  46.4 14.8 %collective-permute-start.14 = (bf16[256,1024]{1,0:T(8,128)(2,1)}, bf16[256,1024]{1,0:T(8,128)(2,1)S(1)}, u32[]{:S(2)}, u32[]{:S(2)}) collective-permute-start(bf16[256,1024]{1,0:T(8,128)(2,1)} %collective-permute-done.2.own_ref), channel_id=1, source_target_pairs={{0,2},{1,3},{2,0},{3,1},{4,6},{5,7},{6,4},{7,5},{8,10},{9,11},{10,... | collective-permute-start | bytes 1572872 | tf_op jit(solution)/shard_map/ppermute | solution.py:352
  47.5 14.3 %collective-permute-start.10 = (bf16[256,1024]{1,0:T(8,128)(2,1)}, bf16[256,1024]{1,0:T(8,128)(2,1)S(1)}, u32[]{:S(2)}, u32[]{:S(2)}) collective-permute-start(bf16[256,1024]{1,0:T(8,128)(2,1)} %collective-permute-done.2.own_ref), channel_id=1, source_target_pairs={{0,1},{1,0},{2,3},{3,2},{4,5},{5,4},{6,7},{7,6},{8,9},{9,8},{10,11... | collective-permute-start | bytes 1572872 | tf_op jit(solution)/shard_map/ppermute | solution.py:352
  48.8 3.9 %collective-permute-start.11 = (bf16[512,256]{1,0:T(8,128)(2,1)S(1)}, bf16[512,256]{1,0:T(8,128)(2,1)S(1)}, u32[]{:S(2)}, u32[]{:S(2)}) collective-permute-start(bf16[512,256]{1,0:T(8,128)(2,1)S(1)} %get-tuple-element.114.refs_0_), channel_id=1, source_target_pairs={{0,4},{4,0},{8,12},{12,8},{16,20},{20,16},{24,28},{28,24},{1,5},{5... | collective-permute-start | bytes 786440 | tf_op jit(solution)/shard_map/ppermute | solution.py:348
  48.8 21.4 %collective-permute-start.3 = (bf16[256,1024]{1,0:T(8,128)(2,1)}, bf16[256,1024]{1,0:T(8,128)(2,1)S(1)}, u32[]{:S(2)}, u32[]{:S(2)}) collective-permute-start(bf16[256,1024]{1,0:T(8,128)(2,1)} %collective-permute-done.2.own_ref), channel_id=1, source_target_pairs={{0,8},{4,12},{8,16},{12,20},{16,24},{20,28},{24,0},{28,4},{1,9},{5... | collective-permute-start | bytes 1572872 | tf_op jit(solution)/shard_map/ppermute | solution.py:344
  49.6 120.9 %copy-start.11 = (s32[3]{0:T(128)}, s32[3]{0:T(128)S(1)}, u32[]{:S(2)}) copy-start(s32[3]{0:T(128)S(1)} %pad_add_fusion.place_ref) | copy-start | bytes 40
  52.7 21.0 %copy-start.4 = (bf16[512,256]{1,0:T(8,128)(2,1)S(1)}, bf16[512,256]{1,0:T(8,128)(2,1)}, u32[]{:S(2)}) copy-start(bf16[512,256]{1,0:T(8,128)(2,1)} %copy-done.3) | copy-start | bytes 786436
  52.8 25.2 %collective-permute-start.17 = (bf16[1344,256]{1,0:T(8,128)(2,1)S(1)}, bf16[1344,256]{1,0:T(8,128)(2,1)S(1)}, u32[]{:S(2)}, u32[]{:S(2)}) collective-permute-start(bf16[1344,256]{1,0:T(8,128)(2,1)S(1)} %pad_maximum_fusion.1.refs_6_.refs_0_), channel_id=1, source_target_pairs={{0,4},{4,0},{8,12},{12,8},{16,20},{20,16},{24,28},{28,24},{1,5},{5... | collective-permute-start | bytes 2064392 | tf_op jit(solution)/shard_map/ppermute | solution.py:348
  61.2 12.6 %collective-permute-start.18 = (bf16[512,256]{1,0:T(8,128)(2,1)S(1)}, bf16[512,256]{1,0:T(8,128)(2,1)S(1)}, u32[]{:S(2)}, u32[]{:S(2)}) collective-permute-start(bf16[512,256]{1,0:T(8,128)(2,1)S(1)} %collective-permute-done.1.refs_1_), channel_id=1, source_target_pairs={{0,4},{4,0},{8,12},{12,8},{16,20},{20,16},{24,28},{28,24},{1,5},{5... | collective-permute-start | bytes 786440 | tf_op jit(solution)/shard_map/ppermute | solution.py:348
  61.2 10.8 %collective-permute-start.15 = (bf16[128,1024]{1,0:T(8,128)(2,1)S(1)}, bf16[128,1024]{1,0:T(8,128)(2,1)S(1)}, u32[]{:S(2)}, u32[]{:S(2)}) collective-permute-start(bf16[128,1024]{1,0:T(8,128)(2,1)S(1)} %slice.35), channel_id=1, source_target_pairs={{0,1},{1,0},{2,3},{3,2},{4,5},{5,4},{6,7},{7,6},{8,9},{9,8},{10,11... | collective-permute-start | bytes 786440 | tf_op jit(solution)/shard_map/ppermute | solution.py:352
  61.8 10.2 %collective-permute-start.13 = (bf16[128,1024]{1,0:T(8,128)(2,1)S(1)}, bf16[128,1024]{1,0:T(8,128)(2,1)S(1)}, u32[]{:S(2)}, u32[]{:S(2)}) collective-permute-start(bf16[128,1024]{1,0:T(8,128)(2,1)S(1)} %slice.34), channel_id=1, source_target_pairs={{0,2},{1,3},{2,0},{3,1},{4,6},{5,7},{6,4},{7,5},{8,10},{9,11},{10,... | collective-permute-start | bytes 786440 | tf_op jit(solution)/shard_map/ppermute | solution.py:352
  63.1 37.1 %copy-start.13 = (bf16[512,256]{1,0:T(8,128)(2,1)S(1)}, bf16[512,256]{1,0:T(8,128)(2,1)}, u32[]{:S(2)}) copy-start(bf16[512,256]{1,0:T(8,128)(2,1)} %get-tuple-element.106) | copy-start | bytes 786436
  70.3 17.7 %collective-permute-start.20 = (bf16[1344,256]{1,0:T(8,128)(2,1)S(1)}, bf16[1344,256]{1,0:T(8,128)(2,1)S(1)}, u32[]{:S(2)}, u32[]{:S(2)}) collective-permute-start(bf16[1344,256]{1,0:T(8,128)(2,1)S(1)} %pad_maximum_fusion.2), channel_id=1, source_target_pairs={{0,24},{4,28},{8,0},{12,4},{16,8},{20,12},{24,16},{28,20},{1,25},{... | collective-permute-start | bytes 2064392 | tf_op jit(solution)/shard_map/ppermute | solution.py:344
  72.0 15.9 %collective-permute-start.22 = (bf16[256,1024]{1,0:T(8,128)(2,1)S(1)}, bf16[256,1024]{1,0:T(8,128)(2,1)S(1)}, u32[]{:S(2)}, u32[]{:S(2)}) collective-permute-start(bf16[256,1024]{1,0:T(8,128)(2,1)S(1)} %collective-permute-done.3.own_ref), channel_id=1, source_target_pairs={{0,2},{1,3},{2,0},{3,1},{4,6},{5,7},{6,4},{7,5},{8,10},{9,11},{10,... | collective-permute-start | bytes 1572872 | tf_op jit(solution)/shard_map/ppermute | solution.py:352
  72.5 16.0 %collective-permute-start.16 = (bf16[256,1024]{1,0:T(8,128)(2,1)S(1)}, bf16[256,1024]{1,0:T(8,128)(2,1)S(1)}, u32[]{:S(2)}, u32[]{:S(2)}) collective-permute-start(bf16[256,1024]{1,0:T(8,128)(2,1)S(1)} %collective-permute-done.3.own_ref), channel_id=1, source_target_pairs={{0,1},{1,0},{2,3},{3,2},{4,5},{5,4},{6,7},{7,6},{8,9},{9,8},{10,11... | collective-permute-start | bytes 1572872 | tf_op jit(solution)/shard_map/ppermute | solution.py:352
  73.8 1.5 collective-permute-start.19
  75.3 22.5 %collective-permute-start.4 = (bf16[256,1024]{1,0:T(8,128)(2,1)S(1)}, bf16[256,1024]{1,0:T(8,128)(2,1)S(1)}, u32[]{:S(2)}, u32[]{:S(2)}) collective-permute-start(bf16[256,1024]{1,0:T(8,128)(2,1)S(1)} %collective-permute-done.3.own_ref), channel_id=1, source_target_pairs={{0,8},{4,12},{8,16},{12,20},{16,24},{20,28},{24,0},{28,4},{1,9},{5... | collective-permute-start | bytes 1572872 | tf_op jit(solution)/shard_map/ppermute | solution.py:344
  88.0 9.8 %collective-permute-start.23 = (bf16[128,1024]{1,0:T(8,128)(2,1)S(1)}, bf16[128,1024]{1,0:T(8,128)(2,1)S(1)}, u32[]{:S(2)}, u32[]{:S(2)}) collective-permute-start(bf16[128,1024]{1,0:T(8,128)(2,1)S(1)} %slice.37), channel_id=1, source_target_pairs={{0,1},{1,0},{2,3},{3,2},{4,5},{5,4},{6,7},{7,6},{8,9},{9,8},{10,11... | collective-permute-start | bytes 786440 | tf_op jit(solution)/shard_map/ppermute | solution.py:352
  88.6 9.2 %collective-permute-start.21 = (bf16[128,1024]{1,0:T(8,128)(2,1)S(1)}, bf16[128,1024]{1,0:T(8,128)(2,1)S(1)}, u32[]{:S(2)}, u32[]{:S(2)}) collective-permute-start(bf16[128,1024]{1,0:T(8,128)(2,1)S(1)} %slice.36), channel_id=1, source_target_pairs={{0,2},{1,3},{2,0},{3,1},{4,6},{5,7},{6,4},{7,5},{8,10},{9,11},{10,... | collective-permute-start | bytes 786440 | tf_op jit(solution)/shard_map/ppermute | solution.py:352
  89.9 14.1 %collective-permute-start.25 = (bf16[1344,256]{1,0:T(8,128)(2,1)S(1)}, bf16[1344,256]{1,0:T(8,128)(2,1)S(1)}, u32[]{:S(2)}, u32[]{:S(2)}) collective-permute-start(bf16[1344,256]{1,0:T(8,128)(2,1)S(1)} %collective-permute-done.12.refs_7_.refs_1_), channel_id=1, source_target_pairs={{0,4},{4,0},{8,12},{12,8},{16,20},{20,16},{24,28},{28,24},{1,5},{5... | collective-permute-start | bytes 2064392 | tf_op jit(solution)/shard_map/ppermute | solution.py:348
  89.9 14.1 %collective-permute-start.26 = (bf16[1344,256]{1,0:T(8,128)(2,1)S(1)}, bf16[1344,256]{1,0:T(8,128)(2,1)S(1)}, u32[]{:S(2)}, u32[]{:S(2)}) collective-permute-start(bf16[1344,256]{1,0:T(8,128)(2,1)S(1)} %collective-permute-done.20.refs_8_.refs_3_), channel_id=1, source_target_pairs={{0,4},{4,0},{8,12},{12,8},{16,20},{20,16},{24,28},{28,24},{1,5},{5... | collective-permute-start | bytes 2064392 | tf_op jit(solution)/shard_map/ppermute | solution.py:348
  97.8 12.1 %collective-permute-start.27 = (bf16[256,1024]{1,0:T(8,128)(2,1)S(1)}, bf16[256,1024]{1,0:T(8,128)(2,1)S(1)}, u32[]{:S(2)}, u32[]{:S(2)}) collective-permute-start(bf16[256,1024]{1,0:T(8,128)(2,1)S(1)} %collective-permute-done.4.own_ref), channel_id=1, source_target_pairs={{0,2},{1,3},{2,0},{3,1},{4,6},{5,7},{6,4},{7,5},{8,10},{9,11},{10,... | collective-permute-start | bytes 1572872 | tf_op jit(solution)/shard_map/ppermute | solution.py:352
  98.6 12.6 %collective-permute-start.24 = (bf16[256,1024]{1,0:T(8,128)(2,1)S(1)}, bf16[256,1024]{1,0:T(8,128)(2,1)S(1)}, u32[]{:S(2)}, u32[]{:S(2)}) collective-permute-start(bf16[256,1024]{1,0:T(8,128)(2,1)S(1)} %collective-permute-done.4.own_ref), channel_id=1, source_target_pairs={{0,1},{1,0},{2,3},{3,2},{4,5},{5,4},{6,7},{7,6},{8,9},{9,8},{10,11... | collective-permute-start | bytes 1572872 | tf_op jit(solution)/shard_map/ppermute | solution.py:352
  100.2 20.5 %collective-permute-start.31 = (bf16[832,256]{1,0:T(8,128)(2,1)S(1)}, bf16[832,256]{1,0:T(8,128)(2,1)S(1)}, u32[]{:S(2)}, u32[]{:S(2)}) collective-permute-start(bf16[832,256]{1,0:T(8,128)(2,1)S(1)} %pad_maximum_fusion.3), channel_id=1, source_target_pairs={{0,16},{4,20},{8,24},{12,28},{16,0},{20,4},{24,8},{28,12},{1,17},{... | collective-permute-start | bytes 1277960 | tf_op jit(solution)/shard_map/ppermute | solution.py:344
  104.0 16.7 %copy-start.19 = (bf16[512,256]{1,0:T(8,128)(2,1)S(1)}, bf16[512,256]{1,0:T(8,128)(2,1)}, u32[]{:S(2)}) copy-start(bf16[512,256]{1,0:T(8,128)(2,1)} %get-tuple-element.75) | copy-start | bytes 786436
  109.9 10.7 %collective-permute-start.29 = (bf16[128,1024]{1,0:T(8,128)(2,1)S(1)}, bf16[128,1024]{1,0:T(8,128)(2,1)S(1)}, u32[]{:S(2)}, u32[]{:S(2)}) collective-permute-start(bf16[128,1024]{1,0:T(8,128)(2,1)S(1)} %slice.39), channel_id=1, source_target_pairs={{0,1},{1,0},{2,3},{3,2},{4,5},{5,4},{6,7},{7,6},{8,9},{9,8},{10,11... | collective-permute-start | bytes 786440 | tf_op jit(solution)/shard_map/ppermute | solution.py:352
  111.3 9.4 %collective-permute-start.28 = (bf16[128,1024]{1,0:T(8,128)(2,1)S(1)}, bf16[128,1024]{1,0:T(8,128)(2,1)S(1)}, u32[]{:S(2)}, u32[]{:S(2)}) collective-permute-start(bf16[128,1024]{1,0:T(8,128)(2,1)S(1)} %slice.38), channel_id=1, source_target_pairs={{0,2},{1,3},{2,0},{3,1},{4,6},{5,7},{6,4},{7,5},{8,10},{9,11},{10,... | collective-permute-start | bytes 786440 | tf_op jit(solution)/shard_map/ppermute | solution.py:352
  120.7 5.3 %collective-permute-start.32 = (bf16[832,256]{1,0:T(8,128)(2,1)S(1)}, bf16[832,256]{1,0:T(8,128)(2,1)S(1)}, u32[]{:S(2)}, u32[]{:S(2)}) collective-permute-start(bf16[832,256]{1,0:T(8,128)(2,1)S(1)} %collective-permute-done.31.refs_2_.refs_0_), channel_id=1, source_target_pairs={{0,4},{4,0},{8,12},{12,8},{16,20},{20,16},{24,28},{28,24},{1,5},{5... | collective-permute-start | bytes 1277960 | tf_op jit(solution)/shard_map/ppermute | solution.py:348
  120.7 15.2 %collective-permute-start.30 = (bf16[512,256]{1,0:T(8,128)(2,1)S(1)}, bf16[512,256]{1,0:T(8,128)(2,1)S(1)}, u32[]{:S(2)}, u32[]{:S(2)}) collective-permute-start(bf16[512,256]{1,0:T(8,128)(2,1)S(1)} %copy-done.19), channel_id=1, source_target_pairs={{0,16},{4,20},{8,24},{12,28},{16,0},{20,4},{24,8},{28,12},{1,17},{... | collective-permute-start | bytes 786440 | tf_op jit(solution)/shard_map/ppermute | solution.py:344
  135.9 1.5 collective-permute-start.33
  135.9 14.7 %collective-permute-start.38 = (bf16[512,256]{1,0:T(8,128)(2,1)S(1)}, bf16[512,256]{1,0:T(8,128)(2,1)S(1)}, u32[]{:S(2)}, u32[]{:S(2)}) collective-permute-start(bf16[512,256]{1,0:T(8,128)(2,1)S(1)} %copy-done.18), channel_id=1, source_target_pairs={{0,16},{4,20},{8,24},{12,28},{16,0},{20,4},{24,8},{28,12},{1,17},{... | collective-permute-start | bytes 786440 | tf_op jit(solution)/shard_map/ppermute | solution.py:344
  135.9 2.9 %collective-permute-start.34 = (bf16[256,256]{1,0:T(8,128)(2,1)S(1)}, bf16[256,256]{1,0:T(8,128)(2,1)S(1)}, u32[]{:S(2)}, u32[]{:S(2)}) collective-permute-start(bf16[256,256]{1,0:T(8,128)(2,1)S(1)} %get-tuple-element.81.refs_0_), channel_id=1, source_target_pairs={{0,4},{4,0},{8,12},{12,8},{16,20},{20,16},{24,28},{28,24},{1,5},{5... | collective-permute-start | bytes 393224 | tf_op jit(solution)/shard_map/ppermute | solution.py:348
  136.4 2.4 %collective-permute-start.35 = (bf16[256,256]{1,0:T(8,128)(2,1)S(1)}, bf16[256,256]{1,0:T(8,128)(2,1)S(1)}, u32[]{:S(2)}, u32[]{:S(2)}) collective-permute-start(bf16[256,256]{1,0:T(8,128)(2,1)S(1)} %get-tuple-element.84.refs_1_), channel_id=1, source_target_pairs={{0,4},{4,0},{8,12},{12,8},{16,20},{20,16},{24,28},{28,24},{1,5},{5... | collective-permute-start | bytes 393224 | tf_op jit(solution)/shard_map/ppermute | solution.py:348
  136.5 2.4 %collective-permute-start.36 = (bf16[256,256]{1,0:T(8,128)(2,1)S(1)}, bf16[256,256]{1,0:T(8,128)(2,1)S(1)}, u32[]{:S(2)}, u32[]{:S(2)}) collective-permute-start(bf16[256,256]{1,0:T(8,128)(2,1)S(1)} %get-tuple-element.85.refs_2_), channel_id=1, source_target_pairs={{0,4},{4,0},{8,12},{12,8},{16,20},{20,16},{24,28},{28,24},{1,5},{5... | collective-permute-start | bytes 393224 | tf_op jit(solution)/shard_map/ppermute | solution.py:348
  137.5 1.4 collective-permute-start.37
  150.6 3.6 %collective-permute-start.39 = (bf16[512,256]{1,0:T(8,128)(2,1)S(1)}, bf16[512,256]{1,0:T(8,128)(2,1)S(1)}, u32[]{:S(2)}, u32[]{:S(2)}) collective-permute-start(bf16[512,256]{1,0:T(8,128)(2,1)S(1)} %collective-permute-done.38.refs_0_), channel_id=1, source_target_pairs={{0,4},{4,0},{8,12},{12,8},{16,20},{20,16},{24,28},{28,24},{1,5},{5... | collective-permute-start | bytes 786440 | tf_op jit(solution)/shard_map/ppermute | solution.py:348
  155.5 4.9 %collective-permute-start.40 = (bf16[4,256,256]{2,1,0:T(8,128)(2,1)S(1)}, bf16[4,256,256]{2,1,0:T(8,128)(2,1)S(1)}, u32[]{:S(2)}, u32[]{:S(2)}) collective-permute-start(bf16[4,256,256]{2,1,0:T(8,128)(2,1)S(1)} %project.9.v_ref), channel_id=1, source_target_pairs={{0,4},{4,0},{8,12},{12,8},{16,20},{20,16},{24,28},{28,24},{1,5},{5... | collective-permute-start | bytes 1572872 | tf_op jit(solution)/shard_map/ppermute | solution.py:348
  162.4 8.1 %collective-permute-start.41 = (bf16[256,256]{1,0:T(8,128)(2,1)S(1)}, bf16[256,256]{1,0:T(8,128)(2,1)S(1)}, u32[]{:S(2)}, u32[]{:S(2)}) collective-permute-start(bf16[256,256]{1,0:T(8,128)(2,1)S(1)} %mix.3), channel_id=1, source_target_pairs={{0,16},{4,20},{8,24},{12,28},{16,0},{20,4},{24,8},{28,12},{1,17},{... | collective-permute-start | bytes 393224 | tf_op jit(solution)/shard_map/ppermute | solution.py:344
  165.8 8.3 %collective-permute-start.42 = (bf16[256,256]{1,0:T(8,128)(2,1)S(1)}, bf16[256,256]{1,0:T(8,128)(2,1)S(1)}, u32[]{:S(2)}, u32[]{:S(2)}) collective-permute-start(bf16[256,256]{1,0:T(8,128)(2,1)S(1)} %get-tuple-element.102), channel_id=1, source_target_pairs={{0,8},{4,12},{8,16},{12,20},{16,24},{20,28},{24,0},{28,4},{1,9},{5... | collective-permute-start | bytes 393224 | tf_op jit(solution)/shard_map/ppermute | solution.py:344
  167.3 8.7 %collective-permute-start.43 = (bf16[256,256]{1,0:T(8,128)(2,1)S(1)}, bf16[256,256]{1,0:T(8,128)(2,1)S(1)}, u32[]{:S(2)}, u32[]{:S(2)}) collective-permute-start(bf16[256,256]{1,0:T(8,128)(2,1)S(1)} %get-tuple-element.104), channel_id=1, source_target_pairs={{0,24},{4,28},{8,0},{12,4},{16,8},{20,12},{24,16},{28,20},{1,25},{... | collective-permute-start | bytes 393224 | tf_op jit(solution)/shard_map/ppermute | solution.py:344
  (20 other events, 118.3 us)

commit v12 on v3

--- a/solution.py
+++ b/solution.py
@@ -166,12 +166,6 @@
 NT = (((1,), (1,)), ((), ()))
 
 
-def lanes(op, s):
-    full = s.shape[1] - s.shape[1] % LANES
-    rest = s[:, full:] if full < s.shape[1] else None
-    return functools.reduce(op, [s[:, i : i + LANES] for i in range(0, full, LANES)]), rest
-
-
 def attend_kernel(shifts, place_ref, q_ref, k_ref, v_ref, ks_ref, vs_ref, ck_ref, cv_ref, *refs):
     outs, (old, new) = refs[: len(shifts)], refs[len(shifts) :]
     z, core = place_ref[1], place_ref[2]
@@ -182,40 +176,42 @@
     hcols = [slice(h * HEAD, (h + 1) * HEAD) for h in heads]
     row = lax.broadcasted_iota(jnp.int32, (rows, rows), 0)
     col = lax.broadcasted_iota(jnp.int32, (rows, rows), 1)
-    causal = col <= row
+    causal = row <= col
+
+    def score(key, query):
+        return lax.dot_general(key, query, NT, preferred_element_type=F32)
+
+    def mix(value, probs):
+        return lax.dot_general(value, probs, (((0,), (0,)), ((), ())), preferred_element_type=F32)
+
+    def fold(op, s):
+        return op(s.reshape(s.shape[0] // 8, 8, s.shape[1]), axis=0)
 
     for shift, out_ref in zip(shifts, outs):
         block = lax.rem(z + shift, zs)
         mine = lax.rem(zs - shift, zs)
         queries = [q_ref[mine, :, hcol] for hcol in hcols]
 
-        def score(b, tops, diagonal):
+        def scores(b, tops, diagonal):
             at = lax.rem(z + zs - b, zs)
             result = []
             for h, top in zip(heads, tops):
-                s = lax.dot_general(queries[h], k_ref[at, :, hcols[h]], NT, preferred_element_type=F32)
-                t = lax.dot_general(queries[h], ks_ref[at, :, hcols[h]], NT, preferred_element_type=F32)
+                s, t = score(k_ref[at, :, hcols[h]], queries[h]), score(ks_ref[at, :, hcols[h]], queries[h])
                 if diagonal:
                     s, t = jnp.where(causal, s, low), jnp.where(core == 1, t, low)
-                new[h, b, :, :rows] = s
-                new[h, b, :, rows:] = t
-                folded = jnp.maximum(lanes(jnp.maximum, s)[0], lanes(jnp.maximum, t)[0])
-                result.append(jnp.maximum(top, folded))
+                new[h, b, :rows] = s
+                new[h, b, rows:] = t
+                result.append(jnp.maximum(top, jnp.maximum(fold(jnp.max, s), fold(jnp.max, t))))
             return tuple(result)
 
-        tops, ends = [], []
+        tops = []
         for h in heads:
-            s = lax.dot_general(queries[h], ck_ref[:, hcols[h]], NT, preferred_element_type=F32)
+            s = score(ck_ref[:, hcols[h]], queries[h])
             old[h] = s
-            folded, rest = lanes(jnp.maximum, s)
-            tops.append(folded)
-            ends.append(low if rest is None else jnp.max(rest, axis=-1, keepdims=True))
-        tops = lax.fori_loop(0, block, functools.partial(score, diagonal=False), tuple(tops))
-        tops = score(block, tops, True)
-        tops = [
-            jnp.maximum(jnp.max(top, axis=-1, keepdims=True), end) * factor
-            for top, end in zip(tops, ends)
-        ]
+            tops.append(fold(jnp.max, s))
+        tops = lax.fori_loop(0, block, functools.partial(scores, diagonal=False), tuple(tops))
+        tops = scores(block, tops, True)
+        tops = [jnp.max(top, axis=0, keepdims=True) * factor for top in tops]
 
         def weigh(b, state):
             at = lax.rem(z + zs - b, zs)
@@ -223,23 +219,18 @@
             for h, (total, summed) in zip(heads, state):
                 weights = jnp.exp2(new[h, b] * factor - tops[h])
                 probs = weights.astype(BF16)
-                summed += jnp.dot(probs[:, :rows], v_ref[at, :, hcols[h]], preferred_element_type=F32)
-                summed += jnp.dot(probs[:, rows:], vs_ref[at, :, hcols[h]], preferred_element_type=F32)
-                result.append((total + lanes(jnp.add, weights)[0], summed))
+                summed += mix(v_ref[at, :, hcols[h]], probs[:rows]) + mix(vs_ref[at, :, hcols[h]], probs[rows:])
+                result.append((total + fold(jnp.sum, weights), summed))
             return tuple(result)
 
-        state, ends = [], []
+        state = []
         for h in heads:
             weights = jnp.exp2(old[h] * factor - tops[h])
-            folded, rest = lanes(jnp.add, weights)
-            ends.append(0.0 if rest is None else jnp.sum(rest, axis=-1, keepdims=True))
-            state.append(
-                (folded, jnp.dot(weights.astype(BF16), cv_ref[:, hcols[h]], preferred_element_type=F32))
-            )
+            state.append((fold(jnp.sum, weights), mix(cv_ref[:, hcols[h]], weights.astype(BF16))))
         state = lax.fori_loop(0, block + 1, weigh, tuple(state))
-        for h, (total, summed), end in zip(heads, state, ends):
-            total = jnp.sum(total, axis=-1, keepdims=True) + end
-            out_ref[:, hcols[h]] = (summed / total).astype(BF16)
+        for h, (total, summed) in zip(heads, state):
+            result = summed / jnp.sum(total, axis=0, keepdims=True)
+            out_ref[:, hcols[h]] = result.T.astype(BF16)
 
 
 def attend(shifts, place, q, k, v, k_sib, v_sib, ck, cv):
@@ -251,8 +242,8 @@
         out_specs=[VMEM] * len(shifts),
         out_shape=[jax.ShapeDtypeStruct((rows, cols), BF16)] * len(shifts),
         scratch_shapes=[
-            pltpu.VMEM((heads, rows, ck.shape[0]), F32),
-            pltpu.VMEM((heads, zs, rows, 2 * rows), F32),
+            pltpu.VMEM((heads, ck.shape[0], rows), F32),
+            pltpu.VMEM((heads, zs, 2 * rows, rows), F32),
         ],
         compiler_params=pltpu.CompilerParams(vmem_limit_bytes=20 * MIB),
         cost_estimate=BRIEF,
@@ -284,12 +275,17 @@
 
 
 def join_kernel(place_ref, *refs):
-    pieces, out_ref = refs[:-1], refs[-1]
+    pieces, (out_ref, sems) = refs[:-2], refs[-2:]
     zs = len(pieces)
     cols = pieces[0].shape[1]
+    copies = []
     for r, piece in enumerate(pieces):
-        at = lax.rem(place_ref[1] + zs - r, zs) * cols
-        out_ref[:, pl.ds(pl.multiple_of(at, cols), cols)] = piece[...]
+        at = pl.multiple_of(lax.rem(place_ref[1] + zs - r, zs) * cols, cols)
+        copies.append(pltpu.make_async_copy(piece, out_ref.at[:, pl.ds(at, cols)], sems.at[r]))
+    for copy in copies:
+        copy.start()
+    for copy in copies:
+        copy.wait()
 
 
 def join(place, pieces):
@@ -297,9 +293,10 @@
     out = (rows, cols * len(pieces))
     return pl.pallas_call(
         join_kernel,
-        in_specs=[SMEM] + [VMEM] * len(pieces),
-        out_specs=whole(out),
+        in_specs=[SMEM] + [pl.BlockSpec(memory_space=pl.ANY)] * len(pieces),
+        out_specs=pl.BlockSpec(memory_space=pl.ANY),
         out_shape=jax.ShapeDtypeStruct(out, BF16),
+        scratch_shapes=[pltpu.SemaphoreType.DMA((len(pieces),))],
         name="join",
     )(place, *pieces)
 

time: 170 us -> 186 us (1.094)
  Pallas kernels: 40.1 us -> 55.5 us
    pallas_call x1, Pallas kernels: 1.97 us -> 17.7 us  [join(): pl.pallas_call(join_kernel, in_specs=[SMEM] + [pl.BlockSpec(memory_space=...]
  transfers between devices with their start and end apart: 41 -> 41, of which waited for: 20 -> 20; matrix products, arithmetic and copies ran while one was open for 4% -> 3% of each run, Pallas kernels for 20% -> 18%
where the time goes in v12:
time: 186 us
  waiting for transfers between devices  79 us (42%)
  Pallas kernels  55.5 us (30%)
  starting transfers between devices  36.2 us (19%)
  local copies, waits for them, and re-layouts  11.7 us (6%)
  other arithmetic  2.46 us (1%)
    ppermute x13, waiting for transfers between devices, shift_z(): return lax.ppermute(value, 'seq', pairs)  62.1 us
    pallas_call x1, Pallas kernels, join(): pl.pallas_call(join_kernel, in_specs=[SMEM] + [pl.BlockSpec(memory_space=...  17.7 us
    ppermute x16, starting transfers between devices, swap_chan(): return lax.ppermute(value, 'chan', [(c, c ^ bit) for c in range(4)])  17.5 us
    ppermute x13, starting transfers between devices, shift_z(): return lax.ppermute(value, 'seq', pairs)  14.5 us
    pallas_call x3, Pallas kernels, attend(): pl.pallas_call(functools.partial(attend_kernel, shifts), in_specs=[SMEM]...  13.6 us
    ppermute x16, waiting for transfers between devices, swap_chan(): return lax.ppermute(value, 'chan', [(c, c ^ bit) for c in range(4)])  11.5 us
    pallas_call x4, Pallas kernels, project(): pl.pallas_call(functools.partial(project_kernel, shifts, zs, count), in_s...  9.86 us
    pallas_call x4, Pallas kernels, norm(): pl.pallas_call(functools.partial(norm_kernel, j), in_specs=[SMEM] + [VMEM...  8.27 us
  transfers between devices with their start and end apart: 41, of which 20 were waited for; matrix products, arithmetic and copies ran while one was open for 3% of the time, Pallas kernels for 18%

profile of v12, /device:TPU:0, one launch (start us, length us, event | category | flops | bytes accessed | tf_op | source)
XLA Modules:
  0.0 185.5 jit_solution(14929915087722090817)
XLA Ops:
  0.0 1.2 fusion
  1.2 2.4 %collective-permute-start = (bf16[128,1024]{1,0:T(8,128)(2,1)S(1)}, bf16[128,1024]{1,0:T(8,128)(2,1)S(1)}, u32[]{:S(2)}, u32[]{:S(2)}) collective-permute-start(bf16[128,1024]{1,0:T(8,128)(2,1)S(1)} %fusion), channel_id=1, source_target_pairs={{0,4},{4,8},{8,12},{12,16},{16,20},{20,24},{24,28},{1,5},{5,9},{9,... | collective-permute-start | bytes 786440 | tf_op jit(solution)/shard_map/ppermute | solution.py:350
  3.7 1.9 %dynamic-slice_bitcast_fusion.10 = (bf16[512,256]{1,0:T(8,128)(2,1)}, bf16[512,256]{1,0:T(8,128)(2,1)}) fusion(bf16[512,3,1024]{2,0,1:T(8,128)(2,1)} %param.11, s32[]{:T(128)S(6)} %select_n.80, s32[]{:T(128)S(6)} %select_n.78), kind=kLoop, calls=%fused_computation.16 | loop fusion | bytes 1048584 | tf_op jit(solution)/shard_map/squeeze | solution.py:340
  5.6 4.6 %collective-permute-start.5 = (bf16[512,256]{1,0:T(8,128)(2,1)}, bf16[512,256]{1,0:T(8,128)(2,1)S(1)}, u32[]{:S(2)}, u32[]{:S(2)}) collective-permute-start(bf16[512,256]{1,0:T(8,128)(2,1)} %get-tuple-element.77), channel_id=1, source_target_pairs={{0,24},{4,28},{8,0},{12,4},{16,8},{20,12},{24,16},{28,20},{1,25},{... | collective-permute-start | bytes 786440 | tf_op jit(solution)/shard_map/ppermute | solution.py:306
  10.3 6.0 %hyena_filters.1.own_ref = bf16[256,1024]{1,0:T(8,128)(2,1)S(1)} custom-call(bf16[3,256,1024]{2,1,0:T(8,128)(2,1)S(1)} %bitcast.33, bf16[128,1024]{1,0:T(8,128)(2,1)S(1)} %pad_select_fusion.halo_ref, f32[64,128]{1,0:T(8,128)S(1)} %copy-done.16), custom_call_target="tpu_custom_call" | custom-call | flops 1 | bytes 1 | tf_op jit(solution)/shard_map/hyena_filters/pallas_call | solution.py:80
  17.3 5.6 %collective-permute-done.1.refs_1_ = bf16[512,256]{1,0:T(8,128)(2,1)S(1)} collective-permute-done((bf16[512,256]{1,0:T(8,128)(2,1)}, bf16[512,256]{1,0:T(8,128)(2,1)S(1)}, u32[]{:S(2)}, u32[]{:S(2)}) %collective-permute-start.1) | collective-permute-done | bytes 262176 | tf_op jit(solution)/shard_map/ppermute | solution.py:306
  22.9 1.5 collective-permute-start.6
  24.4 1.5 collective-permute-start.8
  27.2 1.2 dynamic-slice_bitcast_fusion
  29.4 1.4 collective-permute-start.13
  30.7 6.5 %collective-permute-done.6.x_ref = bf16[256,1024]{1,0:T(8,128)(2,1)S(1)} collective-permute-done((bf16[256,1024]{1,0:T(8,128)(2,1)S(1)}, bf16[256,1024]{1,0:T(8,128)(2,1)S(1)}, u32[]{:S(2)}, u32[]{:S(2)}) %collective-permute-start.6) | collective-permute-done | bytes 524320 | tf_op jit(solution)/shard_map/ppermute | solution.py:314
  37.3 1.6 collective-permute-start.7
  38.9 1.6 collective-permute-start.9
  40.6 2.8 %collective-permute-done.2.own_ref = bf16[256,1024]{1,0:T(8,128)(2,1)} collective-permute-done((bf16[256,1024]{1,0:T(8,128)(2,1)S(1)}, bf16[256,1024]{1,0:T(8,128)(2,1)}, u32[]{:S(2)}, u32[]{:S(2)}) %collective-permute-start.2) | collective-permute-done | bytes 524320 | tf_op jit(solution)/shard_map/ppermute | solution.py:306
  43.4 2.0 %collective-permute-done.7.d0_ref = bf16[128,1024]{1,0:T(8,128)(2,1)S(1)} collective-permute-done((bf16[128,1024]{1,0:T(8,128)(2,1)S(1)}, bf16[128,1024]{1,0:T(8,128)(2,1)S(1)}, u32[]{:S(2)}, u32[]{:S(2)}) %collective-permute-start.7) | collective-permute-done | bytes 262176 | tf_op jit(solution)/shard_map/ppermute | solution.py:314
  47.4 1.1 collective-permute-start.15
  48.5 1.3 collective-permute-start.10
  49.8 1.7 collective-permute-done.12.refs_4_
  51.5 1.0 copy-done.2
  52.6 1.0 copy-done.4
  55.5 1.9 %norm.4.rest_0_ = bf16[4,4,256,1024]{3,2,1,0:T(8,128)(2,1)S(1)} custom-call(s32[3]{0:T(128)S(1)} %pad_add_fusion.place_ref, bf16[256,1024]{1,0:T(8,128)(2,1)S(1)} %hyena_filters.1.own_ref, bf16[256,1024]{1,0:T(8,128)(2,1)S(1)} %copy-done.2, bf16[256,1024]{1,0:T(8,128)(2,1)S(1)} %copy-done.4, bf16[128,1024]{1,0:T(8,128)(2,1)S(1)} %copy-done.12, ...), custom_call_target="tpu_custom_call" | custom-call | flops 1 | bytes 1 | tf_op jit(solution)/shard_map/norm/pallas_call | solution.py:119
  57.7 2.3 %collective-permute-done.15.y_ref = bf16[256,1024]{1,0:T(8,128)(2,1)S(1)} collective-permute-done((bf16[256,1024]{1,0:T(8,128)(2,1)}, bf16[256,1024]{1,0:T(8,128)(2,1)S(1)}, u32[]{:S(2)}, u32[]{:S(2)}) %collective-permute-start.15) | collective-permute-done | bytes 524320 | tf_op jit(solution)/shard_map/ppermute | solution.py:314
  60.1 1.6 collective-permute-start.16
  62.6 1.3 collective-permute-start.14
  65.0 4.0 %collective-permute-done.3.own_ref = bf16[256,1024]{1,0:T(8,128)(2,1)S(1)} collective-permute-done((bf16[256,1024]{1,0:T(8,128)(2,1)}, bf16[256,1024]{1,0:T(8,128)(2,1)S(1)}, u32[]{:S(2)}, u32[]{:S(2)}) %collective-permute-start.3) | collective-permute-done | bytes 524320 | tf_op jit(solution)/shard_map/ppermute | solution.py:306
  69.0 1.2 collective-permute-start.22
  72.3 2.6 %norm.5.rest_0_ = bf16[4,4,256,1024]{3,2,1,0:T(8,128)(2,1)S(1)} custom-call(s32[3]{0:T(128)S(1)} %pad_add_fusion.place_ref, bf16[256,1024]{1,0:T(8,128)(2,1)} %collective-permute-done.2.own_ref, bf16[256,1024]{1,0:T(8,128)(2,1)} %collective-permute-done.10.x_ref, ...), custom_call_target="tpu_custom_call", output_to_operand_aliasing={{}: (7, {})} | custom-call | flops 1 | bytes 1 | tf_op jit(solution)/shard_map/norm/pallas_call | solution.py:119
  74.9 8.9 %collective-permute-done.20.refs_3_.refs_2_ = bf16[1344,256]{1,0:T(8,128)(2,1)S(1)} collective-permute-done((bf16[1344,256]{1,0:T(8,128)(2,1)S(1)}, bf16[1344,256]{1,0:T(8,128)(2,1)S(1)}, u32[]{:S(2)}, u32[]{:S(2)}) %collective-permute-start.20) | collective-permute-done | bytes 688160 | tf_op jit(solution)/shard_map/ppermute | solution.py:306
  84.9 9.4 %collective-permute-done.4.own_ref = bf16[256,1024]{1,0:T(8,128)(2,1)S(1)} collective-permute-done((bf16[256,1024]{1,0:T(8,128)(2,1)S(1)}, bf16[256,1024]{1,0:T(8,128)(2,1)S(1)}, u32[]{:S(2)}, u32[]{:S(2)}) %collective-permute-start.4) | collective-permute-done | bytes 524320 | tf_op jit(solution)/shard_map/ppermute | solution.py:306
  95.5 2.9 %collective-permute-start.31 = (bf16[832,256]{1,0:T(8,128)(2,1)S(1)}, bf16[832,256]{1,0:T(8,128)(2,1)S(1)}, u32[]{:S(2)}, u32[]{:S(2)}) collective-permute-start(bf16[832,256]{1,0:T(8,128)(2,1)S(1)} %pad_maximum_fusion.3), channel_id=1, source_target_pairs={{0,16},{4,20},{8,24},{12,28},{16,0},{20,4},{24,8},{28,12},{1,17},{... | collective-permute-start | bytes 1277960 | tf_op jit(solution)/shard_map/ppermute | solution.py:306
  98.3 1.9 %norm.6.rest_0_ = bf16[4,4,256,1024]{3,2,1,0:T(8,128)(2,1)S(1)} custom-call(s32[3]{0:T(128)S(1)} %pad_add_fusion.place_ref, bf16[256,1024]{1,0:T(8,128)(2,1)S(1)} %collective-permute-done.3.own_ref, bf16[256,1024]{1,0:T(8,128)(2,1)S(1)} %collective-permute-done.17.x_ref, ...), custom_call_target="tpu_custom_call", output_to_operand_aliasing={{}: (7, {})} | custom-call | flops 1 | bytes 1 | tf_op jit(solution)/shard_map/norm/pallas_call | solution.py:119
  100.3 16.8 %collective-permute-done.26.refs_3_ = bf16[512,256]{1,0:T(8,128)(2,1)S(1)} collective-permute-done((bf16[512,256]{1,0:T(8,128)(2,1)S(1)}, bf16[512,256]{1,0:T(8,128)(2,1)S(1)}, u32[]{:S(2)}, u32[]{:S(2)}) %collective-permute-start.26) | collective-permute-done | bytes 262176 | tf_op jit(solution)/shard_map/ppermute | solution.py:306
  118.0 1.6 collective-permute-start.28
  119.6 6.6 %collective-permute-done.31.refs_2_.refs_0_ = bf16[832,256]{1,0:T(8,128)(2,1)S(1)} collective-permute-done((bf16[832,256]{1,0:T(8,128)(2,1)S(1)}, bf16[832,256]{1,0:T(8,128)(2,1)S(1)}, u32[]{:S(2)}, u32[]{:S(2)}) %collective-permute-start.31) | collective-permute-done | bytes 426016 | tf_op jit(solution)/shard_map/ppermute | solution.py:306
  126.7 1.9 %norm.7.normed_ref = bf16[4,4,256,1024]{3,2,1,0:T(8,128)(2,1)S(1)} custom-call(s32[3]{0:T(128)S(1)} %pad_add_fusion.place_ref, bf16[256,1024]{1,0:T(8,128)(2,1)S(1)} %collective-permute-done.4.own_ref, bf16[256,1024]{1,0:T(8,128)(2,1)S(1)} %collective-permute-done.24.x_ref, ...), custom_call_target="tpu_custom_call", output_to_operand_aliasing={{}: (7, {})} | custom-call | flops 1 | bytes 1 | tf_op jit(solution)/shard_map/norm/pallas_call | solution.py:119
  128.7 4.0 %project.5 = (f32[4,256,256]{2,1,0:T(8,128)S(1)}, f32[4,256,256]{2,1,0:T(8,128)S(1)}) custom-call(s32[3]{0:T(128)S(1)} %pad_add_fusion.place_ref, bf16[4,4,256,1024]{3,2,1,0:T(8,128)(2,1)S(1)} %norm.7.normed_ref, bf16[1344,256]{1,0:T(8,128)(2,1)S(1)} %pad_maximum_fusion.refs_0_, bf16[1344,256]{1,0:T(8,128)(2,1)S(1)} %collective-permute-done.13.refs_1_, ...), custom_call_target="tpu_custom_call" | custom-call | flops 1 | bytes 1 | tf_op jit(solution)/shard_map/project/pallas_call | solution.py:155
  132.7 3.3 %project.4.q_ref = bf16[4,256,256]{2,1,0:T(8,128)(2,1)S(1)} custom-call(s32[3]{0:T(128)S(1)} %pad_add_fusion.place_ref, bf16[4,4,256,1024]{3,2,1,0:T(8,128)(2,1)S(1)} %norm.7.normed_ref, bf16[512,256]{1,0:T(8,128)(2,1)S(1)} %get-tuple-element.74.refs_0_, bf16[512,256]{1,0:T(8,128)(2,1)S(1)} %copy-done.10, bf16[512,256]{1,0:T(8,128)(2,1)S(1)} %copy-done.8, ...), custom_call_target="tpu_custom_call" | custom-call | flops 1 | bytes 1 | tf_op jit(solution)/shard_map/project/pallas_call | solution.py:155
  136.1 1.3 project.6.k_ref
  137.4 4.1 %collective-permute-done.34.refs_0_ = bf16[512,256]{1,0:T(8,128)(2,1)S(1)} collective-permute-done((bf16[512,256]{1,0:T(8,128)(2,1)S(1)}, bf16[512,256]{1,0:T(8,128)(2,1)S(1)}, u32[]{:S(2)}, u32[]{:S(2)}) %collective-permute-start.34) | collective-permute-done | bytes 262176 | tf_op jit(solution)/shard_map/ppermute | solution.py:306
  143.0 1.3 project.7.v_ref
  144.5 1.8 collective-permute-done.37.vs_ref
  146.2 4.0 %attend.3 = bf16[256,256]{1,0:T(8,128)(2,1)S(1)} custom-call(s32[3]{0:T(128)S(1)} %pad_add_fusion.place_ref, bf16[4,256,256]{2,1,0:T(8,128)(2,1)S(1)} %project.4.q_ref, bf16[4,256,256]{2,1,0:T(8,128)(2,1)S(1)} %project.6.k_ref, bf16[4,256,256]{2,1,0:T(8,128)(2,1)S(1)} %project.7.v_ref, bf16[4,256,256]{2,1,0:T(8,128)(2,1)S(1)} %collective-permute-done.36.ks_ref, ...), custom_call_target="tpu_custom_call" | custom-call | flops 1 | bytes 1 | tf_op jit(solution)/shard_map/attend/pallas_call | solution.py:239
  150.4 7.1 %attend.4 = (bf16[256,256]{1,0:T(8,128)(2,1)S(1)}, bf16[256,256]{1,0:T(8,128)(2,1)S(1)}) custom-call(s32[3]{0:T(128)S(1)} %pad_add_fusion.place_ref, bf16[4,256,256]{2,1,0:T(8,128)(2,1)S(1)} %project.4.q_ref, bf16[4,256,256]{2,1,0:T(8,128)(2,1)S(1)} %project.6.k_ref, bf16[4,256,256]{2,1,0:T(8,128)(2,1)S(1)} %project.7.v_ref, ...), custom_call_target="tpu_custom_call" | custom-call | flops 1 | bytes 1 | tf_op jit(solution)/shard_map/attend/pallas_call | solution.py:239
  157.5 3.8 %collective-permute-start.40 = (bf16[256,256]{1,0:T(8,128)(2,1)S(1)}, bf16[256,256]{1,0:T(8,128)(2,1)S(1)}, u32[]{:S(2)}, u32[]{:S(2)}) collective-permute-start(bf16[256,256]{1,0:T(8,128)(2,1)S(1)} %get-tuple-element.66), channel_id=1, source_target_pairs={{0,24},{4,28},{8,0},{12,4},{16,8},{20,12},{24,16},{28,20},{1,25},{... | collective-permute-start | bytes 393224 | tf_op jit(solution)/shard_map/ppermute | solution.py:306
  161.4 2.5 %attend.5.refs_0_ = bf16[256,256]{1,0:T(8,128)(2,1)S(1)} custom-call(s32[3]{0:T(128)S(1)} %pad_add_fusion.place_ref, bf16[4,256,256]{2,1,0:T(8,128)(2,1)S(1)} %project.4.q_ref, bf16[4,256,256]{2,1,0:T(8,128)(2,1)S(1)} %project.6.k_ref, bf16[4,256,256]{2,1,0:T(8,128)(2,1)S(1)} %project.7.v_ref, bf16[4,256,256]{2,1,0:T(8,128)(2,1)S(1)} %collective-permute-done.36.ks_ref, ...), custom_call_target="tpu_custom_call" | custom-call | flops 1 | bytes 1 | tf_op jit(solution)/shard_map/attend/pallas_call | solution.py:239
  164.5 1.2 collective-permute-done.39.refs_1_
  165.7 1.4 collective-permute-done.40.refs_3_
  167.7 17.7 %join.1 = bf16[256,1024]{1,0:T(8,128)(2,1)} custom-call(s32[3]{0:T(128)} %copy-done.15, bf16[256,256]{1,0:T(8,128)(2,1)} %copy-done.5, bf16[256,256]{1,0:T(8,128)(2,1)} %copy-done.29, bf16[256,256]{1,0:T(8,128)(2,1)} %copy-done.28, bf16[256,256]{1,0:T(8,128)(2,1)} %copy-done.30), custom_call_target="tpu_custom_call" | custom-call | tf_op jit(solution)/shard_map/join/pallas_call | solution.py:294
  (128 shorter events, 18.8 us)
Async XLA Ops:
  1.2 8.9 %collective-permute-start = (bf16[128,1024]{1,0:T(8,128)(2,1)S(1)}, bf16[128,1024]{1,0:T(8,128)(2,1)S(1)}, u32[]{:S(2)}, u32[]{:S(2)}) collective-permute-start(bf16[128,1024]{1,0:T(8,128)(2,1)S(1)} %fusion), channel_id=1, source_target_pairs={{0,4},{4,8},{8,12},{12,16},{16,20},{20,24},{24,28},{1,5},{5,9},{9,... | collective-permute-start | bytes 786440 | tf_op jit(solution)/shard_map/ppermute | solution.py:350
  5.6 11.7 %collective-permute-start.5 = (bf16[512,256]{1,0:T(8,128)(2,1)}, bf16[512,256]{1,0:T(8,128)(2,1)S(1)}, u32[]{:S(2)}, u32[]{:S(2)}) collective-permute-start(bf16[512,256]{1,0:T(8,128)(2,1)} %get-tuple-element.77), channel_id=1, source_target_pairs={{0,24},{4,28},{8,0},{12,4},{16,8},{20,12},{24,16},{28,20},{1,25},{... | collective-permute-start | bytes 786440 | tf_op jit(solution)/shard_map/ppermute | solution.py:306
  10.2 12.8 %collective-permute-start.1 = (bf16[512,256]{1,0:T(8,128)(2,1)}, bf16[512,256]{1,0:T(8,128)(2,1)S(1)}, u32[]{:S(2)}, u32[]{:S(2)}) collective-permute-start(bf16[512,256]{1,0:T(8,128)(2,1)} %get-tuple-element.78), channel_id=1, source_target_pairs={{0,8},{4,12},{8,16},{12,20},{16,24},{20,28},{24,0},{28,4},{1,9},{5... | collective-permute-start | bytes 786440 | tf_op jit(solution)/shard_map/ppermute | solution.py:306
  10.2 15.8 %copy-start.23 = (bf16[152,1024]{1,0:T(8,128)(2,1)S(1)}, bf16[152,1024]{1,0:T(8,128)(2,1)}, u32[]{:S(2)}) copy-start(bf16[152,1024]{1,0:T(8,128)(2,1)} %param.13) | copy-start | bytes 933892
  10.3 16.9 %copy-start.17 = (bf16[512,3,1024]{2,0,1:T(8,128)(2,1)S(1)}, bf16[512,3,1024]{2,0,1:T(8,128)(2,1)}, u32[]{:S(2)}) copy-start(bf16[512,3,1024]{2,0,1:T(8,128)(2,1)} %param.11) | copy-start | bytes 9437188
  22.9 14.3 %collective-permute-start.6 = (bf16[256,1024]{1,0:T(8,128)(2,1)S(1)}, bf16[256,1024]{1,0:T(8,128)(2,1)S(1)}, u32[]{:S(2)}, u32[]{:S(2)}) collective-permute-start(bf16[256,1024]{1,0:T(8,128)(2,1)S(1)} %hyena_filters.1.own_ref), channel_id=1, source_target_pairs={{0,1},{1,0},{2,3},{3,2},{4,5},{5,4},{6,7},{7,6},{8,9},{9,8},{10,11... | collective-permute-start | bytes 1572872 | tf_op jit(solution)/shard_map/ppermute | solution.py:314
  24.4 14.4 %collective-permute-start.8 = (bf16[256,1024]{1,0:T(8,128)(2,1)S(1)}, bf16[256,1024]{1,0:T(8,128)(2,1)S(1)}, u32[]{:S(2)}, u32[]{:S(2)}) collective-permute-start(bf16[256,1024]{1,0:T(8,128)(2,1)S(1)} %hyena_filters.1.own_ref), channel_id=1, source_target_pairs={{0,2},{1,3},{2,0},{3,1},{4,6},{5,7},{6,4},{7,5},{8,10},{9,11},{10,... | collective-permute-start | bytes 1572872 | tf_op jit(solution)/shard_map/ppermute | solution.py:314
  26.7 16.7 %collective-permute-start.2 = (bf16[256,1024]{1,0:T(8,128)(2,1)S(1)}, bf16[256,1024]{1,0:T(8,128)(2,1)}, u32[]{:S(2)}, u32[]{:S(2)}) collective-permute-start(bf16[256,1024]{1,0:T(8,128)(2,1)S(1)} %hyena_filters.1.own_ref), channel_id=1, source_target_pairs={{0,8},{4,12},{8,16},{12,20},{16,24},{20,28},{24,0},{28,4},{1,9},{5... | collective-permute-start | bytes 1572872 | tf_op jit(solution)/shard_map/ppermute | solution.py:306
  29.4 22.2 %copy-start.6 = (f32[4096]{0:T(1024)S(1)}, f32[4096]{0:T(1024)}, u32[]{:S(2)}) copy-start(f32[4096]{0:T(1024)} %param.10) | copy-start | bytes 49156
  29.4 28.3 %collective-permute-start.13 = (bf16[1344,256]{1,0:T(8,128)(2,1)}, bf16[1344,256]{1,0:T(8,128)(2,1)S(1)}, u32[]{:S(2)}, u32[]{:S(2)}) collective-permute-start(bf16[1344,256]{1,0:T(8,128)(2,1)} %pad_maximum_fusion.1), channel_id=1, source_target_pairs={{0,8},{4,12},{8,16},{12,20},{16,24},{20,28},{24,0},{28,4},{1,9},{5... | collective-permute-start | bytes 2064392 | tf_op jit(solution)/shard_map/ppermute | solution.py:306
  37.3 8.1 %collective-permute-start.7 = (bf16[128,1024]{1,0:T(8,128)(2,1)S(1)}, bf16[128,1024]{1,0:T(8,128)(2,1)S(1)}, u32[]{:S(2)}, u32[]{:S(2)}) collective-permute-start(bf16[128,1024]{1,0:T(8,128)(2,1)S(1)} %slice.42), channel_id=1, source_target_pairs={{0,2},{1,3},{2,0},{3,1},{4,6},{5,7},{6,4},{7,5},{8,10},{9,11},{10,... | collective-permute-start | bytes 786440 | tf_op jit(solution)/shard_map/ppermute | solution.py:314
  38.9 7.8 %collective-permute-start.9 = (bf16[128,1024]{1,0:T(8,128)(2,1)S(1)}, bf16[128,1024]{1,0:T(8,128)(2,1)S(1)}, u32[]{:S(2)}, u32[]{:S(2)}) collective-permute-start(bf16[128,1024]{1,0:T(8,128)(2,1)S(1)} %slice.43), channel_id=1, source_target_pairs={{0,1},{1,0},{2,3},{3,2},{4,5},{5,4},{6,7},{7,6},{8,9},{9,8},{10,11... | collective-permute-start | bytes 786440 | tf_op jit(solution)/shard_map/ppermute | solution.py:314
  40.5 17.2 %collective-permute-start.11 = (bf16[1344,256]{1,0:T(8,128)(2,1)S(1)}, bf16[1344,256]{1,0:T(8,128)(2,1)S(1)}, u32[]{:S(2)}, u32[]{:S(2)}) collective-permute-start(bf16[1344,256]{1,0:T(8,128)(2,1)S(1)} %pad_maximum_fusion.refs_0_), channel_id=1, source_target_pairs={{0,4},{4,0},{8,12},{12,8},{16,20},{20,16},{24,28},{28,24},{1,5},{5... | collective-permute-start | bytes 2064392 | tf_op jit(solution)/shard_map/ppermute | solution.py:310
  47.4 12.7 %collective-permute-start.15 = (bf16[256,1024]{1,0:T(8,128)(2,1)}, bf16[256,1024]{1,0:T(8,128)(2,1)S(1)}, u32[]{:S(2)}, u32[]{:S(2)}) collective-permute-start(bf16[256,1024]{1,0:T(8,128)(2,1)} %collective-permute-done.2.own_ref), channel_id=1, source_target_pairs={{0,2},{1,3},{2,0},{3,1},{4,6},{5,7},{6,4},{7,5},{8,10},{9,11},{10,... | collective-permute-start | bytes 1572872 | tf_op jit(solution)/shard_map/ppermute | solution.py:314
  48.5 13.2 %collective-permute-start.10 = (bf16[256,1024]{1,0:T(8,128)(2,1)}, bf16[256,1024]{1,0:T(8,128)(2,1)}, u32[]{:S(2)}, u32[]{:S(2)}) collective-permute-start(bf16[256,1024]{1,0:T(8,128)(2,1)} %collective-permute-done.2.own_ref), channel_id=1, source_target_pairs={{0,1},{1,0},{2,3},{3,2},{4,5},{5,4},{6,7},{7,6},{8,9},{9,8},{10,11... | collective-permute-start | bytes 1572872 | tf_op jit(solution)/shard_map/ppermute | solution.py:314
  49.8 1.7 collective-permute-start.12
  51.4 17.6 %collective-permute-start.3 = (bf16[256,1024]{1,0:T(8,128)(2,1)}, bf16[256,1024]{1,0:T(8,128)(2,1)S(1)}, u32[]{:S(2)}, u32[]{:S(2)}) collective-permute-start(bf16[256,1024]{1,0:T(8,128)(2,1)} %collective-permute-done.2.own_ref), channel_id=1, source_target_pairs={{0,8},{4,12},{8,16},{12,20},{16,24},{20,28},{24,0},{28,4},{1,9},{5... | collective-permute-start | bytes 1572872 | tf_op jit(solution)/shard_map/ppermute | solution.py:306
  51.5 109.8 %copy-start.15 = (s32[3]{0:T(128)}, s32[3]{0:T(128)S(1)}, u32[]{:S(2)}) copy-start(s32[3]{0:T(128)S(1)} %pad_add_fusion.place_ref) | copy-start | bytes 40
  60.1 9.0 %collective-permute-start.16 = (bf16[128,1024]{1,0:T(8,128)(2,1)S(1)}, bf16[128,1024]{1,0:T(8,128)(2,1)S(1)}, u32[]{:S(2)}, u32[]{:S(2)}) collective-permute-start(bf16[128,1024]{1,0:T(8,128)(2,1)S(1)} %slice.35), channel_id=1, source_target_pairs={{0,1},{1,0},{2,3},{3,2},{4,5},{5,4},{6,7},{7,6},{8,9},{9,8},{10,11... | collective-permute-start | bytes 786440 | tf_op jit(solution)/shard_map/ppermute | solution.py:314
  62.6 6.4 %collective-permute-start.14 = (bf16[128,1024]{1,0:T(8,128)(2,1)S(1)}, bf16[128,1024]{1,0:T(8,128)(2,1)S(1)}, u32[]{:S(2)}, u32[]{:S(2)}) collective-permute-start(bf16[128,1024]{1,0:T(8,128)(2,1)S(1)} %slice.34), channel_id=1, source_target_pairs={{0,2},{1,3},{2,0},{3,1},{4,6},{5,7},{6,4},{7,5},{8,10},{9,11},{10,... | collective-permute-start | bytes 786440 | tf_op jit(solution)/shard_map/ppermute | solution.py:314
  63.9 31.4 %copy-start.26 = (bf16[512,256]{1,0:T(8,128)(2,1)S(1)}, bf16[512,256]{1,0:T(8,128)(2,1)}, u32[]{:S(2)}) copy-start(bf16[512,256]{1,0:T(8,128)(2,1)} %get-tuple-element.50) | copy-start | bytes 786436
  63.9 31.5 %copy-start.18 = (bf16[512,256]{1,0:T(8,128)(2,1)S(1)}, bf16[512,256]{1,0:T(8,128)(2,1)}, u32[]{:S(2)}) copy-start(bf16[512,256]{1,0:T(8,128)(2,1)} %get-tuple-element.68) | copy-start | bytes 786436
  64.0 19.8 %collective-permute-start.20 = (bf16[1344,256]{1,0:T(8,128)(2,1)S(1)}, bf16[1344,256]{1,0:T(8,128)(2,1)S(1)}, u32[]{:S(2)}, u32[]{:S(2)}) collective-permute-start(bf16[1344,256]{1,0:T(8,128)(2,1)S(1)} %pad_maximum_fusion.2), channel_id=1, source_target_pairs={{0,24},{4,28},{8,0},{12,4},{16,8},{20,12},{24,16},{28,20},{1,25},{... | collective-permute-start | bytes 2064392 | tf_op jit(solution)/shard_map/ppermute | solution.py:306
  69.0 14.8 %collective-permute-start.22 = (bf16[256,1024]{1,0:T(8,128)(2,1)S(1)}, bf16[256,1024]{1,0:T(8,128)(2,1)S(1)}, u32[]{:S(2)}, u32[]{:S(2)}) collective-permute-start(bf16[256,1024]{1,0:T(8,128)(2,1)S(1)} %collective-permute-done.3.own_ref), channel_id=1, source_target_pairs={{0,2},{1,3},{2,0},{3,1},{4,6},{5,7},{6,4},{7,5},{8,10},{9,11},{10,... | collective-permute-start | bytes 1572872 | tf_op jit(solution)/shard_map/ppermute | solution.py:314
  70.2 13.9 %collective-permute-start.17 = (bf16[256,1024]{1,0:T(8,128)(2,1)S(1)}, bf16[256,1024]{1,0:T(8,128)(2,1)S(1)}, u32[]{:S(2)}, u32[]{:S(2)}) collective-permute-start(bf16[256,1024]{1,0:T(8,128)(2,1)S(1)} %collective-permute-done.3.own_ref), channel_id=1, source_target_pairs={{0,1},{1,0},{2,3},{3,2},{4,5},{5,4},{6,7},{7,6},{8,9},{9,8},{10,11... | collective-permute-start | bytes 1572872 | tf_op jit(solution)/shard_map/ppermute | solution.py:314
  70.8 1.5 collective-permute-start.18
  70.8 4.1 %collective-permute-start.19 = (bf16[512,256]{1,0:T(8,128)(2,1)S(1)}, bf16[512,256]{1,0:T(8,128)(2,1)S(1)}, u32[]{:S(2)}, u32[]{:S(2)}) collective-permute-start(bf16[512,256]{1,0:T(8,128)(2,1)S(1)} %copy-done.8), channel_id=1, source_target_pairs={{0,4},{4,0},{8,12},{12,8},{16,20},{20,16},{24,28},{28,24},{1,5},{5... | collective-permute-start | bytes 786440 | tf_op jit(solution)/shard_map/ppermute | solution.py:310
  72.3 22.0 %collective-permute-start.4 = (bf16[256,1024]{1,0:T(8,128)(2,1)S(1)}, bf16[256,1024]{1,0:T(8,128)(2,1)S(1)}, u32[]{:S(2)}, u32[]{:S(2)}) collective-permute-start(bf16[256,1024]{1,0:T(8,128)(2,1)S(1)} %collective-permute-done.3.own_ref), channel_id=1, source_target_pairs={{0,8},{4,12},{8,16},{12,20},{16,24},{20,28},{24,0},{28,4},{1,9},{5... | collective-permute-start | bytes 1572872 | tf_op jit(solution)/shard_map/ppermute | solution.py:306
  83.8 10.5 %collective-permute-start.23 = (bf16[128,1024]{1,0:T(8,128)(2,1)S(1)}, bf16[128,1024]{1,0:T(8,128)(2,1)S(1)}, u32[]{:S(2)}, u32[]{:S(2)}) collective-permute-start(bf16[128,1024]{1,0:T(8,128)(2,1)S(1)} %slice.37), channel_id=1, source_target_pairs={{0,1},{1,0},{2,3},{3,2},{4,5},{5,4},{6,7},{7,6},{8,9},{9,8},{10,11... | collective-permute-start | bytes 786440 | tf_op jit(solution)/shard_map/ppermute | solution.py:314
  84.1 10.2 %collective-permute-start.21 = (bf16[128,1024]{1,0:T(8,128)(2,1)S(1)}, bf16[128,1024]{1,0:T(8,128)(2,1)S(1)}, u32[]{:S(2)}, u32[]{:S(2)}) collective-permute-start(bf16[128,1024]{1,0:T(8,128)(2,1)S(1)} %slice.36), channel_id=1, source_target_pairs={{0,2},{1,3},{2,0},{3,1},{4,6},{5,7},{6,4},{7,5},{8,10},{9,11},{10,... | collective-permute-start | bytes 786440 | tf_op jit(solution)/shard_map/ppermute | solution.py:314
  84.9 15.4 %collective-permute-start.25 = (bf16[1344,256]{1,0:T(8,128)(2,1)S(1)}, bf16[1344,256]{1,0:T(8,128)(2,1)S(1)}, u32[]{:S(2)}, u32[]{:S(2)}) collective-permute-start(bf16[1344,256]{1,0:T(8,128)(2,1)S(1)} %collective-permute-done.13.refs_1_), channel_id=1, source_target_pairs={{0,4},{4,0},{8,12},{12,8},{16,20},{20,16},{24,28},{28,24},{1,5},{5... | collective-permute-start | bytes 2064392 | tf_op jit(solution)/shard_map/ppermute | solution.py:310
  94.3 22.9 %collective-permute-start.27 = (bf16[256,1024]{1,0:T(8,128)(2,1)S(1)}, bf16[256,1024]{1,0:T(8,128)(2,1)S(1)}, u32[]{:S(2)}, u32[]{:S(2)}) collective-permute-start(bf16[256,1024]{1,0:T(8,128)(2,1)S(1)} %collective-permute-done.4.own_ref), channel_id=1, source_target_pairs={{0,2},{1,3},{2,0},{3,1},{4,6},{5,7},{6,4},{7,5},{8,10},{9,11},{10,... | collective-permute-start | bytes 1572872 | tf_op jit(solution)/shard_map/ppermute | solution.py:314
  94.8 23.2 %collective-permute-start.24 = (bf16[256,1024]{1,0:T(8,128)(2,1)S(1)}, bf16[256,1024]{1,0:T(8,128)(2,1)S(1)}, u32[]{:S(2)}, u32[]{:S(2)}) collective-permute-start(bf16[256,1024]{1,0:T(8,128)(2,1)S(1)} %collective-permute-done.4.own_ref), channel_id=1, source_target_pairs={{0,1},{1,0},{2,3},{3,2},{4,5},{5,4},{6,7},{7,6},{8,9},{9,8},{10,11... | collective-permute-start | bytes 1572872 | tf_op jit(solution)/shard_map/ppermute | solution.py:314
  95.3 21.9 %collective-permute-start.26 = (bf16[512,256]{1,0:T(8,128)(2,1)S(1)}, bf16[512,256]{1,0:T(8,128)(2,1)S(1)}, u32[]{:S(2)}, u32[]{:S(2)}) collective-permute-start(bf16[512,256]{1,0:T(8,128)(2,1)S(1)} %copy-done.26), channel_id=1, source_target_pairs={{0,16},{4,20},{8,24},{12,28},{16,0},{20,4},{24,8},{28,12},{1,17},{... | collective-permute-start | bytes 786440 | tf_op jit(solution)/shard_map/ppermute | solution.py:306
  95.4 31.3 %copy-start.25 = (bf16[512,256]{1,0:T(8,128)(2,1)S(1)}, bf16[512,256]{1,0:T(8,128)(2,1)}, u32[]{:S(2)}) copy-start(bf16[512,256]{1,0:T(8,128)(2,1)} %get-tuple-element.59) | copy-start | bytes 786436
  95.5 30.8 %collective-permute-start.31 = (bf16[832,256]{1,0:T(8,128)(2,1)S(1)}, bf16[832,256]{1,0:T(8,128)(2,1)S(1)}, u32[]{:S(2)}, u32[]{:S(2)}) collective-permute-start(bf16[832,256]{1,0:T(8,128)(2,1)S(1)} %pad_maximum_fusion.3), channel_id=1, source_target_pairs={{0,16},{4,20},{8,24},{12,28},{16,0},{20,4},{24,8},{28,12},{1,17},{... | collective-permute-start | bytes 1277960 | tf_op jit(solution)/shard_map/ppermute | solution.py:306
  100.3 28.4 %collective-permute-start.33 = (bf16[1344,256]{1,0:T(8,128)(2,1)S(1)}, bf16[1344,256]{1,0:T(8,128)(2,1)S(1)}, u32[]{:S(2)}, u32[]{:S(2)}) collective-permute-start(bf16[1344,256]{1,0:T(8,128)(2,1)S(1)} %collective-permute-done.20.refs_3_.refs_2_), channel_id=1, source_target_pairs={{0,4},{4,0},{8,12},{12,8},{16,20},{20,16},{24,28},{28,24},{1,5},{5... | collective-permute-start | bytes 2064392 | tf_op jit(solution)/shard_map/ppermute | solution.py:310
  117.2 9.0 %collective-permute-start.29 = (bf16[128,1024]{1,0:T(8,128)(2,1)S(1)}, bf16[128,1024]{1,0:T(8,128)(2,1)S(1)}, u32[]{:S(2)}, u32[]{:S(2)}) collective-permute-start(bf16[128,1024]{1,0:T(8,128)(2,1)S(1)} %slice.39), channel_id=1, source_target_pairs={{0,1},{1,0},{2,3},{3,2},{4,5},{5,4},{6,7},{7,6},{8,9},{9,8},{10,11... | collective-permute-start | bytes 786440 | tf_op jit(solution)/shard_map/ppermute | solution.py:314
  118.0 8.2 %collective-permute-start.28 = (bf16[128,1024]{1,0:T(8,128)(2,1)S(1)}, bf16[128,1024]{1,0:T(8,128)(2,1)S(1)}, u32[]{:S(2)}, u32[]{:S(2)}) collective-permute-start(bf16[128,1024]{1,0:T(8,128)(2,1)S(1)} %slice.38), channel_id=1, source_target_pairs={{0,2},{1,3},{2,0},{3,1},{4,6},{5,7},{6,4},{7,5},{8,10},{9,11},{10,... | collective-permute-start | bytes 786440 | tf_op jit(solution)/shard_map/ppermute | solution.py:314
  126.2 9.8 %collective-permute-start.32 = (bf16[832,256]{1,0:T(8,128)(2,1)S(1)}, bf16[832,256]{1,0:T(8,128)(2,1)S(1)}, u32[]{:S(2)}, u32[]{:S(2)}) collective-permute-start(bf16[832,256]{1,0:T(8,128)(2,1)S(1)} %collective-permute-done.31.refs_2_.refs_0_), channel_id=1, source_target_pairs={{0,4},{4,0},{8,12},{12,8},{16,20},{20,16},{24,28},{28,24},{1,5},{5... | collective-permute-start | bytes 1277960 | tf_op jit(solution)/shard_map/ppermute | solution.py:310
  126.2 6.4 %collective-permute-start.30 = (bf16[512,256]{1,0:T(8,128)(2,1)S(1)}, bf16[512,256]{1,0:T(8,128)(2,1)S(1)}, u32[]{:S(2)}, u32[]{:S(2)}) collective-permute-start(bf16[512,256]{1,0:T(8,128)(2,1)S(1)} %collective-permute-done.26.refs_3_), channel_id=1, source_target_pairs={{0,4},{4,0},{8,12},{12,8},{16,20},{20,16},{24,28},{28,24},{1,5},{5... | collective-permute-start | bytes 786440 | tf_op jit(solution)/shard_map/ppermute | solution.py:310
  126.7 14.7 %collective-permute-start.34 = (bf16[512,256]{1,0:T(8,128)(2,1)S(1)}, bf16[512,256]{1,0:T(8,128)(2,1)S(1)}, u32[]{:S(2)}, u32[]{:S(2)}) collective-permute-start(bf16[512,256]{1,0:T(8,128)(2,1)S(1)} %copy-done.25), channel_id=1, source_target_pairs={{0,16},{4,20},{8,24},{12,28},{16,0},{20,4},{24,8},{28,12},{1,17},{... | collective-permute-start | bytes 786440 | tf_op jit(solution)/shard_map/ppermute | solution.py:306
  141.4 1.5 collective-permute-start.35
  141.5 3.0 %collective-permute-start.36 = (bf16[4,256,256]{2,1,0:T(8,128)(2,1)S(1)}, bf16[4,256,256]{2,1,0:T(8,128)(2,1)S(1)}, u32[]{:S(2)}, u32[]{:S(2)}) collective-permute-start(bf16[4,256,256]{2,1,0:T(8,128)(2,1)S(1)} %project.6.k_ref), channel_id=1, source_target_pairs={{0,4},{4,0},{8,12},{12,8},{16,20},{20,16},{24,28},{28,24},{1,5},{5... | collective-permute-start | bytes 1572872 | tf_op jit(solution)/shard_map/ppermute | solution.py:310
  144.3 2.0 %collective-permute-start.37 = (bf16[4,256,256]{2,1,0:T(8,128)(2,1)S(1)}, bf16[4,256,256]{2,1,0:T(8,128)(2,1)S(1)}, u32[]{:S(2)}, u32[]{:S(2)}) collective-permute-start(bf16[4,256,256]{2,1,0:T(8,128)(2,1)S(1)} %project.7.v_ref), channel_id=1, source_target_pairs={{0,4},{4,0},{8,12},{12,8},{16,20},{20,16},{24,28},{28,24},{1,5},{5... | collective-permute-start | bytes 1572872 | tf_op jit(solution)/shard_map/ppermute | solution.py:310
  150.3 11.1 %collective-permute-start.38 = (bf16[256,256]{1,0:T(8,128)(2,1)S(1)}, bf16[256,256]{1,0:T(8,128)(2,1)S(1)}, u32[]{:S(2)}, u32[]{:S(2)}) collective-permute-start(bf16[256,256]{1,0:T(8,128)(2,1)S(1)} %attend.3), channel_id=1, source_target_pairs={{0,16},{4,20},{8,24},{12,28},{16,0},{20,4},{24,8},{28,12},{1,17},{... | collective-permute-start | bytes 393224 | tf_op jit(solution)/shard_map/ppermute | solution.py:306
  157.5 8.2 %collective-permute-start.39 = (bf16[256,256]{1,0:T(8,128)(2,1)S(1)}, bf16[256,256]{1,0:T(8,128)(2,1)S(1)}, u32[]{:S(2)}, u32[]{:S(2)}) collective-permute-start(bf16[256,256]{1,0:T(8,128)(2,1)S(1)} %get-tuple-element.64), channel_id=1, source_target_pairs={{0,8},{4,12},{8,16},{12,20},{16,24},{20,28},{24,0},{28,4},{1,9},{5... | collective-permute-start | bytes 393224 | tf_op jit(solution)/shard_map/ppermute | solution.py:306
  157.5 9.5 %collective-permute-start.40 = (bf16[256,256]{1,0:T(8,128)(2,1)S(1)}, bf16[256,256]{1,0:T(8,128)(2,1)S(1)}, u32[]{:S(2)}, u32[]{:S(2)}) collective-permute-start(bf16[256,256]{1,0:T(8,128)(2,1)S(1)} %get-tuple-element.66), channel_id=1, source_target_pairs={{0,24},{4,28},{8,0},{12,4},{16,8},{20,12},{24,16},{28,20},{1,25},{... | collective-permute-start | bytes 393224 | tf_op jit(solution)/shard_map/ppermute | solution.py:306
  (24 other events, 143.6 us)

commit v13 on v3

--- a/solution.py
+++ b/solution.py
@@ -344,6 +344,8 @@
             for p in kind
             if p != "c"
         ]
+        if kind == "v":
+            parts.append(jnp.zeros((16, cols), BF16))
         if "c" in kind:
             parts += [lax.dynamic_slice_in_dim(c, at, cols, 1) for c in caches]
         return jnp.concatenate(parts, axis=0)
@@ -392,12 +394,14 @@
         return [[side[item] for item in items] for side in (here, there)]
 
     early = (0, 1, 3)
-    there["q2"] = swap_core(after(here["q2"], diag0, diag1), zs)
-    there["kc2"] = swap_core(after(here["kc2"], diag0, diag1), zs)
+    there["q2"] = swap_core(after(here["q2"], normed), zs)
+    there["kc2"], far_cache = [
+        swap_core(after(here["kc2"][a:b], normed), zs) for a, b in ((0, depth), (depth, None))
+    ]
     (q,) = project(place, normed, *sides("q0", "q1", "q3", "q2"), early + (2,), 1, True)
     k_early, v_early = project(place, normed, *sides("kvc0", "kvc1", "kvc3"), early, 2, False)
-    kept = sum(sides("kvc0", "kvc1", "kc2", "kvc3"), [])
-    ck, cv = pack(kept, [depth if i % zs == 2 else 2 * depth for i in range(2 * zs)], crow)
+    kept = sum(sides("kvc0", "kvc1", "kvc3"), []) + [here["kc2"], far_cache]
+    ck, cv = pack(kept, [2 * depth] * (2 * zs - 2) + [depth, 0], crow)
     (k,) = project(place, after(normed, q, ck), *sides("kc2"), (2,), 1, True, (k_early,))
     k_sib = swap_core(k, zs)
     there["v2"] = swap_core(after(here["v2"], k), zs)

time: 170 us -> 170 us (level)
    ppermute x13, waiting for transfers between devices: 61.9 us -> 55 us  [shift_z(): return lax.ppermute(value, 'seq', pairs)]
    ppermute x16, waiting for transfers between devices: 11.5 us -> 17.6 us  [swap_chan(): return lax.ppermute(value, 'chan', [(c, c ^ bit) for c in range(4)])]
    ppermute x11 -> x12, waiting for transfers between devices: 5.5 us -> 5.87 us  [swap_core(): lax.ppermute(value, 'seq', [(2 * a + k, 2 * a + 1 - k) for a in range(zs)...]
  transfers between devices with their start and end apart: 41 -> 42, of which waited for: 20 -> 22; matrix products, arithmetic and copies ran while one was open for 4% -> 4% of each run, Pallas kernels for 20% -> 20%
where the time goes in v13:
time: 170 us
  waiting for transfers between devices  78.5 us (46%)
  Pallas kernels  40 us (24%)
  starting transfers between devices  36.7 us (22%)
  local copies, waits for them, and re-layouts  11.8 us (7%)
  other arithmetic  2.44 us (1%)
    ppermute x13, waiting for transfers between devices, shift_z(): return lax.ppermute(value, 'seq', pairs)  55 us
    ppermute x16, waiting for transfers between devices, swap_chan(): return lax.ppermute(value, 'chan', [(c, c ^ bit) for c in range(4)])  17.6 us
    ppermute x16, starting transfers between devices, swap_chan(): return lax.ppermute(value, 'chan', [(c, c ^ bit) for c in range(4)])  17.5 us
    ppermute x13, starting transfers between devices, shift_z(): return lax.ppermute(value, 'seq', pairs)  14.6 us
    pallas_call x3, Pallas kernels, attend(): pl.pallas_call(functools.partial(attend_kernel, shifts), in_specs=[SMEM]...  13.9 us
    pallas_call x4, Pallas kernels, project(): pl.pallas_call(functools.partial(project_kernel, shifts, zs, count), in_s...  9.84 us
    pallas_call x4, Pallas kernels, norm(): pl.pallas_call(functools.partial(norm_kernel, j), in_specs=[SMEM] + [VMEM...  8.27 us
    unnamed x62, local copies, waits for them, and re-layouts  6.78 us
  transfers between devices with their start and end apart: 42, of which 22 were waited for; matrix products, arithmetic and copies ran while one was open for 4% of the time, Pallas kernels for 20%

profile of v13, /device:TPU:0, one launch (start us, length us, event | category | flops | bytes accessed | tf_op | source)
XLA Modules:
  0.0 170.0 jit_solution(6290797925416095820)
XLA Ops:
  0.0 1.2 fusion
  1.2 2.4 %collective-permute-start = (bf16[128,1024]{1,0:T(8,128)(2,1)S(1)}, bf16[128,1024]{1,0:T(8,128)(2,1)S(1)}, u32[]{:S(2)}, u32[]{:S(2)}) collective-permute-start(bf16[128,1024]{1,0:T(8,128)(2,1)S(1)} %fusion), channel_id=1, source_target_pairs={{0,4},{4,8},{8,12},{12,16},{16,20},{20,24},{24,28},{1,5},{5,9},{9,... | collective-permute-start | bytes 786440 | tf_op jit(solution)/shard_map/ppermute | solution.py:355
  3.7 1.9 %dynamic-slice_bitcast_fusion.10 = (bf16[512,256]{1,0:T(8,128)(2,1)}, bf16[512,256]{1,0:T(8,128)(2,1)}) fusion(bf16[512,3,1024]{2,0,1:T(8,128)(2,1)} %param.11, s32[]{:T(128)S(6)} %select_n.80, s32[]{:T(128)S(6)} %select_n.78), kind=kLoop, calls=%fused_computation.16 | loop fusion | bytes 1048584 | tf_op jit(solution)/shard_map/squeeze | solution.py:343
  5.6 4.6 %collective-permute-start.5 = (bf16[512,256]{1,0:T(8,128)(2,1)}, bf16[512,256]{1,0:T(8,128)(2,1)S(1)}, u32[]{:S(2)}, u32[]{:S(2)}) collective-permute-start(bf16[512,256]{1,0:T(8,128)(2,1)} %get-tuple-element.79), channel_id=1, source_target_pairs={{0,24},{4,28},{8,0},{12,4},{16,8},{20,12},{24,16},{28,20},{1,25},{... | collective-permute-start | bytes 786440 | tf_op jit(solution)/shard_map/ppermute | solution.py:309
  10.3 6.0 %hyena_filters.1.own_ref = bf16[256,1024]{1,0:T(8,128)(2,1)S(1)} custom-call(bf16[3,256,1024]{2,1,0:T(8,128)(2,1)S(1)} %bitcast.33, bf16[128,1024]{1,0:T(8,128)(2,1)S(1)} %pad_select_fusion.halo_ref, f32[64,128]{1,0:T(8,128)S(1)} %copy-done.16), custom_call_target="tpu_custom_call" | custom-call | flops 1 | bytes 1 | tf_op jit(solution)/shard_map/hyena_filters/pallas_call | solution.py:80
  17.3 5.6 %collective-permute-done.1.refs_1_ = bf16[512,256]{1,0:T(8,128)(2,1)S(1)} collective-permute-done((bf16[512,256]{1,0:T(8,128)(2,1)}, bf16[512,256]{1,0:T(8,128)(2,1)S(1)}, u32[]{:S(2)}, u32[]{:S(2)}) %collective-permute-start.1) | collective-permute-done | bytes 262176 | tf_op jit(solution)/shard_map/ppermute | solution.py:309
  22.9 1.5 collective-permute-start.6
  24.4 1.5 collective-permute-start.8
  27.2 1.2 dynamic-slice_bitcast_fusion
  29.4 1.4 collective-permute-start.13
  30.8 6.5 %collective-permute-done.6.x_ref = bf16[256,1024]{1,0:T(8,128)(2,1)S(1)} collective-permute-done((bf16[256,1024]{1,0:T(8,128)(2,1)S(1)}, bf16[256,1024]{1,0:T(8,128)(2,1)S(1)}, u32[]{:S(2)}, u32[]{:S(2)}) %collective-permute-start.6) | collective-permute-done | bytes 524320 | tf_op jit(solution)/shard_map/ppermute | solution.py:317
  37.3 1.6 collective-permute-start.7
  38.9 1.6 collective-permute-start.9
  40.6 2.8 %collective-permute-done.2.own_ref = bf16[256,1024]{1,0:T(8,128)(2,1)} collective-permute-done((bf16[256,1024]{1,0:T(8,128)(2,1)S(1)}, bf16[256,1024]{1,0:T(8,128)(2,1)}, u32[]{:S(2)}, u32[]{:S(2)}) %collective-permute-start.2) | collective-permute-done | bytes 524320 | tf_op jit(solution)/shard_map/ppermute | solution.py:309
  43.4 2.0 %collective-permute-done.7.d0_ref = bf16[128,1024]{1,0:T(8,128)(2,1)S(1)} collective-permute-done((bf16[128,1024]{1,0:T(8,128)(2,1)S(1)}, bf16[128,1024]{1,0:T(8,128)(2,1)S(1)}, u32[]{:S(2)}, u32[]{:S(2)}) %collective-permute-start.7) | collective-permute-done | bytes 262176 | tf_op jit(solution)/shard_map/ppermute | solution.py:317
  47.4 1.1 collective-permute-start.15
  48.5 1.3 collective-permute-start.10
  49.8 1.7 collective-permute-done.12.refs_4_
  51.5 1.0 copy-done.2
  55.5 1.9 %norm.4.rest_0_ = bf16[4,4,256,1024]{3,2,1,0:T(8,128)(2,1)S(1)} custom-call(s32[3]{0:T(128)S(1)} %pad_add_fusion.place_ref, bf16[256,1024]{1,0:T(8,128)(2,1)S(1)} %hyena_filters.1.own_ref, bf16[256,1024]{1,0:T(8,128)(2,1)S(1)} %copy-done.2, bf16[256,1024]{1,0:T(8,128)(2,1)S(1)} %copy-done.4, bf16[128,1024]{1,0:T(8,128)(2,1)S(1)} %copy-done.12, ...), custom_call_target="tpu_custom_call" | custom-call | flops 1 | bytes 1 | tf_op jit(solution)/shard_map/norm/pallas_call | solution.py:119
  57.7 2.3 %collective-permute-done.15.y_ref = bf16[256,1024]{1,0:T(8,128)(2,1)S(1)} collective-permute-done((bf16[256,1024]{1,0:T(8,128)(2,1)}, bf16[256,1024]{1,0:T(8,128)(2,1)S(1)}, u32[]{:S(2)}, u32[]{:S(2)}) %collective-permute-start.15) | collective-permute-done | bytes 524320 | tf_op jit(solution)/shard_map/ppermute | solution.py:317
  60.1 1.6 collective-permute-start.16
  62.6 1.3 collective-permute-start.14
  65.0 4.1 %collective-permute-done.3.own_ref = bf16[256,1024]{1,0:T(8,128)(2,1)S(1)} collective-permute-done((bf16[256,1024]{1,0:T(8,128)(2,1)}, bf16[256,1024]{1,0:T(8,128)(2,1)S(1)}, u32[]{:S(2)}, u32[]{:S(2)}) %collective-permute-start.3) | collective-permute-done | bytes 524320 | tf_op jit(solution)/shard_map/ppermute | solution.py:309
  69.1 1.2 collective-permute-start.22
  72.9 2.6 %norm.5.rest_0_ = bf16[4,4,256,1024]{3,2,1,0:T(8,128)(2,1)S(1)} custom-call(s32[3]{0:T(128)S(1)} %pad_add_fusion.place_ref, bf16[256,1024]{1,0:T(8,128)(2,1)} %collective-permute-done.2.own_ref, bf16[256,1024]{1,0:T(8,128)(2,1)} %collective-permute-done.10.x_ref, ...), custom_call_target="tpu_custom_call", output_to_operand_aliasing={{}: (7, {})} | custom-call | flops 1 | bytes 1 | tf_op jit(solution)/shard_map/norm/pallas_call | solution.py:119
  75.4 8.4 %collective-permute-done.20.refs_2_ = bf16[1344,256]{1,0:T(8,128)(2,1)S(1)} collective-permute-done((bf16[1344,256]{1,0:T(8,128)(2,1)S(1)}, bf16[1344,256]{1,0:T(8,128)(2,1)S(1)}, u32[]{:S(2)}, u32[]{:S(2)}) %collective-permute-start.20) | collective-permute-done | bytes 688160 | tf_op jit(solution)/shard_map/ppermute | solution.py:309
  84.9 9.4 %collective-permute-done.4.own_ref = bf16[256,1024]{1,0:T(8,128)(2,1)S(1)} collective-permute-done((bf16[256,1024]{1,0:T(8,128)(2,1)S(1)}, bf16[256,1024]{1,0:T(8,128)(2,1)S(1)}, u32[]{:S(2)}, u32[]{:S(2)}) %collective-permute-start.4) | collective-permute-done | bytes 524320 | tf_op jit(solution)/shard_map/ppermute | solution.py:309
  95.6 2.9 %collective-permute-start.32 = (bf16[832,256]{1,0:T(8,128)(2,1)S(1)}, bf16[832,256]{1,0:T(8,128)(2,1)S(1)}, u32[]{:S(2)}, u32[]{:S(2)}) collective-permute-start(bf16[832,256]{1,0:T(8,128)(2,1)S(1)} %pad_maximum_fusion.3), channel_id=1, source_target_pairs={{0,16},{4,20},{8,24},{12,28},{16,0},{20,4},{24,8},{28,12},{1,17},{... | collective-permute-start | bytes 1277960 | tf_op jit(solution)/shard_map/ppermute | solution.py:309
  98.5 1.9 %norm.6.rest_0_ = bf16[4,4,256,1024]{3,2,1,0:T(8,128)(2,1)S(1)} custom-call(s32[3]{0:T(128)S(1)} %pad_add_fusion.place_ref, bf16[256,1024]{1,0:T(8,128)(2,1)S(1)} %collective-permute-done.3.own_ref, bf16[256,1024]{1,0:T(8,128)(2,1)S(1)} %collective-permute-done.17.x_ref, ...), custom_call_target="tpu_custom_call", output_to_operand_aliasing={{}: (7, {})} | custom-call | flops 1 | bytes 1 | tf_op jit(solution)/shard_map/norm/pallas_call | solution.py:119
  100.4 16.8 %collective-permute-done.26.refs_3_ = bf16[512,256]{1,0:T(8,128)(2,1)S(1)} collective-permute-done((bf16[512,256]{1,0:T(8,128)(2,1)S(1)}, bf16[512,256]{1,0:T(8,128)(2,1)S(1)}, u32[]{:S(2)}, u32[]{:S(2)}) %collective-permute-start.26) | collective-permute-done | bytes 262176 | tf_op jit(solution)/shard_map/ppermute | solution.py:309
  118.0 1.6 collective-permute-start.28
  119.7 5.7 %collective-permute-done.29.d1_ref = bf16[128,1024]{1,0:T(8,128)(2,1)S(1)} collective-permute-done((bf16[128,1024]{1,0:T(8,128)(2,1)S(1)}, bf16[128,1024]{1,0:T(8,128)(2,1)S(1)}, u32[]{:S(2)}, u32[]{:S(2)}) %collective-permute-start.29) | collective-permute-done | bytes 262176 | tf_op jit(solution)/shard_map/ppermute | solution.py:317
  126.0 1.9 %norm.7.normed_ref = bf16[4,4,256,1024]{3,2,1,0:T(8,128)(2,1)S(1)} custom-call(s32[3]{0:T(128)S(1)} %pad_add_fusion.place_ref, bf16[256,1024]{1,0:T(8,128)(2,1)S(1)} %collective-permute-done.4.own_ref, bf16[256,1024]{1,0:T(8,128)(2,1)S(1)} %collective-permute-done.24.x_ref, ...), custom_call_target="tpu_custom_call", output_to_operand_aliasing={{}: (7, {})} | custom-call | flops 1 | bytes 1 | tf_op jit(solution)/shard_map/norm/pallas_call | solution.py:119
  127.9 4.1 %collective-permute-done.32.refs_6_.refs_0_ = bf16[832,256]{1,0:T(8,128)(2,1)S(1)} collective-permute-done((bf16[832,256]{1,0:T(8,128)(2,1)S(1)}, bf16[832,256]{1,0:T(8,128)(2,1)S(1)}, u32[]{:S(2)}, u32[]{:S(2)}) %collective-permute-start.32) | collective-permute-done | bytes 426016 | tf_op jit(solution)/shard_map/ppermute | solution.py:309
  132.8 4.0 %project.5 = (f32[4,256,256]{2,1,0:T(8,128)S(1)}, f32[4,256,256]{2,1,0:T(8,128)S(1)}) custom-call(s32[3]{0:T(128)S(1)} %pad_add_fusion.place_ref, bf16[4,4,256,1024]{3,2,1,0:T(8,128)(2,1)S(1)} %norm.7.normed_ref, bf16[1344,256]{1,0:T(8,128)(2,1)S(1)} %pad_maximum_fusion.refs_0_, bf16[1344,256]{1,0:T(8,128)(2,1)S(1)} %collective-permute-done.13.refs_1_, ...), custom_call_target="tpu_custom_call" | custom-call | flops 1 | bytes 1 | tf_op jit(solution)/shard_map/project/pallas_call | solution.py:155
  136.9 3.3 %project.4.q_ref = bf16[4,256,256]{2,1,0:T(8,128)(2,1)S(1)} custom-call(s32[3]{0:T(128)S(1)} %pad_add_fusion.place_ref, bf16[4,4,256,1024]{3,2,1,0:T(8,128)(2,1)S(1)} %norm.7.normed_ref, bf16[512,256]{1,0:T(8,128)(2,1)S(1)} %get-tuple-element.76.refs_0_, bf16[512,256]{1,0:T(8,128)(2,1)S(1)} %copy-done.10, bf16[512,256]{1,0:T(8,128)(2,1)S(1)} %copy-done.8, ...), custom_call_target="tpu_custom_call" | custom-call | flops 1 | bytes 1 | tf_op jit(solution)/shard_map/project/pallas_call | solution.py:155
  140.2 1.3 project.6.k_ref
  143.1 1.3 project.7.v_ref
  144.6 1.8 %collective-permute-done.38.vs_ref = bf16[4,256,256]{2,1,0:T(8,128)(2,1)S(1)} collective-permute-done((bf16[4,256,256]{2,1,0:T(8,128)(2,1)S(1)}, bf16[4,256,256]{2,1,0:T(8,128)(2,1)S(1)}, u32[]{:S(2)}, u32[]{:S(2)}) %collective-permute-start.38) | collective-permute-done | bytes 524320 | tf_op jit(solution)/shard_map/ppermute | solution.py:313
  146.4 3.9 %attend.3 = bf16[256,256]{1,0:T(8,128)(2,1)S(1)} custom-call(s32[3]{0:T(128)S(1)} %pad_add_fusion.place_ref, bf16[4,256,256]{2,1,0:T(8,128)(2,1)S(1)} %project.4.q_ref, bf16[4,256,256]{2,1,0:T(8,128)(2,1)S(1)} %project.6.k_ref, bf16[4,256,256]{2,1,0:T(8,128)(2,1)S(1)} %project.7.v_ref, bf16[4,256,256]{2,1,0:T(8,128)(2,1)S(1)} %collective-permute-done.37.ks_ref, ...), custom_call_target="tpu_custom_call" | custom-call | flops 1 | bytes 1 | tf_op jit(solution)/shard_map/attend/pallas_call | solution.py:248
  150.4 7.4 %attend.4 = (bf16[256,256]{1,0:T(8,128)(2,1)S(1)}, bf16[256,256]{1,0:T(8,128)(2,1)S(1)}) custom-call(s32[3]{0:T(128)S(1)} %pad_add_fusion.place_ref, bf16[4,256,256]{2,1,0:T(8,128)(2,1)S(1)} %project.4.q_ref, bf16[4,256,256]{2,1,0:T(8,128)(2,1)S(1)} %project.6.k_ref, bf16[4,256,256]{2,1,0:T(8,128)(2,1)S(1)} %project.7.v_ref, ...), custom_call_target="tpu_custom_call" | custom-call | flops 1 | bytes 1 | tf_op jit(solution)/shard_map/attend/pallas_call | solution.py:248
  157.7 1.2 collective-permute-start.40
  158.9 2.7 %collective-permute-start.41 = (bf16[256,256]{1,0:T(8,128)(2,1)S(1)}, bf16[256,256]{1,0:T(8,128)(2,1)S(1)}, u32[]{:S(2)}, u32[]{:S(2)}) collective-permute-start(bf16[256,256]{1,0:T(8,128)(2,1)S(1)} %get-tuple-element.68), channel_id=1, source_target_pairs={{0,24},{4,28},{8,0},{12,4},{16,8},{20,12},{24,16},{28,20},{1,25},{... | collective-permute-start | bytes 393224 | tf_op jit(solution)/shard_map/ppermute | solution.py:309
  161.6 2.6 %attend.5.refs_0_ = bf16[256,256]{1,0:T(8,128)(2,1)S(1)} custom-call(s32[3]{0:T(128)S(1)} %pad_add_fusion.place_ref, bf16[4,256,256]{2,1,0:T(8,128)(2,1)S(1)} %project.4.q_ref, bf16[4,256,256]{2,1,0:T(8,128)(2,1)S(1)} %project.6.k_ref, bf16[4,256,256]{2,1,0:T(8,128)(2,1)S(1)} %project.7.v_ref, bf16[4,256,256]{2,1,0:T(8,128)(2,1)S(1)} %collective-permute-done.37.ks_ref, ...), custom_call_target="tpu_custom_call" | custom-call | flops 1 | bytes 1 | tf_op jit(solution)/shard_map/attend/pallas_call | solution.py:248
  164.9 1.1 collective-permute-done.40.refs_1_
  165.9 1.4 collective-permute-done.41.refs_3_
  168.0 2.0 %join.1 = bf16[256,1024]{1,0:T(8,128)(2,1)} custom-call(s32[3]{0:T(128)} %copy-done.15, bf16[256,256]{1,0:T(8,128)(2,1)} %copy-done.5, bf16[256,256]{1,0:T(8,128)(2,1)} %copy-done.29, bf16[256,256]{1,0:T(8,128)(2,1)} %copy-done.28, bf16[256,256]{1,0:T(8,128)(2,1)} %copy-done.30), custom_call_target="tpu_custom_call" | custom-call | tf_op jit(solution)/shard_map/join/pallas_call | solution.py:298
  (133 shorter events, 21.2 us)
Async XLA Ops:
  1.2 8.9 %collective-permute-start = (bf16[128,1024]{1,0:T(8,128)(2,1)S(1)}, bf16[128,1024]{1,0:T(8,128)(2,1)S(1)}, u32[]{:S(2)}, u32[]{:S(2)}) collective-permute-start(bf16[128,1024]{1,0:T(8,128)(2,1)S(1)} %fusion), channel_id=1, source_target_pairs={{0,4},{4,8},{8,12},{12,16},{16,20},{20,24},{24,28},{1,5},{5,9},{9,... | collective-permute-start | bytes 786440 | tf_op jit(solution)/shard_map/ppermute | solution.py:355
  5.6 11.7 %collective-permute-start.5 = (bf16[512,256]{1,0:T(8,128)(2,1)}, bf16[512,256]{1,0:T(8,128)(2,1)S(1)}, u32[]{:S(2)}, u32[]{:S(2)}) collective-permute-start(bf16[512,256]{1,0:T(8,128)(2,1)} %get-tuple-element.79), channel_id=1, source_target_pairs={{0,24},{4,28},{8,0},{12,4},{16,8},{20,12},{24,16},{28,20},{1,25},{... | collective-permute-start | bytes 786440 | tf_op jit(solution)/shard_map/ppermute | solution.py:309
  10.2 12.8 %collective-permute-start.1 = (bf16[512,256]{1,0:T(8,128)(2,1)}, bf16[512,256]{1,0:T(8,128)(2,1)S(1)}, u32[]{:S(2)}, u32[]{:S(2)}) collective-permute-start(bf16[512,256]{1,0:T(8,128)(2,1)} %get-tuple-element.80), channel_id=1, source_target_pairs={{0,8},{4,12},{8,16},{12,20},{16,24},{20,28},{24,0},{28,4},{1,9},{5... | collective-permute-start | bytes 786440 | tf_op jit(solution)/shard_map/ppermute | solution.py:309
  10.3 16.9 %copy-start.17 = (bf16[512,3,1024]{2,0,1:T(8,128)(2,1)S(1)}, bf16[512,3,1024]{2,0,1:T(8,128)(2,1)}, u32[]{:S(2)}) copy-start(bf16[512,3,1024]{2,0,1:T(8,128)(2,1)} %param.11) | copy-start | bytes 9437188
  22.9 14.3 %collective-permute-start.6 = (bf16[256,1024]{1,0:T(8,128)(2,1)S(1)}, bf16[256,1024]{1,0:T(8,128)(2,1)S(1)}, u32[]{:S(2)}, u32[]{:S(2)}) collective-permute-start(bf16[256,1024]{1,0:T(8,128)(2,1)S(1)} %hyena_filters.1.own_ref), channel_id=1, source_target_pairs={{0,1},{1,0},{2,3},{3,2},{4,5},{5,4},{6,7},{7,6},{8,9},{9,8},{10,11... | collective-permute-start | bytes 1572872 | tf_op jit(solution)/shard_map/ppermute | solution.py:317
  24.4 14.4 %collective-permute-start.8 = (bf16[256,1024]{1,0:T(8,128)(2,1)S(1)}, bf16[256,1024]{1,0:T(8,128)(2,1)S(1)}, u32[]{:S(2)}, u32[]{:S(2)}) collective-permute-start(bf16[256,1024]{1,0:T(8,128)(2,1)S(1)} %hyena_filters.1.own_ref), channel_id=1, source_target_pairs={{0,2},{1,3},{2,0},{3,1},{4,6},{5,7},{6,4},{7,5},{8,10},{9,11},{10,... | collective-permute-start | bytes 1572872 | tf_op jit(solution)/shard_map/ppermute | solution.py:317
  26.7 16.7 %collective-permute-start.2 = (bf16[256,1024]{1,0:T(8,128)(2,1)S(1)}, bf16[256,1024]{1,0:T(8,128)(2,1)}, u32[]{:S(2)}, u32[]{:S(2)}) collective-permute-start(bf16[256,1024]{1,0:T(8,128)(2,1)S(1)} %hyena_filters.1.own_ref), channel_id=1, source_target_pairs={{0,8},{4,12},{8,16},{12,20},{16,24},{20,28},{24,0},{28,4},{1,9},{5... | collective-permute-start | bytes 1572872 | tf_op jit(solution)/shard_map/ppermute | solution.py:309
  29.4 22.2 %copy-start.6 = (f32[4096]{0:T(1024)S(1)}, f32[4096]{0:T(1024)}, u32[]{:S(2)}) copy-start(f32[4096]{0:T(1024)} %param.10) | copy-start | bytes 49156
  29.4 28.4 %collective-permute-start.13 = (bf16[1344,256]{1,0:T(8,128)(2,1)}, bf16[1344,256]{1,0:T(8,128)(2,1)S(1)}, u32[]{:S(2)}, u32[]{:S(2)}) collective-permute-start(bf16[1344,256]{1,0:T(8,128)(2,1)} %pad_maximum_fusion.1), channel_id=1, source_target_pairs={{0,8},{4,12},{8,16},{12,20},{16,24},{20,28},{24,0},{28,4},{1,9},{5... | collective-permute-start | bytes 2064392 | tf_op jit(solution)/shard_map/ppermute | solution.py:309
  37.3 8.1 %collective-permute-start.7 = (bf16[128,1024]{1,0:T(8,128)(2,1)S(1)}, bf16[128,1024]{1,0:T(8,128)(2,1)S(1)}, u32[]{:S(2)}, u32[]{:S(2)}) collective-permute-start(bf16[128,1024]{1,0:T(8,128)(2,1)S(1)} %slice.50), channel_id=1, source_target_pairs={{0,2},{1,3},{2,0},{3,1},{4,6},{5,7},{6,4},{7,5},{8,10},{9,11},{10,... | collective-permute-start | bytes 786440 | tf_op jit(solution)/shard_map/ppermute | solution.py:317
  38.9 7.8 %collective-permute-start.9 = (bf16[128,1024]{1,0:T(8,128)(2,1)S(1)}, bf16[128,1024]{1,0:T(8,128)(2,1)S(1)}, u32[]{:S(2)}, u32[]{:S(2)}) collective-permute-start(bf16[128,1024]{1,0:T(8,128)(2,1)S(1)} %slice.51), channel_id=1, source_target_pairs={{0,1},{1,0},{2,3},{3,2},{4,5},{5,4},{6,7},{7,6},{8,9},{9,8},{10,11... | collective-permute-start | bytes 786440 | tf_op jit(solution)/shard_map/ppermute | solution.py:317
  40.5 17.3 %collective-permute-start.11 = (bf16[1344,256]{1,0:T(8,128)(2,1)S(1)}, bf16[1344,256]{1,0:T(8,128)(2,1)S(1)}, u32[]{:S(2)}, u32[]{:S(2)}) collective-permute-start(bf16[1344,256]{1,0:T(8,128)(2,1)S(1)} %pad_maximum_fusion.refs_0_), channel_id=1, source_target_pairs={{0,4},{4,0},{8,12},{12,8},{16,20},{20,16},{24,28},{28,24},{1,5},{5... | collective-permute-start | bytes 2064392 | tf_op jit(solution)/shard_map/ppermute | solution.py:313
  47.4 12.7 %collective-permute-start.15 = (bf16[256,1024]{1,0:T(8,128)(2,1)}, bf16[256,1024]{1,0:T(8,128)(2,1)S(1)}, u32[]{:S(2)}, u32[]{:S(2)}) collective-permute-start(bf16[256,1024]{1,0:T(8,128)(2,1)} %collective-permute-done.2.own_ref), channel_id=1, source_target_pairs={{0,2},{1,3},{2,0},{3,1},{4,6},{5,7},{6,4},{7,5},{8,10},{9,11},{10,... | collective-permute-start | bytes 1572872 | tf_op jit(solution)/shard_map/ppermute | solution.py:317
  48.5 13.2 %collective-permute-start.10 = (bf16[256,1024]{1,0:T(8,128)(2,1)}, bf16[256,1024]{1,0:T(8,128)(2,1)}, u32[]{:S(2)}, u32[]{:S(2)}) collective-permute-start(bf16[256,1024]{1,0:T(8,128)(2,1)} %collective-permute-done.2.own_ref), channel_id=1, source_target_pairs={{0,1},{1,0},{2,3},{3,2},{4,5},{5,4},{6,7},{7,6},{8,9},{9,8},{10,11... | collective-permute-start | bytes 1572872 | tf_op jit(solution)/shard_map/ppermute | solution.py:317
  49.8 1.7 collective-permute-start.12
  51.5 17.6 %collective-permute-start.3 = (bf16[256,1024]{1,0:T(8,128)(2,1)}, bf16[256,1024]{1,0:T(8,128)(2,1)S(1)}, u32[]{:S(2)}, u32[]{:S(2)}) collective-permute-start(bf16[256,1024]{1,0:T(8,128)(2,1)} %collective-permute-done.2.own_ref), channel_id=1, source_target_pairs={{0,8},{4,12},{8,16},{12,20},{16,24},{20,28},{24,0},{28,4},{1,9},{5... | collective-permute-start | bytes 1572872 | tf_op jit(solution)/shard_map/ppermute | solution.py:309
  51.5 110.1 %copy-start.15 = (s32[3]{0:T(128)}, s32[3]{0:T(128)S(1)}, u32[]{:S(2)}) copy-start(s32[3]{0:T(128)S(1)} %pad_add_fusion.place_ref) | copy-start | bytes 40
  60.1 9.0 %collective-permute-start.16 = (bf16[128,1024]{1,0:T(8,128)(2,1)S(1)}, bf16[128,1024]{1,0:T(8,128)(2,1)S(1)}, u32[]{:S(2)}, u32[]{:S(2)}) collective-permute-start(bf16[128,1024]{1,0:T(8,128)(2,1)S(1)} %slice.41), channel_id=1, source_target_pairs={{0,1},{1,0},{2,3},{3,2},{4,5},{5,4},{6,7},{7,6},{8,9},{9,8},{10,11... | collective-permute-start | bytes 786440 | tf_op jit(solution)/shard_map/ppermute | solution.py:317
  62.6 6.5 %collective-permute-start.14 = (bf16[128,1024]{1,0:T(8,128)(2,1)S(1)}, bf16[128,1024]{1,0:T(8,128)(2,1)S(1)}, u32[]{:S(2)}, u32[]{:S(2)}) collective-permute-start(bf16[128,1024]{1,0:T(8,128)(2,1)S(1)} %slice.40), channel_id=1, source_target_pairs={{0,2},{1,3},{2,0},{3,1},{4,6},{5,7},{6,4},{7,5},{8,10},{9,11},{10,... | collective-permute-start | bytes 786440 | tf_op jit(solution)/shard_map/ppermute | solution.py:317
  64.0 31.4 %copy-start.26 = (bf16[512,256]{1,0:T(8,128)(2,1)S(1)}, bf16[512,256]{1,0:T(8,128)(2,1)}, u32[]{:S(2)}) copy-start(bf16[512,256]{1,0:T(8,128)(2,1)} %get-tuple-element.51) | copy-start | bytes 786436
  64.0 31.5 %copy-start.19 = (bf16[512,256]{1,0:T(8,128)(2,1)S(1)}, bf16[512,256]{1,0:T(8,128)(2,1)}, u32[]{:S(2)}) copy-start(bf16[512,256]{1,0:T(8,128)(2,1)} %get-tuple-element.70) | copy-start | bytes 786436
  64.0 19.9 %collective-permute-start.20 = (bf16[1344,256]{1,0:T(8,128)(2,1)S(1)}, bf16[1344,256]{1,0:T(8,128)(2,1)S(1)}, u32[]{:S(2)}, u32[]{:S(2)}) collective-permute-start(bf16[1344,256]{1,0:T(8,128)(2,1)S(1)} %pad_maximum_fusion.2), channel_id=1, source_target_pairs={{0,24},{4,28},{8,0},{12,4},{16,8},{20,12},{24,16},{28,20},{1,25},{... | collective-permute-start | bytes 2064392 | tf_op jit(solution)/shard_map/ppermute | solution.py:309
  69.1 14.8 %collective-permute-start.22 = (bf16[256,1024]{1,0:T(8,128)(2,1)S(1)}, bf16[256,1024]{1,0:T(8,128)(2,1)S(1)}, u32[]{:S(2)}, u32[]{:S(2)}) collective-permute-start(bf16[256,1024]{1,0:T(8,128)(2,1)S(1)} %collective-permute-done.3.own_ref), channel_id=1, source_target_pairs={{0,2},{1,3},{2,0},{3,1},{4,6},{5,7},{6,4},{7,5},{8,10},{9,11},{10,... | collective-permute-start | bytes 1572872 | tf_op jit(solution)/shard_map/ppermute | solution.py:317
  70.3 13.9 %collective-permute-start.17 = (bf16[256,1024]{1,0:T(8,128)(2,1)S(1)}, bf16[256,1024]{1,0:T(8,128)(2,1)S(1)}, u32[]{:S(2)}, u32[]{:S(2)}) collective-permute-start(bf16[256,1024]{1,0:T(8,128)(2,1)S(1)} %collective-permute-done.3.own_ref), channel_id=1, source_target_pairs={{0,1},{1,0},{2,3},{3,2},{4,5},{5,4},{6,7},{7,6},{8,9},{9,8},{10,11... | collective-permute-start | bytes 1572872 | tf_op jit(solution)/shard_map/ppermute | solution.py:317
  70.8 1.5 collective-permute-start.18
  70.8 1.9 %collective-permute-start.19 = (bf16[512,256]{1,0:T(8,128)(2,1)S(1)}, bf16[512,256]{1,0:T(8,128)(2,1)S(1)}, u32[]{:S(2)}, u32[]{:S(2)}) collective-permute-start(bf16[512,256]{1,0:T(8,128)(2,1)S(1)} %copy-done.8), channel_id=1, source_target_pairs={{0,4},{4,0},{8,12},{12,8},{16,20},{20,16},{24,28},{28,24},{1,5},{5... | collective-permute-start | bytes 786440 | tf_op jit(solution)/shard_map/ppermute | solution.py:313
  72.3 22.0 %collective-permute-start.4 = (bf16[256,1024]{1,0:T(8,128)(2,1)S(1)}, bf16[256,1024]{1,0:T(8,128)(2,1)S(1)}, u32[]{:S(2)}, u32[]{:S(2)}) collective-permute-start(bf16[256,1024]{1,0:T(8,128)(2,1)S(1)} %collective-permute-done.3.own_ref), channel_id=1, source_target_pairs={{0,8},{4,12},{8,16},{12,20},{16,24},{20,28},{24,0},{28,4},{1,9},{5... | collective-permute-start | bytes 1572872 | tf_op jit(solution)/shard_map/ppermute | solution.py:309
  72.7 22.8 %collective-permute-start.25 = (bf16[1344,256]{1,0:T(8,128)(2,1)S(1)}, bf16[1344,256]{1,0:T(8,128)(2,1)S(1)}, u32[]{:S(2)}, u32[]{:S(2)}) collective-permute-start(bf16[1344,256]{1,0:T(8,128)(2,1)S(1)} %collective-permute-done.13.refs_1_), channel_id=1, source_target_pairs={{0,4},{4,0},{8,12},{12,8},{16,20},{20,16},{24,28},{28,24},{1,5},{5... | collective-permute-start | bytes 2064392 | tf_op jit(solution)/shard_map/ppermute | solution.py:313
  83.9 10.5 %collective-permute-start.23 = (bf16[128,1024]{1,0:T(8,128)(2,1)S(1)}, bf16[128,1024]{1,0:T(8,128)(2,1)S(1)}, u32[]{:S(2)}, u32[]{:S(2)}) collective-permute-start(bf16[128,1024]{1,0:T(8,128)(2,1)S(1)} %slice.43), channel_id=1, source_target_pairs={{0,1},{1,0},{2,3},{3,2},{4,5},{5,4},{6,7},{7,6},{8,9},{9,8},{10,11... | collective-permute-start | bytes 786440 | tf_op jit(solution)/shard_map/ppermute | solution.py:317
  84.2 10.1 %collective-permute-start.21 = (bf16[128,1024]{1,0:T(8,128)(2,1)S(1)}, bf16[128,1024]{1,0:T(8,128)(2,1)S(1)}, u32[]{:S(2)}, u32[]{:S(2)}) collective-permute-start(bf16[128,1024]{1,0:T(8,128)(2,1)S(1)} %slice.42), channel_id=1, source_target_pairs={{0,2},{1,3},{2,0},{3,1},{4,6},{5,7},{6,4},{7,5},{8,10},{9,11},{10,... | collective-permute-start | bytes 786440 | tf_op jit(solution)/shard_map/ppermute | solution.py:317
  94.3 22.8 %collective-permute-start.27 = (bf16[256,1024]{1,0:T(8,128)(2,1)S(1)}, bf16[256,1024]{1,0:T(8,128)(2,1)S(1)}, u32[]{:S(2)}, u32[]{:S(2)}) collective-permute-start(bf16[256,1024]{1,0:T(8,128)(2,1)S(1)} %collective-permute-done.4.own_ref), channel_id=1, source_target_pairs={{0,2},{1,3},{2,0},{3,1},{4,6},{5,7},{6,4},{7,5},{8,10},{9,11},{10,... | collective-permute-start | bytes 1572872 | tf_op jit(solution)/shard_map/ppermute | solution.py:317
  94.8 23.2 %collective-permute-start.24 = (bf16[256,1024]{1,0:T(8,128)(2,1)S(1)}, bf16[256,1024]{1,0:T(8,128)(2,1)S(1)}, u32[]{:S(2)}, u32[]{:S(2)}) collective-permute-start(bf16[256,1024]{1,0:T(8,128)(2,1)S(1)} %collective-permute-done.4.own_ref), channel_id=1, source_target_pairs={{0,1},{1,0},{2,3},{3,2},{4,5},{5,4},{6,7},{7,6},{8,9},{9,8},{10,11... | collective-permute-start | bytes 1572872 | tf_op jit(solution)/shard_map/ppermute | solution.py:317
  95.3 21.8 %collective-permute-start.26 = (bf16[512,256]{1,0:T(8,128)(2,1)S(1)}, bf16[512,256]{1,0:T(8,128)(2,1)S(1)}, u32[]{:S(2)}, u32[]{:S(2)}) collective-permute-start(bf16[512,256]{1,0:T(8,128)(2,1)S(1)} %copy-done.26), channel_id=1, source_target_pairs={{0,16},{4,20},{8,24},{12,28},{16,0},{20,4},{24,8},{28,12},{1,17},{... | collective-permute-start | bytes 786440 | tf_op jit(solution)/shard_map/ppermute | solution.py:309
  95.5 24.2 %copy-start.18 = (bf16[512,256]{1,0:T(8,128)(2,1)S(1)}, bf16[512,256]{1,0:T(8,128)(2,1)}, u32[]{:S(2)}) copy-start(bf16[512,256]{1,0:T(8,128)(2,1)} %get-tuple-element.69) | copy-start | bytes 786436
  95.5 37.3 %collective-permute-start.31 = (bf16[1344,256]{1,0:T(8,128)(2,1)S(1)}, bf16[1344,256]{1,0:T(8,128)(2,1)S(1)}, u32[]{:S(2)}, u32[]{:S(2)}) collective-permute-start(bf16[1344,256]{1,0:T(8,128)(2,1)S(1)} %collective-permute-done.20.refs_2_), channel_id=1, source_target_pairs={{0,4},{4,0},{8,12},{12,8},{16,20},{20,16},{24,28},{28,24},{1,5},{5... | collective-permute-start | bytes 2064392 | tf_op jit(solution)/shard_map/ppermute | solution.py:313
  95.6 36.5 %collective-permute-start.32 = (bf16[832,256]{1,0:T(8,128)(2,1)S(1)}, bf16[832,256]{1,0:T(8,128)(2,1)S(1)}, u32[]{:S(2)}, u32[]{:S(2)}) collective-permute-start(bf16[832,256]{1,0:T(8,128)(2,1)S(1)} %pad_maximum_fusion.3), channel_id=1, source_target_pairs={{0,16},{4,20},{8,24},{12,28},{16,0},{20,4},{24,8},{28,12},{1,17},{... | collective-permute-start | bytes 1277960 | tf_op jit(solution)/shard_map/ppermute | solution.py:309
  117.2 8.2 %collective-permute-start.29 = (bf16[128,1024]{1,0:T(8,128)(2,1)S(1)}, bf16[128,1024]{1,0:T(8,128)(2,1)S(1)}, u32[]{:S(2)}, u32[]{:S(2)}) collective-permute-start(bf16[128,1024]{1,0:T(8,128)(2,1)S(1)} %slice.45), channel_id=1, source_target_pairs={{0,1},{1,0},{2,3},{3,2},{4,5},{5,4},{6,7},{7,6},{8,9},{9,8},{10,11... | collective-permute-start | bytes 786440 | tf_op jit(solution)/shard_map/ppermute | solution.py:317
  118.0 7.9 %collective-permute-start.28 = (bf16[128,1024]{1,0:T(8,128)(2,1)S(1)}, bf16[128,1024]{1,0:T(8,128)(2,1)S(1)}, u32[]{:S(2)}, u32[]{:S(2)}) collective-permute-start(bf16[128,1024]{1,0:T(8,128)(2,1)S(1)} %slice.44), channel_id=1, source_target_pairs={{0,2},{1,3},{2,0},{3,1},{4,6},{5,7},{6,4},{7,5},{8,10},{9,11},{10,... | collective-permute-start | bytes 786440 | tf_op jit(solution)/shard_map/ppermute | solution.py:317
  119.6 21.9 %collective-permute-start.35 = (bf16[528,256]{1,0:T(8,128)(2,1)S(1)}, bf16[528,256]{1,0:T(8,128)(2,1)S(1)}, u32[]{:S(2)}, u32[]{:S(2)}) collective-permute-start(bf16[528,256]{1,0:T(8,128)(2,1)S(1)} %concatenate.19), channel_id=1, source_target_pairs={{0,16},{4,20},{8,24},{12,28},{16,0},{20,4},{24,8},{28,12},{1,17},{... | collective-permute-start | bytes 811016 | tf_op jit(solution)/shard_map/ppermute | solution.py:309
  127.9 9.0 %collective-permute-start.30 = (bf16[512,256]{1,0:T(8,128)(2,1)S(1)}, bf16[512,256]{1,0:T(8,128)(2,1)S(1)}, u32[]{:S(2)}, u32[]{:S(2)}) collective-permute-start(bf16[512,256]{1,0:T(8,128)(2,1)S(1)} %collective-permute-done.26.refs_3_), channel_id=1, source_target_pairs={{0,4},{4,0},{8,12},{12,8},{16,20},{20,16},{24,28},{28,24},{1,5},{5... | collective-permute-start | bytes 786440 | tf_op jit(solution)/shard_map/ppermute | solution.py:313
  132.1 8.1 %collective-permute-start.34 = (bf16[512,256]{1,0:T(8,128)(2,1)S(1)}, bf16[512,256]{1,0:T(8,128)(2,1)S(1)}, u32[]{:S(2)}, u32[]{:S(2)}) collective-permute-start(bf16[512,256]{1,0:T(8,128)(2,1)S(1)} %slice.53), channel_id=1, source_target_pairs={{0,4},{4,0},{8,12},{12,8},{16,20},{20,16},{24,28},{28,24},{1,5},{5... | collective-permute-start | bytes 786440 | tf_op jit(solution)/shard_map/ppermute | solution.py:313
  132.2 4.6 %collective-permute-start.33 = (bf16[320,256]{1,0:T(8,128)(2,1)S(1)}, bf16[320,256]{1,0:T(8,128)(2,1)S(1)}, u32[]{:S(2)}, u32[]{:S(2)}) collective-permute-start(bf16[320,256]{1,0:T(8,128)(2,1)S(1)} %slice.52), channel_id=1, source_target_pairs={{0,4},{4,0},{8,12},{12,8},{16,20},{20,16},{24,28},{28,24},{1,5},{5... | collective-permute-start | bytes 491528 | tf_op jit(solution)/shard_map/ppermute | solution.py:313
  141.5 1.6 collective-permute-start.36
  141.6 3.0 %collective-permute-start.37 = (bf16[4,256,256]{2,1,0:T(8,128)(2,1)S(1)}, bf16[4,256,256]{2,1,0:T(8,128)(2,1)S(1)}, u32[]{:S(2)}, u32[]{:S(2)}) collective-permute-start(bf16[4,256,256]{2,1,0:T(8,128)(2,1)S(1)} %project.6.k_ref), channel_id=1, source_target_pairs={{0,4},{4,0},{8,12},{12,8},{16,20},{20,16},{24,28},{28,24},{1,5},{5... | collective-permute-start | bytes 1572872 | tf_op jit(solution)/shard_map/ppermute | solution.py:313
  144.4 2.0 %collective-permute-start.38 = (bf16[4,256,256]{2,1,0:T(8,128)(2,1)S(1)}, bf16[4,256,256]{2,1,0:T(8,128)(2,1)S(1)}, u32[]{:S(2)}, u32[]{:S(2)}) collective-permute-start(bf16[4,256,256]{2,1,0:T(8,128)(2,1)S(1)} %project.7.v_ref), channel_id=1, source_target_pairs={{0,4},{4,0},{8,12},{12,8},{16,20},{20,16},{24,28},{28,24},{1,5},{5... | collective-permute-start | bytes 1572872 | tf_op jit(solution)/shard_map/ppermute | solution.py:313
  150.3 11.4 %collective-permute-start.39 = (bf16[256,256]{1,0:T(8,128)(2,1)S(1)}, bf16[256,256]{1,0:T(8,128)(2,1)S(1)}, u32[]{:S(2)}, u32[]{:S(2)}) collective-permute-start(bf16[256,256]{1,0:T(8,128)(2,1)S(1)} %attend.3), channel_id=1, source_target_pairs={{0,16},{4,20},{8,24},{12,28},{16,0},{20,4},{24,8},{28,12},{1,17},{... | collective-permute-start | bytes 393224 | tf_op jit(solution)/shard_map/ppermute | solution.py:309
  157.7 8.2 %collective-permute-start.40 = (bf16[256,256]{1,0:T(8,128)(2,1)S(1)}, bf16[256,256]{1,0:T(8,128)(2,1)S(1)}, u32[]{:S(2)}, u32[]{:S(2)}) collective-permute-start(bf16[256,256]{1,0:T(8,128)(2,1)S(1)} %get-tuple-element.66), channel_id=1, source_target_pairs={{0,8},{4,12},{8,16},{12,20},{16,24},{20,28},{24,0},{28,4},{1,9},{5... | collective-permute-start | bytes 393224 | tf_op jit(solution)/shard_map/ppermute | solution.py:309
  158.9 8.4 %collective-permute-start.41 = (bf16[256,256]{1,0:T(8,128)(2,1)S(1)}, bf16[256,256]{1,0:T(8,128)(2,1)S(1)}, u32[]{:S(2)}, u32[]{:S(2)}) collective-permute-start(bf16[256,256]{1,0:T(8,128)(2,1)S(1)} %get-tuple-element.68), channel_id=1, source_target_pairs={{0,24},{4,28},{8,0},{12,4},{16,8},{20,12},{24,16},{28,20},{1,25},{... | collective-permute-start | bytes 393224 | tf_op jit(solution)/shard_map/ppermute | solution.py:309
  (25 other events, 159.6 us)

commit v14 on v13

--- a/solution.py
+++ b/solution.py
@@ -395,11 +395,10 @@
 
     early = (0, 1, 3)
     there["q2"] = swap_core(after(here["q2"], normed), zs)
-    there["kc2"], far_cache = [
-        swap_core(after(here["kc2"][a:b], normed), zs) for a, b in ((0, depth), (depth, None))
-    ]
     (q,) = project(place, normed, *sides("q0", "q1", "q3", "q2"), early + (2,), 1, True)
     k_early, v_early = project(place, normed, *sides("kvc0", "kvc1", "kvc3"), early, 2, False)
+    here["kc2"] = after(here["kc2"], k_early, v_early)
+    there["kc2"], far_cache = swap_core(here["kc2"][:depth], zs), swap_core(here["kc2"][depth:], zs)
     kept = sum(sides("kvc0", "kvc1", "kvc3"), []) + [here["kc2"], far_cache]
     ck, cv = pack(kept, [2 * depth] * (2 * zs - 2) + [depth, 0], crow)
     (k,) = project(place, after(normed, q, ck), *sides("kc2"), (2,), 1, True, (k_early,))

time: 170 us -> 169 us (level)
    ppermute x13, waiting for transfers between devices: 55 us -> 52.5 us  [shift_z(): return lax.ppermute(value, 'seq', pairs)]
  transfers between devices with their start and end apart: 42 -> 42, of which waited for: 22 -> 23; matrix products, arithmetic and copies ran while one was open for 4% -> 4% of each run, Pallas kernels for 20% -> 20%
where the time goes in v14:
time: 169 us
  waiting for transfers between devices  77.2 us (46%)
  Pallas kernels  40.1 us (24%)
  starting transfers between devices  36.7 us (22%)
  local copies, waits for them, and re-layouts  11.8 us (7%)
  other arithmetic  2.44 us (1%)
    ppermute x13, waiting for transfers between devices, shift_z(): return lax.ppermute(value, 'seq', pairs)  52.5 us
    ppermute x16, waiting for transfers between devices, swap_chan(): return lax.ppermute(value, 'chan', [(c, c ^ bit) for c in range(4)])  17.7 us
    ppermute x16, starting transfers between devices, swap_chan(): return lax.ppermute(value, 'chan', [(c, c ^ bit) for c in range(4)])  17.4 us
    ppermute x13, starting transfers between devices, shift_z(): return lax.ppermute(value, 'seq', pairs)  14.6 us
    pallas_call x3, Pallas kernels, attend(): pl.pallas_call(functools.partial(attend_kernel, shifts), in_specs=[SMEM]...  13.9 us
    pallas_call x4, Pallas kernels, project(): pl.pallas_call(functools.partial(project_kernel, shifts, zs, count), in_s...  9.86 us
    pallas_call x4, Pallas kernels, norm(): pl.pallas_call(functools.partial(norm_kernel, j), in_specs=[SMEM] + [VMEM...  8.27 us
    ppermute x12, waiting for transfers between devices, swap_core(): lax.ppermute(value, 'seq', [(2 * a + k, 2 * a + 1 - k) for a in range(zs)...  7.01 us
  transfers between devices with their start and end apart: 42, of which 23 were waited for; matrix products, arithmetic and copies ran while one was open for 4% of the time, Pallas kernels for 20%

profile of v14, /device:TPU:0, one launch (start us, length us, event | category | flops | bytes accessed | tf_op | source)
XLA Modules:
  0.0 168.7 jit_solution(10896561247612952969)
XLA Ops:
  0.0 1.2 fusion
  1.2 2.4 %collective-permute-start = (bf16[128,1024]{1,0:T(8,128)(2,1)S(1)}, bf16[128,1024]{1,0:T(8,128)(2,1)S(1)}, u32[]{:S(2)}, u32[]{:S(2)}) collective-permute-start(bf16[128,1024]{1,0:T(8,128)(2,1)S(1)} %fusion), channel_id=1, source_target_pairs={{0,4},{4,8},{8,12},{12,16},{16,20},{20,24},{24,28},{1,5},{5,9},{9,... | collective-permute-start | bytes 786440 | tf_op jit(solution)/shard_map/ppermute | solution.py:355
  3.7 1.9 %dynamic-slice_bitcast_fusion.10 = (bf16[512,256]{1,0:T(8,128)(2,1)}, bf16[512,256]{1,0:T(8,128)(2,1)}) fusion(bf16[512,3,1024]{2,0,1:T(8,128)(2,1)} %param.11, s32[]{:T(128)S(6)} %select_n.80, s32[]{:T(128)S(6)} %select_n.78), kind=kLoop, calls=%fused_computation.16 | loop fusion | bytes 1048584 | tf_op jit(solution)/shard_map/squeeze | solution.py:343
  5.6 4.6 %collective-permute-start.5 = (bf16[512,256]{1,0:T(8,128)(2,1)}, bf16[512,256]{1,0:T(8,128)(2,1)S(1)}, u32[]{:S(2)}, u32[]{:S(2)}) collective-permute-start(bf16[512,256]{1,0:T(8,128)(2,1)} %get-tuple-element.77), channel_id=1, source_target_pairs={{0,24},{4,28},{8,0},{12,4},{16,8},{20,12},{24,16},{28,20},{1,25},{... | collective-permute-start | bytes 786440 | tf_op jit(solution)/shard_map/ppermute | solution.py:309
  10.3 6.0 %hyena_filters.1.own_ref = bf16[256,1024]{1,0:T(8,128)(2,1)S(1)} custom-call(bf16[3,256,1024]{2,1,0:T(8,128)(2,1)S(1)} %bitcast.33, bf16[128,1024]{1,0:T(8,128)(2,1)S(1)} %pad_select_fusion.halo_ref, f32[64,128]{1,0:T(8,128)S(1)} %copy-done.16), custom_call_target="tpu_custom_call" | custom-call | flops 1 | bytes 1 | tf_op jit(solution)/shard_map/hyena_filters/pallas_call | solution.py:80
  17.3 5.6 %collective-permute-done.1.refs_1_ = bf16[512,256]{1,0:T(8,128)(2,1)S(1)} collective-permute-done((bf16[512,256]{1,0:T(8,128)(2,1)}, bf16[512,256]{1,0:T(8,128)(2,1)S(1)}, u32[]{:S(2)}, u32[]{:S(2)}) %collective-permute-start.1) | collective-permute-done | bytes 262176 | tf_op jit(solution)/shard_map/ppermute | solution.py:309
  22.9 1.5 collective-permute-start.6
  24.4 1.5 collective-permute-start.8
  27.2 1.2 dynamic-slice_bitcast_fusion
  29.4 1.4 collective-permute-start.13
  30.8 6.5 %collective-permute-done.6.x_ref = bf16[256,1024]{1,0:T(8,128)(2,1)S(1)} collective-permute-done((bf16[256,1024]{1,0:T(8,128)(2,1)S(1)}, bf16[256,1024]{1,0:T(8,128)(2,1)S(1)}, u32[]{:S(2)}, u32[]{:S(2)}) %collective-permute-start.6) | collective-permute-done | bytes 524320 | tf_op jit(solution)/shard_map/ppermute | solution.py:317
  37.3 1.6 collective-permute-start.7
  38.9 1.6 collective-permute-start.9
  40.6 2.8 %collective-permute-done.2.own_ref = bf16[256,1024]{1,0:T(8,128)(2,1)} collective-permute-done((bf16[256,1024]{1,0:T(8,128)(2,1)S(1)}, bf16[256,1024]{1,0:T(8,128)(2,1)}, u32[]{:S(2)}, u32[]{:S(2)}) %collective-permute-start.2) | collective-permute-done | bytes 524320 | tf_op jit(solution)/shard_map/ppermute | solution.py:309
  43.4 2.0 %collective-permute-done.7.d0_ref = bf16[128,1024]{1,0:T(8,128)(2,1)S(1)} collective-permute-done((bf16[128,1024]{1,0:T(8,128)(2,1)S(1)}, bf16[128,1024]{1,0:T(8,128)(2,1)S(1)}, u32[]{:S(2)}, u32[]{:S(2)}) %collective-permute-start.7) | collective-permute-done | bytes 262176 | tf_op jit(solution)/shard_map/ppermute | solution.py:317
  47.4 1.1 collective-permute-start.15
  48.5 1.3 collective-permute-start.10
  49.8 1.7 collective-permute-done.12.refs_4_
  51.5 1.0 copy-done.2
  52.6 1.0 copy-done.4
  55.5 1.9 %norm.4.rest_0_ = bf16[4,4,256,1024]{3,2,1,0:T(8,128)(2,1)S(1)} custom-call(s32[3]{0:T(128)S(1)} %pad_add_fusion.place_ref, bf16[256,1024]{1,0:T(8,128)(2,1)S(1)} %hyena_filters.1.own_ref, bf16[256,1024]{1,0:T(8,128)(2,1)S(1)} %copy-done.2, bf16[256,1024]{1,0:T(8,128)(2,1)S(1)} %copy-done.4, bf16[128,1024]{1,0:T(8,128)(2,1)S(1)} %copy-done.12, ...), custom_call_target="tpu_custom_call" | custom-call | flops 1 | bytes 1 | tf_op jit(solution)/shard_map/norm/pallas_call | solution.py:119
  57.7 2.3 %collective-permute-done.15.y_ref = bf16[256,1024]{1,0:T(8,128)(2,1)S(1)} collective-permute-done((bf16[256,1024]{1,0:T(8,128)(2,1)}, bf16[256,1024]{1,0:T(8,128)(2,1)S(1)}, u32[]{:S(2)}, u32[]{:S(2)}) %collective-permute-start.15) | collective-permute-done | bytes 524320 | tf_op jit(solution)/shard_map/ppermute | solution.py:317
  60.1 1.6 collective-permute-start.16
  62.6 1.3 collective-permute-start.14
  65.0 4.1 %collective-permute-done.3.own_ref = bf16[256,1024]{1,0:T(8,128)(2,1)S(1)} collective-permute-done((bf16[256,1024]{1,0:T(8,128)(2,1)}, bf16[256,1024]{1,0:T(8,128)(2,1)S(1)}, u32[]{:S(2)}, u32[]{:S(2)}) %collective-permute-start.3) | collective-permute-done | bytes 524320 | tf_op jit(solution)/shard_map/ppermute | solution.py:309
  69.1 1.2 collective-permute-start.22
  72.9 2.6 %norm.5.rest_0_ = bf16[4,4,256,1024]{3,2,1,0:T(8,128)(2,1)S(1)} custom-call(s32[3]{0:T(128)S(1)} %pad_add_fusion.place_ref, bf16[256,1024]{1,0:T(8,128)(2,1)} %collective-permute-done.2.own_ref, bf16[256,1024]{1,0:T(8,128)(2,1)} %collective-permute-done.10.x_ref, ...), custom_call_target="tpu_custom_call", output_to_operand_aliasing={{}: (7, {})} | custom-call | flops 1 | bytes 1 | tf_op jit(solution)/shard_map/norm/pallas_call | solution.py:119
  75.4 8.4 %collective-permute-done.20.refs_2_ = bf16[1344,256]{1,0:T(8,128)(2,1)S(1)} collective-permute-done((bf16[1344,256]{1,0:T(8,128)(2,1)S(1)}, bf16[1344,256]{1,0:T(8,128)(2,1)S(1)}, u32[]{:S(2)}, u32[]{:S(2)}) %collective-permute-start.20) | collective-permute-done | bytes 688160 | tf_op jit(solution)/shard_map/ppermute | solution.py:309
  84.9 9.4 %collective-permute-done.4.own_ref = bf16[256,1024]{1,0:T(8,128)(2,1)S(1)} collective-permute-done((bf16[256,1024]{1,0:T(8,128)(2,1)S(1)}, bf16[256,1024]{1,0:T(8,128)(2,1)S(1)}, u32[]{:S(2)}, u32[]{:S(2)}) %collective-permute-start.4) | collective-permute-done | bytes 524320 | tf_op jit(solution)/shard_map/ppermute | solution.py:309
  95.5 2.9 %collective-permute-start.32 = (bf16[832,256]{1,0:T(8,128)(2,1)S(1)}, bf16[832,256]{1,0:T(8,128)(2,1)S(1)}, u32[]{:S(2)}, u32[]{:S(2)}) collective-permute-start(bf16[832,256]{1,0:T(8,128)(2,1)S(1)} %pad_maximum_fusion.3), channel_id=1, source_target_pairs={{0,16},{4,20},{8,24},{12,28},{16,0},{20,4},{24,8},{28,12},{1,17},{... | collective-permute-start | bytes 1277960 | tf_op jit(solution)/shard_map/ppermute | solution.py:309
  98.4 1.9 %norm.6.rest_0_ = bf16[4,4,256,1024]{3,2,1,0:T(8,128)(2,1)S(1)} custom-call(s32[3]{0:T(128)S(1)} %pad_add_fusion.place_ref, bf16[256,1024]{1,0:T(8,128)(2,1)S(1)} %collective-permute-done.3.own_ref, bf16[256,1024]{1,0:T(8,128)(2,1)S(1)} %collective-permute-done.17.x_ref, ...), custom_call_target="tpu_custom_call", output_to_operand_aliasing={{}: (7, {})} | custom-call | flops 1 | bytes 1 | tf_op jit(solution)/shard_map/norm/pallas_call | solution.py:119
  100.3 18.2 %collective-permute-done.26.refs_3_ = bf16[512,256]{1,0:T(8,128)(2,1)S(1)} collective-permute-done((bf16[512,256]{1,0:T(8,128)(2,1)S(1)}, bf16[512,256]{1,0:T(8,128)(2,1)S(1)}, u32[]{:S(2)}, u32[]{:S(2)}) %collective-permute-start.26) | collective-permute-done | bytes 262176 | tf_op jit(solution)/shard_map/ppermute | solution.py:309
  119.3 1.6 collective-permute-start.28
  121.0 5.9 %collective-permute-done.29.d1_ref = bf16[128,1024]{1,0:T(8,128)(2,1)S(1)} collective-permute-done((bf16[128,1024]{1,0:T(8,128)(2,1)S(1)}, bf16[128,1024]{1,0:T(8,128)(2,1)S(1)}, u32[]{:S(2)}, u32[]{:S(2)}) %collective-permute-start.29) | collective-permute-done | bytes 262176 | tf_op jit(solution)/shard_map/ppermute | solution.py:317
  127.3 1.9 %norm.7.normed_ref = bf16[4,4,256,1024]{3,2,1,0:T(8,128)(2,1)S(1)} custom-call(s32[3]{0:T(128)S(1)} %pad_add_fusion.place_ref, bf16[256,1024]{1,0:T(8,128)(2,1)S(1)} %collective-permute-done.4.own_ref, bf16[256,1024]{1,0:T(8,128)(2,1)S(1)} %collective-permute-done.24.x_ref, ...), custom_call_target="tpu_custom_call", output_to_operand_aliasing={{}: (7, {})} | custom-call | flops 1 | bytes 1 | tf_op jit(solution)/shard_map/norm/pallas_call | solution.py:119
  129.3 4.0 %project.5 = (f32[4,256,256]{2,1,0:T(8,128)S(1)}, f32[4,256,256]{2,1,0:T(8,128)S(1)}) custom-call(s32[3]{0:T(128)S(1)} %pad_add_fusion.place_ref, bf16[4,4,256,1024]{3,2,1,0:T(8,128)(2,1)S(1)} %norm.7.normed_ref, bf16[1344,256]{1,0:T(8,128)(2,1)S(1)} %pad_maximum_fusion.refs_0_, bf16[1344,256]{1,0:T(8,128)(2,1)S(1)} %collective-permute-done.13.refs_1_, ...), custom_call_target="tpu_custom_call" | custom-call | flops 1 | bytes 1 | tf_op jit(solution)/shard_map/project/pallas_call | solution.py:155
  134.1 1.3 collective-permute-done.33.refs_7_
  135.5 3.3 %project.4.q_ref = bf16[4,256,256]{2,1,0:T(8,128)(2,1)S(1)} custom-call(s32[3]{0:T(128)S(1)} %pad_add_fusion.place_ref, bf16[4,4,256,1024]{3,2,1,0:T(8,128)(2,1)S(1)} %norm.7.normed_ref, bf16[512,256]{1,0:T(8,128)(2,1)S(1)} %get-tuple-element.74.refs_0_, bf16[512,256]{1,0:T(8,128)(2,1)S(1)} %copy-done.10, bf16[512,256]{1,0:T(8,128)(2,1)S(1)} %copy-done.8, ...), custom_call_target="tpu_custom_call" | custom-call | flops 1 | bytes 1 | tf_op jit(solution)/shard_map/project/pallas_call | solution.py:155
  138.8 1.3 project.6.k_ref
  141.7 1.3 project.7.v_ref
  143.4 1.6 collective-permute-done.38.vs_ref
  145.0 3.9 %attend.3 = bf16[256,256]{1,0:T(8,128)(2,1)S(1)} custom-call(s32[3]{0:T(128)S(1)} %pad_add_fusion.place_ref, bf16[4,256,256]{2,1,0:T(8,128)(2,1)S(1)} %project.4.q_ref, bf16[4,256,256]{2,1,0:T(8,128)(2,1)S(1)} %project.6.k_ref, bf16[4,256,256]{2,1,0:T(8,128)(2,1)S(1)} %project.7.v_ref, bf16[4,256,256]{2,1,0:T(8,128)(2,1)S(1)} %collective-permute-done.37.ks_ref, ...), custom_call_target="tpu_custom_call" | custom-call | flops 1 | bytes 1 | tf_op jit(solution)/shard_map/attend/pallas_call | solution.py:248
  149.0 7.4 %attend.4 = (bf16[256,256]{1,0:T(8,128)(2,1)S(1)}, bf16[256,256]{1,0:T(8,128)(2,1)S(1)}) custom-call(s32[3]{0:T(128)S(1)} %pad_add_fusion.place_ref, bf16[4,256,256]{2,1,0:T(8,128)(2,1)S(1)} %project.4.q_ref, bf16[4,256,256]{2,1,0:T(8,128)(2,1)S(1)} %project.6.k_ref, bf16[4,256,256]{2,1,0:T(8,128)(2,1)S(1)} %project.7.v_ref, ...), custom_call_target="tpu_custom_call" | custom-call | flops 1 | bytes 1 | tf_op jit(solution)/shard_map/attend/pallas_call | solution.py:248
  157.3 2.9 %collective-permute-start.41 = (bf16[256,256]{1,0:T(8,128)(2,1)S(1)}, bf16[256,256]{1,0:T(8,128)(2,1)S(1)}, u32[]{:S(2)}, u32[]{:S(2)}) collective-permute-start(bf16[256,256]{1,0:T(8,128)(2,1)S(1)} %get-tuple-element.66), channel_id=1, source_target_pairs={{0,24},{4,28},{8,0},{12,4},{16,8},{20,12},{24,16},{28,20},{1,25},{... | collective-permute-start | bytes 393224 | tf_op jit(solution)/shard_map/ppermute | solution.py:309
  160.3 2.6 %attend.5.refs_0_ = bf16[256,256]{1,0:T(8,128)(2,1)S(1)} custom-call(s32[3]{0:T(128)S(1)} %pad_add_fusion.place_ref, bf16[4,256,256]{2,1,0:T(8,128)(2,1)S(1)} %project.4.q_ref, bf16[4,256,256]{2,1,0:T(8,128)(2,1)S(1)} %project.6.k_ref, bf16[4,256,256]{2,1,0:T(8,128)(2,1)S(1)} %project.7.v_ref, bf16[4,256,256]{2,1,0:T(8,128)(2,1)S(1)} %collective-permute-done.37.ks_ref, ...), custom_call_target="tpu_custom_call" | custom-call | flops 1 | bytes 1 | tf_op jit(solution)/shard_map/attend/pallas_call | solution.py:248
  163.5 1.1 collective-permute-done.40.refs_1_
  164.6 1.5 collective-permute-done.41.refs_3_
  166.8 2.0 %join.1 = bf16[256,1024]{1,0:T(8,128)(2,1)} custom-call(s32[3]{0:T(128)} %copy-done.15, bf16[256,256]{1,0:T(8,128)(2,1)} %copy-done.5, bf16[256,256]{1,0:T(8,128)(2,1)} %copy-done.29, bf16[256,256]{1,0:T(8,128)(2,1)} %copy-done.28, bf16[256,256]{1,0:T(8,128)(2,1)} %copy-done.30), custom_call_target="tpu_custom_call" | custom-call | tf_op jit(solution)/shard_map/join/pallas_call | solution.py:298
  (133 shorter events, 21.2 us)
Async XLA Ops:
  1.2 8.9 %collective-permute-start = (bf16[128,1024]{1,0:T(8,128)(2,1)S(1)}, bf16[128,1024]{1,0:T(8,128)(2,1)S(1)}, u32[]{:S(2)}, u32[]{:S(2)}) collective-permute-start(bf16[128,1024]{1,0:T(8,128)(2,1)S(1)} %fusion), channel_id=1, source_target_pairs={{0,4},{4,8},{8,12},{12,16},{16,20},{20,24},{24,28},{1,5},{5,9},{9,... | collective-permute-start | bytes 786440 | tf_op jit(solution)/shard_map/ppermute | solution.py:355
  5.6 11.7 %collective-permute-start.5 = (bf16[512,256]{1,0:T(8,128)(2,1)}, bf16[512,256]{1,0:T(8,128)(2,1)S(1)}, u32[]{:S(2)}, u32[]{:S(2)}) collective-permute-start(bf16[512,256]{1,0:T(8,128)(2,1)} %get-tuple-element.77), channel_id=1, source_target_pairs={{0,24},{4,28},{8,0},{12,4},{16,8},{20,12},{24,16},{28,20},{1,25},{... | collective-permute-start | bytes 786440 | tf_op jit(solution)/shard_map/ppermute | solution.py:309
  10.2 12.8 %collective-permute-start.1 = (bf16[512,256]{1,0:T(8,128)(2,1)}, bf16[512,256]{1,0:T(8,128)(2,1)S(1)}, u32[]{:S(2)}, u32[]{:S(2)}) collective-permute-start(bf16[512,256]{1,0:T(8,128)(2,1)} %get-tuple-element.78), channel_id=1, source_target_pairs={{0,8},{4,12},{8,16},{12,20},{16,24},{20,28},{24,0},{28,4},{1,9},{5... | collective-permute-start | bytes 786440 | tf_op jit(solution)/shard_map/ppermute | solution.py:309
  10.3 16.9 %copy-start.17 = (bf16[512,3,1024]{2,0,1:T(8,128)(2,1)S(1)}, bf16[512,3,1024]{2,0,1:T(8,128)(2,1)}, u32[]{:S(2)}) copy-start(bf16[512,3,1024]{2,0,1:T(8,128)(2,1)} %param.11) | copy-start | bytes 9437188
  22.9 14.3 %collective-permute-start.6 = (bf16[256,1024]{1,0:T(8,128)(2,1)S(1)}, bf16[256,1024]{1,0:T(8,128)(2,1)S(1)}, u32[]{:S(2)}, u32[]{:S(2)}) collective-permute-start(bf16[256,1024]{1,0:T(8,128)(2,1)S(1)} %hyena_filters.1.own_ref), channel_id=1, source_target_pairs={{0,1},{1,0},{2,3},{3,2},{4,5},{5,4},{6,7},{7,6},{8,9},{9,8},{10,11... | collective-permute-start | bytes 1572872 | tf_op jit(solution)/shard_map/ppermute | solution.py:317
  24.4 14.4 %collective-permute-start.8 = (bf16[256,1024]{1,0:T(8,128)(2,1)S(1)}, bf16[256,1024]{1,0:T(8,128)(2,1)S(1)}, u32[]{:S(2)}, u32[]{:S(2)}) collective-permute-start(bf16[256,1024]{1,0:T(8,128)(2,1)S(1)} %hyena_filters.1.own_ref), channel_id=1, source_target_pairs={{0,2},{1,3},{2,0},{3,1},{4,6},{5,7},{6,4},{7,5},{8,10},{9,11},{10,... | collective-permute-start | bytes 1572872 | tf_op jit(solution)/shard_map/ppermute | solution.py:317
  26.7 16.7 %collective-permute-start.2 = (bf16[256,1024]{1,0:T(8,128)(2,1)S(1)}, bf16[256,1024]{1,0:T(8,128)(2,1)}, u32[]{:S(2)}, u32[]{:S(2)}) collective-permute-start(bf16[256,1024]{1,0:T(8,128)(2,1)S(1)} %hyena_filters.1.own_ref), channel_id=1, source_target_pairs={{0,8},{4,12},{8,16},{12,20},{16,24},{20,28},{24,0},{28,4},{1,9},{5... | collective-permute-start | bytes 1572872 | tf_op jit(solution)/shard_map/ppermute | solution.py:309
  29.4 22.2 %copy-start.6 = (f32[4096]{0:T(1024)S(1)}, f32[4096]{0:T(1024)}, u32[]{:S(2)}) copy-start(f32[4096]{0:T(1024)} %param.10) | copy-start | bytes 49156
  29.4 28.4 %collective-permute-start.13 = (bf16[1344,256]{1,0:T(8,128)(2,1)}, bf16[1344,256]{1,0:T(8,128)(2,1)S(1)}, u32[]{:S(2)}, u32[]{:S(2)}) collective-permute-start(bf16[1344,256]{1,0:T(8,128)(2,1)} %pad_maximum_fusion.1), channel_id=1, source_target_pairs={{0,8},{4,12},{8,16},{12,20},{16,24},{20,28},{24,0},{28,4},{1,9},{5... | collective-permute-start | bytes 2064392 | tf_op jit(solution)/shard_map/ppermute | solution.py:309
  37.3 8.1 %collective-permute-start.7 = (bf16[128,1024]{1,0:T(8,128)(2,1)S(1)}, bf16[128,1024]{1,0:T(8,128)(2,1)S(1)}, u32[]{:S(2)}, u32[]{:S(2)}) collective-permute-start(bf16[128,1024]{1,0:T(8,128)(2,1)S(1)} %slice.50), channel_id=1, source_target_pairs={{0,2},{1,3},{2,0},{3,1},{4,6},{5,7},{6,4},{7,5},{8,10},{9,11},{10,... | collective-permute-start | bytes 786440 | tf_op jit(solution)/shard_map/ppermute | solution.py:317
  38.9 7.8 %collective-permute-start.9 = (bf16[128,1024]{1,0:T(8,128)(2,1)S(1)}, bf16[128,1024]{1,0:T(8,128)(2,1)S(1)}, u32[]{:S(2)}, u32[]{:S(2)}) collective-permute-start(bf16[128,1024]{1,0:T(8,128)(2,1)S(1)} %slice.51), channel_id=1, source_target_pairs={{0,1},{1,0},{2,3},{3,2},{4,5},{5,4},{6,7},{7,6},{8,9},{9,8},{10,11... | collective-permute-start | bytes 786440 | tf_op jit(solution)/shard_map/ppermute | solution.py:317
  40.5 17.3 %collective-permute-start.11 = (bf16[1344,256]{1,0:T(8,128)(2,1)S(1)}, bf16[1344,256]{1,0:T(8,128)(2,1)S(1)}, u32[]{:S(2)}, u32[]{:S(2)}) collective-permute-start(bf16[1344,256]{1,0:T(8,128)(2,1)S(1)} %pad_maximum_fusion.refs_0_), channel_id=1, source_target_pairs={{0,4},{4,0},{8,12},{12,8},{16,20},{20,16},{24,28},{28,24},{1,5},{5... | collective-permute-start | bytes 2064392 | tf_op jit(solution)/shard_map/ppermute | solution.py:313
  47.4 12.7 %collective-permute-start.15 = (bf16[256,1024]{1,0:T(8,128)(2,1)}, bf16[256,1024]{1,0:T(8,128)(2,1)S(1)}, u32[]{:S(2)}, u32[]{:S(2)}) collective-permute-start(bf16[256,1024]{1,0:T(8,128)(2,1)} %collective-permute-done.2.own_ref), channel_id=1, source_target_pairs={{0,2},{1,3},{2,0},{3,1},{4,6},{5,7},{6,4},{7,5},{8,10},{9,11},{10,... | collective-permute-start | bytes 1572872 | tf_op jit(solution)/shard_map/ppermute | solution.py:317
  48.5 13.2 %collective-permute-start.10 = (bf16[256,1024]{1,0:T(8,128)(2,1)}, bf16[256,1024]{1,0:T(8,128)(2,1)}, u32[]{:S(2)}, u32[]{:S(2)}) collective-permute-start(bf16[256,1024]{1,0:T(8,128)(2,1)} %collective-permute-done.2.own_ref), channel_id=1, source_target_pairs={{0,1},{1,0},{2,3},{3,2},{4,5},{5,4},{6,7},{7,6},{8,9},{9,8},{10,11... | collective-permute-start | bytes 1572872 | tf_op jit(solution)/shard_map/ppermute | solution.py:317
  49.8 1.7 collective-permute-start.12
  51.5 17.6 %collective-permute-start.3 = (bf16[256,1024]{1,0:T(8,128)(2,1)}, bf16[256,1024]{1,0:T(8,128)(2,1)S(1)}, u32[]{:S(2)}, u32[]{:S(2)}) collective-permute-start(bf16[256,1024]{1,0:T(8,128)(2,1)} %collective-permute-done.2.own_ref), channel_id=1, source_target_pairs={{0,8},{4,12},{8,16},{12,20},{16,24},{20,28},{24,0},{28,4},{1,9},{5... | collective-permute-start | bytes 1572872 | tf_op jit(solution)/shard_map/ppermute | solution.py:309
  51.5 108.7 %copy-start.15 = (s32[3]{0:T(128)}, s32[3]{0:T(128)S(1)}, u32[]{:S(2)}) copy-start(s32[3]{0:T(128)S(1)} %pad_add_fusion.place_ref) | copy-start | bytes 40
  60.1 9.0 %collective-permute-start.16 = (bf16[128,1024]{1,0:T(8,128)(2,1)S(1)}, bf16[128,1024]{1,0:T(8,128)(2,1)S(1)}, u32[]{:S(2)}, u32[]{:S(2)}) collective-permute-start(bf16[128,1024]{1,0:T(8,128)(2,1)S(1)} %slice.41), channel_id=1, source_target_pairs={{0,1},{1,0},{2,3},{3,2},{4,5},{5,4},{6,7},{7,6},{8,9},{9,8},{10,11... | collective-permute-start | bytes 786440 | tf_op jit(solution)/shard_map/ppermute | solution.py:317
  62.6 6.5 %collective-permute-start.14 = (bf16[128,1024]{1,0:T(8,128)(2,1)S(1)}, bf16[128,1024]{1,0:T(8,128)(2,1)S(1)}, u32[]{:S(2)}, u32[]{:S(2)}) collective-permute-start(bf16[128,1024]{1,0:T(8,128)(2,1)S(1)} %slice.40), channel_id=1, source_target_pairs={{0,2},{1,3},{2,0},{3,1},{4,6},{5,7},{6,4},{7,5},{8,10},{9,11},{10,... | collective-permute-start | bytes 786440 | tf_op jit(solution)/shard_map/ppermute | solution.py:317
  64.0 31.4 %copy-start.26 = (bf16[512,256]{1,0:T(8,128)(2,1)S(1)}, bf16[512,256]{1,0:T(8,128)(2,1)}, u32[]{:S(2)}) copy-start(bf16[512,256]{1,0:T(8,128)(2,1)} %get-tuple-element.50) | copy-start | bytes 786436
  64.0 31.5 %copy-start.19 = (bf16[512,256]{1,0:T(8,128)(2,1)S(1)}, bf16[512,256]{1,0:T(8,128)(2,1)}, u32[]{:S(2)}) copy-start(bf16[512,256]{1,0:T(8,128)(2,1)} %get-tuple-element.68) | copy-start | bytes 786436
  64.0 19.9 %collective-permute-start.20 = (bf16[1344,256]{1,0:T(8,128)(2,1)S(1)}, bf16[1344,256]{1,0:T(8,128)(2,1)S(1)}, u32[]{:S(2)}, u32[]{:S(2)}) collective-permute-start(bf16[1344,256]{1,0:T(8,128)(2,1)S(1)} %pad_maximum_fusion.2), channel_id=1, source_target_pairs={{0,24},{4,28},{8,0},{12,4},{16,8},{20,12},{24,16},{28,20},{1,25},{... | collective-permute-start | bytes 2064392 | tf_op jit(solution)/shard_map/ppermute | solution.py:309
  69.1 14.8 %collective-permute-start.22 = (bf16[256,1024]{1,0:T(8,128)(2,1)S(1)}, bf16[256,1024]{1,0:T(8,128)(2,1)S(1)}, u32[]{:S(2)}, u32[]{:S(2)}) collective-permute-start(bf16[256,1024]{1,0:T(8,128)(2,1)S(1)} %collective-permute-done.3.own_ref), channel_id=1, source_target_pairs={{0,2},{1,3},{2,0},{3,1},{4,6},{5,7},{6,4},{7,5},{8,10},{9,11},{10,... | collective-permute-start | bytes 1572872 | tf_op jit(solution)/shard_map/ppermute | solution.py:317
  70.3 13.9 %collective-permute-start.17 = (bf16[256,1024]{1,0:T(8,128)(2,1)S(1)}, bf16[256,1024]{1,0:T(8,128)(2,1)S(1)}, u32[]{:S(2)}, u32[]{:S(2)}) collective-permute-start(bf16[256,1024]{1,0:T(8,128)(2,1)S(1)} %collective-permute-done.3.own_ref), channel_id=1, source_target_pairs={{0,1},{1,0},{2,3},{3,2},{4,5},{5,4},{6,7},{7,6},{8,9},{9,8},{10,11... | collective-permute-start | bytes 1572872 | tf_op jit(solution)/shard_map/ppermute | solution.py:317
  70.8 1.5 collective-permute-start.18
  70.8 1.9 %collective-permute-start.19 = (bf16[512,256]{1,0:T(8,128)(2,1)S(1)}, bf16[512,256]{1,0:T(8,128)(2,1)S(1)}, u32[]{:S(2)}, u32[]{:S(2)}) collective-permute-start(bf16[512,256]{1,0:T(8,128)(2,1)S(1)} %copy-done.8), channel_id=1, source_target_pairs={{0,4},{4,0},{8,12},{12,8},{16,20},{20,16},{24,28},{28,24},{1,5},{5... | collective-permute-start | bytes 786440 | tf_op jit(solution)/shard_map/ppermute | solution.py:313
  72.3 22.0 %collective-permute-start.4 = (bf16[256,1024]{1,0:T(8,128)(2,1)S(1)}, bf16[256,1024]{1,0:T(8,128)(2,1)S(1)}, u32[]{:S(2)}, u32[]{:S(2)}) collective-permute-start(bf16[256,1024]{1,0:T(8,128)(2,1)S(1)} %collective-permute-done.3.own_ref), channel_id=1, source_target_pairs={{0,8},{4,12},{8,16},{12,20},{16,24},{20,28},{24,0},{28,4},{1,9},{5... | collective-permute-start | bytes 1572872 | tf_op jit(solution)/shard_map/ppermute | solution.py:309
  72.7 22.8 %collective-permute-start.25 = (bf16[1344,256]{1,0:T(8,128)(2,1)S(1)}, bf16[1344,256]{1,0:T(8,128)(2,1)S(1)}, u32[]{:S(2)}, u32[]{:S(2)}) collective-permute-start(bf16[1344,256]{1,0:T(8,128)(2,1)S(1)} %collective-permute-done.13.refs_1_), channel_id=1, source_target_pairs={{0,4},{4,0},{8,12},{12,8},{16,20},{20,16},{24,28},{28,24},{1,5},{5... | collective-permute-start | bytes 2064392 | tf_op jit(solution)/shard_map/ppermute | solution.py:313
  83.9 10.5 %collective-permute-start.23 = (bf16[128,1024]{1,0:T(8,128)(2,1)S(1)}, bf16[128,1024]{1,0:T(8,128)(2,1)S(1)}, u32[]{:S(2)}, u32[]{:S(2)}) collective-permute-start(bf16[128,1024]{1,0:T(8,128)(2,1)S(1)} %slice.43), channel_id=1, source_target_pairs={{0,1},{1,0},{2,3},{3,2},{4,5},{5,4},{6,7},{7,6},{8,9},{9,8},{10,11... | collective-permute-start | bytes 786440 | tf_op jit(solution)/shard_map/ppermute | solution.py:317
  84.2 10.1 %collective-permute-start.21 = (bf16[128,1024]{1,0:T(8,128)(2,1)S(1)}, bf16[128,1024]{1,0:T(8,128)(2,1)S(1)}, u32[]{:S(2)}, u32[]{:S(2)}) collective-permute-start(bf16[128,1024]{1,0:T(8,128)(2,1)S(1)} %slice.42), channel_id=1, source_target_pairs={{0,2},{1,3},{2,0},{3,1},{4,6},{5,7},{6,4},{7,5},{8,10},{9,11},{10,... | collective-permute-start | bytes 786440 | tf_op jit(solution)/shard_map/ppermute | solution.py:317
  94.3 24.2 %collective-permute-start.27 = (bf16[256,1024]{1,0:T(8,128)(2,1)S(1)}, bf16[256,1024]{1,0:T(8,128)(2,1)S(1)}, u32[]{:S(2)}, u32[]{:S(2)}) collective-permute-start(bf16[256,1024]{1,0:T(8,128)(2,1)S(1)} %collective-permute-done.4.own_ref), channel_id=1, source_target_pairs={{0,2},{1,3},{2,0},{3,1},{4,6},{5,7},{6,4},{7,5},{8,10},{9,11},{10,... | collective-permute-start | bytes 1572872 | tf_op jit(solution)/shard_map/ppermute | solution.py:317
  94.8 24.5 %collective-permute-start.24 = (bf16[256,1024]{1,0:T(8,128)(2,1)S(1)}, bf16[256,1024]{1,0:T(8,128)(2,1)S(1)}, u32[]{:S(2)}, u32[]{:S(2)}) collective-permute-start(bf16[256,1024]{1,0:T(8,128)(2,1)S(1)} %collective-permute-done.4.own_ref), channel_id=1, source_target_pairs={{0,1},{1,0},{2,3},{3,2},{4,5},{5,4},{6,7},{7,6},{8,9},{9,8},{10,11... | collective-permute-start | bytes 1572872 | tf_op jit(solution)/shard_map/ppermute | solution.py:317
  95.3 34.0 %collective-permute-start.31 = (bf16[1344,256]{1,0:T(8,128)(2,1)S(1)}, bf16[1344,256]{1,0:T(8,128)(2,1)S(1)}, u32[]{:S(2)}, u32[]{:S(2)}) collective-permute-start(bf16[1344,256]{1,0:T(8,128)(2,1)S(1)} %collective-permute-done.20.refs_2_), channel_id=1, source_target_pairs={{0,4},{4,0},{8,12},{12,8},{16,20},{20,16},{24,28},{28,24},{1,5},{5... | collective-permute-start | bytes 2064392 | tf_op jit(solution)/shard_map/ppermute | solution.py:313
  95.3 23.2 %collective-permute-start.26 = (bf16[512,256]{1,0:T(8,128)(2,1)S(1)}, bf16[512,256]{1,0:T(8,128)(2,1)S(1)}, u32[]{:S(2)}, u32[]{:S(2)}) collective-permute-start(bf16[512,256]{1,0:T(8,128)(2,1)S(1)} %copy-done.26), channel_id=1, source_target_pairs={{0,16},{4,20},{8,24},{12,28},{16,0},{20,4},{24,8},{28,12},{1,17},{... | collective-permute-start | bytes 786440 | tf_op jit(solution)/shard_map/ppermute | solution.py:309
  95.5 25.4 %copy-start.18 = (bf16[512,256]{1,0:T(8,128)(2,1)S(1)}, bf16[512,256]{1,0:T(8,128)(2,1)}, u32[]{:S(2)}) copy-start(bf16[512,256]{1,0:T(8,128)(2,1)} %get-tuple-element.67) | copy-start | bytes 786436
  95.5 37.9 %collective-permute-start.32 = (bf16[832,256]{1,0:T(8,128)(2,1)S(1)}, bf16[832,256]{1,0:T(8,128)(2,1)S(1)}, u32[]{:S(2)}, u32[]{:S(2)}) collective-permute-start(bf16[832,256]{1,0:T(8,128)(2,1)S(1)} %pad_maximum_fusion.3), channel_id=1, source_target_pairs={{0,16},{4,20},{8,24},{12,28},{16,0},{20,4},{24,8},{28,12},{1,17},{... | collective-permute-start | bytes 1277960 | tf_op jit(solution)/shard_map/ppermute | solution.py:309
  118.5 8.3 %collective-permute-start.29 = (bf16[128,1024]{1,0:T(8,128)(2,1)S(1)}, bf16[128,1024]{1,0:T(8,128)(2,1)S(1)}, u32[]{:S(2)}, u32[]{:S(2)}) collective-permute-start(bf16[128,1024]{1,0:T(8,128)(2,1)S(1)} %slice.45), channel_id=1, source_target_pairs={{0,1},{1,0},{2,3},{3,2},{4,5},{5,4},{6,7},{7,6},{8,9},{9,8},{10,11... | collective-permute-start | bytes 786440 | tf_op jit(solution)/shard_map/ppermute | solution.py:317
  119.3 8.0 %collective-permute-start.28 = (bf16[128,1024]{1,0:T(8,128)(2,1)S(1)}, bf16[128,1024]{1,0:T(8,128)(2,1)S(1)}, u32[]{:S(2)}, u32[]{:S(2)}) collective-permute-start(bf16[128,1024]{1,0:T(8,128)(2,1)S(1)} %slice.44), channel_id=1, source_target_pairs={{0,2},{1,3},{2,0},{3,1},{4,6},{5,7},{6,4},{7,5},{8,10},{9,11},{10,... | collective-permute-start | bytes 786440 | tf_op jit(solution)/shard_map/ppermute | solution.py:317
  120.9 19.2 %collective-permute-start.35 = (bf16[528,256]{1,0:T(8,128)(2,1)S(1)}, bf16[528,256]{1,0:T(8,128)(2,1)S(1)}, u32[]{:S(2)}, u32[]{:S(2)}) collective-permute-start(bf16[528,256]{1,0:T(8,128)(2,1)S(1)} %concatenate.19), channel_id=1, source_target_pairs={{0,16},{4,20},{8,24},{12,28},{16,0},{20,4},{24,8},{28,12},{1,17},{... | collective-permute-start | bytes 811016 | tf_op jit(solution)/shard_map/ppermute | solution.py:309
  129.2 6.3 %collective-permute-start.30 = (bf16[512,256]{1,0:T(8,128)(2,1)S(1)}, bf16[512,256]{1,0:T(8,128)(2,1)S(1)}, u32[]{:S(2)}, u32[]{:S(2)}) collective-permute-start(bf16[512,256]{1,0:T(8,128)(2,1)S(1)} %collective-permute-done.26.refs_3_), channel_id=1, source_target_pairs={{0,4},{4,0},{8,12},{12,8},{16,20},{20,16},{24,28},{28,24},{1,5},{5... | collective-permute-start | bytes 786440 | tf_op jit(solution)/shard_map/ppermute | solution.py:313
  133.4 5.4 %collective-permute-start.34 = (bf16[512,256]{1,0:T(8,128)(2,1)S(1)}, bf16[512,256]{1,0:T(8,128)(2,1)S(1)}, u32[]{:S(2)}, u32[]{:S(2)}) collective-permute-start(bf16[512,256]{1,0:T(8,128)(2,1)S(1)} %slice.47), channel_id=1, source_target_pairs={{0,4},{4,0},{8,12},{12,8},{16,20},{20,16},{24,28},{28,24},{1,5},{5... | collective-permute-start | bytes 786440 | tf_op jit(solution)/shard_map/ppermute | solution.py:313
  133.9 1.5 collective-permute-start.33
  140.1 1.6 collective-permute-start.36
  140.5 2.9 %collective-permute-start.37 = (bf16[4,256,256]{2,1,0:T(8,128)(2,1)S(1)}, bf16[4,256,256]{2,1,0:T(8,128)(2,1)S(1)}, u32[]{:S(2)}, u32[]{:S(2)}) collective-permute-start(bf16[4,256,256]{2,1,0:T(8,128)(2,1)S(1)} %project.6.k_ref), channel_id=1, source_target_pairs={{0,4},{4,0},{8,12},{12,8},{16,20},{20,16},{24,28},{28,24},{1,5},{5... | collective-permute-start | bytes 1572872 | tf_op jit(solution)/shard_map/ppermute | solution.py:313
  143.0 2.0 %collective-permute-start.38 = (bf16[4,256,256]{2,1,0:T(8,128)(2,1)S(1)}, bf16[4,256,256]{2,1,0:T(8,128)(2,1)S(1)}, u32[]{:S(2)}, u32[]{:S(2)}) collective-permute-start(bf16[4,256,256]{2,1,0:T(8,128)(2,1)S(1)} %project.7.v_ref), channel_id=1, source_target_pairs={{0,4},{4,0},{8,12},{12,8},{16,20},{20,16},{24,28},{28,24},{1,5},{5... | collective-permute-start | bytes 1572872 | tf_op jit(solution)/shard_map/ppermute | solution.py:313
  148.9 11.4 %collective-permute-start.39 = (bf16[256,256]{1,0:T(8,128)(2,1)S(1)}, bf16[256,256]{1,0:T(8,128)(2,1)S(1)}, u32[]{:S(2)}, u32[]{:S(2)}) collective-permute-start(bf16[256,256]{1,0:T(8,128)(2,1)S(1)} %attend.3), channel_id=1, source_target_pairs={{0,16},{4,20},{8,24},{12,28},{16,0},{20,4},{24,8},{28,12},{1,17},{... | collective-permute-start | bytes 393224 | tf_op jit(solution)/shard_map/ppermute | solution.py:309
  156.4 8.2 %collective-permute-start.40 = (bf16[256,256]{1,0:T(8,128)(2,1)S(1)}, bf16[256,256]{1,0:T(8,128)(2,1)S(1)}, u32[]{:S(2)}, u32[]{:S(2)}) collective-permute-start(bf16[256,256]{1,0:T(8,128)(2,1)S(1)} %get-tuple-element.64), channel_id=1, source_target_pairs={{0,8},{4,12},{8,16},{12,20},{16,24},{20,28},{24,0},{28,4},{1,9},{5... | collective-permute-start | bytes 393224 | tf_op jit(solution)/shard_map/ppermute | solution.py:309
  157.3 8.8 %collective-permute-start.41 = (bf16[256,256]{1,0:T(8,128)(2,1)S(1)}, bf16[256,256]{1,0:T(8,128)(2,1)S(1)}, u32[]{:S(2)}, u32[]{:S(2)}) collective-permute-start(bf16[256,256]{1,0:T(8,128)(2,1)S(1)} %get-tuple-element.66), channel_id=1, source_target_pairs={{0,24},{4,28},{8,0},{12,4},{16,8},{20,12},{24,16},{28,20},{1,25},{... | collective-permute-start | bytes 393224 | tf_op jit(solution)/shard_map/ppermute | solution.py:309
  (25 other events, 159.7 us)

commit v15 on v12

--- a/solution.py
+++ b/solution.py
@@ -275,17 +275,12 @@
 
 
 def join_kernel(place_ref, *refs):
-    pieces, (out_ref, sems) = refs[:-2], refs[-2:]
+    pieces, out_ref = refs[:-1], refs[-1]
     zs = len(pieces)
     cols = pieces[0].shape[1]
-    copies = []
     for r, piece in enumerate(pieces):
-        at = pl.multiple_of(lax.rem(place_ref[1] + zs - r, zs) * cols, cols)
-        copies.append(pltpu.make_async_copy(piece, out_ref.at[:, pl.ds(at, cols)], sems.at[r]))
-    for copy in copies:
-        copy.start()
-    for copy in copies:
-        copy.wait()
+        at = lax.rem(place_ref[1] + zs - r, zs) * cols
+        out_ref[:, pl.ds(pl.multiple_of(at, cols), cols)] = piece[...]
 
 
 def join(place, pieces):
@@ -293,10 +288,9 @@
     out = (rows, cols * len(pieces))
     return pl.pallas_call(
         join_kernel,
-        in_specs=[SMEM] + [pl.BlockSpec(memory_space=pl.ANY)] * len(pieces),
-        out_specs=pl.BlockSpec(memory_space=pl.ANY),
+        in_specs=[SMEM] + [VMEM] * len(pieces),
+        out_specs=whole(out),
         out_shape=jax.ShapeDtypeStruct(out, BF16),
-        scratch_shapes=[pltpu.SemaphoreType.DMA((len(pieces),))],
         name="join",
     )(place, *pieces)
 
@@ -341,6 +335,8 @@
             for p in kind
             if p != "c"
         ]
+        if kind == "v":
+            parts.append(jnp.zeros((16, cols), BF16))
         if "c" in kind:
             parts += [lax.dynamic_slice_in_dim(c, at, cols, 1) for c in caches]
         return jnp.concatenate(parts, axis=0)
@@ -389,12 +385,13 @@
         return [[side[item] for item in items] for side in (here, there)]
 
     early = (0, 1, 3)
-    there["q2"] = swap_core(after(here["q2"], diag0, diag1), zs)
-    there["kc2"] = swap_core(after(here["kc2"], diag0, diag1), zs)
+    there["q2"] = swap_core(after(here["q2"], normed), zs)
     (q,) = project(place, normed, *sides("q0", "q1", "q3", "q2"), early + (2,), 1, True)
     k_early, v_early = project(place, normed, *sides("kvc0", "kvc1", "kvc3"), early, 2, False)
-    kept = sum(sides("kvc0", "kvc1", "kc2", "kvc3"), [])
-    ck, cv = pack(kept, [depth if i % zs == 2 else 2 * depth for i in range(2 * zs)], crow)
+    here["kc2"] = after(here["kc2"], k_early, v_early)
+    there["kc2"], far_cache = swap_core(here["kc2"][:depth], zs), swap_core(here["kc2"][depth:], zs)
+    kept = sum(sides("kvc0", "kvc1", "kvc3"), []) + [here["kc2"], far_cache]
+    ck, cv = pack(kept, [2 * depth] * (2 * zs - 2) + [depth, 0], crow)
     (k,) = project(place, after(normed, q, ck), *sides("kc2"), (2,), 1, True, (k_early,))
     k_sib = swap_core(k, zs)
     there["v2"] = swap_core(after(here["v2"], k), zs)

time: 186 us -> 169 us (0.909)
  Pallas kernels: 55.5 us -> 39.6 us
    pallas_call x1, Pallas kernels: 17.7 us -> 1.97 us  [join(): pl.pallas_call(join_kernel, in_specs=[SMEM] + [VMEM] * len(pieces), out_s...]
    ppermute x13, waiting for transfers between devices: 62.1 us -> 52.6 us  [shift_z(): return lax.ppermute(value, 'seq', pairs)]
    ppermute x16, waiting for transfers between devices: 11.5 us -> 17.7 us  [swap_chan(): return lax.ppermute(value, 'chan', [(c, c ^ bit) for c in range(4)])]
    ppermute x11 -> x12, waiting for transfers between devices: 5.5 us -> 7.01 us  [swap_core(): lax.ppermute(value, 'seq', [(2 * a + k, 2 * a + 1 - k) for a in range(zs)...]
  transfers between devices with their start and end apart: 41 -> 42, of which waited for: 20 -> 23; matrix products, arithmetic and copies ran while one was open for 3% -> 4% of each run, Pallas kernels for 18% -> 20%
where the time goes in v15:
time: 169 us; the launch traced here: 168 us
  waiting for transfers between devices  77.4 us (46%)
  Pallas kernels  39.6 us (23%)
  starting transfers between devices  36.7 us (22%)
  local copies, waits for them, and re-layouts  11.8 us (7%)
  other arithmetic  2.44 us (1%)
    ppermute x13, waiting for transfers between devices, shift_z(): return lax.ppermute(value, 'seq', pairs)  52.6 us
    ppermute x16, waiting for transfers between devices, swap_chan(): return lax.ppermute(value, 'chan', [(c, c ^ bit) for c in range(4)])  17.7 us
    ppermute x16, starting transfers between devices, swap_chan(): return lax.ppermute(value, 'chan', [(c, c ^ bit) for c in range(4)])  17.4 us
    ppermute x13, starting transfers between devices, shift_z(): return lax.ppermute(value, 'seq', pairs)  14.6 us
    pallas_call x3, Pallas kernels, attend(): pl.pallas_call(functools.partial(attend_kernel, shifts), in_specs=[SMEM]...  13.4 us
    pallas_call x4, Pallas kernels, project(): pl.pallas_call(functools.partial(project_kernel, shifts, zs, count), in_s...  9.86 us
    pallas_call x4, Pallas kernels, norm(): pl.pallas_call(functools.partial(norm_kernel, j), in_specs=[SMEM] + [VMEM...  8.27 us
    ppermute x12, waiting for transfers between devices, swap_core(): lax.ppermute(value, 'seq', [(2 * a + k, 2 * a + 1 - k) for a in range(zs)...  7.01 us
  transfers between devices with their start and end apart: 42, of which 23 were waited for; matrix products, arithmetic and copies ran while one was open for 4% of the time, Pallas kernels for 20%

profile of v15, /device:TPU:0, one launch (start us, length us, event | category | flops | bytes accessed | tf_op | source)
XLA Modules:
  0.0 168.4 jit_solution(16826309465526536574)
XLA Ops:
  0.0 1.2 fusion
  1.2 2.4 %collective-permute-start = (bf16[128,1024]{1,0:T(8,128)(2,1)S(1)}, bf16[128,1024]{1,0:T(8,128)(2,1)S(1)}, u32[]{:S(2)}, u32[]{:S(2)}) collective-permute-start(bf16[128,1024]{1,0:T(8,128)(2,1)S(1)} %fusion), channel_id=1, source_target_pairs={{0,4},{4,8},{8,12},{12,16},{16,20},{20,24},{24,28},{1,5},{5,9},{9,... | collective-permute-start | bytes 786440 | tf_op jit(solution)/shard_map/ppermute | solution.py:346
  3.7 1.9 %dynamic-slice_bitcast_fusion.10 = (bf16[512,256]{1,0:T(8,128)(2,1)}, bf16[512,256]{1,0:T(8,128)(2,1)}) fusion(bf16[512,3,1024]{2,0,1:T(8,128)(2,1)} %param.11, s32[]{:T(128)S(6)} %select_n.80, s32[]{:T(128)S(6)} %select_n.78), kind=kLoop, calls=%fused_computation.16 | loop fusion | bytes 1048584 | tf_op jit(solution)/shard_map/squeeze | solution.py:334
  5.6 4.6 %collective-permute-start.5 = (bf16[512,256]{1,0:T(8,128)(2,1)}, bf16[512,256]{1,0:T(8,128)(2,1)S(1)}, u32[]{:S(2)}, u32[]{:S(2)}) collective-permute-start(bf16[512,256]{1,0:T(8,128)(2,1)} %get-tuple-element.77), channel_id=1, source_target_pairs={{0,24},{4,28},{8,0},{12,4},{16,8},{20,12},{24,16},{28,20},{1,25},{... | collective-permute-start | bytes 786440 | tf_op jit(solution)/shard_map/ppermute | solution.py:300
  10.3 6.0 %hyena_filters.1.own_ref = bf16[256,1024]{1,0:T(8,128)(2,1)S(1)} custom-call(bf16[3,256,1024]{2,1,0:T(8,128)(2,1)S(1)} %bitcast.33, bf16[128,1024]{1,0:T(8,128)(2,1)S(1)} %pad_select_fusion.halo_ref, f32[64,128]{1,0:T(8,128)S(1)} %copy-done.16), custom_call_target="tpu_custom_call" | custom-call | flops 1 | bytes 1 | tf_op jit(solution)/shard_map/hyena_filters/pallas_call | solution.py:80
  17.3 5.6 %collective-permute-done.1.refs_1_ = bf16[512,256]{1,0:T(8,128)(2,1)S(1)} collective-permute-done((bf16[512,256]{1,0:T(8,128)(2,1)}, bf16[512,256]{1,0:T(8,128)(2,1)S(1)}, u32[]{:S(2)}, u32[]{:S(2)}) %collective-permute-start.1) | collective-permute-done | bytes 262176 | tf_op jit(solution)/shard_map/ppermute | solution.py:300
  22.9 1.5 collective-permute-start.6
  24.4 1.5 collective-permute-start.8
  27.2 1.2 dynamic-slice_bitcast_fusion
  29.4 1.4 collective-permute-start.13
  30.8 6.5 %collective-permute-done.6.x_ref = bf16[256,1024]{1,0:T(8,128)(2,1)S(1)} collective-permute-done((bf16[256,1024]{1,0:T(8,128)(2,1)S(1)}, bf16[256,1024]{1,0:T(8,128)(2,1)S(1)}, u32[]{:S(2)}, u32[]{:S(2)}) %collective-permute-start.6) | collective-permute-done | bytes 524320 | tf_op jit(solution)/shard_map/ppermute | solution.py:308
  37.3 1.6 collective-permute-start.7
  38.9 1.6 collective-permute-start.9
  40.6 2.8 %collective-permute-done.2.own_ref = bf16[256,1024]{1,0:T(8,128)(2,1)} collective-permute-done((bf16[256,1024]{1,0:T(8,128)(2,1)S(1)}, bf16[256,1024]{1,0:T(8,128)(2,1)}, u32[]{:S(2)}, u32[]{:S(2)}) %collective-permute-start.2) | collective-permute-done | bytes 524320 | tf_op jit(solution)/shard_map/ppermute | solution.py:300
  43.4 2.0 %collective-permute-done.7.d0_ref = bf16[128,1024]{1,0:T(8,128)(2,1)S(1)} collective-permute-done((bf16[128,1024]{1,0:T(8,128)(2,1)S(1)}, bf16[128,1024]{1,0:T(8,128)(2,1)S(1)}, u32[]{:S(2)}, u32[]{:S(2)}) %collective-permute-start.7) | collective-permute-done | bytes 262176 | tf_op jit(solution)/shard_map/ppermute | solution.py:308
  47.4 1.1 collective-permute-start.15
  48.5 1.3 collective-permute-start.10
  49.8 1.7 collective-permute-done.12.refs_4_
  51.5 1.0 copy-done.2
  52.6 1.0 copy-done.4
  55.5 1.9 %norm.4.rest_0_ = bf16[4,4,256,1024]{3,2,1,0:T(8,128)(2,1)S(1)} custom-call(s32[3]{0:T(128)S(1)} %pad_add_fusion.place_ref, bf16[256,1024]{1,0:T(8,128)(2,1)S(1)} %hyena_filters.1.own_ref, bf16[256,1024]{1,0:T(8,128)(2,1)S(1)} %copy-done.2, bf16[256,1024]{1,0:T(8,128)(2,1)S(1)} %copy-done.4, bf16[128,1024]{1,0:T(8,128)(2,1)S(1)} %copy-done.12, ...), custom_call_target="tpu_custom_call" | custom-call | flops 1 | bytes 1 | tf_op jit(solution)/shard_map/norm/pallas_call | solution.py:119
  57.7 2.3 %collective-permute-done.15.y_ref = bf16[256,1024]{1,0:T(8,128)(2,1)S(1)} collective-permute-done((bf16[256,1024]{1,0:T(8,128)(2,1)}, bf16[256,1024]{1,0:T(8,128)(2,1)S(1)}, u32[]{:S(2)}, u32[]{:S(2)}) %collective-permute-start.15) | collective-permute-done | bytes 524320 | tf_op jit(solution)/shard_map/ppermute | solution.py:308
  60.1 1.6 collective-permute-start.16
  62.6 1.3 collective-permute-start.14
  65.0 4.1 %collective-permute-done.3.own_ref = bf16[256,1024]{1,0:T(8,128)(2,1)S(1)} collective-permute-done((bf16[256,1024]{1,0:T(8,128)(2,1)}, bf16[256,1024]{1,0:T(8,128)(2,1)S(1)}, u32[]{:S(2)}, u32[]{:S(2)}) %collective-permute-start.3) | collective-permute-done | bytes 524320 | tf_op jit(solution)/shard_map/ppermute | solution.py:300
  69.1 1.2 collective-permute-start.22
  72.9 2.6 %norm.5.rest_0_ = bf16[4,4,256,1024]{3,2,1,0:T(8,128)(2,1)S(1)} custom-call(s32[3]{0:T(128)S(1)} %pad_add_fusion.place_ref, bf16[256,1024]{1,0:T(8,128)(2,1)} %collective-permute-done.2.own_ref, bf16[256,1024]{1,0:T(8,128)(2,1)} %collective-permute-done.10.x_ref, ...), custom_call_target="tpu_custom_call", output_to_operand_aliasing={{}: (7, {})} | custom-call | flops 1 | bytes 1 | tf_op jit(solution)/shard_map/norm/pallas_call | solution.py:119
  75.4 8.4 %collective-permute-done.20.refs_2_ = bf16[1344,256]{1,0:T(8,128)(2,1)S(1)} collective-permute-done((bf16[1344,256]{1,0:T(8,128)(2,1)S(1)}, bf16[1344,256]{1,0:T(8,128)(2,1)S(1)}, u32[]{:S(2)}, u32[]{:S(2)}) %collective-permute-start.20) | collective-permute-done | bytes 688160 | tf_op jit(solution)/shard_map/ppermute | solution.py:300
  84.9 9.4 %collective-permute-done.4.own_ref = bf16[256,1024]{1,0:T(8,128)(2,1)S(1)} collective-permute-done((bf16[256,1024]{1,0:T(8,128)(2,1)S(1)}, bf16[256,1024]{1,0:T(8,128)(2,1)S(1)}, u32[]{:S(2)}, u32[]{:S(2)}) %collective-permute-start.4) | collective-permute-done | bytes 524320 | tf_op jit(solution)/shard_map/ppermute | solution.py:300
  95.5 2.9 %collective-permute-start.32 = (bf16[832,256]{1,0:T(8,128)(2,1)S(1)}, bf16[832,256]{1,0:T(8,128)(2,1)S(1)}, u32[]{:S(2)}, u32[]{:S(2)}) collective-permute-start(bf16[832,256]{1,0:T(8,128)(2,1)S(1)} %pad_maximum_fusion.3), channel_id=1, source_target_pairs={{0,16},{4,20},{8,24},{12,28},{16,0},{20,4},{24,8},{28,12},{1,17},{... | collective-permute-start | bytes 1277960 | tf_op jit(solution)/shard_map/ppermute | solution.py:300
  98.4 1.9 %norm.6.rest_0_ = bf16[4,4,256,1024]{3,2,1,0:T(8,128)(2,1)S(1)} custom-call(s32[3]{0:T(128)S(1)} %pad_add_fusion.place_ref, bf16[256,1024]{1,0:T(8,128)(2,1)S(1)} %collective-permute-done.3.own_ref, bf16[256,1024]{1,0:T(8,128)(2,1)S(1)} %collective-permute-done.17.x_ref, ...), custom_call_target="tpu_custom_call", output_to_operand_aliasing={{}: (7, {})} | custom-call | flops 1 | bytes 1 | tf_op jit(solution)/shard_map/norm/pallas_call | solution.py:119
  100.3 18.2 %collective-permute-done.26.refs_3_ = bf16[512,256]{1,0:T(8,128)(2,1)S(1)} collective-permute-done((bf16[512,256]{1,0:T(8,128)(2,1)S(1)}, bf16[512,256]{1,0:T(8,128)(2,1)S(1)}, u32[]{:S(2)}, u32[]{:S(2)}) %collective-permute-start.26) | collective-permute-done | bytes 262176 | tf_op jit(solution)/shard_map/ppermute | solution.py:300
  119.3 1.6 collective-permute-start.28
  121.0 5.9 %collective-permute-done.29.d1_ref = bf16[128,1024]{1,0:T(8,128)(2,1)S(1)} collective-permute-done((bf16[128,1024]{1,0:T(8,128)(2,1)S(1)}, bf16[128,1024]{1,0:T(8,128)(2,1)S(1)}, u32[]{:S(2)}, u32[]{:S(2)}) %collective-permute-start.29) | collective-permute-done | bytes 262176 | tf_op jit(solution)/shard_map/ppermute | solution.py:308
  127.3 1.9 %norm.7.normed_ref = bf16[4,4,256,1024]{3,2,1,0:T(8,128)(2,1)S(1)} custom-call(s32[3]{0:T(128)S(1)} %pad_add_fusion.place_ref, bf16[256,1024]{1,0:T(8,128)(2,1)S(1)} %collective-permute-done.4.own_ref, bf16[256,1024]{1,0:T(8,128)(2,1)S(1)} %collective-permute-done.24.x_ref, ...), custom_call_target="tpu_custom_call", output_to_operand_aliasing={{}: (7, {})} | custom-call | flops 1 | bytes 1 | tf_op jit(solution)/shard_map/norm/pallas_call | solution.py:119
  129.3 4.0 %project.5 = (f32[4,256,256]{2,1,0:T(8,128)S(1)}, f32[4,256,256]{2,1,0:T(8,128)S(1)}) custom-call(s32[3]{0:T(128)S(1)} %pad_add_fusion.place_ref, bf16[4,4,256,1024]{3,2,1,0:T(8,128)(2,1)S(1)} %norm.7.normed_ref, bf16[1344,256]{1,0:T(8,128)(2,1)S(1)} %pad_maximum_fusion.refs_0_, bf16[1344,256]{1,0:T(8,128)(2,1)S(1)} %collective-permute-done.13.refs_1_, ...), custom_call_target="tpu_custom_call" | custom-call | flops 1 | bytes 1 | tf_op jit(solution)/shard_map/project/pallas_call | solution.py:155
  134.1 1.3 collective-permute-done.33.refs_7_
  135.5 3.3 %project.4.q_ref = bf16[4,256,256]{2,1,0:T(8,128)(2,1)S(1)} custom-call(s32[3]{0:T(128)S(1)} %pad_add_fusion.place_ref, bf16[4,4,256,1024]{3,2,1,0:T(8,128)(2,1)S(1)} %norm.7.normed_ref, bf16[512,256]{1,0:T(8,128)(2,1)S(1)} %get-tuple-element.74.refs_0_, bf16[512,256]{1,0:T(8,128)(2,1)S(1)} %copy-done.10, bf16[512,256]{1,0:T(8,128)(2,1)S(1)} %copy-done.8, ...), custom_call_target="tpu_custom_call" | custom-call | flops 1 | bytes 1 | tf_op jit(solution)/shard_map/project/pallas_call | solution.py:155
  138.8 1.3 project.6.k_ref
  141.7 1.3 project.7.v_ref
  143.4 1.6 collective-permute-done.38.vs_ref
  145.0 3.8 %attend.3 = bf16[256,256]{1,0:T(8,128)(2,1)S(1)} custom-call(s32[3]{0:T(128)S(1)} %pad_add_fusion.place_ref, bf16[4,256,256]{2,1,0:T(8,128)(2,1)S(1)} %project.4.q_ref, bf16[4,256,256]{2,1,0:T(8,128)(2,1)S(1)} %project.6.k_ref, bf16[4,256,256]{2,1,0:T(8,128)(2,1)S(1)} %project.7.v_ref, bf16[4,256,256]{2,1,0:T(8,128)(2,1)S(1)} %collective-permute-done.37.ks_ref, ...), custom_call_target="tpu_custom_call" | custom-call | flops 1 | bytes 1 | tf_op jit(solution)/shard_map/attend/pallas_call | solution.py:239
  148.9 7.1 %attend.4 = (bf16[256,256]{1,0:T(8,128)(2,1)S(1)}, bf16[256,256]{1,0:T(8,128)(2,1)S(1)}) custom-call(s32[3]{0:T(128)S(1)} %pad_add_fusion.place_ref, bf16[4,256,256]{2,1,0:T(8,128)(2,1)S(1)} %project.4.q_ref, bf16[4,256,256]{2,1,0:T(8,128)(2,1)S(1)} %project.6.k_ref, bf16[4,256,256]{2,1,0:T(8,128)(2,1)S(1)} %project.7.v_ref, ...), custom_call_target="tpu_custom_call" | custom-call | flops 1 | bytes 1 | tf_op jit(solution)/shard_map/attend/pallas_call | solution.py:239
  156.9 3.0 %collective-permute-start.41 = (bf16[256,256]{1,0:T(8,128)(2,1)S(1)}, bf16[256,256]{1,0:T(8,128)(2,1)S(1)}, u32[]{:S(2)}, u32[]{:S(2)}) collective-permute-start(bf16[256,256]{1,0:T(8,128)(2,1)S(1)} %get-tuple-element.66), channel_id=1, source_target_pairs={{0,24},{4,28},{8,0},{12,4},{16,8},{20,12},{24,16},{28,20},{1,25},{... | collective-permute-start | bytes 393224 | tf_op jit(solution)/shard_map/ppermute | solution.py:300
  159.9 2.5 %attend.5.refs_0_ = bf16[256,256]{1,0:T(8,128)(2,1)S(1)} custom-call(s32[3]{0:T(128)S(1)} %pad_add_fusion.place_ref, bf16[4,256,256]{2,1,0:T(8,128)(2,1)S(1)} %project.4.q_ref, bf16[4,256,256]{2,1,0:T(8,128)(2,1)S(1)} %project.6.k_ref, bf16[4,256,256]{2,1,0:T(8,128)(2,1)S(1)} %project.7.v_ref, bf16[4,256,256]{2,1,0:T(8,128)(2,1)S(1)} %collective-permute-done.37.ks_ref, ...), custom_call_target="tpu_custom_call" | custom-call | flops 1 | bytes 1 | tf_op jit(solution)/shard_map/attend/pallas_call | solution.py:239
  163.0 1.2 collective-permute-done.40.refs_1_
  164.2 1.6 collective-permute-done.41.refs_3_
  166.4 2.0 %join.1 = bf16[256,1024]{1,0:T(8,128)(2,1)} custom-call(s32[3]{0:T(128)} %copy-done.15, bf16[256,256]{1,0:T(8,128)(2,1)} %copy-done.5, bf16[256,256]{1,0:T(8,128)(2,1)} %copy-done.29, bf16[256,256]{1,0:T(8,128)(2,1)} %copy-done.28, bf16[256,256]{1,0:T(8,128)(2,1)} %copy-done.30), custom_call_target="tpu_custom_call" | custom-call | tf_op jit(solution)/shard_map/join/pallas_call | solution.py:289
  (133 shorter events, 21.1 us)
Async XLA Ops:
  1.2 8.9 %collective-permute-start = (bf16[128,1024]{1,0:T(8,128)(2,1)S(1)}, bf16[128,1024]{1,0:T(8,128)(2,1)S(1)}, u32[]{:S(2)}, u32[]{:S(2)}) collective-permute-start(bf16[128,1024]{1,0:T(8,128)(2,1)S(1)} %fusion), channel_id=1, source_target_pairs={{0,4},{4,8},{8,12},{12,16},{16,20},{20,24},{24,28},{1,5},{5,9},{9,... | collective-permute-start | bytes 786440 | tf_op jit(solution)/shard_map/ppermute | solution.py:346
  5.6 11.7 %collective-permute-start.5 = (bf16[512,256]{1,0:T(8,128)(2,1)}, bf16[512,256]{1,0:T(8,128)(2,1)S(1)}, u32[]{:S(2)}, u32[]{:S(2)}) collective-permute-start(bf16[512,256]{1,0:T(8,128)(2,1)} %get-tuple-element.77), channel_id=1, source_target_pairs={{0,24},{4,28},{8,0},{12,4},{16,8},{20,12},{24,16},{28,20},{1,25},{... | collective-permute-start | bytes 786440 | tf_op jit(solution)/shard_map/ppermute | solution.py:300
  10.2 12.8 %collective-permute-start.1 = (bf16[512,256]{1,0:T(8,128)(2,1)}, bf16[512,256]{1,0:T(8,128)(2,1)S(1)}, u32[]{:S(2)}, u32[]{:S(2)}) collective-permute-start(bf16[512,256]{1,0:T(8,128)(2,1)} %get-tuple-element.78), channel_id=1, source_target_pairs={{0,8},{4,12},{8,16},{12,20},{16,24},{20,28},{24,0},{28,4},{1,9},{5... | collective-permute-start | bytes 786440 | tf_op jit(solution)/shard_map/ppermute | solution.py:300
  10.3 16.9 %copy-start.17 = (bf16[512,3,1024]{2,0,1:T(8,128)(2,1)S(1)}, bf16[512,3,1024]{2,0,1:T(8,128)(2,1)}, u32[]{:S(2)}) copy-start(bf16[512,3,1024]{2,0,1:T(8,128)(2,1)} %param.11) | copy-start | bytes 9437188
  22.9 14.3 %collective-permute-start.6 = (bf16[256,1024]{1,0:T(8,128)(2,1)S(1)}, bf16[256,1024]{1,0:T(8,128)(2,1)S(1)}, u32[]{:S(2)}, u32[]{:S(2)}) collective-permute-start(bf16[256,1024]{1,0:T(8,128)(2,1)S(1)} %hyena_filters.1.own_ref), channel_id=1, source_target_pairs={{0,1},{1,0},{2,3},{3,2},{4,5},{5,4},{6,7},{7,6},{8,9},{9,8},{10,11... | collective-permute-start | bytes 1572872 | tf_op jit(solution)/shard_map/ppermute | solution.py:308
  24.4 14.4 %collective-permute-start.8 = (bf16[256,1024]{1,0:T(8,128)(2,1)S(1)}, bf16[256,1024]{1,0:T(8,128)(2,1)S(1)}, u32[]{:S(2)}, u32[]{:S(2)}) collective-permute-start(bf16[256,1024]{1,0:T(8,128)(2,1)S(1)} %hyena_filters.1.own_ref), channel_id=1, source_target_pairs={{0,2},{1,3},{2,0},{3,1},{4,6},{5,7},{6,4},{7,5},{8,10},{9,11},{10,... | collective-permute-start | bytes 1572872 | tf_op jit(solution)/shard_map/ppermute | solution.py:308
  26.7 16.7 %collective-permute-start.2 = (bf16[256,1024]{1,0:T(8,128)(2,1)S(1)}, bf16[256,1024]{1,0:T(8,128)(2,1)}, u32[]{:S(2)}, u32[]{:S(2)}) collective-permute-start(bf16[256,1024]{1,0:T(8,128)(2,1)S(1)} %hyena_filters.1.own_ref), channel_id=1, source_target_pairs={{0,8},{4,12},{8,16},{12,20},{16,24},{20,28},{24,0},{28,4},{1,9},{5... | collective-permute-start | bytes 1572872 | tf_op jit(solution)/shard_map/ppermute | solution.py:300
  29.4 22.2 %copy-start.6 = (f32[4096]{0:T(1024)S(1)}, f32[4096]{0:T(1024)}, u32[]{:S(2)}) copy-start(f32[4096]{0:T(1024)} %param.10) | copy-start | bytes 49156
  29.4 28.4 %collective-permute-start.13 = (bf16[1344,256]{1,0:T(8,128)(2,1)}, bf16[1344,256]{1,0:T(8,128)(2,1)S(1)}, u32[]{:S(2)}, u32[]{:S(2)}) collective-permute-start(bf16[1344,256]{1,0:T(8,128)(2,1)} %pad_maximum_fusion.1), channel_id=1, source_target_pairs={{0,8},{4,12},{8,16},{12,20},{16,24},{20,28},{24,0},{28,4},{1,9},{5... | collective-permute-start | bytes 2064392 | tf_op jit(solution)/shard_map/ppermute | solution.py:300
  37.3 8.1 %collective-permute-start.7 = (bf16[128,1024]{1,0:T(8,128)(2,1)S(1)}, bf16[128,1024]{1,0:T(8,128)(2,1)S(1)}, u32[]{:S(2)}, u32[]{:S(2)}) collective-permute-start(bf16[128,1024]{1,0:T(8,128)(2,1)S(1)} %slice.50), channel_id=1, source_target_pairs={{0,2},{1,3},{2,0},{3,1},{4,6},{5,7},{6,4},{7,5},{8,10},{9,11},{10,... | collective-permute-start | bytes 786440 | tf_op jit(solution)/shard_map/ppermute | solution.py:308
  38.9 7.8 %collective-permute-start.9 = (bf16[128,1024]{1,0:T(8,128)(2,1)S(1)}, bf16[128,1024]{1,0:T(8,128)(2,1)S(1)}, u32[]{:S(2)}, u32[]{:S(2)}) collective-permute-start(bf16[128,1024]{1,0:T(8,128)(2,1)S(1)} %slice.51), channel_id=1, source_target_pairs={{0,1},{1,0},{2,3},{3,2},{4,5},{5,4},{6,7},{7,6},{8,9},{9,8},{10,11... | collective-permute-start | bytes 786440 | tf_op jit(solution)/shard_map/ppermute | solution.py:308
  40.5 17.3 %collective-permute-start.11 = (bf16[1344,256]{1,0:T(8,128)(2,1)S(1)}, bf16[1344,256]{1,0:T(8,128)(2,1)S(1)}, u32[]{:S(2)}, u32[]{:S(2)}) collective-permute-start(bf16[1344,256]{1,0:T(8,128)(2,1)S(1)} %pad_maximum_fusion.refs_0_), channel_id=1, source_target_pairs={{0,4},{4,0},{8,12},{12,8},{16,20},{20,16},{24,28},{28,24},{1,5},{5... | collective-permute-start | bytes 2064392 | tf_op jit(solution)/shard_map/ppermute | solution.py:304
  47.4 12.7 %collective-permute-start.15 = (bf16[256,1024]{1,0:T(8,128)(2,1)}, bf16[256,1024]{1,0:T(8,128)(2,1)S(1)}, u32[]{:S(2)}, u32[]{:S(2)}) collective-permute-start(bf16[256,1024]{1,0:T(8,128)(2,1)} %collective-permute-done.2.own_ref), channel_id=1, source_target_pairs={{0,2},{1,3},{2,0},{3,1},{4,6},{5,7},{6,4},{7,5},{8,10},{9,11},{10,... | collective-permute-start | bytes 1572872 | tf_op jit(solution)/shard_map/ppermute | solution.py:308
  48.5 13.2 %collective-permute-start.10 = (bf16[256,1024]{1,0:T(8,128)(2,1)}, bf16[256,1024]{1,0:T(8,128)(2,1)}, u32[]{:S(2)}, u32[]{:S(2)}) collective-permute-start(bf16[256,1024]{1,0:T(8,128)(2,1)} %collective-permute-done.2.own_ref), channel_id=1, source_target_pairs={{0,1},{1,0},{2,3},{3,2},{4,5},{5,4},{6,7},{7,6},{8,9},{9,8},{10,11... | collective-permute-start | bytes 1572872 | tf_op jit(solution)/shard_map/ppermute | solution.py:308
  49.8 1.7 collective-permute-start.12
  51.5 17.6 %collective-permute-start.3 = (bf16[256,1024]{1,0:T(8,128)(2,1)}, bf16[256,1024]{1,0:T(8,128)(2,1)S(1)}, u32[]{:S(2)}, u32[]{:S(2)}) collective-permute-start(bf16[256,1024]{1,0:T(8,128)(2,1)} %collective-permute-done.2.own_ref), channel_id=1, source_target_pairs={{0,8},{4,12},{8,16},{12,20},{16,24},{20,28},{24,0},{28,4},{1,9},{5... | collective-permute-start | bytes 1572872 | tf_op jit(solution)/shard_map/ppermute | solution.py:300
  51.5 108.4 %copy-start.15 = (s32[3]{0:T(128)}, s32[3]{0:T(128)S(1)}, u32[]{:S(2)}) copy-start(s32[3]{0:T(128)S(1)} %pad_add_fusion.place_ref) | copy-start | bytes 40
  60.1 9.0 %collective-permute-start.16 = (bf16[128,1024]{1,0:T(8,128)(2,1)S(1)}, bf16[128,1024]{1,0:T(8,128)(2,1)S(1)}, u32[]{:S(2)}, u32[]{:S(2)}) collective-permute-start(bf16[128,1024]{1,0:T(8,128)(2,1)S(1)} %slice.41), channel_id=1, source_target_pairs={{0,1},{1,0},{2,3},{3,2},{4,5},{5,4},{6,7},{7,6},{8,9},{9,8},{10,11... | collective-permute-start | bytes 786440 | tf_op jit(solution)/shard_map/ppermute | solution.py:308
  62.6 6.5 %collective-permute-start.14 = (bf16[128,1024]{1,0:T(8,128)(2,1)S(1)}, bf16[128,1024]{1,0:T(8,128)(2,1)S(1)}, u32[]{:S(2)}, u32[]{:S(2)}) collective-permute-start(bf16[128,1024]{1,0:T(8,128)(2,1)S(1)} %slice.40), channel_id=1, source_target_pairs={{0,2},{1,3},{2,0},{3,1},{4,6},{5,7},{6,4},{7,5},{8,10},{9,11},{10,... | collective-permute-start | bytes 786440 | tf_op jit(solution)/shard_map/ppermute | solution.py:308
  64.0 31.4 %copy-start.26 = (bf16[512,256]{1,0:T(8,128)(2,1)S(1)}, bf16[512,256]{1,0:T(8,128)(2,1)}, u32[]{:S(2)}) copy-start(bf16[512,256]{1,0:T(8,128)(2,1)} %get-tuple-element.50) | copy-start | bytes 786436
  64.0 31.5 %copy-start.19 = (bf16[512,256]{1,0:T(8,128)(2,1)S(1)}, bf16[512,256]{1,0:T(8,128)(2,1)}, u32[]{:S(2)}) copy-start(bf16[512,256]{1,0:T(8,128)(2,1)} %get-tuple-element.68) | copy-start | bytes 786436
  64.0 19.9 %collective-permute-start.20 = (bf16[1344,256]{1,0:T(8,128)(2,1)S(1)}, bf16[1344,256]{1,0:T(8,128)(2,1)S(1)}, u32[]{:S(2)}, u32[]{:S(2)}) collective-permute-start(bf16[1344,256]{1,0:T(8,128)(2,1)S(1)} %pad_maximum_fusion.2), channel_id=1, source_target_pairs={{0,24},{4,28},{8,0},{12,4},{16,8},{20,12},{24,16},{28,20},{1,25},{... | collective-permute-start | bytes 2064392 | tf_op jit(solution)/shard_map/ppermute | solution.py:300
  69.1 14.8 %collective-permute-start.22 = (bf16[256,1024]{1,0:T(8,128)(2,1)S(1)}, bf16[256,1024]{1,0:T(8,128)(2,1)S(1)}, u32[]{:S(2)}, u32[]{:S(2)}) collective-permute-start(bf16[256,1024]{1,0:T(8,128)(2,1)S(1)} %collective-permute-done.3.own_ref), channel_id=1, source_target_pairs={{0,2},{1,3},{2,0},{3,1},{4,6},{5,7},{6,4},{7,5},{8,10},{9,11},{10,... | collective-permute-start | bytes 1572872 | tf_op jit(solution)/shard_map/ppermute | solution.py:308
  70.3 13.9 %collective-permute-start.17 = (bf16[256,1024]{1,0:T(8,128)(2,1)S(1)}, bf16[256,1024]{1,0:T(8,128)(2,1)S(1)}, u32[]{:S(2)}, u32[]{:S(2)}) collective-permute-start(bf16[256,1024]{1,0:T(8,128)(2,1)S(1)} %collective-permute-done.3.own_ref), channel_id=1, source_target_pairs={{0,1},{1,0},{2,3},{3,2},{4,5},{5,4},{6,7},{7,6},{8,9},{9,8},{10,11... | collective-permute-start | bytes 1572872 | tf_op jit(solution)/shard_map/ppermute | solution.py:308
  70.8 1.5 collective-permute-start.18
  70.8 1.9 %collective-permute-start.19 = (bf16[512,256]{1,0:T(8,128)(2,1)S(1)}, bf16[512,256]{1,0:T(8,128)(2,1)S(1)}, u32[]{:S(2)}, u32[]{:S(2)}) collective-permute-start(bf16[512,256]{1,0:T(8,128)(2,1)S(1)} %copy-done.8), channel_id=1, source_target_pairs={{0,4},{4,0},{8,12},{12,8},{16,20},{20,16},{24,28},{28,24},{1,5},{5... | collective-permute-start | bytes 786440 | tf_op jit(solution)/shard_map/ppermute | solution.py:304
  72.3 22.0 %collective-permute-start.4 = (bf16[256,1024]{1,0:T(8,128)(2,1)S(1)}, bf16[256,1024]{1,0:T(8,128)(2,1)S(1)}, u32[]{:S(2)}, u32[]{:S(2)}) collective-permute-start(bf16[256,1024]{1,0:T(8,128)(2,1)S(1)} %collective-permute-done.3.own_ref), channel_id=1, source_target_pairs={{0,8},{4,12},{8,16},{12,20},{16,24},{20,28},{24,0},{28,4},{1,9},{5... | collective-permute-start | bytes 1572872 | tf_op jit(solution)/shard_map/ppermute | solution.py:300
  72.7 22.8 %collective-permute-start.25 = (bf16[1344,256]{1,0:T(8,128)(2,1)S(1)}, bf16[1344,256]{1,0:T(8,128)(2,1)S(1)}, u32[]{:S(2)}, u32[]{:S(2)}) collective-permute-start(bf16[1344,256]{1,0:T(8,128)(2,1)S(1)} %collective-permute-done.13.refs_1_), channel_id=1, source_target_pairs={{0,4},{4,0},{8,12},{12,8},{16,20},{20,16},{24,28},{28,24},{1,5},{5... | collective-permute-start | bytes 2064392 | tf_op jit(solution)/shard_map/ppermute | solution.py:304
  83.9 10.5 %collective-permute-start.23 = (bf16[128,1024]{1,0:T(8,128)(2,1)S(1)}, bf16[128,1024]{1,0:T(8,128)(2,1)S(1)}, u32[]{:S(2)}, u32[]{:S(2)}) collective-permute-start(bf16[128,1024]{1,0:T(8,128)(2,1)S(1)} %slice.43), channel_id=1, source_target_pairs={{0,1},{1,0},{2,3},{3,2},{4,5},{5,4},{6,7},{7,6},{8,9},{9,8},{10,11... | collective-permute-start | bytes 786440 | tf_op jit(solution)/shard_map/ppermute | solution.py:308
  84.2 10.1 %collective-permute-start.21 = (bf16[128,1024]{1,0:T(8,128)(2,1)S(1)}, bf16[128,1024]{1,0:T(8,128)(2,1)S(1)}, u32[]{:S(2)}, u32[]{:S(2)}) collective-permute-start(bf16[128,1024]{1,0:T(8,128)(2,1)S(1)} %slice.42), channel_id=1, source_target_pairs={{0,2},{1,3},{2,0},{3,1},{4,6},{5,7},{6,4},{7,5},{8,10},{9,11},{10,... | collective-permute-start | bytes 786440 | tf_op jit(solution)/shard_map/ppermute | solution.py:308
  94.3 24.2 %collective-permute-start.27 = (bf16[256,1024]{1,0:T(8,128)(2,1)S(1)}, bf16[256,1024]{1,0:T(8,128)(2,1)S(1)}, u32[]{:S(2)}, u32[]{:S(2)}) collective-permute-start(bf16[256,1024]{1,0:T(8,128)(2,1)S(1)} %collective-permute-done.4.own_ref), channel_id=1, source_target_pairs={{0,2},{1,3},{2,0},{3,1},{4,6},{5,7},{6,4},{7,5},{8,10},{9,11},{10,... | collective-permute-start | bytes 1572872 | tf_op jit(solution)/shard_map/ppermute | solution.py:308
  94.8 24.5 %collective-permute-start.24 = (bf16[256,1024]{1,0:T(8,128)(2,1)S(1)}, bf16[256,1024]{1,0:T(8,128)(2,1)S(1)}, u32[]{:S(2)}, u32[]{:S(2)}) collective-permute-start(bf16[256,1024]{1,0:T(8,128)(2,1)S(1)} %collective-permute-done.4.own_ref), channel_id=1, source_target_pairs={{0,1},{1,0},{2,3},{3,2},{4,5},{5,4},{6,7},{7,6},{8,9},{9,8},{10,11... | collective-permute-start | bytes 1572872 | tf_op jit(solution)/shard_map/ppermute | solution.py:308
  95.3 34.0 %collective-permute-start.31 = (bf16[1344,256]{1,0:T(8,128)(2,1)S(1)}, bf16[1344,256]{1,0:T(8,128)(2,1)S(1)}, u32[]{:S(2)}, u32[]{:S(2)}) collective-permute-start(bf16[1344,256]{1,0:T(8,128)(2,1)S(1)} %collective-permute-done.20.refs_2_), channel_id=1, source_target_pairs={{0,4},{4,0},{8,12},{12,8},{16,20},{20,16},{24,28},{28,24},{1,5},{5... | collective-permute-start | bytes 2064392 | tf_op jit(solution)/shard_map/ppermute | solution.py:304
  95.3 23.2 %collective-permute-start.26 = (bf16[512,256]{1,0:T(8,128)(2,1)S(1)}, bf16[512,256]{1,0:T(8,128)(2,1)S(1)}, u32[]{:S(2)}, u32[]{:S(2)}) collective-permute-start(bf16[512,256]{1,0:T(8,128)(2,1)S(1)} %copy-done.26), channel_id=1, source_target_pairs={{0,16},{4,20},{8,24},{12,28},{16,0},{20,4},{24,8},{28,12},{1,17},{... | collective-permute-start | bytes 786440 | tf_op jit(solution)/shard_map/ppermute | solution.py:300
  95.5 25.4 %copy-start.18 = (bf16[512,256]{1,0:T(8,128)(2,1)S(1)}, bf16[512,256]{1,0:T(8,128)(2,1)}, u32[]{:S(2)}) copy-start(bf16[512,256]{1,0:T(8,128)(2,1)} %get-tuple-element.67) | copy-start | bytes 786436
  95.5 37.9 %collective-permute-start.32 = (bf16[832,256]{1,0:T(8,128)(2,1)S(1)}, bf16[832,256]{1,0:T(8,128)(2,1)S(1)}, u32[]{:S(2)}, u32[]{:S(2)}) collective-permute-start(bf16[832,256]{1,0:T(8,128)(2,1)S(1)} %pad_maximum_fusion.3), channel_id=1, source_target_pairs={{0,16},{4,20},{8,24},{12,28},{16,0},{20,4},{24,8},{28,12},{1,17},{... | collective-permute-start | bytes 1277960 | tf_op jit(solution)/shard_map/ppermute | solution.py:300
  118.5 8.3 %collective-permute-start.29 = (bf16[128,1024]{1,0:T(8,128)(2,1)S(1)}, bf16[128,1024]{1,0:T(8,128)(2,1)S(1)}, u32[]{:S(2)}, u32[]{:S(2)}) collective-permute-start(bf16[128,1024]{1,0:T(8,128)(2,1)S(1)} %slice.45), channel_id=1, source_target_pairs={{0,1},{1,0},{2,3},{3,2},{4,5},{5,4},{6,7},{7,6},{8,9},{9,8},{10,11... | collective-permute-start | bytes 786440 | tf_op jit(solution)/shard_map/ppermute | solution.py:308
  119.3 8.0 %collective-permute-start.28 = (bf16[128,1024]{1,0:T(8,128)(2,1)S(1)}, bf16[128,1024]{1,0:T(8,128)(2,1)S(1)}, u32[]{:S(2)}, u32[]{:S(2)}) collective-permute-start(bf16[128,1024]{1,0:T(8,128)(2,1)S(1)} %slice.44), channel_id=1, source_target_pairs={{0,2},{1,3},{2,0},{3,1},{4,6},{5,7},{6,4},{7,5},{8,10},{9,11},{10,... | collective-permute-start | bytes 786440 | tf_op jit(solution)/shard_map/ppermute | solution.py:308
  120.9 19.2 %collective-permute-start.35 = (bf16[528,256]{1,0:T(8,128)(2,1)S(1)}, bf16[528,256]{1,0:T(8,128)(2,1)S(1)}, u32[]{:S(2)}, u32[]{:S(2)}) collective-permute-start(bf16[528,256]{1,0:T(8,128)(2,1)S(1)} %concatenate.19), channel_id=1, source_target_pairs={{0,16},{4,20},{8,24},{12,28},{16,0},{20,4},{24,8},{28,12},{1,17},{... | collective-permute-start | bytes 811016 | tf_op jit(solution)/shard_map/ppermute | solution.py:300
  129.2 6.3 %collective-permute-start.30 = (bf16[512,256]{1,0:T(8,128)(2,1)S(1)}, bf16[512,256]{1,0:T(8,128)(2,1)S(1)}, u32[]{:S(2)}, u32[]{:S(2)}) collective-permute-start(bf16[512,256]{1,0:T(8,128)(2,1)S(1)} %collective-permute-done.26.refs_3_), channel_id=1, source_target_pairs={{0,4},{4,0},{8,12},{12,8},{16,20},{20,16},{24,28},{28,24},{1,5},{5... | collective-permute-start | bytes 786440 | tf_op jit(solution)/shard_map/ppermute | solution.py:304
  133.4 5.4 %collective-permute-start.34 = (bf16[512,256]{1,0:T(8,128)(2,1)S(1)}, bf16[512,256]{1,0:T(8,128)(2,1)S(1)}, u32[]{:S(2)}, u32[]{:S(2)}) collective-permute-start(bf16[512,256]{1,0:T(8,128)(2,1)S(1)} %slice.47), channel_id=1, source_target_pairs={{0,4},{4,0},{8,12},{12,8},{16,20},{20,16},{24,28},{28,24},{1,5},{5... | collective-permute-start | bytes 786440 | tf_op jit(solution)/shard_map/ppermute | solution.py:304
  133.9 1.5 collective-permute-start.33
  140.1 1.6 collective-permute-start.36
  140.5 2.9 %collective-permute-start.37 = (bf16[4,256,256]{2,1,0:T(8,128)(2,1)S(1)}, bf16[4,256,256]{2,1,0:T(8,128)(2,1)S(1)}, u32[]{:S(2)}, u32[]{:S(2)}) collective-permute-start(bf16[4,256,256]{2,1,0:T(8,128)(2,1)S(1)} %project.6.k_ref), channel_id=1, source_target_pairs={{0,4},{4,0},{8,12},{12,8},{16,20},{20,16},{24,28},{28,24},{1,5},{5... | collective-permute-start | bytes 1572872 | tf_op jit(solution)/shard_map/ppermute | solution.py:304
  143.0 2.0 %collective-permute-start.38 = (bf16[4,256,256]{2,1,0:T(8,128)(2,1)S(1)}, bf16[4,256,256]{2,1,0:T(8,128)(2,1)S(1)}, u32[]{:S(2)}, u32[]{:S(2)}) collective-permute-start(bf16[4,256,256]{2,1,0:T(8,128)(2,1)S(1)} %project.7.v_ref), channel_id=1, source_target_pairs={{0,4},{4,0},{8,12},{12,8},{16,20},{20,16},{24,28},{28,24},{1,5},{5... | collective-permute-start | bytes 1572872 | tf_op jit(solution)/shard_map/ppermute | solution.py:304
  148.8 11.1 %collective-permute-start.39 = (bf16[256,256]{1,0:T(8,128)(2,1)S(1)}, bf16[256,256]{1,0:T(8,128)(2,1)S(1)}, u32[]{:S(2)}, u32[]{:S(2)}) collective-permute-start(bf16[256,256]{1,0:T(8,128)(2,1)S(1)} %attend.3), channel_id=1, source_target_pairs={{0,16},{4,20},{8,24},{12,28},{16,0},{20,4},{24,8},{28,12},{1,17},{... | collective-permute-start | bytes 393224 | tf_op jit(solution)/shard_map/ppermute | solution.py:300
  156.0 8.2 %collective-permute-start.40 = (bf16[256,256]{1,0:T(8,128)(2,1)S(1)}, bf16[256,256]{1,0:T(8,128)(2,1)S(1)}, u32[]{:S(2)}, u32[]{:S(2)}) collective-permute-start(bf16[256,256]{1,0:T(8,128)(2,1)S(1)} %get-tuple-element.64), channel_id=1, source_target_pairs={{0,8},{4,12},{8,16},{12,20},{16,24},{20,28},{24,0},{28,4},{1,9},{5... | collective-permute-start | bytes 393224 | tf_op jit(solution)/shard_map/ppermute | solution.py:300
  156.9 8.9 %collective-permute-start.41 = (bf16[256,256]{1,0:T(8,128)(2,1)S(1)}, bf16[256,256]{1,0:T(8,128)(2,1)S(1)}, u32[]{:S(2)}, u32[]{:S(2)}) collective-permute-start(bf16[256,256]{1,0:T(8,128)(2,1)S(1)} %get-tuple-element.66), channel_id=1, source_target_pairs={{0,24},{4,28},{8,0},{12,4},{16,8},{20,12},{24,16},{28,20},{1,25},{... | collective-permute-start | bytes 393224 | tf_op jit(solution)/shard_map/ppermute | solution.py:300
  (25 other events, 159.6 us)
